TPU v7x, 32 devices: a whole 2x2x4 slice. The times are simulated.
32 devices in a mesh: grp: 2 (over y), lon: 8 (over z, x), lat: 2 (over core).
Axes of the slice: x: 2, y: 2, z: 4, core: 2. Of those that a mesh axis runs over, the one named last changes fastest.
Arguments:
- tokens: bfloat16 [4, 24, 192, 192], P('grp', 'lat', 'lon'), parts along dimension 0, may hold values from -6 to 6
- cotangent: bfloat16 [4, 24, 192, 192], P('grp', 'lat', 'lon'), parts along dimension 0, may hold values from -6 to 6
- qkv_weight: bfloat16 [2, 192, 576], replicated, may hold values from -0.4375 to 0.4375
- proj_weight: bfloat16 [2, 192, 192], replicated, may hold values from -0.4375 to 0.4375
- up_weight: bfloat16 [2, 192, 768], replicated, may hold values from -0.4375 to 0.4375
- down_weight: bfloat16 [2, 768, 192], replicated, may hold values from -0.21875 to 0.21875
- norm_gain: float32 [2, 2, 192], replicated, may hold values from 0.5 to 1.5
- bias_table: float32 [2, 2, 6, 6336], P(None, 'lat'), may hold values from -4 to 316
Outputs:
- tokens_grad: bfloat16 [4, 24, 192, 192], P('grp', 'lat', 'lon'), parts along dimension 0
- update: bfloat16 [1771008], P('grp'), parts along dimension 0
- bias_grad: float32 [4, 2, 6, 6336], P('grp', 'lat'), parts along dimension 0
There are 2 independent parts, one for each index of `grp`. A program takes and returns all parts, laid end to end along the dimension named above; an argument that names none is the same for every part. Nothing has to cross between parts.
All inputs are finite; a program needn't handle non-finite values.
Results may differ from a plain program's by a relative error of at most 0.02.
Values may be sent and summed in bfloat16 or wider, within the bound.
No kernel may reach another device: no remote copies, remote signals or barrier semaphores. Data moves between devices by JAX's collectives and lax.ppermute only.
A program may use at most 128 MiB of HBM per device.

v0:
```python
import jax
import jax.numpy as jnp
from jax import lax
from jax.sharding import PartitionSpec as P

WLAT = 12
WLON = 6
PAD = 5


EPS = 1e-05
NEGATIVE = -1000000000.0
ROOT_HALF = 0.7071067811865476
INV_ROOT_TAU = 0.3989422804014327


def from_behind(value, axis, steps):
    count = lax.axis_size(axis)
    pairs = [(source, (source + steps) % count) for source in range(count)]
    return lax.ppermute(value, axis, pairs)


def norm_forward(field, gain_row):
    average = jnp.mean(field, axis=-1, keepdims=True)
    centred = field - average
    variance = jnp.mean(centred * centred, axis=-1, keepdims=True)
    inv_std = lax.rsqrt(variance + EPS)
    standard = centred * inv_std
    return (standard * gain_row, standard, inv_std)


def norm_backward(upstream, gain_row, standard, inv_std):
    scaled = upstream * gain_row
    gain_grad = jnp.sum(upstream * standard, axis=(0, 1, 2))
    first_mean = jnp.mean(scaled, axis=-1, keepdims=True)
    second_mean = jnp.mean(scaled * standard, axis=-1, keepdims=True)
    return (inv_std * (scaled - first_mean - standard * second_mean), gain_grad)


def gelu_value(hidden):
    return 0.5 * hidden * (1.0 + lax.erf(hidden * ROOT_HALF))


def gelu_slope(hidden):
    return (
        0.5 * (1.0 + lax.erf(hidden * ROOT_HALF))
        + hidden * jnp.exp(-0.5 * hidden * hidden) * INV_ROOT_TAU
    )


def token_outer(left, right):
    left_rows = left.reshape(-1, left.shape[-1])
    right_rows = right.reshape(-1, right.shape[-1])
    return lax.dot_general(
        left_rows, right_rows, (((0,), (0,)), ((), ())), preferred_element_type=jnp.float32
    )


def times_transposed(field, matrix):
    return lax.dot_general(
        field, matrix, (((field.ndim - 1,), (1,)), ((), ())), preferred_element_type=jnp.float32
    )


def to_windows(field):
    levels, lat_rows, lon_cols, width = field.shape
    field = field.reshape(levels, lat_rows // WLAT, WLAT, lon_cols // WLON, WLON, width)
    field = field.transpose(1, 3, 0, 2, 4, 5)
    return field.reshape(lat_rows // WLAT, lon_cols // WLON, levels * WLAT * WLON, width)


def from_windows(windows, levels):
    row_count, col_count, tokens_w, width = windows.shape
    field = windows.reshape(row_count, col_count, levels, WLAT, WLON, width)
    field = field.transpose(2, 0, 3, 1, 4, 5)
    return field.reshape(levels, row_count * WLAT, col_count * WLON, width)


def shift_table():
    query_lon = jnp.arange(WLON)[:, None]
    key_lon = jnp.arange(WLON)[None, :]
    target = (query_lon - key_lon + WLON - 1).reshape(-1)
    return (jnp.arange(2 * WLON - 1)[:, None] == target[None, :]).astype(jnp.float32)


def expand_bias(rows_table, levels):
    row_count, head_count = (rows_table.shape[0], rows_table.shape[1])
    grid = rows_table.reshape(row_count, head_count, levels, levels, WLAT, WLAT, 2 * WLON - 1)
    spread = jnp.dot(grid, shift_table(), precision=lax.Precision.HIGHEST)
    spread = spread.reshape(row_count, head_count, levels, levels, WLAT, WLAT, WLON, WLON)
    spread = spread.transpose(0, 1, 2, 4, 6, 3, 5, 7)
    tokens_w = levels * WLAT * WLON
    return spread.reshape(row_count, head_count, tokens_w, tokens_w)


def fold_bias(full_grad, levels):
    row_count, head_count = (full_grad.shape[0], full_grad.shape[1])
    grid = full_grad.reshape(row_count, head_count, levels, WLAT, WLON, levels, WLAT, WLON)
    grid = grid.transpose(0, 1, 2, 5, 3, 6, 4, 7)
    grid = grid.reshape(row_count, head_count, levels, levels, WLAT, WLAT, WLON * WLON)
    folded = jnp.dot(grid, shift_table().T, precision=lax.Precision.HIGHEST)
    return folded.reshape(row_count, head_count, -1)


def allowed_rows(first_row, row_count, lat_total, levels, shifted):
    tokens_w = levels * WLAT * WLON
    lat_inside = jnp.arange(tokens_w, dtype=jnp.int32) // WLON % WLAT
    rolled_row = (first_row + jnp.arange(row_count, dtype=jnp.int32))[:, None] * WLAT + lat_inside[
        None, :
    ]
    if shifted:
        anchor = (rolled_row + WLAT // 2) % lat_total
        region = rolled_row >= lat_total - WLAT // 2
    else:
        anchor = rolled_row
        region = rolled_row < 0
    usable = anchor < lat_total - PAD
    return usable[:, None, :] & (region[:, :, None] == region[:, None, :])


def roll_ahead(field):
    half_lon = WLON // 2
    half_lat = WLAT // 2
    arrived = from_behind(field[:, :, :half_lon], "lon", -1)
    field = jnp.concatenate([field[:, :, half_lon:], arrived], axis=2)
    arrived = from_behind(field[:, :half_lat], "lat", -1)
    return jnp.concatenate([field[:, half_lat:], arrived], axis=1)


def roll_behind(field):
    half_lon = WLON // 2
    half_lat = WLAT // 2
    arrived = from_behind(field[:, -half_lat:], "lat", 1)
    field = jnp.concatenate([arrived, field[:, :-half_lat]], axis=1)
    arrived = from_behind(field[:, :, -half_lon:], "lon", 1)
    return jnp.concatenate([arrived, field[:, :, :-half_lon]], axis=2)


def unchanged(field):
    return field


def attend_windows(qkv_windows, bias_full, allowed, heads):
    row_count, window_count, tokens_w, three_width = qkv_windows.shape
    head_dim = three_width // (3 * heads)
    split = qkv_windows.reshape(row_count, window_count, tokens_w, 3, heads, head_dim)
    logits = (
        jnp.einsum(
            "rwihd,rwjhd->rwhij",
            split[:, :, :, 0],
            split[:, :, :, 1],
            preferred_element_type=jnp.float32,
        )
        * head_dim ** (-0.5)
        + bias_full[:, None]
    )
    logits = jnp.where(allowed[:, None, None], logits, NEGATIVE)
    peak = jnp.max(logits, axis=-1, keepdims=True)
    weights = jnp.exp(logits - peak)
    probs = weights / jnp.sum(weights, axis=-1, keepdims=True)
    mixed = jnp.einsum(
        "rwhij,rwjhd->rwihd",
        probs.astype(jnp.bfloat16),
        split[:, :, :, 2],
        preferred_element_type=jnp.float32,
    )
    return (mixed.reshape(row_count, window_count, tokens_w, -1).astype(jnp.bfloat16), probs)


def attend_back(qkv_windows, probs, dmix_windows, heads):
    row_count, window_count, tokens_w, three_width = qkv_windows.shape
    head_dim = three_width // (3 * heads)
    split = qkv_windows.reshape(row_count, window_count, tokens_w, 3, heads, head_dim)
    upstream = dmix_windows.reshape(row_count, window_count, tokens_w, heads, head_dim)
    prob_grad = jnp.einsum(
        "rwihd,rwjhd->rwhij", upstream, split[:, :, :, 2], preferred_element_type=jnp.float32
    )
    logit_grad = probs * (prob_grad - jnp.sum(probs * prob_grad, axis=-1, keepdims=True))
    logit_low = logit_grad.astype(jnp.bfloat16)
    scale = head_dim ** (-0.5)
    query_grad = (
        jnp.einsum(
            "rwhij,rwjhd->rwihd", logit_low, split[:, :, :, 1], preferred_element_type=jnp.float32
        )
        * scale
    )
    key_grad = (
        jnp.einsum(
            "rwhij,rwihd->rwjhd", logit_low, split[:, :, :, 0], preferred_element_type=jnp.float32
        )
        * scale
    )
    value_grad = jnp.einsum(
        "rwhij,rwihd->rwjhd",
        probs.astype(jnp.bfloat16),
        upstream,
        preferred_element_type=jnp.float32,
    )
    qkv_grad = jnp.stack([query_grad, key_grad, value_grad], axis=3)
    qkv_grad = qkv_grad.reshape(row_count, window_count, tokens_w, three_width).astype(jnp.bfloat16)
    return (qkv_grad, jnp.sum(logit_grad, axis=1))


def forward_block(field, shifted, before, after, weights, first_row, lat_total, need_result):
    qkv_w, proj_w, up_w, down_w, gains, bias_rows = weights
    levels = field.shape[0]
    heads = bias_rows.shape[1]
    field32 = field.astype(jnp.float32)
    normed, stand_one, inv_one = norm_forward(field32, gains[0])
    normed = before(normed.astype(jnp.bfloat16))
    qkv = jnp.dot(normed, qkv_w, preferred_element_type=jnp.float32).astype(jnp.bfloat16)
    qkv_windows = to_windows(qkv)
    bias_full = expand_bias(bias_rows, levels)
    allowed = allowed_rows(first_row, bias_rows.shape[0], lat_total, levels, shifted)
    mixed_windows, probs = attend_windows(qkv_windows, bias_full, allowed, heads)
    mixed = from_windows(mixed_windows, levels)
    attended = after(
        jnp.dot(mixed, proj_w, preferred_element_type=jnp.float32).astype(jnp.bfloat16)
    )
    resid = (field32 + attended.astype(jnp.float32)).astype(jnp.bfloat16)
    resid32 = resid.astype(jnp.float32)
    normed_two, stand_two, inv_two = norm_forward(resid32, gains[1])
    normed_two = normed_two.astype(jnp.bfloat16)
    hidden = jnp.dot(normed_two, up_w, preferred_element_type=jnp.float32)
    active = gelu_value(hidden).astype(jnp.bfloat16)
    if need_result:
        result = (resid32 + jnp.dot(active, down_w, preferred_element_type=jnp.float32)).astype(
            jnp.bfloat16
        )
    else:
        result = resid
    saved = (
        normed,
        stand_one,
        inv_one,
        qkv_windows,
        probs,
        mixed,
        stand_two,
        inv_two,
        normed_two,
        hidden,
        active,
    )
    return (saved, result)


def backward_block(upstream, saved, before, after, weights):
    qkv_w, proj_w, up_w, down_w, gains, bias_rows = weights
    (
        normed,
        stand_one,
        inv_one,
        qkv_windows,
        probs,
        mixed,
        stand_two,
        inv_two,
        normed_two,
        hidden,
        active,
    ) = saved
    levels = normed.shape[0]
    heads = bias_rows.shape[1]
    upstream_low = upstream.astype(jnp.bfloat16)
    down_grad = token_outer(active, upstream_low)
    hidden_grad = (times_transposed(upstream_low, down_w) * gelu_slope(hidden)).astype(jnp.bfloat16)
    up_grad = token_outer(normed_two, hidden_grad)
    resid_part, gain_two = norm_backward(
        times_transposed(hidden_grad, up_w), gains[1], stand_two, inv_two
    )
    resid_grad = upstream + resid_part
    resid_low = before(resid_grad.astype(jnp.bfloat16))
    proj_grad = token_outer(mixed, resid_low)
    mixed_grad = times_transposed(resid_low, proj_w).astype(jnp.bfloat16)
    qkv_grad_windows, logit_rows = attend_back(qkv_windows, probs, to_windows(mixed_grad), heads)
    qkv_grad_field = from_windows(qkv_grad_windows, levels)
    qkv_grad = token_outer(normed, qkv_grad_field)
    normed_grad = after(times_transposed(qkv_grad_field, qkv_w).astype(jnp.bfloat16))
    field_part, gain_one = norm_backward(
        normed_grad.astype(jnp.float32), gains[0], stand_one, inv_one
    )
    bias_grad = fold_bias(logit_rows, levels)
    return (
        resid_grad + field_part,
        qkv_grad,
        proj_grad,
        up_grad,
        down_grad,
        jnp.stack([gain_one, gain_two]),
        bias_grad,
    )


def shards(
    tokens, cotangent, qkv_weight, proj_weight, up_weight, down_weight, norm_gain, bias_table
):
    lat_dev = tokens.shape[1]
    row_count = lat_dev // WLAT
    lat_total = lat_dev * lax.axis_size("lat")
    first_row = lax.axis_index("lat") * row_count
    lat_global = lax.axis_index("lat") * lat_dev + jnp.arange(lat_dev, dtype=jnp.int32)
    keep_rows = (lat_global < lat_total - PAD)[None, :, None, None]
    upstream = jnp.where(keep_rows, cotangent, jnp.zeros_like(cotangent))

    def layer_weights(index):
        return (
            qkv_weight[index],
            proj_weight[index],
            up_weight[index],
            down_weight[index],
            norm_gain[index],
            bias_table[index],
        )

    saved_zero, middle = forward_block(
        tokens, False, unchanged, unchanged, layer_weights(0), first_row, lat_total, True
    )
    saved_one, unused = forward_block(
        middle, True, roll_ahead, roll_behind, layer_weights(1), first_row, lat_total, False
    )
    back_one = backward_block(
        upstream.astype(jnp.float32), saved_one, roll_ahead, roll_behind, layer_weights(1)
    )
    middle_grad = back_one[0].astype(jnp.bfloat16)
    back_zero = backward_block(
        middle_grad.astype(jnp.float32), saved_zero, unchanged, unchanged, layer_weights(0)
    )
    tokens_grad = back_zero[0].astype(jnp.bfloat16)
    flat = jnp.concatenate(
        [
            jnp.stack([back_zero[1], back_one[1]]).reshape(-1),
            jnp.stack([back_zero[2], back_one[2]]).reshape(-1),
            jnp.stack([back_zero[3], back_one[3]]).reshape(-1),
            jnp.stack([back_zero[4], back_one[4]]).reshape(-1),
            jnp.stack([back_zero[5], back_one[5]]).reshape(-1),
        ]
    )
    total = lax.psum(flat, ("lon", "lat"))
    update = (total * lax.rsqrt(jnp.mean(total * total) + 1e-06)).astype(jnp.bfloat16)
    bias_local = jnp.stack([back_zero[6], back_one[6]])
    bias_grad = lax.psum(bias_local, "lon")
    return (tokens_grad, update, bias_grad)


def solution(mesh):
    return jax.shard_map(
        shards,
        mesh=mesh,
        in_specs=(
            P("grp", "lat", "lon", None),
            P("grp", "lat", "lon", None),
            P(),
            P(),
            P(),
            P(),
            P(),
            P(None, "lat", None, None),
        ),
        out_specs=(P("grp", "lat", "lon", None), P("grp"), P("grp", "lat", None, None)),
        check_vma=False,
    )
```

profile of v0, /device:TPU:0, one launch (start us, length us, event | category | flops | bytes accessed | tf_op | source)
XLA Modules:
  0.0 558.4 jit_solution(480918577062538119)
XLA Ops:
  11.2 2.5 slice_reduce_fusion
  17.8 2.4 reshape.724
  20.2 4.1 reshape_reshape.22
  24.3 2.0 fusion.186
  26.3 3.2 copy.158
  29.5 3.2 copy.157
  34.6 13.0 %convolution_bitcast_fusion.1 = f32[1,6,2,12,6,2,12,6]{6,7,3,5,2,1,4,0:T(8,128)} fusion(f32[6,2,2,12,12,11,1]{5,4,3,2,1,0,6:T(8,128)S(1)} %copy-done.1, pred[6,6,11,1,1,1,1]{2,1,0,3,4,5,6:T(8,128)(4,1)S(1)} %reshape.723), kind=kOutput, calls=%fused_computation.17 | convolution fusion | flops 16422912 | bytes 650124 | tf_op jit(solution)/shard_map/dot_general | solution.py:89
  47.6 19.7 %copy.153 = f32[1,6,2,12,6,2,12,6]{4,3,2,7,6,5,1,0:T(8,128)} copy(f32[1,6,2,12,6,2,12,6]{6,7,3,5,2,1,4,0:T(8,128)} %convolution_bitcast_fusion.1) | data formatting | bytes 995328 | tf_op jit(solution)/shard_map/add | solution.py:148
  67.3 12.0 %reshape.740 = f32[6,144,144]{1,2,0:T(8,128)} reshape(f32[1,6,2,12,6,2,12,6]{4,3,2,7,6,5,1,0:T(8,128)} %copy.153) | data formatting | bytes 995328 | tf_op jit(solution)/shard_map/add | solution.py:148
  80.0 3.5 fusion.190
  85.3 2.1 fusion.43
  87.4 2.7 copy.85
  95.3 6.1 %collective-permute-start = (bf16[2,12,3,192]{3,2,1,0:T(4,128)(2,1)}, bf16[2,12,3,192]{3,2,1,0:T(4,128)(2,1)}, u32[]{:S(2)}, u32[]{:S(2)}) collective-permute-start(bf16[2,12,3,192]{3,2,1,0:T(4,128)(2,1)} %slice.177), channel_id=1, source_target_pairs={{0,14},{2,0},{4,2},{6,4},{8,6},{10,8},{12,10},{14,12},{1,15},{3,1}... | collective-permute-start | bytes 82952 | tf_op jit(solution)/shard_map/ppermute | solution.py:20
  103.8 2.0 reshape.729
  107.6 13.7 %convolution_bitcast_fusion = f32[1,6,2,12,6,2,12,6]{6,7,3,5,2,1,4,0:T(8,128)} fusion(f32[6,2,2,12,12,11,1]{5,4,3,2,1,0,6:T(8,128)S(1)} %reshape.729, pred[6,6,11,1,1,1,1]{2,1,0,3,4,5,6:T(8,128)(4,1)} %copy-done.78), kind=kOutput, calls=%fused_computation.16 | convolution fusion | flops 16422912 | bytes 650124 | tf_op jit(solution)/shard_map/dot_general | solution.py:89
  121.3 19.7 %copy.154 = f32[1,6,2,12,6,2,12,6]{4,3,2,7,6,5,1,0:T(8,128)} copy(f32[1,6,2,12,6,2,12,6]{6,7,3,5,2,1,4,0:T(8,128)} %convolution_bitcast_fusion) | data formatting | bytes 995328 | tf_op jit(solution)/shard_map/add | solution.py:148
  141.0 11.7 %reshape.742 = f32[6,144,144]{1,2,0:T(8,128)} reshape(f32[1,6,2,12,6,2,12,6]{4,3,2,7,6,5,1,0:T(8,128)} %copy.154) | data formatting | bytes 995328 | tf_op jit(solution)/shard_map/add | solution.py:148
  155.8 4.1 reshape_reshape.23
  159.9 3.7 fusion.185
  163.6 3.1 copy.161
  169.7 4.6 fusion.197
  174.3 3.1 fusion.44
  177.4 2.7 copy.96
  185.8 4.1 collective-permute-done.3
  203.9 2.9 fusion.45
  208.0 2.0 fusion.28
  211.4 6.0 %copy.106 = bf16[1,4,144,3,6,32]{5,4,3,1,2,0:T(8,128)(2,1)} copy(bf16[1,4,144,3,6,32]{2,5,4,1,3,0:T(8,128)(2,1)S(1)} %pad_maximum_fusion) | data formatting | bytes 1327104 | tf_op jit(solution)/shard_map/stack | solution.py:199
  217.3 4.1 convert_element_type.227
  223.1 2.6 copy.127
  228.7 13.6 %reshape.720 = f32[1,6,2,12,6,2,12,6]{7,6,5,4,3,2,1,0:T(8,128)} reshape(f32[6,144,144]{2,1,0:T(8,128)} %copy.127) | data formatting | bytes 995328 | tf_op jit(solution)/shard_map/reshape | solution.py:98
  242.3 16.4 %copy.128 = f32[1,6,2,2,12,12,6,6]{5,3,7,6,4,2,1,0:T(2,128)} copy(f32[1,6,2,2,12,12,6,6]{7,5,3,6,4,2,1,0:T(8,128)} %bitcast.335) | data formatting | bytes 995328 | tf_op jit(solution)/shard_map/transpose | solution.py:99
  258.7 7.1 %fusion.2 = f32[6,2,2,12,12,11]{5,4,3,2,1,0:T(8,128)S(1)} fusion(f32[6,2,2,12,12,36]{4,2,5,3,1,0:T(2,128)} %bitcast.338, s32[36]{0:T(128)} %copy-done.92), kind=kOutput, calls=%fused_computation.2 | convolution fusion | flops 16423308 | bytes 649872 | tf_op jit(solution)/shard_map/dot_general | solution.py:101
  271.2 4.6 collective-permute-done.7
  275.7 2.0 fusion.93
  277.8 2.5 fusion.91
  288.2 2.9 fusion.46
  292.4 2.0 fusion.30
  296.0 5.8 %copy.116 = bf16[1,4,144,3,6,32]{5,4,3,1,2,0:T(8,128)(2,1)} copy(bf16[1,4,144,3,6,32]{2,5,4,1,3,0:T(8,128)(2,1)S(1)} %pad_maximum_fusion.1) | data formatting | bytes 1327104 | tf_op jit(solution)/shard_map/stack | solution.py:199
  301.8 4.4 convert_element_type.236
  319.6 3.2 fusion.79
  326.2 12.9 %reshape.718 = f32[1,6,2,12,6,2,12,6]{7,6,5,4,3,2,1,0:T(8,128)} reshape(f32[6,144,144]{2,1,0:T(8,128)S(1)} %copy-done.15) | data formatting | bytes 995328 | tf_op jit(solution)/shard_map/reshape | solution.py:98
  339.1 16.4 %copy.125 = f32[1,6,2,2,12,12,6,6]{5,3,7,6,4,2,1,0:T(2,128)} copy(f32[1,6,2,2,12,12,6,6]{7,5,3,6,4,2,1,0:T(8,128)} %bitcast.336) | data formatting | bytes 995328 | tf_op jit(solution)/shard_map/transpose | solution.py:99
  355.5 7.0 %fusion.4 = f32[6,2,2,12,12,11]{5,4,3,2,1,0:T(8,128)S(1)} fusion(f32[6,2,2,12,12,36]{4,2,5,3,1,0:T(2,128)} %bitcast.337, s32[36]{0:T(128)} %copy-done.92), kind=kOutput, calls=%fused_computation.4 | convolution fusion | flops 16423308 | bytes 649872 | tf_op jit(solution)/shard_map/dot_general | solution.py:101
  364.1 1.9 pad_maximum_fusion.5
  374.3 61.0 %all-reduce.5.cloned.1.call-done = f32[2,1,6,6336]{3,2,1,0:T(8,128)} async-done(((f32[2,1,6,6336]{3,2,1,0:T(8,128)}), f32[2,1,6,6336]{3,2,1,0:T(8,128)}) %all-reduce.5.cloned.1.call-update) | async-done | bytes 304144 | tf_op jit(solution)/shard_map/psum | solution.py:342
  435.2 2.0 copy.130
  437.3 108.1 %all-reduce.3.cloned.1.call-done = f32[885504]{0:T(1024)} async-done(((f32[885504]{0:T(1024)}), f32[885504]{0:T(1024)}) %all-reduce.3.cloned.1.call-update) | async-done | bytes 3542032 | tf_op jit(solution)/shard_map/psum | solution.py:339
  545.4 3.7 multiply_reduce_fusion
  (339 shorter events, 97.7 us)
Async XLA Ops:
  7.2 8.5 %copy-start.43 = (bf16[2,192,576]{2,1,0:T(8,128)(2,1)S(1)}, bf16[2,192,576]{2,1,0:T(8,128)(2,1)}, u32[]{:S(2)}) copy-start(bf16[2,192,576]{2,1,0:T(8,128)(2,1)} %param.10) | copy-start | bytes 1327108
  7.2 428.1 %all-reduce.5.cloned.1.call-start = ((), (), s32[]{:S(2)}) async-start(), calls=%async_computation.1 | async-start | bytes 819200 | tf_op jit(solution)/shard_map/psum | solution.py:342
  7.3 3.8 copy-start.92
  8.7 7.9 %copy-start.89 = (f32[1,1,192]{2,1,0:T(1,128)}, f32[1,1,192]{2,1,0:T(1,128)S(1)}, u32[]{:S(2)}) copy-start(f32[1,1,192]{2,1,0:T(1,128)S(1)} %get-tuple-element.45) | copy-start | bytes 2308
  8.8 25.8 %copy-start.78 = (pred[6,6,11,1,1,1,1]{2,1,0,3,4,5,6:T(8,128)(4,1)}, pred[6,6,11,1,1,1,1]{2,1,0,3,4,5,6:T(8,128)(4,1)S(1)}, u32[]{:S(2)}) copy-start(pred[6,6,11,1,1,1,1]{2,1,0,3,4,5,6:T(8,128)(4,1)S(1)} %reshape.723) | copy-start | bytes 1192
  9.9 4.9 copy-start.61
  11.2 3.7 copy-start.70
  26.3 6.4 %copy-start.7 = (bf16[1,4,144,1,6,32]{5,4,3,1,2,0:T(8,128)(2,1)S(1)}, bf16[1,4,144,1,6,32]{5,4,3,1,2,0:T(8,128)(2,1)}, u32[]{:S(2)}) copy-start(bf16[1,4,144,1,6,32]{5,4,3,1,2,0:T(8,128)(2,1)} %get-tuple-element.34) | copy-start | bytes 663556
  29.5 5.1 copy-start.1
  87.4 3.8 copy-start.5
  87.4 3.8 copy-start.46
  94.1 9.7 %copy-start.49 = (f32[2,12,24]{2,1,0:T(8,128)}, f32[2,12,24]{2,1,0:T(8,128)S(1)}, u32[]{:S(2)}) copy-start(f32[2,12,24]{2,1,0:T(8,128)S(1)} %broadcast_multiply_fusion.9) | copy-start | bytes 6916
  94.4 9.4 %copy-start.59 = (f32[2,12,24]{2,1,0:T(8,128)}, f32[2,12,24]{2,1,0:T(8,128)S(1)}, u32[]{:S(2)}) copy-start(f32[2,12,24]{2,1,0:T(8,128)S(1)} %add_rsqrt_fusion.1) | copy-start | bytes 6916
  95.3 10.5 %collective-permute-start = (bf16[2,12,3,192]{3,2,1,0:T(4,128)(2,1)}, bf16[2,12,3,192]{3,2,1,0:T(4,128)(2,1)}, u32[]{:S(2)}, u32[]{:S(2)}) collective-permute-start(bf16[2,12,3,192]{3,2,1,0:T(4,128)(2,1)} %slice.177), channel_id=1, source_target_pairs={{0,14},{2,0},{4,2},{6,4},{8,6},{10,8},{12,10},{14,12},{1,15},{3,1}... | collective-permute-start | bytes 82952 | tf_op jit(solution)/shard_map/ppermute | solution.py:20
  107.6 46.0 %collective-permute-start.1 = (bf16[2,6,24,192]{3,2,1,0:T(8,128)(2,1)}, bf16[2,6,24,192]{3,2,1,0:T(8,128)(2,1)}, u32[]{:S(2)}, u32[]{:S(2)}) collective-permute-start(bf16[2,6,24,192]{3,2,1,0:T(8,128)(2,1)} %get-tuple-element.38), channel_id=1, source_target_pairs={{0,1},{1,0},{2,3},{3,2},{4,5},{5,4},{6,7},{7,6},{8,9},{9,8},{10,11... | collective-permute-start | bytes 331784 | tf_op jit(solution)/shard_map/ppermute | solution.py:20
  141.0 11.7 %copy-start.28 = (bf16[2,1,12,4,6,192]{5,4,3,2,0,1:T(8,128)(2,1)S(1)}, bf16[2,1,12,4,6,192]{5,4,3,2,0,1:T(8,128)(2,1)}, u32[]{:S(2)}) copy-start(bf16[2,1,12,4,6,192]{5,4,3,2,0,1:T(8,128)(2,1)} %copy.121) | copy-start | bytes 663556
  141.0 12.6 %copy-start.29 = (bf16[2,6,24,192]{3,2,1,0:T(8,128)(2,1)S(1)}, bf16[2,6,24,192]{3,2,1,0:T(8,128)(2,1)}, u32[]{:S(2)}) copy-start(bf16[2,6,24,192]{3,2,1,0:T(8,128)(2,1)} %get-tuple-element.37) | copy-start | bytes 331780
  141.0 12.6 %copy-start.44 = (bf16[2,192,576]{2,1,0:T(8,128)(2,1)S(1)}, bf16[2,192,576]{2,1,0:T(8,128)(2,1)}, u32[]{:S(2)}) copy-start(bf16[2,192,576]{2,1,0:T(8,128)(2,1)} %param.10) | copy-start | bytes 1327108
  169.7 4.6 copy-start.52
  177.4 3.7 copy-start.47
  181.4 1.6 collective-permute-start.2
  183.0 7.4 %copy-start.82 = (f32[1,1,192]{2,1,0:T(1,128)S(1)}, f32[1,1,192]{2,1,0:T(1,128)}, u32[]{:S(2)}) copy-start(f32[1,1,192]{2,1,0:T(1,128)} %get-tuple-element.43) | copy-start | bytes 2308
  183.0 6.9 %collective-permute-start.3 = (bf16[2,12,3,192]{3,2,1,0:T(4,128)(2,1)S(1)}, bf16[2,12,3,192]{3,2,1,0:T(4,128)(2,1)S(1)}, u32[]{:S(2)}, u32[]{:S(2)}) collective-permute-start(bf16[2,12,3,192]{3,2,1,0:T(4,128)(2,1)S(1)} %pad_maximum_fusion.14), channel_id=1, source_target_pairs={{0,2},{2,4},{4,6},{6,8},{8,10},{10,12},{12,14},{14,0},{1,3},{3,5},... | collective-permute-start | bytes 82952 | tf_op jit(solution)/shard_map/ppermute | solution.py:20
  185.8 6.2 %copy-start.31 = (bf16[2,12,24,192]{3,2,1,0:T(8,128)(2,1)S(1)}, bf16[2,12,24,192]{3,2,1,0:T(8,128)(2,1)}, u32[]{:S(2)}) copy-start(bf16[2,12,24,192]{3,2,1,0:T(8,128)(2,1)} %param.9) | copy-start | bytes 663556
  185.8 6.2 %copy-start.74 = (bf16[2,768,192]{1,2,0:T(8,128)(2,1)S(1)}, bf16[2,768,192]{1,2,0:T(8,128)(2,1)}, u32[]{:S(2)}) copy-start(bf16[2,768,192]{1,2,0:T(8,128)(2,1)} %param.13) | copy-start | bytes 1769476
  185.8 6.2 %copy-start.93 = (pred[12]{0:T(512)(128)(4,1)S(1)}, pred[12]{0:T(512)(128)(4,1)}, u32[]{:S(2)}) copy-start(pred[12]{0:T(512)(128)(4,1)} %add_compare_fusion) | copy-start | bytes 40
  190.1 5.5 copy-start.4
  190.1 5.4 copy-start.50
  190.4 5.1 copy-start.60
  194.5 4.5 collective-permute-start.4
  199.2 1.5 collective-permute-start.5
  203.9 3.4 copy-start.54
  203.9 3.4 copy-start.81
  226.9 40.3 %collective-permute-start.6 = (bf16[2,6,24,192]{3,2,1,0:T(8,128)(2,1)}, bf16[2,6,24,192]{3,2,1,0:T(8,128)(2,1)}, u32[]{:S(2)}, u32[]{:S(2)}) collective-permute-start(bf16[2,6,24,192]{3,2,1,0:T(8,128)(2,1)} %get-tuple-element.39), channel_id=1, source_target_pairs={{0,1},{1,0},{2,3},{3,2},{4,5},{5,4},{6,7},{7,6},{8,9},{9,8},{10,11... | collective-permute-start | bytes 331784 | tf_op jit(solution)/shard_map/ppermute | solution.py:20
  258.7 7.2 %copy-start.16 = (bf16[576,576]{1,0:T(8,128)(2,1)S(1)}, bf16[576,576]{1,0:T(8,128)(2,1)}, u32[]{:S(2)}) copy-start(bf16[576,576]{1,0:T(8,128)(2,1)} %reshape_reshape.25) | copy-start | bytes 1990660
  258.7 7.2 %copy-start.34 = (bf16[2,12,24,192]{3,2,1,0:T(8,128)(2,1)S(1)}, bf16[2,12,24,192]{3,2,1,0:T(8,128)(2,1)}, u32[]{:S(2)}) copy-start(bf16[2,12,24,192]{3,2,1,0:T(8,128)(2,1)} %pad_maximum_fusion.9) | copy-start | bytes 663556
  258.7 8.4 %copy-start.40 = (bf16[2,6,24,192]{3,2,1,0:T(8,128)(2,1)S(1)}, bf16[2,6,24,192]{3,2,1,0:T(8,128)(2,1)}, u32[]{:S(2)}) copy-start(bf16[2,6,24,192]{3,2,1,0:T(8,128)(2,1)} %copy-done.39) | copy-start | bytes 331780
  258.7 8.4 %copy-start.77 = (bf16[2,6,24,192]{3,2,1,0:T(8,128)(2,1)S(1)}, bf16[2,6,24,192]{3,2,1,0:T(8,128)(2,1)}, u32[]{:S(2)}) copy-start(bf16[2,6,24,192]{3,2,1,0:T(8,128)(2,1)} %copy-done.76) | copy-start | bytes 331780
  268.6 7.1 %collective-permute-start.7 = (bf16[2,12,3,192]{3,2,1,0:T(4,128)(2,1)}, bf16[2,12,3,192]{3,2,1,0:T(4,128)(2,1)}, u32[]{:S(2)}, u32[]{:S(2)}) collective-permute-start(bf16[2,12,3,192]{3,2,1,0:T(4,128)(2,1)} %pad_maximum_fusion.13), channel_id=1, source_target_pairs={{0,2},{2,4},{4,6},{6,8},{8,10},{10,12},{12,14},{14,0},{1,3},{3,5},... | collective-permute-start | bytes 82952 | tf_op jit(solution)/shard_map/ppermute | solution.py:20
  271.2 9.2 %copy-start.3 = (bf16[2,12,24,768]{3,2,1,0:T(8,128)(2,1)S(1)}, bf16[2,12,24,768]{3,2,1,0:T(8,128)(2,1)}, u32[]{:S(2)}) copy-start(bf16[2,12,24,768]{3,2,1,0:T(8,128)(2,1)} %copy-done.2) | copy-start | bytes 2654212
  288.2 3.4 copy-start.55
  314.8 3.4 copy-start.11
  316.2 3.3 copy-start.6
  319.6 3.7 copy-start.18
  364.1 4.5 copy-start.8
  366.0 3.6 copy-start.9
  366.1 179.3 %all-reduce.3.cloned.1.call-start = ((), (), s32[]{:S(2)}) async-start(), calls=%async_computation | async-start | bytes 7086080 | tf_op jit(solution)/shard_map/psum | solution.py:339
  545.4 4.4 copy-start
  (58 other events, 110.1 us)
Sparse Core Ops, SparseCore 0:
  366.2 69.0 all-reduce.4
  439.4 105.9 all-reduce.2
where the time goes:
time: 564 us; the launch traced here: 558 us
  local copies, waits for them, and re-layouts  233 us (41%)
  waiting for transfers between devices  180 us (32%)
  matrix products  85.4 us (15%)
  other arithmetic  34.7 us (6%)
  between operations  16.5 us (3%)
  starting transfers between devices  8.46 us (2%)
    psum x1, waiting for transfers between devices, shards(): total = lax.psum(flat, ('lon', 'lat'))  108 us
    add x4, local copies, waits for them, and re-layouts, attend_windows(): jnp.einsum('rwihd,rwjhd->rwhij', split[:, :, :, 0], split[:, :, :, 1], pr...  63 us
    psum x1, waiting for transfers between devices, shards(): bias_grad = lax.psum(bias_local, 'lon')  61 us
    transpose x2, local copies, waits for them, and re-layouts, fold_bias(): grid = grid.transpose(0, 1, 2, 5, 3, 6, 4, 7)  32.8 us
    unnamed x203, local copies, waits for them, and re-layouts  28.1 us
    dot_general x2, matrix products, expand_bias(): spread = jnp.dot(grid, shift_table(), precision=lax.Precision.HIGHEST)  26.6 us
    reshape x2, local copies, waits for them, and re-layouts, fold_bias(): full_grad.reshape(row_count, head_count, levels, WLAT, WLON, levels, WLAT...  26.5 us
    dot_general x2, matrix products, fold_bias(): folded = jnp.dot(grid, shift_table().T, precision=lax.Precision.HIGHEST)  14.1 us
  transfers between devices with their start and end apart: 10, of which 6 were waited for; matrix products, arithmetic and copies ran while one was open for 19% of the time, Pallas kernels for 0%

commit v1 on v0

v1 whole, which is shorter than its diff:
```python
import functools

import jax
import jax.numpy as jnp
import numpy as np
from jax import lax
from jax.experimental import pallas as pl
from jax.experimental.pallas import tpu as pltpu
from jax.sharding import PartitionSpec as P

WLAT = 12
WLON = 6
PAD = 5
LEVELS = 2
HEADS = 6
CHUNK = LEVELS * WLAT
WIN = CHUNK * WLON
SHIFTS = 2 * WLON - 1
PAIR = WLAT * SHIFTS
WIDE = 384

EPS = 1e-05
NEGATIVE = -1000000000.0
ROOT_HALF = 0.7071067811865476
INV_ROOT_TAU = 0.3989422804014327

F32 = jnp.float32
BF16 = jnp.bfloat16
UNIT = 24
BIAS_UNITS = CHUNK * 8 // UNIT * (WIDE // 128)
VMEM_LIMIT = 48 * 1024 * 1024


def dot(a, b):
    return lax.dot_general(a, b, (((1,), (0,)), ((), ())), preferred_element_type=F32)


def dot_nt(a, b):
    return lax.dot_general(a, b, (((1,), (1,)), ((), ())), preferred_element_type=F32)


def dot_tn(a, b):
    return lax.dot_general(a, b, (((0,), (0,)), ((), ())), preferred_element_type=F32)


def row_mean(v):
    return jnp.sum(v, axis=-1, keepdims=True) * (1.0 / v.shape[-1])


def standardize(x):
    centred = x - row_mean(x)
    inv = lax.rsqrt(row_mean(centred * centred) + EPS)
    return centred * inv, inv


def norm_back(d, gain, stand, inv):
    scaled = d * gain
    first = row_mean(scaled)
    second = row_mean(scaled * stand)
    gain_grad = jnp.sum(d * stand, axis=0, keepdims=True)
    return inv * (scaled - first - stand * second), gain_grad


def gelu_parts(hidden):
    half = 0.5 * (1.0 + lax.erf(hidden * ROOT_HALF))
    slope = half + hidden * jnp.exp(-0.5 * hidden * hidden) * INV_ROOT_TAU
    return hidden * half, slope


def split3(v):
    hi = v.astype(BF16)
    rest = v - hi.astype(F32)
    mid = rest.astype(BF16)
    low = (rest - mid.astype(F32)).astype(BF16)
    return hi, mid, low


def spread_matrices():
    out = np.zeros((LEVELS, PAIR, WIDE), np.float32)
    for zj in range(LEVELS):
        for aj in range(WLAT):
            for d in range(SHIFTS):
                out[zj, aj * SHIFTS + d, (SHIFTS - 1 - d) * CHUNK + zj * WLAT + aj] = 1.0
    return out


def put(scr, rows, value):
    width = value.shape[1]
    for tile in range(-(-width // 128)):
        lanes = min(128, width - tile * 128)
        scr[tile, rows, 0:lanes] = value[:, tile * 128 : tile * 128 + lanes]


def get(scr, rows, width):
    parts = [scr[tile, rows, :] for tile in range(-(-width // 128))]
    return jnp.concatenate(parts, axis=1)[:, 0:width]


def head_masks(width, dtype):
    lane = lax.broadcasted_iota(jnp.int32, (1, width), 1)
    size = width // HEADS
    return [((lane >= h * size) & (lane < (h + 1) * size)).astype(dtype) for h in range(HEADS)]


def lat_inside(n):
    return lax.rem(n, WLAT)


def lat_row(row_iota, lat, shifted, lat_total):
    row = lat * WLAT + lat_inside(row_iota)
    if shifted:
        row = row + WLAT // 2
        row = jnp.where(row >= lat_total, row - lat_total, row)
    return row


def expand_bias(table, spread, rows_scr, wide_scr, bias_scr, lat, shifted, lat_total):
    for zi in range(LEVELS):
        for zj in range(LEVELS):
            for ai in range(WLAT):
                at = ((zi * LEVELS + zj) * WLAT + ai) * PAIR
                row = zj * CHUNK * 8 + (zi * WLAT + ai) * 8
                rows_scr[row : row + HEADS, 0:PAIR] = table[:, at : at + PAIR]
    count = CHUNK * 8
    total = jnp.zeros((count, WIDE), F32)
    for zj in range(LEVELS):
        parts = split3(rows_scr[zj * count : (zj + 1) * count, 0:PAIR])
        for part in parts:
            total = total + dot(part, spread[zj])
    put(wide_scr, slice(None), total)
    i = lax.broadcasted_iota(jnp.int32, (CHUNK, WIN), 0)
    j = lax.broadcasted_iota(jnp.int32, (CHUNK, WIN), 1)
    allowed = lat_row(j, lat, shifted, lat_total) < lat_total - PAD
    if shifted:
        last = lat_total - WLAT // 2
        region_i = (lat * WLAT + lat_inside(i)) >= last
        region_j = (lat * WLAT + lat_inside(j)) >= last
        allowed = allowed & (region_i == region_j)
    for h in range(HEADS):
        wide = get(wide_scr, pl.ds(h, CHUNK, stride=8), WIDE)
        for oi in range(WLON):
            back = (WLON - 1 - oi) * CHUNK
            moved = wide if back == 0 else pltpu.roll(wide, WIDE - back, axis=1)
            at = h * WIN + oi * CHUNK
            bias_scr[at : at + CHUNK, :] = jnp.where(allowed, moved[:, 0:WIN], NEGATIVE)


def fold_bias(sums, wide_scr, out):
    wide_scr[...] = jnp.zeros(wide_scr.shape, F32)
    for h in range(HEADS):
        total = jnp.zeros((CHUNK, WIDE), F32)
        for oi in range(WLON):
            back = (WLON - 1 - oi) * CHUNK
            at = h * WIN + oi * CHUNK
            part = sums[at : at + CHUNK, :]
            total = total + (part if back == 0 else pltpu.roll(part, back, axis=1))
        put(wide_scr, pl.ds(h, CHUNK, stride=8), total)
    count, per = out.shape[:2]
    for k in range(count * per):
        tile, at = k % (WIDE // 128), k // (WIDE // 128) * UNIT
        if k < BIAS_UNITS:
            out[k // per, k % per] = wide_scr[tile, at : at + UNIT, :].astype(BF16)
        else:
            out[k // per, k % per] = jnp.zeros((UNIT, 128), BF16)


def attend(qkv, bias, mixed, probs, width):
    masks = head_masks(width, BF16)
    masks32 = head_masks(width, F32)
    scale = (width // HEADS) ** -0.5

    def window(w, carry):
        rows = pl.ds(pl.multiple_of(w * WIN, 16), WIN)
        q = qkv[rows, 0:width]
        k = qkv[rows, width : 2 * width]
        v = qkv[rows, 2 * width : 3 * width]
        total = jnp.zeros((WIN, width), F32)
        for h in range(HEADS):
            logits = dot_nt(q * masks[h], k) * scale + bias[h * WIN : (h + 1) * WIN, :]
            weights = jnp.exp(logits - jnp.max(logits, axis=-1, keepdims=True))
            p = weights * (1.0 / jnp.sum(weights, axis=-1, keepdims=True))
            probs[w, h] = p
            total = total + dot(p.astype(BF16), v) * masks32[h]
        mixed[rows, :] = total.astype(BF16)
        return carry

    lax.fori_loop(0, probs.shape[0], window, 0)


def attend_back(qkv, probs, dmix, field, sums, width):
    masks = head_masks(width, BF16)
    masks32 = head_masks(width, F32)
    scale = (width // HEADS) ** -0.5
    sums[...] = jnp.zeros(sums.shape, F32)

    def window(w, carry):
        rows = pl.ds(pl.multiple_of(w * WIN, 16), WIN)
        q = qkv[rows, 0:width]
        k = qkv[rows, width : 2 * width]
        v = qkv[rows, 2 * width : 3 * width]
        up = dmix[rows, :]
        dq = jnp.zeros((WIN, width), F32)
        dk = jnp.zeros((WIN, width), F32)
        dv = jnp.zeros((WIN, width), F32)
        for h in range(HEADS):
            p = probs[w, h]
            up_h = up * masks[h]
            dp = dot_nt(up_h, v)
            ds = p * (dp - jnp.sum(p * dp, axis=-1, keepdims=True))
            sums[h * WIN : (h + 1) * WIN, 0:WIN] += ds
            low = ds.astype(BF16)
            dq = dq + dot(low, k) * masks32[h]
            dk = dk + dot_tn(low, q * masks[h])
            dv = dv + dot_tn(p.astype(BF16), up_h)
        field[rows, 0:width] = (dq * scale).astype(BF16)
        field[rows, width : 2 * width] = (dk * scale).astype(BF16)
        field[rows, 2 * width : 3 * width] = dv.astype(BF16)
        return carry

    lax.fori_loop(0, probs.shape[0], window, 0)


def lon_major(src, scr):
    levels, lats, lons, width = src.shape
    for z in range(levels):
        for a in range(lats):
            at = (z * lats + a) * lons
            put(scr, slice(at, at + lons), src[z, a].astype(F32))


def lon_column(scr, lon, lons, width):
    return get(scr, pl.ds(lon, CHUNK, stride=lons), width)


def flat_store(dst, at, mat, cols):
    rows = mat.shape[1]
    if cols % 128 == 0:
        per = cols // 128
        for c in range(per):
            dst[pl.ds(at + c, rows, stride=per), :] = mat[c]
        return rows * per
    per = 2 * cols // 128
    half = cols // 128
    even = get(mat, pl.ds(0, rows // 2, stride=2), cols)
    odd = get(mat, pl.ds(1, rows // 2, stride=2), cols)
    for c in range(half):
        dst[pl.ds(at + c, rows // 2, stride=per), :] = even[:, c * 128 : (c + 1) * 128]
    dst[pl.ds(at + half, rows // 2, stride=per), :] = jnp.concatenate(
        [even[:, half * 128 : half * 128 + 64], odd[:, 0:64]], axis=1
    )
    for c in range(half):
        dst[pl.ds(at + half + 1 + c, rows // 2, stride=per), :] = odd[
            :, 64 + c * 128 : 64 + (c + 1) * 128
        ]
    return rows * cols // 128


def send_units(scr, out):
    lats, lons, units = out.shape[:3]
    at = 0
    for i in range(lats):
        for j in range(lons):
            for u in range(units):
                if at < scr.shape[0]:
                    out[i, j, u] = scr[at : at + UNIT, :].astype(BF16)
                else:
                    out[i, j, u] = jnp.zeros((UNIT, 128), BF16)
                at += UNIT


def forward_core(x, b, lat, lat_total, refs, qkv_scr, bias_scr, mixed, probs):
    qkv_w, proj_w, gains = refs
    width = x.shape[-1]
    stand, inv = standardize(x)
    normed = (stand * gains[b, 0:1, :]).astype(BF16)
    qkv_scr[...] = dot(normed, qkv_w[b]).astype(BF16)
    attend(qkv_scr, bias_scr, mixed, probs, width)
    att = dot(mixed[...], proj_w[b]).astype(BF16)
    resid = (x + att.astype(F32)).astype(BF16).astype(F32)
    return resid, normed


def first_kernel(
    lat_total, tokens, table, spread, qkv_w, proj_w, up_w, down_w, gains,
    x_out, tail_out, head_out, qkv_out, mixed_out, probs_out, resid_out, slope_out, active_out,
    scr, rows_scr, wide_scr, bias_scr,
):
    lat = lax.axis_index("lat")
    width = tokens.shape[-1]
    lons = tokens.shape[2]
    expand_bias(
        table.at[0, 0], spread, rows_scr, wide_scr, bias_scr, lat, False, lat_total
    )
    lon_major(tokens, scr)
    x = jnp.concatenate([lon_column(scr, lon, lons, width) for lon in range(lons)], axis=0)
    x_out[...] = x.astype(BF16)
    resid, _ = forward_core(
        x, 0, lat, lat_total, (qkv_w, proj_w, gains), qkv_out, bias_scr, mixed_out, probs_out
    )
    resid_out[...] = resid.astype(BF16)
    stand, _ = standardize(resid)
    normed = (stand * gains[0, 1:2, :]).astype(BF16)
    active, slope = gelu_parts(dot(normed, up_w[0]))
    active = active.astype(BF16)
    active_out[...] = active
    slope_out[...] = slope.astype(BF16)
    result = resid + dot(active, down_w[0])
    cut = CHUNK * (WLON // 2)
    head_out[...] = result[0:cut, :].astype(BF16)
    tail_out[...] = result[cut:, :].astype(BF16)


def merge_ahead(scr_own, scr_oth, rows):
    half = WLAT // 2
    n = lax.broadcasted_iota(jnp.int32, (rows, 1), 0)
    return jnp.where(
        lat_inside(n) < half,
        pltpu.roll(scr_own[...], rows - half, axis=0),
        pltpu.roll(scr_oth[...], half, axis=0),
    )


def merge_behind(scr_own, scr_oth, rows):
    half = WLAT // 2
    n = lax.broadcasted_iota(jnp.int32, (rows, 1), 0)
    return jnp.where(
        lat_inside(n) >= half,
        pltpu.roll(scr_own[...], half, axis=0),
        pltpu.roll(scr_oth[...], rows - half, axis=0),
    )


def second_kernel(
    lat_total,
    tail, lon_head, lat_tail, diag_head, cot, cot_lon, cot_lat, cot_diag,
    table, spread, qkv_w, proj_w, up_w, down_w, gains,
    head_out, tail_out, n1_out, field_out, mixed_out, low_out, n2_out, hg_out, active_out, g_out,
    sums_out, gain_out,
    scr, scr_own, scr_oth, rows_scr, wide_scr, bias_scr, qkv_scr, probs_scr, dmix_scr,
):
    lat = lax.axis_index("lat")
    rows, width = scr_own.shape
    lons = cot.shape[2]
    cut = CHUNK * (WLON // 2)
    step = WLON // 2
    expand_bias(table.at[0, 0], spread, rows_scr, wide_scr, bias_scr, lat, True, lat_total)

    def columns(src, dst, first, last, at):
        lon_major(src, scr)
        for lon in range(first, last):
            dst[at : at + CHUNK, :] = lon_column(scr, lon, lons, width)
            at += CHUNK

    columns(cot, scr_own, step, lons, 0)
    columns(cot_lon, scr_own, 0, step, rows - cut)
    columns(cot_lat, scr_oth, step, lons, 0)
    columns(cot_diag, scr_oth, 0, step, rows - cut)
    g = merge_ahead(scr_own, scr_oth, rows)
    n = lax.broadcasted_iota(jnp.int32, (rows, 1), 0)
    keep = lat_row(n, lat, True, lat_total) < lat_total - PAD
    g = jnp.where(keep, g, 0.0)
    g_out[...] = g.astype(BF16)

    scr_own[0 : rows - cut, :] = tail[...].astype(F32)
    scr_own[rows - cut :, :] = lon_head[...].astype(F32)
    scr_oth[0 : rows - cut, :] = lat_tail[...].astype(F32)
    scr_oth[rows - cut :, :] = diag_head[...].astype(F32)
    x = merge_ahead(scr_own, scr_oth, rows)

    resid, normed = forward_core(
        x, 1, lat, lat_total, (qkv_w, proj_w, gains), qkv_scr, bias_scr, mixed_out, probs_scr
    )
    n1_out[...] = normed
    stand2, inv2 = standardize(resid)
    normed2 = (stand2 * gains[1, 1:2, :]).astype(BF16)
    n2_out[...] = normed2
    active, slope = gelu_parts(dot(normed2, up_w[1]))
    active_out[...] = active.astype(BF16)

    hg = (dot_nt(g_out[...], down_w[1]) * slope).astype(BF16)
    hg_out[...] = hg
    part, gain_two = norm_back(dot_nt(hg, up_w[1]), gains[1, 1:2, :], stand2, inv2)
    rg = g + part
    low = rg.astype(BF16)
    low_out[...] = low
    dmix_scr[...] = dot_nt(low, proj_w[1]).astype(BF16)
    attend_back(qkv_scr, probs_scr, dmix_scr, field_out, sums_out, width)
    ng = dot_nt(field_out[...], qkv_w[1]).astype(BF16).astype(F32)
    stand1, inv1 = standardize(x)
    part, gain_one = norm_back(ng, gains[1, 0:1, :], stand1, inv1)
    dx = rg + part
    head_out[...] = dx[0 : rows - cut, :].astype(BF16)
    tail_out[...] = dx[rows - cut :, :].astype(BF16)
    gain_out[0:1, :] = gain_one
    gain_out[1:2, :] = gain_two


def outer_kernel(
    n1, field, mixed, low, n2, hg, active, g, sums,
    flat_out, bias_out,
    m576, m192, m768, mdown, flat_scr, wide_scr,
):
    put(m576, slice(None), dot_tn(n1[...], field[...]))
    at = flat_store(flat_scr, 0, m576, field.shape[1])
    put(m192, slice(None), dot_tn(mixed[...], low[...]))
    at += flat_store(flat_scr, at, m192, mixed.shape[1])
    put(m768, slice(None), dot_tn(n2[...], hg[...]))
    at += flat_store(flat_scr, at, m768, active.shape[1])
    put(mdown, slice(None), dot_tn(active[...], g[...]))
    at += flat_store(flat_scr, at, mdown, mixed.shape[1])
    send_units(flat_scr, flat_out)
    fold_bias(sums, wide_scr, bias_out)


def third_kernel(
    head, lon_tail, lat_head, diag_tail, resid_in, slope, active, mixed,
    proj_w, up_w, down_w, gains,
    flat_out, rg_out, dmix_out, gain_out,
    scr_own, scr_oth, m192, m768, mdown, flat_scr,
):
    rows, width = scr_own.shape
    cut = CHUNK * (WLON // 2)
    scr_own[0:cut, :] = lon_tail[...].astype(F32)
    scr_own[cut:, :] = head[...].astype(F32)
    scr_oth[0:cut, :] = diag_tail[...].astype(F32)
    scr_oth[cut:, :] = lat_head[...].astype(F32)
    g = merge_behind(scr_own, scr_oth, rows)
    g_low = g.astype(BF16)
    hg = (dot_nt(g_low, down_w[0]) * slope[...].astype(F32)).astype(BF16)
    stand2, inv2 = standardize(resid_in[...].astype(F32))
    normed2 = (stand2 * gains[0, 1:2, :]).astype(BF16)
    part, gain_two = norm_back(dot_nt(hg, up_w[0]), gains[0, 1:2, :], stand2, inv2)
    rg = g + part
    rg_out[...] = rg
    low = rg.astype(BF16)
    dmix_out[...] = dot_nt(low, proj_w[0]).astype(BF16)
    gain_out[...] = gain_two
    put(m192, slice(None), dot_tn(mixed[...], low))
    at = flat_store(flat_scr, 0, m192, mixed.shape[1])
    put(m768, slice(None), dot_tn(normed2, hg))
    at += flat_store(flat_scr, at, m768, active.shape[1])
    put(mdown, slice(None), dot_tn(active[...], g_low))
    at += flat_store(flat_scr, at, mdown, mixed.shape[1])
    send_units(flat_scr, flat_out)


def gain_rows(one, two):
    return jnp.concatenate(
        [
            one[:, 0:128],
            jnp.concatenate([one[:, 128:192], two[:, 0:64]], axis=1),
            two[:, 64:192],
        ],
        axis=0,
    )


def fourth_kernel(
    x_in, qkv, probs, dmix, rg, gain_two, gains_late, qkv_w, gains,
    flat_out, bias_out, tokens_out,
    field, sums, m576, flat_scr, wide_scr, dx_scr,
):
    width = x_in.shape[-1]
    levels, lats, lons = tokens_out.shape[:3]
    attend_back(qkv, probs, dmix, field, sums, width)
    stand1, inv1 = standardize(x_in[...].astype(F32))
    normed = (stand1 * gains[0, 0:1, :]).astype(BF16)
    ng = dot_nt(field[...], qkv_w[0]).astype(BF16).astype(F32)
    part, gain_one = norm_back(ng, gains[0, 0:1, :], stand1, inv1)
    put(m576, slice(None), dot_tn(normed, field[...]))
    at = flat_store(flat_scr, 0, m576, field.shape[1])
    flat_scr[at:, :] = jnp.zeros((flat_scr.shape[0] - at, 128), F32)
    flat_scr[at : at + 3, :] = gain_rows(gain_one, gain_two[...])
    flat_scr[at + 3 : at + 6, :] = gain_rows(gains_late[0:1, :], gains_late[1:2, :])
    send_units(flat_scr, flat_out)
    fold_bias(sums, wide_scr, bias_out)
    put(dx_scr, slice(None), rg[...] + part)
    for z in range(levels):
        for a in range(lats):
            tokens_out[z, a] = get(
                dx_scr, pl.ds(z * lats + a, lons, stride=CHUNK), width
            ).astype(BF16)


def last_kernel(
    own_a, oth_a, own_b, oth_b, own_c, oth_c, spread, update_out, bias_out,
    scr, rows_scr, wide_scr,
):
    lat = lax.axis_index("lat")
    lons = own_a.shape[0]
    extra = -(-BIAS_UNITS // lons)

    def place(own, oth, dests):
        total = jnp.zeros((UNIT, 128), F32)
        per = oth.shape[1]
        k = 0
        for where, room in dests:
            for at in range(where, where + room * UNIT, UNIT):
                half, j, u = k // (per * lons), k // per % lons, k % per
                value = jnp.where(lat == half, own[j, u], oth[j, u]).astype(F32)
                scr[at : at + UNIT, :] = value
                total = total + value * value
                k += 1
        return total

    total = place(own_a, oth_a, [(864, 36), (2016, 12), (3456, 48), (5760, 48)])
    total = total + place(own_b, oth_b, [(1728, 12), (2304, 48), (4608, 48)])
    total = total + place(own_c, oth_c, [(0, 36), (6912, 1)])
    count = update_out.shape[0]
    mean = jnp.sum(total) * (1.0 / (count * 128))
    scale = lax.rsqrt(mean + 1e-06)
    update_out[...] = (scr[0:count, :] * scale).astype(BF16)

    for b, piece in enumerate((own_c, own_a)):
        base = piece.shape[1] - extra
        for k in range(BIAS_UNITS):
            tile, at = k % (WIDE // 128), k // (WIDE // 128) * UNIT
            value = piece[k // extra, base + k % extra]
            wide_scr[tile, at : at + UNIT, :] = value.astype(F32)
        low = get(wide_scr, slice(None), WIDE).astype(BF16)
        for zj in range(LEVELS):
            rows_scr[...] = dot_nt(low, spread[zj])
            for zi in range(LEVELS):
                for ai in range(WLAT):
                    at = ((zi * LEVELS + zj) * WLAT + ai) * PAIR
                    row = (zi * WLAT + ai) * 8
                    bias_out[b, 0, :, at : at + PAIR] = rows_scr[row : row + HEADS, 0:PAIR]


def call(kernel, outs, scratch, args, flops=0, moved=0):
    specs = []
    for arg in args:
        specs.append(pl.BlockSpec(memory_space=pltpu.VMEM))
    return pl.pallas_call(
        kernel,
        out_shape=[jax.ShapeDtypeStruct(shape, dtype) for shape, dtype in outs],
        in_specs=specs,
        out_specs=[pl.BlockSpec(memory_space=pltpu.VMEM)] * len(outs),
        scratch_shapes=[pltpu.VMEM(shape, dtype) for shape, dtype in scratch],
        compiler_params=pltpu.CompilerParams(vmem_limit_bytes=VMEM_LIMIT),
        cost_estimate=pl.CostEstimate(flops=flops, bytes_accessed=moved, transcendentals=0),
    )(*args)


def send(value, axes, pairs):
    return lax.ppermute(value, axes, pairs)


def lat_swap(value):
    return lax.ppermute(value, "lat", [(0, 1), (1, 0)])


def lon_send(value, step):
    count = lax.axis_size("lon")
    return lax.ppermute(value, "lon", [(s, (s + step) % count) for s in range(count)])


def diag_send(value, step):
    count = lax.axis_size("lon")
    pairs = []
    for s in range(count):
        for t in range(2):
            pairs.append((2 * s + t, 2 * ((s + step) % count) + 1 - t))
    return lax.ppermute(value, ("lon", "lat"), pairs)


def scatter_sum(flat, bias):
    lat = lax.axis_index("lat")
    mine = lax.dynamic_index_in_dim(flat, lat, 0, keepdims=False)
    theirs = lax.dynamic_index_in_dim(flat, 1 - lat, 0, keepdims=False)
    got = lat_swap(theirs)
    part = (mine.astype(F32) + got.astype(F32)).astype(BF16)
    if bias is not None:
        part = jnp.concatenate([part, bias], axis=1)
    pieces = lax.all_to_all(part, "lon", 0, 0)
    return jnp.sum(pieces.astype(F32), axis=0).astype(BF16)


def gather(piece, units):
    count = lax.axis_size("lon")
    whole = lax.all_to_all(jnp.broadcast_to(piece[None], (count,) + piece.shape), "lon", 0, 0)
    return whole, lat_swap(whole[:, :units])


def shards(
    tokens, cotangent, qkv_weight, proj_weight, up_weight, down_weight, norm_gain, bias_table
):
    levels, lats, lons, width = tokens.shape
    rows = levels * lats * lons
    wins = rows // WIN
    hid = up_weight.shape[-1]
    heads = bias_table.shape[2]
    lon_size = lax.axis_size("lon")
    lat_total = lats * lax.axis_size("lat")
    cut = CHUNK * (WLON // 2)
    spread = jnp.asarray(spread_matrices(), BF16)
    token = (rows, width)
    bias_scr = ((heads * WIN, WIN), F32)
    sums_shape = ((heads * WIN, WIDE), F32)
    rows_scr = ((LEVELS * CHUNK * 8, PAIR), F32)
    wide_scr = ((WIDE // 128, CHUNK * 8, 128), F32)
    tiles = -(-width // 128)
    token_scr = ((tiles, rows, 128), F32)
    m576 = ((-(-3 * width // 128), width, 128), F32)
    m192 = ((tiles, width, 128), F32)
    m768 = ((hid // 128, width, 128), F32)
    mdown = ((tiles, hid, 128), F32)
    field_shape = ((rows, 3 * width), BF16)

    cot_lon = lon_send(cotangent, -1)
    cot_lat = lat_swap(cotangent)
    cot_diag = diag_send(cotangent, -1)

    x0, tail, head, qkv0, mixed0, probs0, resid0, slope0, active0 = call(
        functools.partial(first_kernel, lat_total),
        [
            (token, BF16),
            ((rows - cut, width), BF16),
            ((cut, width), BF16),
            field_shape,
            (token, BF16),
            ((wins, heads, WIN, WIN), F32),
            (token, BF16),
            ((rows, hid), BF16),
            ((rows, hid), BF16),
        ],
        [token_scr, rows_scr, wide_scr, bias_scr],
        (tokens, bias_table[0:1], spread, qkv_weight, proj_weight, up_weight, down_weight, norm_gain),
        flops=10**9 * 6,
        moved=10**7,
    )
    lon_head = lon_send(head, -1)
    diag_head = diag_send(head, -1)
    lat_tail = lat_swap(tail)

    (
        dhead, dtail, n1, field1, mixed1, low1, n2, hg1, active1, g1, sums1, gains1,
    ) = call(
        functools.partial(second_kernel, lat_total),
        [
            ((rows - cut, width), BF16),
            ((cut, width), BF16),
            (token, BF16),
            field_shape,
            (token, BF16),
            (token, BF16),
            (token, BF16),
            ((rows, hid), BF16),
            ((rows, hid), BF16),
            (token, BF16),
            sums_shape,
            ((2, width), F32),
        ],
        [
            token_scr,
            (token, F32),
            (token, F32),
            rows_scr,
            wide_scr,
            bias_scr,
            field_shape,
            ((wins, heads, WIN, WIN), F32),
            (token, BF16),
        ],
        (
            tail, lon_head, lat_tail, diag_head, cotangent, cot_lon, cot_lat, cot_diag,
            bias_table[1:2], spread, qkv_weight, proj_weight, up_weight, down_weight, norm_gain,
        ),
        flops=10**9 * 10,
        moved=10**7,
    )
    lon_tail = lon_send(dtail, 1)
    diag_tail = diag_send(dtail, 1)
    lat_dhead = lat_swap(dhead)

    total_a = (qkv_weight[0].size + proj_weight[0].size + 2 * up_weight[0].size) // 128
    units_a, units_b, units_c = [-(-count // (2 * lon_size)) for count in (total_a // UNIT, 108, 37)]
    extra = -(-BIAS_UNITS // lon_size)
    flat_a, bias_a = call(
        outer_kernel,
        [((2, lon_size, units_a, UNIT, 128), BF16), ((lon_size, extra, UNIT, 128), BF16)],
        [
            m576,
            m192,
            m768,
            mdown,
            ((total_a, 128), F32),
            wide_scr,
        ],
        (n1, field1, mixed1, low1, n2, hg1, active1, g1, sums1),
        flops=10**9 * 6,
        moved=10**7,
    )

    flat_b, rg0, dmix0, gain_two = call(
        third_kernel,
        [
            ((2, lon_size, units_b, UNIT, 128), BF16),
            (token, F32),
            (token, BF16),
            ((1, width), F32),
        ],
        [
            (token, F32),
            (token, F32),
            m192,
            m768,
            mdown,
            ((108 * UNIT, 128), F32),
        ],
        (
            dhead, lon_tail, lat_dhead, diag_tail, resid0, slope0, active0, mixed0,
            proj_weight, up_weight, down_weight, norm_gain,
        ),
        flops=10**9 * 6,
        moved=10**7,
    )

    flat_c, bias_c, tokens_grad = call(
        fourth_kernel,
        [
            ((2, lon_size, units_c, UNIT, 128), BF16),
            ((lon_size, extra, UNIT, 128), BF16),
            (tokens.shape, BF16),
        ],
        [
            field_shape,
            sums_shape,
            m576,
            ((37 * UNIT, 128), F32),
            wide_scr,
            token_scr,
        ],
        (x0, qkv0, probs0, dmix0, rg0, gain_two, gains1, qkv_weight, norm_gain),
        flops=10**9 * 6,
        moved=10**7,
    )

    own_a, oth_a = gather(scatter_sum(flat_a, bias_a), units_a)
    own_b, oth_b = gather(scatter_sum(flat_b, None), units_b)
    own_c, oth_c = gather(scatter_sum(flat_c, bias_c), units_c)

    flat_rows = (
        2 * (qkv_weight[0].size + proj_weight[0].size + 2 * up_weight[0].size) + norm_gain.size
    ) // 128
    update, bias_grad = call(
        last_kernel,
        [((flat_rows, 128), BF16), (bias_table.shape, F32)],
        [((flat_rows + 18, 128), F32), ((CHUNK * 8, PAIR), F32), wide_scr],
        (own_a, oth_a, own_b, oth_b, own_c, oth_c, spread),
        flops=10**9,
        moved=10**7,
    )
    return (tokens_grad, update.reshape(-1), bias_grad)


def solution(mesh):
    return jax.shard_map(
        shards,
        mesh=mesh,
        in_specs=(
            P("grp", "lat", "lon", None),
            P("grp", "lat", "lon", None),
            P(),
            P(),
            P(),
            P(),
            P(),
            P(None, "lat", None, None),
        ),
        out_specs=(P("grp", "lat", "lon", None), P("grp"), P("grp", "lat", None, None)),
        check_vma=False,
    )
```

time: 564 us -> 196 us (0.35)
  local copies, waits for them, and re-layouts: 233 us -> 28.2 us
  waiting for transfers between devices: 180 us -> 72.6 us
  matrix products: 85.4 us -> 0 us
  Pallas kernels: 0 us -> 49.1 us
  starting transfers between devices: 8.46 us -> 39.2 us
  other arithmetic: 34.7 us -> 4.72 us
  between operations: 16.5 us -> 0.95 us
    psum x2 -> x0, waiting for transfers between devices: 169 us -> none  [the longest x1 108 us: shards(): total = lax.psum(flat, ('lon', 'lat'))]
    dot_general x37 -> x0, matrix products: 77.3 us -> none  [the longest x2 26.6 us: expand_bias(): spread = jnp.dot(grid, shift_table(), precision=lax.Precision.HIGHEST)]
    add x4 -> x0, local copies, waits for them, and re-layouts: 63 us -> none  [attend_windows(): jnp.einsum('rwihd,rwjhd->rwhij', split[:, :, :, 0], split[:, :, :, 1], pr...]
    all_to_all x0 -> x6, waiting for transfers between devices: none -> 61 us  [the longest x3 34.7 us: gather(): lax.all_to_all(jnp.broadcast_to(piece[None], (count,) + piece.shape), 'lo...]
    pallas_call x0 -> x6, Pallas kernels: none -> 49.1 us  [call(): pl.pallas_call(kernel, out_shape=[jax.ShapeDtypeStruct(shape, dtype) for...]
    transpose x14 -> x0, local copies, waits for them, and re-layouts: 40.1 us -> none  [the longest x2 32.8 us: fold_bias(): grid = grid.transpose(0, 1, 2, 5, 3, 6, 4, 7)]
    another operation x17 -> x0, local copies, waits for them, and re-layouts: 37.5 us -> none  [the longest x2 11.8 us: attend_back(): qkv_grad = jnp.stack([query_grad, key_grad, value_grad], axis=3)]
    reshape x7 -> x0, local copies, waits for them, and re-layouts: 30.9 us -> none  [the longest x2 26.5 us: fold_bias(): full_grad.reshape(row_count, head_count, levels, WLAT, WLON, levels, WLAT...]
  transfers between devices with their start and end apart: 10 -> 21, of which waited for: 6 -> 11; matrix products, arithmetic and copies ran while one was open for 19% -> 4% of each run, Pallas kernels for 0% -> 6%
where the time goes in v1:
time: 196 us; the launch traced here: 195 us
  waiting for transfers between devices  72.6 us (37%)
  Pallas kernels  49.1 us (25%)
  starting transfers between devices  39.2 us (20%)
  local copies, waits for them, and re-layouts  28.2 us (14%)
  other arithmetic  4.72 us (2%)
    pallas_call x6, Pallas kernels, call(): pl.pallas_call(kernel, out_shape=[jax.ShapeDtypeStruct(shape, dtype) for...  49.1 us
    all_to_all x3, waiting for transfers between devices, gather(): lax.all_to_all(jnp.broadcast_to(piece[None], (count,) + piece.shape), 'lo...  34.7 us
    all_to_all x3, waiting for transfers between devices, scatter_sum(): pieces = lax.all_to_all(part, 'lon', 0, 0)  26.3 us
    unnamed x84, local copies, waits for them, and re-layouts  23.2 us
    all_to_all x3, starting transfers between devices, scatter_sum(): pieces = lax.all_to_all(part, 'lon', 0, 0)  13.4 us
    all_to_all x3, starting transfers between devices, gather(): lax.all_to_all(jnp.broadcast_to(piece[None], (count,) + piece.shape), 'lo...  11 us
    ppermute x3, starting transfers between devices, lon_send(): lax.ppermute(value, 'lon', [(s, (s + step) % count) for s in range(count)])  8.88 us
    ppermute x3, waiting for transfers between devices, lon_send(): lax.ppermute(value, 'lon', [(s, (s + step) % count) for s in range(count)])  8.07 us
  transfers between devices with their start and end apart: 21, of which 11 were waited for; matrix products, arithmetic and copies ran while one was open for 4% of the time, Pallas kernels for 6%

profile of v1, /device:TPU:0, one launch (start us, length us, event | category | flops | bytes accessed | tf_op | source)
XLA Modules:
  0.0 194.8 jit_solution(2659991744494815541)
XLA Ops:
  0.7 6.0 %collective-permute-start.3 = (bf16[2,12,24,192]{3,2,1,0:T(8,128)(2,1)}, bf16[2,12,24,192]{3,2,1,0:T(8,128)(2,1)S(1)}, u32[]{:S(2)}, u32[]{:S(2)}) collective-permute-start(bf16[2,12,24,192]{3,2,1,0:T(8,128)(2,1)} %cot.1), channel_id=1, source_target_pairs={{0,14},{2,0},{4,2},{6,4},{8,6},{10,8},{12,10},{14,12},{1,15},{3,1}... | collective-permute-start | bytes 663560 | tf_op jit(solution)/shard_map/ppermute | solution.py:555
  7.4 1.7 fusion.3
  9.1 1.3 copy.13.down_w
  10.4 0.9 copy-done.8
  11.4 0.9 copy-done.12
  12.3 8.8 %shard_map.112 = (bf16[576,192]{1,0:T(8,128)(2,1)S(1)}, bf16[504,192]{1,0:T(8,128)(2,1)S(1)}, bf16[72,192]{1,0:T(8,128)(2,1)S(1)}, bf16[576,576]{1,0:T(8,128)(2,...) custom-call(bf16[2,12,24,192]{3,2,1,0:T(8,128)(2,1)S(1)} %copy-done., ...), custom_call_target="tpu_custom_call" | custom-call | flops 6000000000 | bytes 10000000 | tf_op jit(solution)/shard_map/pallas_call | solution.py:534
  21.2 0.9 copy-done.19
  22.8 1.4 collective-permute-start
  24.2 2.6 %collective-permute-done.lon_head = bf16[72,192]{1,0:T(8,128)(2,1)S(1)} collective-permute-done((bf16[72,192]{1,0:T(8,128)(2,1)S(1)}, bf16[72,192]{1,0:T(8,128)(2,1)S(1)}, u32[]{:S(2)}, u32[]{:S(2)}) %collective-permute-start) | collective-permute-done | bytes 27680 | tf_op jit(solution)/shard_map/ppermute | solution.py:555
  26.8 3.0 %collective-permute-start.2 = (bf16[72,192]{1,0:T(8,128)(2,1)S(1)}, bf16[72,192]{1,0:T(8,128)(2,1)S(1)}, u32[]{:S(2)}, u32[]{:S(2)}) collective-permute-start(bf16[72,192]{1,0:T(8,128)(2,1)S(1)} %get-tuple-element.39), channel_id=1, source_target_pairs={{0,15},{1,14},{2,1},{3,0},{4,3},{5,2},{6,5},{7,4},{8,7},{9,6},{10,... | collective-permute-start | bytes 82952 | tf_op jit(solution)/shard_map/ppermute | solution.py:564
  29.8 1.6 collective-permute-done.2.diag_head
  31.4 20.1 %shard_map.113 = (bf16[504,192]{1,0:T(8,128)(2,1)S(1)}, bf16[72,192]{1,0:T(8,128)(2,1)S(1)}, bf16[576,192]{1,0:T(8,128)(2,1)S(1)}, bf16[576,576]{1,0:T(8,128)(2,...) custom-call(bf16[504,192]{1,0:T(8,128)(2,1)S(1)} %get-tuple-element., ...), custom_call_target="tpu_custom_call" | custom-call | flops 10000000000 | bytes 10000000 | tf_op jit(solution)/shard_map/pallas_call | solution.py:534
  51.5 0.9 copy-done.21
  57.4 1.4 collective-permute-start.6
  58.9 5.5 %collective-permute-done.6.lon_tail = bf16[72,192]{1,0:T(8,128)(2,1)S(1)} collective-permute-done((bf16[72,192]{1,0:T(8,128)(2,1)S(1)}, bf16[72,192]{1,0:T(8,128)(2,1)S(1)}, u32[]{:S(2)}, u32[]{:S(2)}) %collective-permute-start.6) | collective-permute-done | bytes 27680 | tf_op jit(solution)/shard_map/ppermute | solution.py:555
  64.9 0.9 copy-done.7
  65.8 0.9 copy-done.10
  66.8 1.2 copy-done.17
  67.9 1.2 copy-done.18
  69.1 1.0 copy-done.36
  70.1 1.0 copy-done.38
  71.0 2.2 %shard_map.114 = (bf16[2,8,7,24,128]{4,3,2,1,0:T(8,128)(2,1)S(1)}, f32[576,192]{1,0:T(8,128)S(1)}, bf16[576,192]{1,0:T(8,128)(2,1)S(1)}, f32[1,192]{1,0:T(1,128)S(1)}) custom-call(bf16[504,192]{1,0:T(8,128)(2,1)S(1)} %copy-done.7, bf16[72,192]{1,0:T(8,128)(2,1)S(1)} %collective-permute-done.6.lon_tail, bf16[504,192]{1,0:T(8,128)(2,1)S(1)} %collective-permute-done.7.lat_head, ...), custom_call_target="tpu_custom_call" | custom-call | flops 6000000000 | bytes 10000000 | tf_op jit(solution)/shard_map/pallas_call | solution.py:534
  73.2 12.9 %shard_map.115 = (bf16[2,8,3,24,128]{4,3,2,1,0:T(8,128)(2,1)S(1)}, bf16[8,3,24,128]{3,2,1,0:T(8,128)(2,1)S(1)}, bf16[2,12,24,192]{3,2,1,0:T(8,128)(2,1)}) custom-call(bf16[576,192]{1,0:T(8,128)(2,1)S(1)} %copy-done.24, bf16[576,576]{1,0:T(8,128)(2,1)S(1)} %copy-done.20, f32[4,6,144,144]{3,2,1,0:T(8,128)} %get-tuple-element.37.probs, ...), custom_call_target="tpu_custom_call" | custom-call | flops 6000000000 | bytes 10000000 | tf_op jit(solution)/shard_map/pallas_call | solution.py:534
  88.4 4.1 %all-to-all-start.4 = ((bf16[8,6,24,128]{3,2,1,0:T(8,128)(2,1)}), bf16[8,6,24,128]{3,2,1,0:T(8,128)(2,1)}, u32[]{:S(2)}, u32[]{:S(2)}) async-start(bf16[8,6,24,128]{3,2,1,0:T(8,128)(2,1)} %pad_maximum_fusion.1), calls=%async_computation.4 | async-start | bytes 589824 | tf_op jit(solution)/shard_map/all_to_all | solution.py:575
  92.5 1.1 copy-done.22
  93.6 1.0 copy-done.26
  94.6 1.0 copy-done.28
  95.6 1.0 copy-done.30
  96.5 1.0 copy-done.32
  97.5 1.0 copy-done.34
  98.4 2.7 %shard_map.116 = (bf16[2,8,9,24,128]{4,3,2,1,0:T(8,128)(2,1)S(1)}, bf16[8,3,24,128]{3,2,1,0:T(8,128)(2,1)S(1)}) custom-call(bf16[576,192]{1,0:T(8,128)(2,1)S(1)} %copy-done.26, bf16[576,576]{1,0:T(8,128)(2,1)S(1)} %copy-done.22, bf16[576,192]{1,0:T(8,128)(2,1)S(1)} %copy-done.28, bf16[576,192]{1,0:T(8,128)(2,1)S(1)} %copy-done.30, ...), custom_call_target="tpu_custom_call" | custom-call | flops 6000000000 | bytes 10000000 | tf_op jit(solution)/shard_map/pallas_call | solution.py:534
  101.5 1.8 fusion.1
  103.3 5.7 %all-to-all-start.2 = ((bf16[8,7,24,128]{3,2,1,0:T(8,128)(2,1)}), bf16[8,7,24,128]{3,2,1,0:T(8,128)(2,1)S(1)}, u32[]{:S(2)}, u32[]{:S(2)}) async-start(bf16[8,7,24,128]{3,2,1,0:T(8,128)(2,1)} %fusion.1), calls=%async_computation.2 | async-start | bytes 688128 | tf_op jit(solution)/shard_map/all_to_all | solution.py:575
  109.2 0.9 pad_maximum_fusion
  110.0 10.3 %all-to-all-done.2 = bf16[8,7,24,128]{3,2,1,0:T(8,128)(2,1)S(1)} async-done(((bf16[8,7,24,128]{3,2,1,0:T(8,128)(2,1)}), bf16[8,7,24,128]{3,2,1,0:T(8,128)(2,1)S(1)}, u32[]{:S(2)}, u32[]{:S(2)}) %all-to-all-start.2) | async-done | bytes 344096 | tf_op jit(solution)/shard_map/all_to_all | solution.py:575
  120.3 3.6 %all-to-all-start = ((bf16[8,12,24,128]{3,2,1,0:T(8,128)(2,1)}), bf16[8,12,24,128]{3,2,1,0:T(8,128)(2,1)S(1)}, u32[]{:S(2)}, u32[]{:S(2)}) async-start(bf16[8,12,24,128]{3,2,1,0:T(8,128)(2,1)} %pad_maximum_fusion), calls=%async_computation | async-start | bytes 1179648 | tf_op jit(solution)/shard_map/all_to_all | solution.py:575
  124.0 16.0 %all-to-all-done = bf16[8,12,24,128]{3,2,1,0:T(8,128)(2,1)S(1)} async-done(((bf16[8,12,24,128]{3,2,1,0:T(8,128)(2,1)}), bf16[8,12,24,128]{3,2,1,0:T(8,128)(2,1)S(1)}, u32[]{:S(2)}, u32[]{:S(2)}) %all-to-all-start) | async-done | bytes 589856 | tf_op jit(solution)/shard_map/all_to_all | solution.py:575
  140.8 3.6 %all-to-all-start.3 = ((bf16[8,7,24,128]{3,2,1,0:T(8,128)(2,1)}), bf16[8,7,24,128]{3,2,1,0:T(8,128)(2,1)S(1)}, u32[]{:S(2)}, u32[]{:S(2)}) async-start(bf16[8,7,24,128]{3,2,1,0:T(8,128)(2,1)} %broadcast_in_dim.7), calls=%async_computation.3 | async-start | bytes 688128 | tf_op jit(solution)/shard_map/all_to_all | solution.py:581
  144.6 10.7 %all-to-all-done.3.own_b = bf16[8,7,24,128]{3,2,1,0:T(8,128)(2,1)S(1)} async-done(((bf16[8,7,24,128]{3,2,1,0:T(8,128)(2,1)}), bf16[8,7,24,128]{3,2,1,0:T(8,128)(2,1)S(1)}, u32[]{:S(2)}, u32[]{:S(2)}) %all-to-all-start.3) | async-done | bytes 344096 | tf_op jit(solution)/shard_map/all_to_all | solution.py:581
  155.3 0.9 broadcast_in_dim.6
  156.2 3.8 %all-to-all-start.1 = ((bf16[8,12,24,128]{3,2,1,0:T(8,128)(2,1)}), bf16[8,12,24,128]{3,2,1,0:T(8,128)(2,1)S(1)}, u32[]{:S(2)}, u32[]{:S(2)}) async-start(bf16[8,12,24,128]{3,2,1,0:T(8,128)(2,1)} %broadcast_in_dim.6), calls=%async_computation.1 | async-start | bytes 1179648 | tf_op jit(solution)/shard_map/all_to_all | solution.py:581
  159.9 1.0 reduce_sum.38
  160.9 14.8 %all-to-all-done.1.own_a = bf16[8,12,24,128]{3,2,1,0:T(8,128)(2,1)S(1)} async-done(((bf16[8,12,24,128]{3,2,1,0:T(8,128)(2,1)}), bf16[8,12,24,128]{3,2,1,0:T(8,128)(2,1)S(1)}, u32[]{:S(2)}, u32[]{:S(2)}) %all-to-all-start.1) | async-done | bytes 589856 | tf_op jit(solution)/shard_map/all_to_all | solution.py:581
  176.5 3.6 %all-to-all-start.5 = ((bf16[8,6,24,128]{3,2,1,0:T(8,128)(2,1)}), bf16[8,6,24,128]{3,2,1,0:T(8,128)(2,1)S(1)}, u32[]{:S(2)}, u32[]{:S(2)}) async-start(bf16[8,6,24,128]{3,2,1,0:T(8,128)(2,1)} %broadcast_in_dim.8), calls=%async_computation.5 | async-start | bytes 589824 | tf_op jit(solution)/shard_map/all_to_all | solution.py:581
  180.8 9.1 %all-to-all-done.5.own_c = bf16[8,6,24,128]{3,2,1,0:T(8,128)(2,1)S(1)} async-done(((bf16[8,6,24,128]{3,2,1,0:T(8,128)(2,1)}), bf16[8,6,24,128]{3,2,1,0:T(8,128)(2,1)S(1)}, u32[]{:S(2)}, u32[]{:S(2)}) %all-to-all-start.5) | async-done | bytes 294944 | tf_op jit(solution)/shard_map/all_to_all | solution.py:581
  190.0 1.4 collective-permute-done.14.oth_c
  191.4 2.4 %shard_map.117 = (bf16[6918,128]{1,0:T(8,128)(2,1)}, f32[2,1,6,6336]{3,2,1,0:T(8,128)S(1)}) custom-call(bf16[8,12,24,128]{3,2,1,0:T(8,128)(2,1)S(1)} %all-to-all-done.1.own_a, bf16[8,9,24,128]{3,2,1,0:T(8,128)(2,1)S(1)} %collective-permute-done.10.oth_a, bf16[8,7,24,128]{3,2,1,0:T(8,128)(2,1)S(1)} %all-to-all-done.3.own_b, ...), custom_call_target="tpu_custom_call" | custom-call | flops 1000000000 | bytes 10000000 | tf_op jit(solution)/shard_map/pallas_call | solution.py:534
  193.8 1.0 copy.17
  (101 shorter events, 12.1 us)
Async XLA Ops:
  0.6 9.8 %copy-start.4 = (bf16[2,12,24,192]{3,2,1,0:T(8,128)(2,1)S(1)}, bf16[2,12,24,192]{3,2,1,0:T(8,128)(2,1)}, u32[]{:S(2)}) copy-start(bf16[2,12,24,192]{3,2,1,0:T(8,128)(2,1)} %tokens.1) | copy-start | bytes 663556
  0.6 9.8 %copy-start.3 = (bf16[2,192,576]{2,1,0:T(8,128)(2,1)S(1)}, bf16[2,192,576]{2,1,0:T(8,128)(2,1)}, u32[]{:S(2)}) copy-start(bf16[2,192,576]{2,1,0:T(8,128)(2,1)} %qkv_w.5) | copy-start | bytes 1327108
  0.7 9.8 %copy-start.2 = (bf16[2,192,768]{2,1,0:T(8,128)(2,1)S(1)}, bf16[2,192,768]{2,1,0:T(8,128)(2,1)}, u32[]{:S(2)}) copy-start(bf16[2,192,768]{2,1,0:T(8,128)(2,1)} %up_w.5) | copy-start | bytes 1769476
  0.7 9.8 %copy-start.11 = (f32[2,2,192]{2,1,0:T(2,128)S(1)}, f32[2,2,192]{2,1,0:T(2,128)}, u32[]{:S(2)}) copy-start(f32[2,2,192]{2,1,0:T(2,128)} %gains.7) | copy-start | bytes 9220
  0.7 30.7 %collective-permute-start.3 = (bf16[2,12,24,192]{3,2,1,0:T(8,128)(2,1)}, bf16[2,12,24,192]{3,2,1,0:T(8,128)(2,1)S(1)}, u32[]{:S(2)}, u32[]{:S(2)}) collective-permute-start(bf16[2,12,24,192]{3,2,1,0:T(8,128)(2,1)} %cot.1), channel_id=1, source_target_pairs={{0,14},{2,0},{4,2},{6,4},{8,6},{10,8},{12,10},{14,12},{1,15},{3,1}... | collective-permute-start | bytes 663560 | tf_op jit(solution)/shard_map/ppermute | solution.py:555
  6.7 24.7 %collective-permute-start.4 = (bf16[2,12,24,192]{3,2,1,0:T(8,128)(2,1)}, bf16[2,12,24,192]{3,2,1,0:T(8,128)(2,1)S(1)}, u32[]{:S(2)}, u32[]{:S(2)}) collective-permute-start(bf16[2,12,24,192]{3,2,1,0:T(8,128)(2,1)} %cot.1), channel_id=1, source_target_pairs={{0,1},{1,0},{2,3},{3,2},{4,5},{5,4},{6,7},{7,6},{8,9},{9,8},{10,11... | collective-permute-start | bytes 663560 | tf_op jit(solution)/shard_map/ppermute | solution.py:550
  6.7 24.7 %collective-permute-start.5 = (bf16[2,12,24,192]{3,2,1,0:T(8,128)(2,1)}, bf16[2,12,24,192]{3,2,1,0:T(8,128)(2,1)S(1)}, u32[]{:S(2)}, u32[]{:S(2)}) collective-permute-start(bf16[2,12,24,192]{3,2,1,0:T(8,128)(2,1)} %cot.1), channel_id=1, source_target_pairs={{0,15},{1,14},{2,1},{3,0},{4,3},{5,2},{6,5},{7,4},{8,7},{9,6},{10,... | collective-permute-start | bytes 663560 | tf_op jit(solution)/shard_map/ppermute | solution.py:564
  12.3 8.9 %copy-start = (bf16[2,768,192]{2,1,0:T(8,128)(2,1)}, bf16[2,768,192]{2,1,0:T(8,128)(2,1)S(1)}, u32[]{:S(2)}) copy-start(bf16[2,768,192]{2,1,0:T(8,128)(2,1)S(1)} %copy.13.down_w) | copy-start | bytes 1769476
  12.3 17.5 %copy-start.39 = (f32[1,1,6,6336]{3,1,2,0:T(1,128)S(1)}, f32[1,1,6,6336]{3,1,2,0:T(1,128)}, u32[]{:S(2)}) copy-start(f32[1,1,6,6336]{3,1,2,0:T(1,128)} %get-tuple-element.70) | copy-start | bytes 456196
  12.3 19.1 %copy-start.5 = (bf16[2,12,24,192]{3,2,1,0:T(8,128)(2,1)S(1)}, bf16[2,12,24,192]{3,2,1,0:T(8,128)(2,1)}, u32[]{:S(2)}) copy-start(bf16[2,12,24,192]{3,2,1,0:T(8,128)(2,1)} %cot.1) | copy-start | bytes 663556
  12.3 19.1 %copy-start.9 = (bf16[2,192,192]{2,1,0:T(8,128)(2,1)S(1)}, bf16[2,192,192]{2,1,0:T(8,128)(2,1)}, u32[]{:S(2)}) copy-start(bf16[2,192,192]{2,1,0:T(8,128)(2,1)} %proj_w.5) | copy-start | bytes 442372
  22.7 28.8 %copy-start.16 = (bf16[576,768]{1,0:T(8,128)(2,1)}, bf16[576,768]{1,0:T(8,128)(2,1)S(1)}, u32[]{:S(2)}) copy-start(bf16[576,768]{1,0:T(8,128)(2,1)S(1)} %get-tuple-element.43.slope) | copy-start | bytes 2654212
  22.7 28.8 %copy-start.23 = (bf16[576,192]{1,0:T(8,128)(2,1)}, bf16[576,192]{1,0:T(8,128)(2,1)S(1)}, u32[]{:S(2)}) copy-start(bf16[576,192]{1,0:T(8,128)(2,1)S(1)} %get-tuple-element.35.x_in) | copy-start | bytes 663556
  22.7 28.8 %copy-start.37 = (bf16[576,192]{1,0:T(8,128)(2,1)}, bf16[576,192]{1,0:T(8,128)(2,1)S(1)}, u32[]{:S(2)}) copy-start(bf16[576,192]{1,0:T(8,128)(2,1)S(1)} %get-tuple-element.42.resid_in) | copy-start | bytes 663556
  22.7 8.6 %collective-permute-start.1 = (bf16[504,192]{1,0:T(8,128)(2,1)S(1)}, bf16[504,192]{1,0:T(8,128)(2,1)S(1)}, u32[]{:S(2)}, u32[]{:S(2)}) collective-permute-start(bf16[504,192]{1,0:T(8,128)(2,1)S(1)} %get-tuple-element.38.tail), channel_id=1, source_target_pairs={{0,1},{1,0},{2,3},{3,2},{4,5},{5,4},{6,7},{7,6},{8,9},{9,8},{10,11... | collective-permute-start | bytes 580616 | tf_op jit(solution)/shard_map/ppermute | solution.py:550
  22.8 4.0 %collective-permute-start = (bf16[72,192]{1,0:T(8,128)(2,1)S(1)}, bf16[72,192]{1,0:T(8,128)(2,1)S(1)}, u32[]{:S(2)}, u32[]{:S(2)}) collective-permute-start(bf16[72,192]{1,0:T(8,128)(2,1)S(1)} %get-tuple-element.39), channel_id=1, source_target_pairs={{0,14},{2,0},{4,2},{6,4},{8,6},{10,8},{12,10},{14,12},{1,15},{3,1}... | collective-permute-start | bytes 82952 | tf_op jit(solution)/shard_map/ppermute | solution.py:555
  26.8 4.6 %collective-permute-start.2 = (bf16[72,192]{1,0:T(8,128)(2,1)S(1)}, bf16[72,192]{1,0:T(8,128)(2,1)S(1)}, u32[]{:S(2)}, u32[]{:S(2)}) collective-permute-start(bf16[72,192]{1,0:T(8,128)(2,1)S(1)} %get-tuple-element.39), channel_id=1, source_target_pairs={{0,15},{1,14},{2,1},{3,0},{4,3},{5,2},{6,5},{7,4},{8,7},{9,6},{10,... | collective-permute-start | bytes 82952 | tf_op jit(solution)/shard_map/ppermute | solution.py:564
  29.8 35.1 %copy-start.1 = (bf16[2,768,192]{2,1,0:T(8,128)(2,1)S(1)}, bf16[2,768,192]{2,1,0:T(8,128)(2,1)}, u32[]{:S(2)}) copy-start(bf16[2,768,192]{2,1,0:T(8,128)(2,1)} %copy-done) | copy-start | bytes 1769476
  56.1 8.8 %collective-permute-start.7 = (bf16[504,192]{1,0:T(8,128)(2,1)S(1)}, bf16[504,192]{1,0:T(8,128)(2,1)S(1)}, u32[]{:S(2)}, u32[]{:S(2)}) collective-permute-start(bf16[504,192]{1,0:T(8,128)(2,1)S(1)} %get-tuple-element.40.head), channel_id=1, source_target_pairs={{0,1},{1,0},{2,3},{3,2},{4,5},{5,4},{6,7},{7,6},{8,9},{9,8},{10,11... | collective-permute-start | bytes 580616 | tf_op jit(solution)/shard_map/ppermute | solution.py:550
  57.4 7.1 %collective-permute-start.6 = (bf16[72,192]{1,0:T(8,128)(2,1)S(1)}, bf16[72,192]{1,0:T(8,128)(2,1)S(1)}, u32[]{:S(2)}, u32[]{:S(2)}) collective-permute-start(bf16[72,192]{1,0:T(8,128)(2,1)S(1)} %get-tuple-element.41), channel_id=1, source_target_pairs={{0,2},{2,4},{4,6},{6,8},{8,10},{10,12},{12,14},{14,0},{1,3},{3,5},... | collective-permute-start | bytes 82952 | tf_op jit(solution)/shard_map/ppermute | solution.py:555
  58.8 6.1 %collective-permute-start.8 = (bf16[72,192]{1,0:T(8,128)(2,1)S(1)}, bf16[72,192]{1,0:T(8,128)(2,1)S(1)}, u32[]{:S(2)}, u32[]{:S(2)}) collective-permute-start(bf16[72,192]{1,0:T(8,128)(2,1)S(1)} %get-tuple-element.41), channel_id=1, source_target_pairs={{0,3},{1,2},{2,5},{3,4},{4,7},{5,6},{6,9},{7,8},{8,11},{9,10},{10,... | collective-permute-start | bytes 82952 | tf_op jit(solution)/shard_map/ppermute | solution.py:564
  66.8 1.2 copy-start.17
  67.9 1.2 copy-start.18
  69.1 1.0 copy-start.36
  70.1 1.0 copy-start.38
  71.0 2.2 %copy-start.20 = (bf16[576,576]{1,0:T(8,128)(2,1)S(1)}, bf16[576,576]{1,0:T(8,128)(2,1)}, u32[]{:S(2)}) copy-start(bf16[576,576]{1,0:T(8,128)(2,1)} %copy-done.19) | copy-start | bytes 1990660
  71.0 2.2 %copy-start.24 = (bf16[576,192]{1,0:T(8,128)(2,1)S(1)}, bf16[576,192]{1,0:T(8,128)(2,1)}, u32[]{:S(2)}) copy-start(bf16[576,192]{1,0:T(8,128)(2,1)} %copy-done.23) | copy-start | bytes 663556
  86.2 6.3 %copy-start.14 = (bf16[576,768]{1,0:T(8,128)(2,1)S(1)}, bf16[576,768]{1,0:T(8,128)(2,1)}, u32[]{:S(2)}) copy-start(bf16[576,768]{1,0:T(8,128)(2,1)} %get-tuple-element.56.hg) | copy-start | bytes 2654212
  86.2 6.3 %copy-start.15 = (bf16[576,768]{1,0:T(8,128)(2,1)S(1)}, bf16[576,768]{1,0:T(8,128)(2,1)}, u32[]{:S(2)}) copy-start(bf16[576,768]{1,0:T(8,128)(2,1)} %get-tuple-element.57.active) | copy-start | bytes 2654212
  86.2 1.4 collective-permute-start.13
  87.3 14.3 %collective-permute-start.11 = (bf16[8,7,24,128]{3,2,1,0:T(8,128)(2,1)}, bf16[8,7,24,128]{3,2,1,0:T(8,128)(2,1)}, u32[]{:S(2)}, u32[]{:S(2)}) collective-permute-start(bf16[8,7,24,128]{3,2,1,0:T(8,128)(2,1)} %dynamic-slice_bitcast_fusion.1), channel_id=1, source_target_pairs={{0,1},{1,0},{2,3},{3,2},{4,5},{5,4},{6,7},{7,6},{8,9},{9,8},{10,11... | collective-permute-start | bytes 1032200 | tf_op jit(solution)/shard_map/ppermute | solution.py:550
  88.4 14.9 %all-to-all-start.4 = ((bf16[8,6,24,128]{3,2,1,0:T(8,128)(2,1)}), bf16[8,6,24,128]{3,2,1,0:T(8,128)(2,1)}, u32[]{:S(2)}, u32[]{:S(2)}) async-start(bf16[8,6,24,128]{3,2,1,0:T(8,128)(2,1)} %pad_maximum_fusion.1), calls=%async_computation.4 | async-start | bytes 589824 | tf_op jit(solution)/shard_map/all_to_all | solution.py:575
  92.5 1.1 copy-start.22
  93.6 1.0 copy-start.26
  94.6 1.0 copy-start.28
  95.6 1.0 copy-start.30
  96.5 1.0 copy-start.32
  97.5 1.0 copy-start.34
  101.2 7.8 %collective-permute-start.9 = (bf16[8,9,24,128]{3,2,1,0:T(8,128)(2,1)S(1)}, bf16[8,9,24,128]{3,2,1,0:T(8,128)(2,1)S(1)}, u32[]{:S(2)}, u32[]{:S(2)}) collective-permute-start(bf16[8,9,24,128]{3,2,1,0:T(8,128)(2,1)S(1)} %dynamic-slice_bitcast_fusion), channel_id=1, source_target_pairs={{0,1},{1,0},{2,3},{3,2},{4,5},{5,4},{6,7},{7,6},{8,9},{9,8},{10,11... | collective-permute-start | bytes 1327112 | tf_op jit(solution)/shard_map/ppermute | solution.py:550
  103.3 17.0 %all-to-all-start.2 = ((bf16[8,7,24,128]{3,2,1,0:T(8,128)(2,1)}), bf16[8,7,24,128]{3,2,1,0:T(8,128)(2,1)S(1)}, u32[]{:S(2)}, u32[]{:S(2)}) async-start(bf16[8,7,24,128]{3,2,1,0:T(8,128)(2,1)} %fusion.1), calls=%async_computation.2 | async-start | bytes 688128 | tf_op jit(solution)/shard_map/all_to_all | solution.py:575
  120.3 19.7 %all-to-all-start = ((bf16[8,12,24,128]{3,2,1,0:T(8,128)(2,1)}), bf16[8,12,24,128]{3,2,1,0:T(8,128)(2,1)S(1)}, u32[]{:S(2)}, u32[]{:S(2)}) async-start(bf16[8,12,24,128]{3,2,1,0:T(8,128)(2,1)} %pad_maximum_fusion), calls=%async_computation | async-start | bytes 1179648 | tf_op jit(solution)/shard_map/all_to_all | solution.py:575
  140.8 14.4 %all-to-all-start.3 = ((bf16[8,7,24,128]{3,2,1,0:T(8,128)(2,1)}), bf16[8,7,24,128]{3,2,1,0:T(8,128)(2,1)S(1)}, u32[]{:S(2)}, u32[]{:S(2)}) async-start(bf16[8,7,24,128]{3,2,1,0:T(8,128)(2,1)} %broadcast_in_dim.7), calls=%async_computation.3 | async-start | bytes 688128 | tf_op jit(solution)/shard_map/all_to_all | solution.py:581
  156.2 35.2 %copy-start.13 = (bf16[2,132,384]{2,1,0:T(8,128)(2,1)S(1)}, bf16[2,132,384]{2,1,0:T(8,128)(2,1)}, u32[]{:S(2)}) copy-start(bf16[2,132,384]{2,1,0:T(8,128)(2,1)} %constant.35.clone.spread) | copy-start | bytes 608260
  156.2 19.6 %all-to-all-start.1 = ((bf16[8,12,24,128]{3,2,1,0:T(8,128)(2,1)}), bf16[8,12,24,128]{3,2,1,0:T(8,128)(2,1)S(1)}, u32[]{:S(2)}, u32[]{:S(2)}) async-start(bf16[8,12,24,128]{3,2,1,0:T(8,128)(2,1)} %broadcast_in_dim.6), calls=%async_computation.1 | async-start | bytes 1179648 | tf_op jit(solution)/shard_map/all_to_all | solution.py:581
  176.5 13.4 %all-to-all-start.5 = ((bf16[8,6,24,128]{3,2,1,0:T(8,128)(2,1)}), bf16[8,6,24,128]{3,2,1,0:T(8,128)(2,1)S(1)}, u32[]{:S(2)}, u32[]{:S(2)}) async-start(bf16[8,6,24,128]{3,2,1,0:T(8,128)(2,1)} %broadcast_in_dim.8), calls=%async_computation.5 | async-start | bytes 589824 | tf_op jit(solution)/shard_map/all_to_all | solution.py:581
  180.2 11.2 %collective-permute-start.10 = (bf16[8,9,24,128]{3,2,1,0:T(8,128)(2,1)S(1)}, bf16[8,9,24,128]{3,2,1,0:T(8,128)(2,1)S(1)}, u32[]{:S(2)}, u32[]{:S(2)}) collective-permute-start(bf16[8,9,24,128]{3,2,1,0:T(8,128)(2,1)S(1)} %slice.16), channel_id=1, source_target_pairs={{0,1},{1,0},{2,3},{3,2},{4,5},{5,4},{6,7},{7,6},{8,9},{9,8},{10,11... | collective-permute-start | bytes 1327112 | tf_op jit(solution)/shard_map/ppermute | solution.py:550
  180.3 11.1 %collective-permute-start.12 = (bf16[8,7,24,128]{3,2,1,0:T(8,128)(2,1)S(1)}, bf16[8,7,24,128]{3,2,1,0:T(8,128)(2,1)S(1)}, u32[]{:S(2)}, u32[]{:S(2)}) collective-permute-start(bf16[8,7,24,128]{3,2,1,0:T(8,128)(2,1)S(1)} %all-to-all-done.3.own_b), channel_id=1, source_target_pairs={{0,1},{1,0},{2,3},{3,2},{4,5},{5,4},{6,7},{7,6},{8,9},{9,8},{10,11... | collective-permute-start | bytes 1032200 | tf_op jit(solution)/shard_map/ppermute | solution.py:550
  190.0 1.4 collective-permute-start.14
  (13 other events, 10.5 us)

commit v2 on v1

--- a/solution.py
+++ b/solution.py
@@ -26,9 +26,9 @@
 
 F32 = jnp.float32
 BF16 = jnp.bfloat16
-UNIT = 24
-BIAS_UNITS = CHUNK * 8 // UNIT * (WIDE // 128)
-VMEM_LIMIT = 48 * 1024 * 1024
+UNIT = 8
+BIAS_UNITS = (2 * HEADS + 1) * CHUNK // UNIT
+MIB = 1024 * 1024
 
 
 def dot(a, b):
@@ -114,13 +114,15 @@
     return row
 
 
-def expand_bias(table, spread, rows_scr, wide_scr, bias_scr, lat, shifted, lat_total):
+def expand_bias(table, spread, tab_scr, rows_scr, wide_scr, bias_scr, lat, shifted, lat_total):
+    for h in range(HEADS):
+        tab_scr[h : h + 1, :] = table[h]
     for zi in range(LEVELS):
         for zj in range(LEVELS):
             for ai in range(WLAT):
                 at = ((zi * LEVELS + zj) * WLAT + ai) * PAIR
                 row = zj * CHUNK * 8 + (zi * WLAT + ai) * 8
-                rows_scr[row : row + HEADS, 0:PAIR] = table[:, at : at + PAIR]
+                rows_scr[row : row + HEADS, 0:PAIR] = tab_scr[0:HEADS, at : at + PAIR]
     count = CHUNK * 8
     total = jnp.zeros((count, WIDE), F32)
     for zj in range(LEVELS):
@@ -145,8 +147,13 @@
             bias_scr[at : at + CHUNK, :] = jnp.where(allowed, moved[:, 0:WIN], NEGATIVE)
 
 
-def fold_bias(sums, wide_scr, out):
-    wide_scr[...] = jnp.zeros(wide_scr.shape, F32)
+def fold_bias(sums, put_unit):
+    rest = jnp.zeros((CHUNK, 128), F32)
+
+    def emit(at, value):
+        for r in range(CHUNK // UNIT):
+            put_unit(at * (CHUNK // UNIT) + r, value[r * UNIT : (r + 1) * UNIT, :].astype(BF16))
+
     for h in range(HEADS):
         total = jnp.zeros((CHUNK, WIDE), F32)
         for oi in range(WLON):
@@ -154,15 +161,11 @@
             at = h * WIN + oi * CHUNK
             part = sums[at : at + CHUNK, :]
             total = total + (part if back == 0 else pltpu.roll(part, back, axis=1))
-        put(wide_scr, pl.ds(h, CHUNK, stride=8), total)
-    count, per = out.shape[:2]
-    for k in range(count * per):
-        tile, at = k % (WIDE // 128), k // (WIDE // 128) * UNIT
-        if k < BIAS_UNITS:
-            out[k // per, k % per] = wide_scr[tile, at : at + UNIT, :].astype(BF16)
-        else:
-            out[k // per, k % per] = jnp.zeros((UNIT, 128), BF16)
-
+        emit(h, total[:, 0:128])
+        emit(HEADS + h, total[:, 128:256])
+        last = total[:, 256:384]
+        rest = rest + (last if h == 0 else pltpu.roll(last, 8 * h, axis=1))
+    emit(2 * HEADS, rest)
 
 def attend(qkv, bias, mixed, probs, width):
     masks = head_masks(width, BF16)
@@ -187,11 +190,10 @@
     lax.fori_loop(0, probs.shape[0], window, 0)
 
 
-def attend_back(qkv, probs, dmix, field, sums, width):
+def attend_back(qkv, probs, dmix, field, sums, width, first, last):
     masks = head_masks(width, BF16)
     masks32 = head_masks(width, F32)
     scale = (width // HEADS) ** -0.5
-    sums[...] = jnp.zeros(sums.shape, F32)
 
     def window(w, carry):
         rows = pl.ds(pl.multiple_of(w * WIN, 16), WIN)
@@ -217,7 +219,7 @@
         field[rows, 2 * width : 3 * width] = dv.astype(BF16)
         return carry
 
-    lax.fori_loop(0, probs.shape[0], window, 0)
+    lax.fori_loop(first, last, window, 0)
 
 
 def lon_major(src, scr):
@@ -255,18 +257,31 @@
     return rows * cols // 128
 
 
-def send_units(scr, out):
-    lats, lons, units = out.shape[:3]
-    at = 0
-    for i in range(lats):
-        for j in range(lons):
-            for u in range(units):
-                if at < scr.shape[0]:
-                    out[i, j, u] = scr[at : at + UNIT, :].astype(BF16)
-                else:
-                    out[i, j, u] = jnp.zeros((UNIT, 128), BF16)
-                at += UNIT
-
+def send_units(scr, base, out):
+    lons, units = out.shape[:2]
+    for j in range(lons):
+        for u in range(units):
+            at = base + (j * units + u) * UNIT
+            if not isinstance(at, int):
+                at = pl.multiple_of(at, UNIT)
+            out[j, u] = scr[pl.ds(at, UNIT), :].astype(BF16)
+
+
+def halves(scr, lat, keep, give):
+    half = keep.shape[0] * keep.shape[1] * UNIT
+    send_units(scr, lat * half, keep)
+    send_units(scr, (1 - lat) * half, give)
+
+
+def bias_units(sums, out):
+    lons, per = out.shape[:2]
+
+    def put_unit(k, value):
+        out[k // per, k % per] = value
+
+    fold_bias(sums, put_unit)
+    for k in range(BIAS_UNITS, lons * per):
+        put_unit(k, jnp.zeros((UNIT, 128), BF16))
 
 def forward_core(x, b, lat, lat_total, refs, qkv_scr, bias_scr, mixed, probs):
     qkv_w, proj_w, gains = refs
@@ -281,15 +296,20 @@
 
 
 def first_kernel(
-    lat_total, tokens, table, spread, qkv_w, proj_w, up_w, down_w, gains,
+    lat_total, tokens, cot, table, spread, qkv_w, proj_w, up_w, down_w, gains,
     x_out, tail_out, head_out, qkv_out, mixed_out, probs_out, resid_out, slope_out, active_out,
-    scr, rows_scr, wide_scr, bias_scr,
+    scr, cot_scr, tab_scr, rows_scr, wide_scr, bias_scr,
 ):
     lat = lax.axis_index("lat")
     width = tokens.shape[-1]
     lons = tokens.shape[2]
+    cut = CHUNK * (WLON // 2)
+    lon_major(cot, cot_scr)
+    g = jnp.concatenate([lon_column(cot_scr, lon, lons, width) for lon in range(lons)], axis=0)
+    head_out[1] = g[0:cut, :].astype(BF16)
+    tail_out[1] = g[cut:, :].astype(BF16)
     expand_bias(
-        table.at[0, 0], spread, rows_scr, wide_scr, bias_scr, lat, False, lat_total
+        table.at[0], spread, tab_scr, rows_scr, wide_scr, bias_scr, lat, False, lat_total
     )
     lon_major(tokens, scr)
     x = jnp.concatenate([lon_column(scr, lon, lons, width) for lon in range(lons)], axis=0)
@@ -304,10 +324,16 @@
     active = active.astype(BF16)
     active_out[...] = active
     slope_out[...] = slope.astype(BF16)
-    result = resid + dot(active, down_w[0])
-    cut = CHUNK * (WLON // 2)
-    head_out[...] = result[0:cut, :].astype(BF16)
-    tail_out[...] = result[cut:, :].astype(BF16)
+    result = resid + dot_nt(active, down_w[0])
+    head_out[0] = result[0:cut, :].astype(BF16)
+    tail_out[0] = result[cut:, :].astype(BF16)
+
+
+def bias_kernel(lat_total, table, spread, bias_out, tab_scr, rows_scr, wide_scr):
+    lat = lax.axis_index("lat")
+    expand_bias(
+        table.at[1], spread, tab_scr, rows_scr, wide_scr, bias_out, lat, True, lat_total
+    )
 
 
 def merge_ahead(scr_own, scr_oth, rows):
@@ -332,43 +358,32 @@
 
 def second_kernel(
     lat_total,
-    tail, lon_head, lat_tail, diag_head, cot, cot_lon, cot_lat, cot_diag,
-    table, spread, qkv_w, proj_w, up_w, down_w, gains,
+    tail, lon_head, lat_tail, diag_head, bias, qkv_w, proj_w, up_w, down_w, gains,
     head_out, tail_out, n1_out, field_out, mixed_out, low_out, n2_out, hg_out, active_out, g_out,
     sums_out, gain_out,
-    scr, scr_own, scr_oth, rows_scr, wide_scr, bias_scr, qkv_scr, probs_scr, dmix_scr,
+    scr_own, scr_oth, qkv_scr, probs_scr, dmix_scr,
 ):
     lat = lax.axis_index("lat")
     rows, width = scr_own.shape
-    lons = cot.shape[2]
     cut = CHUNK * (WLON // 2)
-    step = WLON // 2
-    expand_bias(table.at[0, 0], spread, rows_scr, wide_scr, bias_scr, lat, True, lat_total)
-
-    def columns(src, dst, first, last, at):
-        lon_major(src, scr)
-        for lon in range(first, last):
-            dst[at : at + CHUNK, :] = lon_column(scr, lon, lons, width)
-            at += CHUNK
-
-    columns(cot, scr_own, step, lons, 0)
-    columns(cot_lon, scr_own, 0, step, rows - cut)
-    columns(cot_lat, scr_oth, step, lons, 0)
-    columns(cot_diag, scr_oth, 0, step, rows - cut)
-    g = merge_ahead(scr_own, scr_oth, rows)
+
+    def rolled(which):
+        scr_own[0 : rows - cut, :] = tail[which].astype(F32)
+        scr_own[rows - cut :, :] = lon_head[which].astype(F32)
+        scr_oth[0 : rows - cut, :] = lat_tail[which].astype(F32)
+        scr_oth[rows - cut :, :] = diag_head[which].astype(F32)
+        return merge_ahead(scr_own, scr_oth, rows)
+
+    g = rolled(1)
     n = lax.broadcasted_iota(jnp.int32, (rows, 1), 0)
     keep = lat_row(n, lat, True, lat_total) < lat_total - PAD
     g = jnp.where(keep, g, 0.0)
     g_out[...] = g.astype(BF16)
 
-    scr_own[0 : rows - cut, :] = tail[...].astype(F32)
-    scr_own[rows - cut :, :] = lon_head[...].astype(F32)
-    scr_oth[0 : rows - cut, :] = lat_tail[...].astype(F32)
-    scr_oth[rows - cut :, :] = diag_head[...].astype(F32)
-    x = merge_ahead(scr_own, scr_oth, rows)
+    x = rolled(0)
 
     resid, normed = forward_core(
-        x, 1, lat, lat_total, (qkv_w, proj_w, gains), qkv_scr, bias_scr, mixed_out, probs_scr
+        x, 1, lat, lat_total, (qkv_w, proj_w, gains), qkv_scr, bias, mixed_out, probs_scr
     )
     n1_out[...] = normed
     stand2, inv2 = standardize(resid)
@@ -377,14 +392,17 @@
     active, slope = gelu_parts(dot(normed2, up_w[1]))
     active_out[...] = active.astype(BF16)
 
-    hg = (dot_nt(g_out[...], down_w[1]) * slope).astype(BF16)
+    hg = (dot(g_out[...], down_w[1]) * slope).astype(BF16)
     hg_out[...] = hg
     part, gain_two = norm_back(dot_nt(hg, up_w[1]), gains[1, 1:2, :], stand2, inv2)
     rg = g + part
     low = rg.astype(BF16)
     low_out[...] = low
     dmix_scr[...] = dot_nt(low, proj_w[1]).astype(BF16)
-    attend_back(qkv_scr, probs_scr, dmix_scr, field_out, sums_out, width)
+    sums_out[...] = jnp.zeros(sums_out.shape, F32)
+    attend_back(
+        qkv_scr, probs_scr, dmix_scr, field_out, sums_out, width, 0, probs_scr.shape[0]
+    )
     ng = dot_nt(field_out[...], qkv_w[1]).astype(BF16).astype(F32)
     stand1, inv1 = standardize(x)
     part, gain_one = norm_back(ng, gains[1, 0:1, :], stand1, inv1)
@@ -397,8 +415,8 @@
 
 def outer_kernel(
     n1, field, mixed, low, n2, hg, active, g, sums,
-    flat_out, bias_out,
-    m576, m192, m768, mdown, flat_scr, wide_scr,
+    keep, give, bias_out,
+    m576, m192, m768, mdown, flat_scr,
 ):
     put(m576, slice(None), dot_tn(n1[...], field[...]))
     at = flat_store(flat_scr, 0, m576, field.shape[1])
@@ -408,16 +426,56 @@
     at += flat_store(flat_scr, at, m768, active.shape[1])
     put(mdown, slice(None), dot_tn(active[...], g[...]))
     at += flat_store(flat_scr, at, mdown, mixed.shape[1])
-    send_units(flat_scr, flat_out)
-    fold_bias(sums, wide_scr, bias_out)
+    halves(flat_scr, lax.axis_index("lat"), keep, give)
+    bias_units(sums, bias_out)
+
+
+def split_x(x, keep, got, bias, keep_out, give_out):
+    units = keep.shape[1]
+    for z in range(keep_out.shape[0]):
+        for out, side in ((keep_out, x), (give_out, 1 - x)):
+            at = 2 * z + side
+            out[z, 0:units] = (keep[at].astype(F32) + got[at].astype(F32)).astype(BF16)
+            if bias is not None:
+                out[z, units:] = bias[at]
+
+
+def split_z(z, keep, got, own_out, *give_outs):
+    count = keep.shape[0]
+    for k, out in enumerate((own_out,) + give_outs):
+        at = lax.rem(z + k, count)
+        out[...] = (keep[at].astype(F32) + got[at].astype(F32)).astype(BF16)
+
+
+def sum_all(*refs):
+    total = refs[0][...].astype(F32)
+    for ref in refs[1:-1]:
+        total = total + ref[...].astype(F32)
+    refs[-1][...] = total.astype(BF16)
+
+
+def join_z(z, *refs):
+    count = len(refs) - 1
+    for k in range(count):
+        refs[-1][lax.rem(z + count - k, count)] = refs[k][...]
+
+
+def join_x(x, mine, other, whole_out, flat_out):
+    units = flat_out.shape[1]
+    for z in range(mine.shape[0]):
+        whole_out[2 * z + x] = mine[z]
+        whole_out[2 * z + 1 - x] = other[z]
+        flat_out[2 * z + x] = mine[z, 0:units]
+        flat_out[2 * z + 1 - x] = other[z, 0:units]
 
 
 def third_kernel(
     head, lon_tail, lat_head, diag_tail, resid_in, slope, active, mixed,
-    proj_w, up_w, down_w, gains,
-    flat_out, rg_out, dmix_out, gain_out,
+    proj_w, up_w, down_w, gains, keep_a, got_a, bias_a,
+    keep_out, give_out, rg_out, dmix_out, gain_out, keep_xa, give_xa,
     scr_own, scr_oth, m192, m768, mdown, flat_scr,
 ):
+    split_x(lax.rem(lax.axis_index("lon"), 2), keep_a, got_a, bias_a, keep_xa, give_xa)
     rows, width = scr_own.shape
     cut = CHUNK * (WLON // 2)
     scr_own[0:cut, :] = lon_tail[...].astype(F32)
@@ -426,7 +484,7 @@
     scr_oth[cut:, :] = lat_head[...].astype(F32)
     g = merge_behind(scr_own, scr_oth, rows)
     g_low = g.astype(BF16)
-    hg = (dot_nt(g_low, down_w[0]) * slope[...].astype(F32)).astype(BF16)
+    hg = (dot(g_low, down_w[0]) * slope[...].astype(F32)).astype(BF16)
     stand2, inv2 = standardize(resid_in[...].astype(F32))
     normed2 = (stand2 * gains[0, 1:2, :]).astype(BF16)
     part, gain_two = norm_back(dot_nt(hg, up_w[0]), gains[0, 1:2, :], stand2, inv2)
@@ -441,7 +499,8 @@
     at += flat_store(flat_scr, at, m768, active.shape[1])
     put(mdown, slice(None), dot_tn(active[...], g_low))
     at += flat_store(flat_scr, at, mdown, mixed.shape[1])
-    send_units(flat_scr, flat_out)
+    flat_scr[at:, :] = jnp.zeros((flat_scr.shape[0] - at, 128), F32)
+    halves(flat_scr, lax.axis_index("lat"), keep_out, give_out)
 
 
 def gain_rows(one, two):
@@ -455,14 +514,24 @@
     )
 
 
-def fourth_kernel(
-    x_in, qkv, probs, dmix, rg, gain_two, gains_late, qkv_w, gains,
-    flat_out, bias_out, tokens_out,
-    field, sums, m576, flat_scr, wide_scr, dx_scr,
+def fourth_kernel(qkv, probs, dmix, field_out, sums_out):
+    width = dmix.shape[-1]
+    sums_out[...] = jnp.zeros(sums_out.shape, F32)
+    attend_back(qkv, probs, dmix, field_out, sums_out, width, 0, probs.shape[0] // 2)
+
+
+def fifth_kernel(
+    x_in, qkv, probs, dmix, rg, gain_two, gains_late, field_in, sums_in, order, qkv_w, gains,
+    tokens_out, own_out, *rest,
 ):
+    field, sums, m576, flat_scr, dx_scr, bias_scr = rest[-6:]
+    rest = rest[:-6]
     width = x_in.shape[-1]
     levels, lats, lons = tokens_out.shape[:3]
-    attend_back(qkv, probs, dmix, field, sums, width)
+    done = probs.shape[0] // 2 * WIN
+    field[0:done, :] = field_in[...]
+    sums[...] = sums_in[...]
+    attend_back(qkv, probs, dmix, field, sums, width, probs.shape[0] // 2, probs.shape[0])
     stand1, inv1 = standardize(x_in[...].astype(F32))
     normed = (stand1 * gains[0, 0:1, :]).astype(BF16)
     ng = dot_nt(field[...], qkv_w[0]).astype(BF16).astype(F32)
@@ -472,8 +541,19 @@
     flat_scr[at:, :] = jnp.zeros((flat_scr.shape[0] - at, 128), F32)
     flat_scr[at : at + 3, :] = gain_rows(gain_one, gain_two[...])
     flat_scr[at + 3 : at + 6, :] = gain_rows(gains_late[0:1, :], gains_late[1:2, :])
-    send_units(flat_scr, flat_out)
-    fold_bias(sums, wide_scr, bias_out)
+    bias_units(sums, bias_scr)
+    lat, lon = lax.axis_index("lat"), lax.axis_index("lon")
+    count = (len(rest) + 1) // 2
+    extra = bias_scr.shape[1]
+    units = own_out.shape[0] - extra
+    for k in range(count):
+        to = lax.rem(lon + k, count)
+        same = own_out if k == 0 else rest[k - 1]
+        for out, side in ((same, lat), (rest[count - 1 + k], 1 - lat)):
+            base = (side * count + to) * (units * UNIT)
+            for u in range(units):
+                out[u] = flat_scr[pl.ds(pl.multiple_of(base + u * UNIT, UNIT), UNIT), :].astype(BF16)
+        same[units:] = bias_scr[to]
     put(dx_scr, slice(None), rg[...] + part)
     for z in range(levels):
         for a in range(lats):
@@ -482,12 +562,65 @@
             ).astype(BF16)
 
 
-def last_kernel(
-    own_a, oth_a, own_b, oth_b, own_c, oth_c, spread, update_out, bias_out,
-    scr, rows_scr, wide_scr,
-):
-    lat = lax.axis_index("lat")
+def sum_direct(*refs):
+    out = refs[-1]
+    fulls = [ref for ref in refs[:-1] if ref.shape == out.shape]
+    flats = [ref for ref in refs[:-1] if ref.shape != out.shape]
+    units = flats[0].shape[0]
+    total = fulls[0][...].astype(F32)
+    for ref in fulls[1:]:
+        total = total + ref[...].astype(F32)
+    part = total[0:units]
+    for ref in flats:
+        part = part + ref[...].astype(F32)
+    out[0:units] = part.astype(BF16)
+    out[units:] = total[units:].astype(BF16)
+
+
+def step_one(keep_xa, got_xa, keep_b, got_b, *outs):
+    lon = lax.axis_index("lon")
+    split_x(lax.rem(lon, 2), keep_b, got_b, None, outs[0], outs[1])
+    split_z(lax.div(lon, 2), keep_xa, got_xa, *outs[2:])
+
+
+def step_two(zs, *refs):
+    lon = lax.axis_index("lon")
+    a_in, keep_xb, got_xb = refs[:zs], refs[zs], refs[zs + 1]
+    outs = refs[zs + 2 :]
+    sum_all(*a_in, outs[0])
+    split_z(lax.div(lon, 2), keep_xb, got_xb, *outs[1:])
+
+
+def step_three(zs, fulls, *refs):
+    lon = lax.axis_index("lon")
+    c_in, a_in, b_in = refs[:fulls], refs[fulls : fulls + zs], refs[fulls + zs : fulls + 2 * zs]
+    c_out, a_out, b_out = refs[fulls + 2 * zs :]
+    sum_direct(*c_in, c_out)
+    join_z(lax.div(lon, 2), *a_in, a_out)
+    sum_all(*b_in, b_out)
+
+
+def step_four(zs, mine_a, other_a, *refs):
+    lon = lax.axis_index("lon")
+    b_in = refs[:zs]
+    whole_a, flat_a, join_b = refs[zs:]
+    join_x(lax.rem(lon, 2), mine_a, other_a, whole_a, flat_a)
+    join_z(lax.div(lon, 2), *b_in, join_b)
+
+
+def step_five(mine_b, other_b, whole_b, flat_b):
+    join_x(lax.rem(lax.axis_index("lon"), 2), mine_b, other_b, whole_b, flat_b)
+
+
+def last_kernel(spread, own_a, oth_a, own_b, oth_b, *refs):
+    update_out, bias_out, scr, rows_scr, wide_scr, c_own, c_oth = refs[-7:]
+    pieces = refs[:-7]
+    lat, lon = lax.axis_index("lat"), lax.axis_index("lon")
     lons = own_a.shape[0]
+    for k in range(lons):
+        at = lax.rem(lon + lons - k, lons)
+        c_own[at] = pieces[k][...]
+        c_oth[at] = pieces[lons + k][...]
     extra = -(-BIAS_UNITS // lons)
 
     def place(own, oth, dests):
@@ -495,28 +628,38 @@
         per = oth.shape[1]
         k = 0
         for where, room in dests:
-            for at in range(where, where + room * UNIT, UNIT):
+            for at in range(where, where + room, UNIT):
                 half, j, u = k // (per * lons), k // per % lons, k % per
-                value = jnp.where(lat == half, own[j, u], oth[j, u]).astype(F32)
+                value = jnp.where(lat == half, own[j, u].astype(F32), oth[j, u].astype(F32))
                 scr[at : at + UNIT, :] = value
                 total = total + value * value
                 k += 1
         return total
 
-    total = place(own_a, oth_a, [(864, 36), (2016, 12), (3456, 48), (5760, 48)])
-    total = total + place(own_b, oth_b, [(1728, 12), (2304, 48), (4608, 48)])
-    total = total + place(own_c, oth_c, [(0, 36), (6912, 1)])
+    total = place(own_a, oth_a, [(864, 864), (2016, 288), (3456, 1152), (5760, 1152)])
+    total = total + place(own_b, oth_b, [(1728, 288), (2304, 1152), (4608, 1152)])
+    total = total + place(c_own, c_oth, [(0, 864), (6912, 8)])
     count = update_out.shape[0]
     mean = jnp.sum(total) * (1.0 / (count * 128))
     scale = lax.rsqrt(mean + 1e-06)
     update_out[...] = (scr[0:count, :] * scale).astype(BF16)
 
-    for b, piece in enumerate((own_c, own_a)):
+    for b, piece in enumerate((c_own, own_a)):
         base = piece.shape[1] - extra
-        for k in range(BIAS_UNITS):
-            tile, at = k % (WIDE // 128), k // (WIDE // 128) * UNIT
-            value = piece[k // extra, base + k % extra]
-            wide_scr[tile, at : at + UNIT, :] = value.astype(F32)
+
+        def read(at):
+            parts = []
+            for r in range(CHUNK // UNIT):
+                k = at * (CHUNK // UNIT) + r
+                parts.append(piece[k // extra, base + k % extra].astype(F32))
+            return jnp.concatenate(parts, axis=0)
+
+        rest = read(2 * HEADS)
+        for h in range(HEADS):
+            rows = pl.ds(h, CHUNK, stride=8)
+            wide_scr[0, rows, :] = read(h)
+            wide_scr[1, rows, :] = read(HEADS + h)
+            wide_scr[2, rows, :] = rest if h == 0 else pltpu.roll(rest, 128 - 8 * h, axis=1)
         low = get(wide_scr, slice(None), WIDE).astype(BF16)
         for zj in range(LEVELS):
             rows_scr[...] = dot_nt(low, spread[zj])
@@ -527,23 +670,18 @@
                     bias_out[b, 0, :, at : at + PAIR] = rows_scr[row : row + HEADS, 0:PAIR]
 
 
-def call(kernel, outs, scratch, args, flops=0, moved=0):
-    specs = []
-    for arg in args:
-        specs.append(pl.BlockSpec(memory_space=pltpu.VMEM))
+def call(kernel, outs, scratch, args, micros, mib):
     return pl.pallas_call(
         kernel,
         out_shape=[jax.ShapeDtypeStruct(shape, dtype) for shape, dtype in outs],
-        in_specs=specs,
+        in_specs=[pl.BlockSpec(memory_space=pltpu.VMEM)] * len(args),
         out_specs=[pl.BlockSpec(memory_space=pltpu.VMEM)] * len(outs),
         scratch_shapes=[pltpu.VMEM(shape, dtype) for shape, dtype in scratch],
-        compiler_params=pltpu.CompilerParams(vmem_limit_bytes=VMEM_LIMIT),
-        cost_estimate=pl.CostEstimate(flops=flops, bytes_accessed=moved, transcendentals=0),
+        compiler_params=pltpu.CompilerParams(vmem_limit_bytes=mib * MIB),
+        cost_estimate=pl.CostEstimate(
+            flops=int(micros * 1.1e9), bytes_accessed=10**5, transcendentals=0
+        ),
     )(*args)
-
-
-def send(value, axes, pairs):
-    return lax.ppermute(value, axes, pairs)
 
 
 def lat_swap(value):
@@ -553,6 +691,11 @@
 def lon_send(value, step):
     count = lax.axis_size("lon")
     return lax.ppermute(value, "lon", [(s, (s + step) % count) for s in range(count)])
+
+
+def x_swap(value):
+    count = lax.axis_size("lon")
+    return lax.ppermute(value, "lon", [(s, s ^ 1) for s in range(count)])
 
 
 def diag_send(value, step):
@@ -562,24 +705,6 @@
         for t in range(2):
             pairs.append((2 * s + t, 2 * ((s + step) % count) + 1 - t))
     return lax.ppermute(value, ("lon", "lat"), pairs)
-
-
-def scatter_sum(flat, bias):
-    lat = lax.axis_index("lat")
-    mine = lax.dynamic_index_in_dim(flat, lat, 0, keepdims=False)
-    theirs = lax.dynamic_index_in_dim(flat, 1 - lat, 0, keepdims=False)
-    got = lat_swap(theirs)
-    part = (mine.astype(F32) + got.astype(F32)).astype(BF16)
-    if bias is not None:
-        part = jnp.concatenate([part, bias], axis=1)
-    pieces = lax.all_to_all(part, "lon", 0, 0)
-    return jnp.sum(pieces.astype(F32), axis=0).astype(BF16)
-
-
-def gather(piece, units):
-    count = lax.axis_size("lon")
-    whole = lax.all_to_all(jnp.broadcast_to(piece[None], (count,) + piece.shape), "lon", 0, 0)
-    return whole, lat_swap(whole[:, :units])
 
 
 def shards(
@@ -591,12 +716,18 @@
     hid = up_weight.shape[-1]
     heads = bias_table.shape[2]
     lon_size = lax.axis_size("lon")
+    zs = lon_size // 2
     lat_total = lats * lax.axis_size("lat")
     cut = CHUNK * (WLON // 2)
     spread = jnp.asarray(spread_matrices(), BF16)
+    down_turned = jnp.swapaxes(down_weight, 1, 2)
+    table = jnp.swapaxes(bias_table, 1, 2)
     token = (rows, width)
-    bias_scr = ((heads * WIN, WIN), F32)
+    field_shape = ((rows, 3 * width), BF16)
+    probs_shape = ((wins, heads, WIN, WIN), F32)
+    bias_shape = ((heads * WIN, WIN), F32)
     sums_shape = ((heads * WIN, WIDE), F32)
+    tab_scr = ((8, table.shape[-1]), F32)
     rows_scr = ((LEVELS * CHUNK * 8, PAIR), F32)
     wide_scr = ((WIDE // 128, CHUNK * 8, 128), F32)
     tiles = -(-width // 128)
@@ -605,33 +736,51 @@
     m192 = ((tiles, width, 128), F32)
     m768 = ((hid // 128, width, 128), F32)
     mdown = ((tiles, hid, 128), F32)
-    field_shape = ((rows, 3 * width), BF16)
-
-    cot_lon = lon_send(cotangent, -1)
-    cot_lat = lat_swap(cotangent)
-    cot_diag = diag_send(cotangent, -1)
+
+    block_rows = (qkv_weight[0].size + proj_weight[0].size + 2 * up_weight[0].size) // 128
+    qkv_rows = qkv_weight[0].size // 128
+    counts = (block_rows, block_rows - qkv_rows, qkv_rows + 8)
+    units_a, units_b, units_c = [-(-count // (2 * lon_size * UNIT)) for count in counts]
+    extra = -(-BIAS_UNITS // lon_size)
+
+    def units(*lead):
+        return (lead + (UNIT, 128), BF16)
+
+    def flat_scr(per):
+        return ((2 * lon_size * per * UNIT, 128), F32)
 
     x0, tail, head, qkv0, mixed0, probs0, resid0, slope0, active0 = call(
         functools.partial(first_kernel, lat_total),
         [
             (token, BF16),
-            ((rows - cut, width), BF16),
-            ((cut, width), BF16),
+            ((2, rows - cut, width), BF16),
+            ((2, cut, width), BF16),
             field_shape,
             (token, BF16),
-            ((wins, heads, WIN, WIN), F32),
+            probs_shape,
             (token, BF16),
             ((rows, hid), BF16),
             ((rows, hid), BF16),
         ],
-        [token_scr, rows_scr, wide_scr, bias_scr],
-        (tokens, bias_table[0:1], spread, qkv_weight, proj_weight, up_weight, down_weight, norm_gain),
-        flops=10**9 * 6,
-        moved=10**7,
+        [token_scr, token_scr, tab_scr, rows_scr, wide_scr, bias_shape],
+        (
+            tokens, cotangent, table, spread, qkv_weight, proj_weight, up_weight, down_turned,
+            norm_gain,
+        ),
+        9,
+        28,
     )
     lon_head = lon_send(head, -1)
     diag_head = diag_send(head, -1)
     lat_tail = lat_swap(tail)
+    (bias1,) = call(
+        functools.partial(bias_kernel, lat_total),
+        [bias_shape],
+        [tab_scr, rows_scr, wide_scr],
+        (table, spread),
+        2,
+        10,
+    )
 
     (
         dhead, dtail, n1, field1, mixed1, low1, n2, hg1, active1, g1, sums1, gains1,
@@ -651,105 +800,159 @@
             sums_shape,
             ((2, width), F32),
         ],
-        [
-            token_scr,
-            (token, F32),
-            (token, F32),
-            rows_scr,
-            wide_scr,
-            bias_scr,
-            field_shape,
-            ((wins, heads, WIN, WIN), F32),
-            (token, BF16),
-        ],
+        [(token, F32), (token, F32), field_shape, probs_shape, (token, BF16)],
         (
-            tail, lon_head, lat_tail, diag_head, cotangent, cot_lon, cot_lat, cot_diag,
-            bias_table[1:2], spread, qkv_weight, proj_weight, up_weight, down_weight, norm_gain,
+            tail, lon_head, lat_tail, diag_head, bias1, qkv_weight, proj_weight, up_weight,
+            down_turned, norm_gain,
         ),
-        flops=10**9 * 10,
-        moved=10**7,
+        19,
+        28,
     )
     lon_tail = lon_send(dtail, 1)
     diag_tail = diag_send(dtail, 1)
     lat_dhead = lat_swap(dhead)
 
-    total_a = (qkv_weight[0].size + proj_weight[0].size + 2 * up_weight[0].size) // 128
-    units_a, units_b, units_c = [-(-count // (2 * lon_size)) for count in (total_a // UNIT, 108, 37)]
-    extra = -(-BIAS_UNITS // lon_size)
-    flat_a, bias_a = call(
+    keep_a, give_a, bias_a = call(
         outer_kernel,
-        [((2, lon_size, units_a, UNIT, 128), BF16), ((lon_size, extra, UNIT, 128), BF16)],
-        [
-            m576,
-            m192,
-            m768,
-            mdown,
-            ((total_a, 128), F32),
-            wide_scr,
-        ],
+        [units(lon_size, units_a), units(lon_size, units_a), units(lon_size, extra)],
+        [m576, m192, m768, mdown, flat_scr(units_a)],
         (n1, field1, mixed1, low1, n2, hg1, active1, g1, sums1),
-        flops=10**9 * 6,
-        moved=10**7,
-    )
-
-    flat_b, rg0, dmix0, gain_two = call(
+        3,
+        20,
+    )
+    got_a = lat_swap(give_a)
+
+    keep_b, give_b, rg0, dmix0, gain_two, keep_xa, give_xa = call(
         third_kernel,
         [
-            ((2, lon_size, units_b, UNIT, 128), BF16),
+            units(lon_size, units_b),
+            units(lon_size, units_b),
             (token, F32),
             (token, BF16),
             ((1, width), F32),
+            units(zs, units_a + extra),
+            units(zs, units_a + extra),
         ],
-        [
-            (token, F32),
-            (token, F32),
-            m192,
-            m768,
-            mdown,
-            ((108 * UNIT, 128), F32),
-        ],
+        [(token, F32), (token, F32), m192, m768, mdown, flat_scr(units_b)],
         (
             dhead, lon_tail, lat_dhead, diag_tail, resid0, slope0, active0, mixed0,
-            proj_weight, up_weight, down_weight, norm_gain,
+            proj_weight, up_weight, down_turned, norm_gain, keep_a, got_a, bias_a,
         ),
-        flops=10**9 * 6,
-        moved=10**7,
-    )
-
-    flat_c, bias_c, tokens_grad = call(
+        3,
+        20,
+    )
+    got_b = lat_swap(give_b)
+    got_xa = x_swap(give_xa)
+
+    field0, sums0 = call(
         fourth_kernel,
-        [
-            ((2, lon_size, units_c, UNIT, 128), BF16),
-            ((lon_size, extra, UNIT, 128), BF16),
-            (tokens.shape, BF16),
-        ],
+        [((wins // 2 * WIN, 3 * width), BF16), sums_shape],
+        [],
+        (qkv0, probs0, dmix0),
+        6,
+        20,
+    )
+    stepped = call(
+        step_one,
+        [units(zs, units_b)] * 2 + [units(units_a + extra)] * zs,
+        [],
+        (keep_xa, got_xa, keep_b, got_b),
+        1,
+        10,
+    )
+    keep_xb, give_xb = stepped[:2]
+    own_a, gives_a = stepped[2], stepped[3:]
+    got_xb = x_swap(give_xb)
+    gots_a = [lon_send(give, 2 * (k + 1)) for k, give in enumerate(gives_a)]
+
+    fulls, flats = [units(units_c + extra)] * lon_size, [units(units_c)] * lon_size
+    finished = call(
+        fifth_kernel,
+        [(tokens.shape, BF16)] + fulls + flats,
         [
             field_shape,
             sums_shape,
             m576,
-            ((37 * UNIT, 128), F32),
-            wide_scr,
+            flat_scr(units_c),
             token_scr,
+            units(lon_size, extra),
         ],
-        (x0, qkv0, probs0, dmix0, rg0, gain_two, gains1, qkv_weight, norm_gain),
-        flops=10**9 * 6,
-        moved=10**7,
-    )
-
-    own_a, oth_a = gather(scatter_sum(flat_a, bias_a), units_a)
-    own_b, oth_b = gather(scatter_sum(flat_b, None), units_b)
-    own_c, oth_c = gather(scatter_sum(flat_c, bias_c), units_c)
-
-    flat_rows = (
-        2 * (qkv_weight[0].size + proj_weight[0].size + 2 * up_weight[0].size) + norm_gain.size
-    ) // 128
+        (
+            x0, qkv0, probs0, dmix0, rg0, gain_two, gains1, field0, sums0, own_a, qkv_weight,
+            norm_gain,
+        ),
+        7,
+        24,
+    )
+    tokens_grad = finished[0]
+    same, cross = finished[1 : 1 + lon_size], finished[1 + lon_size :]
+
+    def spread_direct(same, cross):
+        fulls = [same[0]] + [lon_send(same[k], k) for k in range(1, lon_size)]
+        flats = [lat_swap(cross[0])] + [diag_send(cross[k], k) for k in range(1, lon_size)]
+        return fulls + flats
+
+    gots_c = spread_direct(same, cross)
+
+    stepped = call(
+        functools.partial(step_two, zs),
+        [units(units_a + extra)] + [units(units_b)] * zs,
+        [],
+        (own_a, *gots_a, keep_xb, got_xb),
+        1,
+        10,
+    )
+    sum_a, own_b, gives_b = stepped[0], stepped[1], stepped[2:]
+    gots_b = [lon_send(give, 2 * (k + 1)) for k, give in enumerate(gives_b)]
+    all_a = [sum_a] + [lon_send(sum_a, 2 * k) for k in range(1, zs)]
+
+    sum_c, join_a, sum_b = call(
+        functools.partial(step_three, zs, 2 * lon_size),
+        [units(units_c + extra), units(zs, units_a + extra), units(units_b)],
+        [],
+        (*gots_c, *all_a, own_b, *gots_b),
+        1,
+        10,
+    )
+    flat_c = sum_c[:units_c]
+    pieces_c = spread_direct([sum_c] * lon_size, [flat_c] * lon_size)
+    all_b = [sum_b] + [lon_send(sum_b, 2 * k) for k in range(1, zs)]
+    other_a = x_swap(join_a)
+
+    whole_a, flat_a, join_b = call(
+        functools.partial(step_four, zs),
+        [units(lon_size, units_a + extra), units(lon_size, units_a), units(zs, units_b)],
+        [],
+        (join_a, other_a, *all_b),
+        1,
+        10,
+    )
+    oth_a = lat_swap(flat_a)
+    other_b = x_swap(join_b)
+    whole_b, flat_b = call(
+        step_five,
+        [units(lon_size, units_b), units(lon_size, units_b)],
+        [],
+        (join_b, other_b),
+        1,
+        10,
+    )
+    oth_b = lat_swap(flat_b)
+
+    flat_rows = (2 * block_rows * 128 + norm_gain.size) // 128
     update, bias_grad = call(
         last_kernel,
         [((flat_rows, 128), BF16), (bias_table.shape, F32)],
-        [((flat_rows + 18, 128), F32), ((CHUNK * 8, PAIR), F32), wide_scr],
-        (own_a, oth_a, own_b, oth_b, own_c, oth_c, spread),
-        flops=10**9,
-        moved=10**7,
+        [
+            ((flat_rows + 2, 128), F32),
+            ((CHUNK * 8, PAIR), F32),
+            wide_scr,
+            units(lon_size, units_c + extra),
+            units(lon_size, units_c),
+        ],
+        (spread, whole_a, oth_a, whole_b, oth_b, *pieces_c),
+        3,
+        20,
     )
     return (tokens_grad, update.reshape(-1), bias_grad)
 

time: 196 us -> 169 us (0.86)
  starting transfers between devices: 39.2 us -> 63 us
  waiting for transfers between devices: 72.6 us -> 52.1 us
  local copies, waits for them, and re-layouts: 28.2 us -> 9.65 us
  Pallas kernels: 49.1 us -> 43.3 us
  other arithmetic: 4.72 us -> 0 us
    all_to_all x6 -> x0, waiting for transfers between devices: 61 us -> none  [the longest x3 34.7 us: gather(): lax.all_to_all(jnp.broadcast_to(piece[None], (count,) + piece.shape), 'lo...]
    ppermute x3 -> x28, starting transfers between devices: 8.88 us -> 36.9 us  [lon_send(): lax.ppermute(value, 'lon', [(s, (s + step) % count) for s in range(count)])]
    all_to_all x6 -> x0, starting transfers between devices: 24.4 us -> none  [the longest x3 13.4 us: scatter_sum(): pieces = lax.all_to_all(part, 'lon', 0, 0)]
    ppermute x3 -> x16, starting transfers between devices: 3.77 us -> 23.3 us  [diag_send(): return lax.ppermute(value, ('lon', 'lat'), pairs)]
    ppermute x3 -> x28, waiting for transfers between devices: 8.07 us -> 25.1 us  [lon_send(): lax.ppermute(value, 'lon', [(s, (s + step) % count) for s in range(count)])]
    ppermute x3 -> x16, waiting for transfers between devices: 2.04 us -> 18.3 us  [diag_send(): return lax.ppermute(value, ('lon', 'lat'), pairs)]
    unnamed x84 -> x33, local copies, waits for them, and re-layouts: 23.2 us -> 9.65 us
    ppermute x0 -> x4, waiting for transfers between devices: none -> 8.73 us  [x_swap(): return lax.ppermute(value, 'lon', [(s, s ^ 1) for s in range(count)])]
  transfers between devices with their start and end apart: 21 -> 56, of which waited for: 11 -> 24; matrix products, arithmetic and copies ran while one was open for 4% -> 0% of each run, Pallas kernels for 6% -> 7%
where the time goes in v2:
time: 169 us
  starting transfers between devices  63 us (37%)
  waiting for transfers between devices  52.1 us (31%)
  Pallas kernels  43.3 us (26%)
  local copies, waits for them, and re-layouts  9.65 us (6%)
    pallas_call x13, Pallas kernels, call(): pl.pallas_call(kernel, out_shape=[jax.ShapeDtypeStruct(shape, dtype) for...  43.3 us
    ppermute x28, starting transfers between devices, lon_send(): lax.ppermute(value, 'lon', [(s, (s + step) % count) for s in range(count)])  36.9 us
    ppermute x28, waiting for transfers between devices, lon_send(): lax.ppermute(value, 'lon', [(s, (s + step) % count) for s in range(count)])  25.1 us
    ppermute x16, starting transfers between devices, diag_send(): return lax.ppermute(value, ('lon', 'lat'), pairs)  23.3 us
    ppermute x16, waiting for transfers between devices, diag_send(): return lax.ppermute(value, ('lon', 'lat'), pairs)  18.3 us
    unnamed x33, local copies, waits for them, and re-layouts  9.65 us
    ppermute x4, waiting for transfers between devices, x_swap(): return lax.ppermute(value, 'lon', [(s, s ^ 1) for s in range(count)])  8.73 us
  transfers between devices with their start and end apart: 56, of which 24 were waited for; matrix products, arithmetic and copies ran while one was open for 0% of the time, Pallas kernels for 7%

profile of v2, /device:TPU:0, one launch (start us, length us, event | category | flops | bytes accessed | tf_op | source)
XLA Modules:
  0.0 169.0 jit_solution(10324655255251191112)
XLA Ops:
  0.6 1.1 copy-done
  1.7 1.1 copy-done.2
  9.2 7.1 %shard_map.112 = (bf16[576,192]{1,0:T(8,128)(2,1)S(1)}, bf16[2,504,192]{2,1,0:T(8,128)(2,1)S(1)}, bf16[2,72,192]{2,1,0:T(8,128)(2,1)S(1)}, bf16[576,576]{1,0:T(8...) custom-call(bf16[2,12,24,192]{3,2,1,0:T(8,128)(2,1)S(1)} %copy-done., ...), custom_call_target="tpu_custom_call" | custom-call | flops 9900000256 | bytes 100000 | tf_op jit(solution)/shard_map/pallas_call | solution.py:674
  16.9 5.7 %collective-permute-start.2 = (bf16[2,72,192]{2,1,0:T(8,128)(2,1)S(1)}, bf16[2,72,192]{2,1,0:T(8,128)(2,1)S(1)}, u32[]{:S(2)}, u32[]{:S(2)}) collective-permute-start(bf16[2,72,192]{2,1,0:T(8,128)(2,1)S(1)} %get-tuple-element.78), channel_id=1, source_target_pairs={{0,15},{1,14},{2,1},{3,0},{4,3},{5,2},{6,5},{7,4},{8,7},{9,6},{10,... | collective-permute-start | bytes 165896 | tf_op jit(solution)/shard_map/ppermute | solution.py:707
  24.0 1.1 collective-permute-done.2.diag_head
  25.2 1.7 %collective-permute-done.lon_head = bf16[2,72,192]{2,1,0:T(8,128)(2,1)S(1)} collective-permute-done((bf16[2,72,192]{2,1,0:T(8,128)(2,1)S(1)}, bf16[2,72,192]{2,1,0:T(8,128)(2,1)S(1)}, u32[]{:S(2)}, u32[]{:S(2)}) %collective-permute-start) | collective-permute-done | bytes 55328 | tf_op jit(solution)/shard_map/ppermute | solution.py:693
  27.0 17.1 %shard_map.114 = (bf16[504,192]{1,0:T(8,128)(2,1)S(1)}, bf16[72,192]{1,0:T(8,128)(2,1)S(1)}, bf16[576,192]{1,0:T(8,128)(2,1)S(1)}, bf16[576,576]{1,0:T(8,128)(2,...) custom-call(bf16[2,504,192]{2,1,0:T(8,128)(2,1)S(1)} %get-tuple-elem, ...), custom_call_target="tpu_custom_call" | custom-call | flops 20899999744 | bytes 100000 | tf_op jit(solution)/shard_map/pallas_call | solution.py:674
  44.0 1.6 shard_map.115
  46.3 6.2 %collective-permute-done.5.diag_tail = bf16[72,192]{1,0:T(8,128)(2,1)S(1)} collective-permute-done((bf16[72,192]{1,0:T(8,128)(2,1)S(1)}, bf16[72,192]{1,0:T(8,128)(2,1)S(1)}, u32[]{:S(2)}, u32[]{:S(2)}) %collective-permute-start.5) | collective-permute-done | bytes 27680 | tf_op jit(solution)/shard_map/ppermute | solution.py:707
  52.4 1.1 collective-permute-done.3.lon_tail
  53.5 2.2 %shard_map.116 = (bf16[8,21,8,128]{3,2,1,0:T(8,128)(2,1)S(1)}, bf16[8,21,8,128]{3,2,1,0:T(8,128)(2,1)S(1)}, f32[576,192]{1,0:T(8,128)S(1)}, bf16[576,192]{1,0:T(...) custom-call(bf16[504,192]{1,0:T(8,128)(2,1)S(1)} %get-tuple-element., ...), custom_call_target="tpu_custom_call" | custom-call | flops 3300000000 | bytes 100000 | tf_op jit(solution)/shard_map/pallas_call | solution.py:674
  55.8 4.5 %shard_map.117 = (bf16[288,576]{1,0:T(8,128)(2,1)S(1)}, f32[864,384]{1,0:T(8,128)S(1)}) custom-call(bf16[576,576]{1,0:T(8,128)(2,1)S(1)} %get-tuple-element.75.qkv, f32[4,6,144,144]{3,2,1,0:T(8,128)S(1)} %get-tuple-element.76.probs, bf16[576,192]{1,0:T(8,128)(2,1)S(1)} %get-tuple-element.97.dmix), custom_call_target="tpu_custom_call" | custom-call | flops 6600000000 | bytes 100000 | tf_op jit(solution)/shard_map/pallas_call | solution.py:674
  60.4 3.4 %collective-permute-done.7.got_xa = bf16[4,32,8,128]{3,2,1,0:T(8,128)(2,1)S(1)} collective-permute-done((bf16[4,32,8,128]{3,2,1,0:T(8,128)(2,1)S(1)}, bf16[4,32,8,128]{3,2,1,0:T(8,128)(2,1)S(1)}, u32[]{:S(2)}, u32[]{:S(2)}) %collective-permute-start.7) | collective-permute-done | bytes 262176 | tf_op jit(solution)/shard_map/ppermute | solution.py:698
  64.3 6.6 %shard_map.119 = (bf16[2,12,24,192]{3,2,1,0:T(8,128)(2,1)}, bf16[12,8,128]{2,1,0:T(8,128)(2,1)S(1)}, bf16[12,8,128]{2,1,0:T(8,128)(2,1)S(1)}, bf16[12,8,128]{2,1...) custom-call(bf16[576,192]{1,0:T(8,128)(2,1)S(1)} %get-tuple-element., ...), custom_call_target="tpu_custom_call" | custom-call | flops 7699999744 | bytes 100000 | tf_op jit(solution)/shard_map/pallas_call | solution.py:674
  70.9 1.9 %collective-permute-start.17 = (bf16[7,8,128]{2,1,0:T(8,128)(2,1)S(1)}, bf16[7,8,128]{2,1,0:T(8,128)(2,1)S(1)}, u32[]{:S(2)}, u32[]{:S(2)}) collective-permute-start(bf16[7,8,128]{2,1,0:T(8,128)(2,1)S(1)} %get-tuple-element.118), channel_id=1, source_target_pairs={{0,3},{1,2},{2,5},{3,4},{4,7},{5,6},{6,9},{7,8},{8,11},{9,10},{10,... | collective-permute-start | bytes 43016 | tf_op jit(solution)/shard_map/ppermute | solution.py:707
  72.8 2.0 %collective-permute-start.19 = (bf16[7,8,128]{2,1,0:T(8,128)(2,1)S(1)}, bf16[7,8,128]{2,1,0:T(8,128)(2,1)S(1)}, u32[]{:S(2)}, u32[]{:S(2)}) collective-permute-start(bf16[7,8,128]{2,1,0:T(8,128)(2,1)S(1)} %get-tuple-element.120), channel_id=1, source_target_pairs={{0,7},{1,6},{2,9},{3,8},{4,11},{5,10},{6,13},{7,12},{8,15},{9,14},... | collective-permute-start | bytes 43016 | tf_op jit(solution)/shard_map/ppermute | solution.py:707
  74.8 1.5 collective-permute-start.20
  76.8 1.6 collective-permute-start.21
  78.4 2.1 %collective-permute-start.24 = (bf16[32,8,128]{2,1,0:T(8,128)(2,1)S(1)}, bf16[32,8,128]{2,1,0:T(8,128)(2,1)S(1)}, u32[]{:S(2)}, u32[]{:S(2)}) collective-permute-start(bf16[32,8,128]{2,1,0:T(8,128)(2,1)S(1)} %get-tuple-element.125), channel_id=1, source_target_pairs={{0,4},{2,6},{4,8},{6,10},{8,12},{10,14},{12,0},{14,2},{1,5},{3,7},... | collective-permute-start | bytes 196616 | tf_op jit(solution)/shard_map/ppermute | solution.py:693
  80.5 2.4 %collective-permute-start.26 = (bf16[32,8,128]{2,1,0:T(8,128)(2,1)S(1)}, bf16[32,8,128]{2,1,0:T(8,128)(2,1)S(1)}, u32[]{:S(2)}, u32[]{:S(2)}) collective-permute-start(bf16[32,8,128]{2,1,0:T(8,128)(2,1)S(1)} %get-tuple-element.127), channel_id=1, source_target_pairs={{0,12},{2,14},{4,0},{6,2},{8,4},{10,6},{12,8},{14,10},{1,13},{3,15... | collective-permute-start | bytes 196616 | tf_op jit(solution)/shard_map/ppermute | solution.py:693
  82.9 1.8 %collective-permute-start.22 = (bf16[7,8,128]{2,1,0:T(8,128)(2,1)S(1)}, bf16[7,8,128]{2,1,0:T(8,128)(2,1)S(1)}, u32[]{:S(2)}, u32[]{:S(2)}) collective-permute-start(bf16[7,8,128]{2,1,0:T(8,128)(2,1)S(1)} %get-tuple-element.123), channel_id=1, source_target_pairs={{0,13},{1,12},{2,15},{3,14},{4,1},{5,0},{6,3},{7,2},{8,5},{9,4},{1... | collective-permute-start | bytes 43016 | tf_op jit(solution)/shard_map/ppermute | solution.py:707
  84.7 2.5 %collective-permute-done.22.refs_14_ = bf16[7,8,128]{2,1,0:T(8,128)(2,1)S(1)} collective-permute-done((bf16[7,8,128]{2,1,0:T(8,128)(2,1)S(1)}, bf16[7,8,128]{2,1,0:T(8,128)(2,1)S(1)}, u32[]{:S(2)}, u32[]{:S(2)}) %collective-permute-start.22) | collective-permute-done | bytes 14368 | tf_op jit(solution)/shard_map/ppermute | solution.py:707
  87.2 2.8 %collective-permute-start.23 = (bf16[7,8,128]{2,1,0:T(8,128)(2,1)S(1)}, bf16[7,8,128]{2,1,0:T(8,128)(2,1)S(1)}, u32[]{:S(2)}, u32[]{:S(2)}) collective-permute-start(bf16[7,8,128]{2,1,0:T(8,128)(2,1)S(1)} %get-tuple-element.124), channel_id=1, source_target_pairs={{0,15},{1,14},{2,1},{3,0},{4,3},{5,2},{6,5},{7,4},{8,7},{9,6},{10,... | collective-permute-start | bytes 43016 | tf_op jit(solution)/shard_map/ppermute | solution.py:707
  89.9 1.4 collective-permute-done.23.refs_15_
  91.7 6.2 %collective-permute-done.9.refs_1_ = bf16[12,8,128]{2,1,0:T(8,128)(2,1)S(1)} collective-permute-done((bf16[12,8,128]{2,1,0:T(8,128)(2,1)S(1)}, bf16[12,8,128]{2,1,0:T(8,128)(2,1)S(1)}, u32[]{:S(2)}, u32[]{:S(2)}) %collective-permute-start.9) | collective-permute-done | bytes 24608 | tf_op jit(solution)/shard_map/ppermute | solution.py:693
  97.9 2.1 %collective-permute-start.12 = (bf16[12,8,128]{2,1,0:T(8,128)(2,1)S(1)}, bf16[12,8,128]{2,1,0:T(8,128)(2,1)S(1)}, u32[]{:S(2)}, u32[]{:S(2)}) collective-permute-start(bf16[12,8,128]{2,1,0:T(8,128)(2,1)S(1)} %get-tuple-element.113), channel_id=1, source_target_pairs={{0,8},{2,10},{4,12},{6,14},{8,0},{10,2},{12,4},{14,6},{1,9},{3,11}... | collective-permute-start | bytes 73736 | tf_op jit(solution)/shard_map/ppermute | solution.py:693
  100.1 2.1 %collective-permute-start.13 = (bf16[12,8,128]{2,1,0:T(8,128)(2,1)S(1)}, bf16[12,8,128]{2,1,0:T(8,128)(2,1)S(1)}, u32[]{:S(2)}, u32[]{:S(2)}) collective-permute-start(bf16[12,8,128]{2,1,0:T(8,128)(2,1)S(1)} %get-tuple-element.114), channel_id=1, source_target_pairs={{0,10},{2,12},{4,14},{6,0},{8,2},{10,4},{12,6},{14,8},{1,11},{3,13... | collective-permute-start | bytes 73736 | tf_op jit(solution)/shard_map/ppermute | solution.py:693
  102.2 3.4 %collective-permute-start.14 = (bf16[12,8,128]{2,1,0:T(8,128)(2,1)S(1)}, bf16[12,8,128]{2,1,0:T(8,128)(2,1)S(1)}, u32[]{:S(2)}, u32[]{:S(2)}) collective-permute-start(bf16[12,8,128]{2,1,0:T(8,128)(2,1)S(1)} %get-tuple-element.115), channel_id=1, source_target_pairs={{0,12},{2,14},{4,0},{6,2},{8,4},{10,6},{12,8},{14,10},{1,13},{3,15... | collective-permute-start | bytes 73736 | tf_op jit(solution)/shard_map/ppermute | solution.py:693
  106.3 3.3 %collective-permute-start.15 = (bf16[12,8,128]{2,1,0:T(8,128)(2,1)S(1)}, bf16[12,8,128]{2,1,0:T(8,128)(2,1)S(1)}, u32[]{:S(2)}, u32[]{:S(2)}) collective-permute-start(bf16[12,8,128]{2,1,0:T(8,128)(2,1)S(1)} %get-tuple-element.116), channel_id=1, source_target_pairs={{0,14},{2,0},{4,2},{6,4},{8,6},{10,8},{12,10},{14,12},{1,15},{3,1}... | collective-permute-start | bytes 73736 | tf_op jit(solution)/shard_map/ppermute | solution.py:693
  109.8 1.9 %collective-permute-start.28 = (bf16[32,8,128]{2,1,0:T(8,128)(2,1)S(1)}, bf16[32,8,128]{2,1,0:T(8,128)(2,1)S(1)}, u32[]{:S(2)}, u32[]{:S(2)}) collective-permute-start(bf16[32,8,128]{2,1,0:T(8,128)(2,1)S(1)} %get-tuple-element.130.refs_16_), channel_id=1, source_target_pairs={{0,4},{2,6},{4,8},{6,10},{8,12},{10,14},{12,0},{14,2},{1,5},{3,7},... | collective-permute-start | bytes 196616 | tf_op jit(solution)/shard_map/ppermute | solution.py:693
  111.7 2.9 %collective-permute-start.32 = (bf16[21,8,128]{2,1,0:T(8,128)(2,1)S(1)}, bf16[21,8,128]{2,1,0:T(8,128)(2,1)S(1)}, u32[]{:S(2)}, u32[]{:S(2)}) collective-permute-start(bf16[21,8,128]{2,1,0:T(8,128)(2,1)S(1)} %get-tuple-element.133), channel_id=1, source_target_pairs={{0,8},{2,10},{4,12},{6,14},{8,0},{10,2},{12,4},{14,6},{1,9},{3,11}... | collective-permute-start | bytes 129032 | tf_op jit(solution)/shard_map/ppermute | solution.py:693
  115.5 2.9 %collective-permute-done.32.refs_22_ = bf16[21,8,128]{2,1,0:T(8,128)(2,1)S(1)} collective-permute-done((bf16[21,8,128]{2,1,0:T(8,128)(2,1)S(1)}, bf16[21,8,128]{2,1,0:T(8,128)(2,1)S(1)}, u32[]{:S(2)}, u32[]{:S(2)}) %collective-permute-start.32) | collective-permute-done | bytes 43040 | tf_op jit(solution)/shard_map/ppermute | solution.py:693
  119.5 4.0 %collective-permute-start.37 = (bf16[21,8,128]{2,1,0:T(8,128)(2,1)S(1)}, bf16[21,8,128]{2,1,0:T(8,128)(2,1)S(1)}, u32[]{:S(2)}, u32[]{:S(2)}) collective-permute-start(bf16[21,8,128]{2,1,0:T(8,128)(2,1)S(1)} %get-tuple-element.136.refs_0_), channel_id=1, source_target_pairs={{0,12},{2,14},{4,0},{6,2},{8,4},{10,6},{12,8},{14,10},{1,13},{3,15... | collective-permute-start | bytes 129032 | tf_op jit(solution)/shard_map/ppermute | solution.py:693
  124.0 1.1 collective-permute-done.37.refs_3_
  125.2 3.2 %collective-permute-done.36.refs_2_ = bf16[21,8,128]{2,1,0:T(8,128)(2,1)S(1)} collective-permute-done((bf16[21,8,128]{2,1,0:T(8,128)(2,1)S(1)}, bf16[21,8,128]{2,1,0:T(8,128)(2,1)S(1)}, u32[]{:S(2)}, u32[]{:S(2)}) %collective-permute-start.36) | collective-permute-done | bytes 43040 | tf_op jit(solution)/shard_map/ppermute | solution.py:693
  129.6 5.3 %collective-permute-done.39.other_b = bf16[4,21,8,128]{3,2,1,0:T(8,128)(2,1)S(1)} collective-permute-done((bf16[4,21,8,128]{3,2,1,0:T(8,128)(2,1)S(1)}, bf16[4,21,8,128]{3,2,1,0:T(8,128)(2,1)S(1)}, u32[]{:S(2)}, u32[]{:S(2)}) %collective-permute-start.39) | collective-permute-done | bytes 172064 | tf_op jit(solution)/shard_map/ppermute | solution.py:698
  135.9 1.1 collective-permute-start.54
  138.3 1.3 collective-permute-start.52
  139.6 2.4 %collective-permute-start.51 = (bf16[7,8,128]{2,1,0:T(8,128)(2,1)S(1)}, bf16[7,8,128]{2,1,0:T(8,128)(2,1)S(1)}, u32[]{:S(2)}, u32[]{:S(2)}) collective-permute-start(bf16[7,8,128]{2,1,0:T(8,128)(2,1)S(1)} %slice.3), channel_id=1, source_target_pairs={{0,7},{1,6},{2,9},{3,8},{4,11},{5,10},{6,13},{7,12},{8,15},{9,14},... | collective-permute-start | bytes 43016 | tf_op jit(solution)/shard_map/ppermute | solution.py:707
  142.4 3.7 %collective-permute-start.47 = (bf16[12,8,128]{2,1,0:T(8,128)(2,1)S(1)}, bf16[12,8,128]{2,1,0:T(8,128)(2,1)S(1)}, u32[]{:S(2)}, u32[]{:S(2)}) collective-permute-start(bf16[12,8,128]{2,1,0:T(8,128)(2,1)S(1)} %get-tuple-element.142.refs_0_), channel_id=1, source_target_pairs={{0,14},{2,0},{4,2},{6,4},{8,6},{10,8},{12,10},{14,12},{1,15},{3,1}... | collective-permute-start | bytes 73736 | tf_op jit(solution)/shard_map/ppermute | solution.py:693
  147.3 4.7 %collective-permute-done.49.refs_9_ = bf16[7,8,128]{2,1,0:T(8,128)(2,1)S(1)} collective-permute-done((bf16[7,8,128]{2,1,0:T(8,128)(2,1)S(1)}, bf16[7,8,128]{2,1,0:T(8,128)(2,1)S(1)}, u32[]{:S(2)}, u32[]{:S(2)}) %collective-permute-start.49) | collective-permute-done | bytes 14368 | tf_op jit(solution)/shard_map/ppermute | solution.py:707
  152.0 2.9 %collective-permute-start.44 = (bf16[12,8,128]{2,1,0:T(8,128)(2,1)S(1)}, bf16[12,8,128]{2,1,0:T(8,128)(2,1)S(1)}, u32[]{:S(2)}, u32[]{:S(2)}) collective-permute-start(bf16[12,8,128]{2,1,0:T(8,128)(2,1)S(1)} %get-tuple-element.142.refs_0_), channel_id=1, source_target_pairs={{0,8},{2,10},{4,12},{6,14},{8,0},{10,2},{12,4},{14,6},{1,9},{3,11}... | collective-permute-start | bytes 73736 | tf_op jit(solution)/shard_map/ppermute | solution.py:693
  154.9 1.2 collective-permute-done.46.refs_6_
  156.7 2.0 %collective-permute-start.42 = (bf16[12,8,128]{2,1,0:T(8,128)(2,1)S(1)}, bf16[12,8,128]{2,1,0:T(8,128)(2,1)S(1)}, u32[]{:S(2)}, u32[]{:S(2)}) collective-permute-start(bf16[12,8,128]{2,1,0:T(8,128)(2,1)S(1)} %get-tuple-element.142.refs_0_), channel_id=1, source_target_pairs={{0,4},{2,6},{4,8},{6,10},{8,12},{10,14},{12,0},{14,2},{1,5},{3,7},... | collective-permute-start | bytes 73736 | tf_op jit(solution)/shard_map/ppermute | solution.py:693
  159.7 2.0 %collective-permute-done.43.refs_3_ = bf16[12,8,128]{2,1,0:T(8,128)(2,1)S(1)} collective-permute-done((bf16[12,8,128]{2,1,0:T(8,128)(2,1)S(1)}, bf16[12,8,128]{2,1,0:T(8,128)(2,1)S(1)}, u32[]{:S(2)}, u32[]{:S(2)}) %collective-permute-start.43) | collective-permute-done | bytes 24608 | tf_op jit(solution)/shard_map/ppermute | solution.py:693
  162.4 2.9 %collective-permute-done.41.refs_1_ = bf16[12,8,128]{2,1,0:T(8,128)(2,1)S(1)} collective-permute-done((bf16[12,8,128]{2,1,0:T(8,128)(2,1)S(1)}, bf16[12,8,128]{2,1,0:T(8,128)(2,1)S(1)}, u32[]{:S(2)}, u32[]{:S(2)}) %collective-permute-start.41) | collective-permute-done | bytes 24608 | tf_op jit(solution)/shard_map/ppermute | solution.py:693
  165.3 2.7 %shard_map.124 = (bf16[6918,128]{1,0:T(8,128)(2,1)}, f32[2,1,6,6336]{3,2,1,0:T(8,128)S(1)}) custom-call(bf16[2,132,384]{2,1,0:T(8,128)(2,1)S(1)} %copy-done.15, bf16[8,32,8,128]{3,2,1,0:T(8,128)(2,1)S(1)} %get-tuple-element.137.own_a, bf16[8,27,8,128]{3,2,1,0:T(8,128)(2,1)S(1)} %collective-permute-done.38.oth_a, ...), custom_call_target="tpu_custom_call" | custom-call | flops 3300000000 | bytes 100000 | tf_op jit(solution)/shard_map/pallas_call | solution.py:674
  167.9 1.0 copy.12
  (111 shorter events, 21.4 us)
Async XLA Ops:
  16.3 10.6 %collective-permute-start.1 = (bf16[2,504,192]{2,1,0:T(8,128)(2,1)S(1)}, bf16[2,504,192]{2,1,0:T(8,128)(2,1)S(1)}, u32[]{:S(2)}, u32[]{:S(2)}) collective-permute-start(bf16[2,504,192]{2,1,0:T(8,128)(2,1)S(1)} %get-tuple-element.77.tail), channel_id=1, source_target_pairs={{0,1},{1,0},{2,3},{3,2},{4,5},{5,4},{6,7},{7,6},{8,9},{9,8},{10,11... | collective-permute-start | bytes 1161224 | tf_op jit(solution)/shard_map/ppermute | solution.py:688
  16.9 8.3 %collective-permute-start.2 = (bf16[2,72,192]{2,1,0:T(8,128)(2,1)S(1)}, bf16[2,72,192]{2,1,0:T(8,128)(2,1)S(1)}, u32[]{:S(2)}, u32[]{:S(2)}) collective-permute-start(bf16[2,72,192]{2,1,0:T(8,128)(2,1)S(1)} %get-tuple-element.78), channel_id=1, source_target_pairs={{0,15},{1,14},{2,1},{3,0},{4,3},{5,2},{6,5},{7,4},{8,7},{9,6},{10,... | collective-permute-start | bytes 165896 | tf_op jit(solution)/shard_map/ppermute | solution.py:707
  22.6 4.4 %collective-permute-start = (bf16[2,72,192]{2,1,0:T(8,128)(2,1)S(1)}, bf16[2,72,192]{2,1,0:T(8,128)(2,1)S(1)}, u32[]{:S(2)}, u32[]{:S(2)}) collective-permute-start(bf16[2,72,192]{2,1,0:T(8,128)(2,1)S(1)} %get-tuple-element.78), channel_id=1, source_target_pairs={{0,14},{2,0},{4,2},{6,4},{8,6},{10,8},{12,10},{14,12},{1,15},{3,1}... | collective-permute-start | bytes 165896 | tf_op jit(solution)/shard_map/ppermute | solution.py:693
  45.7 7.8 %collective-permute-start.6 = (bf16[8,27,8,128]{3,2,1,0:T(8,128)(2,1)S(1)}, bf16[8,27,8,128]{3,2,1,0:T(8,128)(2,1)S(1)}, u32[]{:S(2)}, u32[]{:S(2)}) collective-permute-start(bf16[8,27,8,128]{3,2,1,0:T(8,128)(2,1)S(1)} %get-tuple-element.95), channel_id=1, source_target_pairs={{0,1},{1,0},{2,3},{3,2},{4,5},{5,4},{6,7},{7,6},{8,9},{9,8},{10,11... | collective-permute-start | bytes 1327112 | tf_op jit(solution)/shard_map/ppermute | solution.py:688
  45.7 7.8 %collective-permute-start.4 = (bf16[504,192]{1,0:T(8,128)(2,1)S(1)}, bf16[504,192]{1,0:T(8,128)(2,1)S(1)}, u32[]{:S(2)}, u32[]{:S(2)}) collective-permute-start(bf16[504,192]{1,0:T(8,128)(2,1)S(1)} %get-tuple-element.79.head), channel_id=1, source_target_pairs={{0,1},{1,0},{2,3},{3,2},{4,5},{5,4},{6,7},{7,6},{8,9},{9,8},{10,11... | collective-permute-start | bytes 580616 | tf_op jit(solution)/shard_map/ppermute | solution.py:688
  46.2 6.2 %collective-permute-start.5 = (bf16[72,192]{1,0:T(8,128)(2,1)S(1)}, bf16[72,192]{1,0:T(8,128)(2,1)S(1)}, u32[]{:S(2)}, u32[]{:S(2)}) collective-permute-start(bf16[72,192]{1,0:T(8,128)(2,1)S(1)} %get-tuple-element.80), channel_id=1, source_target_pairs={{0,3},{1,2},{2,5},{3,4},{4,7},{5,6},{6,9},{7,8},{8,11},{9,10},{10,... | collective-permute-start | bytes 82952 | tf_op jit(solution)/shard_map/ppermute | solution.py:707
  46.2 7.3 %collective-permute-start.3 = (bf16[72,192]{1,0:T(8,128)(2,1)S(1)}, bf16[72,192]{1,0:T(8,128)(2,1)S(1)}, u32[]{:S(2)}, u32[]{:S(2)}) collective-permute-start(bf16[72,192]{1,0:T(8,128)(2,1)S(1)} %get-tuple-element.80), channel_id=1, source_target_pairs={{0,2},{2,4},{4,6},{6,8},{8,10},{10,12},{12,14},{14,0},{1,3},{3,5},... | collective-permute-start | bytes 82952 | tf_op jit(solution)/shard_map/ppermute | solution.py:693
  55.7 8.1 %collective-permute-start.7 = (bf16[4,32,8,128]{3,2,1,0:T(8,128)(2,1)S(1)}, bf16[4,32,8,128]{3,2,1,0:T(8,128)(2,1)S(1)}, u32[]{:S(2)}, u32[]{:S(2)}) collective-permute-start(bf16[4,32,8,128]{3,2,1,0:T(8,128)(2,1)S(1)} %get-tuple-element.104), channel_id=1, source_target_pairs={{0,2},{2,0},{4,6},{6,4},{8,10},{10,8},{12,14},{14,12},{1,3},{3,1},... | collective-permute-start | bytes 786440 | tf_op jit(solution)/shard_map/ppermute | solution.py:698
  55.8 8.0 %collective-permute-start.8 = (bf16[8,21,8,128]{3,2,1,0:T(8,128)(2,1)S(1)}, bf16[8,21,8,128]{3,2,1,0:T(8,128)(2,1)S(1)}, u32[]{:S(2)}, u32[]{:S(2)}) collective-permute-start(bf16[8,21,8,128]{3,2,1,0:T(8,128)(2,1)S(1)} %get-tuple-element.106), channel_id=1, source_target_pairs={{0,1},{1,0},{2,3},{3,2},{4,5},{5,4},{6,7},{7,6},{8,9},{9,8},{10,11... | collective-permute-start | bytes 1032200 | tf_op jit(solution)/shard_map/ppermute | solution.py:688
  63.9 38.2 %collective-permute-start.27 = (bf16[4,21,8,128]{3,2,1,0:T(8,128)(2,1)S(1)}, bf16[4,21,8,128]{3,2,1,0:T(8,128)(2,1)S(1)}, u32[]{:S(2)}, u32[]{:S(2)}) collective-permute-start(bf16[4,21,8,128]{3,2,1,0:T(8,128)(2,1)S(1)} %get-tuple-element.129), channel_id=1, source_target_pairs={{0,2},{2,0},{4,6},{6,4},{8,10},{10,8},{12,14},{14,12},{1,3},{3,1},... | collective-permute-start | bytes 516104 | tf_op jit(solution)/shard_map/ppermute | solution.py:698
  70.9 5.8 %collective-permute-start.17 = (bf16[7,8,128]{2,1,0:T(8,128)(2,1)S(1)}, bf16[7,8,128]{2,1,0:T(8,128)(2,1)S(1)}, u32[]{:S(2)}, u32[]{:S(2)}) collective-permute-start(bf16[7,8,128]{2,1,0:T(8,128)(2,1)S(1)} %get-tuple-element.118), channel_id=1, source_target_pairs={{0,3},{1,2},{2,5},{3,4},{4,7},{5,6},{6,9},{7,8},{8,11},{9,10},{10,... | collective-permute-start | bytes 43016 | tf_op jit(solution)/shard_map/ppermute | solution.py:707
  72.8 5.6 %collective-permute-start.18 = (bf16[7,8,128]{2,1,0:T(8,128)(2,1)S(1)}, bf16[7,8,128]{2,1,0:T(8,128)(2,1)S(1)}, u32[]{:S(2)}, u32[]{:S(2)}) collective-permute-start(bf16[7,8,128]{2,1,0:T(8,128)(2,1)S(1)} %get-tuple-element.119), channel_id=1, source_target_pairs={{0,5},{1,4},{2,7},{3,6},{4,9},{5,8},{6,11},{7,10},{8,13},{9,12},{1... | collective-permute-start | bytes 43016 | tf_op jit(solution)/shard_map/ppermute | solution.py:707
  72.8 7.7 %collective-permute-start.19 = (bf16[7,8,128]{2,1,0:T(8,128)(2,1)S(1)}, bf16[7,8,128]{2,1,0:T(8,128)(2,1)S(1)}, u32[]{:S(2)}, u32[]{:S(2)}) collective-permute-start(bf16[7,8,128]{2,1,0:T(8,128)(2,1)S(1)} %get-tuple-element.120), channel_id=1, source_target_pairs={{0,7},{1,6},{2,9},{3,8},{4,11},{5,10},{6,13},{7,12},{8,15},{9,14},... | collective-permute-start | bytes 43016 | tf_op jit(solution)/shard_map/ppermute | solution.py:707
  74.8 5.6 %collective-permute-start.20 = (bf16[7,8,128]{2,1,0:T(8,128)(2,1)S(1)}, bf16[7,8,128]{2,1,0:T(8,128)(2,1)S(1)}, u32[]{:S(2)}, u32[]{:S(2)}) collective-permute-start(bf16[7,8,128]{2,1,0:T(8,128)(2,1)S(1)} %get-tuple-element.121), channel_id=1, source_target_pairs={{0,9},{1,8},{2,11},{3,10},{4,13},{5,12},{6,15},{7,14},{8,1},{9,0},... | collective-permute-start | bytes 43016 | tf_op jit(solution)/shard_map/ppermute | solution.py:707
  76.8 6.1 %collective-permute-start.21 = (bf16[7,8,128]{2,1,0:T(8,128)(2,1)S(1)}, bf16[7,8,128]{2,1,0:T(8,128)(2,1)S(1)}, u32[]{:S(2)}, u32[]{:S(2)}) collective-permute-start(bf16[7,8,128]{2,1,0:T(8,128)(2,1)S(1)} %get-tuple-element.122), channel_id=1, source_target_pairs={{0,11},{1,10},{2,13},{3,12},{4,15},{5,14},{6,1},{7,0},{8,3},{9,2},... | collective-permute-start | bytes 43016 | tf_op jit(solution)/shard_map/ppermute | solution.py:707
  78.4 19.5 %collective-permute-start.24 = (bf16[32,8,128]{2,1,0:T(8,128)(2,1)S(1)}, bf16[32,8,128]{2,1,0:T(8,128)(2,1)S(1)}, u32[]{:S(2)}, u32[]{:S(2)}) collective-permute-start(bf16[32,8,128]{2,1,0:T(8,128)(2,1)S(1)} %get-tuple-element.125), channel_id=1, source_target_pairs={{0,4},{2,6},{4,8},{6,10},{8,12},{10,14},{12,0},{14,2},{1,5},{3,7},... | collective-permute-start | bytes 196616 | tf_op jit(solution)/shard_map/ppermute | solution.py:693
  80.5 17.5 %collective-permute-start.25 = (bf16[32,8,128]{2,1,0:T(8,128)(2,1)S(1)}, bf16[32,8,128]{2,1,0:T(8,128)(2,1)S(1)}, u32[]{:S(2)}, u32[]{:S(2)}) collective-permute-start(bf16[32,8,128]{2,1,0:T(8,128)(2,1)S(1)} %get-tuple-element.126), channel_id=1, source_target_pairs={{0,8},{2,10},{4,12},{6,14},{8,0},{10,2},{12,4},{14,6},{1,9},{3,11}... | collective-permute-start | bytes 196616 | tf_op jit(solution)/shard_map/ppermute | solution.py:693
  80.5 19.6 %collective-permute-start.26 = (bf16[32,8,128]{2,1,0:T(8,128)(2,1)S(1)}, bf16[32,8,128]{2,1,0:T(8,128)(2,1)S(1)}, u32[]{:S(2)}, u32[]{:S(2)}) collective-permute-start(bf16[32,8,128]{2,1,0:T(8,128)(2,1)S(1)} %get-tuple-element.127), channel_id=1, source_target_pairs={{0,12},{2,14},{4,0},{6,2},{8,4},{10,6},{12,8},{14,10},{1,13},{3,15... | collective-permute-start | bytes 196616 | tf_op jit(solution)/shard_map/ppermute | solution.py:693
  91.4 6.5 %collective-permute-start.9 = (bf16[12,8,128]{2,1,0:T(8,128)(2,1)S(1)}, bf16[12,8,128]{2,1,0:T(8,128)(2,1)S(1)}, u32[]{:S(2)}, u32[]{:S(2)}) collective-permute-start(bf16[12,8,128]{2,1,0:T(8,128)(2,1)S(1)} %get-tuple-element.110), channel_id=1, source_target_pairs={{0,2},{2,4},{4,6},{6,8},{8,10},{10,12},{12,14},{14,0},{1,3},{3,5},... | collective-permute-start | bytes 73736 | tf_op jit(solution)/shard_map/ppermute | solution.py:693
  97.9 7.8 %collective-permute-start.10 = (bf16[12,8,128]{2,1,0:T(8,128)(2,1)S(1)}, bf16[12,8,128]{2,1,0:T(8,128)(2,1)S(1)}, u32[]{:S(2)}, u32[]{:S(2)}) collective-permute-start(bf16[12,8,128]{2,1,0:T(8,128)(2,1)S(1)} %get-tuple-element.111), channel_id=1, source_target_pairs={{0,4},{2,6},{4,8},{6,10},{8,12},{10,14},{12,0},{14,2},{1,5},{3,7},... | collective-permute-start | bytes 73736 | tf_op jit(solution)/shard_map/ppermute | solution.py:693
  97.9 8.4 %collective-permute-start.11 = (bf16[12,8,128]{2,1,0:T(8,128)(2,1)S(1)}, bf16[12,8,128]{2,1,0:T(8,128)(2,1)S(1)}, u32[]{:S(2)}, u32[]{:S(2)}) collective-permute-start(bf16[12,8,128]{2,1,0:T(8,128)(2,1)S(1)} %get-tuple-element.112), channel_id=1, source_target_pairs={{0,6},{2,8},{4,10},{6,12},{8,14},{10,0},{12,2},{14,4},{1,7},{3,9},... | collective-permute-start | bytes 73736 | tf_op jit(solution)/shard_map/ppermute | solution.py:693
  97.9 11.7 %collective-permute-start.12 = (bf16[12,8,128]{2,1,0:T(8,128)(2,1)S(1)}, bf16[12,8,128]{2,1,0:T(8,128)(2,1)S(1)}, u32[]{:S(2)}, u32[]{:S(2)}) collective-permute-start(bf16[12,8,128]{2,1,0:T(8,128)(2,1)S(1)} %get-tuple-element.113), channel_id=1, source_target_pairs={{0,8},{2,10},{4,12},{6,14},{8,0},{10,2},{12,4},{14,6},{1,9},{3,11}... | collective-permute-start | bytes 73736 | tf_op jit(solution)/shard_map/ppermute | solution.py:693
  100.1 9.6 %collective-permute-start.13 = (bf16[12,8,128]{2,1,0:T(8,128)(2,1)S(1)}, bf16[12,8,128]{2,1,0:T(8,128)(2,1)S(1)}, u32[]{:S(2)}, u32[]{:S(2)}) collective-permute-start(bf16[12,8,128]{2,1,0:T(8,128)(2,1)S(1)} %get-tuple-element.114), channel_id=1, source_target_pairs={{0,10},{2,12},{4,14},{6,0},{8,2},{10,4},{12,6},{14,8},{1,11},{3,13... | collective-permute-start | bytes 73736 | tf_op jit(solution)/shard_map/ppermute | solution.py:693
  102.2 7.7 %collective-permute-start.14 = (bf16[12,8,128]{2,1,0:T(8,128)(2,1)S(1)}, bf16[12,8,128]{2,1,0:T(8,128)(2,1)S(1)}, u32[]{:S(2)}, u32[]{:S(2)}) collective-permute-start(bf16[12,8,128]{2,1,0:T(8,128)(2,1)S(1)} %get-tuple-element.115), channel_id=1, source_target_pairs={{0,12},{2,14},{4,0},{6,2},{8,4},{10,6},{12,8},{14,10},{1,13},{3,15... | collective-permute-start | bytes 73736 | tf_op jit(solution)/shard_map/ppermute | solution.py:693
  105.7 8.9 %collective-permute-start.31 = (bf16[21,8,128]{2,1,0:T(8,128)(2,1)S(1)}, bf16[21,8,128]{2,1,0:T(8,128)(2,1)S(1)}, u32[]{:S(2)}, u32[]{:S(2)}) collective-permute-start(bf16[21,8,128]{2,1,0:T(8,128)(2,1)S(1)} %get-tuple-element.132), channel_id=1, source_target_pairs={{0,4},{2,6},{4,8},{6,10},{8,12},{10,14},{12,0},{14,2},{1,5},{3,7},... | collective-permute-start | bytes 129032 | tf_op jit(solution)/shard_map/ppermute | solution.py:693
  106.3 5.4 %collective-permute-start.15 = (bf16[12,8,128]{2,1,0:T(8,128)(2,1)S(1)}, bf16[12,8,128]{2,1,0:T(8,128)(2,1)S(1)}, u32[]{:S(2)}, u32[]{:S(2)}) collective-permute-start(bf16[12,8,128]{2,1,0:T(8,128)(2,1)S(1)} %get-tuple-element.116), channel_id=1, source_target_pairs={{0,14},{2,0},{4,2},{6,4},{8,6},{10,8},{12,10},{14,12},{1,15},{3,1}... | collective-permute-start | bytes 73736 | tf_op jit(solution)/shard_map/ppermute | solution.py:693
  109.6 9.3 %collective-permute-start.30 = (bf16[32,8,128]{2,1,0:T(8,128)(2,1)S(1)}, bf16[32,8,128]{2,1,0:T(8,128)(2,1)S(1)}, u32[]{:S(2)}, u32[]{:S(2)}) collective-permute-start(bf16[32,8,128]{2,1,0:T(8,128)(2,1)S(1)} %get-tuple-element.130.refs_16_), channel_id=1, source_target_pairs={{0,12},{2,14},{4,0},{6,2},{8,4},{10,6},{12,8},{14,10},{1,13},{3,15... | collective-permute-start | bytes 196616 | tf_op jit(solution)/shard_map/ppermute | solution.py:693
  109.6 9.2 %collective-permute-start.29 = (bf16[32,8,128]{2,1,0:T(8,128)(2,1)S(1)}, bf16[32,8,128]{2,1,0:T(8,128)(2,1)S(1)}, u32[]{:S(2)}, u32[]{:S(2)}) collective-permute-start(bf16[32,8,128]{2,1,0:T(8,128)(2,1)S(1)} %get-tuple-element.130.refs_16_), channel_id=1, source_target_pairs={{0,8},{2,10},{4,12},{6,14},{8,0},{10,2},{12,4},{14,6},{1,9},{3,11}... | collective-permute-start | bytes 196616 | tf_op jit(solution)/shard_map/ppermute | solution.py:693
  109.8 9.0 %collective-permute-start.28 = (bf16[32,8,128]{2,1,0:T(8,128)(2,1)S(1)}, bf16[32,8,128]{2,1,0:T(8,128)(2,1)S(1)}, u32[]{:S(2)}, u32[]{:S(2)}) collective-permute-start(bf16[32,8,128]{2,1,0:T(8,128)(2,1)S(1)} %get-tuple-element.130.refs_16_), channel_id=1, source_target_pairs={{0,4},{2,6},{4,8},{6,10},{8,12},{10,14},{12,0},{14,2},{1,5},{3,7},... | collective-permute-start | bytes 196616 | tf_op jit(solution)/shard_map/ppermute | solution.py:693
  111.7 6.7 %collective-permute-start.32 = (bf16[21,8,128]{2,1,0:T(8,128)(2,1)S(1)}, bf16[21,8,128]{2,1,0:T(8,128)(2,1)S(1)}, u32[]{:S(2)}, u32[]{:S(2)}) collective-permute-start(bf16[21,8,128]{2,1,0:T(8,128)(2,1)S(1)} %get-tuple-element.133), channel_id=1, source_target_pairs={{0,8},{2,10},{4,12},{6,14},{8,0},{10,2},{12,4},{14,6},{1,9},{3,11}... | collective-permute-start | bytes 129032 | tf_op jit(solution)/shard_map/ppermute | solution.py:693
  118.9 10.4 %collective-permute-start.34 = (bf16[4,32,8,128]{3,2,1,0:T(8,128)(2,1)S(1)}, bf16[4,32,8,128]{3,2,1,0:T(8,128)(2,1)S(1)}, u32[]{:S(2)}, u32[]{:S(2)}) collective-permute-start(bf16[4,32,8,128]{3,2,1,0:T(8,128)(2,1)S(1)} %get-tuple-element.135.mine_a), channel_id=1, source_target_pairs={{0,2},{2,0},{4,6},{6,4},{8,10},{10,8},{12,14},{14,12},{1,3},{3,1},... | collective-permute-start | bytes 786440 | tf_op jit(solution)/shard_map/ppermute | solution.py:698
  119.5 5.7 %collective-permute-start.37 = (bf16[21,8,128]{2,1,0:T(8,128)(2,1)S(1)}, bf16[21,8,128]{2,1,0:T(8,128)(2,1)S(1)}, u32[]{:S(2)}, u32[]{:S(2)}) collective-permute-start(bf16[21,8,128]{2,1,0:T(8,128)(2,1)S(1)} %get-tuple-element.136.refs_0_), channel_id=1, source_target_pairs={{0,12},{2,14},{4,0},{6,2},{8,4},{10,6},{12,8},{14,10},{1,13},{3,15... | collective-permute-start | bytes 129032 | tf_op jit(solution)/shard_map/ppermute | solution.py:693
  123.5 4.9 %collective-permute-start.36 = (bf16[21,8,128]{2,1,0:T(8,128)(2,1)S(1)}, bf16[21,8,128]{2,1,0:T(8,128)(2,1)S(1)}, u32[]{:S(2)}, u32[]{:S(2)}) collective-permute-start(bf16[21,8,128]{2,1,0:T(8,128)(2,1)S(1)} %get-tuple-element.136.refs_0_), channel_id=1, source_target_pairs={{0,8},{2,10},{4,12},{6,14},{8,0},{10,2},{12,4},{14,6},{1,9},{3,11}... | collective-permute-start | bytes 129032 | tf_op jit(solution)/shard_map/ppermute | solution.py:693
  123.5 5.8 %collective-permute-start.35 = (bf16[21,8,128]{2,1,0:T(8,128)(2,1)S(1)}, bf16[21,8,128]{2,1,0:T(8,128)(2,1)S(1)}, u32[]{:S(2)}, u32[]{:S(2)}) collective-permute-start(bf16[21,8,128]{2,1,0:T(8,128)(2,1)S(1)} %get-tuple-element.136.refs_0_), channel_id=1, source_target_pairs={{0,4},{2,6},{4,8},{6,10},{8,12},{10,14},{12,0},{14,2},{1,5},{3,7},... | collective-permute-start | bytes 129032 | tf_op jit(solution)/shard_map/ppermute | solution.py:693
  129.5 5.5 %collective-permute-start.39 = (bf16[4,21,8,128]{3,2,1,0:T(8,128)(2,1)S(1)}, bf16[4,21,8,128]{3,2,1,0:T(8,128)(2,1)S(1)}, u32[]{:S(2)}, u32[]{:S(2)}) collective-permute-start(bf16[4,21,8,128]{3,2,1,0:T(8,128)(2,1)S(1)} %get-tuple-element.139.mine_b), channel_id=1, source_target_pairs={{0,2},{2,0},{4,6},{6,4},{8,10},{10,8},{12,14},{14,12},{1,3},{3,1},... | collective-permute-start | bytes 516104 | tf_op jit(solution)/shard_map/ppermute | solution.py:698
  129.6 35.7 %collective-permute-start.38 = (bf16[8,27,8,128]{3,2,1,0:T(8,128)(2,1)S(1)}, bf16[8,27,8,128]{3,2,1,0:T(8,128)(2,1)S(1)}, u32[]{:S(2)}, u32[]{:S(2)}) collective-permute-start(bf16[8,27,8,128]{3,2,1,0:T(8,128)(2,1)S(1)} %get-tuple-element.138), channel_id=1, source_target_pairs={{0,1},{1,0},{2,3},{3,2},{4,5},{5,4},{6,7},{7,6},{8,9},{9,8},{10,11... | collective-permute-start | bytes 1327112 | tf_op jit(solution)/shard_map/ppermute | solution.py:688
  135.0 30.3 %collective-permute-start.40 = (bf16[8,21,8,128]{3,2,1,0:T(8,128)(2,1)S(1)}, bf16[8,21,8,128]{3,2,1,0:T(8,128)(2,1)S(1)}, u32[]{:S(2)}, u32[]{:S(2)}) collective-permute-start(bf16[8,21,8,128]{3,2,1,0:T(8,128)(2,1)S(1)} %get-tuple-element.141), channel_id=1, source_target_pairs={{0,1},{1,0},{2,3},{3,2},{4,5},{5,4},{6,7},{7,6},{8,9},{9,8},{10,11... | collective-permute-start | bytes 1032200 | tf_op jit(solution)/shard_map/ppermute | solution.py:688
  137.0 5.0 %collective-permute-start.53 = (bf16[7,8,128]{2,1,0:T(8,128)(2,1)S(1)}, bf16[7,8,128]{2,1,0:T(8,128)(2,1)S(1)}, u32[]{:S(2)}, u32[]{:S(2)}) collective-permute-start(bf16[7,8,128]{2,1,0:T(8,128)(2,1)S(1)} %slice.3), channel_id=1, source_target_pairs={{0,11},{1,10},{2,13},{3,12},{4,15},{5,14},{6,1},{7,0},{8,3},{9,2},... | collective-permute-start | bytes 43016 | tf_op jit(solution)/shard_map/ppermute | solution.py:707
  139.6 6.5 %collective-permute-start.51 = (bf16[7,8,128]{2,1,0:T(8,128)(2,1)S(1)}, bf16[7,8,128]{2,1,0:T(8,128)(2,1)S(1)}, u32[]{:S(2)}, u32[]{:S(2)}) collective-permute-start(bf16[7,8,128]{2,1,0:T(8,128)(2,1)S(1)} %slice.3), channel_id=1, source_target_pairs={{0,7},{1,6},{2,9},{3,8},{4,11},{5,10},{6,13},{7,12},{8,15},{9,14},... | collective-permute-start | bytes 43016 | tf_op jit(solution)/shard_map/ppermute | solution.py:707
  142.0 4.9 %collective-permute-start.50 = (bf16[7,8,128]{2,1,0:T(8,128)(2,1)S(1)}, bf16[7,8,128]{2,1,0:T(8,128)(2,1)S(1)}, u32[]{:S(2)}, u32[]{:S(2)}) collective-permute-start(bf16[7,8,128]{2,1,0:T(8,128)(2,1)S(1)} %slice.3), channel_id=1, source_target_pairs={{0,5},{1,4},{2,7},{3,6},{4,9},{5,8},{6,11},{7,10},{8,13},{9,12},{1... | collective-permute-start | bytes 43016 | tf_op jit(solution)/shard_map/ppermute | solution.py:707
  142.4 9.6 %collective-permute-start.47 = (bf16[12,8,128]{2,1,0:T(8,128)(2,1)S(1)}, bf16[12,8,128]{2,1,0:T(8,128)(2,1)S(1)}, u32[]{:S(2)}, u32[]{:S(2)}) collective-permute-start(bf16[12,8,128]{2,1,0:T(8,128)(2,1)S(1)} %get-tuple-element.142.refs_0_), channel_id=1, source_target_pairs={{0,14},{2,0},{4,2},{6,4},{8,6},{10,8},{12,10},{14,12},{1,15},{3,1}... | collective-permute-start | bytes 73736 | tf_op jit(solution)/shard_map/ppermute | solution.py:693
  146.0 6.0 %collective-permute-start.49 = (bf16[7,8,128]{2,1,0:T(8,128)(2,1)S(1)}, bf16[7,8,128]{2,1,0:T(8,128)(2,1)S(1)}, u32[]{:S(2)}, u32[]{:S(2)}) collective-permute-start(bf16[7,8,128]{2,1,0:T(8,128)(2,1)S(1)} %slice.3), channel_id=1, source_target_pairs={{0,3},{1,2},{2,5},{3,4},{4,7},{5,6},{6,9},{7,8},{8,11},{9,10},{10,... | collective-permute-start | bytes 43016 | tf_op jit(solution)/shard_map/ppermute | solution.py:707
  146.9 5.1 %collective-permute-start.48 = (bf16[7,8,128]{2,1,0:T(8,128)(2,1)S(1)}, bf16[7,8,128]{2,1,0:T(8,128)(2,1)S(1)}, u32[]{:S(2)}, u32[]{:S(2)}) collective-permute-start(bf16[7,8,128]{2,1,0:T(8,128)(2,1)S(1)} %slice.3), channel_id=1, source_target_pairs={{0,1},{1,0},{2,3},{3,2},{4,5},{5,4},{6,7},{7,6},{8,9},{9,8},{10,11... | collective-permute-start | bytes 43016 | tf_op jit(solution)/shard_map/ppermute | solution.py:688
  152.0 4.7 %collective-permute-start.45 = (bf16[12,8,128]{2,1,0:T(8,128)(2,1)S(1)}, bf16[12,8,128]{2,1,0:T(8,128)(2,1)S(1)}, u32[]{:S(2)}, u32[]{:S(2)}) collective-permute-start(bf16[12,8,128]{2,1,0:T(8,128)(2,1)S(1)} %get-tuple-element.142.refs_0_), channel_id=1, source_target_pairs={{0,10},{2,12},{4,14},{6,0},{8,2},{10,4},{12,6},{14,8},{1,11},{3,13... | collective-permute-start | bytes 73736 | tf_op jit(solution)/shard_map/ppermute | solution.py:693
  152.0 6.7 %collective-permute-start.44 = (bf16[12,8,128]{2,1,0:T(8,128)(2,1)S(1)}, bf16[12,8,128]{2,1,0:T(8,128)(2,1)S(1)}, u32[]{:S(2)}, u32[]{:S(2)}) collective-permute-start(bf16[12,8,128]{2,1,0:T(8,128)(2,1)S(1)} %get-tuple-element.142.refs_0_), channel_id=1, source_target_pairs={{0,8},{2,10},{4,12},{6,14},{8,0},{10,2},{12,4},{14,6},{1,9},{3,11}... | collective-permute-start | bytes 73736 | tf_op jit(solution)/shard_map/ppermute | solution.py:693
  156.1 5.6 %collective-permute-start.43 = (bf16[12,8,128]{2,1,0:T(8,128)(2,1)S(1)}, bf16[12,8,128]{2,1,0:T(8,128)(2,1)S(1)}, u32[]{:S(2)}, u32[]{:S(2)}) collective-permute-start(bf16[12,8,128]{2,1,0:T(8,128)(2,1)S(1)} %get-tuple-element.142.refs_0_), channel_id=1, source_target_pairs={{0,6},{2,8},{4,10},{6,12},{8,14},{10,0},{12,2},{14,4},{1,7},{3,9},... | collective-permute-start | bytes 73736 | tf_op jit(solution)/shard_map/ppermute | solution.py:693
  156.7 5.6 %collective-permute-start.42 = (bf16[12,8,128]{2,1,0:T(8,128)(2,1)S(1)}, bf16[12,8,128]{2,1,0:T(8,128)(2,1)S(1)}, u32[]{:S(2)}, u32[]{:S(2)}) collective-permute-start(bf16[12,8,128]{2,1,0:T(8,128)(2,1)S(1)} %get-tuple-element.142.refs_0_), channel_id=1, source_target_pairs={{0,4},{2,6},{4,8},{6,10},{8,12},{10,14},{12,0},{14,2},{1,5},{3,7},... | collective-permute-start | bytes 73736 | tf_op jit(solution)/shard_map/ppermute | solution.py:693
  158.8 6.5 %collective-permute-start.41 = (bf16[12,8,128]{2,1,0:T(8,128)(2,1)S(1)}, bf16[12,8,128]{2,1,0:T(8,128)(2,1)S(1)}, u32[]{:S(2)}, u32[]{:S(2)}) collective-permute-start(bf16[12,8,128]{2,1,0:T(8,128)(2,1)S(1)} %get-tuple-element.142.refs_0_), channel_id=1, source_target_pairs={{0,2},{2,4},{4,6},{6,8},{8,10},{10,12},{12,14},{14,0},{1,3},{3,5},... | collective-permute-start | bytes 73736 | tf_op jit(solution)/shard_map/ppermute | solution.py:693
  (24 other events, 118.4 us)

commit v3 on v2

--- a/solution.py
+++ b/solution.py
@@ -296,24 +296,46 @@
 
 
 def first_kernel(
-    lat_total, tokens, cot, table, spread, qkv_w, proj_w, up_w, down_w, gains,
+    lat_total, tokens_in, cot_in, table_in, spread_in, qkv_in, proj_in, up_in, down_in, gains_in,
     x_out, tail_out, head_out, qkv_out, mixed_out, probs_out, resid_out, slope_out, active_out,
     scr, cot_scr, tab_scr, rows_scr, wide_scr, bias_scr,
+    cot, table, spread, tokens, qkv_w, gains, proj_w, up_w, down_w, sems,
 ):
+    copies = []
+    for source, target in (
+        (cot_in, cot),
+        (table_in.at[0:1], table),
+        (spread_in, spread),
+        (tokens_in, tokens),
+        (qkv_in.at[0:1], qkv_w),
+        (gains_in, gains),
+        (proj_in.at[0:1], proj_w),
+        (up_in.at[0:1], up_w),
+        (down_in.at[0:1], down_w),
+    ):
+        copies.append(pltpu.make_async_copy(source, target, sems.at[len(copies)]))
+    for copy in copies:
+        copy.start()
     lat = lax.axis_index("lat")
     width = tokens.shape[-1]
     lons = tokens.shape[2]
     cut = CHUNK * (WLON // 2)
+    copies[0].wait()
     lon_major(cot, cot_scr)
     g = jnp.concatenate([lon_column(cot_scr, lon, lons, width) for lon in range(lons)], axis=0)
     head_out[1] = g[0:cut, :].astype(BF16)
     tail_out[1] = g[cut:, :].astype(BF16)
+    copies[1].wait()
+    copies[2].wait()
     expand_bias(
         table.at[0], spread, tab_scr, rows_scr, wide_scr, bias_scr, lat, False, lat_total
     )
+    copies[3].wait()
     lon_major(tokens, scr)
     x = jnp.concatenate([lon_column(scr, lon, lons, width) for lon in range(lons)], axis=0)
     x_out[...] = x.astype(BF16)
+    for copy in copies[4:]:
+        copy.wait()
     resid, _ = forward_core(
         x, 0, lat, lat_total, (qkv_w, proj_w, gains), qkv_out, bias_scr, mixed_out, probs_out
     )
@@ -430,52 +452,39 @@
     bias_units(sums, bias_out)
 
 
-def split_x(x, keep, got, bias, keep_out, give_out):
-    units = keep.shape[1]
-    for z in range(keep_out.shape[0]):
-        for out, side in ((keep_out, x), (give_out, 1 - x)):
-            at = 2 * z + side
-            out[z, 0:units] = (keep[at].astype(F32) + got[at].astype(F32)).astype(BF16)
-            if bias is not None:
-                out[z, units:] = bias[at]
-
-
-def split_z(z, keep, got, own_out, *give_outs):
-    count = keep.shape[0]
-    for k, out in enumerate((own_out,) + give_outs):
-        at = lax.rem(z + k, count)
-        out[...] = (keep[at].astype(F32) + got[at].astype(F32)).astype(BF16)
-
-
-def sum_all(*refs):
-    total = refs[0][...].astype(F32)
-    for ref in refs[1:-1]:
-        total = total + ref[...].astype(F32)
-    refs[-1][...] = total.astype(BF16)
-
-
-def join_z(z, *refs):
-    count = len(refs) - 1
-    for k in range(count):
-        refs[-1][lax.rem(z + count - k, count)] = refs[k][...]
-
-
-def join_x(x, mine, other, whole_out, flat_out):
-    units = flat_out.shape[1]
-    for z in range(mine.shape[0]):
-        whole_out[2 * z + x] = mine[z]
-        whole_out[2 * z + 1 - x] = other[z]
-        flat_out[2 * z + x] = mine[z, 0:units]
-        flat_out[2 * z + 1 - x] = other[z, 0:units]
+def lat_sum(keep_a, got_a, bias_a, keep_b, got_b, out):
+    one, two = keep_a.shape[1], bias_a.shape[1]
+    out[:, 0:one] = (keep_a[...].astype(F32) + got_a[...].astype(F32)).astype(BF16)
+    out[:, one : one + two] = bias_a[...]
+    out[:, one + two :] = (keep_b[...].astype(F32) + got_b[...].astype(F32)).astype(BF16)
+
+
+def sum_pieces(pieces, out):
+    total = pieces[0].astype(F32)
+    for k in range(1, pieces.shape[0]):
+        total = total + pieces[k].astype(F32)
+    out[...] = total.astype(BF16)
+
+
+def sum_direct(extra, pieces, out):
+    lat = lax.axis_index("lat")
+    units = out.shape[0] - extra
+    total = pieces[0, 0:units].astype(F32)
+    for k in range(1, pieces.shape[0]):
+        total = total + pieces[k, 0:units].astype(F32)
+    out[0:units] = total.astype(BF16)
+    total = pieces[lat, units:].astype(F32)
+    for k in range(1, pieces.shape[0] // 2):
+        total = total + pieces[2 * k + lat, units:].astype(F32)
+    out[units:] = total.astype(BF16)
 
 
 def third_kernel(
     head, lon_tail, lat_head, diag_tail, resid_in, slope, active, mixed,
-    proj_w, up_w, down_w, gains, keep_a, got_a, bias_a,
-    keep_out, give_out, rg_out, dmix_out, gain_out, keep_xa, give_xa,
+    proj_w, up_w, down_w, gains, keep_a,
+    keep_out, give_out, rg_out, dmix_out, gain_out,
     scr_own, scr_oth, m192, m768, mdown, flat_scr,
 ):
-    split_x(lax.rem(lax.axis_index("lon"), 2), keep_a, got_a, bias_a, keep_xa, give_xa)
     rows, width = scr_own.shape
     cut = CHUNK * (WLON // 2)
     scr_own[0:cut, :] = lon_tail[...].astype(F32)
@@ -514,24 +523,15 @@
     )
 
 
-def fourth_kernel(qkv, probs, dmix, field_out, sums_out):
-    width = dmix.shape[-1]
-    sums_out[...] = jnp.zeros(sums_out.shape, F32)
-    attend_back(qkv, probs, dmix, field_out, sums_out, width, 0, probs.shape[0] // 2)
-
-
-def fifth_kernel(
-    x_in, qkv, probs, dmix, rg, gain_two, gains_late, field_in, sums_in, order, qkv_w, gains,
-    tokens_out, own_out, *rest,
+def fourth_kernel(
+    x_in, qkv, probs, dmix, rg, gain_two, gains_late, order, qkv_w, gains,
+    tokens_out, pieces_out,
+    field, sums, m576, flat_scr, dx_scr, bias_scr,
 ):
-    field, sums, m576, flat_scr, dx_scr, bias_scr = rest[-6:]
-    rest = rest[:-6]
     width = x_in.shape[-1]
     levels, lats, lons = tokens_out.shape[:3]
-    done = probs.shape[0] // 2 * WIN
-    field[0:done, :] = field_in[...]
-    sums[...] = sums_in[...]
-    attend_back(qkv, probs, dmix, field, sums, width, probs.shape[0] // 2, probs.shape[0])
+    sums[...] = jnp.zeros(sums.shape, F32)
+    attend_back(qkv, probs, dmix, field, sums, width, 0, probs.shape[0])
     stand1, inv1 = standardize(x_in[...].astype(F32))
     normed = (stand1 * gains[0, 0:1, :]).astype(BF16)
     ng = dot_nt(field[...], qkv_w[0]).astype(BF16).astype(F32)
@@ -542,18 +542,15 @@
     flat_scr[at : at + 3, :] = gain_rows(gain_one, gain_two[...])
     flat_scr[at + 3 : at + 6, :] = gain_rows(gains_late[0:1, :], gains_late[1:2, :])
     bias_units(sums, bias_scr)
-    lat, lon = lax.axis_index("lat"), lax.axis_index("lon")
-    count = (len(rest) + 1) // 2
-    extra = bias_scr.shape[1]
-    units = own_out.shape[0] - extra
-    for k in range(count):
-        to = lax.rem(lon + k, count)
-        same = own_out if k == 0 else rest[k - 1]
-        for out, side in ((same, lat), (rest[count - 1 + k], 1 - lat)):
-            base = (side * count + to) * (units * UNIT)
+    count, extra = bias_scr.shape[:2]
+    units = pieces_out.shape[1] - extra
+    for lon in range(count):
+        for lat in range(2):
+            base = (lat * count + lon) * units * UNIT
             for u in range(units):
-                out[u] = flat_scr[pl.ds(pl.multiple_of(base + u * UNIT, UNIT), UNIT), :].astype(BF16)
-        same[units:] = bias_scr[to]
+                at = base + u * UNIT
+                pieces_out[2 * lon + lat, u] = flat_scr[at : at + UNIT, :].astype(BF16)
+            pieces_out[2 * lon + lat, units:] = bias_scr[lon]
     put(dx_scr, slice(None), rg[...] + part)
     for z in range(levels):
         for a in range(lats):
@@ -562,96 +559,45 @@
             ).astype(BF16)
 
 
-def sum_direct(*refs):
-    out = refs[-1]
-    fulls = [ref for ref in refs[:-1] if ref.shape == out.shape]
-    flats = [ref for ref in refs[:-1] if ref.shape != out.shape]
-    units = flats[0].shape[0]
-    total = fulls[0][...].astype(F32)
-    for ref in fulls[1:]:
-        total = total + ref[...].astype(F32)
-    part = total[0:units]
-    for ref in flats:
-        part = part + ref[...].astype(F32)
-    out[0:units] = part.astype(BF16)
-    out[units:] = total[units:].astype(BF16)
-
-
-def step_one(keep_xa, got_xa, keep_b, got_b, *outs):
-    lon = lax.axis_index("lon")
-    split_x(lax.rem(lon, 2), keep_b, got_b, None, outs[0], outs[1])
-    split_z(lax.div(lon, 2), keep_xa, got_xa, *outs[2:])
-
-
-def step_two(zs, *refs):
-    lon = lax.axis_index("lon")
-    a_in, keep_xb, got_xb = refs[:zs], refs[zs], refs[zs + 1]
-    outs = refs[zs + 2 :]
-    sum_all(*a_in, outs[0])
-    split_z(lax.div(lon, 2), keep_xb, got_xb, *outs[1:])
-
-
-def step_three(zs, fulls, *refs):
-    lon = lax.axis_index("lon")
-    c_in, a_in, b_in = refs[:fulls], refs[fulls : fulls + zs], refs[fulls + zs : fulls + 2 * zs]
-    c_out, a_out, b_out = refs[fulls + 2 * zs :]
-    sum_direct(*c_in, c_out)
-    join_z(lax.div(lon, 2), *a_in, a_out)
-    sum_all(*b_in, b_out)
-
-
-def step_four(zs, mine_a, other_a, *refs):
-    lon = lax.axis_index("lon")
-    b_in = refs[:zs]
-    whole_a, flat_a, join_b = refs[zs:]
-    join_x(lax.rem(lon, 2), mine_a, other_a, whole_a, flat_a)
-    join_z(lax.div(lon, 2), *b_in, join_b)
-
-
-def step_five(mine_b, other_b, whole_b, flat_b):
-    join_x(lax.rem(lax.axis_index("lon"), 2), mine_b, other_b, whole_b, flat_b)
-
-
-def last_kernel(spread, own_a, oth_a, own_b, oth_b, *refs):
-    update_out, bias_out, scr, rows_scr, wide_scr, c_own, c_oth = refs[-7:]
-    pieces = refs[:-7]
-    lat, lon = lax.axis_index("lat"), lax.axis_index("lon")
-    lons = own_a.shape[0]
-    for k in range(lons):
-        at = lax.rem(lon + lons - k, lons)
-        c_own[at] = pieces[k][...]
-        c_oth[at] = pieces[lons + k][...]
-    extra = -(-BIAS_UNITS // lons)
-
-    def place(own, oth, dests):
+def last_kernel(
+    units_a, units_c, extra, spread, pieces_ab, pieces_c, update_out, bias_out,
+    scr, rows_scr, wide_scr,
+):
+    lat = lax.axis_index("lat")
+    lons = pieces_ab.shape[0] // 2
+
+    def place(pieces, first, last, dests):
         total = jnp.zeros((UNIT, 128), F32)
-        per = oth.shape[1]
+        per = last - first
         k = 0
         for where, room in dests:
             for at in range(where, where + room, UNIT):
                 half, j, u = k // (per * lons), k // per % lons, k % per
-                value = jnp.where(lat == half, own[j, u].astype(F32), oth[j, u].astype(F32))
+                value = pieces[2 * j + half, first + u].astype(F32)
                 scr[at : at + UNIT, :] = value
                 total = total + value * value
                 k += 1
         return total
 
-    total = place(own_a, oth_a, [(864, 864), (2016, 288), (3456, 1152), (5760, 1152)])
-    total = total + place(own_b, oth_b, [(1728, 288), (2304, 1152), (4608, 1152)])
-    total = total + place(c_own, c_oth, [(0, 864), (6912, 8)])
+    total = place(
+        pieces_ab, 0, units_a, [(864, 864), (2016, 288), (3456, 1152), (5760, 1152)]
+    )
+    total = total + place(
+        pieces_ab, units_a + extra, pieces_ab.shape[1], [(1728, 288), (2304, 1152), (4608, 1152)]
+    )
+    total = total + place(pieces_c, 0, units_c, [(0, 864), (6912, 8)])
     count = update_out.shape[0]
     mean = jnp.sum(total) * (1.0 / (count * 128))
     scale = lax.rsqrt(mean + 1e-06)
     update_out[...] = (scr[0:count, :] * scale).astype(BF16)
 
-    for b, piece in enumerate((c_own, own_a)):
-        base = piece.shape[1] - extra
+    for b, (piece, base) in enumerate(((pieces_c, units_c), (pieces_ab, units_a))):
 
         def read(at):
             parts = []
             for r in range(CHUNK // UNIT):
                 k = at * (CHUNK // UNIT) + r
-                parts.append(piece[k // extra, base + k % extra].astype(F32))
+                parts.append(piece[k // extra * 2 + lat, base + k % extra].astype(F32))
             return jnp.concatenate(parts, axis=0)
 
         rest = read(2 * HEADS)
@@ -670,13 +616,15 @@
                     bias_out[b, 0, :, at : at + PAIR] = rows_scr[row : row + HEADS, 0:PAIR]
 
 
-def call(kernel, outs, scratch, args, micros, mib):
+def call(kernel, outs, scratch, args, micros, mib, space=pltpu.VMEM):
     return pl.pallas_call(
         kernel,
         out_shape=[jax.ShapeDtypeStruct(shape, dtype) for shape, dtype in outs],
-        in_specs=[pl.BlockSpec(memory_space=pltpu.VMEM)] * len(args),
+        in_specs=[pl.BlockSpec(memory_space=space)] * len(args),
         out_specs=[pl.BlockSpec(memory_space=pltpu.VMEM)] * len(outs),
-        scratch_shapes=[pltpu.VMEM(shape, dtype) for shape, dtype in scratch],
+        scratch_shapes=[
+            pltpu.VMEM(*entry) if isinstance(entry, tuple) else entry for entry in scratch
+        ],
         compiler_params=pltpu.CompilerParams(vmem_limit_bytes=mib * MIB),
         cost_estimate=pl.CostEstimate(
             flops=int(micros * 1.1e9), bytes_accessed=10**5, transcendentals=0
@@ -691,11 +639,6 @@
 def lon_send(value, step):
     count = lax.axis_size("lon")
     return lax.ppermute(value, "lon", [(s, (s + step) % count) for s in range(count)])
-
-
-def x_swap(value):
-    count = lax.axis_size("lon")
-    return lax.ppermute(value, "lon", [(s, s ^ 1) for s in range(count)])
 
 
 def diag_send(value, step):
@@ -762,13 +705,31 @@
             ((rows, hid), BF16),
             ((rows, hid), BF16),
         ],
-        [token_scr, token_scr, tab_scr, rows_scr, wide_scr, bias_shape],
+        [
+            token_scr,
+            token_scr,
+            tab_scr,
+            rows_scr,
+            wide_scr,
+            bias_shape,
+            (cotangent.shape, BF16),
+            ((1,) + table.shape[1:], F32),
+            (spread.shape, BF16),
+            (tokens.shape, BF16),
+            ((1,) + qkv_weight.shape[1:], BF16),
+            (norm_gain.shape, F32),
+            ((1,) + proj_weight.shape[1:], BF16),
+            ((1,) + up_weight.shape[1:], BF16),
+            ((1,) + down_turned.shape[1:], BF16),
+            pltpu.SemaphoreType.DMA((9,)),
+        ],
         (
             tokens, cotangent, table, spread, qkv_weight, proj_weight, up_weight, down_turned,
             norm_gain,
         ),
-        9,
+        8,
         28,
+        pltpu.HBM,
     )
     lon_head = lon_send(head, -1)
     diag_head = diag_send(head, -1)
@@ -822,7 +783,7 @@
     )
     got_a = lat_swap(give_a)
 
-    keep_b, give_b, rg0, dmix0, gain_two, keep_xa, give_xa = call(
+    keep_b, give_b, rg0, dmix0, gain_two = call(
         third_kernel,
         [
             units(lon_size, units_b),
@@ -830,45 +791,29 @@
             (token, F32),
             (token, BF16),
             ((1, width), F32),
-            units(zs, units_a + extra),
-            units(zs, units_a + extra),
         ],
         [(token, F32), (token, F32), m192, m768, mdown, flat_scr(units_b)],
         (
             dhead, lon_tail, lat_dhead, diag_tail, resid0, slope0, active0, mixed0,
-            proj_weight, up_weight, down_turned, norm_gain, keep_a, got_a, bias_a,
+            proj_weight, up_weight, down_turned, norm_gain, keep_a,
         ),
-        3,
+        2,
         20,
     )
     got_b = lat_swap(give_b)
-    got_xa = x_swap(give_xa)
-
-    field0, sums0 = call(
-        fourth_kernel,
-        [((wins // 2 * WIN, 3 * width), BF16), sums_shape],
+    (part_ab,) = call(
+        lat_sum,
+        [units(lon_size, units_a + extra + units_b)],
         [],
-        (qkv0, probs0, dmix0),
-        6,
-        20,
-    )
-    stepped = call(
-        step_one,
-        [units(zs, units_b)] * 2 + [units(units_a + extra)] * zs,
-        [],
-        (keep_xa, got_xa, keep_b, got_b),
+        (keep_a, got_a, bias_a, keep_b, got_b),
         1,
         10,
     )
-    keep_xb, give_xb = stepped[:2]
-    own_a, gives_a = stepped[2], stepped[3:]
-    got_xb = x_swap(give_xb)
-    gots_a = [lon_send(give, 2 * (k + 1)) for k, give in enumerate(gives_a)]
-
-    fulls, flats = [units(units_c + extra)] * lon_size, [units(units_c)] * lon_size
-    finished = call(
-        fifth_kernel,
-        [(tokens.shape, BF16)] + fulls + flats,
+    pieces_ab = lax.all_to_all(part_ab, "lon", 0, 0)
+
+    tokens_grad, pieces_c = call(
+        fourth_kernel,
+        [(tokens.shape, BF16), units(2 * lon_size, units_c + extra)],
         [
             field_shape,
             sums_shape,
@@ -878,79 +823,28 @@
             units(lon_size, extra),
         ],
         (
-            x0, qkv0, probs0, dmix0, rg0, gain_two, gains1, field0, sums0, own_a, qkv_weight,
-            norm_gain,
+            x0, qkv0, probs0, dmix0, rg0, gain_two, gains1, part_ab, qkv_weight, norm_gain,
         ),
-        7,
+        11,
         24,
     )
-    tokens_grad = finished[0]
-    same, cross = finished[1 : 1 + lon_size], finished[1 + lon_size :]
-
-    def spread_direct(same, cross):
-        fulls = [same[0]] + [lon_send(same[k], k) for k in range(1, lon_size)]
-        flats = [lat_swap(cross[0])] + [diag_send(cross[k], k) for k in range(1, lon_size)]
-        return fulls + flats
-
-    gots_c = spread_direct(same, cross)
-
-    stepped = call(
-        functools.partial(step_two, zs),
-        [units(units_a + extra)] + [units(units_b)] * zs,
-        [],
-        (own_a, *gots_a, keep_xb, got_xb),
-        1,
-        10,
-    )
-    sum_a, own_b, gives_b = stepped[0], stepped[1], stepped[2:]
-    gots_b = [lon_send(give, 2 * (k + 1)) for k, give in enumerate(gives_b)]
-    all_a = [sum_a] + [lon_send(sum_a, 2 * k) for k in range(1, zs)]
-
-    sum_c, join_a, sum_b = call(
-        functools.partial(step_three, zs, 2 * lon_size),
-        [units(units_c + extra), units(zs, units_a + extra), units(units_b)],
-        [],
-        (*gots_c, *all_a, own_b, *gots_b),
-        1,
-        10,
-    )
-    flat_c = sum_c[:units_c]
-    pieces_c = spread_direct([sum_c] * lon_size, [flat_c] * lon_size)
-    all_b = [sum_b] + [lon_send(sum_b, 2 * k) for k in range(1, zs)]
-    other_a = x_swap(join_a)
-
-    whole_a, flat_a, join_b = call(
-        functools.partial(step_four, zs),
-        [units(lon_size, units_a + extra), units(lon_size, units_a), units(zs, units_b)],
-        [],
-        (join_a, other_a, *all_b),
-        1,
-        10,
-    )
-    oth_a = lat_swap(flat_a)
-    other_b = x_swap(join_b)
-    whole_b, flat_b = call(
-        step_five,
-        [units(lon_size, units_b), units(lon_size, units_b)],
-        [],
-        (join_b, other_b),
-        1,
-        10,
-    )
-    oth_b = lat_swap(flat_b)
+    got_c = lax.all_to_all(pieces_c, ("lon", "lat"), 0, 0)
+
+    (sum_ab,) = call(sum_pieces, [units(units_a + extra + units_b)], [], (pieces_ab,), 1, 10)
+    whole_ab = lax.all_gather(sum_ab, ("lon", "lat"))
+    (sum_c,) = call(
+        functools.partial(sum_direct, extra), [units(units_c + extra)], [], (got_c,), 1, 10
+    )
+    whole_c = lax.all_to_all(
+        jnp.broadcast_to(sum_c[None], (2 * lon_size,) + sum_c.shape), ("lon", "lat"), 0, 0
+    )
 
     flat_rows = (2 * block_rows * 128 + norm_gain.size) // 128
     update, bias_grad = call(
-        last_kernel,
+        functools.partial(last_kernel, units_a, units_c, extra),
         [((flat_rows, 128), BF16), (bias_table.shape, F32)],
-        [
-            ((flat_rows + 2, 128), F32),
-            ((CHUNK * 8, PAIR), F32),
-            wide_scr,
-            units(lon_size, units_c + extra),
-            units(lon_size, units_c),
-        ],
-        (spread, whole_a, oth_a, whole_b, oth_b, *pieces_c),
+        [((flat_rows + 2, 128), F32), ((CHUNK * 8, PAIR), F32), wide_scr],
+        (spread, whole_ab, whole_c),
         3,
         20,
     )

time: 169 us -> 150 us (0.89)
  blocking collectives: 0 us -> 59.9 us
  starting transfers between devices: 63 us -> 7.77 us
  waiting for transfers between devices: 52.1 us -> 9.29 us
  between operations: 0.88 us -> 14.2 us
  local copies, waits for them, and re-layouts: 9.65 us -> 13.2 us
  Pallas kernels: 43.3 us -> 45.1 us
    all_to_all x0 -> x3, blocking collectives: none -> 59.9 us  [the longest x1 25.9 us: shards(): pieces_ab = lax.all_to_all(part_ab, 'lon', 0, 0)]
    ppermute x28 -> x2, starting transfers between devices: 36.9 us -> 0.77 us  [lon_send(): lax.ppermute(value, 'lon', [(s, (s + step) % count) for s in range(count)])]
    ppermute x28 -> x2, waiting for transfers between devices: 25.1 us -> 2.82 us  [lon_send(): lax.ppermute(value, 'lon', [(s, (s + step) % count) for s in range(count)])]
    ppermute x16 -> x2, starting transfers between devices: 23.3 us -> 5.75 us  [diag_send(): return lax.ppermute(value, ('lon', 'lat'), pairs)]
    ppermute x16 -> x2, waiting for transfers between devices: 18.3 us -> 4.81 us  [diag_send(): return lax.ppermute(value, ('lon', 'lat'), pairs)]
    ppermute x4 -> x0, waiting for transfers between devices: 8.73 us -> none  [x_swap(): return lax.ppermute(value, 'lon', [(s, s ^ 1) for s in range(count)])]
    unnamed x33 -> x39, local copies, waits for them, and re-layouts: 9.65 us -> 13.1 us
    pallas_call x13 -> x10, Pallas kernels: 43.3 us -> 45.1 us  [call(): pl.pallas_call(kernel, out_shape=[jax.ShapeDtypeStruct(shape, dtype) for...]
  transfers between devices with their start and end apart: 56 -> 9, of which waited for: 24 -> 5; matrix products, arithmetic and copies ran while one was open for 0% -> 0% of each run, Pallas kernels for 7% -> 10%
where the time goes in v3:
time: 150 us; the launch traced here: 149 us
  blocking collectives  59.9 us (40%)
  Pallas kernels  45.1 us (30%)
  between operations  14.2 us (9%)
  local copies, waits for them, and re-layouts  13.2 us (9%)
  waiting for transfers between devices  9.29 us (6%)
  starting transfers between devices  7.77 us (5%)
    pallas_call x10, Pallas kernels, call(): pl.pallas_call(kernel, out_shape=[jax.ShapeDtypeStruct(shape, dtype) for...  45.1 us
    all_to_all x1, blocking collectives, shards(): pieces_ab = lax.all_to_all(part_ab, 'lon', 0, 0)  25.9 us
    all_to_all x1, blocking collectives, shards(): lax.all_to_all(jnp.broadcast_to(sum_c[None], (2 * lon_size,) + sum_c.shap...  18.8 us
    all_to_all x1, blocking collectives, shards(): got_c = lax.all_to_all(pieces_c, ('lon', 'lat'), 0, 0)  15.2 us
    unnamed x39, local copies, waits for them, and re-layouts  13.1 us
    ppermute x2, starting transfers between devices, diag_send(): return lax.ppermute(value, ('lon', 'lat'), pairs)  5.75 us
    ppermute x2, waiting for transfers between devices, diag_send(): return lax.ppermute(value, ('lon', 'lat'), pairs)  4.81 us
  transfers between devices with their start and end apart: 9, of which 5 were waited for; matrix products, arithmetic and copies ran while one was open for 0% of the time, Pallas kernels for 10%

profile of v3, /device:TPU:0, one launch (start us, length us, event | category | flops | bytes accessed | tf_op | source)
XLA Modules:
  0.0 149.5 jit_solution(699822528139499389)
XLA Ops:
  7.2 0.0 all-gather.3.cloned.1.call-start
  7.2 0.0 copy-start.1
  7.2 1.1 copy-done.1
  8.3 1.1 copy-done.3
  9.3 1.0 copy-done.5
  10.4 1.0 copy-done.7
  11.3 1.0 copy-done.9
  12.3 1.0 copy-done.10
  13.3 0.9 copy-done.11
  14.2 0.7 copy-done.13
  14.9 0.9 copy-done.15
  15.8 9.0 %shard_map.112 = (bf16[576,192]{1,0:T(8,128)(2,1)S(1)}, bf16[2,504,192]{2,1,0:T(8,128)(2,1)S(1)}, bf16[2,72,192]{2,1,0:T(8,128)(2,1)S(1)}, bf16[576,576]{1,0:T(8...) custom-call(bf16[2,12,24,192]{3,2,1,0:T(8,128)(2,1)S(1)} %copy-done., ...), custom_call_target="tpu_custom_call" | custom-call | flops 8800000000 | bytes 100000 | tf_op jit(solution)/shard_map/pallas_call | solution.py:620
  24.9 0.0 copy-start.17
  24.9 0.5 collective-permute-start.1
  25.4 0.0 copy-start.14
  25.4 5.7 %collective-permute-start.2 = (bf16[2,72,192]{2,1,0:T(8,128)(2,1)S(1)}, bf16[2,72,192]{2,1,0:T(8,128)(2,1)S(1)}, u32[]{:S(2)}, u32[]{:S(2)}) collective-permute-start(bf16[2,72,192]{2,1,0:T(8,128)(2,1)S(1)} %get-tuple-element.40), channel_id=1, source_target_pairs={{0,15},{1,14},{2,1},{3,0},{4,3},{5,2},{6,5},{7,4},{8,7},{9,6},{10,... | collective-permute-start | bytes 165896 | tf_op jit(solution)/shard_map/ppermute | solution.py:650
  31.1 0.5 collective-permute-start
  31.6 0.9 shard_map.113.bias
  32.6 1.2 collective-permute-done.2.diag_head
  33.7 1.7 %collective-permute-done.lon_head = bf16[2,72,192]{2,1,0:T(8,128)(2,1)S(1)} collective-permute-done((bf16[2,72,192]{2,1,0:T(8,128)(2,1)S(1)}, bf16[2,72,192]{2,1,0:T(8,128)(2,1)S(1)}, u32[]{:S(2)}, u32[]{:S(2)}) %collective-permute-start) | collective-permute-done | bytes 55328 | tf_op jit(solution)/shard_map/ppermute | solution.py:641
  35.5 0.0 collective-permute-done.1.lat_tail
  35.5 0.0 copy-done.4
  35.5 0.0 copy-done.6
  35.5 17.1 %shard_map.114 = (bf16[504,192]{1,0:T(8,128)(2,1)S(1)}, bf16[72,192]{1,0:T(8,128)(2,1)S(1)}, bf16[576,192]{1,0:T(8,128)(2,1)S(1)}, bf16[576,576]{1,0:T(8,128)(2,...) custom-call(bf16[2,504,192]{2,1,0:T(8,128)(2,1)S(1)} %get-tuple-elem, ...), custom_call_target="tpu_custom_call" | custom-call | flops 20899999744 | bytes 100000 | tf_op jit(solution)/shard_map/pallas_call | solution.py:620
  52.6 0.1 collective-permute-start.5
  52.6 0.2 collective-permute-start.3
  52.9 0.1 collective-permute-start.4
  53.0 1.6 %shard_map.115 = (bf16[8,27,8,128]{3,2,1,0:T(8,128)(2,1)S(1)}, bf16[8,27,8,128]{3,2,1,0:T(8,128)(2,1)S(1)}, bf16[8,5,8,128]{3,2,1,0:T(8,128)(2,1)S(1)}) custom-call(bf16[576,192]{1,0:T(8,128)(2,1)S(1)} %get-tuple-element.47.n1, bf16[576,576]{1,0:T(8,128)(2,1)S(1)} %get-tuple-element.48.field, bf16[576,192]{1,0:T(8,128)(2,1)S(1)} %get-tuple-element.49.mixed, ...), custom_call_target="tpu_custom_call" | custom-call | flops 3300000000 | bytes 100000 | tf_op jit(solution)/shard_map/pallas_call | solution.py:620
  54.6 0.6 collective-permute-start.6
  55.2 3.7 %collective-permute-done.5.diag_tail = bf16[72,192]{1,0:T(8,128)(2,1)S(1)} collective-permute-done((bf16[72,192]{1,0:T(8,128)(2,1)S(1)}, bf16[72,192]{1,0:T(8,128)(2,1)S(1)}, u32[]{:S(2)}, u32[]{:S(2)}) %collective-permute-start.5) | collective-permute-done | bytes 27680 | tf_op jit(solution)/shard_map/ppermute | solution.py:650
  58.8 1.1 collective-permute-done.3.lon_tail
  59.9 0.0 collective-permute-done.4.lat_head
  59.9 2.2 %shard_map.116 = (bf16[8,21,8,128]{3,2,1,0:T(8,128)(2,1)S(1)}, bf16[8,21,8,128]{3,2,1,0:T(8,128)(2,1)S(1)}, f32[576,192]{1,0:T(8,128)S(1)}, bf16[576,192]{1,0:T(8,128)(2,1)S(1)}, f32[1,192]{1,0:T(1,128)S(1)}) custom-call(bf16[504,192]{1,0:T(8,128)(2,1)S(1)} %get-tuple-element.41.head, bf16[72,192]{1,0:T(8,128)(2,1)S(1)} %collective-permute-done.3.lon_tail, ...), custom_call_target="tpu_custom_call" | custom-call | flops 2200000000 | bytes 100000 | tf_op jit(solution)/shard_map/pallas_call | solution.py:620
  62.1 0.1 collective-permute-start.7
  62.1 0.0 collective-permute-done.6.got_a
  62.2 1.6 %collective-permute-done.7.got_b = bf16[8,21,8,128]{3,2,1,0:T(8,128)(2,1)S(1)} collective-permute-done((bf16[8,21,8,128]{3,2,1,0:T(8,128)(2,1)S(1)}, bf16[8,21,8,128]{3,2,1,0:T(8,128)(2,1)S(1)}, u32[]{:S(2)}, u32[]{:S(2)}) %collective-permute-start.7) | collective-permute-done | bytes 344096 | tf_op jit(solution)/shard_map/ppermute | solution.py:636
  63.8 0.2 shard_map.117.order
  64.0 25.9 %all_to_all.15.pieces = bf16[8,53,8,128]{3,2,1,0:T(8,128)(2,1)S(1)} all-to-all(bf16[8,53,8,128]{3,2,1,0:T(8,128)(2,1)S(1)} %shard_map.117.order), channel_id=1, replica_groups=mesh['grp'=2,'lon'=8,'lat'=2] {'lon'}, dimensions={0} | all-to-all | bytes 1736704 | tf_op jit(solution)/shard_map/all_to_all | solution.py:812
  89.9 0.8 shard_map.119
  90.7 0.0 all-gather.3.cloned.1.call-update
  90.7 2.0 %copy-done.18 = f32[4,6,144,144]{3,2,1,0:T(8,128)S(1)} copy-done((f32[4,6,144,144]{3,2,1,0:T(8,128)S(1)}, f32[4,6,144,144]{3,2,1,0:T(8,128)}, u32[]{:S(2)}) %copy-start.18) | copy-done | bytes 1990680
  92.7 10.9 %shard_map.118 = (bf16[2,12,24,192]{3,2,1,0:T(8,128)(2,1)}, bf16[16,12,8,128]{3,2,1,0:T(8,128)(2,1)S(1)}) custom-call(bf16[576,192]{1,0:T(8,128)(2,1)S(1)} %get-tuple-element.36.x_in, bf16[576,576]{1,0:T(8,128)(2,1)S(1)} %get-tuple-element.37.qkv, f32[4,6,144,144]{3,2,1,0:T(8,128)S(1)} %copy-done.18, bf16[576,192]{1,0:T(8,128)(2,1)S(1)} %get-tuple-element.57.dmix, ...), custom_call_target="tpu_custom_call" | custom-call | flops 12099999744 | bytes 100000 | tf_op jit(solution)/shard_map/pallas_call | solution.py:620
  103.6 15.2 %all_to_all.16.pieces = bf16[16,12,8,128]{3,2,1,0:T(8,128)(2,1)S(1)} all-to-all(bf16[16,12,8,128]{3,2,1,0:T(8,128)(2,1)S(1)} %get-tuple-element.66), channel_id=1, replica_groups=mesh['grp'=2,'lon'=8,'lat'=2] {'lon','lat'}, dimensions={0} | all-to-all | bytes 786432 | tf_op jit(solution)/shard_map/all_to_all | solution.py:831
  118.9 0.1 broadcast_in_dim.2
  118.9 18.8 %all_to_all.17.pieces_c = bf16[16,12,8,128]{3,2,1,0:T(8,128)(2,1)S(1)} all-to-all(bf16[16,12,8,128]{3,2,1,0:T(8,128)(2,1)S(1)} %broadcast_in_dim.2), channel_id=1, replica_groups=mesh['grp'=2,'lon'=8,'lat'=2] {'lon','lat'}, dimensions={0} | all-to-all | bytes 786432 | tf_op jit(solution)/shard_map/all_to_all | solution.py:838
  137.7 1.5 copy-done
  139.2 2.4 %shard_map.121 = (bf16[6918,128]{1,0:T(8,128)(2,1)}, f32[2,1,6,6336]{3,2,1,0:T(8,128)S(1)}) custom-call(bf16[2,132,384]{2,1,0:T(8,128)(2,1)S(1)} %copy-done.16, bf16[16,53,8,128]{3,2,1,0:T(8,128)(2,1)S(1)} %bitcast.4, bf16[16,12,8,128]{3,2,1,0:T(8,128)(2,1)S(1)} %all_to_all.17.pieces_c), custom_call_target="tpu_custom_call" | custom-call | flops 3300000000 | bytes 100000 | tf_op jit(solution)/shard_map/pallas_call | solution.py:620
  141.6 1.0 copy.13
  (24 shorter events, 0.1 us)
Async XLA Ops:
  7.2 130.6 %all-gather.3.cloned.1.call-start = ((), (), s32[]{:S(2)}) async-start(), calls=%async_computation.3 | async-start | bytes 1845248 | tf_op jit(solution)/shard_map/all_gather | solution.py:834
  7.2 1.1 copy-start.1
  8.3 1.1 copy-start.3
  9.3 1.0 copy-start.5
  10.4 1.0 copy-start.7
  11.3 1.0 copy-start.9
  12.3 1.0 copy-start.10
  13.3 0.9 copy-start.11
  14.2 0.7 copy-start.13
  14.9 0.9 copy-start.15
  15.8 15.8 %copy-start.8 = (f32[2,1,6,6336]{3,1,2,0:T(1,128)S(1)}, f32[2,1,6,6336]{3,1,2,0:T(1,128)}, u32[]{:S(2)}) copy-start(f32[2,1,6,6336]{3,1,2,0:T(1,128)} %param.16) | copy-start | bytes 912388
  15.8 15.8 %copy-start.16 = (bf16[2,132,384]{2,1,0:T(8,128)(2,1)S(1)}, bf16[2,132,384]{2,1,0:T(8,128)(2,1)}, u32[]{:S(2)}) copy-start(bf16[2,132,384]{2,1,0:T(8,128)(2,1)} %constant.2.clone.spread_in.spread) | copy-start | bytes 608260
  24.9 7.7 %copy-start.17 = (f32[4,6,144,144]{3,2,1,0:T(8,128)}, f32[4,6,144,144]{3,2,1,0:T(8,128)S(1)}, u32[]{:S(2)}) copy-start(f32[4,6,144,144]{3,2,1,0:T(8,128)S(1)} %get-tuple-element.38.probs) | copy-start | bytes 5971972
  24.9 10.6 %collective-permute-start.1 = (bf16[2,504,192]{2,1,0:T(8,128)(2,1)S(1)}, bf16[2,504,192]{2,1,0:T(8,128)(2,1)S(1)}, u32[]{:S(2)}, u32[]{:S(2)}) collective-permute-start(bf16[2,504,192]{2,1,0:T(8,128)(2,1)S(1)} %get-tuple-element.39.tail), channel_id=1, source_target_pairs={{0,1},{1,0},{2,3},{3,2},{4,5},{5,4},{6,7},{7,6},{8,9},{9,8},{10,11... | collective-permute-start | bytes 1161224 | tf_op jit(solution)/shard_map/ppermute | solution.py:636
  25.4 10.1 %copy-start.2 = (bf16[2,192,768]{2,1,0:T(8,128)(2,1)S(1)}, bf16[2,192,768]{2,1,0:T(8,128)(2,1)}, u32[]{:S(2)}) copy-start(bf16[2,192,768]{2,1,0:T(8,128)(2,1)} %up_w.3) | copy-start | bytes 1769476
  25.4 10.1 %copy-start.4 = (bf16[2,768,192]{1,2,0:T(8,128)(2,1)S(1)}, bf16[2,768,192]{1,2,0:T(8,128)(2,1)}, u32[]{:S(2)}) copy-start(bf16[2,768,192]{1,2,0:T(8,128)(2,1)} %param.14) | copy-start | bytes 1769476
  25.4 10.1 %copy-start.6 = (bf16[2,192,576]{2,1,0:T(8,128)(2,1)S(1)}, bf16[2,192,576]{2,1,0:T(8,128)(2,1)}, u32[]{:S(2)}) copy-start(bf16[2,192,576]{2,1,0:T(8,128)(2,1)} %qkv_w.3) | copy-start | bytes 1327108
  25.4 10.1 %copy-start.12 = (bf16[2,192,192]{2,1,0:T(8,128)(2,1)S(1)}, bf16[2,192,192]{2,1,0:T(8,128)(2,1)}, u32[]{:S(2)}) copy-start(bf16[2,192,192]{2,1,0:T(8,128)(2,1)} %proj_w.3) | copy-start | bytes 442372
  25.4 10.1 %copy-start.14 = (f32[2,2,192]{2,1,0:T(2,128)S(1)}, f32[2,2,192]{2,1,0:T(2,128)}, u32[]{:S(2)}) copy-start(f32[2,2,192]{2,1,0:T(2,128)} %gains.5) | copy-start | bytes 9220
  25.4 8.3 %collective-permute-start.2 = (bf16[2,72,192]{2,1,0:T(8,128)(2,1)S(1)}, bf16[2,72,192]{2,1,0:T(8,128)(2,1)S(1)}, u32[]{:S(2)}, u32[]{:S(2)}) collective-permute-start(bf16[2,72,192]{2,1,0:T(8,128)(2,1)S(1)} %get-tuple-element.40), channel_id=1, source_target_pairs={{0,15},{1,14},{2,1},{3,0},{4,3},{5,2},{6,5},{7,4},{8,7},{9,6},{10,... | collective-permute-start | bytes 165896 | tf_op jit(solution)/shard_map/ppermute | solution.py:650
  31.1 4.4 %collective-permute-start = (bf16[2,72,192]{2,1,0:T(8,128)(2,1)S(1)}, bf16[2,72,192]{2,1,0:T(8,128)(2,1)S(1)}, u32[]{:S(2)}, u32[]{:S(2)}) collective-permute-start(bf16[2,72,192]{2,1,0:T(8,128)(2,1)S(1)} %get-tuple-element.40), channel_id=1, source_target_pairs={{0,14},{2,0},{4,2},{6,4},{8,6},{10,8},{12,10},{14,12},{1,15},{3,1}... | collective-permute-start | bytes 165896 | tf_op jit(solution)/shard_map/ppermute | solution.py:641
  52.6 6.2 %collective-permute-start.5 = (bf16[72,192]{1,0:T(8,128)(2,1)S(1)}, bf16[72,192]{1,0:T(8,128)(2,1)S(1)}, u32[]{:S(2)}, u32[]{:S(2)}) collective-permute-start(bf16[72,192]{1,0:T(8,128)(2,1)S(1)} %get-tuple-element.42), channel_id=1, source_target_pairs={{0,3},{1,2},{2,5},{3,4},{4,7},{5,6},{6,9},{7,8},{8,11},{9,10},{10,... | collective-permute-start | bytes 82952 | tf_op jit(solution)/shard_map/ppermute | solution.py:650
  52.6 7.3 %collective-permute-start.3 = (bf16[72,192]{1,0:T(8,128)(2,1)S(1)}, bf16[72,192]{1,0:T(8,128)(2,1)S(1)}, u32[]{:S(2)}, u32[]{:S(2)}) collective-permute-start(bf16[72,192]{1,0:T(8,128)(2,1)S(1)} %get-tuple-element.42), channel_id=1, source_target_pairs={{0,2},{2,4},{4,6},{6,8},{8,10},{10,12},{12,14},{14,0},{1,3},{3,5},... | collective-permute-start | bytes 82952 | tf_op jit(solution)/shard_map/ppermute | solution.py:641
  52.9 7.0 %collective-permute-start.4 = (bf16[504,192]{1,0:T(8,128)(2,1)S(1)}, bf16[504,192]{1,0:T(8,128)(2,1)S(1)}, u32[]{:S(2)}, u32[]{:S(2)}) collective-permute-start(bf16[504,192]{1,0:T(8,128)(2,1)S(1)} %get-tuple-element.41.head), channel_id=1, source_target_pairs={{0,1},{1,0},{2,3},{3,2},{4,5},{5,4},{6,7},{7,6},{8,9},{9,8},{10,11... | collective-permute-start | bytes 580616 | tf_op jit(solution)/shard_map/ppermute | solution.py:636
  54.6 7.5 %collective-permute-start.6 = (bf16[8,27,8,128]{3,2,1,0:T(8,128)(2,1)S(1)}, bf16[8,27,8,128]{3,2,1,0:T(8,128)(2,1)S(1)}, u32[]{:S(2)}, u32[]{:S(2)}) collective-permute-start(bf16[8,27,8,128]{3,2,1,0:T(8,128)(2,1)S(1)} %get-tuple-element.61), channel_id=1, source_target_pairs={{0,1},{1,0},{2,3},{3,2},{4,5},{5,4},{6,7},{7,6},{8,9},{9,8},{10,11... | collective-permute-start | bytes 1327112 | tf_op jit(solution)/shard_map/ppermute | solution.py:636
  62.1 1.7 %collective-permute-start.7 = (bf16[8,21,8,128]{3,2,1,0:T(8,128)(2,1)S(1)}, bf16[8,21,8,128]{3,2,1,0:T(8,128)(2,1)S(1)}, u32[]{:S(2)}, u32[]{:S(2)}) collective-permute-start(bf16[8,21,8,128]{3,2,1,0:T(8,128)(2,1)S(1)} %get-tuple-element.64), channel_id=1, source_target_pairs={{0,1},{1,0},{2,3},{3,2},{4,5},{5,4},{6,7},{7,6},{8,9},{9,8},{10,11... | collective-permute-start | bytes 1032200 | tf_op jit(solution)/shard_map/ppermute | solution.py:636
  90.7 2.0 %copy-start.18 = (f32[4,6,144,144]{3,2,1,0:T(8,128)S(1)}, f32[4,6,144,144]{3,2,1,0:T(8,128)}, u32[]{:S(2)}) copy-start(f32[4,6,144,144]{3,2,1,0:T(8,128)} %copy-done.17) | copy-start | bytes 5971972
  137.7 1.5 copy-start
Sparse Core Ops, SparseCore 0:
  90.8 39.3 all-gather.2

commit v4 on v3

--- a/solution.py
+++ b/solution.py
@@ -459,24 +459,18 @@
     out[:, one + two :] = (keep_b[...].astype(F32) + got_b[...].astype(F32)).astype(BF16)
 
 
-def sum_pieces(pieces, out):
+def lat_sum_late(keep, got, bias, out):
+    one = keep.shape[1]
+    out[:, 0:one] = (keep[...].astype(F32) + got[...].astype(F32)).astype(BF16)
+    out[:, one:] = bias[...]
+
+
+def sum_pieces(pieces, order, out):
     total = pieces[0].astype(F32)
     for k in range(1, pieces.shape[0]):
         total = total + pieces[k].astype(F32)
-    out[...] = total.astype(BF16)
-
-
-def sum_direct(extra, pieces, out):
-    lat = lax.axis_index("lat")
-    units = out.shape[0] - extra
-    total = pieces[0, 0:units].astype(F32)
-    for k in range(1, pieces.shape[0]):
-        total = total + pieces[k, 0:units].astype(F32)
-    out[0:units] = total.astype(BF16)
-    total = pieces[lat, units:].astype(F32)
-    for k in range(1, pieces.shape[0] // 2):
-        total = total + pieces[2 * k + lat, units:].astype(F32)
-    out[units:] = total.astype(BF16)
+    for k in range(out.shape[0]):
+        out[k] = total.astype(BF16)
 
 
 def third_kernel(
@@ -524,13 +518,21 @@
 
 
 def fourth_kernel(
-    x_in, qkv, probs, dmix, rg, gain_two, gains_late, order, qkv_w, gains,
-    tokens_out, pieces_out,
-    field, sums, m576, flat_scr, dx_scr, bias_scr,
+    x_in, qkv, probs_in, dmix, rg, gain_two, gains_late, order, qkv_w, gains,
+    tokens_out, keep, give, bias_out,
+    field, sums, m576, flat_scr, dx_scr, probs, sems,
 ):
+    copies = [
+        pltpu.make_async_copy(probs_in.at[w], probs.at[w], sems.at[w])
+        for w in range(probs.shape[0])
+    ]
+    for copy in copies:
+        copy.start()
     width = x_in.shape[-1]
     levels, lats, lons = tokens_out.shape[:3]
     sums[...] = jnp.zeros(sums.shape, F32)
+    for copy in copies:
+        copy.wait()
     attend_back(qkv, probs, dmix, field, sums, width, 0, probs.shape[0])
     stand1, inv1 = standardize(x_in[...].astype(F32))
     normed = (stand1 * gains[0, 0:1, :]).astype(BF16)
@@ -541,16 +543,8 @@
     flat_scr[at:, :] = jnp.zeros((flat_scr.shape[0] - at, 128), F32)
     flat_scr[at : at + 3, :] = gain_rows(gain_one, gain_two[...])
     flat_scr[at + 3 : at + 6, :] = gain_rows(gains_late[0:1, :], gains_late[1:2, :])
-    bias_units(sums, bias_scr)
-    count, extra = bias_scr.shape[:2]
-    units = pieces_out.shape[1] - extra
-    for lon in range(count):
-        for lat in range(2):
-            base = (lat * count + lon) * units * UNIT
-            for u in range(units):
-                at = base + u * UNIT
-                pieces_out[2 * lon + lat, u] = flat_scr[at : at + UNIT, :].astype(BF16)
-            pieces_out[2 * lon + lat, units:] = bias_scr[lon]
+    bias_units(sums, bias_out)
+    halves(flat_scr, lax.axis_index("lat"), keep, give)
     put(dx_scr, slice(None), rg[...] + part)
     for z in range(levels):
         for a in range(lats):
@@ -560,44 +554,47 @@
 
 
 def last_kernel(
-    units_a, units_c, extra, spread, pieces_ab, pieces_c, update_out, bias_out,
-    scr, rows_scr, wide_scr,
+    units_a, units_c, extra, spread, own_ab, oth_ab, own_c, oth_c, update_out, bias_out,
+    scr, rows_scr, wide_scr, tab_scr,
 ):
     lat = lax.axis_index("lat")
-    lons = pieces_ab.shape[0] // 2
-
-    def place(pieces, first, last, dests):
+    lons = own_ab.shape[0]
+
+    def place(own, oth, first, last, dests):
         total = jnp.zeros((UNIT, 128), F32)
         per = last - first
         k = 0
         for where, room in dests:
             for at in range(where, where + room, UNIT):
                 half, j, u = k // (per * lons), k // per % lons, k % per
-                value = pieces[2 * j + half, first + u].astype(F32)
+                value = jnp.where(
+                    lat == half, own[j, first + u].astype(F32), oth[j, first + u].astype(F32)
+                )
                 scr[at : at + UNIT, :] = value
                 total = total + value * value
                 k += 1
         return total
 
     total = place(
-        pieces_ab, 0, units_a, [(864, 864), (2016, 288), (3456, 1152), (5760, 1152)]
+        own_ab, oth_ab, 0, units_a, [(864, 864), (2016, 288), (3456, 1152), (5760, 1152)]
     )
     total = total + place(
-        pieces_ab, units_a + extra, pieces_ab.shape[1], [(1728, 288), (2304, 1152), (4608, 1152)]
-    )
-    total = total + place(pieces_c, 0, units_c, [(0, 864), (6912, 8)])
+        own_ab, oth_ab, units_a + extra, own_ab.shape[1],
+        [(1728, 288), (2304, 1152), (4608, 1152)],
+    )
+    total = total + place(own_c, oth_c, 0, units_c, [(0, 864), (6912, 8)])
     count = update_out.shape[0]
     mean = jnp.sum(total) * (1.0 / (count * 128))
     scale = lax.rsqrt(mean + 1e-06)
     update_out[...] = (scr[0:count, :] * scale).astype(BF16)
 
-    for b, (piece, base) in enumerate(((pieces_c, units_c), (pieces_ab, units_a))):
+    for b, (piece, base) in enumerate(((own_c, units_c), (own_ab, units_a))):
 
         def read(at):
             parts = []
             for r in range(CHUNK // UNIT):
                 k = at * (CHUNK // UNIT) + r
-                parts.append(piece[k // extra * 2 + lat, base + k % extra].astype(F32))
+                parts.append(piece[k // extra, base + k % extra].astype(F32))
             return jnp.concatenate(parts, axis=0)
 
         rest = read(2 * HEADS)
@@ -613,14 +610,17 @@
                 for ai in range(WLAT):
                     at = ((zi * LEVELS + zj) * WLAT + ai) * PAIR
                     row = (zi * WLAT + ai) * 8
-                    bias_out[b, 0, :, at : at + PAIR] = rows_scr[row : row + HEADS, 0:PAIR]
-
-
-def call(kernel, outs, scratch, args, micros, mib, space=pltpu.VMEM):
+                    tab_scr[0:HEADS, at : at + PAIR] = rows_scr[row : row + HEADS, 0:PAIR]
+        for h in range(HEADS):
+            bias_out[b, h] = tab_scr[h : h + 1, :]
+
+
+def call(kernel, outs, scratch, args, micros, mib, spaces=None):
+    spaces = spaces or [pltpu.VMEM] * len(args)
     return pl.pallas_call(
         kernel,
         out_shape=[jax.ShapeDtypeStruct(shape, dtype) for shape, dtype in outs],
-        in_specs=[pl.BlockSpec(memory_space=space)] * len(args),
+        in_specs=[pl.BlockSpec(memory_space=space) for space in spaces],
         out_specs=[pl.BlockSpec(memory_space=pltpu.VMEM)] * len(outs),
         scratch_shapes=[
             pltpu.VMEM(*entry) if isinstance(entry, tuple) else entry for entry in scratch
@@ -723,13 +723,16 @@
             ((1,) + down_turned.shape[1:], BF16),
             pltpu.SemaphoreType.DMA((9,)),
         ],
-        (
-            tokens, cotangent, table, spread, qkv_weight, proj_weight, up_weight, down_turned,
-            norm_gain,
-        ),
+        [
+            pltpu.with_memory_space_constraint(arg, pltpu.HBM)
+            for arg in (
+                tokens, cotangent, table, spread, qkv_weight, proj_weight, up_weight, down_turned,
+                norm_gain,
+            )
+        ],
         8,
         28,
-        pltpu.HBM,
+        [pltpu.HBM] * 9,
     )
     lon_head = lon_send(head, -1)
     diag_head = diag_send(head, -1)
@@ -811,43 +814,58 @@
     )
     pieces_ab = lax.all_to_all(part_ab, "lon", 0, 0)
 
-    tokens_grad, pieces_c = call(
+    tokens_grad, keep_c, give_c, bias_c = call(
         fourth_kernel,
-        [(tokens.shape, BF16), units(2 * lon_size, units_c + extra)],
+        [
+            (tokens.shape, BF16),
+            units(lon_size, units_c),
+            units(lon_size, units_c),
+            units(lon_size, extra),
+        ],
         [
             field_shape,
             sums_shape,
             m576,
             flat_scr(units_c),
             token_scr,
-            units(lon_size, extra),
+            probs_shape,
+            pltpu.SemaphoreType.DMA((wins,)),
         ],
         (
-            x0, qkv0, probs0, dmix0, rg0, gain_two, gains1, part_ab, qkv_weight, norm_gain,
+            x0, qkv0, pltpu.with_memory_space_constraint(probs0, pltpu.HBM), dmix0, rg0, gain_two,
+            gains1, part_ab, qkv_weight, norm_gain,
         ),
         11,
         24,
-    )
-    got_c = lax.all_to_all(pieces_c, ("lon", "lat"), 0, 0)
-
-    (sum_ab,) = call(sum_pieces, [units(units_a + extra + units_b)], [], (pieces_ab,), 1, 10)
-    whole_ab = lax.all_gather(sum_ab, ("lon", "lat"))
+        [pltpu.VMEM] * 2 + [pltpu.HBM] + [pltpu.VMEM] * 7,
+    )
+    got_c = lat_swap(give_c)
+    (part_c,) = call(
+        lat_sum_late, [units(lon_size, units_c + extra)], [], (keep_c, got_c, bias_c), 1, 10
+    )
+    pieces_c = lax.all_to_all(part_c, "lon", 0, 0)
+
+    (sum_ab,) = call(
+        sum_pieces, [units(lon_size, units_a + extra + units_b)], [], (pieces_ab, part_c), 1, 10
+    )
+    whole_ab = lax.all_to_all(sum_ab, "lon", 0, 0)
     (sum_c,) = call(
-        functools.partial(sum_direct, extra), [units(units_c + extra)], [], (got_c,), 1, 10
-    )
-    whole_c = lax.all_to_all(
-        jnp.broadcast_to(sum_c[None], (2 * lon_size,) + sum_c.shape), ("lon", "lat"), 0, 0
-    )
+        sum_pieces, [units(lon_size, units_c + extra)], [], (pieces_c, sum_ab), 1, 10
+    )
+    whole_c = lax.all_to_all(sum_c, "lon", 0, 0)
+    oth_ab = lat_swap(whole_ab)
+    oth_c = lat_swap(whole_c)
 
     flat_rows = (2 * block_rows * 128 + norm_gain.size) // 128
     update, bias_grad = call(
         functools.partial(last_kernel, units_a, units_c, extra),
-        [((flat_rows, 128), BF16), (bias_table.shape, F32)],
-        [((flat_rows + 2, 128), F32), ((CHUNK * 8, PAIR), F32), wide_scr],
-        (spread, whole_ab, whole_c),
+        [((flat_rows, 128), BF16), (table.shape, F32)],
+        [((flat_rows + 2, 128), F32), ((CHUNK * 8, PAIR), F32), wide_scr, tab_scr],
+        (spread, whole_ab, oth_ab, whole_c, oth_c),
         3,
         20,
     )
+    bias_grad = jnp.swapaxes(bias_grad, 1, 2)
     return (tokens_grad, update.reshape(-1), bias_grad)
 
 

time: 150 us -> 133 us (0.89)
  blocking collectives: 59.9 us -> 36.6 us
  waiting for transfers between devices: 9.29 us -> 23.7 us
  between operations: 14.2 us -> 0.82 us
  starting transfers between devices: 7.77 us -> 14.8 us
  local copies, waits for them, and re-layouts: 13.2 us -> 6.26 us
  Pallas kernels: 45.1 us -> 50.2 us
    all_to_all x3 -> x2, blocking collectives: 59.9 us -> 36.6 us  [the longest x1 26 us: shards(): whole_ab = lax.all_to_all(sum_ab, 'lon', 0, 0)]
    all_to_all x0 -> x2, waiting for transfers between devices: none -> 11.8 us  [the longest x1 7.64 us: shards(): pieces_c = lax.all_to_all(part_c, 'lon', 0, 0)]
    all_to_all x0 -> x2, starting transfers between devices: none -> 6.94 us  [the longest x1 3.55 us: shards(): pieces_ab = lax.all_to_all(part_ab, 'lon', 0, 0)]
    unnamed x39 -> x28, local copies, waits for them, and re-layouts: 13.1 us -> 6.26 us
    pallas_call x10 -> x11, Pallas kernels: 45.1 us -> 50.2 us  [call(): pl.pallas_call(kernel, out_shape=[jax.ShapeDtypeStruct(shape, dtype) for...]
    ppermute x4 -> x7, waiting for transfers between devices: 1.64 us -> 4.29 us  [lat_swap(): return lax.ppermute(value, 'lat', [(0, 1), (1, 0)])]
  transfers between devices with their start and end apart: 9 -> 13, of which waited for: 5 -> 9; matrix products, arithmetic and copies ran while one was open for 0% -> 0% of each run, Pallas kernels for 10% -> 15%
where the time goes in v4:
time: 133 us; the launch traced here: 132 us
  Pallas kernels  50.2 us (38%)
  blocking collectives  36.6 us (28%)
  waiting for transfers between devices  23.7 us (18%)
  starting transfers between devices  14.8 us (11%)
  local copies, waits for them, and re-layouts  6.26 us (5%)
    pallas_call x11, Pallas kernels, call(): pl.pallas_call(kernel, out_shape=[jax.ShapeDtypeStruct(shape, dtype) for...  50.2 us
    all_to_all x1, blocking collectives, shards(): whole_ab = lax.all_to_all(sum_ab, 'lon', 0, 0)  26 us
    all_to_all x1, blocking collectives, shards(): whole_c = lax.all_to_all(sum_c, 'lon', 0, 0)  10.5 us
    all_to_all x1, waiting for transfers between devices, shards(): pieces_c = lax.all_to_all(part_c, 'lon', 0, 0)  7.64 us
    unnamed x28, local copies, waits for them, and re-layouts  6.26 us
    ppermute x2, starting transfers between devices, diag_send(): return lax.ppermute(value, ('lon', 'lat'), pairs)  5.74 us
    ppermute x2, waiting for transfers between devices, diag_send(): return lax.ppermute(value, ('lon', 'lat'), pairs)  4.84 us
    ppermute x7, waiting for transfers between devices, lat_swap(): return lax.ppermute(value, 'lat', [(0, 1), (1, 0)])  4.29 us
  transfers between devices with their start and end apart: 13, of which 9 were waited for; matrix products, arithmetic and copies ran while one was open for 0% of the time, Pallas kernels for 15%

profile of v4, /device:TPU:0, one launch (start us, length us, event | category | flops | bytes accessed | tf_op | source)
XLA Modules:
  0.0 132.3 jit_solution(11182888656317792768)
XLA Ops:
  0.6 0.0 copy-start.6
  0.7 8.9 %shard_map.112 = (bf16[576,192]{1,0:T(8,128)(2,1)S(1)}, bf16[2,504,192]{2,1,0:T(8,128)(2,1)S(1)}, bf16[2,72,192]{2,1,0:T(8,128)(2,1)S(1)}, bf16[576,576]{1,0:T(8...) custom-call(bf16[2,12,24,192]{3,2,1,0:T(8,128)(2,1)} %tokens_in.1, ...), custom_call_target="tpu_custom_call" | custom-call | flops 8800000000 | bytes 100000 | tf_op jit(solution)/shard_map/pallas_call | solution.py:620
  9.6 1.7 %copy-done.9 = f32[4,6,144,144]{3,2,1,0:T(8,128)} copy-done((f32[4,6,144,144]{3,2,1,0:T(8,128)}, f32[4,6,144,144]{3,2,1,0:T(8,128)S(1)}, u32[]{:S(2)}) %copy-start.9) | copy-done | bytes 1990680
  11.3 0.9 copy-done.10
  12.2 0.7 copy-done.12
  12.9 0.5 collective-permute-start.1
  13.4 0.0 copy-start.5
  13.4 5.7 %collective-permute-start.2 = (bf16[2,72,192]{2,1,0:T(8,128)(2,1)S(1)}, bf16[2,72,192]{2,1,0:T(8,128)(2,1)S(1)}, u32[]{:S(2)}, u32[]{:S(2)}) collective-permute-start(bf16[2,72,192]{2,1,0:T(8,128)(2,1)S(1)} %get-tuple-element.42), channel_id=1, source_target_pairs={{0,15},{1,14},{2,1},{3,0},{4,3},{5,2},{6,5},{7,4},{8,7},{9,6},{10,... | collective-permute-start | bytes 165896 | tf_op jit(solution)/shard_map/ppermute | solution.py:650
  19.1 0.5 collective-permute-start
  19.6 0.0 copy-done.6
  19.6 0.9 shard_map.113.bias
  20.5 1.1 collective-permute-done.2.diag_head
  21.7 1.7 %collective-permute-done.lon_head = bf16[2,72,192]{2,1,0:T(8,128)(2,1)S(1)} collective-permute-done((bf16[2,72,192]{2,1,0:T(8,128)(2,1)S(1)}, bf16[2,72,192]{2,1,0:T(8,128)(2,1)S(1)}, u32[]{:S(2)}, u32[]{:S(2)}) %collective-permute-start) | collective-permute-done | bytes 55328 | tf_op jit(solution)/shard_map/ppermute | solution.py:641
  23.4 0.0 collective-permute-done.1.lat_tail
  23.4 0.0 copy-done
  23.5 17.1 %shard_map.114 = (bf16[504,192]{1,0:T(8,128)(2,1)S(1)}, bf16[72,192]{1,0:T(8,128)(2,1)S(1)}, bf16[576,192]{1,0:T(8,128)(2,1)S(1)}, bf16[576,576]{1,0:T(8,128)(2,...) custom-call(bf16[2,504,192]{2,1,0:T(8,128)(2,1)S(1)} %get-tuple-elem, ...), custom_call_target="tpu_custom_call" | custom-call | flops 20899999744 | bytes 100000 | tf_op jit(solution)/shard_map/pallas_call | solution.py:620
  40.5 0.1 collective-permute-start.5
  40.6 0.2 collective-permute-start.3
  40.8 0.1 collective-permute-start.4
  40.9 1.6 %shard_map.115 = (bf16[8,27,8,128]{3,2,1,0:T(8,128)(2,1)S(1)}, bf16[8,27,8,128]{3,2,1,0:T(8,128)(2,1)S(1)}, bf16[8,5,8,128]{3,2,1,0:T(8,128)(2,1)S(1)}) custom-call(bf16[576,192]{1,0:T(8,128)(2,1)S(1)} %get-tuple-element.49.n1, bf16[576,576]{1,0:T(8,128)(2,1)S(1)} %get-tuple-element.50.field, bf16[576,192]{1,0:T(8,128)(2,1)S(1)} %get-tuple-element.51.mixed, ...), custom_call_target="tpu_custom_call" | custom-call | flops 3300000000 | bytes 100000 | tf_op jit(solution)/shard_map/pallas_call | solution.py:620
  42.6 0.6 collective-permute-start.6
  43.1 3.7 %collective-permute-done.5.diag_tail = bf16[72,192]{1,0:T(8,128)(2,1)S(1)} collective-permute-done((bf16[72,192]{1,0:T(8,128)(2,1)S(1)}, bf16[72,192]{1,0:T(8,128)(2,1)S(1)}, u32[]{:S(2)}, u32[]{:S(2)}) %collective-permute-start.5) | collective-permute-done | bytes 27680 | tf_op jit(solution)/shard_map/ppermute | solution.py:650
  46.8 1.0 collective-permute-done.3.lon_tail
  47.8 0.0 collective-permute-done.4.lat_head
  47.9 2.1 %shard_map.116 = (bf16[8,21,8,128]{3,2,1,0:T(8,128)(2,1)S(1)}, bf16[8,21,8,128]{3,2,1,0:T(8,128)(2,1)S(1)}, f32[576,192]{1,0:T(8,128)S(1)}, bf16[576,192]{1,0:T(8,128)(2,1)S(1)}, f32[1,192]{1,0:T(1,128)S(1)}) custom-call(bf16[504,192]{1,0:T(8,128)(2,1)S(1)} %get-tuple-element.43.head, bf16[72,192]{1,0:T(8,128)(2,1)S(1)} %collective-permute-done.3.lon_tail, ...), custom_call_target="tpu_custom_call" | custom-call | flops 2200000000 | bytes 100000 | tf_op jit(solution)/shard_map/pallas_call | solution.py:620
  50.0 0.8 copy-done.7
  50.8 0.0 collective-permute-start.7
  50.8 0.0 collective-permute-done.6.got_a
  50.8 1.6 %collective-permute-done.7.got_b = bf16[8,21,8,128]{3,2,1,0:T(8,128)(2,1)S(1)} collective-permute-done((bf16[8,21,8,128]{3,2,1,0:T(8,128)(2,1)S(1)}, bf16[8,21,8,128]{3,2,1,0:T(8,128)(2,1)S(1)}, u32[]{:S(2)}, u32[]{:S(2)}) %collective-permute-start.7) | collective-permute-done | bytes 344096 | tf_op jit(solution)/shard_map/ppermute | solution.py:636
  52.5 1.1 shard_map.117.order
  53.6 3.6 %all-to-all-start = ((bf16[8,53,8,128]{3,2,1,0:T(8,128)(2,1)}), bf16[8,53,8,128]{3,2,1,0:T(8,128)(2,1)S(1)}, u32[]{:S(2)}, u32[]{:S(2)}) async-start(bf16[8,53,8,128]{3,2,1,0:T(8,128)(2,1)} %shard_map.117.order), calls=%async_computation | async-start | bytes 1736704 | tf_op jit(solution)/shard_map/all_to_all | solution.py:815
  57.1 1.1 copy-done.11
  58.3 1.0 copy-done.13
  59.2 14.1 %shard_map.118 = (bf16[2,12,24,192]{3,2,1,0:T(8,128)(2,1)}, bf16[8,7,8,128]{3,2,1,0:T(8,128)(2,1)S(1)}, bf16[8,7,8,128]{3,2,1,0:T(8,128)(2,1)S(1)}, bf16[8,5,8,128]{3,2,1,0:T(8,128)(2,1)S(1)}) custom-call(bf16[576,192]{1,0:T(8,128)(2,1)S(1)} %copy-done.13, bf16[576,576]{1,0:T(8,128)(2,1)S(1)} %copy-done.11, f32[4,6,144,144]{3,2,1,0:T(8,128)} %copy-done.9, ...), custom_call_target="tpu_custom_call" | custom-call | flops 12099999744 | bytes 100000 | tf_op jit(solution)/shard_map/pallas_call | solution.py:620
  73.3 0.2 collective-permute-start.8
  73.5 1.2 collective-permute-done.8.got
  74.7 0.7 shard_map.119.order
  75.4 4.1 %all-to-all-done.pieces = bf16[8,53,8,128]{3,2,1,0:T(8,128)(2,1)S(1)} async-done(((bf16[8,53,8,128]{3,2,1,0:T(8,128)(2,1)}), bf16[8,53,8,128]{3,2,1,0:T(8,128)(2,1)S(1)}, u32[]{:S(2)}, u32[]{:S(2)}) %all-to-all-start) | async-done | bytes 868384 | tf_op jit(solution)/shard_map/all_to_all | solution.py:815
  79.5 1.1 shard_map.120.order
  80.6 26.0 %all_to_all.20.own_ab = bf16[8,53,8,128]{3,2,1,0:T(8,128)(2,1)S(1)} all-to-all(bf16[8,53,8,128]{3,2,1,0:T(8,128)(2,1)S(1)} %shard_map.120.order), channel_id=1, replica_groups=mesh['grp'=2,'lon'=8,'lat'=2] {'lon'}, dimensions={0} | all-to-all | bytes 1736704 | tf_op jit(solution)/shard_map/all_to_all | solution.py:851
  106.6 3.4 %all-to-all-start.2 = ((bf16[8,12,8,128]{3,2,1,0:T(8,128)(2,1)}), bf16[8,12,8,128]{3,2,1,0:T(8,128)(2,1)S(1)}, u32[]{:S(2)}, u32[]{:S(2)}) async-start(bf16[8,12,8,128]{3,2,1,0:T(8,128)(2,1)} %shard_map.119.order), calls=%async_computation.2 | async-start | bytes 393216 | tf_op jit(solution)/shard_map/all_to_all | solution.py:846
  110.0 0.1 collective-permute-start.9
  110.1 7.6 %all-to-all-done.2.pieces = bf16[8,12,8,128]{3,2,1,0:T(8,128)(2,1)S(1)} async-done(((bf16[8,12,8,128]{3,2,1,0:T(8,128)(2,1)}), bf16[8,12,8,128]{3,2,1,0:T(8,128)(2,1)S(1)}, u32[]{:S(2)}, u32[]{:S(2)}) %all-to-all-start.2) | async-done | bytes 196640 | tf_op jit(solution)/shard_map/all_to_all | solution.py:846
  117.8 10.5 %all_to_all.21.own_c = bf16[8,12,8,128]{3,2,1,0:T(8,128)(2,1)S(1)} all-to-all(bf16[8,12,8,128]{3,2,1,0:T(8,128)(2,1)S(1)} %shard_map.121), channel_id=1, replica_groups=mesh['grp'=2,'lon'=8,'lat'=2] {'lon'}, dimensions={0} | all-to-all | bytes 393216 | tf_op jit(solution)/shard_map/all_to_all | solution.py:855
  128.3 0.0 collective-permute-start.10
  128.3 1.4 %collective-permute-done.10.oth_c = bf16[8,12,8,128]{3,2,1,0:T(8,128)(2,1)S(1)} collective-permute-done((bf16[8,12,8,128]{3,2,1,0:T(8,128)(2,1)S(1)}, bf16[8,12,8,128]{3,2,1,0:T(8,128)(2,1)S(1)}, u32[]{:S(2)}, u32[]{:S(2)}) %collective-permute-start.10) | collective-permute-done | bytes 196640 | tf_op jit(solution)/shard_map/ppermute | solution.py:636
  129.8 0.0 collective-permute-done.9.oth_ab
  129.8 2.6 %shard_map.122 = (bf16[6918,128]{1,0:T(8,128)(2,1)}, f32[2,6,1,6336]{3,2,1,0:T(1,128)}) custom-call(bf16[2,132,384]{2,1,0:T(8,128)(2,1)S(1)} %copy-done.6, bf16[8,53,8,128]{3,2,1,0:T(8,128)(2,1)S(1)} %all_to_all.20.own_ab, bf16[8,53,8,128]{3,2,1,0:T(8,128)(2,1)S(1)} %collective-permute-done.9.oth_ab, bf16[8,12,8,128]{3,2,1,0:T(8,128)(2,1)S(1)} %all_to_all.21.own_c, ...), custom_call_target="tpu_custom_call" | custom-call | flops 3300000000 | bytes 100000 | tf_op jit(solution)/shard_map/pallas_call | solution.py:620
  (19 shorter events, 0.1 us)
Async XLA Ops:
  0.6 19.0 %copy-start.3 = (f32[2,1,6,6336]{3,1,2,0:T(1,128)S(1)}, f32[2,1,6,6336]{3,1,2,0:T(1,128)}, u32[]{:S(2)}) copy-start(f32[2,1,6,6336]{3,1,2,0:T(1,128)} %param.16) | copy-start | bytes 912388
  0.6 19.0 %copy-start.6 = (bf16[2,132,384]{2,1,0:T(8,128)(2,1)S(1)}, bf16[2,132,384]{2,1,0:T(8,128)(2,1)}, u32[]{:S(2)}) copy-start(bf16[2,132,384]{2,1,0:T(8,128)(2,1)} %constant.2.clone.spread_in.spread) | copy-start | bytes 608260
  9.6 1.8 %copy-start.9 = (f32[4,6,144,144]{3,2,1,0:T(8,128)}, f32[4,6,144,144]{3,2,1,0:T(8,128)S(1)}, u32[]{:S(2)}) copy-start(f32[4,6,144,144]{3,2,1,0:T(8,128)S(1)} %get-tuple-element.40.probs_in) | copy-start | bytes 5971972
  11.3 0.9 copy-start.10
  12.2 0.7 copy-start.12
  12.9 10.5 %collective-permute-start.1 = (bf16[2,504,192]{2,1,0:T(8,128)(2,1)S(1)}, bf16[2,504,192]{2,1,0:T(8,128)(2,1)S(1)}, u32[]{:S(2)}, u32[]{:S(2)}) collective-permute-start(bf16[2,504,192]{2,1,0:T(8,128)(2,1)S(1)} %get-tuple-element.41.tail), channel_id=1, source_target_pairs={{0,1},{1,0},{2,3},{3,2},{4,5},{5,4},{6,7},{7,6},{8,9},{9,8},{10,11... | collective-permute-start | bytes 1161224 | tf_op jit(solution)/shard_map/ppermute | solution.py:636
  13.3 10.1 %copy-start = (bf16[2,192,768]{2,1,0:T(8,128)(2,1)S(1)}, bf16[2,192,768]{2,1,0:T(8,128)(2,1)}, u32[]{:S(2)}) copy-start(bf16[2,192,768]{2,1,0:T(8,128)(2,1)} %up_w.3) | copy-start | bytes 1769476
  13.4 10.1 %copy-start.1 = (bf16[2,768,192]{1,2,0:T(8,128)(2,1)S(1)}, bf16[2,768,192]{1,2,0:T(8,128)(2,1)}, u32[]{:S(2)}) copy-start(bf16[2,768,192]{1,2,0:T(8,128)(2,1)} %param.14) | copy-start | bytes 1769476
  13.4 10.1 %copy-start.2 = (bf16[2,192,576]{2,1,0:T(8,128)(2,1)S(1)}, bf16[2,192,576]{2,1,0:T(8,128)(2,1)}, u32[]{:S(2)}) copy-start(bf16[2,192,576]{2,1,0:T(8,128)(2,1)} %qkv_w.3) | copy-start | bytes 1327108
  13.4 10.1 %copy-start.4 = (bf16[2,192,192]{2,1,0:T(8,128)(2,1)S(1)}, bf16[2,192,192]{2,1,0:T(8,128)(2,1)}, u32[]{:S(2)}) copy-start(bf16[2,192,192]{2,1,0:T(8,128)(2,1)} %proj_w.3) | copy-start | bytes 442372
  13.4 10.1 %copy-start.5 = (f32[2,2,192]{2,1,0:T(2,128)S(1)}, f32[2,2,192]{2,1,0:T(2,128)}, u32[]{:S(2)}) copy-start(f32[2,2,192]{2,1,0:T(2,128)} %gains.5) | copy-start | bytes 9220
  13.4 8.3 %collective-permute-start.2 = (bf16[2,72,192]{2,1,0:T(8,128)(2,1)S(1)}, bf16[2,72,192]{2,1,0:T(8,128)(2,1)S(1)}, u32[]{:S(2)}, u32[]{:S(2)}) collective-permute-start(bf16[2,72,192]{2,1,0:T(8,128)(2,1)S(1)} %get-tuple-element.42), channel_id=1, source_target_pairs={{0,15},{1,14},{2,1},{3,0},{4,3},{5,2},{6,5},{7,4},{8,7},{9,6},{10,... | collective-permute-start | bytes 165896 | tf_op jit(solution)/shard_map/ppermute | solution.py:650
  19.1 4.4 %collective-permute-start = (bf16[2,72,192]{2,1,0:T(8,128)(2,1)S(1)}, bf16[2,72,192]{2,1,0:T(8,128)(2,1)S(1)}, u32[]{:S(2)}, u32[]{:S(2)}) collective-permute-start(bf16[2,72,192]{2,1,0:T(8,128)(2,1)S(1)} %get-tuple-element.42), channel_id=1, source_target_pairs={{0,14},{2,0},{4,2},{6,4},{8,6},{10,8},{12,10},{14,12},{1,15},{3,1}... | collective-permute-start | bytes 165896 | tf_op jit(solution)/shard_map/ppermute | solution.py:641
  40.5 6.3 %collective-permute-start.5 = (bf16[72,192]{1,0:T(8,128)(2,1)S(1)}, bf16[72,192]{1,0:T(8,128)(2,1)S(1)}, u32[]{:S(2)}, u32[]{:S(2)}) collective-permute-start(bf16[72,192]{1,0:T(8,128)(2,1)S(1)} %get-tuple-element.44), channel_id=1, source_target_pairs={{0,3},{1,2},{2,5},{3,4},{4,7},{5,6},{6,9},{7,8},{8,11},{9,10},{10,... | collective-permute-start | bytes 82952 | tf_op jit(solution)/shard_map/ppermute | solution.py:650
  40.6 7.3 %collective-permute-start.3 = (bf16[72,192]{1,0:T(8,128)(2,1)S(1)}, bf16[72,192]{1,0:T(8,128)(2,1)S(1)}, u32[]{:S(2)}, u32[]{:S(2)}) collective-permute-start(bf16[72,192]{1,0:T(8,128)(2,1)S(1)} %get-tuple-element.44), channel_id=1, source_target_pairs={{0,2},{2,4},{4,6},{6,8},{8,10},{10,12},{12,14},{14,0},{1,3},{3,5},... | collective-permute-start | bytes 82952 | tf_op jit(solution)/shard_map/ppermute | solution.py:641
  40.8 7.0 %collective-permute-start.4 = (bf16[504,192]{1,0:T(8,128)(2,1)S(1)}, bf16[504,192]{1,0:T(8,128)(2,1)S(1)}, u32[]{:S(2)}, u32[]{:S(2)}) collective-permute-start(bf16[504,192]{1,0:T(8,128)(2,1)S(1)} %get-tuple-element.43.head), channel_id=1, source_target_pairs={{0,1},{1,0},{2,3},{3,2},{4,5},{5,4},{6,7},{7,6},{8,9},{9,8},{10,11... | collective-permute-start | bytes 580616 | tf_op jit(solution)/shard_map/ppermute | solution.py:636
  42.6 8.3 %collective-permute-start.6 = (bf16[8,27,8,128]{3,2,1,0:T(8,128)(2,1)S(1)}, bf16[8,27,8,128]{3,2,1,0:T(8,128)(2,1)S(1)}, u32[]{:S(2)}, u32[]{:S(2)}) collective-permute-start(bf16[8,27,8,128]{3,2,1,0:T(8,128)(2,1)S(1)} %get-tuple-element.63), channel_id=1, source_target_pairs={{0,1},{1,0},{2,3},{3,2},{4,5},{5,4},{6,7},{7,6},{8,9},{9,8},{10,11... | collective-permute-start | bytes 1327112 | tf_op jit(solution)/shard_map/ppermute | solution.py:636
  50.0 0.8 copy-start.7
  50.8 1.7 %collective-permute-start.7 = (bf16[8,21,8,128]{3,2,1,0:T(8,128)(2,1)S(1)}, bf16[8,21,8,128]{3,2,1,0:T(8,128)(2,1)S(1)}, u32[]{:S(2)}, u32[]{:S(2)}) collective-permute-start(bf16[8,21,8,128]{3,2,1,0:T(8,128)(2,1)S(1)} %get-tuple-element.66), channel_id=1, source_target_pairs={{0,1},{1,0},{2,3},{3,2},{4,5},{5,4},{6,7},{7,6},{8,9},{9,8},{10,11... | collective-permute-start | bytes 1032200 | tf_op jit(solution)/shard_map/ppermute | solution.py:636
  52.5 4.7 %copy-start.8 = (f32[576,192]{1,0:T(8,128)S(1)}, f32[576,192]{1,0:T(8,128)}, u32[]{:S(2)}) copy-start(f32[576,192]{1,0:T(8,128)} %copy-done.7) | copy-start | bytes 1327108
  53.6 26.0 %all-to-all-start = ((bf16[8,53,8,128]{3,2,1,0:T(8,128)(2,1)}), bf16[8,53,8,128]{3,2,1,0:T(8,128)(2,1)S(1)}, u32[]{:S(2)}, u32[]{:S(2)}) async-start(bf16[8,53,8,128]{3,2,1,0:T(8,128)(2,1)} %shard_map.117.order), calls=%async_computation | async-start | bytes 1736704 | tf_op jit(solution)/shard_map/all_to_all | solution.py:815
  57.1 1.1 copy-start.11
  58.3 1.0 copy-start.13
  73.3 1.4 %collective-permute-start.8 = (bf16[8,7,8,128]{3,2,1,0:T(8,128)(2,1)S(1)}, bf16[8,7,8,128]{3,2,1,0:T(8,128)(2,1)S(1)}, u32[]{:S(2)}, u32[]{:S(2)}) collective-permute-start(bf16[8,7,8,128]{3,2,1,0:T(8,128)(2,1)S(1)} %get-tuple-element.69), channel_id=1, source_target_pairs={{0,1},{1,0},{2,3},{3,2},{4,5},{5,4},{6,7},{7,6},{8,9},{9,8},{10,11... | collective-permute-start | bytes 344072 | tf_op jit(solution)/shard_map/ppermute | solution.py:636
  106.6 11.1 %all-to-all-start.2 = ((bf16[8,12,8,128]{3,2,1,0:T(8,128)(2,1)}), bf16[8,12,8,128]{3,2,1,0:T(8,128)(2,1)S(1)}, u32[]{:S(2)}, u32[]{:S(2)}) async-start(bf16[8,12,8,128]{3,2,1,0:T(8,128)(2,1)} %shard_map.119.order), calls=%async_computation.2 | async-start | bytes 393216 | tf_op jit(solution)/shard_map/all_to_all | solution.py:846
  110.0 19.7 %collective-permute-start.9 = (bf16[8,53,8,128]{3,2,1,0:T(8,128)(2,1)S(1)}, bf16[8,53,8,128]{3,2,1,0:T(8,128)(2,1)S(1)}, u32[]{:S(2)}, u32[]{:S(2)}) collective-permute-start(bf16[8,53,8,128]{3,2,1,0:T(8,128)(2,1)S(1)} %all_to_all.20.own_ab), channel_id=1, source_target_pairs={{0,1},{1,0},{2,3},{3,2},{4,5},{5,4},{6,7},{7,6},{8,9},{9,8},{10,11... | collective-permute-start | bytes 2605064 | tf_op jit(solution)/shard_map/ppermute | solution.py:636
  128.3 1.4 %collective-permute-start.10 = (bf16[8,12,8,128]{3,2,1,0:T(8,128)(2,1)S(1)}, bf16[8,12,8,128]{3,2,1,0:T(8,128)(2,1)S(1)}, u32[]{:S(2)}, u32[]{:S(2)}) collective-permute-start(bf16[8,12,8,128]{3,2,1,0:T(8,128)(2,1)S(1)} %all_to_all.21.own_c), channel_id=1, source_target_pairs={{0,1},{1,0},{2,3},{3,2},{4,5},{5,4},{6,7},{7,6},{8,9},{9,8},{10,11... | collective-permute-start | bytes 589832 | tf_op jit(solution)/shard_map/ppermute | solution.py:636

commit v5 on v4

--- a/solution.py
+++ b/solution.py
@@ -167,7 +167,18 @@
         rest = rest + (last if h == 0 else pltpu.roll(last, 8 * h, axis=1))
     emit(2 * HEADS, rest)
 
-def attend(qkv, bias, mixed, probs, width):
+def stack_heads(v, masks):
+    return jnp.concatenate([v * mask for mask in masks], axis=0)
+
+
+def pick_heads(v, masks):
+    total = v[0:WIN] * masks[0]
+    for h in range(1, HEADS):
+        total = total + v[h * WIN : (h + 1) * WIN] * masks[h]
+    return total
+
+
+def attend(qkv, bias, mixed, probs, stack_scr, width, finish=None):
     masks = head_masks(width, BF16)
     masks32 = head_masks(width, F32)
     scale = (width // HEADS) ** -0.5
@@ -177,20 +188,23 @@
         q = qkv[rows, 0:width]
         k = qkv[rows, width : 2 * width]
         v = qkv[rows, 2 * width : 3 * width]
-        total = jnp.zeros((WIN, width), F32)
+        scores = dot_nt(stack_heads(q, masks), k)
         for h in range(HEADS):
-            logits = dot_nt(q * masks[h], k) * scale + bias[h * WIN : (h + 1) * WIN, :]
+            part = slice(h * WIN, (h + 1) * WIN)
+            logits = scores[part] * scale + bias[part, :]
             weights = jnp.exp(logits - jnp.max(logits, axis=-1, keepdims=True))
             p = weights * (1.0 / jnp.sum(weights, axis=-1, keepdims=True))
             probs[w, h] = p
-            total = total + dot(p.astype(BF16), v) * masks32[h]
-        mixed[rows, :] = total.astype(BF16)
+            stack_scr[part, :] = p.astype(BF16)
+        mixed[rows, :] = pick_heads(dot(stack_scr[...], v), masks32).astype(BF16)
+        if finish is not None:
+            finish(w)
         return carry
 
     lax.fori_loop(0, probs.shape[0], window, 0)
 
 
-def attend_back(qkv, probs, dmix, field, sums, width, first, last):
+def attend_back(qkv, probs, dmix, field, sums, low_scr, prob_scr, width, begin=None):
     masks = head_masks(width, BF16)
     masks32 = head_masks(width, F32)
     scale = (width // HEADS) ** -0.5
@@ -200,26 +214,28 @@
         q = qkv[rows, 0:width]
         k = qkv[rows, width : 2 * width]
         v = qkv[rows, 2 * width : 3 * width]
-        up = dmix[rows, :]
-        dq = jnp.zeros((WIN, width), F32)
-        dk = jnp.zeros((WIN, width), F32)
-        dv = jnp.zeros((WIN, width), F32)
+        up = stack_heads(dmix[rows, :], masks)
+        prob_grad = dot_nt(up, v)
+        if begin is not None:
+            begin(w)
         for h in range(HEADS):
+            part = slice(h * WIN, (h + 1) * WIN)
             p = probs[w, h]
-            up_h = up * masks[h]
-            dp = dot_nt(up_h, v)
-            ds = p * (dp - jnp.sum(p * dp, axis=-1, keepdims=True))
-            sums[h * WIN : (h + 1) * WIN, 0:WIN] += ds
-            low = ds.astype(BF16)
-            dq = dq + dot(low, k) * masks32[h]
-            dk = dk + dot_tn(low, q * masks[h])
-            dv = dv + dot_tn(p.astype(BF16), up_h)
+            weighted = p * prob_grad[part]
+            ds = weighted - p * jnp.sum(weighted, axis=-1, keepdims=True)
+            sums[part, 0:WIN] += ds
+            low_scr[part, :] = ds.astype(BF16)
+            prob_scr[part, :] = p.astype(BF16)
+        low = low_scr[...]
+        dq = pick_heads(dot(low, k), masks32)
+        dk = dot_tn(low, stack_heads(q, masks))
+        dv = dot_tn(prob_scr[...], up)
         field[rows, 0:width] = (dq * scale).astype(BF16)
         field[rows, width : 2 * width] = (dk * scale).astype(BF16)
         field[rows, 2 * width : 3 * width] = dv.astype(BF16)
         return carry
 
-    lax.fori_loop(first, last, window, 0)
+    lax.fori_loop(0, probs.shape[0], window, 0)
 
 
 def lon_major(src, scr):
@@ -283,13 +299,13 @@
     for k in range(BIAS_UNITS, lons * per):
         put_unit(k, jnp.zeros((UNIT, 128), BF16))
 
-def forward_core(x, b, lat, lat_total, refs, qkv_scr, bias_scr, mixed, probs):
+def forward_core(x, b, refs, qkv_scr, bias_scr, mixed, probs, stack_scr, finish=None):
     qkv_w, proj_w, gains = refs
     width = x.shape[-1]
     stand, inv = standardize(x)
     normed = (stand * gains[b, 0:1, :]).astype(BF16)
     qkv_scr[...] = dot(normed, qkv_w[b]).astype(BF16)
-    attend(qkv_scr, bias_scr, mixed, probs, width)
+    attend(qkv_scr, bias_scr, mixed, probs, stack_scr, width, finish)
     att = dot(mixed[...], proj_w[b]).astype(BF16)
     resid = (x + att.astype(F32)).astype(BF16).astype(F32)
     return resid, normed
@@ -299,7 +315,8 @@
     lat_total, tokens_in, cot_in, table_in, spread_in, qkv_in, proj_in, up_in, down_in, gains_in,
     x_out, tail_out, head_out, qkv_out, mixed_out, probs_out, resid_out, slope_out, active_out,
     scr, cot_scr, tab_scr, rows_scr, wide_scr, bias_scr,
-    cot, table, spread, tokens, qkv_w, gains, proj_w, up_w, down_w, sems,
+    cot, table, spread, tokens, qkv_w, gains, proj_w, up_w, down_w, stack_scr,
+    probs, slope_scr, active_scr, sems, out_sems,
 ):
     copies = []
     for source, target in (
@@ -336,19 +353,33 @@
     x_out[...] = x.astype(BF16)
     for copy in copies[4:]:
         copy.wait()
+
+    def probs_copy(w):
+        return pltpu.make_async_copy(probs.at[w], probs_out.at[w], out_sems.at[w])
+
     resid, _ = forward_core(
-        x, 0, lat, lat_total, (qkv_w, proj_w, gains), qkv_out, bias_scr, mixed_out, probs_out
+        x, 0, (qkv_w, proj_w, gains), qkv_out, bias_scr, mixed_out, probs, stack_scr,
+        lambda w: probs_copy(w).start(),
     )
     resid_out[...] = resid.astype(BF16)
     stand, _ = standardize(resid)
     normed = (stand * gains[0, 1:2, :]).astype(BF16)
     active, slope = gelu_parts(dot(normed, up_w[0]))
     active = active.astype(BF16)
-    active_out[...] = active
-    slope_out[...] = slope.astype(BF16)
+    active_scr[...] = active
+    slope_scr[...] = slope.astype(BF16)
+    wins = probs.shape[0]
+    last = [
+        pltpu.make_async_copy(active_scr, active_out, out_sems.at[wins]),
+        pltpu.make_async_copy(slope_scr, slope_out, out_sems.at[wins + 1]),
+    ]
+    for copy in last:
+        copy.start()
     result = resid + dot_nt(active, down_w[0])
     head_out[0] = result[0:cut, :].astype(BF16)
     tail_out[0] = result[cut:, :].astype(BF16)
+    for copy in [probs_copy(w) for w in range(wins)] + last:
+        copy.wait()
 
 
 def bias_kernel(lat_total, table, spread, bias_out, tab_scr, rows_scr, wide_scr):
@@ -383,7 +414,7 @@
     tail, lon_head, lat_tail, diag_head, bias, qkv_w, proj_w, up_w, down_w, gains,
     head_out, tail_out, n1_out, field_out, mixed_out, low_out, n2_out, hg_out, active_out, g_out,
     sums_out, gain_out,
-    scr_own, scr_oth, qkv_scr, probs_scr, dmix_scr,
+    scr_own, scr_oth, qkv_scr, probs_scr, dmix_scr, low_scr, prob_scr,
 ):
     lat = lax.axis_index("lat")
     rows, width = scr_own.shape
@@ -405,7 +436,7 @@
     x = rolled(0)
 
     resid, normed = forward_core(
-        x, 1, lat, lat_total, (qkv_w, proj_w, gains), qkv_scr, bias, mixed_out, probs_scr
+        x, 1, (qkv_w, proj_w, gains), qkv_scr, bias, mixed_out, probs_scr, low_scr
     )
     n1_out[...] = normed
     stand2, inv2 = standardize(resid)
@@ -423,7 +454,7 @@
     dmix_scr[...] = dot_nt(low, proj_w[1]).astype(BF16)
     sums_out[...] = jnp.zeros(sums_out.shape, F32)
     attend_back(
-        qkv_scr, probs_scr, dmix_scr, field_out, sums_out, width, 0, probs_scr.shape[0]
+        qkv_scr, probs_scr, dmix_scr, field_out, sums_out, low_scr, prob_scr, width
     )
     ng = dot_nt(field_out[...], qkv_w[1]).astype(BF16).astype(F32)
     stand1, inv1 = standardize(x)
@@ -469,16 +500,34 @@
     total = pieces[0].astype(F32)
     for k in range(1, pieces.shape[0]):
         total = total + pieces[k].astype(F32)
-    for k in range(out.shape[0]):
-        out[k] = total.astype(BF16)
+    total = total.astype(BF16)
+    if len(out.shape) == len(pieces.shape):
+        for k in range(out.shape[0]):
+            out[k] = total
+    else:
+        out[...] = total
+
+
+def join_z(*refs):
+    out = refs[-1]
+    count = out.shape[0]
+    z = lax.div(lax.axis_index("lon"), 2)
+    for k in range(count):
+        out[lax.rem(z + count - k, count)] = refs[k][...]
 
 
 def third_kernel(
-    head, lon_tail, lat_head, diag_tail, resid_in, slope, active, mixed,
+    head, lon_tail, lat_head, diag_tail, resid_in, slope_in, active_in, mixed,
     proj_w, up_w, down_w, gains, keep_a,
     keep_out, give_out, rg_out, dmix_out, gain_out,
-    scr_own, scr_oth, m192, m768, mdown, flat_scr,
+    scr_own, scr_oth, m192, m768, mdown, flat_scr, slope, active, sems,
 ):
+    copies = [
+        pltpu.make_async_copy(slope_in, slope, sems.at[0]),
+        pltpu.make_async_copy(active_in, active, sems.at[1]),
+    ]
+    for copy in copies:
+        copy.start()
     rows, width = scr_own.shape
     cut = CHUNK * (WLON // 2)
     scr_own[0:cut, :] = lon_tail[...].astype(F32)
@@ -487,6 +536,8 @@
     scr_oth[cut:, :] = lat_head[...].astype(F32)
     g = merge_behind(scr_own, scr_oth, rows)
     g_low = g.astype(BF16)
+    for copy in copies:
+        copy.wait()
     hg = (dot(g_low, down_w[0]) * slope[...].astype(F32)).astype(BF16)
     stand2, inv2 = standardize(resid_in[...].astype(F32))
     normed2 = (stand2 * gains[0, 1:2, :]).astype(BF16)
@@ -520,20 +571,19 @@
 def fourth_kernel(
     x_in, qkv, probs_in, dmix, rg, gain_two, gains_late, order, qkv_w, gains,
     tokens_out, keep, give, bias_out,
-    field, sums, m576, flat_scr, dx_scr, probs, sems,
+    field, sums, m576, flat_scr, dx_scr, low_scr, prob_scr, probs, sems,
 ):
-    copies = [
-        pltpu.make_async_copy(probs_in.at[w], probs.at[w], sems.at[w])
-        for w in range(probs.shape[0])
-    ]
-    for copy in copies:
-        copy.start()
+    def probs_copy(w):
+        return pltpu.make_async_copy(probs_in.at[w], probs.at[w], sems.at[w])
+
+    for w in range(probs.shape[0]):
+        probs_copy(w).start()
     width = x_in.shape[-1]
     levels, lats, lons = tokens_out.shape[:3]
     sums[...] = jnp.zeros(sums.shape, F32)
-    for copy in copies:
-        copy.wait()
-    attend_back(qkv, probs, dmix, field, sums, width, 0, probs.shape[0])
+    attend_back(
+        qkv, probs, dmix, field, sums, low_scr, prob_scr, width, lambda w: probs_copy(w).wait()
+    )
     stand1, inv1 = standardize(x_in[...].astype(F32))
     normed = (stand1 * gains[0, 0:1, :]).astype(BF16)
     ng = dot_nt(field[...], qkv_w[0]).astype(BF16).astype(F32)
@@ -554,47 +604,54 @@
 
 
 def last_kernel(
-    units_a, units_c, extra, spread, own_ab, oth_ab, own_c, oth_c, update_out, bias_out,
-    scr, rows_scr, wide_scr, tab_scr,
+    units_a, units_c, extra, spread, same, same_x, cross, cross_x, own_c, oth_c,
+    update_out, bias_out, scr, rows_scr, wide_scr, tab_scr, ab, c,
 ):
     lat = lax.axis_index("lat")
-    lons = own_ab.shape[0]
-
-    def place(own, oth, first, last, dests):
+    x = lax.rem(lax.axis_index("lon"), 2)
+    lons = own_c.shape[0]
+    for j in range(lons):
+        c[lat, j] = own_c[j]
+        c[1 - lat, j] = oth_c[j]
+    for z in range(lons // 2):
+        ab[lat, 2 * z + x] = same[z]
+        ab[lat, 2 * z + 1 - x] = same_x[z]
+        ab[1 - lat, 2 * z + x] = cross[z]
+        ab[1 - lat, 2 * z + 1 - x] = cross_x[z]
+
+    def place(pieces, first, last, dests):
         total = jnp.zeros((UNIT, 128), F32)
         per = last - first
         k = 0
         for where, room in dests:
             for at in range(where, where + room, UNIT):
                 half, j, u = k // (per * lons), k // per % lons, k % per
-                value = jnp.where(
-                    lat == half, own[j, first + u].astype(F32), oth[j, first + u].astype(F32)
-                )
+                value = pieces[half, j, first + u].astype(F32)
                 scr[at : at + UNIT, :] = value
                 total = total + value * value
                 k += 1
         return total
 
     total = place(
-        own_ab, oth_ab, 0, units_a, [(864, 864), (2016, 288), (3456, 1152), (5760, 1152)]
+        ab, 0, units_a, [(864, 864), (2016, 288), (3456, 1152), (5760, 1152)]
     )
     total = total + place(
-        own_ab, oth_ab, units_a + extra, own_ab.shape[1],
+        ab, units_a + extra, ab.shape[2],
         [(1728, 288), (2304, 1152), (4608, 1152)],
     )
-    total = total + place(own_c, oth_c, 0, units_c, [(0, 864), (6912, 8)])
+    total = total + place(c, 0, units_c, [(0, 864), (6912, 8)])
     count = update_out.shape[0]
     mean = jnp.sum(total) * (1.0 / (count * 128))
     scale = lax.rsqrt(mean + 1e-06)
     update_out[...] = (scr[0:count, :] * scale).astype(BF16)
 
-    for b, (piece, base) in enumerate(((own_c, units_c), (own_ab, units_a))):
+    for b, (piece, base) in enumerate(((c, units_c), (ab, units_a))):
 
         def read(at):
             parts = []
             for r in range(CHUNK // UNIT):
                 k = at * (CHUNK // UNIT) + r
-                parts.append(piece[k // extra, base + k % extra].astype(F32))
+                parts.append(piece[lat, k // extra, base + k % extra].astype(F32))
             return jnp.concatenate(parts, axis=0)
 
         rest = read(2 * HEADS)
@@ -615,13 +672,17 @@
             bias_out[b, h] = tab_scr[h : h + 1, :]
 
 
-def call(kernel, outs, scratch, args, micros, mib, spaces=None):
+def call(kernel, outs, scratch, args, micros, mib, spaces=None, out_spaces=None):
     spaces = spaces or [pltpu.VMEM] * len(args)
+    out_spaces = out_spaces or [pltpu.VMEM] * len(outs)
     return pl.pallas_call(
         kernel,
-        out_shape=[jax.ShapeDtypeStruct(shape, dtype) for shape, dtype in outs],
+        out_shape=[
+            pltpu.HBM(*entry) if space == pltpu.HBM else jax.ShapeDtypeStruct(*entry)
+            for entry, space in zip(outs, out_spaces)
+        ],
         in_specs=[pl.BlockSpec(memory_space=space) for space in spaces],
-        out_specs=[pl.BlockSpec(memory_space=pltpu.VMEM)] * len(outs),
+        out_specs=[pl.BlockSpec(memory_space=space) for space in out_spaces],
         scratch_shapes=[
             pltpu.VMEM(*entry) if isinstance(entry, tuple) else entry for entry in scratch
         ],
@@ -639,6 +700,11 @@
 def lon_send(value, step):
     count = lax.axis_size("lon")
     return lax.ppermute(value, "lon", [(s, (s + step) % count) for s in range(count)])
+
+
+def x_swap(value):
+    count = lax.axis_size("lon")
+    return lax.ppermute(value, "lon", [(s, s ^ 1) for s in range(count)])
 
 
 def diag_send(value, step):
@@ -668,6 +734,7 @@
     token = (rows, width)
     field_shape = ((rows, 3 * width), BF16)
     probs_shape = ((wins, heads, WIN, WIN), F32)
+    stack_shape = ((heads * WIN, WIN), BF16)
     bias_shape = ((heads * WIN, WIN), F32)
     sums_shape = ((heads * WIN, WIDE), F32)
     tab_scr = ((8, table.shape[-1]), F32)
@@ -721,7 +788,12 @@
             ((1,) + proj_weight.shape[1:], BF16),
             ((1,) + up_weight.shape[1:], BF16),
             ((1,) + down_turned.shape[1:], BF16),
+            stack_shape,
+            probs_shape,
+            ((rows, hid), BF16),
+            ((rows, hid), BF16),
             pltpu.SemaphoreType.DMA((9,)),
+            pltpu.SemaphoreType.DMA((wins + 2,)),
         ],
         [
             pltpu.with_memory_space_constraint(arg, pltpu.HBM)
@@ -733,6 +805,7 @@
         8,
         28,
         [pltpu.HBM] * 9,
+        [pltpu.VMEM] * 5 + [pltpu.HBM, pltpu.VMEM, pltpu.HBM, pltpu.HBM],
     )
     lon_head = lon_send(head, -1)
     diag_head = diag_send(head, -1)
@@ -764,7 +837,15 @@
             sums_shape,
             ((2, width), F32),
         ],
-        [(token, F32), (token, F32), field_shape, probs_shape, (token, BF16)],
+        [
+            (token, F32),
+            (token, F32),
+            field_shape,
+            probs_shape,
+            (token, BF16),
+            stack_shape,
+            stack_shape,
+        ],
         (
             tail, lon_head, lat_tail, diag_head, bias1, qkv_weight, proj_weight, up_weight,
             down_turned, norm_gain,
@@ -795,13 +876,26 @@
             (token, BF16),
             ((1, width), F32),
         ],
-        [(token, F32), (token, F32), m192, m768, mdown, flat_scr(units_b)],
+        [
+            (token, F32),
+            (token, F32),
+            m192,
+            m768,
+            mdown,
+            flat_scr(units_b),
+            ((rows, hid), BF16),
+            ((rows, hid), BF16),
+            pltpu.SemaphoreType.DMA((2,)),
+        ],
         (
-            dhead, lon_tail, lat_dhead, diag_tail, resid0, slope0, active0, mixed0,
-            proj_weight, up_weight, down_turned, norm_gain, keep_a,
+            dhead, lon_tail, lat_dhead, diag_tail, resid0,
+            pltpu.with_memory_space_constraint(slope0, pltpu.HBM),
+            pltpu.with_memory_space_constraint(active0, pltpu.HBM),
+            mixed0, proj_weight, up_weight, down_turned, norm_gain, keep_a,
         ),
         2,
         20,
+        [pltpu.VMEM] * 5 + [pltpu.HBM] * 2 + [pltpu.VMEM] * 6,
     )
     got_b = lat_swap(give_b)
     (part_ab,) = call(
@@ -828,6 +922,8 @@
             m576,
             flat_scr(units_c),
             token_scr,
+            stack_shape,
+            stack_shape,
             probs_shape,
             pltpu.SemaphoreType.DMA((wins,)),
         ],
@@ -846,22 +942,38 @@
     pieces_c = lax.all_to_all(part_c, "lon", 0, 0)
 
     (sum_ab,) = call(
-        sum_pieces, [units(lon_size, units_a + extra + units_b)], [], (pieces_ab, part_c), 1, 10
-    )
-    whole_ab = lax.all_to_all(sum_ab, "lon", 0, 0)
+        sum_pieces, [units(units_a + extra + units_b)], [], (pieces_ab, part_c), 1, 10
+    )
     (sum_c,) = call(
         sum_pieces, [units(lon_size, units_c + extra)], [], (pieces_c, sum_ab), 1, 10
     )
+    (same_ab,) = call(
+        join_z,
+        [units(zs, units_a + extra + units_b)],
+        [],
+        [sum_ab] + [lon_send(sum_ab, 2 * k) for k in range(1, zs)] + [sum_c],
+        1,
+        10,
+    )
     whole_c = lax.all_to_all(sum_c, "lon", 0, 0)
-    oth_ab = lat_swap(whole_ab)
+    same_x = x_swap(same_ab)
+    cross = lat_swap(same_ab)
+    cross_x = lat_swap(same_x)
     oth_c = lat_swap(whole_c)
 
     flat_rows = (2 * block_rows * 128 + norm_gain.size) // 128
     update, bias_grad = call(
         functools.partial(last_kernel, units_a, units_c, extra),
         [((flat_rows, 128), BF16), (table.shape, F32)],
-        [((flat_rows + 2, 128), F32), ((CHUNK * 8, PAIR), F32), wide_scr, tab_scr],
-        (spread, whole_ab, oth_ab, whole_c, oth_c),
+        [
+            ((flat_rows + 2, 128), F32),
+            ((CHUNK * 8, PAIR), F32),
+            wide_scr,
+            tab_scr,
+            units(2, lon_size, units_a + extra + units_b),
+            units(2, lon_size, units_c + extra),
+        ],
+        (spread, same_ab, same_x, cross, cross_x, whole_c, oth_c),
         3,
         20,
     )

time: 133 us -> 112 us (0.84)
  blocking collectives: 36.6 us -> 0 us
  waiting for transfers between devices: 23.7 us -> 40.8 us
  starting transfers between devices: 14.8 us -> 25.2 us
  Pallas kernels: 50.2 us -> 42.9 us
  local copies, waits for them, and re-layouts: 6.26 us -> 1.15 us
    all_to_all x2 -> x0, blocking collectives: 36.6 us -> none  [the longest x1 26 us: shards(): whole_ab = lax.all_to_all(sum_ab, 'lon', 0, 0)]
    ppermute x0 -> x1, waiting for transfers between devices: none -> 7.97 us  [x_swap(): return lax.ppermute(value, 'lon', [(s, s ^ 1) for s in range(count)])]
    pallas_call x11 -> x12, Pallas kernels: 50.2 us -> 42.9 us  [call(): pl.pallas_call(kernel, out_shape=[pltpu.HBM(*entry) if space == pltpu.HBM...]
    ppermute x2 -> x5, waiting for transfers between devices: 2.78 us -> 10.1 us  [lon_send(): lax.ppermute(value, 'lon', [(s, (s + step) % count) for s in range(count)])]
    all_to_all x1, waiting for transfers between devices: 4.11 us -> 10.3 us  [shards(): pieces_ab = lax.all_to_all(part_ab, 'lon', 0, 0)]
    unnamed x28 -> x18, local copies, waits for them, and re-layouts: 6.26 us -> 1.15 us
    ppermute x2 -> x5, starting transfers between devices: 0.78 us -> 5.78 us  [lon_send(): lax.ppermute(value, 'lon', [(s, (s + step) % count) for s in range(count)])]
    all_to_all x1, waiting for transfers between devices: 7.64 us -> 3.05 us  [shards(): pieces_c = lax.all_to_all(part_c, 'lon', 0, 0)]
  transfers between devices with their start and end apart: 13 -> 19, of which waited for: 9 -> 12; matrix products, arithmetic and copies ran while one was open for 0% -> 0% of each run, Pallas kernels for 15% -> 16%
where the time goes in v5:
time: 112 us; the launch traced here: 111 us
  Pallas kernels  42.9 us (38%)
  waiting for transfers between devices  40.8 us (36%)
  starting transfers between devices  25.2 us (22%)
  local copies, waits for them, and re-layouts  1.15 us (1%)
    pallas_call x12, Pallas kernels, call(): pl.pallas_call(kernel, out_shape=[pltpu.HBM(*entry) if space == pltpu.HBM...  42.9 us
    all_to_all x1, waiting for transfers between devices, shards(): pieces_ab = lax.all_to_all(part_ab, 'lon', 0, 0)  10.3 us
    ppermute x5, waiting for transfers between devices, lon_send(): lax.ppermute(value, 'lon', [(s, (s + step) % count) for s in range(count)])  10.1 us
    ppermute x1, waiting for transfers between devices, x_swap(): return lax.ppermute(value, 'lon', [(s, s ^ 1) for s in range(count)])  7.97 us
    ppermute x5, starting transfers between devices, lon_send(): lax.ppermute(value, 'lon', [(s, (s + step) % count) for s in range(count)])  5.78 us
    ppermute x2, starting transfers between devices, diag_send(): return lax.ppermute(value, ('lon', 'lat'), pairs)  5.74 us
    ppermute x2, waiting for transfers between devices, diag_send(): return lax.ppermute(value, ('lon', 'lat'), pairs)  4.77 us
    ppermute x8, waiting for transfers between devices, lat_swap(): return lax.ppermute(value, 'lat', [(0, 1), (1, 0)])  4.38 us
  transfers between devices with their start and end apart: 19, of which 12 were waited for; matrix products, arithmetic and copies ran while one was open for 0% of the time, Pallas kernels for 16%

profile of v5, /device:TPU:0, one launch (start us, length us, event | category | flops | bytes accessed | tf_op | source)
XLA Modules:
  0.0 110.9 jit_solution(2515763085270444448)
XLA Ops:
  0.6 0.0 copy-start.6
  0.7 9.3 %shard_map.112 = (bf16[576,192]{1,0:T(8,128)(2,1)S(1)}, bf16[2,504,192]{2,1,0:T(8,128)(2,1)S(1)}, bf16[2,72,192]{2,1,0:T(8,128)(2,1)S(1)}, bf16[576,576]{1,0:T(8...) custom-call(bf16[2,12,24,192]{3,2,1,0:T(8,128)(2,1)} %tokens_in.1, ...), custom_call_target="tpu_custom_call" | custom-call | flops 8800000000 | bytes 100000 | tf_op jit(solution)/shard_map/pallas_call | solution.py:678
  10.0 0.5 collective-permute-start.1
  10.5 0.0 copy-start.5
  10.5 5.7 %collective-permute-start.2 = (bf16[2,72,192]{2,1,0:T(8,128)(2,1)S(1)}, bf16[2,72,192]{2,1,0:T(8,128)(2,1)S(1)}, u32[]{:S(2)}, u32[]{:S(2)}) collective-permute-start(bf16[2,72,192]{2,1,0:T(8,128)(2,1)S(1)} %get-tuple-element.42), channel_id=1, source_target_pairs={{0,15},{1,14},{2,1},{3,0},{4,3},{5,2},{6,5},{7,4},{8,7},{9,6},{10,... | collective-permute-start | bytes 165896 | tf_op jit(solution)/shard_map/ppermute | solution.py:716
  16.2 0.5 collective-permute-start
  16.8 0.9 shard_map.113.bias
  17.7 1.1 %collective-permute-done.2.diag_head = bf16[2,72,192]{2,1,0:T(8,128)(2,1)S(1)} collective-permute-done((bf16[2,72,192]{2,1,0:T(8,128)(2,1)S(1)}, bf16[2,72,192]{2,1,0:T(8,128)(2,1)S(1)}, u32[]{:S(2)}, u32[]{:S(2)}) %collective-permute-start.2) | collective-permute-done | bytes 55328 | tf_op jit(solution)/shard_map/ppermute | solution.py:716
  18.8 1.7 %collective-permute-done.lon_head = bf16[2,72,192]{2,1,0:T(8,128)(2,1)S(1)} collective-permute-done((bf16[2,72,192]{2,1,0:T(8,128)(2,1)S(1)}, bf16[2,72,192]{2,1,0:T(8,128)(2,1)S(1)}, u32[]{:S(2)}, u32[]{:S(2)}) %collective-permute-start) | collective-permute-done | bytes 55328 | tf_op jit(solution)/shard_map/ppermute | solution.py:702
  20.6 0.0 collective-permute-done.1.lat_tail
  20.6 11.5 %shard_map.114 = (bf16[504,192]{1,0:T(8,128)(2,1)S(1)}, bf16[72,192]{1,0:T(8,128)(2,1)S(1)}, bf16[576,192]{1,0:T(8,128)(2,1)S(1)}, bf16[576,576]{1,0:T(8,128)(2,...) custom-call(bf16[2,504,192]{2,1,0:T(8,128)(2,1)S(1)} %get-tuple-elem, ...), custom_call_target="tpu_custom_call" | custom-call | flops 20899999744 | bytes 100000 | tf_op jit(solution)/shard_map/pallas_call | solution.py:678
  32.2 0.1 collective-permute-start.5
  32.2 0.2 collective-permute-start.3
  32.5 0.1 collective-permute-start.4
  32.5 1.7 %shard_map.115 = (bf16[8,27,8,128]{3,2,1,0:T(8,128)(2,1)S(1)}, bf16[8,27,8,128]{3,2,1,0:T(8,128)(2,1)S(1)}, bf16[8,5,8,128]{3,2,1,0:T(8,128)(2,1)S(1)}) custom-call(bf16[576,192]{1,0:T(8,128)(2,1)S(1)} %get-tuple-element.49.n1, bf16[576,576]{1,0:T(8,128)(2,1)S(1)} %get-tuple-element.50.field, bf16[576,192]{1,0:T(8,128)(2,1)S(1)} %get-tuple-element.51.mixed, ...), custom_call_target="tpu_custom_call" | custom-call | flops 3300000000 | bytes 100000 | tf_op jit(solution)/shard_map/pallas_call | solution.py:678
  34.2 0.6 collective-permute-start.6
  34.8 3.6 %collective-permute-done.5.diag_tail = bf16[72,192]{1,0:T(8,128)(2,1)S(1)} collective-permute-done((bf16[72,192]{1,0:T(8,128)(2,1)S(1)}, bf16[72,192]{1,0:T(8,128)(2,1)S(1)}, u32[]{:S(2)}, u32[]{:S(2)}) %collective-permute-start.5) | collective-permute-done | bytes 27680 | tf_op jit(solution)/shard_map/ppermute | solution.py:716
  38.4 1.1 collective-permute-done.3.lon_tail
  39.5 3.5 %shard_map.116 = (bf16[8,21,8,128]{3,2,1,0:T(8,128)(2,1)S(1)}, bf16[8,21,8,128]{3,2,1,0:T(8,128)(2,1)S(1)}, f32[576,192]{1,0:T(8,128)S(1)}, bf16[576,192]{1,0:T(8,128)(2,1)S(1)}, f32[1,192]{1,0:T(1,128)S(1)}) custom-call(bf16[504,192]{1,0:T(8,128)(2,1)S(1)} %get-tuple-element.43.head, bf16[72,192]{1,0:T(8,128)(2,1)S(1)} %collective-permute-done.3.lon_tail, ...), custom_call_target="tpu_custom_call" | custom-call | flops 2200000000 | bytes 100000 | tf_op jit(solution)/shard_map/pallas_call | solution.py:678
  43.0 0.1 collective-permute-start.7
  43.1 1.6 %collective-permute-done.7.got_b = bf16[8,21,8,128]{3,2,1,0:T(8,128)(2,1)S(1)} collective-permute-done((bf16[8,21,8,128]{3,2,1,0:T(8,128)(2,1)S(1)}, bf16[8,21,8,128]{3,2,1,0:T(8,128)(2,1)S(1)}, u32[]{:S(2)}, u32[]{:S(2)}) %collective-permute-start.7) | collective-permute-done | bytes 344096 | tf_op jit(solution)/shard_map/ppermute | solution.py:697
  44.7 1.1 shard_map.117.order
  45.8 3.6 %all-to-all-start = ((bf16[8,53,8,128]{3,2,1,0:T(8,128)(2,1)}), bf16[8,53,8,128]{3,2,1,0:T(8,128)(2,1)S(1)}, u32[]{:S(2)}, u32[]{:S(2)}) async-start(bf16[8,53,8,128]{3,2,1,0:T(8,128)(2,1)} %shard_map.117.order), calls=%async_computation | async-start | bytes 1736704 | tf_op jit(solution)/shard_map/all_to_all | solution.py:909
  49.3 1.1 copy-done.8
  50.4 8.9 %shard_map.118 = (bf16[2,12,24,192]{3,2,1,0:T(8,128)(2,1)}, bf16[8,7,8,128]{3,2,1,0:T(8,128)(2,1)S(1)}, bf16[8,7,8,128]{3,2,1,0:T(8,128)(2,1)S(1)}, bf16[8,5,8,128]{3,2,1,0:T(8,128)(2,1)S(1)}) custom-call(bf16[576,192]{1,0:T(8,128)(2,1)S(1)} %get-tuple-element.38.x_in, bf16[576,576]{1,0:T(8,128)(2,1)S(1)} %copy-done.8, ...), custom_call_target="tpu_custom_call" | custom-call | flops 12099999744 | bytes 100000 | tf_op jit(solution)/shard_map/pallas_call | solution.py:678
  59.3 0.2 collective-permute-start.8
  59.5 1.2 %collective-permute-done.8.got = bf16[8,7,8,128]{3,2,1,0:T(8,128)(2,1)S(1)} collective-permute-done((bf16[8,7,8,128]{3,2,1,0:T(8,128)(2,1)S(1)}, bf16[8,7,8,128]{3,2,1,0:T(8,128)(2,1)S(1)}, u32[]{:S(2)}, u32[]{:S(2)}) %collective-permute-start.8) | collective-permute-done | bytes 114720 | tf_op jit(solution)/shard_map/ppermute | solution.py:697
  60.7 0.7 shard_map.119.order
  61.4 10.3 %all-to-all-done.pieces = bf16[8,53,8,128]{3,2,1,0:T(8,128)(2,1)S(1)} async-done(((bf16[8,53,8,128]{3,2,1,0:T(8,128)(2,1)}), bf16[8,53,8,128]{3,2,1,0:T(8,128)(2,1)S(1)}, u32[]{:S(2)}, u32[]{:S(2)}) %all-to-all-start) | async-done | bytes 868384 | tf_op jit(solution)/shard_map/all_to_all | solution.py:909
  71.7 3.6 %all-to-all-start.1 = ((bf16[8,12,8,128]{3,2,1,0:T(8,128)(2,1)}), bf16[8,12,8,128]{3,2,1,0:T(8,128)(2,1)S(1)}, u32[]{:S(2)}, u32[]{:S(2)}) async-start(bf16[8,12,8,128]{3,2,1,0:T(8,128)(2,1)} %shard_map.119.order), calls=%async_computation.1 | async-start | bytes 393216 | tf_op jit(solution)/shard_map/all_to_all | solution.py:942
  75.4 1.1 shard_map.120.order.refs_0_
  76.4 3.9 %collective-permute-start.11 = (bf16[53,8,128]{2,1,0:T(8,128)(2,1)S(1)}, bf16[53,8,128]{2,1,0:T(8,128)(2,1)S(1)}, u32[]{:S(2)}, u32[]{:S(2)}) collective-permute-start(bf16[53,8,128]{2,1,0:T(8,128)(2,1)S(1)} %shard_map.120.order.refs_0_), channel_id=1, source_target_pairs={{0,12},{2,14},{4,0},{6,2},{8,4},{10,6},{12,8},{14,10},{1,13},{3,15... | collective-permute-start | bytes 325640 | tf_op jit(solution)/shard_map/ppermute | solution.py:702
  80.3 0.0 collective-permute-start.10
  80.3 1.1 %collective-permute-start.9 = (bf16[53,8,128]{2,1,0:T(8,128)(2,1)S(1)}, bf16[53,8,128]{2,1,0:T(8,128)(2,1)S(1)}, u32[]{:S(2)}, u32[]{:S(2)}) collective-permute-start(bf16[53,8,128]{2,1,0:T(8,128)(2,1)S(1)} %shard_map.120.order.refs_0_), channel_id=1, source_target_pairs={{0,4},{2,6},{4,8},{6,10},{8,12},{10,14},{12,0},{14,2},{1,5},{3,7},... | collective-permute-start | bytes 325640 | tf_op jit(solution)/shard_map/ppermute | solution.py:702
  81.4 3.1 %all-to-all-done.1.pieces = bf16[8,12,8,128]{3,2,1,0:T(8,128)(2,1)S(1)} async-done(((bf16[8,12,8,128]{3,2,1,0:T(8,128)(2,1)}), bf16[8,12,8,128]{3,2,1,0:T(8,128)(2,1)S(1)}, u32[]{:S(2)}, u32[]{:S(2)}) %all-to-all-start.1) | async-done | bytes 196640 | tf_op jit(solution)/shard_map/all_to_all | solution.py:942
  84.5 0.7 shard_map.121.refs_4_
  85.2 0.0 collective-permute-done.11.refs_3_
  85.2 7.2 %collective-permute-done.10.refs_2_ = bf16[53,8,128]{2,1,0:T(8,128)(2,1)S(1)} collective-permute-done((bf16[53,8,128]{2,1,0:T(8,128)(2,1)S(1)}, bf16[53,8,128]{2,1,0:T(8,128)(2,1)S(1)}, u32[]{:S(2)}, u32[]{:S(2)}) %collective-permute-start.10) | collective-permute-done | bytes 108576 | tf_op jit(solution)/shard_map/ppermute | solution.py:702
  92.4 1.0 shard_map.122.same
  93.4 1.4 %collective-permute-start.12 = (bf16[4,53,8,128]{3,2,1,0:T(8,128)(2,1)S(1)}, bf16[4,53,8,128]{3,2,1,0:T(8,128)(2,1)S(1)}, u32[]{:S(2)}, u32[]{:S(2)}) collective-permute-start(bf16[4,53,8,128]{3,2,1,0:T(8,128)(2,1)S(1)} %shard_map.122.same), channel_id=1, source_target_pairs={{0,2},{2,0},{4,6},{6,4},{8,10},{10,8},{12,14},{14,12},{1,3},{3,1},... | collective-permute-start | bytes 1302536 | tf_op jit(solution)/shard_map/ppermute | solution.py:707
  94.8 3.4 %all-to-all-start.2 = ((bf16[8,12,8,128]{3,2,1,0:T(8,128)(2,1)}), bf16[8,12,8,128]{3,2,1,0:T(8,128)(2,1)S(1)}, u32[]{:S(2)}, u32[]{:S(2)}) async-start(bf16[8,12,8,128]{3,2,1,0:T(8,128)(2,1)} %shard_map.121.refs_4_), calls=%async_computation.2 | async-start | bytes 393216 | tf_op jit(solution)/shard_map/all_to_all | solution.py:958
  98.2 0.1 collective-permute-start.13
  98.3 8.0 %collective-permute-done.12.same_x = bf16[4,53,8,128]{3,2,1,0:T(8,128)(2,1)S(1)} collective-permute-done((bf16[4,53,8,128]{3,2,1,0:T(8,128)(2,1)S(1)}, bf16[4,53,8,128]{3,2,1,0:T(8,128)(2,1)S(1)}, u32[]{:S(2)}, u32[]{:S(2)}) %collective-permute-start.12) | collective-permute-done | bytes 434208 | tf_op jit(solution)/shard_map/ppermute | solution.py:707
  106.3 0.0 collective-permute-start.14
  106.3 0.3 all-to-all-done.2.own_c
  106.5 0.3 collective-permute-start.15
  106.8 1.5 %collective-permute-done.15.oth_c = bf16[8,12,8,128]{3,2,1,0:T(8,128)(2,1)S(1)} collective-permute-done((bf16[8,12,8,128]{3,2,1,0:T(8,128)(2,1)S(1)}, bf16[8,12,8,128]{3,2,1,0:T(8,128)(2,1)S(1)}, u32[]{:S(2)}, u32[]{:S(2)}) %collective-permute-start.15) | collective-permute-done | bytes 196640 | tf_op jit(solution)/shard_map/ppermute | solution.py:697
  108.3 2.6 %shard_map.123 = (bf16[6918,128]{1,0:T(8,128)(2,1)}, f32[2,6,1,6336]{3,2,1,0:T(1,128)}) custom-call(bf16[2,132,384]{2,1,0:T(8,128)(2,1)S(1)} %copy-done.6, bf16[4,53,8,128]{3,2,1,0:T(8,128)(2,1)S(1)} %shard_map.122.same, bf16[4,53,8,128]{3,2,1,0:T(8,128)(2,1)S(1)} %collective-permute-done.12.same_x, ...), custom_call_target="tpu_custom_call" | custom-call | flops 3300000000 | bytes 100000 | tf_op jit(solution)/shard_map/pallas_call | solution.py:678
  (20 shorter events, 0.0 us)
Async XLA Ops:
  0.6 16.1 %copy-start.3 = (f32[2,1,6,6336]{3,1,2,0:T(1,128)S(1)}, f32[2,1,6,6336]{3,1,2,0:T(1,128)}, u32[]{:S(2)}) copy-start(f32[2,1,6,6336]{3,1,2,0:T(1,128)} %param.16) | copy-start | bytes 912388
  0.6 16.1 %copy-start.6 = (bf16[2,132,384]{2,1,0:T(8,128)(2,1)S(1)}, bf16[2,132,384]{2,1,0:T(8,128)(2,1)}, u32[]{:S(2)}) copy-start(bf16[2,132,384]{2,1,0:T(8,128)(2,1)} %constant.2.clone.spread_in.spread) | copy-start | bytes 608260
  10.0 7.7 %copy-start.7 = (bf16[576,576]{1,0:T(8,128)(2,1)}, bf16[576,576]{1,0:T(8,128)(2,1)S(1)}, u32[]{:S(2)}) copy-start(bf16[576,576]{1,0:T(8,128)(2,1)S(1)} %get-tuple-element.39.qkv) | copy-start | bytes 1990660
  10.0 10.6 %collective-permute-start.1 = (bf16[2,504,192]{2,1,0:T(8,128)(2,1)S(1)}, bf16[2,504,192]{2,1,0:T(8,128)(2,1)S(1)}, u32[]{:S(2)}, u32[]{:S(2)}) collective-permute-start(bf16[2,504,192]{2,1,0:T(8,128)(2,1)S(1)} %get-tuple-element.41.tail), channel_id=1, source_target_pairs={{0,1},{1,0},{2,3},{3,2},{4,5},{5,4},{6,7},{7,6},{8,9},{9,8},{10,11... | collective-permute-start | bytes 1161224 | tf_op jit(solution)/shard_map/ppermute | solution.py:697
  10.5 10.1 %copy-start = (bf16[2,192,768]{2,1,0:T(8,128)(2,1)S(1)}, bf16[2,192,768]{2,1,0:T(8,128)(2,1)}, u32[]{:S(2)}) copy-start(bf16[2,192,768]{2,1,0:T(8,128)(2,1)} %up_w.3) | copy-start | bytes 1769476
  10.5 10.1 %copy-start.1 = (bf16[2,768,192]{1,2,0:T(8,128)(2,1)S(1)}, bf16[2,768,192]{1,2,0:T(8,128)(2,1)}, u32[]{:S(2)}) copy-start(bf16[2,768,192]{1,2,0:T(8,128)(2,1)} %param.14) | copy-start | bytes 1769476
  10.5 10.1 %copy-start.2 = (bf16[2,192,576]{2,1,0:T(8,128)(2,1)S(1)}, bf16[2,192,576]{2,1,0:T(8,128)(2,1)}, u32[]{:S(2)}) copy-start(bf16[2,192,576]{2,1,0:T(8,128)(2,1)} %qkv_w.3) | copy-start | bytes 1327108
  10.5 10.1 %copy-start.4 = (bf16[2,192,192]{2,1,0:T(8,128)(2,1)S(1)}, bf16[2,192,192]{2,1,0:T(8,128)(2,1)}, u32[]{:S(2)}) copy-start(bf16[2,192,192]{2,1,0:T(8,128)(2,1)} %proj_w.3) | copy-start | bytes 442372
  10.5 10.1 %copy-start.5 = (f32[2,2,192]{2,1,0:T(2,128)S(1)}, f32[2,2,192]{2,1,0:T(2,128)}, u32[]{:S(2)}) copy-start(f32[2,2,192]{2,1,0:T(2,128)} %gains.5) | copy-start | bytes 9220
  10.5 8.3 %collective-permute-start.2 = (bf16[2,72,192]{2,1,0:T(8,128)(2,1)S(1)}, bf16[2,72,192]{2,1,0:T(8,128)(2,1)S(1)}, u32[]{:S(2)}, u32[]{:S(2)}) collective-permute-start(bf16[2,72,192]{2,1,0:T(8,128)(2,1)S(1)} %get-tuple-element.42), channel_id=1, source_target_pairs={{0,15},{1,14},{2,1},{3,0},{4,3},{5,2},{6,5},{7,4},{8,7},{9,6},{10,... | collective-permute-start | bytes 165896 | tf_op jit(solution)/shard_map/ppermute | solution.py:716
  16.2 4.4 %collective-permute-start = (bf16[2,72,192]{2,1,0:T(8,128)(2,1)S(1)}, bf16[2,72,192]{2,1,0:T(8,128)(2,1)S(1)}, u32[]{:S(2)}, u32[]{:S(2)}) collective-permute-start(bf16[2,72,192]{2,1,0:T(8,128)(2,1)S(1)} %get-tuple-element.42), channel_id=1, source_target_pairs={{0,14},{2,0},{4,2},{6,4},{8,6},{10,8},{12,10},{14,12},{1,15},{3,1}... | collective-permute-start | bytes 165896 | tf_op jit(solution)/shard_map/ppermute | solution.py:702
  32.2 6.2 %collective-permute-start.5 = (bf16[72,192]{1,0:T(8,128)(2,1)S(1)}, bf16[72,192]{1,0:T(8,128)(2,1)S(1)}, u32[]{:S(2)}, u32[]{:S(2)}) collective-permute-start(bf16[72,192]{1,0:T(8,128)(2,1)S(1)} %get-tuple-element.44), channel_id=1, source_target_pairs={{0,3},{1,2},{2,5},{3,4},{4,7},{5,6},{6,9},{7,8},{8,11},{9,10},{10,... | collective-permute-start | bytes 82952 | tf_op jit(solution)/shard_map/ppermute | solution.py:716
  32.2 7.3 %collective-permute-start.3 = (bf16[72,192]{1,0:T(8,128)(2,1)S(1)}, bf16[72,192]{1,0:T(8,128)(2,1)S(1)}, u32[]{:S(2)}, u32[]{:S(2)}) collective-permute-start(bf16[72,192]{1,0:T(8,128)(2,1)S(1)} %get-tuple-element.44), channel_id=1, source_target_pairs={{0,2},{2,4},{4,6},{6,8},{8,10},{10,12},{12,14},{14,0},{1,3},{3,5},... | collective-permute-start | bytes 82952 | tf_op jit(solution)/shard_map/ppermute | solution.py:702
  32.5 7.0 %collective-permute-start.4 = (bf16[504,192]{1,0:T(8,128)(2,1)S(1)}, bf16[504,192]{1,0:T(8,128)(2,1)S(1)}, u32[]{:S(2)}, u32[]{:S(2)}) collective-permute-start(bf16[504,192]{1,0:T(8,128)(2,1)S(1)} %get-tuple-element.43.head), channel_id=1, source_target_pairs={{0,1},{1,0},{2,3},{3,2},{4,5},{5,4},{6,7},{7,6},{8,9},{9,8},{10,11... | collective-permute-start | bytes 580616 | tf_op jit(solution)/shard_map/ppermute | solution.py:697
  34.2 8.8 %collective-permute-start.6 = (bf16[8,27,8,128]{3,2,1,0:T(8,128)(2,1)S(1)}, bf16[8,27,8,128]{3,2,1,0:T(8,128)(2,1)S(1)}, u32[]{:S(2)}, u32[]{:S(2)}) collective-permute-start(bf16[8,27,8,128]{3,2,1,0:T(8,128)(2,1)S(1)} %get-tuple-element.63), channel_id=1, source_target_pairs={{0,1},{1,0},{2,3},{3,2},{4,5},{5,4},{6,7},{7,6},{8,9},{9,8},{10,11... | collective-permute-start | bytes 1327112 | tf_op jit(solution)/shard_map/ppermute | solution.py:697
  43.0 1.7 %collective-permute-start.7 = (bf16[8,21,8,128]{3,2,1,0:T(8,128)(2,1)S(1)}, bf16[8,21,8,128]{3,2,1,0:T(8,128)(2,1)S(1)}, u32[]{:S(2)}, u32[]{:S(2)}) collective-permute-start(bf16[8,21,8,128]{3,2,1,0:T(8,128)(2,1)S(1)} %get-tuple-element.66), channel_id=1, source_target_pairs={{0,1},{1,0},{2,3},{3,2},{4,5},{5,4},{6,7},{7,6},{8,9},{9,8},{10,11... | collective-permute-start | bytes 1032200 | tf_op jit(solution)/shard_map/ppermute | solution.py:697
  45.8 26.0 %all-to-all-start = ((bf16[8,53,8,128]{3,2,1,0:T(8,128)(2,1)}), bf16[8,53,8,128]{3,2,1,0:T(8,128)(2,1)S(1)}, u32[]{:S(2)}, u32[]{:S(2)}) async-start(bf16[8,53,8,128]{3,2,1,0:T(8,128)(2,1)} %shard_map.117.order), calls=%async_computation | async-start | bytes 1736704 | tf_op jit(solution)/shard_map/all_to_all | solution.py:909
  49.3 1.1 %copy-start.8 = (bf16[576,576]{1,0:T(8,128)(2,1)S(1)}, bf16[576,576]{1,0:T(8,128)(2,1)}, u32[]{:S(2)}) copy-start(bf16[576,576]{1,0:T(8,128)(2,1)} %copy-done.7) | copy-start | bytes 1990660
  59.3 1.4 %collective-permute-start.8 = (bf16[8,7,8,128]{3,2,1,0:T(8,128)(2,1)S(1)}, bf16[8,7,8,128]{3,2,1,0:T(8,128)(2,1)S(1)}, u32[]{:S(2)}, u32[]{:S(2)}) collective-permute-start(bf16[8,7,8,128]{3,2,1,0:T(8,128)(2,1)S(1)} %get-tuple-element.69), channel_id=1, source_target_pairs={{0,1},{1,0},{2,3},{3,2},{4,5},{5,4},{6,7},{7,6},{8,9},{9,8},{10,11... | collective-permute-start | bytes 344072 | tf_op jit(solution)/shard_map/ppermute | solution.py:697
  71.7 12.7 %all-to-all-start.1 = ((bf16[8,12,8,128]{3,2,1,0:T(8,128)(2,1)}), bf16[8,12,8,128]{3,2,1,0:T(8,128)(2,1)S(1)}, u32[]{:S(2)}, u32[]{:S(2)}) async-start(bf16[8,12,8,128]{3,2,1,0:T(8,128)(2,1)} %shard_map.119.order), calls=%async_computation.1 | async-start | bytes 393216 | tf_op jit(solution)/shard_map/all_to_all | solution.py:942
  76.4 8.8 %collective-permute-start.11 = (bf16[53,8,128]{2,1,0:T(8,128)(2,1)S(1)}, bf16[53,8,128]{2,1,0:T(8,128)(2,1)S(1)}, u32[]{:S(2)}, u32[]{:S(2)}) collective-permute-start(bf16[53,8,128]{2,1,0:T(8,128)(2,1)S(1)} %shard_map.120.order.refs_0_), channel_id=1, source_target_pairs={{0,12},{2,14},{4,0},{6,2},{8,4},{10,6},{12,8},{14,10},{1,13},{3,15... | collective-permute-start | bytes 325640 | tf_op jit(solution)/shard_map/ppermute | solution.py:702
  80.3 12.1 %collective-permute-start.10 = (bf16[53,8,128]{2,1,0:T(8,128)(2,1)S(1)}, bf16[53,8,128]{2,1,0:T(8,128)(2,1)S(1)}, u32[]{:S(2)}, u32[]{:S(2)}) collective-permute-start(bf16[53,8,128]{2,1,0:T(8,128)(2,1)S(1)} %shard_map.120.order.refs_0_), channel_id=1, source_target_pairs={{0,8},{2,10},{4,12},{6,14},{8,0},{10,2},{12,4},{14,6},{1,9},{3,11}... | collective-permute-start | bytes 325640 | tf_op jit(solution)/shard_map/ppermute | solution.py:702
  80.3 12.1 %collective-permute-start.9 = (bf16[53,8,128]{2,1,0:T(8,128)(2,1)S(1)}, bf16[53,8,128]{2,1,0:T(8,128)(2,1)S(1)}, u32[]{:S(2)}, u32[]{:S(2)}) collective-permute-start(bf16[53,8,128]{2,1,0:T(8,128)(2,1)S(1)} %shard_map.120.order.refs_0_), channel_id=1, source_target_pairs={{0,4},{2,6},{4,8},{6,10},{8,12},{10,14},{12,0},{14,2},{1,5},{3,7},... | collective-permute-start | bytes 325640 | tf_op jit(solution)/shard_map/ppermute | solution.py:702
  93.4 12.9 %collective-permute-start.12 = (bf16[4,53,8,128]{3,2,1,0:T(8,128)(2,1)S(1)}, bf16[4,53,8,128]{3,2,1,0:T(8,128)(2,1)S(1)}, u32[]{:S(2)}, u32[]{:S(2)}) collective-permute-start(bf16[4,53,8,128]{3,2,1,0:T(8,128)(2,1)S(1)} %shard_map.122.same), channel_id=1, source_target_pairs={{0,2},{2,0},{4,6},{6,4},{8,10},{10,8},{12,14},{14,12},{1,3},{3,1},... | collective-permute-start | bytes 1302536 | tf_op jit(solution)/shard_map/ppermute | solution.py:707
  94.8 11.7 %all-to-all-start.2 = ((bf16[8,12,8,128]{3,2,1,0:T(8,128)(2,1)}), bf16[8,12,8,128]{3,2,1,0:T(8,128)(2,1)S(1)}, u32[]{:S(2)}, u32[]{:S(2)}) async-start(bf16[8,12,8,128]{3,2,1,0:T(8,128)(2,1)} %shard_map.121.refs_4_), calls=%async_computation.2 | async-start | bytes 393216 | tf_op jit(solution)/shard_map/all_to_all | solution.py:958
  98.2 10.1 %collective-permute-start.13 = (bf16[4,53,8,128]{3,2,1,0:T(8,128)(2,1)S(1)}, bf16[4,53,8,128]{3,2,1,0:T(8,128)(2,1)S(1)}, u32[]{:S(2)}, u32[]{:S(2)}) collective-permute-start(bf16[4,53,8,128]{3,2,1,0:T(8,128)(2,1)S(1)} %shard_map.122.same), channel_id=1, source_target_pairs={{0,1},{1,0},{2,3},{3,2},{4,5},{5,4},{6,7},{7,6},{8,9},{9,8},{10,11... | collective-permute-start | bytes 1302536 | tf_op jit(solution)/shard_map/ppermute | solution.py:697
  106.3 2.1 %collective-permute-start.14 = (bf16[4,53,8,128]{3,2,1,0:T(8,128)(2,1)S(1)}, bf16[4,53,8,128]{3,2,1,0:T(8,128)(2,1)S(1)}, u32[]{:S(2)}, u32[]{:S(2)}) collective-permute-start(bf16[4,53,8,128]{3,2,1,0:T(8,128)(2,1)S(1)} %collective-permute-done.12.same_x), channel_id=1, source_target_pairs={{0,1},{1,0},{2,3},{3,2},{4,5},{5,4},{6,7},{7,6},{8,9},{9,8},{10,11... | collective-permute-start | bytes 1302536 | tf_op jit(solution)/shard_map/ppermute | solution.py:697
  106.5 1.8 %collective-permute-start.15 = (bf16[8,12,8,128]{3,2,1,0:T(8,128)(2,1)S(1)}, bf16[8,12,8,128]{3,2,1,0:T(8,128)(2,1)S(1)}, u32[]{:S(2)}, u32[]{:S(2)}) collective-permute-start(bf16[8,12,8,128]{3,2,1,0:T(8,128)(2,1)S(1)} %all-to-all-done.2.own_c), channel_id=1, source_target_pairs={{0,1},{1,0},{2,3},{3,2},{4,5},{5,4},{6,7},{7,6},{8,9},{9,8},{10,11... | collective-permute-start | bytes 589832 | tf_op jit(solution)/shard_map/ppermute | solution.py:697

commit v6 on v5

--- a/solution.py
+++ b/solution.py
@@ -59,6 +59,10 @@
     second = row_mean(scaled * stand)
     gain_grad = jnp.sum(d * stand, axis=0, keepdims=True)
     return inv * (scaled - first - stand * second), gain_grad
+
+
+def gelu_value(hidden):
+    return 0.5 * hidden * (1.0 + lax.erf(hidden * ROOT_HALF))
 
 
 def gelu_parts(hidden):
@@ -313,10 +317,10 @@
 
 def first_kernel(
     lat_total, tokens_in, cot_in, table_in, spread_in, qkv_in, proj_in, up_in, down_in, gains_in,
-    x_out, tail_out, head_out, qkv_out, mixed_out, probs_out, resid_out, slope_out, active_out,
+    x_out, tail_out, head_out, qkv_out, mixed_out, probs_out, resid_out, hidden_out, active_out,
     scr, cot_scr, tab_scr, rows_scr, wide_scr, bias_scr,
     cot, table, spread, tokens, qkv_w, gains, proj_w, up_w, down_w, stack_scr,
-    probs, slope_scr, active_scr, sems, out_sems,
+    probs, active_scr, sems, out_sems,
 ):
     copies = []
     for source, target in (
@@ -364,29 +368,37 @@
     resid_out[...] = resid.astype(BF16)
     stand, _ = standardize(resid)
     normed = (stand * gains[0, 1:2, :]).astype(BF16)
-    active, slope = gelu_parts(dot(normed, up_w[0]))
-    active = active.astype(BF16)
+    hidden = dot(normed, up_w[0])
+    hidden_out[...] = hidden
+    active = gelu_value(hidden).astype(BF16)
     active_scr[...] = active
-    slope_scr[...] = slope.astype(BF16)
     wins = probs.shape[0]
-    last = [
-        pltpu.make_async_copy(active_scr, active_out, out_sems.at[wins]),
-        pltpu.make_async_copy(slope_scr, slope_out, out_sems.at[wins + 1]),
-    ]
-    for copy in last:
-        copy.start()
+    last = pltpu.make_async_copy(active_scr, active_out, out_sems.at[wins])
+    last.start()
     result = resid + dot_nt(active, down_w[0])
     head_out[0] = result[0:cut, :].astype(BF16)
     tail_out[0] = result[cut:, :].astype(BF16)
-    for copy in [probs_copy(w) for w in range(wins)] + last:
+    for copy in [probs_copy(w) for w in range(wins)] + [last]:
         copy.wait()
 
 
-def bias_kernel(lat_total, table, spread, bias_out, tab_scr, rows_scr, wide_scr):
+def bias_kernel(
+    lat_total, table, spread, hidden, bias_out, slope_out, tab_scr, rows_scr, wide_scr, slope_scr, sems
+):
+    half = hidden.shape[0] // 2
+    copies = []
+    for rows in (slice(0, half), slice(half, 2 * half)):
+        slope_scr[rows, :] = gelu_parts(hidden[rows, :])[1].astype(BF16)
+        copies.append(
+            pltpu.make_async_copy(slope_scr.at[rows], slope_out.at[rows], sems.at[len(copies)])
+        )
+        copies[-1].start()
     lat = lax.axis_index("lat")
     expand_bias(
         table.at[1], spread, tab_scr, rows_scr, wide_scr, bias_out, lat, True, lat_total
     )
+    for copy in copies:
+        copy.wait()
 
 
 def merge_ahead(scr_own, scr_oth, rows):
@@ -412,9 +424,9 @@
 def second_kernel(
     lat_total,
     tail, lon_head, lat_tail, diag_head, bias, qkv_w, proj_w, up_w, down_w, gains,
-    head_out, tail_out, n1_out, field_out, mixed_out, low_out, n2_out, hg_out, active_out, g_out,
-    sums_out, gain_out,
-    scr_own, scr_oth, qkv_scr, probs_scr, dmix_scr, low_scr, prob_scr,
+    x_out, n1_out, qkv_out, probs_out, mixed_out, low_out, n2_out, hg_out, active_out, g_out,
+    rg_out, dmix_out, gain_out,
+    scr_own, scr_oth, stack_scr,
 ):
     lat = lax.axis_index("lat")
     rows, width = scr_own.shape
@@ -434,9 +446,9 @@
     g_out[...] = g.astype(BF16)
 
     x = rolled(0)
-
+    x_out[...] = x.astype(BF16)
     resid, normed = forward_core(
-        x, 1, (qkv_w, proj_w, gains), qkv_scr, bias, mixed_out, probs_scr, low_scr
+        x, 1, (qkv_w, proj_w, gains), qkv_out, bias, mixed_out, probs_out, stack_scr
     )
     n1_out[...] = normed
     stand2, inv2 = standardize(resid)
@@ -449,38 +461,53 @@
     hg_out[...] = hg
     part, gain_two = norm_back(dot_nt(hg, up_w[1]), gains[1, 1:2, :], stand2, inv2)
     rg = g + part
+    rg_out[...] = rg
     low = rg.astype(BF16)
     low_out[...] = low
-    dmix_scr[...] = dot_nt(low, proj_w[1]).astype(BF16)
+    dmix_out[...] = dot_nt(low, proj_w[1]).astype(BF16)
+    gain_out[...] = gain_two
+
+
+def middle_kernel(
+    x_in, qkv, probs, dmix, rg, gain_two, order, qkv_w, gains,
+    head_out, tail_out, field_out, sums_out, gain_out,
+    low_scr, prob_scr,
+):
+    rows, width = x_in.shape
+    cut = CHUNK * (WLON // 2)
     sums_out[...] = jnp.zeros(sums_out.shape, F32)
-    attend_back(
-        qkv_scr, probs_scr, dmix_scr, field_out, sums_out, low_scr, prob_scr, width
-    )
+    attend_back(qkv, probs, dmix, field_out, sums_out, low_scr, prob_scr, width)
     ng = dot_nt(field_out[...], qkv_w[1]).astype(BF16).astype(F32)
-    stand1, inv1 = standardize(x)
+    stand1, inv1 = standardize(x_in[...].astype(F32))
     part, gain_one = norm_back(ng, gains[1, 0:1, :], stand1, inv1)
-    dx = rg + part
+    dx = rg[...] + part
     head_out[...] = dx[0 : rows - cut, :].astype(BF16)
     tail_out[...] = dx[rows - cut :, :].astype(BF16)
     gain_out[0:1, :] = gain_one
-    gain_out[1:2, :] = gain_two
-
-
-def outer_kernel(
-    n1, field, mixed, low, n2, hg, active, g, sums,
-    keep, give, bias_out,
-    m576, m192, m768, mdown, flat_scr,
+    gain_out[1:2, :] = gain_two[...]
+
+
+def outer_wide(n2, hg, active, g, keep, give, m768, mdown, flat_scr):
+    put(m768, slice(None), dot_tn(n2[...], hg[...]))
+    at = flat_store(flat_scr, 0, m768, hg.shape[1])
+    put(mdown, slice(None), dot_tn(active[...], g[...]))
+    flat_store(flat_scr, at, mdown, g.shape[1])
+    halves(flat_scr, lax.axis_index("lat"), keep, give)
+
+
+def outer_attention(
+    n1, field, mixed, low, sums, keep, give, bias_out, m576, m192, flat_scr
 ):
     put(m576, slice(None), dot_tn(n1[...], field[...]))
     at = flat_store(flat_scr, 0, m576, field.shape[1])
     put(m192, slice(None), dot_tn(mixed[...], low[...]))
-    at += flat_store(flat_scr, at, m192, mixed.shape[1])
-    put(m768, slice(None), dot_tn(n2[...], hg[...]))
-    at += flat_store(flat_scr, at, m768, active.shape[1])
-    put(mdown, slice(None), dot_tn(active[...], g[...]))
-    at += flat_store(flat_scr, at, mdown, mixed.shape[1])
+    flat_store(flat_scr, at, m192, low.shape[1])
     halves(flat_scr, lax.axis_index("lat"), keep, give)
     bias_units(sums, bias_out)
+
+
+def add_halves(keep, got, out):
+    out[...] = (keep[...].astype(F32) + got[...].astype(F32)).astype(BF16)
 
 
 def lat_sum(keep_a, got_a, bias_a, keep_b, got_b, out):
@@ -494,6 +521,16 @@
     one = keep.shape[1]
     out[:, 0:one] = (keep[...].astype(F32) + got[...].astype(F32)).astype(BF16)
     out[:, one:] = bias[...]
+
+
+def sum_both(first, second, order, out):
+    at = 0
+    for pieces in (first, second):
+        total = pieces[0].astype(F32)
+        for k in range(1, pieces.shape[0]):
+            total = total + pieces[k].astype(F32)
+        out[at : at + pieces.shape[1]] = total.astype(BF16)
+        at += pieces.shape[1]
 
 
 def sum_pieces(pieces, order, out):
@@ -518,7 +555,7 @@
 
 def third_kernel(
     head, lon_tail, lat_head, diag_tail, resid_in, slope_in, active_in, mixed,
-    proj_w, up_w, down_w, gains, keep_a,
+    proj_w, up_w, down_w, gains, order, order_too,
     keep_out, give_out, rg_out, dmix_out, gain_out,
     scr_own, scr_oth, m192, m768, mdown, flat_scr, slope, active, sems,
 ):
@@ -536,11 +573,11 @@
     scr_oth[cut:, :] = lat_head[...].astype(F32)
     g = merge_behind(scr_own, scr_oth, rows)
     g_low = g.astype(BF16)
-    for copy in copies:
-        copy.wait()
-    hg = (dot(g_low, down_w[0]) * slope[...].astype(F32)).astype(BF16)
     stand2, inv2 = standardize(resid_in[...].astype(F32))
     normed2 = (stand2 * gains[0, 1:2, :]).astype(BF16)
+    hg = dot(g_low, down_w[0])
+    copies[0].wait()
+    hg = (hg * slope[...].astype(F32)).astype(BF16)
     part, gain_two = norm_back(dot_nt(hg, up_w[0]), gains[0, 1:2, :], stand2, inv2)
     rg = g + part
     rg_out[...] = rg
@@ -551,6 +588,7 @@
     at = flat_store(flat_scr, 0, m192, mixed.shape[1])
     put(m768, slice(None), dot_tn(normed2, hg))
     at += flat_store(flat_scr, at, m768, active.shape[1])
+    copies[1].wait()
     put(mdown, slice(None), dot_tn(active[...], g_low))
     at += flat_store(flat_scr, at, mdown, mixed.shape[1])
     flat_scr[at:, :] = jnp.zeros((flat_scr.shape[0] - at, 128), F32)
@@ -604,7 +642,7 @@
 
 
 def last_kernel(
-    units_a, units_c, extra, spread, same, same_x, cross, cross_x, own_c, oth_c,
+    units_a, units_b, units_c, extra, spread, same, same_x, cross, cross_x, own_c, oth_c,
     update_out, bias_out, scr, rows_scr, wide_scr, tab_scr, ab, c,
 ):
     lat = lax.axis_index("lat")
@@ -632,13 +670,10 @@
                 k += 1
         return total
 
-    total = place(
-        ab, 0, units_a, [(864, 864), (2016, 288), (3456, 1152), (5760, 1152)]
-    )
-    total = total + place(
-        ab, units_a + extra, ab.shape[2],
-        [(1728, 288), (2304, 1152), (4608, 1152)],
-    )
+    at = units_a + extra
+    total = place(ab, 0, units_a, [(864, 864), (2016, 288)])
+    total = total + place(ab, at, at + units_b, [(1728, 288), (2304, 1152), (4608, 1152)])
+    total = total + place(ab, at + units_b, ab.shape[2], [(3456, 1152), (5760, 1152)])
     total = total + place(c, 0, units_c, [(0, 864), (6912, 8)])
     count = update_out.shape[0]
     mean = jnp.sum(total) * (1.0 / (count * 128))
@@ -749,8 +784,11 @@
 
     block_rows = (qkv_weight[0].size + proj_weight[0].size + 2 * up_weight[0].size) // 128
     qkv_rows = qkv_weight[0].size // 128
-    counts = (block_rows, block_rows - qkv_rows, qkv_rows + 8)
-    units_a, units_b, units_c = [-(-count // (2 * lon_size * UNIT)) for count in counts]
+    wide_rows = 2 * up_weight[0].size // 128
+    counts = (wide_rows, block_rows - wide_rows, block_rows - qkv_rows, qkv_rows + 8)
+    units_wide, units_a, units_b, units_c = [
+        -(-count // (2 * lon_size * UNIT)) for count in counts
+    ]
     extra = -(-BIAS_UNITS // lon_size)
 
     def units(*lead):
@@ -759,7 +797,7 @@
     def flat_scr(per):
         return ((2 * lon_size * per * UNIT, 128), F32)
 
-    x0, tail, head, qkv0, mixed0, probs0, resid0, slope0, active0 = call(
+    x0, tail, head, qkv0, mixed0, probs0, resid0, hidden0, active0 = call(
         functools.partial(first_kernel, lat_total),
         [
             (token, BF16),
@@ -769,7 +807,7 @@
             (token, BF16),
             probs_shape,
             (token, BF16),
-            ((rows, hid), BF16),
+            ((rows, hid), F32),
             ((rows, hid), BF16),
         ],
         [
@@ -791,9 +829,8 @@
             stack_shape,
             probs_shape,
             ((rows, hid), BF16),
-            ((rows, hid), BF16),
             pltpu.SemaphoreType.DMA((9,)),
-            pltpu.SemaphoreType.DMA((wins + 2,)),
+            pltpu.SemaphoreType.DMA((wins + 1,)),
         ],
         [
             pltpu.with_memory_space_constraint(arg, pltpu.HBM)
@@ -805,67 +842,85 @@
         8,
         28,
         [pltpu.HBM] * 9,
-        [pltpu.VMEM] * 5 + [pltpu.HBM, pltpu.VMEM, pltpu.HBM, pltpu.HBM],
+        [pltpu.VMEM] * 5 + [pltpu.HBM, pltpu.VMEM, pltpu.VMEM, pltpu.HBM],
     )
     lon_head = lon_send(head, -1)
     diag_head = diag_send(head, -1)
     lat_tail = lat_swap(tail)
-    (bias1,) = call(
+    bias1, slope0 = call(
         functools.partial(bias_kernel, lat_total),
-        [bias_shape],
-        [tab_scr, rows_scr, wide_scr],
-        (table, spread),
-        2,
+        [bias_shape, ((rows, hid), BF16)],
+        [tab_scr, rows_scr, wide_scr, ((rows, hid), BF16), pltpu.SemaphoreType.DMA((2,))],
+        (table, spread, hidden0),
+        3,
         10,
-    )
-
-    (
-        dhead, dtail, n1, field1, mixed1, low1, n2, hg1, active1, g1, sums1, gains1,
-    ) = call(
+        None,
+        [pltpu.VMEM, pltpu.HBM],
+    )
+
+    x1, n1, qkv1, probs1, mixed1, low1, n2, hg1, active1, g1, rg1, dmix1, gain_late = call(
         functools.partial(second_kernel, lat_total),
         [
-            ((rows - cut, width), BF16),
-            ((cut, width), BF16),
+            (token, BF16),
             (token, BF16),
             field_shape,
+            probs_shape,
             (token, BF16),
             (token, BF16),
             (token, BF16),
             ((rows, hid), BF16),
             ((rows, hid), BF16),
             (token, BF16),
-            sums_shape,
-            ((2, width), F32),
-        ],
-        [
             (token, F32),
-            (token, F32),
-            field_shape,
-            probs_shape,
             (token, BF16),
-            stack_shape,
-            stack_shape,
-        ],
+            ((1, width), F32),
+        ],
+        [(token, F32), (token, F32), stack_shape],
         (
             tail, lon_head, lat_tail, diag_head, bias1, qkv_weight, proj_weight, up_weight,
             down_turned, norm_gain,
         ),
-        19,
-        28,
+        7,
+        24,
+    )
+    keep_w, give_w = call(
+        outer_wide,
+        [units(lon_size, units_wide), units(lon_size, units_wide)],
+        [m768, mdown, flat_scr(units_wide)],
+        (n2, hg1, active1, g1),
+        1,
+        16,
+    )
+    got_w = lat_swap(give_w)
+    dhead, dtail, field1, sums1, gains1 = call(
+        middle_kernel,
+        [
+            ((rows - cut, width), BF16),
+            ((cut, width), BF16),
+            field_shape,
+            sums_shape,
+            ((2, width), F32),
+        ],
+        [stack_shape, stack_shape],
+        (x1, qkv1, probs1, dmix1, rg1, gain_late, keep_w, qkv_weight, norm_gain),
+        5,
+        20,
     )
     lon_tail = lon_send(dtail, 1)
     diag_tail = diag_send(dtail, 1)
     lat_dhead = lat_swap(dhead)
 
     keep_a, give_a, bias_a = call(
-        outer_kernel,
+        outer_attention,
         [units(lon_size, units_a), units(lon_size, units_a), units(lon_size, extra)],
-        [m576, m192, m768, mdown, flat_scr(units_a)],
-        (n1, field1, mixed1, low1, n2, hg1, active1, g1, sums1),
-        3,
-        20,
+        [m576, m192, flat_scr(units_a)],
+        (n1, field1, mixed1, low1, sums1),
+        1,
+        16,
     )
     got_a = lat_swap(give_a)
+    (part_w,) = call(add_halves, [units(lon_size, units_wide)], [], (keep_w, got_w), 1, 10)
+    pieces_w = lax.all_to_all(part_w, "lon", 0, 0)
 
     keep_b, give_b, rg0, dmix0, gain_two = call(
         third_kernel,
@@ -891,11 +946,11 @@
             dhead, lon_tail, lat_dhead, diag_tail, resid0,
             pltpu.with_memory_space_constraint(slope0, pltpu.HBM),
             pltpu.with_memory_space_constraint(active0, pltpu.HBM),
-            mixed0, proj_weight, up_weight, down_turned, norm_gain, keep_a,
+            mixed0, proj_weight, up_weight, down_turned, norm_gain, keep_a, part_w,
         ),
         2,
         20,
-        [pltpu.VMEM] * 5 + [pltpu.HBM] * 2 + [pltpu.VMEM] * 6,
+        [pltpu.VMEM] * 5 + [pltpu.HBM] * 2 + [pltpu.VMEM] * 7,
     )
     got_b = lat_swap(give_b)
     (part_ab,) = call(
@@ -941,15 +996,16 @@
     )
     pieces_c = lax.all_to_all(part_c, "lon", 0, 0)
 
+    units_ab = units_a + extra + units_b + units_wide
     (sum_ab,) = call(
-        sum_pieces, [units(units_a + extra + units_b)], [], (pieces_ab, part_c), 1, 10
+        sum_both, [units(units_ab)], [], (pieces_ab, pieces_w, part_c), 1, 10
     )
     (sum_c,) = call(
         sum_pieces, [units(lon_size, units_c + extra)], [], (pieces_c, sum_ab), 1, 10
     )
     (same_ab,) = call(
         join_z,
-        [units(zs, units_a + extra + units_b)],
+        [units(zs, units_ab)],
         [],
         [sum_ab] + [lon_send(sum_ab, 2 * k) for k in range(1, zs)] + [sum_c],
         1,
@@ -963,14 +1019,14 @@
 
     flat_rows = (2 * block_rows * 128 + norm_gain.size) // 128
     update, bias_grad = call(
-        functools.partial(last_kernel, units_a, units_c, extra),
+        functools.partial(last_kernel, units_a, units_b, units_c, extra),
         [((flat_rows, 128), BF16), (table.shape, F32)],
         [
             ((flat_rows + 2, 128), F32),
             ((CHUNK * 8, PAIR), F32),
             wide_scr,
             tab_scr,
-            units(2, lon_size, units_a + extra + units_b),
+            units(2, lon_size, units_ab),
             units(2, lon_size, units_c + extra),
         ],
         (spread, same_ab, same_x, cross, cross_x, whole_c, oth_c),

time: 112 us -> 116 us (1.036)
  waiting for transfers between devices: 40.8 us -> 25.6 us
  starting transfers between devices: 25.2 us -> 35.5 us
  local copies, waits for them, and re-layouts: 1.15 us -> 6.53 us
  Pallas kernels: 42.9 us -> 46.3 us
    all_to_all x1, waiting for transfers between devices: 10.3 us -> 1.94 us  [shards(): pieces_ab = lax.all_to_all(part_ab, 'lon', 0, 0)]
    all_to_all x0 -> x1, starting transfers between devices: none -> 6.71 us  [shards(): pieces_w = lax.all_to_all(part_w, 'lon', 0, 0)]
    unnamed x18 -> x38, local copies, waits for them, and re-layouts: 1.15 us -> 6.53 us
    ppermute x2, waiting for transfers between devices: 4.77 us -> 0.01 us  [diag_send(): return lax.ppermute(value, ('lon', 'lat'), pairs)]
    pallas_call x12 -> x15, Pallas kernels: 42.9 us -> 46.3 us  [call(): pl.pallas_call(kernel, out_shape=[pltpu.HBM(*entry) if space == pltpu.HBM...]
    all_to_all x1, starting transfers between devices: 3.55 us -> 5.99 us  [shards(): pieces_ab = lax.all_to_all(part_ab, 'lon', 0, 0)]
    ppermute x5, waiting for transfers between devices: 10.1 us -> 8.13 us  [lon_send(): lax.ppermute(value, 'lon', [(s, (s + step) % count) for s in range(count)])]
    ppermute x8 -> x9, waiting for transfers between devices: 4.38 us -> 4.23 us  [lat_swap(): return lax.ppermute(value, 'lat', [(0, 1), (1, 0)])]
  transfers between devices with their start and end apart: 19 -> 21, of which waited for: 12 -> 9; matrix products, arithmetic and copies ran while one was open for 0% -> 0% of each run, Pallas kernels for 16% -> 23%
where the time goes in v6:
time: 116 us; the launch traced here: 115 us
  Pallas kernels  46.3 us (40%)
  starting transfers between devices  35.5 us (31%)
  waiting for transfers between devices  25.6 us (22%)
  local copies, waits for them, and re-layouts  6.53 us (6%)
    pallas_call x15, Pallas kernels, call(): pl.pallas_call(kernel, out_shape=[pltpu.HBM(*entry) if space == pltpu.HBM...  46.3 us
    ppermute x5, waiting for transfers between devices, lon_send(): lax.ppermute(value, 'lon', [(s, (s + step) % count) for s in range(count)])  8.13 us
    ppermute x1, waiting for transfers between devices, x_swap(): return lax.ppermute(value, 'lon', [(s, s ^ 1) for s in range(count)])  8 us
    all_to_all x1, starting transfers between devices, shards(): pieces_w = lax.all_to_all(part_w, 'lon', 0, 0)  6.71 us
    unnamed x38, local copies, waits for them, and re-layouts  6.53 us
    ppermute x2, starting transfers between devices, diag_send(): return lax.ppermute(value, ('lon', 'lat'), pairs)  6.47 us
    all_to_all x1, starting transfers between devices, shards(): pieces_ab = lax.all_to_all(part_ab, 'lon', 0, 0)  5.99 us
    ppermute x5, starting transfers between devices, lon_send(): lax.ppermute(value, 'lon', [(s, (s + step) % count) for s in range(count)])  5.69 us
  transfers between devices with their start and end apart: 21, of which 9 were waited for; matrix products, arithmetic and copies ran while one was open for 0% of the time, Pallas kernels for 23%

profile of v6, /device:TPU:0, one launch (start us, length us, event | category | flops | bytes accessed | tf_op | source)
XLA Modules:
  0.0 114.9 jit_solution(18166764744991764799)
XLA Ops:
  0.7 8.8 %shard_map.112 = (bf16[576,192]{1,0:T(8,128)(2,1)S(1)}, bf16[2,504,192]{2,1,0:T(8,128)(2,1)S(1)}, bf16[2,72,192]{2,1,0:T(8,128)(2,1)S(1)}, bf16[576,576]{1,0:T(8...) custom-call(bf16[2,12,24,192]{3,2,1,0:T(8,128)(2,1)} %tokens_in.1, ...), custom_call_target="tpu_custom_call" | custom-call | flops 8800000000 | bytes 100000 | tf_op jit(solution)/shard_map/pallas_call | solution.py:713
  9.5 0.5 collective-permute-start.1
  10.0 5.6 %collective-permute-start.2 = (bf16[2,72,192]{2,1,0:T(8,128)(2,1)S(1)}, bf16[2,72,192]{2,1,0:T(8,128)(2,1)S(1)}, u32[]{:S(2)}, u32[]{:S(2)}) collective-permute-start(bf16[2,72,192]{2,1,0:T(8,128)(2,1)S(1)} %get-tuple-element.52), channel_id=1, source_target_pairs={{0,15},{1,14},{2,1},{3,0},{4,3},{5,2},{6,5},{7,4},{8,7},{9,6},{10,... | collective-permute-start | bytes 165896 | tf_op jit(solution)/shard_map/ppermute | solution.py:751
  15.6 0.5 collective-permute-start
  16.2 2.9 %shard_map.113 = (f32[864,144]{1,0:T(8,128)S(1)}, bf16[576,768]{1,0:T(8,128)(2,1)}) custom-call(f32[2,6,1,6336]{3,2,1,0:T(1,128)S(1)} %bitcast.8, bf16[2,132,384]{2,1,0:T(8,128)(2,1)S(1)} %copy-done.6, f32[576,768]{1,0:T(8,128)S(1)} %get-tuple-element.53.hidden), custom_call_target="tpu_custom_call" | custom-call | flops 3300000000 | bytes 100000 | tf_op jit(solution)/shard_map/pallas_call | solution.py:713
  19.1 0.8 collective-permute-done.lon_head
  20.0 6.9 %shard_map.114 = (bf16[576,192]{1,0:T(8,128)(2,1)S(1)}, bf16[576,192]{1,0:T(8,128)(2,1)S(1)}, bf16[576,576]{1,0:T(8,128)(2,1)S(1)}, f32[4,6,144,144]{3,2,1,0:T(8...) custom-call(bf16[2,504,192]{2,1,0:T(8,128)(2,1)S(1)} %get-tuple-elem, ...), custom_call_target="tpu_custom_call" | custom-call | flops 7699999744 | bytes 100000 | tf_op jit(solution)/shard_map/pallas_call | solution.py:713
  26.9 1.0 shard_map.115
  27.9 0.1 collective-permute-start.6
  28.0 4.9 %shard_map.116 = (bf16[504,192]{1,0:T(8,128)(2,1)S(1)}, bf16[72,192]{1,0:T(8,128)(2,1)S(1)}, bf16[576,576]{1,0:T(8,128)(2,1)S(1)}, f32[864,384]{1,0:T(8,128)S(1)}, f32[2,192]{1,0:T(2,128)S(1)}) custom-call(bf16[576,192]{1,0:T(8,128)(2,1)S(1)} %get-tuple-element.55.x_in, bf16[576,576]{1,0:T(8,128)(2,1)S(1)} %get-tuple-element.56.qkv, ...), custom_call_target="tpu_custom_call" | custom-call | flops 5500000256 | bytes 100000 | tf_op jit(solution)/shard_map/pallas_call | solution.py:713
  32.9 0.8 collective-permute-start.5
  33.7 0.1 collective-permute-start.3
  33.9 0.2 collective-permute-start.4
  34.1 1.0 shard_map.117
  35.1 0.8 shard_map.118.order_too
  35.9 6.7 %all-to-all-start.1 = ((bf16[8,18,8,128]{3,2,1,0:T(8,128)(2,1)}), bf16[8,18,8,128]{3,2,1,0:T(8,128)(2,1)S(1)}, u32[]{:S(2)}, u32[]{:S(2)}) async-start(bf16[8,18,8,128]{3,2,1,0:T(8,128)(2,1)} %shard_map.118.order_too), calls=%async_computation.1 | async-start | bytes 589824 | tf_op jit(solution)/shard_map/all_to_all | solution.py:923
  42.6 1.0 copy-done.10
  43.6 1.0 copy-done.12
  44.5 4.4 %shard_map.119 = (bf16[8,21,8,128]{3,2,1,0:T(8,128)(2,1)S(1)}, bf16[8,21,8,128]{3,2,1,0:T(8,128)(2,1)S(1)}, f32[576,192]{1,0:T(8,128)S(1)}, bf16[576,192]{1,0:T(8,128)(2,1)S(1)}, f32[1,192]{1,0:T(1,128)S(1)}) custom-call(bf16[504,192]{1,0:T(8,128)(2,1)S(1)} %get-tuple-element.66.head, bf16[72,192]{1,0:T(8,128)(2,1)S(1)} %collective-permute-done.3.lon_tail, ...), custom_call_target="tpu_custom_call" | custom-call | flops 2200000000 | bytes 100000 | tf_op jit(solution)/shard_map/pallas_call | solution.py:713
  48.9 0.8 copy-done.7
  49.7 0.7 copy-done.13
  50.4 0.2 collective-permute-start.8
  50.7 0.3 collective-permute-start.7
  51.0 1.4 %collective-permute-done.7.got_a = bf16[8,9,8,128]{3,2,1,0:T(8,128)(2,1)S(1)} collective-permute-done((bf16[8,9,8,128]{3,2,1,0:T(8,128)(2,1)S(1)}, bf16[8,9,8,128]{3,2,1,0:T(8,128)(2,1)S(1)}, u32[]{:S(2)}, u32[]{:S(2)}) %collective-permute-start.7) | collective-permute-done | bytes 147488 | tf_op jit(solution)/shard_map/ppermute | solution.py:732
  52.3 0.9 shard_map.120.order
  53.2 6.0 %all-to-all-start = ((bf16[8,35,8,128]{3,2,1,0:T(8,128)(2,1)}), bf16[8,35,8,128]{3,2,1,0:T(8,128)(2,1)S(1)}, u32[]{:S(2)}, u32[]{:S(2)}) async-start(bf16[8,35,8,128]{3,2,1,0:T(8,128)(2,1)} %shard_map.120.order), calls=%async_computation | async-start | bytes 1146880 | tf_op jit(solution)/shard_map/all_to_all | solution.py:964
  59.3 1.0 copy-done.14
  60.2 1.1 copy-done.16
  61.3 1.0 copy-done.18
  62.3 8.7 %shard_map.121 = (bf16[2,12,24,192]{3,2,1,0:T(8,128)(2,1)}, bf16[8,7,8,128]{3,2,1,0:T(8,128)(2,1)S(1)}, bf16[8,7,8,128]{3,2,1,0:T(8,128)(2,1)S(1)}, bf16[8,5,8,128]{3,2,1,0:T(8,128)(2,1)S(1)}) custom-call(bf16[576,192]{1,0:T(8,128)(2,1)S(1)} %copy-done.18, bf16[576,576]{1,0:T(8,128)(2,1)S(1)} %copy-done.16, f32[4,6,144,144]{3,2,1,0:T(8,128)} %get-tuple-element.50.probs_in, ...), custom_call_target="tpu_custom_call" | custom-call | flops 12099999744 | bytes 100000 | tf_op jit(solution)/shard_map/pallas_call | solution.py:713
  71.1 1.3 %collective-permute-done.9.got = bf16[8,7,8,128]{3,2,1,0:T(8,128)(2,1)S(1)} collective-permute-done((bf16[8,7,8,128]{3,2,1,0:T(8,128)(2,1)S(1)}, bf16[8,7,8,128]{3,2,1,0:T(8,128)(2,1)S(1)}, u32[]{:S(2)}, u32[]{:S(2)}) %collective-permute-start.9) | collective-permute-done | bytes 114720 | tf_op jit(solution)/shard_map/ppermute | solution.py:732
  72.4 0.7 shard_map.122.order
  73.1 1.9 %all-to-all-done.first = bf16[8,35,8,128]{3,2,1,0:T(8,128)(2,1)S(1)} async-done(((bf16[8,35,8,128]{3,2,1,0:T(8,128)(2,1)}), bf16[8,35,8,128]{3,2,1,0:T(8,128)(2,1)S(1)}, u32[]{:S(2)}, u32[]{:S(2)}) %all-to-all-start) | async-done | bytes 573472 | tf_op jit(solution)/shard_map/all_to_all | solution.py:964
  75.1 4.1 %all-to-all-start.2 = ((bf16[8,12,8,128]{3,2,1,0:T(8,128)(2,1)}), bf16[8,12,8,128]{3,2,1,0:T(8,128)(2,1)S(1)}, u32[]{:S(2)}, u32[]{:S(2)}) async-start(bf16[8,12,8,128]{3,2,1,0:T(8,128)(2,1)} %shard_map.122.order), calls=%async_computation.2 | async-start | bytes 393216 | tf_op jit(solution)/shard_map/all_to_all | solution.py:997
  79.1 1.1 shard_map.123.order.refs_0_
  80.2 3.9 %collective-permute-start.12 = (bf16[53,8,128]{2,1,0:T(8,128)(2,1)S(1)}, bf16[53,8,128]{2,1,0:T(8,128)(2,1)S(1)}, u32[]{:S(2)}, u32[]{:S(2)}) collective-permute-start(bf16[53,8,128]{2,1,0:T(8,128)(2,1)S(1)} %shard_map.123.order.refs_0_), channel_id=1, source_target_pairs={{0,12},{2,14},{4,0},{6,2},{8,4},{10,6},{12,8},{14,10},{1,13},{3,15... | collective-permute-start | bytes 325640 | tf_op jit(solution)/shard_map/ppermute | solution.py:737
  84.1 1.1 collective-permute-start.10
  85.2 3.1 %all-to-all-done.2.pieces = bf16[8,12,8,128]{3,2,1,0:T(8,128)(2,1)S(1)} async-done(((bf16[8,12,8,128]{3,2,1,0:T(8,128)(2,1)}), bf16[8,12,8,128]{3,2,1,0:T(8,128)(2,1)S(1)}, u32[]{:S(2)}, u32[]{:S(2)}) %all-to-all-start.2) | async-done | bytes 196640 | tf_op jit(solution)/shard_map/all_to_all | solution.py:997
  88.3 0.7 shard_map.124.refs_4_
  89.0 7.3 %collective-permute-done.11.refs_2_ = bf16[53,8,128]{2,1,0:T(8,128)(2,1)S(1)} collective-permute-done((bf16[53,8,128]{2,1,0:T(8,128)(2,1)S(1)}, bf16[53,8,128]{2,1,0:T(8,128)(2,1)S(1)}, u32[]{:S(2)}, u32[]{:S(2)}) %collective-permute-start.11) | collective-permute-done | bytes 108576 | tf_op jit(solution)/shard_map/ppermute | solution.py:737
  96.3 1.0 shard_map.125.same
  97.2 1.5 %collective-permute-start.13 = (bf16[4,53,8,128]{3,2,1,0:T(8,128)(2,1)S(1)}, bf16[4,53,8,128]{3,2,1,0:T(8,128)(2,1)S(1)}, u32[]{:S(2)}, u32[]{:S(2)}) collective-permute-start(bf16[4,53,8,128]{3,2,1,0:T(8,128)(2,1)S(1)} %shard_map.125.same), channel_id=1, source_target_pairs={{0,2},{2,0},{4,6},{6,4},{8,10},{10,8},{12,14},{14,12},{1,3},{3,1},... | collective-permute-start | bytes 1302536 | tf_op jit(solution)/shard_map/ppermute | solution.py:742
  98.7 3.4 %all-to-all-start.3 = ((bf16[8,12,8,128]{3,2,1,0:T(8,128)(2,1)}), bf16[8,12,8,128]{3,2,1,0:T(8,128)(2,1)S(1)}, u32[]{:S(2)}, u32[]{:S(2)}) async-start(bf16[8,12,8,128]{3,2,1,0:T(8,128)(2,1)} %shard_map.124.refs_4_), calls=%async_computation.3 | async-start | bytes 393216 | tf_op jit(solution)/shard_map/all_to_all | solution.py:1014
  102.2 8.0 %collective-permute-done.13.same_x = bf16[4,53,8,128]{3,2,1,0:T(8,128)(2,1)S(1)} collective-permute-done((bf16[4,53,8,128]{3,2,1,0:T(8,128)(2,1)S(1)}, bf16[4,53,8,128]{3,2,1,0:T(8,128)(2,1)S(1)}, u32[]{:S(2)}, u32[]{:S(2)}) %collective-permute-start.13) | collective-permute-done | bytes 434208 | tf_op jit(solution)/shard_map/ppermute | solution.py:742
  110.2 0.3 all-to-all-done.3.own_c
  110.5 0.3 collective-permute-start.16
  110.7 1.5 %collective-permute-done.16.oth_c = bf16[8,12,8,128]{3,2,1,0:T(8,128)(2,1)S(1)} collective-permute-done((bf16[8,12,8,128]{3,2,1,0:T(8,128)(2,1)S(1)}, bf16[8,12,8,128]{3,2,1,0:T(8,128)(2,1)S(1)}, u32[]{:S(2)}, u32[]{:S(2)}) %collective-permute-start.16) | collective-permute-done | bytes 196640 | tf_op jit(solution)/shard_map/ppermute | solution.py:732
  112.3 2.6 %shard_map.126 = (bf16[6918,128]{1,0:T(8,128)(2,1)}, f32[2,6,1,6336]{3,2,1,0:T(1,128)}) custom-call(bf16[2,132,384]{2,1,0:T(8,128)(2,1)S(1)} %copy-done.6, bf16[4,53,8,128]{3,2,1,0:T(8,128)(2,1)S(1)} %shard_map.125.same, bf16[4,53,8,128]{3,2,1,0:T(8,128)(2,1)S(1)} %collective-permute-done.13.same_x, ...), custom_call_target="tpu_custom_call" | custom-call | flops 3300000000 | bytes 100000 | tf_op jit(solution)/shard_map/pallas_call | solution.py:713
  (47 shorter events, 0.3 us)
Async XLA Ops:
  0.6 15.5 %copy-start.3 = (f32[2,1,6,6336]{3,1,2,0:T(1,128)S(1)}, f32[2,1,6,6336]{3,1,2,0:T(1,128)}, u32[]{:S(2)}) copy-start(f32[2,1,6,6336]{3,1,2,0:T(1,128)} %param.16) | copy-start | bytes 912388
  0.6 15.5 %copy-start.6 = (bf16[2,132,384]{2,1,0:T(8,128)(2,1)S(1)}, bf16[2,132,384]{2,1,0:T(8,128)(2,1)}, u32[]{:S(2)}) copy-start(bf16[2,132,384]{2,1,0:T(8,128)(2,1)} %constant.2.clone.spread_in.spread) | copy-start | bytes 608260
  9.4 9.7 %copy-start.9 = (bf16[576,192]{1,0:T(8,128)(2,1)}, bf16[576,192]{1,0:T(8,128)(2,1)S(1)}, u32[]{:S(2)}) copy-start(bf16[576,192]{1,0:T(8,128)(2,1)S(1)} %get-tuple-element.71.mixed) | copy-start | bytes 663556
  9.4 9.7 %copy-start.11 = (bf16[576,192]{1,0:T(8,128)(2,1)}, bf16[576,192]{1,0:T(8,128)(2,1)S(1)}, u32[]{:S(2)}) copy-start(bf16[576,192]{1,0:T(8,128)(2,1)S(1)} %get-tuple-element.68.resid_in) | copy-start | bytes 663556
  9.4 9.7 %copy-start.15 = (bf16[576,576]{1,0:T(8,128)(2,1)}, bf16[576,576]{1,0:T(8,128)(2,1)S(1)}, u32[]{:S(2)}) copy-start(bf16[576,576]{1,0:T(8,128)(2,1)S(1)} %get-tuple-element.49.qkv) | copy-start | bytes 1990660
  9.5 9.7 %copy-start.17 = (bf16[576,192]{1,0:T(8,128)(2,1)}, bf16[576,192]{1,0:T(8,128)(2,1)S(1)}, u32[]{:S(2)}) copy-start(bf16[576,192]{1,0:T(8,128)(2,1)S(1)} %get-tuple-element.48.x_in) | copy-start | bytes 663556
  9.5 10.5 %collective-permute-start.1 = (bf16[2,504,192]{2,1,0:T(8,128)(2,1)S(1)}, bf16[2,504,192]{2,1,0:T(8,128)(2,1)S(1)}, u32[]{:S(2)}, u32[]{:S(2)}) collective-permute-start(bf16[2,504,192]{2,1,0:T(8,128)(2,1)S(1)} %get-tuple-element.51.tail), channel_id=1, source_target_pairs={{0,1},{1,0},{2,3},{3,2},{4,5},{5,4},{6,7},{7,6},{8,9},{9,8},{10,11... | collective-permute-start | bytes 1161224 | tf_op jit(solution)/shard_map/ppermute | solution.py:732
  10.0 9.1 %collective-permute-start.2 = (bf16[2,72,192]{2,1,0:T(8,128)(2,1)S(1)}, bf16[2,72,192]{2,1,0:T(8,128)(2,1)S(1)}, u32[]{:S(2)}, u32[]{:S(2)}) collective-permute-start(bf16[2,72,192]{2,1,0:T(8,128)(2,1)S(1)} %get-tuple-element.52), channel_id=1, source_target_pairs={{0,15},{1,14},{2,1},{3,0},{4,3},{5,2},{6,5},{7,4},{8,7},{9,6},{10,... | collective-permute-start | bytes 165896 | tf_op jit(solution)/shard_map/ppermute | solution.py:751
  15.6 4.4 %collective-permute-start = (bf16[2,72,192]{2,1,0:T(8,128)(2,1)S(1)}, bf16[2,72,192]{2,1,0:T(8,128)(2,1)S(1)}, u32[]{:S(2)}, u32[]{:S(2)}) collective-permute-start(bf16[2,72,192]{2,1,0:T(8,128)(2,1)S(1)} %get-tuple-element.52), channel_id=1, source_target_pairs={{0,14},{2,0},{4,2},{6,4},{8,6},{10,8},{12,10},{14,12},{1,15},{3,1}... | collective-permute-start | bytes 165896 | tf_op jit(solution)/shard_map/ppermute | solution.py:737
  16.2 3.8 %copy-start = (bf16[2,192,768]{2,1,0:T(8,128)(2,1)S(1)}, bf16[2,192,768]{2,1,0:T(8,128)(2,1)}, u32[]{:S(2)}) copy-start(bf16[2,192,768]{2,1,0:T(8,128)(2,1)} %up_w.3) | copy-start | bytes 1769476
  16.2 3.8 %copy-start.1 = (bf16[2,768,192]{1,2,0:T(8,128)(2,1)S(1)}, bf16[2,768,192]{1,2,0:T(8,128)(2,1)}, u32[]{:S(2)}) copy-start(bf16[2,768,192]{1,2,0:T(8,128)(2,1)} %param.14) | copy-start | bytes 1769476
  16.2 3.8 %copy-start.2 = (bf16[2,192,576]{2,1,0:T(8,128)(2,1)S(1)}, bf16[2,192,576]{2,1,0:T(8,128)(2,1)}, u32[]{:S(2)}) copy-start(bf16[2,192,576]{2,1,0:T(8,128)(2,1)} %qkv_w.5) | copy-start | bytes 1327108
  16.2 3.8 %copy-start.4 = (bf16[2,192,192]{2,1,0:T(8,128)(2,1)S(1)}, bf16[2,192,192]{2,1,0:T(8,128)(2,1)}, u32[]{:S(2)}) copy-start(bf16[2,192,192]{2,1,0:T(8,128)(2,1)} %proj_w.3) | copy-start | bytes 442372
  16.2 3.8 %copy-start.5 = (f32[2,2,192]{2,1,0:T(2,128)S(1)}, f32[2,2,192]{2,1,0:T(2,128)}, u32[]{:S(2)}) copy-start(f32[2,2,192]{2,1,0:T(2,128)} %gains.7) | copy-start | bytes 9220
  27.9 7.1 %collective-permute-start.6 = (bf16[8,18,8,128]{3,2,1,0:T(8,128)(2,1)S(1)}, bf16[8,18,8,128]{3,2,1,0:T(8,128)(2,1)S(1)}, u32[]{:S(2)}, u32[]{:S(2)}) collective-permute-start(bf16[8,18,8,128]{3,2,1,0:T(8,128)(2,1)S(1)} %get-tuple-element.78), channel_id=1, source_target_pairs={{0,1},{1,0},{2,3},{3,2},{4,5},{5,4},{6,7},{7,6},{8,9},{9,8},{10,11... | collective-permute-start | bytes 884744 | tf_op jit(solution)/shard_map/ppermute | solution.py:732
  32.9 9.7 %collective-permute-start.5 = (bf16[72,192]{1,0:T(8,128)(2,1)S(1)}, bf16[72,192]{1,0:T(8,128)(2,1)S(1)}, u32[]{:S(2)}, u32[]{:S(2)}) collective-permute-start(bf16[72,192]{1,0:T(8,128)(2,1)S(1)} %get-tuple-element.67), channel_id=1, source_target_pairs={{0,3},{1,2},{2,5},{3,4},{4,7},{5,6},{6,9},{7,8},{8,11},{9,10},{10,... | collective-permute-start | bytes 82952 | tf_op jit(solution)/shard_map/ppermute | solution.py:751
  33.7 8.9 %collective-permute-start.3 = (bf16[72,192]{1,0:T(8,128)(2,1)S(1)}, bf16[72,192]{1,0:T(8,128)(2,1)S(1)}, u32[]{:S(2)}, u32[]{:S(2)}) collective-permute-start(bf16[72,192]{1,0:T(8,128)(2,1)S(1)} %get-tuple-element.67), channel_id=1, source_target_pairs={{0,2},{2,4},{4,6},{6,8},{8,10},{10,12},{12,14},{14,0},{1,3},{3,5},... | collective-permute-start | bytes 82952 | tf_op jit(solution)/shard_map/ppermute | solution.py:737
  33.9 8.7 %collective-permute-start.4 = (bf16[504,192]{1,0:T(8,128)(2,1)S(1)}, bf16[504,192]{1,0:T(8,128)(2,1)S(1)}, u32[]{:S(2)}, u32[]{:S(2)}) collective-permute-start(bf16[504,192]{1,0:T(8,128)(2,1)S(1)} %get-tuple-element.66.head), channel_id=1, source_target_pairs={{0,1},{1,0},{2,3},{3,2},{4,5},{5,4},{6,7},{7,6},{8,9},{9,8},{10,11... | collective-permute-start | bytes 580616 | tf_op jit(solution)/shard_map/ppermute | solution.py:732
  35.9 17.4 %all-to-all-start.1 = ((bf16[8,18,8,128]{3,2,1,0:T(8,128)(2,1)}), bf16[8,18,8,128]{3,2,1,0:T(8,128)(2,1)S(1)}, u32[]{:S(2)}, u32[]{:S(2)}) async-start(bf16[8,18,8,128]{3,2,1,0:T(8,128)(2,1)} %shard_map.118.order_too), calls=%async_computation.1 | async-start | bytes 589824 | tf_op jit(solution)/shard_map/all_to_all | solution.py:923
  42.6 1.0 copy-start.10
  43.6 1.0 copy-start.12
  48.9 0.8 copy-start.7
  49.7 0.7 copy-start.13
  50.4 1.9 %collective-permute-start.8 = (bf16[8,21,8,128]{3,2,1,0:T(8,128)(2,1)S(1)}, bf16[8,21,8,128]{3,2,1,0:T(8,128)(2,1)S(1)}, u32[]{:S(2)}, u32[]{:S(2)}) collective-permute-start(bf16[8,21,8,128]{3,2,1,0:T(8,128)(2,1)S(1)} %get-tuple-element.86), channel_id=1, source_target_pairs={{0,1},{1,0},{2,3},{3,2},{4,5},{5,4},{6,7},{7,6},{8,9},{9,8},{10,11... | collective-permute-start | bytes 1032200 | tf_op jit(solution)/shard_map/ppermute | solution.py:732
  50.7 1.6 %collective-permute-start.7 = (bf16[8,9,8,128]{3,2,1,0:T(8,128)(2,1)S(1)}, bf16[8,9,8,128]{3,2,1,0:T(8,128)(2,1)S(1)}, u32[]{:S(2)}, u32[]{:S(2)}) collective-permute-start(bf16[8,9,8,128]{3,2,1,0:T(8,128)(2,1)S(1)} %get-tuple-element.83), channel_id=1, source_target_pairs={{0,1},{1,0},{2,3},{3,2},{4,5},{5,4},{6,7},{7,6},{8,9},{9,8},{10,11... | collective-permute-start | bytes 442376 | tf_op jit(solution)/shard_map/ppermute | solution.py:732
  52.3 6.9 %copy-start.8 = (f32[576,192]{1,0:T(8,128)S(1)}, f32[576,192]{1,0:T(8,128)}, u32[]{:S(2)}) copy-start(f32[576,192]{1,0:T(8,128)} %copy-done.7) | copy-start | bytes 1327108
  53.2 21.8 %all-to-all-start = ((bf16[8,35,8,128]{3,2,1,0:T(8,128)(2,1)}), bf16[8,35,8,128]{3,2,1,0:T(8,128)(2,1)S(1)}, u32[]{:S(2)}, u32[]{:S(2)}) async-start(bf16[8,35,8,128]{3,2,1,0:T(8,128)(2,1)} %shard_map.120.order), calls=%async_computation | async-start | bytes 1146880 | tf_op jit(solution)/shard_map/all_to_all | solution.py:964
  59.2 1.0 copy-start.14
  60.2 1.1 copy-start.16
  61.3 1.0 copy-start.18
  71.0 1.4 %collective-permute-start.9 = (bf16[8,7,8,128]{3,2,1,0:T(8,128)(2,1)S(1)}, bf16[8,7,8,128]{3,2,1,0:T(8,128)(2,1)S(1)}, u32[]{:S(2)}, u32[]{:S(2)}) collective-permute-start(bf16[8,7,8,128]{3,2,1,0:T(8,128)(2,1)S(1)} %get-tuple-element.89), channel_id=1, source_target_pairs={{0,1},{1,0},{2,3},{3,2},{4,5},{5,4},{6,7},{7,6},{8,9},{9,8},{10,11... | collective-permute-start | bytes 344072 | tf_op jit(solution)/shard_map/ppermute | solution.py:732
  75.1 13.2 %all-to-all-start.2 = ((bf16[8,12,8,128]{3,2,1,0:T(8,128)(2,1)}), bf16[8,12,8,128]{3,2,1,0:T(8,128)(2,1)S(1)}, u32[]{:S(2)}, u32[]{:S(2)}) async-start(bf16[8,12,8,128]{3,2,1,0:T(8,128)(2,1)} %shard_map.122.order), calls=%async_computation.2 | async-start | bytes 393216 | tf_op jit(solution)/shard_map/all_to_all | solution.py:997
  80.2 8.8 %collective-permute-start.12 = (bf16[53,8,128]{2,1,0:T(8,128)(2,1)S(1)}, bf16[53,8,128]{2,1,0:T(8,128)(2,1)S(1)}, u32[]{:S(2)}, u32[]{:S(2)}) collective-permute-start(bf16[53,8,128]{2,1,0:T(8,128)(2,1)S(1)} %shard_map.123.order.refs_0_), channel_id=1, source_target_pairs={{0,12},{2,14},{4,0},{6,2},{8,4},{10,6},{12,8},{14,10},{1,13},{3,15... | collective-permute-start | bytes 325640 | tf_op jit(solution)/shard_map/ppermute | solution.py:737
  84.1 12.2 %collective-permute-start.11 = (bf16[53,8,128]{2,1,0:T(8,128)(2,1)S(1)}, bf16[53,8,128]{2,1,0:T(8,128)(2,1)S(1)}, u32[]{:S(2)}, u32[]{:S(2)}) collective-permute-start(bf16[53,8,128]{2,1,0:T(8,128)(2,1)S(1)} %shard_map.123.order.refs_0_), channel_id=1, source_target_pairs={{0,8},{2,10},{4,12},{6,14},{8,0},{10,2},{12,4},{14,6},{1,9},{3,11}... | collective-permute-start | bytes 325640 | tf_op jit(solution)/shard_map/ppermute | solution.py:737
  84.1 12.2 %collective-permute-start.10 = (bf16[53,8,128]{2,1,0:T(8,128)(2,1)S(1)}, bf16[53,8,128]{2,1,0:T(8,128)(2,1)S(1)}, u32[]{:S(2)}, u32[]{:S(2)}) collective-permute-start(bf16[53,8,128]{2,1,0:T(8,128)(2,1)S(1)} %shard_map.123.order.refs_0_), channel_id=1, source_target_pairs={{0,4},{2,6},{4,8},{6,10},{8,12},{10,14},{12,0},{14,2},{1,5},{3,7},... | collective-permute-start | bytes 325640 | tf_op jit(solution)/shard_map/ppermute | solution.py:737
  97.2 13.0 %collective-permute-start.13 = (bf16[4,53,8,128]{3,2,1,0:T(8,128)(2,1)S(1)}, bf16[4,53,8,128]{3,2,1,0:T(8,128)(2,1)S(1)}, u32[]{:S(2)}, u32[]{:S(2)}) collective-permute-start(bf16[4,53,8,128]{3,2,1,0:T(8,128)(2,1)S(1)} %shard_map.125.same), channel_id=1, source_target_pairs={{0,2},{2,0},{4,6},{6,4},{8,10},{10,8},{12,14},{14,12},{1,3},{3,1},... | collective-permute-start | bytes 1302536 | tf_op jit(solution)/shard_map/ppermute | solution.py:742
  98.7 11.7 %all-to-all-start.3 = ((bf16[8,12,8,128]{3,2,1,0:T(8,128)(2,1)}), bf16[8,12,8,128]{3,2,1,0:T(8,128)(2,1)S(1)}, u32[]{:S(2)}, u32[]{:S(2)}) async-start(bf16[8,12,8,128]{3,2,1,0:T(8,128)(2,1)} %shard_map.124.refs_4_), calls=%async_computation.3 | async-start | bytes 393216 | tf_op jit(solution)/shard_map/all_to_all | solution.py:1014
  102.1 10.1 %collective-permute-start.14 = (bf16[4,53,8,128]{3,2,1,0:T(8,128)(2,1)S(1)}, bf16[4,53,8,128]{3,2,1,0:T(8,128)(2,1)S(1)}, u32[]{:S(2)}, u32[]{:S(2)}) collective-permute-start(bf16[4,53,8,128]{3,2,1,0:T(8,128)(2,1)S(1)} %shard_map.125.same), channel_id=1, source_target_pairs={{0,1},{1,0},{2,3},{3,2},{4,5},{5,4},{6,7},{7,6},{8,9},{9,8},{10,11... | collective-permute-start | bytes 1302536 | tf_op jit(solution)/shard_map/ppermute | solution.py:732
  110.2 2.1 %collective-permute-start.15 = (bf16[4,53,8,128]{3,2,1,0:T(8,128)(2,1)S(1)}, bf16[4,53,8,128]{3,2,1,0:T(8,128)(2,1)S(1)}, u32[]{:S(2)}, u32[]{:S(2)}) collective-permute-start(bf16[4,53,8,128]{3,2,1,0:T(8,128)(2,1)S(1)} %collective-permute-done.13.same_x), channel_id=1, source_target_pairs={{0,1},{1,0},{2,3},{3,2},{4,5},{5,4},{6,7},{7,6},{8,9},{9,8},{10,11... | collective-permute-start | bytes 1302536 | tf_op jit(solution)/shard_map/ppermute | solution.py:732
  110.5 1.8 %collective-permute-start.16 = (bf16[8,12,8,128]{3,2,1,0:T(8,128)(2,1)S(1)}, bf16[8,12,8,128]{3,2,1,0:T(8,128)(2,1)S(1)}, u32[]{:S(2)}, u32[]{:S(2)}) collective-permute-start(bf16[8,12,8,128]{3,2,1,0:T(8,128)(2,1)S(1)} %all-to-all-done.3.own_c), channel_id=1, source_target_pairs={{0,1},{1,0},{2,3},{3,2},{4,5},{5,4},{6,7},{7,6},{8,9},{9,8},{10,11... | collective-permute-start | bytes 589832 | tf_op jit(solution)/shard_map/ppermute | solution.py:732

commit v7 on v5

--- a/solution.py
+++ b/solution.py
@@ -59,6 +59,10 @@
     second = row_mean(scaled * stand)
     gain_grad = jnp.sum(d * stand, axis=0, keepdims=True)
     return inv * (scaled - first - stand * second), gain_grad
+
+
+def gelu_value(hidden):
+    return 0.5 * hidden * (1.0 + lax.erf(hidden * ROOT_HALF))
 
 
 def gelu_parts(hidden):
@@ -178,7 +182,7 @@
     return total
 
 
-def attend(qkv, bias, mixed, probs, stack_scr, width, finish=None):
+def attend(qkv, bias, mixed, probs, stack_scr, width):
     masks = head_masks(width, BF16)
     masks32 = head_masks(width, F32)
     scale = (width // HEADS) ** -0.5
@@ -197,14 +201,12 @@
             probs[w, h] = p
             stack_scr[part, :] = p.astype(BF16)
         mixed[rows, :] = pick_heads(dot(stack_scr[...], v), masks32).astype(BF16)
-        if finish is not None:
-            finish(w)
         return carry
 
     lax.fori_loop(0, probs.shape[0], window, 0)
 
 
-def attend_back(qkv, probs, dmix, field, sums, low_scr, prob_scr, width, begin=None):
+def attend_back(qkv, probs, dmix, field, sums, low_scr, prob_scr, width):
     masks = head_masks(width, BF16)
     masks32 = head_masks(width, F32)
     scale = (width // HEADS) ** -0.5
@@ -216,8 +218,6 @@
         v = qkv[rows, 2 * width : 3 * width]
         up = stack_heads(dmix[rows, :], masks)
         prob_grad = dot_nt(up, v)
-        if begin is not None:
-            begin(w)
         for h in range(HEADS):
             part = slice(h * WIN, (h + 1) * WIN)
             p = probs[w, h]
@@ -299,13 +299,13 @@
     for k in range(BIAS_UNITS, lons * per):
         put_unit(k, jnp.zeros((UNIT, 128), BF16))
 
-def forward_core(x, b, refs, qkv_scr, bias_scr, mixed, probs, stack_scr, finish=None):
+def forward_core(x, b, refs, qkv_scr, bias_scr, mixed, probs, stack_scr):
     qkv_w, proj_w, gains = refs
     width = x.shape[-1]
     stand, inv = standardize(x)
     normed = (stand * gains[b, 0:1, :]).astype(BF16)
     qkv_scr[...] = dot(normed, qkv_w[b]).astype(BF16)
-    attend(qkv_scr, bias_scr, mixed, probs, stack_scr, width, finish)
+    attend(qkv_scr, bias_scr, mixed, probs, stack_scr, width)
     att = dot(mixed[...], proj_w[b]).astype(BF16)
     resid = (x + att.astype(F32)).astype(BF16).astype(F32)
     return resid, normed
@@ -313,10 +313,9 @@
 
 def first_kernel(
     lat_total, tokens_in, cot_in, table_in, spread_in, qkv_in, proj_in, up_in, down_in, gains_in,
-    x_out, tail_out, head_out, qkv_out, mixed_out, probs_out, resid_out, slope_out, active_out,
+    x_out, tail_out, head_out, qkv_out, mixed_out, probs_out, resid_out, hidden_out, active_out,
     scr, cot_scr, tab_scr, rows_scr, wide_scr, bias_scr,
-    cot, table, spread, tokens, qkv_w, gains, proj_w, up_w, down_w, stack_scr,
-    probs, slope_scr, active_scr, sems, out_sems,
+    cot, table, spread, tokens, qkv_w, gains, proj_w, up_w, down_w, stack_scr, sems,
 ):
     copies = []
     for source, target in (
@@ -354,39 +353,29 @@
     for copy in copies[4:]:
         copy.wait()
 
-    def probs_copy(w):
-        return pltpu.make_async_copy(probs.at[w], probs_out.at[w], out_sems.at[w])
-
     resid, _ = forward_core(
-        x, 0, (qkv_w, proj_w, gains), qkv_out, bias_scr, mixed_out, probs, stack_scr,
-        lambda w: probs_copy(w).start(),
+        x, 0, (qkv_w, proj_w, gains), qkv_out, bias_scr, mixed_out, probs_out, stack_scr
     )
     resid_out[...] = resid.astype(BF16)
     stand, _ = standardize(resid)
     normed = (stand * gains[0, 1:2, :]).astype(BF16)
-    active, slope = gelu_parts(dot(normed, up_w[0]))
-    active = active.astype(BF16)
-    active_scr[...] = active
-    slope_scr[...] = slope.astype(BF16)
-    wins = probs.shape[0]
-    last = [
-        pltpu.make_async_copy(active_scr, active_out, out_sems.at[wins]),
-        pltpu.make_async_copy(slope_scr, slope_out, out_sems.at[wins + 1]),
-    ]
-    for copy in last:
-        copy.start()
+    hidden = dot(normed, up_w[0])
+    hidden_out[...] = hidden
+    active = gelu_value(hidden).astype(BF16)
+    active_out[...] = active
     result = resid + dot_nt(active, down_w[0])
     head_out[0] = result[0:cut, :].astype(BF16)
     tail_out[0] = result[cut:, :].astype(BF16)
-    for copy in [probs_copy(w) for w in range(wins)] + last:
-        copy.wait()
-
-
-def bias_kernel(lat_total, table, spread, bias_out, tab_scr, rows_scr, wide_scr):
+
+
+def bias_kernel(
+    lat_total, table, spread, hidden, bias_out, slope_out, tab_scr, rows_scr, wide_scr
+):
     lat = lax.axis_index("lat")
     expand_bias(
         table.at[1], spread, tab_scr, rows_scr, wide_scr, bias_out, lat, True, lat_total
     )
+    slope_out[...] = gelu_parts(hidden[...])[1].astype(BF16)
 
 
 def merge_ahead(scr_own, scr_oth, rows):
@@ -483,17 +472,15 @@
     bias_units(sums, bias_out)
 
 
-def lat_sum(keep_a, got_a, bias_a, keep_b, got_b, out):
-    one, two = keep_a.shape[1], bias_a.shape[1]
-    out[:, 0:one] = (keep_a[...].astype(F32) + got_a[...].astype(F32)).astype(BF16)
-    out[:, one : one + two] = bias_a[...]
-    out[:, one + two :] = (keep_b[...].astype(F32) + got_b[...].astype(F32)).astype(BF16)
-
-
-def lat_sum_late(keep, got, bias, out):
-    one = keep.shape[1]
-    out[:, 0:one] = (keep[...].astype(F32) + got[...].astype(F32)).astype(BF16)
-    out[:, one:] = bias[...]
+def lat_sums(*refs):
+    out = refs[-1]
+    at = 0
+    for k in range(0, len(refs) - 2, 2):
+        keep, got = refs[k], refs[k + 1]
+        count = keep.shape[1]
+        out[:, at : at + count] = (keep[...].astype(F32) + got[...].astype(F32)).astype(BF16)
+        at += count
+    out[:, at:] = refs[-2][...]
 
 
 def sum_pieces(pieces, order, out):
@@ -517,17 +504,11 @@
 
 
 def third_kernel(
-    head, lon_tail, lat_head, diag_tail, resid_in, slope_in, active_in, mixed,
-    proj_w, up_w, down_w, gains, keep_a,
+    head, lon_tail, lat_head, diag_tail, resid_in, slope, active, mixed,
+    proj_w, up_w, down_w, gains, order,
     keep_out, give_out, rg_out, dmix_out, gain_out,
-    scr_own, scr_oth, m192, m768, mdown, flat_scr, slope, active, sems,
+    scr_own, scr_oth, m192, m768, mdown, flat_scr,
 ):
-    copies = [
-        pltpu.make_async_copy(slope_in, slope, sems.at[0]),
-        pltpu.make_async_copy(active_in, active, sems.at[1]),
-    ]
-    for copy in copies:
-        copy.start()
     rows, width = scr_own.shape
     cut = CHUNK * (WLON // 2)
     scr_own[0:cut, :] = lon_tail[...].astype(F32)
@@ -536,11 +517,10 @@
     scr_oth[cut:, :] = lat_head[...].astype(F32)
     g = merge_behind(scr_own, scr_oth, rows)
     g_low = g.astype(BF16)
-    for copy in copies:
-        copy.wait()
-    hg = (dot(g_low, down_w[0]) * slope[...].astype(F32)).astype(BF16)
     stand2, inv2 = standardize(resid_in[...].astype(F32))
     normed2 = (stand2 * gains[0, 1:2, :]).astype(BF16)
+    hg = dot(g_low, down_w[0])
+    hg = (hg * slope[...].astype(F32)).astype(BF16)
     part, gain_two = norm_back(dot_nt(hg, up_w[0]), gains[0, 1:2, :], stand2, inv2)
     rg = g + part
     rg_out[...] = rg
@@ -569,21 +549,14 @@
 
 
 def fourth_kernel(
-    x_in, qkv, probs_in, dmix, rg, gain_two, gains_late, order, qkv_w, gains,
+    x_in, qkv, probs, dmix, rg, gain_two, gains_late, order, qkv_w, gains,
     tokens_out, keep, give, bias_out,
-    field, sums, m576, flat_scr, dx_scr, low_scr, prob_scr, probs, sems,
+    field, sums, m576, flat_scr, dx_scr, low_scr, prob_scr,
 ):
-    def probs_copy(w):
-        return pltpu.make_async_copy(probs_in.at[w], probs.at[w], sems.at[w])
-
-    for w in range(probs.shape[0]):
-        probs_copy(w).start()
     width = x_in.shape[-1]
     levels, lats, lons = tokens_out.shape[:3]
     sums[...] = jnp.zeros(sums.shape, F32)
-    attend_back(
-        qkv, probs, dmix, field, sums, low_scr, prob_scr, width, lambda w: probs_copy(w).wait()
-    )
+    attend_back(qkv, probs, dmix, field, sums, low_scr, prob_scr, width)
     stand1, inv1 = standardize(x_in[...].astype(F32))
     normed = (stand1 * gains[0, 0:1, :]).astype(BF16)
     ng = dot_nt(field[...], qkv_w[0]).astype(BF16).astype(F32)
@@ -604,20 +577,21 @@
 
 
 def last_kernel(
-    units_a, units_c, extra, spread, same, same_x, cross, cross_x, own_c, oth_c,
-    update_out, bias_out, scr, rows_scr, wide_scr, tab_scr, ab, c,
+    units_a, units_b, units_c, spread, same, same_x, cross, cross_x, own_bc, oth_bc,
+    update_out, bias_out, scr, rows_scr, wide_scr, tab_scr, a, bc,
 ):
     lat = lax.axis_index("lat")
     x = lax.rem(lax.axis_index("lon"), 2)
-    lons = own_c.shape[0]
+    lons = own_bc.shape[0]
+    extra = bc.shape[2] - units_b - units_c
     for j in range(lons):
-        c[lat, j] = own_c[j]
-        c[1 - lat, j] = oth_c[j]
+        bc[lat, j] = own_bc[j]
+        bc[1 - lat, j] = oth_bc[j]
     for z in range(lons // 2):
-        ab[lat, 2 * z + x] = same[z]
-        ab[lat, 2 * z + 1 - x] = same_x[z]
-        ab[1 - lat, 2 * z + x] = cross[z]
-        ab[1 - lat, 2 * z + 1 - x] = cross_x[z]
+        a[lat, 2 * z + x] = same[z]
+        a[lat, 2 * z + 1 - x] = same_x[z]
+        a[1 - lat, 2 * z + x] = cross[z]
+        a[1 - lat, 2 * z + 1 - x] = cross_x[z]
 
     def place(pieces, first, last, dests):
         total = jnp.zeros((UNIT, 128), F32)
@@ -632,20 +606,15 @@
                 k += 1
         return total
 
-    total = place(
-        ab, 0, units_a, [(864, 864), (2016, 288), (3456, 1152), (5760, 1152)]
-    )
-    total = total + place(
-        ab, units_a + extra, ab.shape[2],
-        [(1728, 288), (2304, 1152), (4608, 1152)],
-    )
-    total = total + place(c, 0, units_c, [(0, 864), (6912, 8)])
+    total = place(a, 0, units_a, [(864, 864), (2016, 288), (3456, 1152), (5760, 1152)])
+    total = total + place(bc, 0, units_b, [(1728, 288), (2304, 1152), (4608, 1152)])
+    total = total + place(bc, units_b, units_b + units_c, [(0, 864), (6912, 8)])
     count = update_out.shape[0]
     mean = jnp.sum(total) * (1.0 / (count * 128))
     scale = lax.rsqrt(mean + 1e-06)
     update_out[...] = (scr[0:count, :] * scale).astype(BF16)
 
-    for b, (piece, base) in enumerate(((c, units_c), (ab, units_a))):
+    for b, (piece, base) in enumerate(((bc, units_b + units_c), (a, units_a))):
 
         def read(at):
             parts = []
@@ -672,17 +641,16 @@
             bias_out[b, h] = tab_scr[h : h + 1, :]
 
 
-def call(kernel, outs, scratch, args, micros, mib, spaces=None, out_spaces=None):
+def call(kernel, outs, scratch, args, micros, mib, spaces=None, pinned=()):
     spaces = spaces or [pltpu.VMEM] * len(args)
-    out_spaces = out_spaces or [pltpu.VMEM] * len(outs)
     return pl.pallas_call(
         kernel,
         out_shape=[
-            pltpu.HBM(*entry) if space == pltpu.HBM else jax.ShapeDtypeStruct(*entry)
-            for entry, space in zip(outs, out_spaces)
+            pltpu.VMEM(*entry) if at in pinned else jax.ShapeDtypeStruct(*entry)
+            for at, entry in enumerate(outs)
         ],
         in_specs=[pl.BlockSpec(memory_space=space) for space in spaces],
-        out_specs=[pl.BlockSpec(memory_space=space) for space in out_spaces],
+        out_specs=[pl.BlockSpec(memory_space=pltpu.VMEM)] * len(outs),
         scratch_shapes=[
             pltpu.VMEM(*entry) if isinstance(entry, tuple) else entry for entry in scratch
         ],
@@ -759,7 +727,7 @@
     def flat_scr(per):
         return ((2 * lon_size * per * UNIT, 128), F32)
 
-    x0, tail, head, qkv0, mixed0, probs0, resid0, slope0, active0 = call(
+    x0, tail, head, qkv0, mixed0, probs0, resid0, hidden0, active0 = call(
         functools.partial(first_kernel, lat_total),
         [
             (token, BF16),
@@ -769,7 +737,7 @@
             (token, BF16),
             probs_shape,
             (token, BF16),
-            ((rows, hid), BF16),
+            ((rows, hid), F32),
             ((rows, hid), BF16),
         ],
         [
@@ -789,11 +757,7 @@
             ((1,) + up_weight.shape[1:], BF16),
             ((1,) + down_turned.shape[1:], BF16),
             stack_shape,
-            probs_shape,
-            ((rows, hid), BF16),
-            ((rows, hid), BF16),
             pltpu.SemaphoreType.DMA((9,)),
-            pltpu.SemaphoreType.DMA((wins + 2,)),
         ],
         [
             pltpu.with_memory_space_constraint(arg, pltpu.HBM)
@@ -805,18 +769,20 @@
         8,
         28,
         [pltpu.HBM] * 9,
-        [pltpu.VMEM] * 5 + [pltpu.HBM, pltpu.VMEM, pltpu.HBM, pltpu.HBM],
+        (0, 3, 4, 5, 6, 8),
     )
     lon_head = lon_send(head, -1)
     diag_head = diag_send(head, -1)
     lat_tail = lat_swap(tail)
-    (bias1,) = call(
+    bias1, slope0 = call(
         functools.partial(bias_kernel, lat_total),
-        [bias_shape],
+        [bias_shape, ((rows, hid), BF16)],
         [tab_scr, rows_scr, wide_scr],
-        (table, spread),
-        2,
+        (table, spread, hidden0),
+        3,
         10,
+        None,
+        (1,),
     )
 
     (
@@ -876,37 +842,19 @@
             (token, BF16),
             ((1, width), F32),
         ],
-        [
-            (token, F32),
-            (token, F32),
-            m192,
-            m768,
-            mdown,
-            flat_scr(units_b),
-            ((rows, hid), BF16),
-            ((rows, hid), BF16),
-            pltpu.SemaphoreType.DMA((2,)),
-        ],
+        [(token, F32), (token, F32), m192, m768, mdown, flat_scr(units_b)],
         (
-            dhead, lon_tail, lat_dhead, diag_tail, resid0,
-            pltpu.with_memory_space_constraint(slope0, pltpu.HBM),
-            pltpu.with_memory_space_constraint(active0, pltpu.HBM),
-            mixed0, proj_weight, up_weight, down_turned, norm_gain, keep_a,
+            dhead, lon_tail, lat_dhead, diag_tail, resid0, slope0, active0, mixed0, proj_weight,
+            up_weight, down_turned, norm_gain, keep_a,
         ),
-        2,
+        3,
         20,
-        [pltpu.VMEM] * 5 + [pltpu.HBM] * 2 + [pltpu.VMEM] * 6,
     )
     got_b = lat_swap(give_b)
-    (part_ab,) = call(
-        lat_sum,
-        [units(lon_size, units_a + extra + units_b)],
-        [],
-        (keep_a, got_a, bias_a, keep_b, got_b),
-        1,
-        10,
-    )
-    pieces_ab = lax.all_to_all(part_ab, "lon", 0, 0)
+    (part_a,) = call(
+        lat_sums, [units(lon_size, units_a + extra)], [], (keep_a, got_a, bias_a), 1, 10
+    )
+    pieces_a = lax.all_to_all(part_a, "lon", 0, 0)
 
     tokens_grad, keep_c, give_c, bias_c = call(
         fourth_kernel,
@@ -924,56 +872,62 @@
             token_scr,
             stack_shape,
             stack_shape,
-            probs_shape,
-            pltpu.SemaphoreType.DMA((wins,)),
         ],
         (
-            x0, qkv0, pltpu.with_memory_space_constraint(probs0, pltpu.HBM), dmix0, rg0, gain_two,
-            gains1, part_ab, qkv_weight, norm_gain,
+            x0, qkv0, probs0, dmix0, rg0, gain_two, gains1, part_a, qkv_weight, norm_gain,
         ),
-        11,
-        24,
-        [pltpu.VMEM] * 2 + [pltpu.HBM] + [pltpu.VMEM] * 7,
+        9,
+        20,
     )
     got_c = lat_swap(give_c)
-    (part_c,) = call(
-        lat_sum_late, [units(lon_size, units_c + extra)], [], (keep_c, got_c, bias_c), 1, 10
-    )
-    pieces_c = lax.all_to_all(part_c, "lon", 0, 0)
-
-    (sum_ab,) = call(
-        sum_pieces, [units(units_a + extra + units_b)], [], (pieces_ab, part_c), 1, 10
-    )
-    (sum_c,) = call(
-        sum_pieces, [units(lon_size, units_c + extra)], [], (pieces_c, sum_ab), 1, 10
-    )
-    (same_ab,) = call(
-        join_z,
-        [units(zs, units_a + extra + units_b)],
+    (part_bc,) = call(
+        lat_sums,
+        [units(lon_size, units_b + units_c + extra)],
         [],
-        [sum_ab] + [lon_send(sum_ab, 2 * k) for k in range(1, zs)] + [sum_c],
+        (keep_b, got_b, keep_c, got_c, bias_c),
         1,
         10,
     )
-    whole_c = lax.all_to_all(sum_c, "lon", 0, 0)
-    same_x = x_swap(same_ab)
-    cross = lat_swap(same_ab)
+    pieces_bc = lax.all_to_all(part_bc, "lon", 0, 0)
+
+    (sum_a,) = call(
+        sum_pieces, [units(units_a + extra)], [], (pieces_a, part_bc), 1, 10
+    )
+    (sum_bc,) = call(
+        sum_pieces,
+        [units(lon_size, units_b + units_c + extra)],
+        [],
+        (pieces_bc, sum_a),
+        1,
+        10,
+    )
+    whole_bc = lax.all_to_all(sum_bc, "lon", 0, 0)
+    (same,) = call(
+        join_z,
+        [units(zs, units_a + extra)],
+        [],
+        [sum_a] + [lon_send(sum_a, 2 * k) for k in range(1, zs)],
+        1,
+        10,
+    )
+    same_x = x_swap(same)
+    cross = lat_swap(same)
     cross_x = lat_swap(same_x)
-    oth_c = lat_swap(whole_c)
+    oth_bc = lat_swap(whole_bc)
 
     flat_rows = (2 * block_rows * 128 + norm_gain.size) // 128
     update, bias_grad = call(
-        functools.partial(last_kernel, units_a, units_c, extra),
+        functools.partial(last_kernel, units_a, units_b, units_c),
         [((flat_rows, 128), BF16), (table.shape, F32)],
         [
             ((flat_rows + 2, 128), F32),
             ((CHUNK * 8, PAIR), F32),
             wide_scr,
             tab_scr,
-            units(2, lon_size, units_a + extra + units_b),
-            units(2, lon_size, units_c + extra),
-        ],
-        (spread, same_ab, same_x, cross, cross_x, whole_c, oth_c),
+            units(2, lon_size, units_a + extra),
+            units(2, lon_size, units_b + units_c + extra),
+        ],
+        (spread, same, same_x, cross, cross_x, whole_bc, oth_bc),
         3,
         20,
     )

time: 112 us -> 120 us (1.071)
  waiting for transfers between devices: 40.8 us -> 49.2 us
  local copies, waits for them, and re-layouts: 1.15 us -> 4.88 us
  Pallas kernels: 42.9 us -> 39.2 us
    all_to_all x3, waiting for transfers between devices: 13.6 us -> 30.6 us  [the longest x1 14.1 us: shards(): whole_bc = lax.all_to_all(sum_bc, 'lon', 0, 0)]
    ppermute x5, waiting for transfers between devices: 10.1 us -> 4.31 us  [lon_send(): lax.ppermute(value, 'lon', [(s, (s + step) % count) for s in range(count)])]
    unnamed x18 -> x22, local copies, waits for them, and re-layouts: 1.15 us -> 4.88 us
    pallas_call x12, Pallas kernels: 42.9 us -> 39.2 us  [call(): pl.pallas_call(kernel, out_shape=[pltpu.VMEM(*entry) if at in pinned else...]
    ppermute x1, waiting for transfers between devices: 7.97 us -> 5.72 us  [x_swap(): return lax.ppermute(value, 'lon', [(s, s ^ 1) for s in range(count)])]
    ppermute x8, waiting for transfers between devices: 4.38 us -> 2.54 us  [lat_swap(): return lax.ppermute(value, 'lat', [(0, 1), (1, 0)])]
    ppermute x2, waiting for transfers between devices: 4.77 us -> 6.04 us  [diag_send(): return lax.ppermute(value, ('lon', 'lat'), pairs)]
  transfers between devices with their start and end apart: 19 -> 19, of which waited for: 12 -> 10; matrix products, arithmetic and copies ran while one was open for 0% -> 0% of each run, Pallas kernels for 16% -> 14%
where the time goes in v7:
time: 120 us; the launch traced here: 119 us
  waiting for transfers between devices  49.2 us (41%)
  Pallas kernels  39.2 us (33%)
  starting transfers between devices  25.1 us (21%)
  local copies, waits for them, and re-layouts  4.88 us (4%)
    pallas_call x12, Pallas kernels, call(): pl.pallas_call(kernel, out_shape=[pltpu.VMEM(*entry) if at in pinned else...  39.2 us
    all_to_all x1, waiting for transfers between devices, shards(): whole_bc = lax.all_to_all(sum_bc, 'lon', 0, 0)  14.1 us
    all_to_all x1, waiting for transfers between devices, shards(): pieces_bc = lax.all_to_all(part_bc, 'lon', 0, 0)  13.9 us
    ppermute x2, waiting for transfers between devices, diag_send(): return lax.ppermute(value, ('lon', 'lat'), pairs)  6.04 us
    ppermute x1, waiting for transfers between devices, x_swap(): return lax.ppermute(value, 'lon', [(s, s ^ 1) for s in range(count)])  5.72 us
    ppermute x2, starting transfers between devices, diag_send(): return lax.ppermute(value, ('lon', 'lat'), pairs)  5.64 us
    ppermute x5, starting transfers between devices, lon_send(): lax.ppermute(value, 'lon', [(s, (s + step) % count) for s in range(count)])  5.52 us
    unnamed x22, local copies, waits for them, and re-layouts  4.88 us
  transfers between devices with their start and end apart: 19, of which 10 were waited for; matrix products, arithmetic and copies ran while one was open for 0% of the time, Pallas kernels for 14%

profile of v7, /device:TPU:0, one launch (start us, length us, event | category | flops | bytes accessed | tf_op | source)
XLA Modules:
  0.0 119.2 jit_solution(2549043624191172534)
XLA Ops:
  0.6 0.0 copy-start.6
  0.7 7.9 %shard_map.112 = (bf16[576,192]{1,0:T(8,128)(2,1)S(1)}, bf16[2,504,192]{2,1,0:T(8,128)(2,1)S(1)}, bf16[2,72,192]{2,1,0:T(8,128)(2,1)S(1)}, bf16[576,576]{1,0:T(8...) custom-call(bf16[2,12,24,192]{3,2,1,0:T(8,128)(2,1)} %tokens_in.1, ...), custom_call_target="tpu_custom_call" | custom-call | flops 8800000000 | bytes 100000 | tf_op jit(solution)/shard_map/pallas_call | solution.py:646
  8.6 1.7 %copy-done.7 = f32[4,6,144,144]{3,2,1,0:T(8,128)} copy-done((f32[4,6,144,144]{3,2,1,0:T(8,128)}, f32[4,6,144,144]{3,2,1,0:T(8,128)S(1)}, u32[]{:S(2)}) %copy-start.7) | copy-done | bytes 1990680
  10.3 0.5 collective-permute-start.1
  10.8 5.6 %collective-permute-start.2 = (bf16[2,72,192]{2,1,0:T(8,128)(2,1)S(1)}, bf16[2,72,192]{2,1,0:T(8,128)(2,1)S(1)}, u32[]{:S(2)}, u32[]{:S(2)}) collective-permute-start(bf16[2,72,192]{2,1,0:T(8,128)(2,1)S(1)} %get-tuple-element.44), channel_id=1, source_target_pairs={{0,15},{1,14},{2,1},{3,0},{4,3},{5,2},{6,5},{7,4},{8,7},{9,6},{10,... | collective-permute-start | bytes 165896 | tf_op jit(solution)/shard_map/ppermute | solution.py:684
  16.4 0.5 collective-permute-start
  17.0 0.0 copy-start.2
  17.0 0.0 copy-start.4
  17.0 0.0 copy-start.5
  17.0 2.2 %shard_map.113 = (f32[864,144]{1,0:T(8,128)S(1)}, bf16[576,768]{1,0:T(8,128)(2,1)S(1)}) custom-call(f32[2,6,1,6336]{3,2,1,0:T(1,128)S(1)} %bitcast.8, bf16[2,132,384]{2,1,0:T(8,128)(2,1)S(1)} %copy-done.6, f32[576,768]{1,0:T(8,128)S(1)} %get-tuple-element.45.hidden), custom_call_target="tpu_custom_call" | custom-call | flops 3300000000 | bytes 100000 | tf_op jit(solution)/shard_map/pallas_call | solution.py:646
  19.2 0.0 collective-permute-done.2.diag_head
  19.2 1.6 %collective-permute-done.lon_head = bf16[2,72,192]{2,1,0:T(8,128)(2,1)S(1)} collective-permute-done((bf16[2,72,192]{2,1,0:T(8,128)(2,1)S(1)}, bf16[2,72,192]{2,1,0:T(8,128)(2,1)S(1)}, u32[]{:S(2)}, u32[]{:S(2)}) %collective-permute-start) | collective-permute-done | bytes 55328 | tf_op jit(solution)/shard_map/ppermute | solution.py:670
  20.8 0.0 collective-permute-done.1.lat_tail
  20.8 11.5 %shard_map.114 = (bf16[504,192]{1,0:T(8,128)(2,1)S(1)}, bf16[72,192]{1,0:T(8,128)(2,1)S(1)}, bf16[576,192]{1,0:T(8,128)(2,1)S(1)}, bf16[576,576]{1,0:T(8,128)(2,...) custom-call(bf16[2,504,192]{2,1,0:T(8,128)(2,1)S(1)} %get-tuple-elem, ...), custom_call_target="tpu_custom_call" | custom-call | flops 20899999744 | bytes 100000 | tf_op jit(solution)/shard_map/pallas_call | solution.py:646
  32.4 0.1 collective-permute-start.4
  32.4 1.7 %shard_map.115 = (bf16[8,27,8,128]{3,2,1,0:T(8,128)(2,1)S(1)}, bf16[8,27,8,128]{3,2,1,0:T(8,128)(2,1)S(1)}, bf16[8,5,8,128]{3,2,1,0:T(8,128)(2,1)S(1)}) custom-call(bf16[576,192]{1,0:T(8,128)(2,1)S(1)} %get-tuple-element.53.n1, bf16[576,576]{1,0:T(8,128)(2,1)S(1)} %get-tuple-element.54.field, bf16[576,192]{1,0:T(8,128)(2,1)S(1)} %get-tuple-element.55.mixed, ...), custom_call_target="tpu_custom_call" | custom-call | flops 3300000000 | bytes 100000 | tf_op jit(solution)/shard_map/pallas_call | solution.py:646
  34.1 0.6 collective-permute-start.6
  34.6 0.0 collective-permute-start.5
  34.6 0.0 collective-permute-start.3
  34.7 6.0 %collective-permute-done.5.diag_tail = bf16[72,192]{1,0:T(8,128)(2,1)S(1)} collective-permute-done((bf16[72,192]{1,0:T(8,128)(2,1)S(1)}, bf16[72,192]{1,0:T(8,128)(2,1)S(1)}, u32[]{:S(2)}, u32[]{:S(2)}) %collective-permute-start.5) | collective-permute-done | bytes 27680 | tf_op jit(solution)/shard_map/ppermute | solution.py:684
  40.7 1.2 collective-permute-done.3.lon_tail
  41.9 0.0 collective-permute-done.4.lat_head
  41.9 2.1 %shard_map.116 = (bf16[8,21,8,128]{3,2,1,0:T(8,128)(2,1)S(1)}, bf16[8,21,8,128]{3,2,1,0:T(8,128)(2,1)S(1)}, f32[576,192]{1,0:T(8,128)S(1)}, bf16[576,192]{1,0:T(8,128)(2,1)S(1)}, f32[1,192]{1,0:T(1,128)S(1)}) custom-call(bf16[504,192]{1,0:T(8,128)(2,1)S(1)} %get-tuple-element.47.head, bf16[72,192]{1,0:T(8,128)(2,1)S(1)} %collective-permute-done.3.lon_tail, ...), custom_call_target="tpu_custom_call" | custom-call | flops 3300000000 | bytes 100000 | tf_op jit(solution)/shard_map/pallas_call | solution.py:646
  44.0 0.1 collective-permute-start.7
  44.1 0.9 shard_map.117.order
  45.0 3.7 %all-to-all-start = ((bf16[8,32,8,128]{3,2,1,0:T(8,128)(2,1)}), bf16[8,32,8,128]{3,2,1,0:T(8,128)(2,1)S(1)}, u32[]{:S(2)}, u32[]{:S(2)}) async-start(bf16[8,32,8,128]{3,2,1,0:T(8,128)(2,1)} %shard_map.117.order), calls=%async_computation | async-start | bytes 1048576 | tf_op jit(solution)/shard_map/all_to_all | solution.py:857
  48.7 2.0 %copy-done.8 = f32[4,6,144,144]{3,2,1,0:T(8,128)S(1)} copy-done((f32[4,6,144,144]{3,2,1,0:T(8,128)S(1)}, f32[4,6,144,144]{3,2,1,0:T(8,128)}, u32[]{:S(2)}) %copy-start.8) | copy-done | bytes 1990680
  50.7 1.1 copy-done.10
  51.8 7.3 %shard_map.118 = (bf16[2,12,24,192]{3,2,1,0:T(8,128)(2,1)}, bf16[8,7,8,128]{3,2,1,0:T(8,128)(2,1)S(1)}, bf16[8,7,8,128]{3,2,1,0:T(8,128)(2,1)S(1)}, bf16[8,5,8,128]{3,2,1,0:T(8,128)(2,1)S(1)}) custom-call(bf16[576,192]{1,0:T(8,128)(2,1)S(1)} %get-tuple-element.40.x_in, bf16[576,576]{1,0:T(8,128)(2,1)S(1)} %copy-done.10, f32[4,6,144,144]{3,2,1,0:T(8,128)S(1)} %copy-done.8, ...), custom_call_target="tpu_custom_call" | custom-call | flops 9900000256 | bytes 100000 | tf_op jit(solution)/shard_map/pallas_call | solution.py:646
  59.1 0.3 collective-permute-start.8
  59.4 0.0 collective-permute-done.7.refs_1_
  59.4 1.0 collective-permute-done.8.refs_3_
  60.4 0.9 shard_map.119.order
  61.3 2.6 %all-to-all-done.pieces = bf16[8,32,8,128]{3,2,1,0:T(8,128)(2,1)S(1)} async-done(((bf16[8,32,8,128]{3,2,1,0:T(8,128)(2,1)}), bf16[8,32,8,128]{3,2,1,0:T(8,128)(2,1)S(1)}, u32[]{:S(2)}, u32[]{:S(2)}) %all-to-all-start) | async-done | bytes 524320 | tf_op jit(solution)/shard_map/all_to_all | solution.py:857
  63.9 3.6 %all-to-all-start.1 = ((bf16[8,33,8,128]{3,2,1,0:T(8,128)(2,1)}), bf16[8,33,8,128]{3,2,1,0:T(8,128)(2,1)S(1)}, u32[]{:S(2)}, u32[]{:S(2)}) async-start(bf16[8,33,8,128]{3,2,1,0:T(8,128)(2,1)} %shard_map.119.order), calls=%async_computation.1 | async-start | bytes 1081344 | tf_op jit(solution)/shard_map/all_to_all | solution.py:891
  67.5 1.2 shard_map.120.refs_0_.order
  68.6 13.9 %all-to-all-done.1.pieces = bf16[8,33,8,128]{3,2,1,0:T(8,128)(2,1)S(1)} async-done(((bf16[8,33,8,128]{3,2,1,0:T(8,128)(2,1)}), bf16[8,33,8,128]{3,2,1,0:T(8,128)(2,1)S(1)}, u32[]{:S(2)}, u32[]{:S(2)}) %all-to-all-start.1) | async-done | bytes 540704 | tf_op jit(solution)/shard_map/all_to_all | solution.py:891
  82.5 0.9 shard_map.122
  83.4 3.6 %all-to-all-start.2 = ((bf16[8,33,8,128]{3,2,1,0:T(8,128)(2,1)}), bf16[8,33,8,128]{3,2,1,0:T(8,128)(2,1)S(1)}, u32[]{:S(2)}, u32[]{:S(2)}) async-start(bf16[8,33,8,128]{3,2,1,0:T(8,128)(2,1)} %shard_map.122), calls=%async_computation.2 | async-start | bytes 1081344 | tf_op jit(solution)/shard_map/all_to_all | solution.py:904
  87.0 3.8 %collective-permute-start.11 = (bf16[32,8,128]{2,1,0:T(8,128)(2,1)S(1)}, bf16[32,8,128]{2,1,0:T(8,128)(2,1)S(1)}, u32[]{:S(2)}, u32[]{:S(2)}) collective-permute-start(bf16[32,8,128]{2,1,0:T(8,128)(2,1)S(1)} %shard_map.120.refs_0_.order), channel_id=1, source_target_pairs={{0,12},{2,14},{4,0},{6,2},{8,4},{10,6},{12,8},{14,10},{1,13},{3,15... | collective-permute-start | bytes 196616 | tf_op jit(solution)/shard_map/ppermute | solution.py:670
  90.9 0.0 collective-permute-start.10
  90.9 1.1 collective-permute-start.9
  92.0 14.1 %all-to-all-done.2.own_bc = bf16[8,33,8,128]{3,2,1,0:T(8,128)(2,1)S(1)} async-done(((bf16[8,33,8,128]{3,2,1,0:T(8,128)(2,1)}), bf16[8,33,8,128]{3,2,1,0:T(8,128)(2,1)S(1)}, u32[]{:S(2)}, u32[]{:S(2)}) %all-to-all-start.2) | async-done | bytes 540704 | tf_op jit(solution)/shard_map/all_to_all | solution.py:904
  106.1 1.5 %collective-permute-done.10.refs_2_ = bf16[32,8,128]{2,1,0:T(8,128)(2,1)S(1)} collective-permute-done((bf16[32,8,128]{2,1,0:T(8,128)(2,1)S(1)}, bf16[32,8,128]{2,1,0:T(8,128)(2,1)S(1)}, u32[]{:S(2)}, u32[]{:S(2)}) %collective-permute-start.10) | collective-permute-done | bytes 65568 | tf_op jit(solution)/shard_map/ppermute | solution.py:670
  107.7 1.5 %collective-permute-start.12 = (bf16[4,32,8,128]{3,2,1,0:T(8,128)(2,1)S(1)}, bf16[4,32,8,128]{3,2,1,0:T(8,128)(2,1)S(1)}, u32[]{:S(2)}, u32[]{:S(2)}) collective-permute-start(bf16[4,32,8,128]{3,2,1,0:T(8,128)(2,1)S(1)} %shard_map.121.same), channel_id=1, source_target_pairs={{0,2},{2,0},{4,6},{6,4},{8,10},{10,8},{12,14},{14,12},{1,3},{3,1},... | collective-permute-start | bytes 786440 | tf_op jit(solution)/shard_map/ppermute | solution.py:675
  109.3 5.7 %collective-permute-done.12.same_x = bf16[4,32,8,128]{3,2,1,0:T(8,128)(2,1)S(1)} collective-permute-done((bf16[4,32,8,128]{3,2,1,0:T(8,128)(2,1)S(1)}, bf16[4,32,8,128]{3,2,1,0:T(8,128)(2,1)S(1)}, u32[]{:S(2)}, u32[]{:S(2)}) %collective-permute-start.12) | collective-permute-done | bytes 262176 | tf_op jit(solution)/shard_map/ppermute | solution.py:675
  115.0 1.5 %collective-permute-done.14.cross_x = bf16[4,32,8,128]{3,2,1,0:T(8,128)(2,1)S(1)} collective-permute-done((bf16[4,32,8,128]{3,2,1,0:T(8,128)(2,1)S(1)}, bf16[4,32,8,128]{3,2,1,0:T(8,128)(2,1)S(1)}, u32[]{:S(2)}, u32[]{:S(2)}) %collective-permute-start.14) | collective-permute-done | bytes 262176 | tf_op jit(solution)/shard_map/ppermute | solution.py:665
  116.5 2.7 %shard_map.123 = (bf16[6918,128]{1,0:T(8,128)(2,1)}, f32[2,6,1,6336]{3,2,1,0:T(1,128)}) custom-call(bf16[2,132,384]{2,1,0:T(8,128)(2,1)S(1)} %copy-done.6, bf16[4,32,8,128]{3,2,1,0:T(8,128)(2,1)S(1)} %shard_map.121.same, bf16[4,32,8,128]{3,2,1,0:T(8,128)(2,1)S(1)} %collective-permute-done.12.same_x, ...), custom_call_target="tpu_custom_call" | custom-call | flops 3300000000 | bytes 100000 | tf_op jit(solution)/shard_map/pallas_call | solution.py:646
  (24 shorter events, 0.1 us)
Async XLA Ops:
  0.6 16.3 %copy-start.3 = (f32[2,1,6,6336]{3,1,2,0:T(1,128)S(1)}, f32[2,1,6,6336]{3,1,2,0:T(1,128)}, u32[]{:S(2)}) copy-start(f32[2,1,6,6336]{3,1,2,0:T(1,128)} %param.16) | copy-start | bytes 912388
  0.6 16.3 %copy-start.6 = (bf16[2,132,384]{2,1,0:T(8,128)(2,1)S(1)}, bf16[2,132,384]{2,1,0:T(8,128)(2,1)}, u32[]{:S(2)}) copy-start(bf16[2,132,384]{2,1,0:T(8,128)(2,1)} %constant.2.clone.spread_in.spread) | copy-start | bytes 608260
  8.6 1.7 %copy-start.7 = (f32[4,6,144,144]{3,2,1,0:T(8,128)}, f32[4,6,144,144]{3,2,1,0:T(8,128)S(1)}, u32[]{:S(2)}) copy-start(f32[4,6,144,144]{3,2,1,0:T(8,128)S(1)} %get-tuple-element.42.probs) | copy-start | bytes 5971972
  10.3 8.8 %copy-start.9 = (bf16[576,576]{1,0:T(8,128)(2,1)}, bf16[576,576]{1,0:T(8,128)(2,1)S(1)}, u32[]{:S(2)}) copy-start(bf16[576,576]{1,0:T(8,128)(2,1)S(1)} %get-tuple-element.41.qkv) | copy-start | bytes 1990660
  10.3 10.5 %collective-permute-start.1 = (bf16[2,504,192]{2,1,0:T(8,128)(2,1)S(1)}, bf16[2,504,192]{2,1,0:T(8,128)(2,1)S(1)}, u32[]{:S(2)}, u32[]{:S(2)}) collective-permute-start(bf16[2,504,192]{2,1,0:T(8,128)(2,1)S(1)} %get-tuple-element.43.tail), channel_id=1, source_target_pairs={{0,1},{1,0},{2,3},{3,2},{4,5},{5,4},{6,7},{7,6},{8,9},{9,8},{10,11... | collective-permute-start | bytes 1161224 | tf_op jit(solution)/shard_map/ppermute | solution.py:665
  10.8 8.4 %collective-permute-start.2 = (bf16[2,72,192]{2,1,0:T(8,128)(2,1)S(1)}, bf16[2,72,192]{2,1,0:T(8,128)(2,1)S(1)}, u32[]{:S(2)}, u32[]{:S(2)}) collective-permute-start(bf16[2,72,192]{2,1,0:T(8,128)(2,1)S(1)} %get-tuple-element.44), channel_id=1, source_target_pairs={{0,15},{1,14},{2,1},{3,0},{4,3},{5,2},{6,5},{7,4},{8,7},{9,6},{10,... | collective-permute-start | bytes 165896 | tf_op jit(solution)/shard_map/ppermute | solution.py:684
  16.4 4.4 %collective-permute-start = (bf16[2,72,192]{2,1,0:T(8,128)(2,1)S(1)}, bf16[2,72,192]{2,1,0:T(8,128)(2,1)S(1)}, u32[]{:S(2)}, u32[]{:S(2)}) collective-permute-start(bf16[2,72,192]{2,1,0:T(8,128)(2,1)S(1)} %get-tuple-element.44), channel_id=1, source_target_pairs={{0,14},{2,0},{4,2},{6,4},{8,6},{10,8},{12,10},{14,12},{1,15},{3,1}... | collective-permute-start | bytes 165896 | tf_op jit(solution)/shard_map/ppermute | solution.py:670
  17.0 3.8 %copy-start = (bf16[2,192,768]{2,1,0:T(8,128)(2,1)S(1)}, bf16[2,192,768]{2,1,0:T(8,128)(2,1)}, u32[]{:S(2)}) copy-start(bf16[2,192,768]{2,1,0:T(8,128)(2,1)} %up_w.3) | copy-start | bytes 1769476
  17.0 3.8 %copy-start.1 = (bf16[2,768,192]{1,2,0:T(8,128)(2,1)S(1)}, bf16[2,768,192]{1,2,0:T(8,128)(2,1)}, u32[]{:S(2)}) copy-start(bf16[2,768,192]{1,2,0:T(8,128)(2,1)} %param.14) | copy-start | bytes 1769476
  17.0 3.8 %copy-start.2 = (bf16[2,192,576]{2,1,0:T(8,128)(2,1)S(1)}, bf16[2,192,576]{2,1,0:T(8,128)(2,1)}, u32[]{:S(2)}) copy-start(bf16[2,192,576]{2,1,0:T(8,128)(2,1)} %qkv_w.3) | copy-start | bytes 1327108
  17.0 3.8 %copy-start.4 = (bf16[2,192,192]{2,1,0:T(8,128)(2,1)S(1)}, bf16[2,192,192]{2,1,0:T(8,128)(2,1)}, u32[]{:S(2)}) copy-start(bf16[2,192,192]{2,1,0:T(8,128)(2,1)} %proj_w.3) | copy-start | bytes 442372
  17.0 3.8 %copy-start.5 = (f32[2,2,192]{2,1,0:T(2,128)S(1)}, f32[2,2,192]{2,1,0:T(2,128)}, u32[]{:S(2)}) copy-start(f32[2,2,192]{2,1,0:T(2,128)} %gains.5) | copy-start | bytes 9220
  32.4 9.6 %collective-permute-start.4 = (bf16[504,192]{1,0:T(8,128)(2,1)S(1)}, bf16[504,192]{1,0:T(8,128)(2,1)S(1)}, u32[]{:S(2)}, u32[]{:S(2)}) collective-permute-start(bf16[504,192]{1,0:T(8,128)(2,1)S(1)} %get-tuple-element.47.head), channel_id=1, source_target_pairs={{0,1},{1,0},{2,3},{3,2},{4,5},{5,4},{6,7},{7,6},{8,9},{9,8},{10,11... | collective-permute-start | bytes 580616 | tf_op jit(solution)/shard_map/ppermute | solution.py:665
  34.1 10.0 %collective-permute-start.6 = (bf16[8,27,8,128]{3,2,1,0:T(8,128)(2,1)S(1)}, bf16[8,27,8,128]{3,2,1,0:T(8,128)(2,1)S(1)}, u32[]{:S(2)}, u32[]{:S(2)}) collective-permute-start(bf16[8,27,8,128]{3,2,1,0:T(8,128)(2,1)S(1)} %get-tuple-element.67), channel_id=1, source_target_pairs={{0,1},{1,0},{2,3},{3,2},{4,5},{5,4},{6,7},{7,6},{8,9},{9,8},{10,11... | collective-permute-start | bytes 1327112 | tf_op jit(solution)/shard_map/ppermute | solution.py:665
  34.6 6.1 %collective-permute-start.5 = (bf16[72,192]{1,0:T(8,128)(2,1)S(1)}, bf16[72,192]{1,0:T(8,128)(2,1)S(1)}, u32[]{:S(2)}, u32[]{:S(2)}) collective-permute-start(bf16[72,192]{1,0:T(8,128)(2,1)S(1)} %get-tuple-element.48), channel_id=1, source_target_pairs={{0,3},{1,2},{2,5},{3,4},{4,7},{5,6},{6,9},{7,8},{8,11},{9,10},{10,... | collective-permute-start | bytes 82952 | tf_op jit(solution)/shard_map/ppermute | solution.py:684
  34.6 7.3 %collective-permute-start.3 = (bf16[72,192]{1,0:T(8,128)(2,1)S(1)}, bf16[72,192]{1,0:T(8,128)(2,1)S(1)}, u32[]{:S(2)}, u32[]{:S(2)}) collective-permute-start(bf16[72,192]{1,0:T(8,128)(2,1)S(1)} %get-tuple-element.48), channel_id=1, source_target_pairs={{0,2},{2,4},{4,6},{6,8},{8,10},{10,12},{12,14},{14,0},{1,3},{3,5},... | collective-permute-start | bytes 82952 | tf_op jit(solution)/shard_map/ppermute | solution.py:670
  44.0 15.4 %collective-permute-start.7 = (bf16[8,21,8,128]{3,2,1,0:T(8,128)(2,1)S(1)}, bf16[8,21,8,128]{3,2,1,0:T(8,128)(2,1)S(1)}, u32[]{:S(2)}, u32[]{:S(2)}) collective-permute-start(bf16[8,21,8,128]{3,2,1,0:T(8,128)(2,1)S(1)} %get-tuple-element.71), channel_id=1, source_target_pairs={{0,1},{1,0},{2,3},{3,2},{4,5},{5,4},{6,7},{7,6},{8,9},{9,8},{10,11... | collective-permute-start | bytes 1032200 | tf_op jit(solution)/shard_map/ppermute | solution.py:665
  45.0 18.8 %all-to-all-start = ((bf16[8,32,8,128]{3,2,1,0:T(8,128)(2,1)}), bf16[8,32,8,128]{3,2,1,0:T(8,128)(2,1)S(1)}, u32[]{:S(2)}, u32[]{:S(2)}) async-start(bf16[8,32,8,128]{3,2,1,0:T(8,128)(2,1)} %shard_map.117.order), calls=%async_computation | async-start | bytes 1048576 | tf_op jit(solution)/shard_map/all_to_all | solution.py:857
  48.7 2.0 %copy-start.8 = (f32[4,6,144,144]{3,2,1,0:T(8,128)S(1)}, f32[4,6,144,144]{3,2,1,0:T(8,128)}, u32[]{:S(2)}) copy-start(f32[4,6,144,144]{3,2,1,0:T(8,128)} %copy-done.7) | copy-start | bytes 5971972
  50.7 1.1 copy-start.10
  59.1 1.3 %collective-permute-start.8 = (bf16[8,7,8,128]{3,2,1,0:T(8,128)(2,1)S(1)}, bf16[8,7,8,128]{3,2,1,0:T(8,128)(2,1)S(1)}, u32[]{:S(2)}, u32[]{:S(2)}) collective-permute-start(bf16[8,7,8,128]{3,2,1,0:T(8,128)(2,1)S(1)} %get-tuple-element.73), channel_id=1, source_target_pairs={{0,1},{1,0},{2,3},{3,2},{4,5},{5,4},{6,7},{7,6},{8,9},{9,8},{10,11... | collective-permute-start | bytes 344072 | tf_op jit(solution)/shard_map/ppermute | solution.py:665
  63.9 18.7 %all-to-all-start.1 = ((bf16[8,33,8,128]{3,2,1,0:T(8,128)(2,1)}), bf16[8,33,8,128]{3,2,1,0:T(8,128)(2,1)S(1)}, u32[]{:S(2)}, u32[]{:S(2)}) async-start(bf16[8,33,8,128]{3,2,1,0:T(8,128)(2,1)} %shard_map.119.order), calls=%async_computation.1 | async-start | bytes 1081344 | tf_op jit(solution)/shard_map/all_to_all | solution.py:891
  83.4 22.7 %all-to-all-start.2 = ((bf16[8,33,8,128]{3,2,1,0:T(8,128)(2,1)}), bf16[8,33,8,128]{3,2,1,0:T(8,128)(2,1)S(1)}, u32[]{:S(2)}, u32[]{:S(2)}) async-start(bf16[8,33,8,128]{3,2,1,0:T(8,128)(2,1)} %shard_map.122), calls=%async_computation.2 | async-start | bytes 1081344 | tf_op jit(solution)/shard_map/all_to_all | solution.py:904
  87.0 19.1 %collective-permute-start.11 = (bf16[32,8,128]{2,1,0:T(8,128)(2,1)S(1)}, bf16[32,8,128]{2,1,0:T(8,128)(2,1)S(1)}, u32[]{:S(2)}, u32[]{:S(2)}) collective-permute-start(bf16[32,8,128]{2,1,0:T(8,128)(2,1)S(1)} %shard_map.120.refs_0_.order), channel_id=1, source_target_pairs={{0,12},{2,14},{4,0},{6,2},{8,4},{10,6},{12,8},{14,10},{1,13},{3,15... | collective-permute-start | bytes 196616 | tf_op jit(solution)/shard_map/ppermute | solution.py:670
  90.9 16.8 %collective-permute-start.10 = (bf16[32,8,128]{2,1,0:T(8,128)(2,1)S(1)}, bf16[32,8,128]{2,1,0:T(8,128)(2,1)S(1)}, u32[]{:S(2)}, u32[]{:S(2)}) collective-permute-start(bf16[32,8,128]{2,1,0:T(8,128)(2,1)S(1)} %shard_map.120.refs_0_.order), channel_id=1, source_target_pairs={{0,8},{2,10},{4,12},{6,14},{8,0},{10,2},{12,4},{14,6},{1,9},{3,11}... | collective-permute-start | bytes 196616 | tf_op jit(solution)/shard_map/ppermute | solution.py:670
  90.9 16.8 %collective-permute-start.9 = (bf16[32,8,128]{2,1,0:T(8,128)(2,1)S(1)}, bf16[32,8,128]{2,1,0:T(8,128)(2,1)S(1)}, u32[]{:S(2)}, u32[]{:S(2)}) collective-permute-start(bf16[32,8,128]{2,1,0:T(8,128)(2,1)S(1)} %shard_map.120.refs_0_.order), channel_id=1, source_target_pairs={{0,4},{2,6},{4,8},{6,10},{8,12},{10,14},{12,0},{14,2},{1,5},{3,7},... | collective-permute-start | bytes 196616 | tf_op jit(solution)/shard_map/ppermute | solution.py:670
  106.1 10.4 %collective-permute-start.15 = (bf16[8,33,8,128]{3,2,1,0:T(8,128)(2,1)S(1)}, bf16[8,33,8,128]{3,2,1,0:T(8,128)(2,1)S(1)}, u32[]{:S(2)}, u32[]{:S(2)}) collective-permute-start(bf16[8,33,8,128]{3,2,1,0:T(8,128)(2,1)S(1)} %all-to-all-done.2.own_bc), channel_id=1, source_target_pairs={{0,1},{1,0},{2,3},{3,2},{4,5},{5,4},{6,7},{7,6},{8,9},{9,8},{10,11... | collective-permute-start | bytes 1622024 | tf_op jit(solution)/shard_map/ppermute | solution.py:665
  107.7 7.3 %collective-permute-start.12 = (bf16[4,32,8,128]{3,2,1,0:T(8,128)(2,1)S(1)}, bf16[4,32,8,128]{3,2,1,0:T(8,128)(2,1)S(1)}, u32[]{:S(2)}, u32[]{:S(2)}) collective-permute-start(bf16[4,32,8,128]{3,2,1,0:T(8,128)(2,1)S(1)} %shard_map.121.same), channel_id=1, source_target_pairs={{0,2},{2,0},{4,6},{6,4},{8,10},{10,8},{12,14},{14,12},{1,3},{3,1},... | collective-permute-start | bytes 786440 | tf_op jit(solution)/shard_map/ppermute | solution.py:675
  109.2 5.7 %collective-permute-start.13 = (bf16[4,32,8,128]{3,2,1,0:T(8,128)(2,1)S(1)}, bf16[4,32,8,128]{3,2,1,0:T(8,128)(2,1)S(1)}, u32[]{:S(2)}, u32[]{:S(2)}) collective-permute-start(bf16[4,32,8,128]{3,2,1,0:T(8,128)(2,1)S(1)} %shard_map.121.same), channel_id=1, source_target_pairs={{0,1},{1,0},{2,3},{3,2},{4,5},{5,4},{6,7},{7,6},{8,9},{9,8},{10,11... | collective-permute-start | bytes 786440 | tf_op jit(solution)/shard_map/ppermute | solution.py:665
  115.0 1.5 %collective-permute-start.14 = (bf16[4,32,8,128]{3,2,1,0:T(8,128)(2,1)S(1)}, bf16[4,32,8,128]{3,2,1,0:T(8,128)(2,1)S(1)}, u32[]{:S(2)}, u32[]{:S(2)}) collective-permute-start(bf16[4,32,8,128]{3,2,1,0:T(8,128)(2,1)S(1)} %collective-permute-done.12.same_x), channel_id=1, source_target_pairs={{0,1},{1,0},{2,3},{3,2},{4,5},{5,4},{6,7},{7,6},{8,9},{9,8},{10,11... | collective-permute-start | bytes 786440 | tf_op jit(solution)/shard_map/ppermute | solution.py:665

commit v8 on v7

--- a/solution.py
+++ b/solution.py
@@ -182,7 +182,7 @@
     return total
 
 
-def attend(qkv, bias, mixed, probs, stack_scr, width):
+def attend(qkv, bias, mixed, probs, stack_scr, width, finish=None):
     masks = head_masks(width, BF16)
     masks32 = head_masks(width, F32)
     scale = (width // HEADS) ** -0.5
@@ -201,12 +201,14 @@
             probs[w, h] = p
             stack_scr[part, :] = p.astype(BF16)
         mixed[rows, :] = pick_heads(dot(stack_scr[...], v), masks32).astype(BF16)
+        if finish is not None:
+            finish(w)
         return carry
 
-    lax.fori_loop(0, probs.shape[0], window, 0)
-
-
-def attend_back(qkv, probs, dmix, field, sums, low_scr, prob_scr, width):
+    lax.fori_loop(0, probs.shape[0], window, 0, unroll=True)
+
+
+def attend_back(qkv, probs, dmix, field, sums, low_scr, prob_scr, width, first=0):
     masks = head_masks(width, BF16)
     masks32 = head_masks(width, F32)
     scale = (width // HEADS) ** -0.5
@@ -220,7 +222,7 @@
         prob_grad = dot_nt(up, v)
         for h in range(HEADS):
             part = slice(h * WIN, (h + 1) * WIN)
-            p = probs[w, h]
+            p = probs[w - first, h]
             weighted = p * prob_grad[part]
             ds = weighted - p * jnp.sum(weighted, axis=-1, keepdims=True)
             sums[part, 0:WIN] += ds
@@ -235,7 +237,7 @@
         field[rows, 2 * width : 3 * width] = dv.astype(BF16)
         return carry
 
-    lax.fori_loop(0, probs.shape[0], window, 0)
+    lax.fori_loop(first, first + probs.shape[0], window, 0, unroll=True)
 
 
 def lon_major(src, scr):
@@ -299,13 +301,13 @@
     for k in range(BIAS_UNITS, lons * per):
         put_unit(k, jnp.zeros((UNIT, 128), BF16))
 
-def forward_core(x, b, refs, qkv_scr, bias_scr, mixed, probs, stack_scr):
+def forward_core(x, b, refs, qkv_scr, bias_scr, mixed, probs, stack_scr, finish=None):
     qkv_w, proj_w, gains = refs
     width = x.shape[-1]
     stand, inv = standardize(x)
     normed = (stand * gains[b, 0:1, :]).astype(BF16)
     qkv_scr[...] = dot(normed, qkv_w[b]).astype(BF16)
-    attend(qkv_scr, bias_scr, mixed, probs, stack_scr, width)
+    attend(qkv_scr, bias_scr, mixed, probs, stack_scr, width, finish)
     att = dot(mixed[...], proj_w[b]).astype(BF16)
     resid = (x + att.astype(F32)).astype(BF16).astype(F32)
     return resid, normed
@@ -315,7 +317,7 @@
     lat_total, tokens_in, cot_in, table_in, spread_in, qkv_in, proj_in, up_in, down_in, gains_in,
     x_out, tail_out, head_out, qkv_out, mixed_out, probs_out, resid_out, hidden_out, active_out,
     scr, cot_scr, tab_scr, rows_scr, wide_scr, bias_scr,
-    cot, table, spread, tokens, qkv_w, gains, proj_w, up_w, down_w, stack_scr, sems,
+    cot, table, spread, tokens, qkv_w, gains, proj_w, up_w, down_w, stack_scr, probs, sems, out_sems,
 ):
     copies = []
     for source, target in (
@@ -353,8 +355,12 @@
     for copy in copies[4:]:
         copy.wait()
 
+    def probs_copy(w):
+        return pltpu.make_async_copy(probs.at[w], probs_out.at[w], out_sems.at[w])
+
     resid, _ = forward_core(
-        x, 0, (qkv_w, proj_w, gains), qkv_out, bias_scr, mixed_out, probs_out, stack_scr
+        x, 0, (qkv_w, proj_w, gains), qkv_out, bias_scr, mixed_out, probs, stack_scr,
+        lambda w: probs_copy(w).start(),
     )
     resid_out[...] = resid.astype(BF16)
     stand, _ = standardize(resid)
@@ -366,6 +372,8 @@
     result = resid + dot_nt(active, down_w[0])
     head_out[0] = result[0:cut, :].astype(BF16)
     tail_out[0] = result[cut:, :].astype(BF16)
+    for w in range(probs.shape[0]):
+        probs_copy(w).wait()
 
 
 def bias_kernel(
@@ -505,10 +513,16 @@
 
 def third_kernel(
     head, lon_tail, lat_head, diag_tail, resid_in, slope, active, mixed,
-    proj_w, up_w, down_w, gains, order,
-    keep_out, give_out, rg_out, dmix_out, gain_out,
-    scr_own, scr_oth, m192, m768, mdown, flat_scr,
+    proj_w, up_w, down_w, gains, probs_in, qkv_in, order,
+    keep_out, give_out, rg_out, dmix_out, gain_out, probs_out, qkv_out,
+    scr_own, scr_oth, m192, m768, mdown, flat_scr, sems,
 ):
+    copies = [
+        pltpu.make_async_copy(qkv_in, qkv_out, sems.at[0]),
+        pltpu.make_async_copy(probs_in.at[0 : probs_out.shape[0]], probs_out, sems.at[1]),
+    ]
+    for copy in copies:
+        copy.start()
     rows, width = scr_own.shape
     cut = CHUNK * (WLON // 2)
     scr_own[0:cut, :] = lon_tail[...].astype(F32)
@@ -535,6 +549,8 @@
     at += flat_store(flat_scr, at, mdown, mixed.shape[1])
     flat_scr[at:, :] = jnp.zeros((flat_scr.shape[0] - at, 128), F32)
     halves(flat_scr, lax.axis_index("lat"), keep_out, give_out)
+    for copy in copies:
+        copy.wait()
 
 
 def gain_rows(one, two):
@@ -549,14 +565,19 @@
 
 
 def fourth_kernel(
-    x_in, qkv, probs, dmix, rg, gain_two, gains_late, order, qkv_w, gains,
+    x_in, qkv, probs_near, probs_in, dmix, rg, gain_two, gains_late, qkv_w, gains,
     tokens_out, keep, give, bias_out,
-    field, sums, m576, flat_scr, dx_scr, low_scr, prob_scr,
+    field, sums, m576, flat_scr, dx_scr, low_scr, prob_scr, probs, sem,
 ):
+    near = probs_near.shape[0]
+    copy = pltpu.make_async_copy(probs_in.at[near : probs_in.shape[0]], probs, sem)
+    copy.start()
     width = x_in.shape[-1]
     levels, lats, lons = tokens_out.shape[:3]
     sums[...] = jnp.zeros(sums.shape, F32)
-    attend_back(qkv, probs, dmix, field, sums, low_scr, prob_scr, width)
+    attend_back(qkv, probs_near, dmix, field, sums, low_scr, prob_scr, width)
+    copy.wait()
+    attend_back(qkv, probs, dmix, field, sums, low_scr, prob_scr, width, near)
     stand1, inv1 = standardize(x_in[...].astype(F32))
     normed = (stand1 * gains[0, 0:1, :]).astype(BF16)
     ng = dot_nt(field[...], qkv_w[0]).astype(BF16).astype(F32)
@@ -641,16 +662,19 @@
             bias_out[b, h] = tab_scr[h : h + 1, :]
 
 
-def call(kernel, outs, scratch, args, micros, mib, spaces=None, pinned=()):
+def call(kernel, outs, scratch, args, micros, mib, spaces=None, far=()):
     spaces = spaces or [pltpu.VMEM] * len(args)
     return pl.pallas_call(
         kernel,
         out_shape=[
-            pltpu.VMEM(*entry) if at in pinned else jax.ShapeDtypeStruct(*entry)
+            pltpu.HBM(*entry) if at in far else jax.ShapeDtypeStruct(*entry)
             for at, entry in enumerate(outs)
         ],
         in_specs=[pl.BlockSpec(memory_space=space) for space in spaces],
-        out_specs=[pl.BlockSpec(memory_space=pltpu.VMEM)] * len(outs),
+        out_specs=[
+            pl.BlockSpec(memory_space=pltpu.HBM if at in far else pltpu.VMEM)
+            for at in range(len(outs))
+        ],
         scratch_shapes=[
             pltpu.VMEM(*entry) if isinstance(entry, tuple) else entry for entry in scratch
         ],
@@ -757,7 +781,9 @@
             ((1,) + up_weight.shape[1:], BF16),
             ((1,) + down_turned.shape[1:], BF16),
             stack_shape,
+            probs_shape,
             pltpu.SemaphoreType.DMA((9,)),
+            pltpu.SemaphoreType.DMA((wins,)),
         ],
         [
             pltpu.with_memory_space_constraint(arg, pltpu.HBM)
@@ -769,7 +795,7 @@
         8,
         28,
         [pltpu.HBM] * 9,
-        (0, 3, 4, 5, 6, 8),
+        (5,),
     )
     lon_head = lon_send(head, -1)
     diag_head = diag_send(head, -1)
@@ -781,8 +807,6 @@
         (table, spread, hidden0),
         3,
         10,
-        None,
-        (1,),
     )
 
     (
@@ -833,7 +857,14 @@
     )
     got_a = lat_swap(give_a)
 
-    keep_b, give_b, rg0, dmix0, gain_two = call(
+    (part_a,) = call(
+        lat_sums, [units(lon_size, units_a + extra)], [], (keep_a, got_a, bias_a), 1, 10
+    )
+    pieces_a = lax.all_to_all(part_a, "lon", 0, 0)
+
+    near = wins // 2
+    probs_far = pltpu.with_memory_space_constraint(probs0, pltpu.HBM)
+    keep_b, give_b, rg0, dmix0, gain_two, probs_near, qkv_near = call(
         third_kernel,
         [
             units(lon_size, units_b),
@@ -841,20 +872,28 @@
             (token, F32),
             (token, BF16),
             ((1, width), F32),
-        ],
-        [(token, F32), (token, F32), m192, m768, mdown, flat_scr(units_b)],
+            ((near,) + probs_shape[0][1:], F32),
+            field_shape,
+        ],
+        [
+            (token, F32),
+            (token, F32),
+            m192,
+            m768,
+            mdown,
+            flat_scr(units_b),
+            pltpu.SemaphoreType.DMA((2,)),
+        ],
         (
             dhead, lon_tail, lat_dhead, diag_tail, resid0, slope0, active0, mixed0, proj_weight,
-            up_weight, down_turned, norm_gain, keep_a,
+            up_weight, down_turned, norm_gain, probs_far,
+            pltpu.with_memory_space_constraint(qkv0, pltpu.HBM), part_a,
         ),
         3,
         20,
+        [pltpu.VMEM] * 12 + [pltpu.HBM] * 2 + [pltpu.VMEM],
     )
     got_b = lat_swap(give_b)
-    (part_a,) = call(
-        lat_sums, [units(lon_size, units_a + extra)], [], (keep_a, got_a, bias_a), 1, 10
-    )
-    pieces_a = lax.all_to_all(part_a, "lon", 0, 0)
 
     tokens_grad, keep_c, give_c, bias_c = call(
         fourth_kernel,
@@ -872,12 +911,16 @@
             token_scr,
             stack_shape,
             stack_shape,
+            ((wins - near,) + probs_shape[0][1:], F32),
+            pltpu.SemaphoreType.DMA,
         ],
         (
-            x0, qkv0, probs0, dmix0, rg0, gain_two, gains1, part_a, qkv_weight, norm_gain,
+            x0, qkv_near, probs_near, probs_far, dmix0, rg0, gain_two, gains1, qkv_weight,
+            norm_gain,
         ),
-        9,
+        8,
         20,
+        [pltpu.VMEM] * 3 + [pltpu.HBM] + [pltpu.VMEM] * 6,
     )
     got_c = lat_swap(give_c)
     (part_bc,) = call(
@@ -893,15 +936,6 @@
     (sum_a,) = call(
         sum_pieces, [units(units_a + extra)], [], (pieces_a, part_bc), 1, 10
     )
-    (sum_bc,) = call(
-        sum_pieces,
-        [units(lon_size, units_b + units_c + extra)],
-        [],
-        (pieces_bc, sum_a),
-        1,
-        10,
-    )
-    whole_bc = lax.all_to_all(sum_bc, "lon", 0, 0)
     (same,) = call(
         join_z,
         [units(zs, units_a + extra)],
@@ -910,6 +944,15 @@
         1,
         10,
     )
+    (sum_bc,) = call(
+        sum_pieces,
+        [units(lon_size, units_b + units_c + extra)],
+        [],
+        (pieces_bc, same),
+        1,
+        10,
+    )
+    whole_bc = lax.all_to_all(sum_bc, "lon", 0, 0)
     same_x = x_swap(same)
     cross = lat_swap(same)
     cross_x = lat_swap(same_x)

time: 120 us -> 116 us (0.967)
  waiting for transfers between devices: 49.2 us -> 28 us
  blocking collectives: 0 us -> 18.4 us
  Pallas kernels: 39.2 us -> 35.1 us
  local copies, waits for them, and re-layouts: 4.88 us -> 7.5 us
    all_to_all x0 -> x1, blocking collectives: none -> 18.4 us  [shards(): whole_bc = lax.all_to_all(sum_bc, 'lon', 0, 0)]
    all_to_all x1 -> x0, waiting for transfers between devices: 14.1 us -> none  [shards(): whole_bc = lax.all_to_all(sum_bc, 'lon', 0, 0)]
    all_to_all x1, waiting for transfers between devices: 13.9 us -> 0.01 us  [shards(): pieces_bc = lax.all_to_all(part_bc, 'lon', 0, 0)]
    ppermute x5, waiting for transfers between devices: 4.31 us -> 16.4 us  [lon_send(): lax.ppermute(value, 'lon', [(s, (s + step) % count) for s in range(count)])]
    ppermute x2, waiting for transfers between devices: 6.04 us -> 0.01 us  [diag_send(): return lax.ppermute(value, ('lon', 'lat'), pairs)]
    pallas_call x12, Pallas kernels: 39.2 us -> 35.1 us  [call(): pl.pallas_call(kernel, out_shape=[pltpu.HBM(*entry) if at in far else jax...]
    all_to_all x1 -> x0, starting transfers between devices: 3.64 us -> none  [shards(): whole_bc = lax.all_to_all(sum_bc, 'lon', 0, 0)]
    unnamed x22 -> x36, local copies, waits for them, and re-layouts: 4.88 us -> 7.5 us
  transfers between devices with their start and end apart: 19 -> 18, of which waited for: 10 -> 7; matrix products, arithmetic and copies ran while one was open for 0% -> 0% of each run, Pallas kernels for 14% -> 13%
where the time goes in v8:
time: 116 us
  Pallas kernels  35.1 us (30%)
  waiting for transfers between devices  28 us (24%)
  starting transfers between devices  25.8 us (22%)
  blocking collectives  18.4 us (16%)
  local copies, waits for them, and re-layouts  7.5 us (6%)
    pallas_call x12, Pallas kernels, call(): pl.pallas_call(kernel, out_shape=[pltpu.HBM(*entry) if at in far else jax...  35.1 us
    all_to_all x1, blocking collectives, shards(): whole_bc = lax.all_to_all(sum_bc, 'lon', 0, 0)  18.4 us
    ppermute x5, waiting for transfers between devices, lon_send(): lax.ppermute(value, 'lon', [(s, (s + step) % count) for s in range(count)])  16.4 us
    ppermute x1, waiting for transfers between devices, x_swap(): return lax.ppermute(value, 'lon', [(s, s ^ 1) for s in range(count)])  7.86 us
    unnamed x36, local copies, waits for them, and re-layouts  7.5 us
    all_to_all x1, starting transfers between devices, shards(): pieces_a = lax.all_to_all(part_a, 'lon', 0, 0)  6.09 us
    all_to_all x1, starting transfers between devices, shards(): pieces_bc = lax.all_to_all(part_bc, 'lon', 0, 0)  6.01 us
    ppermute x2, starting transfers between devices, diag_send(): return lax.ppermute(value, ('lon', 'lat'), pairs)  5.64 us
  transfers between devices with their start and end apart: 18, of which 7 were waited for; matrix products, arithmetic and copies ran while one was open for 0% of the time, Pallas kernels for 13%

profile of v8, /device:TPU:0, one launch (start us, length us, event | category | flops | bytes accessed | tf_op | source)
XLA Modules:
  0.0 115.6 jit_solution(11230433911732376649)
XLA Ops:
  0.6 0.0 copy-start.6
  0.7 6.7 %shard_map.112 = (bf16[576,192]{1,0:T(8,128)(2,1)S(1)}, bf16[2,504,192]{2,1,0:T(8,128)(2,1)S(1)}, bf16[2,72,192]{2,1,0:T(8,128)(2,1)S(1)}, bf16[576,576]{1,0:T(8...) custom-call(bf16[2,12,24,192]{3,2,1,0:T(8,128)(2,1)} %tokens_in.1, ...), custom_call_target="tpu_custom_call" | custom-call | flops 8800000000 | bytes 100000 | tf_op jit(solution)/shard_map/pallas_call | solution.py:667
  7.4 0.9 copy-done.7
  8.3 0.9 copy-done.11
  9.1 0.7 copy-done.12
  9.9 0.7 copy-done.14
  10.6 0.5 collective-permute-start.1
  11.0 5.6 %collective-permute-start.2 = (bf16[2,72,192]{2,1,0:T(8,128)(2,1)S(1)}, bf16[2,72,192]{2,1,0:T(8,128)(2,1)S(1)}, u32[]{:S(2)}, u32[]{:S(2)}) collective-permute-start(bf16[2,72,192]{2,1,0:T(8,128)(2,1)S(1)} %get-tuple-element.44), channel_id=1, source_target_pairs={{0,15},{1,14},{2,1},{3,0},{4,3},{5,2},{6,5},{7,4},{8,7},{9,6},{10,... | collective-permute-start | bytes 165896 | tf_op jit(solution)/shard_map/ppermute | solution.py:708
  16.7 0.5 collective-permute-start
  17.2 0.0 copy-start.2
  17.2 0.0 copy-start.4
  17.2 0.0 copy-start.5
  17.2 2.2 %shard_map.113 = (f32[864,144]{1,0:T(8,128)S(1)}, bf16[576,768]{1,0:T(8,128)(2,1)S(1)}) custom-call(f32[2,6,1,6336]{3,2,1,0:T(1,128)S(1)} %bitcast.8, bf16[2,132,384]{2,1,0:T(8,128)(2,1)S(1)} %copy-done.6, f32[576,768]{1,0:T(8,128)S(1)} %get-tuple-element.45.hidden), custom_call_target="tpu_custom_call" | custom-call | flops 3300000000 | bytes 100000 | tf_op jit(solution)/shard_map/pallas_call | solution.py:667
  19.4 0.0 copy-start.9
  19.4 1.6 %collective-permute-done.lon_head = bf16[2,72,192]{2,1,0:T(8,128)(2,1)S(1)} collective-permute-done((bf16[2,72,192]{2,1,0:T(8,128)(2,1)S(1)}, bf16[2,72,192]{2,1,0:T(8,128)(2,1)S(1)}, u32[]{:S(2)}, u32[]{:S(2)}) %collective-permute-start) | collective-permute-done | bytes 55328 | tf_op jit(solution)/shard_map/ppermute | solution.py:694
  21.0 0.0 collective-permute-done.1.lat_tail
  21.1 8.9 %shard_map.114 = (bf16[504,192]{1,0:T(8,128)(2,1)S(1)}, bf16[72,192]{1,0:T(8,128)(2,1)S(1)}, bf16[576,192]{1,0:T(8,128)(2,1)S(1)}, bf16[576,576]{1,0:T(8,128)(2,...) custom-call(bf16[2,504,192]{2,1,0:T(8,128)(2,1)S(1)} %get-tuple-elem, ...), custom_call_target="tpu_custom_call" | custom-call | flops 20899999744 | bytes 100000 | tf_op jit(solution)/shard_map/pallas_call | solution.py:667
  30.0 1.6 %shard_map.115 = (bf16[8,27,8,128]{3,2,1,0:T(8,128)(2,1)S(1)}, bf16[8,27,8,128]{3,2,1,0:T(8,128)(2,1)S(1)}, bf16[8,5,8,128]{3,2,1,0:T(8,128)(2,1)S(1)}) custom-call(bf16[576,192]{1,0:T(8,128)(2,1)S(1)} %get-tuple-element.55.n1, bf16[576,576]{1,0:T(8,128)(2,1)S(1)} %get-tuple-element.56.field, bf16[576,192]{1,0:T(8,128)(2,1)S(1)} %get-tuple-element.57.mixed, ...), custom_call_target="tpu_custom_call" | custom-call | flops 3300000000 | bytes 100000 | tf_op jit(solution)/shard_map/pallas_call | solution.py:667
  31.6 0.1 collective-permute-start.6
  31.7 0.5 collective-permute-start.4
  32.2 0.0 collective-permute-start.5
  32.2 0.0 collective-permute-start.3
  32.2 1.3 %collective-permute-done.6.refs_1_ = bf16[8,27,8,128]{3,2,1,0:T(8,128)(2,1)S(1)} collective-permute-done((bf16[8,27,8,128]{3,2,1,0:T(8,128)(2,1)S(1)}, bf16[8,27,8,128]{3,2,1,0:T(8,128)(2,1)S(1)}, u32[]{:S(2)}, u32[]{:S(2)}) %collective-permute-start.6) | collective-permute-done | bytes 442400 | tf_op jit(solution)/shard_map/ppermute | solution.py:689
  33.5 0.9 shard_map.116.order
  34.4 6.1 %all-to-all-start = ((bf16[8,32,8,128]{3,2,1,0:T(8,128)(2,1)}), bf16[8,32,8,128]{3,2,1,0:T(8,128)(2,1)S(1)}, u32[]{:S(2)}, u32[]{:S(2)}) async-start(bf16[8,32,8,128]{3,2,1,0:T(8,128)(2,1)} %shard_map.116.order), calls=%async_computation | async-start | bytes 1048576 | tf_op jit(solution)/shard_map/all_to_all | solution.py:863
  40.5 1.2 %copy-done.8 = bf16[576,768]{1,0:T(8,128)(2,1)S(1)} copy-done((bf16[576,768]{1,0:T(8,128)(2,1)S(1)}, bf16[576,768]{1,0:T(8,128)(2,1)}, u32[]{:S(2)}) %copy-start.8) | copy-done | bytes 884760
  41.7 1.2 %copy-done.10 = bf16[576,768]{1,0:T(8,128)(2,1)S(1)} copy-done((bf16[576,768]{1,0:T(8,128)(2,1)S(1)}, bf16[576,768]{1,0:T(8,128)(2,1)}, u32[]{:S(2)}) %copy-start.10) | copy-done | bytes 884760
  42.8 1.0 copy-done.13
  43.8 1.0 copy-done.15
  44.7 4.3 %shard_map.117 = (bf16[8,21,8,128]{3,2,1,0:T(8,128)(2,1)S(1)}, bf16[8,21,8,128]{3,2,1,0:T(8,128)(2,1)S(1)}, f32[576,192]{1,0:T(8,128)S(1)}, bf16[576,192]{1,0:T(...) custom-call(bf16[504,192]{1,0:T(8,128)(2,1)S(1)} %get-tuple-element.47.head, ...), custom_call_target="tpu_custom_call" | custom-call | flops 3300000000 | bytes 100000 | tf_op jit(solution)/shard_map/pallas_call | solution.py:667
  49.0 0.1 collective-permute-start.7
  49.1 5.6 %shard_map.118 = (bf16[2,12,24,192]{3,2,1,0:T(8,128)(2,1)}, bf16[8,7,8,128]{3,2,1,0:T(8,128)(2,1)S(1)}, bf16[8,7,8,128]{3,2,1,0:T(8,128)(2,1)S(1)}, bf16[8,5,8,128]{3,2,1,0:T(8,128)(2,1)S(1)}) custom-call(bf16[576,192]{1,0:T(8,128)(2,1)S(1)} %copy-done.17, bf16[576,576]{1,0:T(8,128)(2,1)S(1)} %get-tuple-element.67.qkv, ...), custom_call_target="tpu_custom_call" | custom-call | flops 8800000000 | bytes 100000 | tf_op jit(solution)/shard_map/pallas_call | solution.py:667
  54.7 0.6 collective-permute-start.8
  55.3 1.0 collective-permute-done.8.refs_3_
  56.3 0.9 shard_map.119.order
  57.2 6.0 %all-to-all-start.1 = ((bf16[8,33,8,128]{3,2,1,0:T(8,128)(2,1)}), bf16[8,33,8,128]{3,2,1,0:T(8,128)(2,1)S(1)}, u32[]{:S(2)}, u32[]{:S(2)}) async-start(bf16[8,33,8,128]{3,2,1,0:T(8,128)(2,1)} %shard_map.119.order), calls=%async_computation.1 | async-start | bytes 1081344 | tf_op jit(solution)/shard_map/all_to_all | solution.py:934
  63.2 1.2 shard_map.120.refs_0_
  64.3 3.9 %collective-permute-start.11 = (bf16[32,8,128]{2,1,0:T(8,128)(2,1)S(1)}, bf16[32,8,128]{2,1,0:T(8,128)(2,1)S(1)}, u32[]{:S(2)}, u32[]{:S(2)}) collective-permute-start(bf16[32,8,128]{2,1,0:T(8,128)(2,1)S(1)} %shard_map.120.refs_0_), channel_id=1, source_target_pairs={{0,12},{2,14},{4,0},{6,2},{8,4},{10,6},{12,8},{14,10},{1,13},{3,15... | collective-permute-start | bytes 196616 | tf_op jit(solution)/shard_map/ppermute | solution.py:694
  68.2 1.1 collective-permute-start.9
  69.3 5.2 %collective-permute-done.11.refs_3_ = bf16[32,8,128]{2,1,0:T(8,128)(2,1)S(1)} collective-permute-done((bf16[32,8,128]{2,1,0:T(8,128)(2,1)S(1)}, bf16[32,8,128]{2,1,0:T(8,128)(2,1)S(1)}, u32[]{:S(2)}, u32[]{:S(2)}) %collective-permute-start.11) | collective-permute-done | bytes 65568 | tf_op jit(solution)/shard_map/ppermute | solution.py:694
  74.5 9.6 %collective-permute-done.10.refs_2_ = bf16[32,8,128]{2,1,0:T(8,128)(2,1)S(1)} collective-permute-done((bf16[32,8,128]{2,1,0:T(8,128)(2,1)S(1)}, bf16[32,8,128]{2,1,0:T(8,128)(2,1)S(1)}, u32[]{:S(2)}, u32[]{:S(2)}) %collective-permute-start.10) | collective-permute-done | bytes 65568 | tf_op jit(solution)/shard_map/ppermute | solution.py:694
  84.2 0.1 shard_map.122
  84.3 18.4 %all_to_all.15.own_bc = bf16[8,33,8,128]{3,2,1,0:T(8,128)(2,1)S(1)} all-to-all(bf16[8,33,8,128]{3,2,1,0:T(8,128)(2,1)S(1)} %shard_map.122), channel_id=1, replica_groups=mesh['grp'=2,'lon'=8,'lat'=2] {'lon'}, dimensions={0} | all-to-all | bytes 1081344 | tf_op jit(solution)/shard_map/all_to_all | solution.py:955
  102.7 0.6 collective-permute-start.12
  103.3 0.2 collective-permute-start.13
  103.5 7.9 %collective-permute-done.12.same_x = bf16[4,32,8,128]{3,2,1,0:T(8,128)(2,1)S(1)} collective-permute-done((bf16[4,32,8,128]{3,2,1,0:T(8,128)(2,1)S(1)}, bf16[4,32,8,128]{3,2,1,0:T(8,128)(2,1)S(1)}, u32[]{:S(2)}, u32[]{:S(2)}) %collective-permute-start.12) | collective-permute-done | bytes 262176 | tf_op jit(solution)/shard_map/ppermute | solution.py:699
  111.4 1.5 %collective-permute-done.14.cross_x = bf16[4,32,8,128]{3,2,1,0:T(8,128)(2,1)S(1)} collective-permute-done((bf16[4,32,8,128]{3,2,1,0:T(8,128)(2,1)S(1)}, bf16[4,32,8,128]{3,2,1,0:T(8,128)(2,1)S(1)}, u32[]{:S(2)}, u32[]{:S(2)}) %collective-permute-start.14) | collective-permute-done | bytes 262176 | tf_op jit(solution)/shard_map/ppermute | solution.py:689
  112.9 2.7 %shard_map.123 = (bf16[6918,128]{1,0:T(8,128)(2,1)}, f32[2,6,1,6336]{3,2,1,0:T(1,128)}) custom-call(bf16[2,132,384]{2,1,0:T(8,128)(2,1)S(1)} %copy-done.6, bf16[4,32,8,128]{3,2,1,0:T(8,128)(2,1)S(1)} %shard_map.121.order.same, bf16[4,32,8,128]{3,2,1,0:T(8,128)(2,1)S(1)} %collective-permute-done.12.same_x, ...), custom_call_target="tpu_custom_call" | custom-call | flops 3300000000 | bytes 100000 | tf_op jit(solution)/shard_map/pallas_call | solution.py:667
  (37 shorter events, 0.1 us)
Async XLA Ops:
  0.6 16.6 %copy-start.3 = (f32[2,1,6,6336]{3,1,2,0:T(1,128)S(1)}, f32[2,1,6,6336]{3,1,2,0:T(1,128)}, u32[]{:S(2)}) copy-start(f32[2,1,6,6336]{3,1,2,0:T(1,128)} %param.16) | copy-start | bytes 912388
  0.6 16.6 %copy-start.6 = (bf16[2,132,384]{2,1,0:T(8,128)(2,1)S(1)}, bf16[2,132,384]{2,1,0:T(8,128)(2,1)}, u32[]{:S(2)}) copy-start(bf16[2,132,384]{2,1,0:T(8,128)(2,1)} %constant.2.clone.spread_in.spread) | copy-start | bytes 608260
  7.4 0.9 copy-start.7
  8.3 0.9 copy-start.11
  9.1 0.7 copy-start.12
  9.9 0.7 copy-start.14
  10.6 8.8 %copy-start.16 = (bf16[576,192]{1,0:T(8,128)(2,1)}, bf16[576,192]{1,0:T(8,128)(2,1)S(1)}, u32[]{:S(2)}) copy-start(bf16[576,192]{1,0:T(8,128)(2,1)S(1)} %get-tuple-element.42.x_in) | copy-start | bytes 663556
  10.6 10.4 %collective-permute-start.1 = (bf16[2,504,192]{2,1,0:T(8,128)(2,1)S(1)}, bf16[2,504,192]{2,1,0:T(8,128)(2,1)S(1)}, u32[]{:S(2)}, u32[]{:S(2)}) collective-permute-start(bf16[2,504,192]{2,1,0:T(8,128)(2,1)S(1)} %get-tuple-element.43.tail), channel_id=1, source_target_pairs={{0,1},{1,0},{2,3},{3,2},{4,5},{5,4},{6,7},{7,6},{8,9},{9,8},{10,11... | collective-permute-start | bytes 1161224 | tf_op jit(solution)/shard_map/ppermute | solution.py:689
  11.0 8.4 %collective-permute-start.2 = (bf16[2,72,192]{2,1,0:T(8,128)(2,1)S(1)}, bf16[2,72,192]{2,1,0:T(8,128)(2,1)S(1)}, u32[]{:S(2)}, u32[]{:S(2)}) collective-permute-start(bf16[2,72,192]{2,1,0:T(8,128)(2,1)S(1)} %get-tuple-element.44), channel_id=1, source_target_pairs={{0,15},{1,14},{2,1},{3,0},{4,3},{5,2},{6,5},{7,4},{8,7},{9,6},{10,... | collective-permute-start | bytes 165896 | tf_op jit(solution)/shard_map/ppermute | solution.py:708
  16.7 4.4 %collective-permute-start = (bf16[2,72,192]{2,1,0:T(8,128)(2,1)S(1)}, bf16[2,72,192]{2,1,0:T(8,128)(2,1)S(1)}, u32[]{:S(2)}, u32[]{:S(2)}) collective-permute-start(bf16[2,72,192]{2,1,0:T(8,128)(2,1)S(1)} %get-tuple-element.44), channel_id=1, source_target_pairs={{0,14},{2,0},{4,2},{6,4},{8,6},{10,8},{12,10},{14,12},{1,15},{3,1}... | collective-permute-start | bytes 165896 | tf_op jit(solution)/shard_map/ppermute | solution.py:694
  17.2 3.8 %copy-start = (bf16[2,192,768]{2,1,0:T(8,128)(2,1)S(1)}, bf16[2,192,768]{2,1,0:T(8,128)(2,1)}, u32[]{:S(2)}) copy-start(bf16[2,192,768]{2,1,0:T(8,128)(2,1)} %up_w.3) | copy-start | bytes 1769476
  17.2 3.8 %copy-start.1 = (bf16[2,768,192]{1,2,0:T(8,128)(2,1)S(1)}, bf16[2,768,192]{1,2,0:T(8,128)(2,1)}, u32[]{:S(2)}) copy-start(bf16[2,768,192]{1,2,0:T(8,128)(2,1)} %param.14) | copy-start | bytes 1769476
  17.2 3.8 %copy-start.2 = (bf16[2,192,576]{2,1,0:T(8,128)(2,1)S(1)}, bf16[2,192,576]{2,1,0:T(8,128)(2,1)}, u32[]{:S(2)}) copy-start(bf16[2,192,576]{2,1,0:T(8,128)(2,1)} %qkv_w.3) | copy-start | bytes 1327108
  17.2 3.8 %copy-start.4 = (bf16[2,192,192]{2,1,0:T(8,128)(2,1)S(1)}, bf16[2,192,192]{2,1,0:T(8,128)(2,1)}, u32[]{:S(2)}) copy-start(bf16[2,192,192]{2,1,0:T(8,128)(2,1)} %proj_w.3) | copy-start | bytes 442372
  17.2 3.8 %copy-start.5 = (f32[2,2,192]{2,1,0:T(2,128)S(1)}, f32[2,2,192]{2,1,0:T(2,128)}, u32[]{:S(2)}) copy-start(f32[2,2,192]{2,1,0:T(2,128)} %gains.5) | copy-start | bytes 9220
  19.4 10.6 %copy-start.9 = (bf16[576,768]{1,0:T(8,128)(2,1)}, bf16[576,768]{1,0:T(8,128)(2,1)S(1)}, u32[]{:S(2)}) copy-start(bf16[576,768]{1,0:T(8,128)(2,1)S(1)} %get-tuple-element.50.slope) | copy-start | bytes 2654212
  31.6 1.8 %collective-permute-start.6 = (bf16[8,27,8,128]{3,2,1,0:T(8,128)(2,1)S(1)}, bf16[8,27,8,128]{3,2,1,0:T(8,128)(2,1)S(1)}, u32[]{:S(2)}, u32[]{:S(2)}) collective-permute-start(bf16[8,27,8,128]{3,2,1,0:T(8,128)(2,1)S(1)} %get-tuple-element.65), channel_id=1, source_target_pairs={{0,1},{1,0},{2,3},{3,2},{4,5},{5,4},{6,7},{7,6},{8,9},{9,8},{10,11... | collective-permute-start | bytes 1327112 | tf_op jit(solution)/shard_map/ppermute | solution.py:689
  31.7 8.8 %collective-permute-start.4 = (bf16[504,192]{1,0:T(8,128)(2,1)S(1)}, bf16[504,192]{1,0:T(8,128)(2,1)S(1)}, u32[]{:S(2)}, u32[]{:S(2)}) collective-permute-start(bf16[504,192]{1,0:T(8,128)(2,1)S(1)} %get-tuple-element.47.head), channel_id=1, source_target_pairs={{0,1},{1,0},{2,3},{3,2},{4,5},{5,4},{6,7},{7,6},{8,9},{9,8},{10,11... | collective-permute-start | bytes 580616 | tf_op jit(solution)/shard_map/ppermute | solution.py:689
  32.2 8.3 %collective-permute-start.5 = (bf16[72,192]{1,0:T(8,128)(2,1)S(1)}, bf16[72,192]{1,0:T(8,128)(2,1)S(1)}, u32[]{:S(2)}, u32[]{:S(2)}) collective-permute-start(bf16[72,192]{1,0:T(8,128)(2,1)S(1)} %get-tuple-element.48), channel_id=1, source_target_pairs={{0,3},{1,2},{2,5},{3,4},{4,7},{5,6},{6,9},{7,8},{8,11},{9,10},{10,... | collective-permute-start | bytes 82952 | tf_op jit(solution)/shard_map/ppermute | solution.py:708
  32.2 8.3 %collective-permute-start.3 = (bf16[72,192]{1,0:T(8,128)(2,1)S(1)}, bf16[72,192]{1,0:T(8,128)(2,1)S(1)}, u32[]{:S(2)}, u32[]{:S(2)}) collective-permute-start(bf16[72,192]{1,0:T(8,128)(2,1)S(1)} %get-tuple-element.48), channel_id=1, source_target_pairs={{0,2},{2,4},{4,6},{6,8},{8,10},{10,12},{12,14},{14,0},{1,3},{3,5},... | collective-permute-start | bytes 82952 | tf_op jit(solution)/shard_map/ppermute | solution.py:694
  34.4 22.8 %all-to-all-start = ((bf16[8,32,8,128]{3,2,1,0:T(8,128)(2,1)}), bf16[8,32,8,128]{3,2,1,0:T(8,128)(2,1)S(1)}, u32[]{:S(2)}, u32[]{:S(2)}) async-start(bf16[8,32,8,128]{3,2,1,0:T(8,128)(2,1)} %shard_map.116.order), calls=%async_computation | async-start | bytes 1048576 | tf_op jit(solution)/shard_map/all_to_all | solution.py:863
  40.5 1.2 %copy-start.8 = (bf16[576,768]{1,0:T(8,128)(2,1)S(1)}, bf16[576,768]{1,0:T(8,128)(2,1)}, u32[]{:S(2)}) copy-start(bf16[576,768]{1,0:T(8,128)(2,1)} %copy-done.7) | copy-start | bytes 2654212
  41.7 1.2 %copy-start.10 = (bf16[576,768]{1,0:T(8,128)(2,1)S(1)}, bf16[576,768]{1,0:T(8,128)(2,1)}, u32[]{:S(2)}) copy-start(bf16[576,768]{1,0:T(8,128)(2,1)} %copy-done.9) | copy-start | bytes 2654212
  42.8 1.0 copy-start.13
  43.8 1.0 copy-start.15
  44.7 4.4 %copy-start.17 = (bf16[576,192]{1,0:T(8,128)(2,1)S(1)}, bf16[576,192]{1,0:T(8,128)(2,1)}, u32[]{:S(2)}) copy-start(bf16[576,192]{1,0:T(8,128)(2,1)} %copy-done.16) | copy-start | bytes 663556
  49.0 7.2 %collective-permute-start.7 = (bf16[8,21,8,128]{3,2,1,0:T(8,128)(2,1)S(1)}, bf16[8,21,8,128]{3,2,1,0:T(8,128)(2,1)S(1)}, u32[]{:S(2)}, u32[]{:S(2)}) collective-permute-start(bf16[8,21,8,128]{3,2,1,0:T(8,128)(2,1)S(1)} %get-tuple-element.75), channel_id=1, source_target_pairs={{0,1},{1,0},{2,3},{3,2},{4,5},{5,4},{6,7},{7,6},{8,9},{9,8},{10,11... | collective-permute-start | bytes 1032200 | tf_op jit(solution)/shard_map/ppermute | solution.py:689
  54.7 1.5 %collective-permute-start.8 = (bf16[8,7,8,128]{3,2,1,0:T(8,128)(2,1)S(1)}, bf16[8,7,8,128]{3,2,1,0:T(8,128)(2,1)S(1)}, u32[]{:S(2)}, u32[]{:S(2)}) collective-permute-start(bf16[8,7,8,128]{3,2,1,0:T(8,128)(2,1)S(1)} %get-tuple-element.77), channel_id=1, source_target_pairs={{0,1},{1,0},{2,3},{3,2},{4,5},{5,4},{6,7},{7,6},{8,9},{9,8},{10,11... | collective-permute-start | bytes 344072 | tf_op jit(solution)/shard_map/ppermute | solution.py:689
  57.2 27.0 %all-to-all-start.1 = ((bf16[8,33,8,128]{3,2,1,0:T(8,128)(2,1)}), bf16[8,33,8,128]{3,2,1,0:T(8,128)(2,1)S(1)}, u32[]{:S(2)}, u32[]{:S(2)}) async-start(bf16[8,33,8,128]{3,2,1,0:T(8,128)(2,1)} %shard_map.119.order), calls=%async_computation.1 | async-start | bytes 1081344 | tf_op jit(solution)/shard_map/all_to_all | solution.py:934
  64.3 10.2 %collective-permute-start.11 = (bf16[32,8,128]{2,1,0:T(8,128)(2,1)S(1)}, bf16[32,8,128]{2,1,0:T(8,128)(2,1)S(1)}, u32[]{:S(2)}, u32[]{:S(2)}) collective-permute-start(bf16[32,8,128]{2,1,0:T(8,128)(2,1)S(1)} %shard_map.120.refs_0_), channel_id=1, source_target_pairs={{0,12},{2,14},{4,0},{6,2},{8,4},{10,6},{12,8},{14,10},{1,13},{3,15... | collective-permute-start | bytes 196616 | tf_op jit(solution)/shard_map/ppermute | solution.py:694
  68.2 15.9 %collective-permute-start.10 = (bf16[32,8,128]{2,1,0:T(8,128)(2,1)S(1)}, bf16[32,8,128]{2,1,0:T(8,128)(2,1)S(1)}, u32[]{:S(2)}, u32[]{:S(2)}) collective-permute-start(bf16[32,8,128]{2,1,0:T(8,128)(2,1)S(1)} %shard_map.120.refs_0_), channel_id=1, source_target_pairs={{0,8},{2,10},{4,12},{6,14},{8,0},{10,2},{12,4},{14,6},{1,9},{3,11}... | collective-permute-start | bytes 196616 | tf_op jit(solution)/shard_map/ppermute | solution.py:694
  68.2 15.9 %collective-permute-start.9 = (bf16[32,8,128]{2,1,0:T(8,128)(2,1)S(1)}, bf16[32,8,128]{2,1,0:T(8,128)(2,1)S(1)}, u32[]{:S(2)}, u32[]{:S(2)}) collective-permute-start(bf16[32,8,128]{2,1,0:T(8,128)(2,1)S(1)} %shard_map.120.refs_0_), channel_id=1, source_target_pairs={{0,4},{2,6},{4,8},{6,10},{8,12},{10,14},{12,0},{14,2},{1,5},{3,7},... | collective-permute-start | bytes 196616 | tf_op jit(solution)/shard_map/ppermute | solution.py:694
  102.7 10.3 %collective-permute-start.15 = (bf16[8,33,8,128]{3,2,1,0:T(8,128)(2,1)S(1)}, bf16[8,33,8,128]{3,2,1,0:T(8,128)(2,1)S(1)}, u32[]{:S(2)}, u32[]{:S(2)}) collective-permute-start(bf16[8,33,8,128]{3,2,1,0:T(8,128)(2,1)S(1)} %all_to_all.15.own_bc), channel_id=1, source_target_pairs={{0,1},{1,0},{2,3},{3,2},{4,5},{5,4},{6,7},{7,6},{8,9},{9,8},{10,11... | collective-permute-start | bytes 1622024 | tf_op jit(solution)/shard_map/ppermute | solution.py:689
  102.7 8.7 %collective-permute-start.12 = (bf16[4,32,8,128]{3,2,1,0:T(8,128)(2,1)S(1)}, bf16[4,32,8,128]{3,2,1,0:T(8,128)(2,1)S(1)}, u32[]{:S(2)}, u32[]{:S(2)}) collective-permute-start(bf16[4,32,8,128]{3,2,1,0:T(8,128)(2,1)S(1)} %shard_map.121.order.same), channel_id=1, source_target_pairs={{0,2},{2,0},{4,6},{6,4},{8,10},{10,8},{12,14},{14,12},{1,3},{3,1},... | collective-permute-start | bytes 786440 | tf_op jit(solution)/shard_map/ppermute | solution.py:699
  103.3 8.1 %collective-permute-start.13 = (bf16[4,32,8,128]{3,2,1,0:T(8,128)(2,1)S(1)}, bf16[4,32,8,128]{3,2,1,0:T(8,128)(2,1)S(1)}, u32[]{:S(2)}, u32[]{:S(2)}) collective-permute-start(bf16[4,32,8,128]{3,2,1,0:T(8,128)(2,1)S(1)} %shard_map.121.order.same), channel_id=1, source_target_pairs={{0,1},{1,0},{2,3},{3,2},{4,5},{5,4},{6,7},{7,6},{8,9},{9,8},{10,11... | collective-permute-start | bytes 786440 | tf_op jit(solution)/shard_map/ppermute | solution.py:689
  111.4 1.5 %collective-permute-start.14 = (bf16[4,32,8,128]{3,2,1,0:T(8,128)(2,1)S(1)}, bf16[4,32,8,128]{3,2,1,0:T(8,128)(2,1)S(1)}, u32[]{:S(2)}, u32[]{:S(2)}) collective-permute-start(bf16[4,32,8,128]{3,2,1,0:T(8,128)(2,1)S(1)} %collective-permute-done.12.same_x), channel_id=1, source_target_pairs={{0,1},{1,0},{2,3},{3,2},{4,5},{5,4},{6,7},{7,6},{8,9},{9,8},{10,11... | collective-permute-start | bytes 786440 | tf_op jit(solution)/shard_map/ppermute | solution.py:689

commit v9 on v8

--- a/solution.py
+++ b/solution.py
@@ -513,16 +513,12 @@
 
 def third_kernel(
     head, lon_tail, lat_head, diag_tail, resid_in, slope, active, mixed,
-    proj_w, up_w, down_w, gains, probs_in, qkv_in, order,
-    keep_out, give_out, rg_out, dmix_out, gain_out, probs_out, qkv_out,
-    scr_own, scr_oth, m192, m768, mdown, flat_scr, sems,
+    proj_w, up_w, down_w, gains, probs_in, order,
+    keep_out, give_out, rg_out, dmix_out, gain_out, probs_out,
+    scr_own, scr_oth, m192, m768, mdown, flat_scr, sem,
 ):
-    copies = [
-        pltpu.make_async_copy(qkv_in, qkv_out, sems.at[0]),
-        pltpu.make_async_copy(probs_in.at[0 : probs_out.shape[0]], probs_out, sems.at[1]),
-    ]
-    for copy in copies:
-        copy.start()
+    copy = pltpu.make_async_copy(probs_in.at[0 : probs_out.shape[0]], probs_out, sem)
+    copy.start()
     rows, width = scr_own.shape
     cut = CHUNK * (WLON // 2)
     scr_own[0:cut, :] = lon_tail[...].astype(F32)
@@ -549,8 +545,7 @@
     at += flat_store(flat_scr, at, mdown, mixed.shape[1])
     flat_scr[at:, :] = jnp.zeros((flat_scr.shape[0] - at, 128), F32)
     halves(flat_scr, lax.axis_index("lat"), keep_out, give_out)
-    for copy in copies:
-        copy.wait()
+    copy.wait()
 
 
 def gain_rows(one, two):
@@ -597,69 +592,88 @@
             ).astype(BF16)
 
 
-def last_kernel(
-    units_a, units_b, units_c, spread, same, same_x, cross, cross_x, own_bc, oth_bc,
-    update_out, bias_out, scr, rows_scr, wide_scr, tab_scr, a, bc,
+def place(pieces, first, last, dests, scr):
+    total = jnp.zeros((UNIT, 128), F32)
+    lons = pieces.shape[1]
+    per = last - first
+    k = 0
+    for where, room in dests:
+        for at in range(where, where + room, UNIT):
+            half, j, u = k // (per * lons), k // per % lons, k % per
+            value = pieces[half, j, first + u].astype(F32)
+            scr[at : at + UNIT, :] = value
+            total = total + value * value
+            k += 1
+    return total
+
+
+def bias_rows(piece, base, spread, out, rows_scr, wide_scr, tab_scr):
+    lat = lax.axis_index("lat")
+    extra = -(-BIAS_UNITS // piece.shape[1])
+
+    def read(at):
+        parts = []
+        for r in range(CHUNK // UNIT):
+            k = at * (CHUNK // UNIT) + r
+            parts.append(piece[lat, k // extra, base + k % extra].astype(F32))
+        return jnp.concatenate(parts, axis=0)
+
+    rest = read(2 * HEADS)
+    for h in range(HEADS):
+        rows = pl.ds(h, CHUNK, stride=8)
+        wide_scr[0, rows, :] = read(h)
+        wide_scr[1, rows, :] = read(HEADS + h)
+        wide_scr[2, rows, :] = rest if h == 0 else pltpu.roll(rest, 128 - 8 * h, axis=1)
+    low = get(wide_scr, slice(None), WIDE).astype(BF16)
+    for zj in range(LEVELS):
+        rows_scr[...] = dot_nt(low, spread[zj])
+        for zi in range(LEVELS):
+            for ai in range(WLAT):
+                at = ((zi * LEVELS + zj) * WLAT + ai) * PAIR
+                row = (zi * WLAT + ai) * 8
+                tab_scr[0:HEADS, at : at + PAIR] = rows_scr[row : row + HEADS, 0:PAIR]
+    for h in range(HEADS):
+        out[h] = tab_scr[h : h + 1, :]
+
+
+def late_kernel(
+    units_a, spread, same, same_x, cross, cross_x, flat_out, squares_out, bias_out,
+    rows_scr, wide_scr, tab_scr, a,
 ):
     lat = lax.axis_index("lat")
     x = lax.rem(lax.axis_index("lon"), 2)
-    lons = own_bc.shape[0]
-    extra = bc.shape[2] - units_b - units_c
-    for j in range(lons):
-        bc[lat, j] = own_bc[j]
-        bc[1 - lat, j] = oth_bc[j]
-    for z in range(lons // 2):
+    for z in range(same.shape[0]):
         a[lat, 2 * z + x] = same[z]
         a[lat, 2 * z + 1 - x] = same_x[z]
         a[1 - lat, 2 * z + x] = cross[z]
         a[1 - lat, 2 * z + 1 - x] = cross_x[z]
-
-    def place(pieces, first, last, dests):
-        total = jnp.zeros((UNIT, 128), F32)
-        per = last - first
-        k = 0
-        for where, room in dests:
-            for at in range(where, where + room, UNIT):
-                half, j, u = k // (per * lons), k // per % lons, k % per
-                value = pieces[half, j, first + u].astype(F32)
-                scr[at : at + UNIT, :] = value
-                total = total + value * value
-                k += 1
-        return total
-
-    total = place(a, 0, units_a, [(864, 864), (2016, 288), (3456, 1152), (5760, 1152)])
-    total = total + place(bc, 0, units_b, [(1728, 288), (2304, 1152), (4608, 1152)])
-    total = total + place(bc, units_b, units_b + units_c, [(0, 864), (6912, 8)])
+    squares_out[...] = place(a, 0, units_a, [(0, flat_out.shape[0])], flat_out)
+    bias_rows(a, units_a, spread, bias_out, rows_scr, wide_scr, tab_scr)
+
+
+def last_kernel(
+    units_b, units_c, spread, flat_a, squares, bias_late, own_bc, oth_bc, update_out, bias_out,
+    scr, rows_scr, wide_scr, tab_scr, bc,
+):
+    lat = lax.axis_index("lat")
+    for j in range(own_bc.shape[0]):
+        bc[lat, j] = own_bc[j]
+        bc[1 - lat, j] = oth_bc[j]
+    total = squares[...]
+    total = total + place(bc, 0, units_b, [(864, 288), (1152, 1152), (2304, 1152)], scr)
+    total = total + place(bc, units_b, units_b + units_c, [(0, 864), (3456, 8)], scr)
     count = update_out.shape[0]
     mean = jnp.sum(total) * (1.0 / (count * 128))
     scale = lax.rsqrt(mean + 1e-06)
-    update_out[...] = (scr[0:count, :] * scale).astype(BF16)
-
-    for b, (piece, base) in enumerate(((bc, units_b + units_c), (a, units_a))):
-
-        def read(at):
-            parts = []
-            for r in range(CHUNK // UNIT):
-                k = at * (CHUNK // UNIT) + r
-                parts.append(piece[lat, k // extra, base + k % extra].astype(F32))
-            return jnp.concatenate(parts, axis=0)
-
-        rest = read(2 * HEADS)
-        for h in range(HEADS):
-            rows = pl.ds(h, CHUNK, stride=8)
-            wide_scr[0, rows, :] = read(h)
-            wide_scr[1, rows, :] = read(HEADS + h)
-            wide_scr[2, rows, :] = rest if h == 0 else pltpu.roll(rest, 128 - 8 * h, axis=1)
-        low = get(wide_scr, slice(None), WIDE).astype(BF16)
-        for zj in range(LEVELS):
-            rows_scr[...] = dot_nt(low, spread[zj])
-            for zi in range(LEVELS):
-                for ai in range(WLAT):
-                    at = ((zi * LEVELS + zj) * WLAT + ai) * PAIR
-                    row = (zi * WLAT + ai) * 8
-                    tab_scr[0:HEADS, at : at + PAIR] = rows_scr[row : row + HEADS, 0:PAIR]
-        for h in range(HEADS):
-            bias_out[b, h] = tab_scr[h : h + 1, :]
+    early, late = (0, 1728, 2304, 4608), (864, 2016, 3456, 5760)
+    at = 0
+    for first, second, rows in zip(early, late, (864, 288, 1152, 1152)):
+        update_out[first : first + rows, :] = (scr[at : at + rows, :] * scale).astype(BF16)
+        update_out[second : second + rows, :] = (flat_a[at : at + rows, :] * scale).astype(BF16)
+        at += rows
+    update_out[6912:count, :] = (scr[at : at + count - 6912, :] * scale).astype(BF16)
+    bias_rows(bc, units_b + units_c, spread, bias_out.at[0], rows_scr, wide_scr, tab_scr)
+    bias_out[1] = bias_late[...]
 
 
 def call(kernel, outs, scratch, args, micros, mib, spaces=None, far=()):
@@ -793,7 +807,7 @@
             )
         ],
         8,
-        28,
+        16,
         [pltpu.HBM] * 9,
         (5,),
     )
@@ -841,7 +855,7 @@
             down_turned, norm_gain,
         ),
         19,
-        28,
+        16,
     )
     lon_tail = lon_send(dtail, 1)
     diag_tail = diag_send(dtail, 1)
@@ -853,7 +867,7 @@
         [m576, m192, m768, mdown, flat_scr(units_a)],
         (n1, field1, mixed1, low1, n2, hg1, active1, g1, sums1),
         3,
-        20,
+        14,
     )
     got_a = lat_swap(give_a)
 
@@ -864,7 +878,7 @@
 
     near = wins // 2
     probs_far = pltpu.with_memory_space_constraint(probs0, pltpu.HBM)
-    keep_b, give_b, rg0, dmix0, gain_two, probs_near, qkv_near = call(
+    keep_b, give_b, rg0, dmix0, gain_two, probs_near = call(
         third_kernel,
         [
             units(lon_size, units_b),
@@ -873,7 +887,6 @@
             (token, BF16),
             ((1, width), F32),
             ((near,) + probs_shape[0][1:], F32),
-            field_shape,
         ],
         [
             (token, F32),
@@ -882,16 +895,15 @@
             m768,
             mdown,
             flat_scr(units_b),
-            pltpu.SemaphoreType.DMA((2,)),
+            pltpu.SemaphoreType.DMA,
         ],
         (
             dhead, lon_tail, lat_dhead, diag_tail, resid0, slope0, active0, mixed0, proj_weight,
-            up_weight, down_turned, norm_gain, probs_far,
-            pltpu.with_memory_space_constraint(qkv0, pltpu.HBM), part_a,
+            up_weight, down_turned, norm_gain, probs_far, part_a,
         ),
         3,
-        20,
-        [pltpu.VMEM] * 12 + [pltpu.HBM] * 2 + [pltpu.VMEM],
+        14,
+        [pltpu.VMEM] * 12 + [pltpu.HBM, pltpu.VMEM],
     )
     got_b = lat_swap(give_b)
 
@@ -915,11 +927,11 @@
             pltpu.SemaphoreType.DMA,
         ],
         (
-            x0, qkv_near, probs_near, probs_far, dmix0, rg0, gain_two, gains1, qkv_weight,
+            x0, qkv0, probs_near, probs_far, dmix0, rg0, gain_two, gains1, qkv_weight,
             norm_gain,
         ),
         8,
-        20,
+        14,
         [pltpu.VMEM] * 3 + [pltpu.HBM] + [pltpu.VMEM] * 6,
     )
     got_c = lat_swap(give_c)
@@ -959,20 +971,26 @@
     oth_bc = lat_swap(whole_bc)
 
     flat_rows = (2 * block_rows * 128 + norm_gain.size) // 128
+    fold_scr = [((CHUNK * 8, PAIR), F32), wide_scr, tab_scr]
+    flat_a, squares, bias_late = call(
+        functools.partial(late_kernel, units_a),
+        [((block_rows, 128), F32), ((UNIT, 128), F32), (table.shape[1:], F32)],
+        [*fold_scr, units(2, lon_size, units_a + extra)],
+        (spread, same, same_x, cross, cross_x),
+        2,
+        14,
+    )
     update, bias_grad = call(
-        functools.partial(last_kernel, units_a, units_b, units_c),
+        functools.partial(last_kernel, units_b, units_c),
         [((flat_rows, 128), BF16), (table.shape, F32)],
         [
-            ((flat_rows + 2, 128), F32),
-            ((CHUNK * 8, PAIR), F32),
-            wide_scr,
-            tab_scr,
-            units(2, lon_size, units_a + extra),
+            ((block_rows + 8, 128), F32),
+            *fold_scr,
             units(2, lon_size, units_b + units_c + extra),
         ],
-        (spread, same, same_x, cross, cross_x, whole_bc, oth_bc),
-        3,
-        20,
+        (spread, flat_a, squares, bias_late, whole_bc, oth_bc),
+        2,
+        14,
     )
     bias_grad = jnp.swapaxes(bias_grad, 1, 2)
     return (tokens_grad, update.reshape(-1), bias_grad)

time: 116 us -> 108 us (0.931)
  blocking collectives: 18.4 us -> 0 us
  waiting for transfers between devices: 28 us -> 33.2 us
  starting transfers between devices: 25.8 us -> 30.9 us
    all_to_all x1 -> x0, blocking collectives: 18.4 us -> none  [shards(): whole_bc = lax.all_to_all(sum_bc, 'lon', 0, 0)]
    all_to_all x0 -> x1, waiting for transfers between devices: none -> 12.3 us  [shards(): whole_bc = lax.all_to_all(sum_bc, 'lon', 0, 0)]
    ppermute x1, waiting for transfers between devices: 7.86 us -> 0.01 us  [x_swap(): return lax.ppermute(value, 'lon', [(s, s ^ 1) for s in range(count)])]
    all_to_all x0 -> x1, starting transfers between devices: none -> 3.54 us  [shards(): whole_bc = lax.all_to_all(sum_bc, 'lon', 0, 0)]
    ppermute x1, starting transfers between devices: 0.63 us -> 1.92 us  [x_swap(): return lax.ppermute(value, 'lon', [(s, s ^ 1) for s in range(count)])]
    unnamed x36 -> x38, local copies, waits for them, and re-layouts: 7.5 us -> 7.54 us
    pallas_call x12 -> x13, Pallas kernels: 35.1 us -> 35.1 us  [call(): pl.pallas_call(kernel, out_shape=[pltpu.HBM(*entry) if at in far else jax...]
  transfers between devices with their start and end apart: 18 -> 19, of which waited for: 7 -> 8; matrix products, arithmetic and copies ran while one was open for 0% -> 0% of each run, Pallas kernels for 13% -> 14%
where the time goes in v9:
time: 108 us
  Pallas kernels  35.1 us (32%)
  waiting for transfers between devices  33.2 us (31%)
  starting transfers between devices  30.9 us (29%)
  local copies, waits for them, and re-layouts  7.54 us (7%)
    pallas_call x13, Pallas kernels, call(): pl.pallas_call(kernel, out_shape=[pltpu.HBM(*entry) if at in far else jax...  35.1 us
    ppermute x5, waiting for transfers between devices, lon_send(): lax.ppermute(value, 'lon', [(s, (s + step) % count) for s in range(count)])  16.4 us
    all_to_all x1, waiting for transfers between devices, shards(): whole_bc = lax.all_to_all(sum_bc, 'lon', 0, 0)  12.3 us
    unnamed x38, local copies, waits for them, and re-layouts  7.54 us
    all_to_all x1, starting transfers between devices, shards(): pieces_a = lax.all_to_all(part_a, 'lon', 0, 0)  6.09 us
    all_to_all x1, starting transfers between devices, shards(): pieces_bc = lax.all_to_all(part_bc, 'lon', 0, 0)  6.01 us
    ppermute x2, starting transfers between devices, diag_send(): return lax.ppermute(value, ('lon', 'lat'), pairs)  5.64 us
    ppermute x5, starting transfers between devices, lon_send(): lax.ppermute(value, 'lon', [(s, (s + step) % count) for s in range(count)])  5.54 us
  transfers between devices with their start and end apart: 19, of which 8 were waited for; matrix products, arithmetic and copies ran while one was open for 0% of the time, Pallas kernels for 14%

profile of v9, /device:TPU:0, one launch (start us, length us, event | category | flops | bytes accessed | tf_op | source)
XLA Modules:
  0.0 107.5 jit_solution(10279978540360497405)
XLA Ops:
  0.6 0.0 copy-start.6
  0.7 6.7 %shard_map.112 = (bf16[576,192]{1,0:T(8,128)(2,1)S(1)}, bf16[2,504,192]{2,1,0:T(8,128)(2,1)S(1)}, bf16[2,72,192]{2,1,0:T(8,128)(2,1)S(1)}, bf16[576,576]{1,0:T(8...) custom-call(bf16[2,12,24,192]{3,2,1,0:T(8,128)(2,1)} %tokens_in.1, ...), custom_call_target="tpu_custom_call" | custom-call | flops 8800000000 | bytes 100000 | tf_op jit(solution)/shard_map/pallas_call | solution.py:681
  7.3 0.9 copy-done.7
  8.3 0.7 copy-done.11
  9.0 0.7 copy-done.13
  9.7 0.9 copy-done.15
  10.6 0.5 collective-permute-start.1
  11.0 5.6 %collective-permute-start.2 = (bf16[2,72,192]{2,1,0:T(8,128)(2,1)S(1)}, bf16[2,72,192]{2,1,0:T(8,128)(2,1)S(1)}, u32[]{:S(2)}, u32[]{:S(2)}) collective-permute-start(bf16[2,72,192]{2,1,0:T(8,128)(2,1)S(1)} %get-tuple-element.47), channel_id=1, source_target_pairs={{0,15},{1,14},{2,1},{3,0},{4,3},{5,2},{6,5},{7,4},{8,7},{9,6},{10,... | collective-permute-start | bytes 165896 | tf_op jit(solution)/shard_map/ppermute | solution.py:722
  16.7 0.5 collective-permute-start
  17.2 0.0 copy-start.2
  17.2 0.0 copy-start.4
  17.3 0.0 copy-start.5
  17.3 2.2 %shard_map.113 = (f32[864,144]{1,0:T(8,128)S(1)}, bf16[576,768]{1,0:T(8,128)(2,1)S(1)}) custom-call(f32[2,6,1,6336]{3,2,1,0:T(1,128)S(1)} %bitcast.8, bf16[2,132,384]{2,1,0:T(8,128)(2,1)S(1)} %copy-done.6, f32[576,768]{1,0:T(8,128)S(1)} %get-tuple-element.48.hidden), custom_call_target="tpu_custom_call" | custom-call | flops 3300000000 | bytes 100000 | tf_op jit(solution)/shard_map/pallas_call | solution.py:681
  19.4 0.0 copy-start.9
  19.5 1.6 %collective-permute-done.lon_head = bf16[2,72,192]{2,1,0:T(8,128)(2,1)S(1)} collective-permute-done((bf16[2,72,192]{2,1,0:T(8,128)(2,1)S(1)}, bf16[2,72,192]{2,1,0:T(8,128)(2,1)S(1)}, u32[]{:S(2)}, u32[]{:S(2)}) %collective-permute-start) | collective-permute-done | bytes 55328 | tf_op jit(solution)/shard_map/ppermute | solution.py:708
  21.1 8.9 %shard_map.114 = (bf16[504,192]{1,0:T(8,128)(2,1)S(1)}, bf16[72,192]{1,0:T(8,128)(2,1)S(1)}, bf16[576,192]{1,0:T(8,128)(2,1)S(1)}, bf16[576,576]{1,0:T(8,128)(2,...) custom-call(bf16[2,504,192]{2,1,0:T(8,128)(2,1)S(1)} %get-tuple-elem, ...), custom_call_target="tpu_custom_call" | custom-call | flops 20899999744 | bytes 100000 | tf_op jit(solution)/shard_map/pallas_call | solution.py:681
  30.0 1.7 %shard_map.115 = (bf16[8,27,8,128]{3,2,1,0:T(8,128)(2,1)S(1)}, bf16[8,27,8,128]{3,2,1,0:T(8,128)(2,1)S(1)}, bf16[8,5,8,128]{3,2,1,0:T(8,128)(2,1)S(1)}) custom-call(bf16[576,192]{1,0:T(8,128)(2,1)S(1)} %get-tuple-element.57.n1, bf16[576,576]{1,0:T(8,128)(2,1)S(1)} %get-tuple-element.58.field, bf16[576,192]{1,0:T(8,128)(2,1)S(1)} %get-tuple-element.59.mixed, ...), custom_call_target="tpu_custom_call" | custom-call | flops 3300000000 | bytes 100000 | tf_op jit(solution)/shard_map/pallas_call | solution.py:681
  31.7 0.1 collective-permute-start.6
  31.7 0.5 collective-permute-start.4
  32.2 1.3 %collective-permute-done.6.refs_1_ = bf16[8,27,8,128]{3,2,1,0:T(8,128)(2,1)S(1)} collective-permute-done((bf16[8,27,8,128]{3,2,1,0:T(8,128)(2,1)S(1)}, bf16[8,27,8,128]{3,2,1,0:T(8,128)(2,1)S(1)}, u32[]{:S(2)}, u32[]{:S(2)}) %collective-permute-start.6) | collective-permute-done | bytes 442400 | tf_op jit(solution)/shard_map/ppermute | solution.py:703
  33.5 0.9 shard_map.116.order
  34.4 6.1 %all-to-all-start = ((bf16[8,32,8,128]{3,2,1,0:T(8,128)(2,1)}), bf16[8,32,8,128]{3,2,1,0:T(8,128)(2,1)S(1)}, u32[]{:S(2)}, u32[]{:S(2)}) async-start(bf16[8,32,8,128]{3,2,1,0:T(8,128)(2,1)} %shard_map.116.order), calls=%async_computation | async-start | bytes 1048576 | tf_op jit(solution)/shard_map/all_to_all | solution.py:877
  40.5 1.2 %copy-done.8 = bf16[576,768]{1,0:T(8,128)(2,1)S(1)} copy-done((bf16[576,768]{1,0:T(8,128)(2,1)S(1)}, bf16[576,768]{1,0:T(8,128)(2,1)}, u32[]{:S(2)}) %copy-start.8) | copy-done | bytes 884760
  41.7 1.2 %copy-done.10 = bf16[576,768]{1,0:T(8,128)(2,1)S(1)} copy-done((bf16[576,768]{1,0:T(8,128)(2,1)S(1)}, bf16[576,768]{1,0:T(8,128)(2,1)}, u32[]{:S(2)}) %copy-start.10) | copy-done | bytes 884760
  42.9 1.0 copy-done.12
  43.8 1.0 copy-done.14
  44.8 3.3 %shard_map.117 = (bf16[8,21,8,128]{3,2,1,0:T(8,128)(2,1)S(1)}, bf16[8,21,8,128]{3,2,1,0:T(8,128)(2,1)S(1)}, f32[576,192]{1,0:T(8,128)S(1)}, bf16[576,192]{1,0:T(...) custom-call(bf16[504,192]{1,0:T(8,128)(2,1)S(1)} %get-tuple-element.50.head, ...), custom_call_target="tpu_custom_call" | custom-call | flops 3300000000 | bytes 100000 | tf_op jit(solution)/shard_map/pallas_call | solution.py:681
  48.1 0.1 collective-permute-start.7
  48.2 5.6 %shard_map.118 = (bf16[2,12,24,192]{3,2,1,0:T(8,128)(2,1)}, bf16[8,7,8,128]{3,2,1,0:T(8,128)(2,1)S(1)}, bf16[8,7,8,128]{3,2,1,0:T(8,128)(2,1)S(1)}, bf16[8,5,8,128]{3,2,1,0:T(8,128)(2,1)S(1)}) custom-call(bf16[576,192]{1,0:T(8,128)(2,1)S(1)} %copy-done.18, bf16[576,576]{1,0:T(8,128)(2,1)S(1)} %copy-done.16, ...), custom_call_target="tpu_custom_call" | custom-call | flops 8800000000 | bytes 100000 | tf_op jit(solution)/shard_map/pallas_call | solution.py:681
  53.8 0.5 collective-permute-start.8
  54.3 1.0 collective-permute-done.8.refs_3_
  55.3 0.9 shard_map.119.order
  56.2 6.0 %all-to-all-start.1 = ((bf16[8,33,8,128]{3,2,1,0:T(8,128)(2,1)}), bf16[8,33,8,128]{3,2,1,0:T(8,128)(2,1)S(1)}, u32[]{:S(2)}, u32[]{:S(2)}) async-start(bf16[8,33,8,128]{3,2,1,0:T(8,128)(2,1)} %shard_map.119.order), calls=%async_computation.1 | async-start | bytes 1081344 | tf_op jit(solution)/shard_map/all_to_all | solution.py:946
  62.2 1.2 %shard_map.120.refs_0_ = bf16[32,8,128]{2,1,0:T(8,128)(2,1)S(1)} custom-call(bf16[8,32,8,128]{3,2,1,0:T(8,128)(2,1)S(1)} %all-to-all-done.pieces, bf16[8,33,8,128]{3,2,1,0:T(8,128)(2,1)} %shard_map.119.order), custom_call_target="tpu_custom_call" | custom-call | flops 1100000000 | bytes 100000 | tf_op jit(solution)/shard_map/pallas_call | solution.py:681
  63.4 3.9 %collective-permute-start.11 = (bf16[32,8,128]{2,1,0:T(8,128)(2,1)S(1)}, bf16[32,8,128]{2,1,0:T(8,128)(2,1)S(1)}, u32[]{:S(2)}, u32[]{:S(2)}) collective-permute-start(bf16[32,8,128]{2,1,0:T(8,128)(2,1)S(1)} %shard_map.120.refs_0_), channel_id=1, source_target_pairs={{0,12},{2,14},{4,0},{6,2},{8,4},{10,6},{12,8},{14,10},{1,13},{3,15... | collective-permute-start | bytes 196616 | tf_op jit(solution)/shard_map/ppermute | solution.py:708
  67.2 1.1 %collective-permute-start.9 = (bf16[32,8,128]{2,1,0:T(8,128)(2,1)S(1)}, bf16[32,8,128]{2,1,0:T(8,128)(2,1)S(1)}, u32[]{:S(2)}, u32[]{:S(2)}) collective-permute-start(bf16[32,8,128]{2,1,0:T(8,128)(2,1)S(1)} %shard_map.120.refs_0_), channel_id=1, source_target_pairs={{0,4},{2,6},{4,8},{6,10},{8,12},{10,14},{12,0},{14,2},{1,5},{3,7},... | collective-permute-start | bytes 196616 | tf_op jit(solution)/shard_map/ppermute | solution.py:708
  68.4 5.2 %collective-permute-done.11.refs_3_ = bf16[32,8,128]{2,1,0:T(8,128)(2,1)S(1)} collective-permute-done((bf16[32,8,128]{2,1,0:T(8,128)(2,1)S(1)}, bf16[32,8,128]{2,1,0:T(8,128)(2,1)S(1)}, u32[]{:S(2)}, u32[]{:S(2)}) %collective-permute-start.11) | collective-permute-done | bytes 65568 | tf_op jit(solution)/shard_map/ppermute | solution.py:708
  73.5 9.6 %collective-permute-done.10.refs_2_ = bf16[32,8,128]{2,1,0:T(8,128)(2,1)S(1)} collective-permute-done((bf16[32,8,128]{2,1,0:T(8,128)(2,1)S(1)}, bf16[32,8,128]{2,1,0:T(8,128)(2,1)S(1)}, u32[]{:S(2)}, u32[]{:S(2)}) %collective-permute-start.10) | collective-permute-done | bytes 65568 | tf_op jit(solution)/shard_map/ppermute | solution.py:708
  83.2 0.9 shard_map.123
  84.1 3.5 %all-to-all-start.2 = ((bf16[8,33,8,128]{3,2,1,0:T(8,128)(2,1)}), bf16[8,33,8,128]{3,2,1,0:T(8,128)(2,1)S(1)}, u32[]{:S(2)}, u32[]{:S(2)}) async-start(bf16[8,33,8,128]{3,2,1,0:T(8,128)(2,1)} %shard_map.123), calls=%async_computation.2 | async-start | bytes 1081344 | tf_op jit(solution)/shard_map/all_to_all | solution.py:967
  87.7 1.9 %collective-permute-start.12 = (bf16[4,32,8,128]{3,2,1,0:T(8,128)(2,1)S(1)}, bf16[4,32,8,128]{3,2,1,0:T(8,128)(2,1)S(1)}, u32[]{:S(2)}, u32[]{:S(2)}) collective-permute-start(bf16[4,32,8,128]{3,2,1,0:T(8,128)(2,1)S(1)} %shard_map.121.same.order), channel_id=1, source_target_pairs={{0,2},{2,0},{4,6},{6,4},{8,10},{10,8},{12,14},{14,12},{1,3},{3,1},... | collective-permute-start | bytes 786440 | tf_op jit(solution)/shard_map/ppermute | solution.py:713
  89.6 12.3 %all-to-all-done.2.own_bc = bf16[8,33,8,128]{3,2,1,0:T(8,128)(2,1)S(1)} async-done(((bf16[8,33,8,128]{3,2,1,0:T(8,128)(2,1)}), bf16[8,33,8,128]{3,2,1,0:T(8,128)(2,1)S(1)}, u32[]{:S(2)}, u32[]{:S(2)}) %all-to-all-start.2) | async-done | bytes 540704 | tf_op jit(solution)/shard_map/all_to_all | solution.py:967
  101.9 0.5 collective-permute-start.13
  102.4 0.0 collective-permute-start.14
  102.4 1.8 %collective-permute-done.13.cross = bf16[4,32,8,128]{3,2,1,0:T(8,128)(2,1)S(1)} collective-permute-done((bf16[4,32,8,128]{3,2,1,0:T(8,128)(2,1)S(1)}, bf16[4,32,8,128]{3,2,1,0:T(8,128)(2,1)S(1)}, u32[]{:S(2)}, u32[]{:S(2)}) %collective-permute-start.13) | collective-permute-done | bytes 262176 | tf_op jit(solution)/shard_map/ppermute | solution.py:703
  104.2 0.4 collective-permute-done.14.cross_x
  104.6 0.6 shard_map.122
  105.2 2.3 %shard_map.124 = (bf16[6918,128]{1,0:T(8,128)(2,1)}, f32[2,6,1,6336]{3,2,1,0:T(1,128)}) custom-call(bf16[2,132,384]{2,1,0:T(8,128)(2,1)S(1)} %copy-done.6, f32[3456,128]{1,0:T(8,128)S(1)} %get-tuple-element.80.flat_a, f32[8,128]{1,0:T(8,128)S(1)} %get-tuple-element.81.squares, f32[6,1,6336]{2,1,0:T(1,128)S(1)} %get-tuple-element.82.bias_late, ...), custom_call_target="tpu_custom_call" | custom-call | flops 2200000000 | bytes 100000 | tf_op jit(solution)/shard_map/pallas_call | solution.py:681
  (41 shorter events, 0.1 us)
Async XLA Ops:
  0.6 16.6 %copy-start.3 = (f32[2,1,6,6336]{3,1,2,0:T(1,128)S(1)}, f32[2,1,6,6336]{3,1,2,0:T(1,128)}, u32[]{:S(2)}) copy-start(f32[2,1,6,6336]{3,1,2,0:T(1,128)} %param.16) | copy-start | bytes 912388
  0.6 16.6 %copy-start.6 = (bf16[2,132,384]{2,1,0:T(8,128)(2,1)S(1)}, bf16[2,132,384]{2,1,0:T(8,128)(2,1)}, u32[]{:S(2)}) copy-start(bf16[2,132,384]{2,1,0:T(8,128)(2,1)} %constant.2.clone.spread_in.spread) | copy-start | bytes 608260
  7.3 0.9 copy-start.7
  8.3 0.7 copy-start.11
  9.0 0.7 copy-start.13
  9.7 0.9 copy-start.15
  10.6 8.8 %copy-start.17 = (bf16[576,192]{1,0:T(8,128)(2,1)}, bf16[576,192]{1,0:T(8,128)(2,1)S(1)}, u32[]{:S(2)}) copy-start(bf16[576,192]{1,0:T(8,128)(2,1)S(1)} %get-tuple-element.44.x_in) | copy-start | bytes 663556
  10.6 10.4 %collective-permute-start.1 = (bf16[2,504,192]{2,1,0:T(8,128)(2,1)S(1)}, bf16[2,504,192]{2,1,0:T(8,128)(2,1)S(1)}, u32[]{:S(2)}, u32[]{:S(2)}) collective-permute-start(bf16[2,504,192]{2,1,0:T(8,128)(2,1)S(1)} %get-tuple-element.46.tail), channel_id=1, source_target_pairs={{0,1},{1,0},{2,3},{3,2},{4,5},{5,4},{6,7},{7,6},{8,9},{9,8},{10,11... | collective-permute-start | bytes 1161224 | tf_op jit(solution)/shard_map/ppermute | solution.py:703
  11.0 8.4 %collective-permute-start.2 = (bf16[2,72,192]{2,1,0:T(8,128)(2,1)S(1)}, bf16[2,72,192]{2,1,0:T(8,128)(2,1)S(1)}, u32[]{:S(2)}, u32[]{:S(2)}) collective-permute-start(bf16[2,72,192]{2,1,0:T(8,128)(2,1)S(1)} %get-tuple-element.47), channel_id=1, source_target_pairs={{0,15},{1,14},{2,1},{3,0},{4,3},{5,2},{6,5},{7,4},{8,7},{9,6},{10,... | collective-permute-start | bytes 165896 | tf_op jit(solution)/shard_map/ppermute | solution.py:722
  16.7 4.4 %collective-permute-start = (bf16[2,72,192]{2,1,0:T(8,128)(2,1)S(1)}, bf16[2,72,192]{2,1,0:T(8,128)(2,1)S(1)}, u32[]{:S(2)}, u32[]{:S(2)}) collective-permute-start(bf16[2,72,192]{2,1,0:T(8,128)(2,1)S(1)} %get-tuple-element.47), channel_id=1, source_target_pairs={{0,14},{2,0},{4,2},{6,4},{8,6},{10,8},{12,10},{14,12},{1,15},{3,1}... | collective-permute-start | bytes 165896 | tf_op jit(solution)/shard_map/ppermute | solution.py:708
  17.2 3.8 %copy-start = (bf16[2,192,768]{2,1,0:T(8,128)(2,1)S(1)}, bf16[2,192,768]{2,1,0:T(8,128)(2,1)}, u32[]{:S(2)}) copy-start(bf16[2,192,768]{2,1,0:T(8,128)(2,1)} %up_w.3) | copy-start | bytes 1769476
  17.2 3.8 %copy-start.1 = (bf16[2,768,192]{1,2,0:T(8,128)(2,1)S(1)}, bf16[2,768,192]{1,2,0:T(8,128)(2,1)}, u32[]{:S(2)}) copy-start(bf16[2,768,192]{1,2,0:T(8,128)(2,1)} %param.14) | copy-start | bytes 1769476
  17.2 3.8 %copy-start.2 = (bf16[2,192,576]{2,1,0:T(8,128)(2,1)S(1)}, bf16[2,192,576]{2,1,0:T(8,128)(2,1)}, u32[]{:S(2)}) copy-start(bf16[2,192,576]{2,1,0:T(8,128)(2,1)} %qkv_w.3) | copy-start | bytes 1327108
  17.2 3.8 %copy-start.4 = (bf16[2,192,192]{2,1,0:T(8,128)(2,1)S(1)}, bf16[2,192,192]{2,1,0:T(8,128)(2,1)}, u32[]{:S(2)}) copy-start(bf16[2,192,192]{2,1,0:T(8,128)(2,1)} %proj_w.3) | copy-start | bytes 442372
  17.3 3.8 %copy-start.5 = (f32[2,2,192]{2,1,0:T(2,128)S(1)}, f32[2,2,192]{2,1,0:T(2,128)}, u32[]{:S(2)}) copy-start(f32[2,2,192]{2,1,0:T(2,128)} %gains.5) | copy-start | bytes 9220
  19.4 10.6 %copy-start.9 = (bf16[576,768]{1,0:T(8,128)(2,1)}, bf16[576,768]{1,0:T(8,128)(2,1)S(1)}, u32[]{:S(2)}) copy-start(bf16[576,768]{1,0:T(8,128)(2,1)S(1)} %get-tuple-element.53.slope) | copy-start | bytes 2654212
  31.7 1.8 %collective-permute-start.6 = (bf16[8,27,8,128]{3,2,1,0:T(8,128)(2,1)S(1)}, bf16[8,27,8,128]{3,2,1,0:T(8,128)(2,1)S(1)}, u32[]{:S(2)}, u32[]{:S(2)}) collective-permute-start(bf16[8,27,8,128]{3,2,1,0:T(8,128)(2,1)S(1)} %get-tuple-element.67), channel_id=1, source_target_pairs={{0,1},{1,0},{2,3},{3,2},{4,5},{5,4},{6,7},{7,6},{8,9},{9,8},{10,11... | collective-permute-start | bytes 1327112 | tf_op jit(solution)/shard_map/ppermute | solution.py:703
  31.7 8.8 %collective-permute-start.4 = (bf16[504,192]{1,0:T(8,128)(2,1)S(1)}, bf16[504,192]{1,0:T(8,128)(2,1)S(1)}, u32[]{:S(2)}, u32[]{:S(2)}) collective-permute-start(bf16[504,192]{1,0:T(8,128)(2,1)S(1)} %get-tuple-element.50.head), channel_id=1, source_target_pairs={{0,1},{1,0},{2,3},{3,2},{4,5},{5,4},{6,7},{7,6},{8,9},{9,8},{10,11... | collective-permute-start | bytes 580616 | tf_op jit(solution)/shard_map/ppermute | solution.py:703
  32.2 8.3 %collective-permute-start.5 = (bf16[72,192]{1,0:T(8,128)(2,1)S(1)}, bf16[72,192]{1,0:T(8,128)(2,1)S(1)}, u32[]{:S(2)}, u32[]{:S(2)}) collective-permute-start(bf16[72,192]{1,0:T(8,128)(2,1)S(1)} %get-tuple-element.51), channel_id=1, source_target_pairs={{0,3},{1,2},{2,5},{3,4},{4,7},{5,6},{6,9},{7,8},{8,11},{9,10},{10,... | collective-permute-start | bytes 82952 | tf_op jit(solution)/shard_map/ppermute | solution.py:722
  32.2 8.3 %collective-permute-start.3 = (bf16[72,192]{1,0:T(8,128)(2,1)S(1)}, bf16[72,192]{1,0:T(8,128)(2,1)S(1)}, u32[]{:S(2)}, u32[]{:S(2)}) collective-permute-start(bf16[72,192]{1,0:T(8,128)(2,1)S(1)} %get-tuple-element.51), channel_id=1, source_target_pairs={{0,2},{2,4},{4,6},{6,8},{8,10},{10,12},{12,14},{14,0},{1,3},{3,5},... | collective-permute-start | bytes 82952 | tf_op jit(solution)/shard_map/ppermute | solution.py:708
  34.4 21.8 %all-to-all-start = ((bf16[8,32,8,128]{3,2,1,0:T(8,128)(2,1)}), bf16[8,32,8,128]{3,2,1,0:T(8,128)(2,1)S(1)}, u32[]{:S(2)}, u32[]{:S(2)}) async-start(bf16[8,32,8,128]{3,2,1,0:T(8,128)(2,1)} %shard_map.116.order), calls=%async_computation | async-start | bytes 1048576 | tf_op jit(solution)/shard_map/all_to_all | solution.py:877
  40.5 1.2 %copy-start.8 = (bf16[576,768]{1,0:T(8,128)(2,1)S(1)}, bf16[576,768]{1,0:T(8,128)(2,1)}, u32[]{:S(2)}) copy-start(bf16[576,768]{1,0:T(8,128)(2,1)} %copy-done.7) | copy-start | bytes 2654212
  41.7 1.2 %copy-start.10 = (bf16[576,768]{1,0:T(8,128)(2,1)S(1)}, bf16[576,768]{1,0:T(8,128)(2,1)}, u32[]{:S(2)}) copy-start(bf16[576,768]{1,0:T(8,128)(2,1)} %copy-done.9) | copy-start | bytes 2654212
  42.9 1.0 copy-start.12
  43.8 1.0 copy-start.14
  44.8 3.4 %copy-start.16 = (bf16[576,576]{1,0:T(8,128)(2,1)S(1)}, bf16[576,576]{1,0:T(8,128)(2,1)}, u32[]{:S(2)}) copy-start(bf16[576,576]{1,0:T(8,128)(2,1)} %copy-done.15) | copy-start | bytes 1990660
  44.8 3.4 %copy-start.18 = (bf16[576,192]{1,0:T(8,128)(2,1)S(1)}, bf16[576,192]{1,0:T(8,128)(2,1)}, u32[]{:S(2)}) copy-start(bf16[576,192]{1,0:T(8,128)(2,1)} %copy-done.17) | copy-start | bytes 663556
  48.1 7.2 %collective-permute-start.7 = (bf16[8,21,8,128]{3,2,1,0:T(8,128)(2,1)S(1)}, bf16[8,21,8,128]{3,2,1,0:T(8,128)(2,1)S(1)}, u32[]{:S(2)}, u32[]{:S(2)}) collective-permute-start(bf16[8,21,8,128]{3,2,1,0:T(8,128)(2,1)S(1)} %get-tuple-element.76), channel_id=1, source_target_pairs={{0,1},{1,0},{2,3},{3,2},{4,5},{5,4},{6,7},{7,6},{8,9},{9,8},{10,11... | collective-permute-start | bytes 1032200 | tf_op jit(solution)/shard_map/ppermute | solution.py:703
  53.8 1.5 %collective-permute-start.8 = (bf16[8,7,8,128]{3,2,1,0:T(8,128)(2,1)S(1)}, bf16[8,7,8,128]{3,2,1,0:T(8,128)(2,1)S(1)}, u32[]{:S(2)}, u32[]{:S(2)}) collective-permute-start(bf16[8,7,8,128]{3,2,1,0:T(8,128)(2,1)S(1)} %get-tuple-element.78), channel_id=1, source_target_pairs={{0,1},{1,0},{2,3},{3,2},{4,5},{5,4},{6,7},{7,6},{8,9},{9,8},{10,11... | collective-permute-start | bytes 344072 | tf_op jit(solution)/shard_map/ppermute | solution.py:703
  56.2 27.0 %all-to-all-start.1 = ((bf16[8,33,8,128]{3,2,1,0:T(8,128)(2,1)}), bf16[8,33,8,128]{3,2,1,0:T(8,128)(2,1)S(1)}, u32[]{:S(2)}, u32[]{:S(2)}) async-start(bf16[8,33,8,128]{3,2,1,0:T(8,128)(2,1)} %shard_map.119.order), calls=%async_computation.1 | async-start | bytes 1081344 | tf_op jit(solution)/shard_map/all_to_all | solution.py:946
  63.4 10.2 %collective-permute-start.11 = (bf16[32,8,128]{2,1,0:T(8,128)(2,1)S(1)}, bf16[32,8,128]{2,1,0:T(8,128)(2,1)S(1)}, u32[]{:S(2)}, u32[]{:S(2)}) collective-permute-start(bf16[32,8,128]{2,1,0:T(8,128)(2,1)S(1)} %shard_map.120.refs_0_), channel_id=1, source_target_pairs={{0,12},{2,14},{4,0},{6,2},{8,4},{10,6},{12,8},{14,10},{1,13},{3,15... | collective-permute-start | bytes 196616 | tf_op jit(solution)/shard_map/ppermute | solution.py:708
  67.2 15.9 %collective-permute-start.10 = (bf16[32,8,128]{2,1,0:T(8,128)(2,1)S(1)}, bf16[32,8,128]{2,1,0:T(8,128)(2,1)S(1)}, u32[]{:S(2)}, u32[]{:S(2)}) collective-permute-start(bf16[32,8,128]{2,1,0:T(8,128)(2,1)S(1)} %shard_map.120.refs_0_), channel_id=1, source_target_pairs={{0,8},{2,10},{4,12},{6,14},{8,0},{10,2},{12,4},{14,6},{1,9},{3,11}... | collective-permute-start | bytes 196616 | tf_op jit(solution)/shard_map/ppermute | solution.py:708
  67.2 15.9 %collective-permute-start.9 = (bf16[32,8,128]{2,1,0:T(8,128)(2,1)S(1)}, bf16[32,8,128]{2,1,0:T(8,128)(2,1)S(1)}, u32[]{:S(2)}, u32[]{:S(2)}) collective-permute-start(bf16[32,8,128]{2,1,0:T(8,128)(2,1)S(1)} %shard_map.120.refs_0_), channel_id=1, source_target_pairs={{0,4},{2,6},{4,8},{6,10},{8,12},{10,14},{12,0},{14,2},{1,5},{3,7},... | collective-permute-start | bytes 196616 | tf_op jit(solution)/shard_map/ppermute | solution.py:708
  84.1 17.8 %all-to-all-start.2 = ((bf16[8,33,8,128]{3,2,1,0:T(8,128)(2,1)}), bf16[8,33,8,128]{3,2,1,0:T(8,128)(2,1)S(1)}, u32[]{:S(2)}, u32[]{:S(2)}) async-start(bf16[8,33,8,128]{3,2,1,0:T(8,128)(2,1)} %shard_map.123), calls=%async_computation.2 | async-start | bytes 1081344 | tf_op jit(solution)/shard_map/all_to_all | solution.py:967
  87.7 14.8 %collective-permute-start.12 = (bf16[4,32,8,128]{3,2,1,0:T(8,128)(2,1)S(1)}, bf16[4,32,8,128]{3,2,1,0:T(8,128)(2,1)S(1)}, u32[]{:S(2)}, u32[]{:S(2)}) collective-permute-start(bf16[4,32,8,128]{3,2,1,0:T(8,128)(2,1)S(1)} %shard_map.121.same.order), channel_id=1, source_target_pairs={{0,2},{2,0},{4,6},{6,4},{8,10},{10,8},{12,14},{14,12},{1,3},{3,1},... | collective-permute-start | bytes 786440 | tf_op jit(solution)/shard_map/ppermute | solution.py:713
  101.9 3.3 %collective-permute-start.15 = (bf16[8,33,8,128]{3,2,1,0:T(8,128)(2,1)S(1)}, bf16[8,33,8,128]{3,2,1,0:T(8,128)(2,1)S(1)}, u32[]{:S(2)}, u32[]{:S(2)}) collective-permute-start(bf16[8,33,8,128]{3,2,1,0:T(8,128)(2,1)S(1)} %all-to-all-done.2.own_bc), channel_id=1, source_target_pairs={{0,1},{1,0},{2,3},{3,2},{4,5},{5,4},{6,7},{7,6},{8,9},{9,8},{10,11... | collective-permute-start | bytes 1622024 | tf_op jit(solution)/shard_map/ppermute | solution.py:703
  101.9 2.3 %collective-permute-start.13 = (bf16[4,32,8,128]{3,2,1,0:T(8,128)(2,1)S(1)}, bf16[4,32,8,128]{3,2,1,0:T(8,128)(2,1)S(1)}, u32[]{:S(2)}, u32[]{:S(2)}) collective-permute-start(bf16[4,32,8,128]{3,2,1,0:T(8,128)(2,1)S(1)} %shard_map.121.same.order), channel_id=1, source_target_pairs={{0,1},{1,0},{2,3},{3,2},{4,5},{5,4},{6,7},{7,6},{8,9},{9,8},{10,11... | collective-permute-start | bytes 786440 | tf_op jit(solution)/shard_map/ppermute | solution.py:703
  102.4 2.2 %collective-permute-start.14 = (bf16[4,32,8,128]{3,2,1,0:T(8,128)(2,1)S(1)}, bf16[4,32,8,128]{3,2,1,0:T(8,128)(2,1)S(1)}, u32[]{:S(2)}, u32[]{:S(2)}) collective-permute-start(bf16[4,32,8,128]{3,2,1,0:T(8,128)(2,1)S(1)} %collective-permute-done.12.same_x), channel_id=1, source_target_pairs={{0,1},{1,0},{2,3},{3,2},{4,5},{5,4},{6,7},{7,6},{8,9},{9,8},{10,11... | collective-permute-start | bytes 786440 | tf_op jit(solution)/shard_map/ppermute | solution.py:703

commit v10 on v9

--- a/solution.py
+++ b/solution.py
@@ -208,7 +208,7 @@
     lax.fori_loop(0, probs.shape[0], window, 0, unroll=True)
 
 
-def attend_back(qkv, probs, dmix, field, sums, low_scr, prob_scr, width, first=0):
+def attend_back(qkv, probs, dmix, field, sums, low_scr, prob_scr, width, first=0, begin=None):
     masks = head_masks(width, BF16)
     masks32 = head_masks(width, F32)
     scale = (width // HEADS) ** -0.5
@@ -220,6 +220,8 @@
         v = qkv[rows, 2 * width : 3 * width]
         up = stack_heads(dmix[rows, :], masks)
         prob_grad = dot_nt(up, v)
+        if begin is not None:
+            begin(w)
         for h in range(HEADS):
             part = slice(h * WIN, (h + 1) * WIN)
             p = probs[w - first, h]
@@ -489,6 +491,26 @@
         out[:, at : at + count] = (keep[...].astype(F32) + got[...].astype(F32)).astype(BF16)
         at += count
     out[:, at:] = refs[-2][...]
+
+
+def lat_sums_split(*refs):
+    keep_out, give_out = refs[-2:]
+    x = lax.rem(lax.axis_index("lon"), 2)
+    for out, side in ((keep_out, x), (give_out, 1 - x)):
+        for z in range(out.shape[0]):
+            j = 2 * z + side
+            at = 0
+            for k in range(0, len(refs) - 3, 2):
+                keep, got = refs[k], refs[k + 1]
+                count = keep.shape[1]
+                total = keep[j].astype(F32) + got[j].astype(F32)
+                out[z, at : at + count] = total.astype(BF16)
+                at += count
+            out[z, at:] = refs[-3][j]
+
+
+def add_pair(keep, got, out):
+    out[...] = (keep[...].astype(F32) + got[...].astype(F32)).astype(BF16)
 
 
 def sum_pieces(pieces, order, out):
@@ -562,17 +584,23 @@
 def fourth_kernel(
     x_in, qkv, probs_near, probs_in, dmix, rg, gain_two, gains_late, qkv_w, gains,
     tokens_out, keep, give, bias_out,
-    field, sums, m576, flat_scr, dx_scr, low_scr, prob_scr, probs, sem,
+    field, sums, m576, flat_scr, dx_scr, low_scr, prob_scr, probs, sems,
 ):
     near = probs_near.shape[0]
-    copy = pltpu.make_async_copy(probs_in.at[near : probs_in.shape[0]], probs, sem)
-    copy.start()
+
+    def probs_copy(w):
+        return pltpu.make_async_copy(probs_in.at[w], probs.at[w - near], sems.at[w - near])
+
+    for w in range(near, probs_in.shape[0]):
+        probs_copy(w).start()
     width = x_in.shape[-1]
     levels, lats, lons = tokens_out.shape[:3]
     sums[...] = jnp.zeros(sums.shape, F32)
     attend_back(qkv, probs_near, dmix, field, sums, low_scr, prob_scr, width)
-    copy.wait()
-    attend_back(qkv, probs, dmix, field, sums, low_scr, prob_scr, width, near)
+    attend_back(
+        qkv, probs, dmix, field, sums, low_scr, prob_scr, width, near,
+        lambda w: probs_copy(w).wait(),
+    )
     stand1, inv1 = standardize(x_in[...].astype(F32))
     normed = (stand1 * gains[0, 0:1, :]).astype(BF16)
     ng = dot_nt(field[...], qkv_w[0]).astype(BF16).astype(F32)
@@ -676,12 +704,14 @@
     bias_out[1] = bias_late[...]
 
 
-def call(kernel, outs, scratch, args, micros, mib, spaces=None, far=()):
+def call(kernel, outs, scratch, args, micros, mib, spaces=None, far=(), near=()):
     spaces = spaces or [pltpu.VMEM] * len(args)
     return pl.pallas_call(
         kernel,
         out_shape=[
-            pltpu.HBM(*entry) if at in far else jax.ShapeDtypeStruct(*entry)
+            pltpu.HBM(*entry)
+            if at in far
+            else (pltpu.VMEM if at in near else jax.ShapeDtypeStruct)(*entry)
             for at, entry in enumerate(outs)
         ],
         in_specs=[pl.BlockSpec(memory_space=space) for space in spaces],
@@ -810,6 +840,7 @@
         16,
         [pltpu.HBM] * 9,
         (5,),
+        (0, 3, 4, 6, 8),
     )
     lon_head = lon_send(head, -1)
     diag_head = diag_send(head, -1)
@@ -821,6 +852,7 @@
         (table, spread, hidden0),
         3,
         10,
+        near=(1,),
     )
 
     (
@@ -876,7 +908,7 @@
     )
     pieces_a = lax.all_to_all(part_a, "lon", 0, 0)
 
-    near = wins // 2
+    near = 1
     probs_far = pltpu.with_memory_space_constraint(probs0, pltpu.HBM)
     keep_b, give_b, rg0, dmix0, gain_two, probs_near = call(
         third_kernel,
@@ -924,7 +956,7 @@
             stack_shape,
             stack_shape,
             ((wins - near,) + probs_shape[0][1:], F32),
-            pltpu.SemaphoreType.DMA,
+            pltpu.SemaphoreType.DMA((wins - near,)),
         ],
         (
             x0, qkv0, probs_near, probs_far, dmix0, rg0, gain_two, gains1, qkv_weight,
@@ -935,30 +967,37 @@
         [pltpu.VMEM] * 3 + [pltpu.HBM] + [pltpu.VMEM] * 6,
     )
     got_c = lat_swap(give_c)
-    (part_bc,) = call(
-        lat_sums,
-        [units(lon_size, units_b + units_c + extra)],
+    units_bc = units_b + units_c + extra
+    keep_x, give_x = call(
+        lat_sums_split,
+        [units(zs, units_bc)] * 2,
         [],
         (keep_b, got_b, keep_c, got_c, bias_c),
         1,
         10,
     )
-    pieces_bc = lax.all_to_all(part_bc, "lon", 0, 0)
-
-    (sum_a,) = call(
-        sum_pieces, [units(units_a + extra)], [], (pieces_a, part_bc), 1, 10
-    )
+    got_x = x_swap(give_x)
+    (sum_a,) = call(sum_pieces, [units(units_a + extra)], [], (pieces_a, keep_x), 1, 10)
+    (part_z,) = call(add_pair, [units(zs, units_bc)], [], (keep_x, got_x), 1, 10)
+    pieces_bc = lax.all_to_all(
+        part_z,
+        "lon",
+        0,
+        0,
+        axis_index_groups=[[2 * z + x for z in range(zs)] for x in range(2)],
+    )
+
     (same,) = call(
         join_z,
         [units(zs, units_a + extra)],
         [],
-        [sum_a] + [lon_send(sum_a, 2 * k) for k in range(1, zs)],
+        [sum_a] + [lon_send(sum_a, 2 * k) for k in range(1, zs)] + [part_z],
         1,
         10,
     )
     (sum_bc,) = call(
         sum_pieces,
-        [units(lon_size, units_b + units_c + extra)],
+        [units(lon_size, units_bc)],
         [],
         (pieces_bc, same),
         1,

time: 108 us -> 109 us (level)
  local copies, waits for them, and re-layouts: 7.54 us -> 5.87 us
  waiting for transfers between devices: 33.2 us -> 34.4 us
    ppermute x1 -> x2, waiting for transfers between devices: 0.01 us -> 6.99 us  [x_swap(): return lax.ppermute(value, 'lon', [(s, s ^ 1) for s in range(count)])]
    ppermute x5, waiting for transfers between devices: 16.4 us -> 10.9 us  [lon_send(): lax.ppermute(value, 'lon', [(s, (s + step) % count) for s in range(count)])]
    ppermute x1 -> x2, starting transfers between devices: 1.92 us -> 4.01 us  [x_swap(): return lax.ppermute(value, 'lon', [(s, s ^ 1) for s in range(count)])]
    unnamed x38 -> x34, local copies, waits for them, and re-layouts: 7.54 us -> 5.87 us
    all_to_all x1, starting transfers between devices: 6.01 us -> 4.81 us  [shards(): lax.all_to_all(part_z, 'lon', 0, 0, axis_index_groups=[[2 * z + x for z i...]
    pallas_call x13 -> x14, Pallas kernels: 35.1 us -> 35.9 us  [call(): pl.pallas_call(kernel, out_shape=[pltpu.HBM(*entry) if at in far else (pl...]
  transfers between devices with their start and end apart: 19 -> 20, of which waited for: 8 -> 9; matrix products, arithmetic and copies ran while one was open for 0% -> 0% of each run, Pallas kernels for 14% -> 14%
where the time goes in v10:
time: 109 us
  Pallas kernels  35.9 us (33%)
  waiting for transfers between devices  34.4 us (32%)
  starting transfers between devices  31.8 us (29%)
  local copies, waits for them, and re-layouts  5.87 us (5%)
    pallas_call x14, Pallas kernels, call(): pl.pallas_call(kernel, out_shape=[pltpu.HBM(*entry) if at in far else (pl...  35.9 us
    all_to_all x1, waiting for transfers between devices, shards(): whole_bc = lax.all_to_all(sum_bc, 'lon', 0, 0)  12.1 us
    ppermute x5, waiting for transfers between devices, lon_send(): lax.ppermute(value, 'lon', [(s, (s + step) % count) for s in range(count)])  10.9 us
    ppermute x2, waiting for transfers between devices, x_swap(): return lax.ppermute(value, 'lon', [(s, s ^ 1) for s in range(count)])  6.99 us
    all_to_all x1, starting transfers between devices, shards(): pieces_a = lax.all_to_all(part_a, 'lon', 0, 0)  6.09 us
    unnamed x34, local copies, waits for them, and re-layouts  5.87 us
    ppermute x2, starting transfers between devices, diag_send(): return lax.ppermute(value, ('lon', 'lat'), pairs)  5.64 us
    ppermute x5, starting transfers between devices, lon_send(): lax.ppermute(value, 'lon', [(s, (s + step) % count) for s in range(count)])  5.54 us
  transfers between devices with their start and end apart: 20, of which 9 were waited for; matrix products, arithmetic and copies ran while one was open for 0% of the time, Pallas kernels for 14%

profile of v10, /device:TPU:0, one launch (start us, length us, event | category | flops | bytes accessed | tf_op | source)
XLA Modules:
  0.0 108.8 jit_solution(7508696871991294216)
XLA Ops:
  0.6 0.0 copy-start.6
  0.7 6.7 %shard_map.112 = (bf16[576,192]{1,0:T(8,128)(2,1)S(1)}, bf16[2,504,192]{2,1,0:T(8,128)(2,1)S(1)}, bf16[2,72,192]{2,1,0:T(8,128)(2,1)S(1)}, bf16[576,576]{1,0:T(8...) custom-call(bf16[2,12,24,192]{3,2,1,0:T(8,128)(2,1)} %tokens_in.1, ...), custom_call_target="tpu_custom_call" | custom-call | flops 8800000000 | bytes 100000 | tf_op jit(solution)/shard_map/pallas_call | solution.py:709
  7.4 0.9 copy-done.7
  8.3 0.7 copy-done.11
  9.0 0.9 copy-done.13
  9.9 0.5 collective-permute-start.1
  10.3 5.6 %collective-permute-start.2 = (bf16[2,72,192]{2,1,0:T(8,128)(2,1)S(1)}, bf16[2,72,192]{2,1,0:T(8,128)(2,1)S(1)}, u32[]{:S(2)}, u32[]{:S(2)}) collective-permute-start(bf16[2,72,192]{2,1,0:T(8,128)(2,1)S(1)} %get-tuple-element.49), channel_id=1, source_target_pairs={{0,15},{1,14},{2,1},{3,0},{4,3},{5,2},{6,5},{7,4},{8,7},{9,6},{10,... | collective-permute-start | bytes 165896 | tf_op jit(solution)/shard_map/ppermute | solution.py:752
  16.0 0.5 collective-permute-start
  16.5 0.0 copy-start.2
  16.5 0.0 copy-start.4
  16.6 0.0 copy-start.5
  16.6 2.2 %shard_map.113 = (f32[864,144]{1,0:T(8,128)S(1)}, bf16[576,768]{1,0:T(8,128)(2,1)S(1)}) custom-call(f32[2,6,1,6336]{3,2,1,0:T(1,128)S(1)} %bitcast.8, bf16[2,132,384]{2,1,0:T(8,128)(2,1)S(1)} %copy-done.6, f32[576,768]{1,0:T(8,128)S(1)} %get-tuple-element.50.hidden), custom_call_target="tpu_custom_call" | custom-call | flops 3300000000 | bytes 100000 | tf_op jit(solution)/shard_map/pallas_call | solution.py:709
  18.8 1.6 %collective-permute-done.lon_head = bf16[2,72,192]{2,1,0:T(8,128)(2,1)S(1)} collective-permute-done((bf16[2,72,192]{2,1,0:T(8,128)(2,1)S(1)}, bf16[2,72,192]{2,1,0:T(8,128)(2,1)S(1)}, u32[]{:S(2)}, u32[]{:S(2)}) %collective-permute-start) | collective-permute-done | bytes 55328 | tf_op jit(solution)/shard_map/ppermute | solution.py:738
  20.4 8.9 %shard_map.114 = (bf16[504,192]{1,0:T(8,128)(2,1)S(1)}, bf16[72,192]{1,0:T(8,128)(2,1)S(1)}, bf16[576,192]{1,0:T(8,128)(2,1)S(1)}, bf16[576,576]{1,0:T(8,128)(2,...) custom-call(bf16[2,504,192]{2,1,0:T(8,128)(2,1)S(1)} %get-tuple-elem, ...), custom_call_target="tpu_custom_call" | custom-call | flops 20899999744 | bytes 100000 | tf_op jit(solution)/shard_map/pallas_call | solution.py:709
  29.3 1.6 %shard_map.115 = (bf16[8,27,8,128]{3,2,1,0:T(8,128)(2,1)S(1)}, bf16[8,27,8,128]{3,2,1,0:T(8,128)(2,1)S(1)}, bf16[8,5,8,128]{3,2,1,0:T(8,128)(2,1)S(1)}) custom-call(bf16[576,192]{1,0:T(8,128)(2,1)S(1)} %get-tuple-element.59.n1, bf16[576,576]{1,0:T(8,128)(2,1)S(1)} %get-tuple-element.60.field, bf16[576,192]{1,0:T(8,128)(2,1)S(1)} %get-tuple-element.61.mixed, ...), custom_call_target="tpu_custom_call" | custom-call | flops 3300000000 | bytes 100000 | tf_op jit(solution)/shard_map/pallas_call | solution.py:709
  31.0 0.1 collective-permute-start.6
  31.0 0.5 collective-permute-start.4
  31.5 1.3 %collective-permute-done.6.refs_1_ = bf16[8,27,8,128]{3,2,1,0:T(8,128)(2,1)S(1)} collective-permute-done((bf16[8,27,8,128]{3,2,1,0:T(8,128)(2,1)S(1)}, bf16[8,27,8,128]{3,2,1,0:T(8,128)(2,1)S(1)}, u32[]{:S(2)}, u32[]{:S(2)}) %collective-permute-start.6) | collective-permute-done | bytes 442400 | tf_op jit(solution)/shard_map/ppermute | solution.py:733
  32.8 0.9 shard_map.116.order
  33.7 6.1 %all-to-all-start = ((bf16[8,32,8,128]{3,2,1,0:T(8,128)(2,1)}), bf16[8,32,8,128]{3,2,1,0:T(8,128)(2,1)S(1)}, u32[]{:S(2)}, u32[]{:S(2)}) async-start(bf16[8,32,8,128]{3,2,1,0:T(8,128)(2,1)} %shard_map.116.order), calls=%async_computation | async-start | bytes 1048576 | tf_op jit(solution)/shard_map/all_to_all | solution.py:909
  39.8 1.2 %copy-done.8 = bf16[576,768]{1,0:T(8,128)(2,1)S(1)} copy-done((bf16[576,768]{1,0:T(8,128)(2,1)S(1)}, bf16[576,768]{1,0:T(8,128)(2,1)}, u32[]{:S(2)}) %copy-start.8) | copy-done | bytes 884760
  41.0 1.2 %copy-done.10 = bf16[576,768]{1,0:T(8,128)(2,1)S(1)} copy-done((bf16[576,768]{1,0:T(8,128)(2,1)S(1)}, bf16[576,768]{1,0:T(8,128)(2,1)}, u32[]{:S(2)}) %copy-start.10) | copy-done | bytes 884760
  42.2 1.0 copy-done.12
  43.1 3.3 %shard_map.117 = (bf16[8,21,8,128]{3,2,1,0:T(8,128)(2,1)S(1)}, bf16[8,21,8,128]{3,2,1,0:T(8,128)(2,1)S(1)}, f32[576,192]{1,0:T(8,128)S(1)}, bf16[576,192]{1,0:T(...) custom-call(bf16[504,192]{1,0:T(8,128)(2,1)S(1)} %get-tuple-element.52.head, ...), custom_call_target="tpu_custom_call" | custom-call | flops 3300000000 | bytes 100000 | tf_op jit(solution)/shard_map/pallas_call | solution.py:709
  46.4 0.1 collective-permute-start.7
  46.5 6.5 %shard_map.118 = (bf16[2,12,24,192]{3,2,1,0:T(8,128)(2,1)}, bf16[8,7,8,128]{3,2,1,0:T(8,128)(2,1)S(1)}, bf16[8,7,8,128]{3,2,1,0:T(8,128)(2,1)S(1)}, bf16[8,5,8,128]{3,2,1,0:T(8,128)(2,1)S(1)}) custom-call(bf16[576,192]{1,0:T(8,128)(2,1)S(1)} %copy-done.16, bf16[576,576]{1,0:T(8,128)(2,1)S(1)} %copy-done.14, ...), custom_call_target="tpu_custom_call" | custom-call | flops 8800000000 | bytes 100000 | tf_op jit(solution)/shard_map/pallas_call | solution.py:709
  53.1 0.6 collective-permute-start.8
  53.6 1.0 collective-permute-done.8.refs_3_
  54.6 0.1 shard_map.119
  54.7 2.1 %collective-permute-start.12 = (bf16[4,33,8,128]{3,2,1,0:T(8,128)(2,1)S(1)}, bf16[4,33,8,128]{3,2,1,0:T(8,128)(2,1)S(1)}, u32[]{:S(2)}, u32[]{:S(2)}) collective-permute-start(bf16[4,33,8,128]{3,2,1,0:T(8,128)(2,1)S(1)} %get-tuple-element.83), channel_id=1, source_target_pairs={{0,2},{2,0},{4,6},{6,4},{8,10},{10,8},{12,14},{14,12},{1,3},{3,1},... | collective-permute-start | bytes 811016 | tf_op jit(solution)/shard_map/ppermute | solution.py:743
  56.8 7.0 %collective-permute-done.12.got = bf16[4,33,8,128]{3,2,1,0:T(8,128)(2,1)S(1)} collective-permute-done((bf16[4,33,8,128]{3,2,1,0:T(8,128)(2,1)S(1)}, bf16[4,33,8,128]{3,2,1,0:T(8,128)(2,1)S(1)}, u32[]{:S(2)}, u32[]{:S(2)}) %collective-permute-start.12) | collective-permute-done | bytes 270368 | tf_op jit(solution)/shard_map/ppermute | solution.py:743
  63.8 0.8 shard_map.121.refs_4_
  64.6 4.8 %all-to-all-start.1 = ((bf16[4,33,8,128]{3,2,1,0:T(8,128)(2,1)}), bf16[4,33,8,128]{3,2,1,0:T(8,128)(2,1)S(1)}, u32[]{:S(2)}, u32[]{:S(2)}) async-start(bf16[4,33,8,128]{3,2,1,0:T(8,128)(2,1)} %shard_map.121.refs_4_), calls=%async_computation.1 | async-start | bytes 540672 | tf_op jit(solution)/shard_map/all_to_all | solution.py:982
  69.4 0.1 shard_map.120.refs_0_
  69.4 3.9 %collective-permute-start.11 = (bf16[32,8,128]{2,1,0:T(8,128)(2,1)S(1)}, bf16[32,8,128]{2,1,0:T(8,128)(2,1)S(1)}, u32[]{:S(2)}, u32[]{:S(2)}) collective-permute-start(bf16[32,8,128]{2,1,0:T(8,128)(2,1)S(1)} %shard_map.120.refs_0_), channel_id=1, source_target_pairs={{0,12},{2,14},{4,0},{6,2},{8,4},{10,6},{12,8},{14,10},{1,13},{3,15... | collective-permute-start | bytes 196616 | tf_op jit(solution)/shard_map/ppermute | solution.py:738
  73.3 1.1 %collective-permute-start.9 = (bf16[32,8,128]{2,1,0:T(8,128)(2,1)S(1)}, bf16[32,8,128]{2,1,0:T(8,128)(2,1)S(1)}, u32[]{:S(2)}, u32[]{:S(2)}) collective-permute-start(bf16[32,8,128]{2,1,0:T(8,128)(2,1)S(1)} %shard_map.120.refs_0_), channel_id=1, source_target_pairs={{0,4},{2,6},{4,8},{6,10},{8,12},{10,14},{12,0},{14,2},{1,5},{3,7},... | collective-permute-start | bytes 196616 | tf_op jit(solution)/shard_map/ppermute | solution.py:738
  74.4 2.2 %collective-permute-done.11.refs_3_ = bf16[32,8,128]{2,1,0:T(8,128)(2,1)S(1)} collective-permute-done((bf16[32,8,128]{2,1,0:T(8,128)(2,1)S(1)}, bf16[32,8,128]{2,1,0:T(8,128)(2,1)S(1)}, u32[]{:S(2)}, u32[]{:S(2)}) %collective-permute-start.11) | collective-permute-done | bytes 65568 | tf_op jit(solution)/shard_map/ppermute | solution.py:738
  76.7 7.1 %collective-permute-done.10.refs_2_ = bf16[32,8,128]{2,1,0:T(8,128)(2,1)S(1)} collective-permute-done((bf16[32,8,128]{2,1,0:T(8,128)(2,1)S(1)}, bf16[32,8,128]{2,1,0:T(8,128)(2,1)S(1)}, u32[]{:S(2)}, u32[]{:S(2)}) %collective-permute-start.10) | collective-permute-done | bytes 65568 | tf_op jit(solution)/shard_map/ppermute | solution.py:738
  83.7 1.0 shard_map.122.same.order
  84.7 0.9 shard_map.124
  85.6 3.5 %all-to-all-start.2 = ((bf16[8,33,8,128]{3,2,1,0:T(8,128)(2,1)}), bf16[8,33,8,128]{3,2,1,0:T(8,128)(2,1)S(1)}, u32[]{:S(2)}, u32[]{:S(2)}) async-start(bf16[8,33,8,128]{3,2,1,0:T(8,128)(2,1)} %shard_map.124), calls=%async_computation.2 | async-start | bytes 1081344 | tf_op jit(solution)/shard_map/all_to_all | solution.py:1006
  89.1 1.9 %collective-permute-start.13 = (bf16[4,32,8,128]{3,2,1,0:T(8,128)(2,1)S(1)}, bf16[4,32,8,128]{3,2,1,0:T(8,128)(2,1)S(1)}, u32[]{:S(2)}, u32[]{:S(2)}) collective-permute-start(bf16[4,32,8,128]{3,2,1,0:T(8,128)(2,1)S(1)} %shard_map.122.same.order), channel_id=1, source_target_pairs={{0,2},{2,0},{4,6},{6,4},{8,10},{10,8},{12,14},{14,12},{1,3},{3,1},... | collective-permute-start | bytes 786440 | tf_op jit(solution)/shard_map/ppermute | solution.py:743
  91.1 12.1 %all-to-all-done.2.own_bc = bf16[8,33,8,128]{3,2,1,0:T(8,128)(2,1)S(1)} async-done(((bf16[8,33,8,128]{3,2,1,0:T(8,128)(2,1)}), bf16[8,33,8,128]{3,2,1,0:T(8,128)(2,1)S(1)}, u32[]{:S(2)}, u32[]{:S(2)}) %all-to-all-start.2) | async-done | bytes 540704 | tf_op jit(solution)/shard_map/all_to_all | solution.py:1006
  103.1 0.5 collective-permute-start.14
  103.7 1.8 %collective-permute-done.14.cross = bf16[4,32,8,128]{3,2,1,0:T(8,128)(2,1)S(1)} collective-permute-done((bf16[4,32,8,128]{3,2,1,0:T(8,128)(2,1)S(1)}, bf16[4,32,8,128]{3,2,1,0:T(8,128)(2,1)S(1)}, u32[]{:S(2)}, u32[]{:S(2)}) %collective-permute-start.14) | collective-permute-done | bytes 262176 | tf_op jit(solution)/shard_map/ppermute | solution.py:733
  105.5 0.4 collective-permute-done.15.cross_x
  105.8 0.6 shard_map.123
  106.4 2.4 %shard_map.125 = (bf16[6918,128]{1,0:T(8,128)(2,1)}, f32[2,6,1,6336]{3,2,1,0:T(1,128)}) custom-call(bf16[2,132,384]{2,1,0:T(8,128)(2,1)S(1)} %copy-done.6, f32[3456,128]{1,0:T(8,128)S(1)} %get-tuple-element.84.flat_a, f32[8,128]{1,0:T(8,128)S(1)} %get-tuple-element.85.squares, f32[6,1,6336]{2,1,0:T(1,128)S(1)} %get-tuple-element.86.bias_late, ...), custom_call_target="tpu_custom_call" | custom-call | flops 2200000000 | bytes 100000 | tf_op jit(solution)/shard_map/pallas_call | solution.py:709
  (40 shorter events, 0.1 us)
Async XLA Ops:
  0.6 15.9 %copy-start.3 = (f32[2,1,6,6336]{3,1,2,0:T(1,128)S(1)}, f32[2,1,6,6336]{3,1,2,0:T(1,128)}, u32[]{:S(2)}) copy-start(f32[2,1,6,6336]{3,1,2,0:T(1,128)} %param.16) | copy-start | bytes 912388
  0.6 15.9 %copy-start.6 = (bf16[2,132,384]{2,1,0:T(8,128)(2,1)S(1)}, bf16[2,132,384]{2,1,0:T(8,128)(2,1)}, u32[]{:S(2)}) copy-start(bf16[2,132,384]{2,1,0:T(8,128)(2,1)} %constant.2.clone.spread_in.spread) | copy-start | bytes 608260
  7.3 0.9 copy-start.7
  8.3 0.7 copy-start.11
  9.0 0.9 copy-start.13
  9.9 8.8 %copy-start.15 = (bf16[576,192]{1,0:T(8,128)(2,1)}, bf16[576,192]{1,0:T(8,128)(2,1)S(1)}, u32[]{:S(2)}) copy-start(bf16[576,192]{1,0:T(8,128)(2,1)S(1)} %get-tuple-element.46.x_in) | copy-start | bytes 663556
  9.9 10.4 %collective-permute-start.1 = (bf16[2,504,192]{2,1,0:T(8,128)(2,1)S(1)}, bf16[2,504,192]{2,1,0:T(8,128)(2,1)S(1)}, u32[]{:S(2)}, u32[]{:S(2)}) collective-permute-start(bf16[2,504,192]{2,1,0:T(8,128)(2,1)S(1)} %get-tuple-element.48.tail), channel_id=1, source_target_pairs={{0,1},{1,0},{2,3},{3,2},{4,5},{5,4},{6,7},{7,6},{8,9},{9,8},{10,11... | collective-permute-start | bytes 1161224 | tf_op jit(solution)/shard_map/ppermute | solution.py:733
  10.3 8.4 %collective-permute-start.2 = (bf16[2,72,192]{2,1,0:T(8,128)(2,1)S(1)}, bf16[2,72,192]{2,1,0:T(8,128)(2,1)S(1)}, u32[]{:S(2)}, u32[]{:S(2)}) collective-permute-start(bf16[2,72,192]{2,1,0:T(8,128)(2,1)S(1)} %get-tuple-element.49), channel_id=1, source_target_pairs={{0,15},{1,14},{2,1},{3,0},{4,3},{5,2},{6,5},{7,4},{8,7},{9,6},{10,... | collective-permute-start | bytes 165896 | tf_op jit(solution)/shard_map/ppermute | solution.py:752
  16.0 4.4 %collective-permute-start = (bf16[2,72,192]{2,1,0:T(8,128)(2,1)S(1)}, bf16[2,72,192]{2,1,0:T(8,128)(2,1)S(1)}, u32[]{:S(2)}, u32[]{:S(2)}) collective-permute-start(bf16[2,72,192]{2,1,0:T(8,128)(2,1)S(1)} %get-tuple-element.49), channel_id=1, source_target_pairs={{0,14},{2,0},{4,2},{6,4},{8,6},{10,8},{12,10},{14,12},{1,15},{3,1}... | collective-permute-start | bytes 165896 | tf_op jit(solution)/shard_map/ppermute | solution.py:738
  16.5 3.8 %copy-start = (bf16[2,192,768]{2,1,0:T(8,128)(2,1)S(1)}, bf16[2,192,768]{2,1,0:T(8,128)(2,1)}, u32[]{:S(2)}) copy-start(bf16[2,192,768]{2,1,0:T(8,128)(2,1)} %up_w.3) | copy-start | bytes 1769476
  16.5 3.8 %copy-start.1 = (bf16[2,768,192]{1,2,0:T(8,128)(2,1)S(1)}, bf16[2,768,192]{1,2,0:T(8,128)(2,1)}, u32[]{:S(2)}) copy-start(bf16[2,768,192]{1,2,0:T(8,128)(2,1)} %param.14) | copy-start | bytes 1769476
  16.5 3.8 %copy-start.2 = (bf16[2,192,576]{2,1,0:T(8,128)(2,1)S(1)}, bf16[2,192,576]{2,1,0:T(8,128)(2,1)}, u32[]{:S(2)}) copy-start(bf16[2,192,576]{2,1,0:T(8,128)(2,1)} %qkv_w.3) | copy-start | bytes 1327108
  16.5 3.8 %copy-start.4 = (bf16[2,192,192]{2,1,0:T(8,128)(2,1)S(1)}, bf16[2,192,192]{2,1,0:T(8,128)(2,1)}, u32[]{:S(2)}) copy-start(bf16[2,192,192]{2,1,0:T(8,128)(2,1)} %proj_w.3) | copy-start | bytes 442372
  16.6 3.8 %copy-start.5 = (f32[2,2,192]{2,1,0:T(2,128)S(1)}, f32[2,2,192]{2,1,0:T(2,128)}, u32[]{:S(2)}) copy-start(f32[2,2,192]{2,1,0:T(2,128)} %gains.5) | copy-start | bytes 9220
  18.7 10.6 %copy-start.9 = (bf16[576,768]{1,0:T(8,128)(2,1)}, bf16[576,768]{1,0:T(8,128)(2,1)S(1)}, u32[]{:S(2)}) copy-start(bf16[576,768]{1,0:T(8,128)(2,1)S(1)} %get-tuple-element.55.slope) | copy-start | bytes 2654212
  31.0 1.8 %collective-permute-start.6 = (bf16[8,27,8,128]{3,2,1,0:T(8,128)(2,1)S(1)}, bf16[8,27,8,128]{3,2,1,0:T(8,128)(2,1)S(1)}, u32[]{:S(2)}, u32[]{:S(2)}) collective-permute-start(bf16[8,27,8,128]{3,2,1,0:T(8,128)(2,1)S(1)} %get-tuple-element.69), channel_id=1, source_target_pairs={{0,1},{1,0},{2,3},{3,2},{4,5},{5,4},{6,7},{7,6},{8,9},{9,8},{10,11... | collective-permute-start | bytes 1327112 | tf_op jit(solution)/shard_map/ppermute | solution.py:733
  31.0 8.8 %collective-permute-start.4 = (bf16[504,192]{1,0:T(8,128)(2,1)S(1)}, bf16[504,192]{1,0:T(8,128)(2,1)S(1)}, u32[]{:S(2)}, u32[]{:S(2)}) collective-permute-start(bf16[504,192]{1,0:T(8,128)(2,1)S(1)} %get-tuple-element.52.head), channel_id=1, source_target_pairs={{0,1},{1,0},{2,3},{3,2},{4,5},{5,4},{6,7},{7,6},{8,9},{9,8},{10,11... | collective-permute-start | bytes 580616 | tf_op jit(solution)/shard_map/ppermute | solution.py:733
  31.5 8.3 %collective-permute-start.5 = (bf16[72,192]{1,0:T(8,128)(2,1)S(1)}, bf16[72,192]{1,0:T(8,128)(2,1)S(1)}, u32[]{:S(2)}, u32[]{:S(2)}) collective-permute-start(bf16[72,192]{1,0:T(8,128)(2,1)S(1)} %get-tuple-element.53), channel_id=1, source_target_pairs={{0,3},{1,2},{2,5},{3,4},{4,7},{5,6},{6,9},{7,8},{8,11},{9,10},{10,... | collective-permute-start | bytes 82952 | tf_op jit(solution)/shard_map/ppermute | solution.py:752
  31.5 8.3 %collective-permute-start.3 = (bf16[72,192]{1,0:T(8,128)(2,1)S(1)}, bf16[72,192]{1,0:T(8,128)(2,1)S(1)}, u32[]{:S(2)}, u32[]{:S(2)}) collective-permute-start(bf16[72,192]{1,0:T(8,128)(2,1)S(1)} %get-tuple-element.53), channel_id=1, source_target_pairs={{0,2},{2,4},{4,6},{6,8},{8,10},{10,12},{12,14},{14,0},{1,3},{3,5},... | collective-permute-start | bytes 82952 | tf_op jit(solution)/shard_map/ppermute | solution.py:738
  33.7 30.9 %all-to-all-start = ((bf16[8,32,8,128]{3,2,1,0:T(8,128)(2,1)}), bf16[8,32,8,128]{3,2,1,0:T(8,128)(2,1)S(1)}, u32[]{:S(2)}, u32[]{:S(2)}) async-start(bf16[8,32,8,128]{3,2,1,0:T(8,128)(2,1)} %shard_map.116.order), calls=%async_computation | async-start | bytes 1048576 | tf_op jit(solution)/shard_map/all_to_all | solution.py:909
  39.8 1.2 %copy-start.8 = (bf16[576,768]{1,0:T(8,128)(2,1)S(1)}, bf16[576,768]{1,0:T(8,128)(2,1)}, u32[]{:S(2)}) copy-start(bf16[576,768]{1,0:T(8,128)(2,1)} %copy-done.7) | copy-start | bytes 2654212
  41.0 1.2 %copy-start.10 = (bf16[576,768]{1,0:T(8,128)(2,1)S(1)}, bf16[576,768]{1,0:T(8,128)(2,1)}, u32[]{:S(2)}) copy-start(bf16[576,768]{1,0:T(8,128)(2,1)} %copy-done.9) | copy-start | bytes 2654212
  42.2 1.0 copy-start.12
  43.1 3.4 %copy-start.14 = (bf16[576,576]{1,0:T(8,128)(2,1)S(1)}, bf16[576,576]{1,0:T(8,128)(2,1)}, u32[]{:S(2)}) copy-start(bf16[576,576]{1,0:T(8,128)(2,1)} %copy-done.13) | copy-start | bytes 1990660
  43.1 3.4 %copy-start.16 = (bf16[576,192]{1,0:T(8,128)(2,1)S(1)}, bf16[576,192]{1,0:T(8,128)(2,1)}, u32[]{:S(2)}) copy-start(bf16[576,192]{1,0:T(8,128)(2,1)} %copy-done.15) | copy-start | bytes 663556
  46.4 8.2 %collective-permute-start.7 = (bf16[8,21,8,128]{3,2,1,0:T(8,128)(2,1)S(1)}, bf16[8,21,8,128]{3,2,1,0:T(8,128)(2,1)S(1)}, u32[]{:S(2)}, u32[]{:S(2)}) collective-permute-start(bf16[8,21,8,128]{3,2,1,0:T(8,128)(2,1)S(1)} %get-tuple-element.78), channel_id=1, source_target_pairs={{0,1},{1,0},{2,3},{3,2},{4,5},{5,4},{6,7},{7,6},{8,9},{9,8},{10,11... | collective-permute-start | bytes 1032200 | tf_op jit(solution)/shard_map/ppermute | solution.py:733
  53.1 1.5 %collective-permute-start.8 = (bf16[8,7,8,128]{3,2,1,0:T(8,128)(2,1)S(1)}, bf16[8,7,8,128]{3,2,1,0:T(8,128)(2,1)S(1)}, u32[]{:S(2)}, u32[]{:S(2)}) collective-permute-start(bf16[8,7,8,128]{3,2,1,0:T(8,128)(2,1)S(1)} %get-tuple-element.80), channel_id=1, source_target_pairs={{0,1},{1,0},{2,3},{3,2},{4,5},{5,4},{6,7},{7,6},{8,9},{9,8},{10,11... | collective-permute-start | bytes 344072 | tf_op jit(solution)/shard_map/ppermute | solution.py:733
  54.7 9.1 %collective-permute-start.12 = (bf16[4,33,8,128]{3,2,1,0:T(8,128)(2,1)S(1)}, bf16[4,33,8,128]{3,2,1,0:T(8,128)(2,1)S(1)}, u32[]{:S(2)}, u32[]{:S(2)}) collective-permute-start(bf16[4,33,8,128]{3,2,1,0:T(8,128)(2,1)S(1)} %get-tuple-element.83), channel_id=1, source_target_pairs={{0,2},{2,0},{4,6},{6,4},{8,10},{10,8},{12,14},{14,12},{1,3},{3,1},... | collective-permute-start | bytes 811016 | tf_op jit(solution)/shard_map/ppermute | solution.py:743
  64.6 20.2 %all-to-all-start.1 = ((bf16[4,33,8,128]{3,2,1,0:T(8,128)(2,1)}), bf16[4,33,8,128]{3,2,1,0:T(8,128)(2,1)S(1)}, u32[]{:S(2)}, u32[]{:S(2)}) async-start(bf16[4,33,8,128]{3,2,1,0:T(8,128)(2,1)} %shard_map.121.refs_4_), calls=%async_computation.1 | async-start | bytes 540672 | tf_op jit(solution)/shard_map/all_to_all | solution.py:982
  69.4 7.2 %collective-permute-start.11 = (bf16[32,8,128]{2,1,0:T(8,128)(2,1)S(1)}, bf16[32,8,128]{2,1,0:T(8,128)(2,1)S(1)}, u32[]{:S(2)}, u32[]{:S(2)}) collective-permute-start(bf16[32,8,128]{2,1,0:T(8,128)(2,1)S(1)} %shard_map.120.refs_0_), channel_id=1, source_target_pairs={{0,12},{2,14},{4,0},{6,2},{8,4},{10,6},{12,8},{14,10},{1,13},{3,15... | collective-permute-start | bytes 196616 | tf_op jit(solution)/shard_map/ppermute | solution.py:738
  73.3 10.4 %collective-permute-start.10 = (bf16[32,8,128]{2,1,0:T(8,128)(2,1)S(1)}, bf16[32,8,128]{2,1,0:T(8,128)(2,1)S(1)}, u32[]{:S(2)}, u32[]{:S(2)}) collective-permute-start(bf16[32,8,128]{2,1,0:T(8,128)(2,1)S(1)} %shard_map.120.refs_0_), channel_id=1, source_target_pairs={{0,8},{2,10},{4,12},{6,14},{8,0},{10,2},{12,4},{14,6},{1,9},{3,11}... | collective-permute-start | bytes 196616 | tf_op jit(solution)/shard_map/ppermute | solution.py:738
  73.3 10.4 %collective-permute-start.9 = (bf16[32,8,128]{2,1,0:T(8,128)(2,1)S(1)}, bf16[32,8,128]{2,1,0:T(8,128)(2,1)S(1)}, u32[]{:S(2)}, u32[]{:S(2)}) collective-permute-start(bf16[32,8,128]{2,1,0:T(8,128)(2,1)S(1)} %shard_map.120.refs_0_), channel_id=1, source_target_pairs={{0,4},{2,6},{4,8},{6,10},{8,12},{10,14},{12,0},{14,2},{1,5},{3,7},... | collective-permute-start | bytes 196616 | tf_op jit(solution)/shard_map/ppermute | solution.py:738
  85.6 17.5 %all-to-all-start.2 = ((bf16[8,33,8,128]{3,2,1,0:T(8,128)(2,1)}), bf16[8,33,8,128]{3,2,1,0:T(8,128)(2,1)S(1)}, u32[]{:S(2)}, u32[]{:S(2)}) async-start(bf16[8,33,8,128]{3,2,1,0:T(8,128)(2,1)} %shard_map.124), calls=%async_computation.2 | async-start | bytes 1081344 | tf_op jit(solution)/shard_map/all_to_all | solution.py:1006
  89.1 14.5 %collective-permute-start.13 = (bf16[4,32,8,128]{3,2,1,0:T(8,128)(2,1)S(1)}, bf16[4,32,8,128]{3,2,1,0:T(8,128)(2,1)S(1)}, u32[]{:S(2)}, u32[]{:S(2)}) collective-permute-start(bf16[4,32,8,128]{3,2,1,0:T(8,128)(2,1)S(1)} %shard_map.122.same.order), channel_id=1, source_target_pairs={{0,2},{2,0},{4,6},{6,4},{8,10},{10,8},{12,14},{14,12},{1,3},{3,1},... | collective-permute-start | bytes 786440 | tf_op jit(solution)/shard_map/ppermute | solution.py:743
  103.1 3.3 %collective-permute-start.16 = (bf16[8,33,8,128]{3,2,1,0:T(8,128)(2,1)S(1)}, bf16[8,33,8,128]{3,2,1,0:T(8,128)(2,1)S(1)}, u32[]{:S(2)}, u32[]{:S(2)}) collective-permute-start(bf16[8,33,8,128]{3,2,1,0:T(8,128)(2,1)S(1)} %all-to-all-done.2.own_bc), channel_id=1, source_target_pairs={{0,1},{1,0},{2,3},{3,2},{4,5},{5,4},{6,7},{7,6},{8,9},{9,8},{10,11... | collective-permute-start | bytes 1622024 | tf_op jit(solution)/shard_map/ppermute | solution.py:733
  103.1 2.3 %collective-permute-start.14 = (bf16[4,32,8,128]{3,2,1,0:T(8,128)(2,1)S(1)}, bf16[4,32,8,128]{3,2,1,0:T(8,128)(2,1)S(1)}, u32[]{:S(2)}, u32[]{:S(2)}) collective-permute-start(bf16[4,32,8,128]{3,2,1,0:T(8,128)(2,1)S(1)} %shard_map.122.same.order), channel_id=1, source_target_pairs={{0,1},{1,0},{2,3},{3,2},{4,5},{5,4},{6,7},{7,6},{8,9},{9,8},{10,11... | collective-permute-start | bytes 786440 | tf_op jit(solution)/shard_map/ppermute | solution.py:733
  103.7 2.2 %collective-permute-start.15 = (bf16[4,32,8,128]{3,2,1,0:T(8,128)(2,1)S(1)}, bf16[4,32,8,128]{3,2,1,0:T(8,128)(2,1)S(1)}, u32[]{:S(2)}, u32[]{:S(2)}) collective-permute-start(bf16[4,32,8,128]{3,2,1,0:T(8,128)(2,1)S(1)} %collective-permute-done.13.same_x), channel_id=1, source_target_pairs={{0,1},{1,0},{2,3},{3,2},{4,5},{5,4},{6,7},{7,6},{8,9},{9,8},{10,11... | collective-permute-start | bytes 786440 | tf_op jit(solution)/shard_map/ppermute | solution.py:733

commit v11 on v10

--- a/solution.py
+++ b/solution.py
@@ -319,7 +319,8 @@
     lat_total, tokens_in, cot_in, table_in, spread_in, qkv_in, proj_in, up_in, down_in, gains_in,
     x_out, tail_out, head_out, qkv_out, mixed_out, probs_out, resid_out, hidden_out, active_out,
     scr, cot_scr, tab_scr, rows_scr, wide_scr, bias_scr,
-    cot, table, spread, tokens, qkv_w, gains, proj_w, up_w, down_w, stack_scr, probs, sems, out_sems,
+    cot, table, spread, tokens, qkv_w, gains, proj_w, up_w, down_w, stack_scr, probs,
+    mixed, resid_scr, active_scr, sems, out_sems,
 ):
     copies = []
     for source, target in (
@@ -361,31 +362,44 @@
         return pltpu.make_async_copy(probs.at[w], probs_out.at[w], out_sems.at[w])
 
     resid, _ = forward_core(
-        x, 0, (qkv_w, proj_w, gains), qkv_out, bias_scr, mixed_out, probs, stack_scr,
+        x, 0, (qkv_w, proj_w, gains), qkv_out, bias_scr, mixed, probs, stack_scr,
         lambda w: probs_copy(w).start(),
     )
-    resid_out[...] = resid.astype(BF16)
+    resid_scr[...] = resid.astype(BF16)
+    wins = probs.shape[0]
+    saved = [
+        pltpu.make_async_copy(source, target, out_sems.at[wins + k])
+        for k, (source, target) in enumerate(
+            ((mixed, mixed_out), (resid_scr, resid_out), (active_scr, active_out))
+        )
+    ]
+    saved[0].start()
+    saved[1].start()
     stand, _ = standardize(resid)
     normed = (stand * gains[0, 1:2, :]).astype(BF16)
     hidden = dot(normed, up_w[0])
     hidden_out[...] = hidden
     active = gelu_value(hidden).astype(BF16)
-    active_out[...] = active
+    active_scr[...] = active
+    saved[2].start()
     result = resid + dot_nt(active, down_w[0])
     head_out[0] = result[0:cut, :].astype(BF16)
     tail_out[0] = result[cut:, :].astype(BF16)
-    for w in range(probs.shape[0]):
-        probs_copy(w).wait()
+    for copy in [probs_copy(w) for w in range(wins)] + saved:
+        copy.wait()
 
 
 def bias_kernel(
-    lat_total, table, spread, hidden, bias_out, slope_out, tab_scr, rows_scr, wide_scr
+    lat_total, table, spread, hidden, bias_out, slope_out, tab_scr, rows_scr, wide_scr, slope, sem
 ):
     lat = lax.axis_index("lat")
+    slope[...] = gelu_parts(hidden[...])[1].astype(BF16)
+    copy = pltpu.make_async_copy(slope, slope_out, sem)
+    copy.start()
     expand_bias(
         table.at[1], spread, tab_scr, rows_scr, wide_scr, bias_out, lat, True, lat_total
     )
-    slope_out[...] = gelu_parts(hidden[...])[1].astype(BF16)
+    copy.wait()
 
 
 def merge_ahead(scr_own, scr_oth, rows):
@@ -509,7 +523,7 @@
             out[z, at:] = refs[-3][j]
 
 
-def add_pair(keep, got, out):
+def add_pair(keep, got, order, out):
     out[...] = (keep[...].astype(F32) + got[...].astype(F32)).astype(BF16)
 
 
@@ -534,13 +548,26 @@
 
 
 def third_kernel(
-    head, lon_tail, lat_head, diag_tail, resid_in, slope, active, mixed,
+    head, lon_tail, lat_head, diag_tail, resid_in, slope_in, active_in, mixed_in,
     proj_w, up_w, down_w, gains, probs_in, order,
     keep_out, give_out, rg_out, dmix_out, gain_out, probs_out,
-    scr_own, scr_oth, m192, m768, mdown, flat_scr, sem,
+    scr_own, scr_oth, m192, m768, mdown, flat_scr,
+    resid, slope, active, mixed, sems,
 ):
-    copy = pltpu.make_async_copy(probs_in.at[0 : probs_out.shape[0]], probs_out, sem)
-    copy.start()
+    copies = [
+        pltpu.make_async_copy(source, target, sems.at[k])
+        for k, (source, target) in enumerate(
+            (
+                (resid_in, resid),
+                (slope_in, slope),
+                (mixed_in, mixed),
+                (active_in, active),
+                (probs_in.at[0 : probs_out.shape[0]], probs_out),
+            )
+        )
+    ]
+    for copy in copies:
+        copy.start()
     rows, width = scr_own.shape
     cut = CHUNK * (WLON // 2)
     scr_own[0:cut, :] = lon_tail[...].astype(F32)
@@ -549,9 +576,11 @@
     scr_oth[cut:, :] = lat_head[...].astype(F32)
     g = merge_behind(scr_own, scr_oth, rows)
     g_low = g.astype(BF16)
-    stand2, inv2 = standardize(resid_in[...].astype(F32))
+    hg = dot(g_low, down_w[0])
+    copies[0].wait()
+    stand2, inv2 = standardize(resid[...].astype(F32))
     normed2 = (stand2 * gains[0, 1:2, :]).astype(BF16)
-    hg = dot(g_low, down_w[0])
+    copies[1].wait()
     hg = (hg * slope[...].astype(F32)).astype(BF16)
     part, gain_two = norm_back(dot_nt(hg, up_w[0]), gains[0, 1:2, :], stand2, inv2)
     rg = g + part
@@ -559,15 +588,17 @@
     low = rg.astype(BF16)
     dmix_out[...] = dot_nt(low, proj_w[0]).astype(BF16)
     gain_out[...] = gain_two
+    copies[2].wait()
     put(m192, slice(None), dot_tn(mixed[...], low))
     at = flat_store(flat_scr, 0, m192, mixed.shape[1])
     put(m768, slice(None), dot_tn(normed2, hg))
     at += flat_store(flat_scr, at, m768, active.shape[1])
+    copies[3].wait()
     put(mdown, slice(None), dot_tn(active[...], g_low))
     at += flat_store(flat_scr, at, mdown, mixed.shape[1])
     flat_scr[at:, :] = jnp.zeros((flat_scr.shape[0] - at, 128), F32)
     halves(flat_scr, lax.axis_index("lat"), keep_out, give_out)
-    copy.wait()
+    copies[4].wait()
 
 
 def gain_rows(one, two):
@@ -826,8 +857,11 @@
             ((1,) + down_turned.shape[1:], BF16),
             stack_shape,
             probs_shape,
+            (token, BF16),
+            (token, BF16),
+            ((rows, hid), BF16),
             pltpu.SemaphoreType.DMA((9,)),
-            pltpu.SemaphoreType.DMA((wins,)),
+            pltpu.SemaphoreType.DMA((wins + 3,)),
         ],
         [
             pltpu.with_memory_space_constraint(arg, pltpu.HBM)
@@ -839,8 +873,8 @@
         8,
         16,
         [pltpu.HBM] * 9,
-        (5,),
-        (0, 3, 4, 6, 8),
+        (4, 5, 6, 8),
+        (0, 3),
     )
     lon_head = lon_send(head, -1)
     diag_head = diag_send(head, -1)
@@ -848,11 +882,11 @@
     bias1, slope0 = call(
         functools.partial(bias_kernel, lat_total),
         [bias_shape, ((rows, hid), BF16)],
-        [tab_scr, rows_scr, wide_scr],
+        [tab_scr, rows_scr, wide_scr, ((rows, hid), BF16), pltpu.SemaphoreType.DMA],
         (table, spread, hidden0),
         3,
-        10,
-        near=(1,),
+        12,
+        far=(1,),
     )
 
     (
@@ -927,15 +961,23 @@
             m768,
             mdown,
             flat_scr(units_b),
-            pltpu.SemaphoreType.DMA,
+            (token, BF16),
+            ((rows, hid), BF16),
+            ((rows, hid), BF16),
+            (token, BF16),
+            pltpu.SemaphoreType.DMA((5,)),
         ],
         (
-            dhead, lon_tail, lat_dhead, diag_tail, resid0, slope0, active0, mixed0, proj_weight,
-            up_weight, down_turned, norm_gain, probs_far, part_a,
+            dhead, lon_tail, lat_dhead, diag_tail,
+            *[
+                pltpu.with_memory_space_constraint(saved, pltpu.HBM)
+                for saved in (resid0, slope0, active0, mixed0)
+            ],
+            proj_weight, up_weight, down_turned, norm_gain, probs_far, part_a,
         ),
         3,
         14,
-        [pltpu.VMEM] * 12 + [pltpu.HBM, pltpu.VMEM],
+        [pltpu.VMEM] * 4 + [pltpu.HBM] * 4 + [pltpu.VMEM] * 4 + [pltpu.HBM, pltpu.VMEM],
     )
     got_b = lat_swap(give_b)
 
@@ -978,7 +1020,15 @@
     )
     got_x = x_swap(give_x)
     (sum_a,) = call(sum_pieces, [units(units_a + extra)], [], (pieces_a, keep_x), 1, 10)
-    (part_z,) = call(add_pair, [units(zs, units_bc)], [], (keep_x, got_x), 1, 10)
+    (same,) = call(
+        join_z,
+        [units(zs, units_a + extra)],
+        [],
+        [sum_a] + [lon_send(sum_a, 2 * k) for k in range(1, zs)],
+        1,
+        10,
+    )
+    (part_z,) = call(add_pair, [units(zs, units_bc)], [], (keep_x, got_x, same), 1, 10)
     pieces_bc = lax.all_to_all(
         part_z,
         "lon",
@@ -987,26 +1037,18 @@
         axis_index_groups=[[2 * z + x for z in range(zs)] for x in range(2)],
     )
 
-    (same,) = call(
-        join_z,
-        [units(zs, units_a + extra)],
-        [],
-        [sum_a] + [lon_send(sum_a, 2 * k) for k in range(1, zs)] + [part_z],
-        1,
-        10,
-    )
+    same_x = x_swap(same)
+    cross = lat_swap(same)
+    cross_x = lat_swap(same_x)
     (sum_bc,) = call(
         sum_pieces,
         [units(lon_size, units_bc)],
         [],
-        (pieces_bc, same),
+        (pieces_bc, cross_x),
         1,
         10,
     )
     whole_bc = lax.all_to_all(sum_bc, "lon", 0, 0)
-    same_x = x_swap(same)
-    cross = lat_swap(same)
-    cross_x = lat_swap(same_x)
     oth_bc = lat_swap(whole_bc)
 
     flat_rows = (2 * block_rows * 128 + norm_gain.size) // 128

time: 109 us -> 102 us (0.936)
  blocking collectives: 0 us -> 18.3 us
  waiting for transfers between devices: 34.4 us -> 18.4 us
  starting transfers between devices: 31.8 us -> 26 us
  local copies, waits for them, and re-layouts: 5.87 us -> 0.91 us
  Pallas kernels: 35.9 us -> 37.6 us
    all_to_all x0 -> x1, blocking collectives: none -> 18.3 us  [shards(): whole_bc = lax.all_to_all(sum_bc, 'lon', 0, 0)]
    all_to_all x1 -> x0, waiting for transfers between devices: 12.1 us -> none  [shards(): whole_bc = lax.all_to_all(sum_bc, 'lon', 0, 0)]
    all_to_all x1, waiting for transfers between devices: 0.01 us -> 5.81 us  [shards(): lax.all_to_all(part_z, 'lon', 0, 0, axis_index_groups=[[2 * z + x for z i...]
    unnamed x34 -> x18, local copies, waits for them, and re-layouts: 5.87 us -> 0.91 us
    ppermute x5, waiting for transfers between devices: 10.9 us -> 6.2 us  [lon_send(): lax.ppermute(value, 'lon', [(s, (s + step) % count) for s in range(count)])]
    ppermute x2, waiting for transfers between devices: 6.99 us -> 3.33 us  [x_swap(): return lax.ppermute(value, 'lon', [(s, s ^ 1) for s in range(count)])]
    all_to_all x1 -> x0, starting transfers between devices: 3.54 us -> none  [shards(): whole_bc = lax.all_to_all(sum_bc, 'lon', 0, 0)]
    pallas_call x14, Pallas kernels: 35.9 us -> 37.6 us  [call(): pl.pallas_call(kernel, out_shape=[pltpu.HBM(*entry) if at in far else (pl...]
  transfers between devices with their start and end apart: 20 -> 19, of which waited for: 9 -> 8; matrix products, arithmetic and copies ran while one was open for 0% -> 0% of each run, Pallas kernels for 14% -> 17%
where the time goes in v11:
time: 102 us
  Pallas kernels  37.6 us (37%)
  starting transfers between devices  26 us (25%)
  waiting for transfers between devices  18.4 us (18%)
  blocking collectives  18.3 us (18%)
    pallas_call x14, Pallas kernels, call(): pl.pallas_call(kernel, out_shape=[pltpu.HBM(*entry) if at in far else (pl...  37.6 us
    all_to_all x1, blocking collectives, shards(): whole_bc = lax.all_to_all(sum_bc, 'lon', 0, 0)  18.3 us
    ppermute x2, starting transfers between devices, diag_send(): return lax.ppermute(value, ('lon', 'lat'), pairs)  6.3 us
    ppermute x5, waiting for transfers between devices, lon_send(): lax.ppermute(value, 'lon', [(s, (s + step) % count) for s in range(count)])  6.2 us
    all_to_all x1, starting transfers between devices, shards(): pieces_a = lax.all_to_all(part_a, 'lon', 0, 0)  6.09 us
    all_to_all x1, waiting for transfers between devices, shards(): lax.all_to_all(part_z, 'lon', 0, 0, axis_index_groups=[[2 * z + x for z i...  5.81 us
    ppermute x5, starting transfers between devices, lon_send(): lax.ppermute(value, 'lon', [(s, (s + step) % count) for s in range(count)])  5.33 us
    all_to_all x1, starting transfers between devices, shards(): lax.all_to_all(part_z, 'lon', 0, 0, axis_index_groups=[[2 * z + x for z i...  3.45 us
  transfers between devices with their start and end apart: 19, of which 8 were waited for; matrix products, arithmetic and copies ran while one was open for 0% of the time, Pallas kernels for 17%

profile of v11, /device:TPU:0, one launch (start us, length us, event | category | flops | bytes accessed | tf_op | source)
XLA Modules:
  0.0 102.1 jit_solution(18034207193103501984)
XLA Ops:
  0.6 0.0 copy-start.6
  0.7 7.2 %shard_map.112 = (bf16[576,192]{1,0:T(8,128)(2,1)S(1)}, bf16[2,504,192]{2,1,0:T(8,128)(2,1)S(1)}, bf16[2,72,192]{2,1,0:T(8,128)(2,1)S(1)}, bf16[576,576]{1,0:T(8...) custom-call(bf16[2,12,24,192]{3,2,1,0:T(8,128)(2,1)} %tokens_in.1, ...), custom_call_target="tpu_custom_call" | custom-call | flops 8800000000 | bytes 100000 | tf_op jit(solution)/shard_map/pallas_call | solution.py:740
  7.9 0.9 copy-done.7
  8.8 0.5 collective-permute-start.1
  9.2 5.6 %collective-permute-start.2 = (bf16[2,72,192]{2,1,0:T(8,128)(2,1)S(1)}, bf16[2,72,192]{2,1,0:T(8,128)(2,1)S(1)}, u32[]{:S(2)}, u32[]{:S(2)}) collective-permute-start(bf16[2,72,192]{2,1,0:T(8,128)(2,1)S(1)} %get-tuple-element.49), channel_id=1, source_target_pairs={{0,15},{1,14},{2,1},{3,0},{4,3},{5,2},{6,5},{7,4},{8,7},{9,6},{10,... | collective-permute-start | bytes 165896 | tf_op jit(solution)/shard_map/ppermute | solution.py:783
  14.9 0.5 collective-permute-start
  15.4 0.0 copy-start.2
  15.4 0.0 copy-start.4
  15.4 0.0 copy-start.5
  15.4 3.2 %shard_map.113 = (f32[864,144]{1,0:T(8,128)S(1)}, bf16[576,768]{1,0:T(8,128)(2,1)}) custom-call(f32[2,6,1,6336]{3,2,1,0:T(1,128)S(1)} %bitcast.8, bf16[2,132,384]{2,1,0:T(8,128)(2,1)S(1)} %copy-done.6, f32[576,768]{1,0:T(8,128)S(1)} %get-tuple-element.50.hidden), custom_call_target="tpu_custom_call" | custom-call | flops 3300000000 | bytes 100000 | tf_op jit(solution)/shard_map/pallas_call | solution.py:740
  18.7 0.0 collective-permute-done.2.diag_head
  18.7 0.5 collective-permute-done.lon_head
  19.2 0.0 collective-permute-done.1.lat_tail
  19.3 8.9 %shard_map.114 = (bf16[504,192]{1,0:T(8,128)(2,1)S(1)}, bf16[72,192]{1,0:T(8,128)(2,1)S(1)}, bf16[576,192]{1,0:T(8,128)(2,1)S(1)}, bf16[576,576]{1,0:T(8,128)(2,...) custom-call(bf16[2,504,192]{2,1,0:T(8,128)(2,1)S(1)} %get-tuple-elem, ...), custom_call_target="tpu_custom_call" | custom-call | flops 20899999744 | bytes 100000 | tf_op jit(solution)/shard_map/pallas_call | solution.py:740
  28.2 1.6 %shard_map.115 = (bf16[8,27,8,128]{3,2,1,0:T(8,128)(2,1)S(1)}, bf16[8,27,8,128]{3,2,1,0:T(8,128)(2,1)S(1)}, bf16[8,5,8,128]{3,2,1,0:T(8,128)(2,1)S(1)}) custom-call(bf16[576,192]{1,0:T(8,128)(2,1)S(1)} %get-tuple-element.59.n1, bf16[576,576]{1,0:T(8,128)(2,1)S(1)} %get-tuple-element.60.field, bf16[576,192]{1,0:T(8,128)(2,1)S(1)} %get-tuple-element.61.mixed, ...), custom_call_target="tpu_custom_call" | custom-call | flops 3300000000 | bytes 100000 | tf_op jit(solution)/shard_map/pallas_call | solution.py:740
  29.8 0.1 collective-permute-start.6
  29.9 0.5 collective-permute-start.4
  30.4 0.7 collective-permute-start.5
  31.0 0.3 collective-permute-start.3
  31.4 0.3 collective-permute-done.6.refs_1_
  31.7 0.9 shard_map.116.order
  32.6 6.1 %all-to-all-start = ((bf16[8,32,8,128]{3,2,1,0:T(8,128)(2,1)}), bf16[8,32,8,128]{3,2,1,0:T(8,128)(2,1)S(1)}, u32[]{:S(2)}, u32[]{:S(2)}) async-start(bf16[8,32,8,128]{3,2,1,0:T(8,128)(2,1)} %shard_map.116.order), calls=%async_computation | async-start | bytes 1048576 | tf_op jit(solution)/shard_map/all_to_all | solution.py:943
  38.7 0.0 collective-permute-done.5.diag_tail
  38.7 0.0 collective-permute-done.3.lon_tail
  38.7 0.0 collective-permute-done.4.lat_head
  38.7 5.1 %shard_map.117 = (bf16[8,21,8,128]{3,2,1,0:T(8,128)(2,1)S(1)}, bf16[8,21,8,128]{3,2,1,0:T(8,128)(2,1)S(1)}, f32[576,192]{1,0:T(8,128)S(1)}, bf16[576,192]{1,0:T(...) custom-call(bf16[504,192]{1,0:T(8,128)(2,1)S(1)} %get-tuple-element.52.head, ...), custom_call_target="tpu_custom_call" | custom-call | flops 3300000000 | bytes 100000 | tf_op jit(solution)/shard_map/pallas_call | solution.py:740
  43.8 0.1 collective-permute-start.7
  43.9 6.5 %shard_map.118 = (bf16[2,12,24,192]{3,2,1,0:T(8,128)(2,1)}, bf16[8,7,8,128]{3,2,1,0:T(8,128)(2,1)S(1)}, bf16[8,7,8,128]{3,2,1,0:T(8,128)(2,1)S(1)}, bf16[8,5,8,128]{3,2,1,0:T(8,128)(2,1)S(1)}) custom-call(bf16[576,192]{1,0:T(8,128)(2,1)S(1)} %get-tuple-element.46.x_in, bf16[576,576]{1,0:T(8,128)(2,1)S(1)} %copy-done.8, ...), custom_call_target="tpu_custom_call" | custom-call | flops 8800000000 | bytes 100000 | tf_op jit(solution)/shard_map/pallas_call | solution.py:740
  50.4 0.6 collective-permute-start.8
  51.0 1.0 collective-permute-done.8.refs_3_
  52.0 0.1 shard_map.119
  52.1 2.1 %collective-permute-start.15 = (bf16[4,33,8,128]{3,2,1,0:T(8,128)(2,1)S(1)}, bf16[4,33,8,128]{3,2,1,0:T(8,128)(2,1)S(1)}, u32[]{:S(2)}, u32[]{:S(2)}) collective-permute-start(bf16[4,33,8,128]{3,2,1,0:T(8,128)(2,1)S(1)} %get-tuple-element.86), channel_id=1, source_target_pairs={{0,2},{2,0},{4,6},{6,4},{8,10},{10,8},{12,14},{14,12},{1,3},{3,1},... | collective-permute-start | bytes 811016 | tf_op jit(solution)/shard_map/ppermute | solution.py:774
  54.2 0.1 shard_map.120.refs_0_
  54.3 3.3 %collective-permute-start.11 = (bf16[32,8,128]{2,1,0:T(8,128)(2,1)S(1)}, bf16[32,8,128]{2,1,0:T(8,128)(2,1)S(1)}, u32[]{:S(2)}, u32[]{:S(2)}) collective-permute-start(bf16[32,8,128]{2,1,0:T(8,128)(2,1)S(1)} %shard_map.120.refs_0_), channel_id=1, source_target_pairs={{0,12},{2,14},{4,0},{6,2},{8,4},{10,6},{12,8},{14,10},{1,13},{3,15... | collective-permute-start | bytes 196616 | tf_op jit(solution)/shard_map/ppermute | solution.py:769
  57.6 1.1 %collective-permute-start.9 = (bf16[32,8,128]{2,1,0:T(8,128)(2,1)S(1)}, bf16[32,8,128]{2,1,0:T(8,128)(2,1)S(1)}, u32[]{:S(2)}, u32[]{:S(2)}) collective-permute-start(bf16[32,8,128]{2,1,0:T(8,128)(2,1)S(1)} %shard_map.120.refs_0_), channel_id=1, source_target_pairs={{0,4},{2,6},{4,8},{6,10},{8,12},{10,14},{12,0},{14,2},{1,5},{3,7},... | collective-permute-start | bytes 196616 | tf_op jit(solution)/shard_map/ppermute | solution.py:769
  58.7 1.4 %collective-permute-done.11.refs_3_ = bf16[32,8,128]{2,1,0:T(8,128)(2,1)S(1)} collective-permute-done((bf16[32,8,128]{2,1,0:T(8,128)(2,1)S(1)}, bf16[32,8,128]{2,1,0:T(8,128)(2,1)S(1)}, u32[]{:S(2)}, u32[]{:S(2)}) %collective-permute-start.11) | collective-permute-done | bytes 65568 | tf_op jit(solution)/shard_map/ppermute | solution.py:769
  60.1 4.3 %collective-permute-done.10.refs_2_ = bf16[32,8,128]{2,1,0:T(8,128)(2,1)S(1)} collective-permute-done((bf16[32,8,128]{2,1,0:T(8,128)(2,1)S(1)}, bf16[32,8,128]{2,1,0:T(8,128)(2,1)S(1)}, u32[]{:S(2)}, u32[]{:S(2)}) %collective-permute-start.10) | collective-permute-done | bytes 65568 | tf_op jit(solution)/shard_map/ppermute | solution.py:769
  64.4 0.6 collective-permute-start.12
  65.0 0.8 shard_map.123
  65.8 3.4 %all-to-all-start.1 = ((bf16[4,33,8,128]{3,2,1,0:T(8,128)(2,1)}), bf16[4,33,8,128]{3,2,1,0:T(8,128)(2,1)S(1)}, u32[]{:S(2)}, u32[]{:S(2)}) async-start(bf16[4,33,8,128]{3,2,1,0:T(8,128)(2,1)} %shard_map.123), calls=%async_computation.1 | async-start | bytes 540672 | tf_op jit(solution)/shard_map/all_to_all | solution.py:1032
  69.3 3.3 %collective-permute-done.12.same_x = bf16[4,32,8,128]{3,2,1,0:T(8,128)(2,1)S(1)} collective-permute-done((bf16[4,32,8,128]{3,2,1,0:T(8,128)(2,1)S(1)}, bf16[4,32,8,128]{3,2,1,0:T(8,128)(2,1)S(1)}, u32[]{:S(2)}, u32[]{:S(2)}) %collective-permute-start.12) | collective-permute-done | bytes 262176 | tf_op jit(solution)/shard_map/ppermute | solution.py:774
  72.6 5.8 %all-to-all-done.1.pieces = bf16[4,33,8,128]{3,2,1,0:T(8,128)(2,1)S(1)} async-done(((bf16[4,33,8,128]{3,2,1,0:T(8,128)(2,1)}), bf16[4,33,8,128]{3,2,1,0:T(8,128)(2,1)S(1)}, u32[]{:S(2)}, u32[]{:S(2)}) %all-to-all-start.1) | async-done | bytes 270368 | tf_op jit(solution)/shard_map/all_to_all | solution.py:1032
  78.4 0.1 shard_map.124
  78.5 18.3 %all_to_all.15.own_bc = bf16[8,33,8,128]{3,2,1,0:T(8,128)(2,1)S(1)} all-to-all(bf16[8,33,8,128]{3,2,1,0:T(8,128)(2,1)S(1)} %shard_map.124), channel_id=1, replica_groups=mesh['grp'=2,'lon'=8,'lat'=2] {'lon'}, dimensions={0} | all-to-all | bytes 1081344 | tf_op jit(solution)/shard_map/all_to_all | solution.py:1051
  96.8 0.5 collective-permute-start.13
  97.3 1.8 %collective-permute-done.13.cross = bf16[4,32,8,128]{3,2,1,0:T(8,128)(2,1)S(1)} collective-permute-done((bf16[4,32,8,128]{3,2,1,0:T(8,128)(2,1)S(1)}, bf16[4,32,8,128]{3,2,1,0:T(8,128)(2,1)S(1)}, u32[]{:S(2)}, u32[]{:S(2)}) %collective-permute-start.13) | collective-permute-done | bytes 262176 | tf_op jit(solution)/shard_map/ppermute | solution.py:764
  99.1 0.6 shard_map.122
  99.7 2.4 %shard_map.125 = (bf16[6918,128]{1,0:T(8,128)(2,1)}, f32[2,6,1,6336]{3,2,1,0:T(1,128)}) custom-call(bf16[2,132,384]{2,1,0:T(8,128)(2,1)S(1)} %copy-done.6, f32[3456,128]{1,0:T(8,128)S(1)} %get-tuple-element.83.flat_a, f32[8,128]{1,0:T(8,128)S(1)} %get-tuple-element.84.squares, f32[6,1,6336]{2,1,0:T(1,128)S(1)} %get-tuple-element.85.bias_late, ...), custom_call_target="tpu_custom_call" | custom-call | flops 2200000000 | bytes 100000 | tf_op jit(solution)/shard_map/pallas_call | solution.py:740
  (23 shorter events, 0.1 us)
Async XLA Ops:
  0.6 14.8 %copy-start.3 = (f32[2,1,6,6336]{3,1,2,0:T(1,128)S(1)}, f32[2,1,6,6336]{3,1,2,0:T(1,128)}, u32[]{:S(2)}) copy-start(f32[2,1,6,6336]{3,1,2,0:T(1,128)} %param.16) | copy-start | bytes 912388
  0.6 14.8 %copy-start.6 = (bf16[2,132,384]{2,1,0:T(8,128)(2,1)S(1)}, bf16[2,132,384]{2,1,0:T(8,128)(2,1)}, u32[]{:S(2)}) copy-start(bf16[2,132,384]{2,1,0:T(8,128)(2,1)} %constant.2.clone.spread_in.spread) | copy-start | bytes 608260
  7.9 0.9 copy-start.7
  8.8 10.4 %collective-permute-start.1 = (bf16[2,504,192]{2,1,0:T(8,128)(2,1)S(1)}, bf16[2,504,192]{2,1,0:T(8,128)(2,1)S(1)}, u32[]{:S(2)}, u32[]{:S(2)}) collective-permute-start(bf16[2,504,192]{2,1,0:T(8,128)(2,1)S(1)} %get-tuple-element.48.tail), channel_id=1, source_target_pairs={{0,1},{1,0},{2,3},{3,2},{4,5},{5,4},{6,7},{7,6},{8,9},{9,8},{10,11... | collective-permute-start | bytes 1161224 | tf_op jit(solution)/shard_map/ppermute | solution.py:764
  9.2 9.4 %collective-permute-start.2 = (bf16[2,72,192]{2,1,0:T(8,128)(2,1)S(1)}, bf16[2,72,192]{2,1,0:T(8,128)(2,1)S(1)}, u32[]{:S(2)}, u32[]{:S(2)}) collective-permute-start(bf16[2,72,192]{2,1,0:T(8,128)(2,1)S(1)} %get-tuple-element.49), channel_id=1, source_target_pairs={{0,15},{1,14},{2,1},{3,0},{4,3},{5,2},{6,5},{7,4},{8,7},{9,6},{10,... | collective-permute-start | bytes 165896 | tf_op jit(solution)/shard_map/ppermute | solution.py:783
  14.9 4.4 %collective-permute-start = (bf16[2,72,192]{2,1,0:T(8,128)(2,1)S(1)}, bf16[2,72,192]{2,1,0:T(8,128)(2,1)S(1)}, u32[]{:S(2)}, u32[]{:S(2)}) collective-permute-start(bf16[2,72,192]{2,1,0:T(8,128)(2,1)S(1)} %get-tuple-element.49), channel_id=1, source_target_pairs={{0,14},{2,0},{4,2},{6,4},{8,6},{10,8},{12,10},{14,12},{1,15},{3,1}... | collective-permute-start | bytes 165896 | tf_op jit(solution)/shard_map/ppermute | solution.py:769
  15.4 3.8 %copy-start = (bf16[2,192,768]{2,1,0:T(8,128)(2,1)S(1)}, bf16[2,192,768]{2,1,0:T(8,128)(2,1)}, u32[]{:S(2)}) copy-start(bf16[2,192,768]{2,1,0:T(8,128)(2,1)} %up_w.3) | copy-start | bytes 1769476
  15.4 3.8 %copy-start.1 = (bf16[2,768,192]{1,2,0:T(8,128)(2,1)S(1)}, bf16[2,768,192]{1,2,0:T(8,128)(2,1)}, u32[]{:S(2)}) copy-start(bf16[2,768,192]{1,2,0:T(8,128)(2,1)} %param.14) | copy-start | bytes 1769476
  15.4 3.8 %copy-start.2 = (bf16[2,192,576]{2,1,0:T(8,128)(2,1)S(1)}, bf16[2,192,576]{2,1,0:T(8,128)(2,1)}, u32[]{:S(2)}) copy-start(bf16[2,192,576]{2,1,0:T(8,128)(2,1)} %qkv_w.3) | copy-start | bytes 1327108
  15.4 3.8 %copy-start.4 = (bf16[2,192,192]{2,1,0:T(8,128)(2,1)S(1)}, bf16[2,192,192]{2,1,0:T(8,128)(2,1)}, u32[]{:S(2)}) copy-start(bf16[2,192,192]{2,1,0:T(8,128)(2,1)} %proj_w.3) | copy-start | bytes 442372
  15.4 3.8 %copy-start.5 = (f32[2,2,192]{2,1,0:T(2,128)S(1)}, f32[2,2,192]{2,1,0:T(2,128)}, u32[]{:S(2)}) copy-start(f32[2,2,192]{2,1,0:T(2,128)} %gains.5) | copy-start | bytes 9220
  29.8 1.8 %collective-permute-start.6 = (bf16[8,27,8,128]{3,2,1,0:T(8,128)(2,1)S(1)}, bf16[8,27,8,128]{3,2,1,0:T(8,128)(2,1)S(1)}, u32[]{:S(2)}, u32[]{:S(2)}) collective-permute-start(bf16[8,27,8,128]{3,2,1,0:T(8,128)(2,1)S(1)} %get-tuple-element.69), channel_id=1, source_target_pairs={{0,1},{1,0},{2,3},{3,2},{4,5},{5,4},{6,7},{7,6},{8,9},{9,8},{10,11... | collective-permute-start | bytes 1327112 | tf_op jit(solution)/shard_map/ppermute | solution.py:764
  29.9 8.8 %collective-permute-start.4 = (bf16[504,192]{1,0:T(8,128)(2,1)S(1)}, bf16[504,192]{1,0:T(8,128)(2,1)S(1)}, u32[]{:S(2)}, u32[]{:S(2)}) collective-permute-start(bf16[504,192]{1,0:T(8,128)(2,1)S(1)} %get-tuple-element.52.head), channel_id=1, source_target_pairs={{0,1},{1,0},{2,3},{3,2},{4,5},{5,4},{6,7},{7,6},{8,9},{9,8},{10,11... | collective-permute-start | bytes 580616 | tf_op jit(solution)/shard_map/ppermute | solution.py:764
  30.4 8.3 %collective-permute-start.5 = (bf16[72,192]{1,0:T(8,128)(2,1)S(1)}, bf16[72,192]{1,0:T(8,128)(2,1)S(1)}, u32[]{:S(2)}, u32[]{:S(2)}) collective-permute-start(bf16[72,192]{1,0:T(8,128)(2,1)S(1)} %get-tuple-element.53), channel_id=1, source_target_pairs={{0,3},{1,2},{2,5},{3,4},{4,7},{5,6},{6,9},{7,8},{8,11},{9,10},{10,... | collective-permute-start | bytes 82952 | tf_op jit(solution)/shard_map/ppermute | solution.py:783
  31.0 7.6 %collective-permute-start.3 = (bf16[72,192]{1,0:T(8,128)(2,1)S(1)}, bf16[72,192]{1,0:T(8,128)(2,1)S(1)}, u32[]{:S(2)}, u32[]{:S(2)}) collective-permute-start(bf16[72,192]{1,0:T(8,128)(2,1)S(1)} %get-tuple-element.53), channel_id=1, source_target_pairs={{0,2},{2,4},{4,6},{6,8},{8,10},{10,12},{12,14},{14,0},{1,3},{3,5},... | collective-permute-start | bytes 82952 | tf_op jit(solution)/shard_map/ppermute | solution.py:769
  32.6 21.6 %all-to-all-start = ((bf16[8,32,8,128]{3,2,1,0:T(8,128)(2,1)}), bf16[8,32,8,128]{3,2,1,0:T(8,128)(2,1)S(1)}, u32[]{:S(2)}, u32[]{:S(2)}) async-start(bf16[8,32,8,128]{3,2,1,0:T(8,128)(2,1)} %shard_map.116.order), calls=%async_computation | async-start | bytes 1048576 | tf_op jit(solution)/shard_map/all_to_all | solution.py:943
  38.7 5.2 %copy-start.8 = (bf16[576,576]{1,0:T(8,128)(2,1)S(1)}, bf16[576,576]{1,0:T(8,128)(2,1)}, u32[]{:S(2)}) copy-start(bf16[576,576]{1,0:T(8,128)(2,1)} %copy-done.7) | copy-start | bytes 1990660
  43.8 8.2 %collective-permute-start.7 = (bf16[8,21,8,128]{3,2,1,0:T(8,128)(2,1)S(1)}, bf16[8,21,8,128]{3,2,1,0:T(8,128)(2,1)S(1)}, u32[]{:S(2)}, u32[]{:S(2)}) collective-permute-start(bf16[8,21,8,128]{3,2,1,0:T(8,128)(2,1)S(1)} %get-tuple-element.78), channel_id=1, source_target_pairs={{0,1},{1,0},{2,3},{3,2},{4,5},{5,4},{6,7},{7,6},{8,9},{9,8},{10,11... | collective-permute-start | bytes 1032200 | tf_op jit(solution)/shard_map/ppermute | solution.py:764
  50.4 1.5 %collective-permute-start.8 = (bf16[8,7,8,128]{3,2,1,0:T(8,128)(2,1)S(1)}, bf16[8,7,8,128]{3,2,1,0:T(8,128)(2,1)S(1)}, u32[]{:S(2)}, u32[]{:S(2)}) collective-permute-start(bf16[8,7,8,128]{3,2,1,0:T(8,128)(2,1)S(1)} %get-tuple-element.80), channel_id=1, source_target_pairs={{0,1},{1,0},{2,3},{3,2},{4,5},{5,4},{6,7},{7,6},{8,9},{9,8},{10,11... | collective-permute-start | bytes 344072 | tf_op jit(solution)/shard_map/ppermute | solution.py:764
  52.1 13.0 %collective-permute-start.15 = (bf16[4,33,8,128]{3,2,1,0:T(8,128)(2,1)S(1)}, bf16[4,33,8,128]{3,2,1,0:T(8,128)(2,1)S(1)}, u32[]{:S(2)}, u32[]{:S(2)}) collective-permute-start(bf16[4,33,8,128]{3,2,1,0:T(8,128)(2,1)S(1)} %get-tuple-element.86), channel_id=1, source_target_pairs={{0,2},{2,0},{4,6},{6,4},{8,10},{10,8},{12,14},{14,12},{1,3},{3,1},... | collective-permute-start | bytes 811016 | tf_op jit(solution)/shard_map/ppermute | solution.py:774
  54.3 5.8 %collective-permute-start.11 = (bf16[32,8,128]{2,1,0:T(8,128)(2,1)S(1)}, bf16[32,8,128]{2,1,0:T(8,128)(2,1)S(1)}, u32[]{:S(2)}, u32[]{:S(2)}) collective-permute-start(bf16[32,8,128]{2,1,0:T(8,128)(2,1)S(1)} %shard_map.120.refs_0_), channel_id=1, source_target_pairs={{0,12},{2,14},{4,0},{6,2},{8,4},{10,6},{12,8},{14,10},{1,13},{3,15... | collective-permute-start | bytes 196616 | tf_op jit(solution)/shard_map/ppermute | solution.py:769
  57.6 6.8 %collective-permute-start.10 = (bf16[32,8,128]{2,1,0:T(8,128)(2,1)S(1)}, bf16[32,8,128]{2,1,0:T(8,128)(2,1)S(1)}, u32[]{:S(2)}, u32[]{:S(2)}) collective-permute-start(bf16[32,8,128]{2,1,0:T(8,128)(2,1)S(1)} %shard_map.120.refs_0_), channel_id=1, source_target_pairs={{0,8},{2,10},{4,12},{6,14},{8,0},{10,2},{12,4},{14,6},{1,9},{3,11}... | collective-permute-start | bytes 196616 | tf_op jit(solution)/shard_map/ppermute | solution.py:769
  57.6 6.8 %collective-permute-start.9 = (bf16[32,8,128]{2,1,0:T(8,128)(2,1)S(1)}, bf16[32,8,128]{2,1,0:T(8,128)(2,1)S(1)}, u32[]{:S(2)}, u32[]{:S(2)}) collective-permute-start(bf16[32,8,128]{2,1,0:T(8,128)(2,1)S(1)} %shard_map.120.refs_0_), channel_id=1, source_target_pairs={{0,4},{2,6},{4,8},{6,10},{8,12},{10,14},{12,0},{14,2},{1,5},{3,7},... | collective-permute-start | bytes 196616 | tf_op jit(solution)/shard_map/ppermute | solution.py:769
  64.4 8.2 %collective-permute-start.12 = (bf16[4,32,8,128]{3,2,1,0:T(8,128)(2,1)S(1)}, bf16[4,32,8,128]{3,2,1,0:T(8,128)(2,1)S(1)}, u32[]{:S(2)}, u32[]{:S(2)}) collective-permute-start(bf16[4,32,8,128]{3,2,1,0:T(8,128)(2,1)S(1)} %shard_map.121.same.order), channel_id=1, source_target_pairs={{0,2},{2,0},{4,6},{6,4},{8,10},{10,8},{12,14},{14,12},{1,3},{3,1},... | collective-permute-start | bytes 786440 | tf_op jit(solution)/shard_map/ppermute | solution.py:774
  65.8 12.6 %all-to-all-start.1 = ((bf16[4,33,8,128]{3,2,1,0:T(8,128)(2,1)}), bf16[4,33,8,128]{3,2,1,0:T(8,128)(2,1)S(1)}, u32[]{:S(2)}, u32[]{:S(2)}) async-start(bf16[4,33,8,128]{3,2,1,0:T(8,128)(2,1)} %shard_map.123), calls=%async_computation.1 | async-start | bytes 540672 | tf_op jit(solution)/shard_map/all_to_all | solution.py:1032
  72.6 5.8 %collective-permute-start.14 = (bf16[4,32,8,128]{3,2,1,0:T(8,128)(2,1)S(1)}, bf16[4,32,8,128]{3,2,1,0:T(8,128)(2,1)S(1)}, u32[]{:S(2)}, u32[]{:S(2)}) collective-permute-start(bf16[4,32,8,128]{3,2,1,0:T(8,128)(2,1)S(1)} %collective-permute-done.12.same_x), channel_id=1, source_target_pairs={{0,1},{1,0},{2,3},{3,2},{4,5},{5,4},{6,7},{7,6},{8,9},{9,8},{10,11... | collective-permute-start | bytes 786440 | tf_op jit(solution)/shard_map/ppermute | solution.py:764
  96.8 2.9 %collective-permute-start.16 = (bf16[8,33,8,128]{3,2,1,0:T(8,128)(2,1)S(1)}, bf16[8,33,8,128]{3,2,1,0:T(8,128)(2,1)S(1)}, u32[]{:S(2)}, u32[]{:S(2)}) collective-permute-start(bf16[8,33,8,128]{3,2,1,0:T(8,128)(2,1)S(1)} %all_to_all.15.own_bc), channel_id=1, source_target_pairs={{0,1},{1,0},{2,3},{3,2},{4,5},{5,4},{6,7},{7,6},{8,9},{9,8},{10,11... | collective-permute-start | bytes 1622024 | tf_op jit(solution)/shard_map/ppermute | solution.py:764
  96.8 2.3 %collective-permute-start.13 = (bf16[4,32,8,128]{3,2,1,0:T(8,128)(2,1)S(1)}, bf16[4,32,8,128]{3,2,1,0:T(8,128)(2,1)S(1)}, u32[]{:S(2)}, u32[]{:S(2)}) collective-permute-start(bf16[4,32,8,128]{3,2,1,0:T(8,128)(2,1)S(1)} %shard_map.121.same.order), channel_id=1, source_target_pairs={{0,1},{1,0},{2,3},{3,2},{4,5},{5,4},{6,7},{7,6},{8,9},{9,8},{10,11... | collective-permute-start | bytes 786440 | tf_op jit(solution)/shard_map/ppermute | solution.py:764

commit v12 on v10

--- a/solution.py
+++ b/solution.py
@@ -182,7 +182,7 @@
     return total
 
 
-def attend(qkv, bias, mixed, probs, stack_scr, width, finish=None):
+def attend(qkv, bias, mixed, probs, stack_scr, width):
     masks = head_masks(width, BF16)
     masks32 = head_masks(width, F32)
     scale = (width // HEADS) ** -0.5
@@ -201,14 +201,12 @@
             probs[w, h] = p
             stack_scr[part, :] = p.astype(BF16)
         mixed[rows, :] = pick_heads(dot(stack_scr[...], v), masks32).astype(BF16)
-        if finish is not None:
-            finish(w)
         return carry
 
     lax.fori_loop(0, probs.shape[0], window, 0, unroll=True)
 
 
-def attend_back(qkv, probs, dmix, field, sums, low_scr, prob_scr, width, first=0, begin=None):
+def attend_back(qkv, probs, dmix, field, sums, low_scr, prob_scr, width):
     masks = head_masks(width, BF16)
     masks32 = head_masks(width, F32)
     scale = (width // HEADS) ** -0.5
@@ -220,11 +218,9 @@
         v = qkv[rows, 2 * width : 3 * width]
         up = stack_heads(dmix[rows, :], masks)
         prob_grad = dot_nt(up, v)
-        if begin is not None:
-            begin(w)
         for h in range(HEADS):
             part = slice(h * WIN, (h + 1) * WIN)
-            p = probs[w - first, h]
+            p = probs[w, h]
             weighted = p * prob_grad[part]
             ds = weighted - p * jnp.sum(weighted, axis=-1, keepdims=True)
             sums[part, 0:WIN] += ds
@@ -239,7 +235,7 @@
         field[rows, 2 * width : 3 * width] = dv.astype(BF16)
         return carry
 
-    lax.fori_loop(first, first + probs.shape[0], window, 0, unroll=True)
+    lax.fori_loop(0, probs.shape[0], window, 0, unroll=True)
 
 
 def lon_major(src, scr):
@@ -303,13 +299,13 @@
     for k in range(BIAS_UNITS, lons * per):
         put_unit(k, jnp.zeros((UNIT, 128), BF16))
 
-def forward_core(x, b, refs, qkv_scr, bias_scr, mixed, probs, stack_scr, finish=None):
+def forward_core(x, b, refs, qkv_scr, bias_scr, mixed, probs, stack_scr):
     qkv_w, proj_w, gains = refs
     width = x.shape[-1]
     stand, inv = standardize(x)
     normed = (stand * gains[b, 0:1, :]).astype(BF16)
     qkv_scr[...] = dot(normed, qkv_w[b]).astype(BF16)
-    attend(qkv_scr, bias_scr, mixed, probs, stack_scr, width, finish)
+    attend(qkv_scr, bias_scr, mixed, probs, stack_scr, width)
     att = dot(mixed[...], proj_w[b]).astype(BF16)
     resid = (x + att.astype(F32)).astype(BF16).astype(F32)
     return resid, normed
@@ -319,7 +315,7 @@
     lat_total, tokens_in, cot_in, table_in, spread_in, qkv_in, proj_in, up_in, down_in, gains_in,
     x_out, tail_out, head_out, qkv_out, mixed_out, probs_out, resid_out, hidden_out, active_out,
     scr, cot_scr, tab_scr, rows_scr, wide_scr, bias_scr,
-    cot, table, spread, tokens, qkv_w, gains, proj_w, up_w, down_w, stack_scr, probs, sems, out_sems,
+    cot, table, spread, tokens, qkv_w, gains, proj_w, up_w, down_w, stack_scr, sems,
 ):
     copies = []
     for source, target in (
@@ -357,12 +353,8 @@
     for copy in copies[4:]:
         copy.wait()
 
-    def probs_copy(w):
-        return pltpu.make_async_copy(probs.at[w], probs_out.at[w], out_sems.at[w])
-
     resid, _ = forward_core(
-        x, 0, (qkv_w, proj_w, gains), qkv_out, bias_scr, mixed_out, probs, stack_scr,
-        lambda w: probs_copy(w).start(),
+        x, 0, (qkv_w, proj_w, gains), qkv_out, bias_scr, mixed_out, probs_out, stack_scr
     )
     resid_out[...] = resid.astype(BF16)
     stand, _ = standardize(resid)
@@ -374,18 +366,16 @@
     result = resid + dot_nt(active, down_w[0])
     head_out[0] = result[0:cut, :].astype(BF16)
     tail_out[0] = result[cut:, :].astype(BF16)
-    for w in range(probs.shape[0]):
-        probs_copy(w).wait()
 
 
 def bias_kernel(
     lat_total, table, spread, hidden, bias_out, slope_out, tab_scr, rows_scr, wide_scr
 ):
     lat = lax.axis_index("lat")
+    slope_out[...] = gelu_parts(hidden[...])[1].astype(BF16)
     expand_bias(
         table.at[1], spread, tab_scr, rows_scr, wide_scr, bias_out, lat, True, lat_total
     )
-    slope_out[...] = gelu_parts(hidden[...])[1].astype(BF16)
 
 
 def merge_ahead(scr_own, scr_oth, rows):
@@ -409,6 +399,16 @@
 
 
 def second_kernel(
+    lat_total,
+    kept, tail, lon_head, lat_tail, diag_head, bias, qkv_w, proj_w, up_w, down_w, gains, *rest
+):
+    run_second(
+        lat_total, tail, lon_head, lat_tail, diag_head, bias, qkv_w, proj_w, up_w, down_w, gains,
+        *rest[kept:kept + 12], *rest[2 * kept + 12 :]
+    )
+
+
+def run_second(
     lat_total,
     tail, lon_head, lat_tail, diag_head, bias, qkv_w, proj_w, up_w, down_w, gains,
     head_out, tail_out, n1_out, field_out, mixed_out, low_out, n2_out, hg_out, active_out, g_out,
@@ -509,7 +509,7 @@
             out[z, at:] = refs[-3][j]
 
 
-def add_pair(keep, got, out):
+def add_pair(keep, got, order, out):
     out[...] = (keep[...].astype(F32) + got[...].astype(F32)).astype(BF16)
 
 
@@ -534,13 +534,11 @@
 
 
 def third_kernel(
-    head, lon_tail, lat_head, diag_tail, resid_in, slope, active, mixed,
-    proj_w, up_w, down_w, gains, probs_in, order,
-    keep_out, give_out, rg_out, dmix_out, gain_out, probs_out,
-    scr_own, scr_oth, m192, m768, mdown, flat_scr, sem,
+    head, lon_tail, lat_head, diag_tail, resid, slope, active, mixed,
+    proj_w, up_w, down_w, gains, order,
+    keep_out, give_out, rg_out, dmix_out, gain_out,
+    scr_own, scr_oth, m192, m768, mdown, flat_scr,
 ):
-    copy = pltpu.make_async_copy(probs_in.at[0 : probs_out.shape[0]], probs_out, sem)
-    copy.start()
     rows, width = scr_own.shape
     cut = CHUNK * (WLON // 2)
     scr_own[0:cut, :] = lon_tail[...].astype(F32)
@@ -549,9 +547,9 @@
     scr_oth[cut:, :] = lat_head[...].astype(F32)
     g = merge_behind(scr_own, scr_oth, rows)
     g_low = g.astype(BF16)
-    stand2, inv2 = standardize(resid_in[...].astype(F32))
+    hg = dot(g_low, down_w[0])
+    stand2, inv2 = standardize(resid[...].astype(F32))
     normed2 = (stand2 * gains[0, 1:2, :]).astype(BF16)
-    hg = dot(g_low, down_w[0])
     hg = (hg * slope[...].astype(F32)).astype(BF16)
     part, gain_two = norm_back(dot_nt(hg, up_w[0]), gains[0, 1:2, :], stand2, inv2)
     rg = g + part
@@ -567,7 +565,6 @@
     at += flat_store(flat_scr, at, mdown, mixed.shape[1])
     flat_scr[at:, :] = jnp.zeros((flat_scr.shape[0] - at, 128), F32)
     halves(flat_scr, lax.axis_index("lat"), keep_out, give_out)
-    copy.wait()
 
 
 def gain_rows(one, two):
@@ -582,25 +579,14 @@
 
 
 def fourth_kernel(
-    x_in, qkv, probs_near, probs_in, dmix, rg, gain_two, gains_late, qkv_w, gains,
+    x_in, qkv, probs, dmix, rg, gain_two, gains_late, qkv_w, gains,
     tokens_out, keep, give, bias_out,
-    field, sums, m576, flat_scr, dx_scr, low_scr, prob_scr, probs, sems,
+    field, sums, m576, flat_scr, dx_scr, low_scr, prob_scr,
 ):
-    near = probs_near.shape[0]
-
-    def probs_copy(w):
-        return pltpu.make_async_copy(probs_in.at[w], probs.at[w - near], sems.at[w - near])
-
-    for w in range(near, probs_in.shape[0]):
-        probs_copy(w).start()
     width = x_in.shape[-1]
     levels, lats, lons = tokens_out.shape[:3]
     sums[...] = jnp.zeros(sums.shape, F32)
-    attend_back(qkv, probs_near, dmix, field, sums, low_scr, prob_scr, width)
-    attend_back(
-        qkv, probs, dmix, field, sums, low_scr, prob_scr, width, near,
-        lambda w: probs_copy(w).wait(),
-    )
+    attend_back(qkv, probs, dmix, field, sums, low_scr, prob_scr, width)
     stand1, inv1 = standardize(x_in[...].astype(F32))
     normed = (stand1 * gains[0, 0:1, :]).astype(BF16)
     ng = dot_nt(field[...], qkv_w[0]).astype(BF16).astype(F32)
@@ -704,21 +690,22 @@
     bias_out[1] = bias_late[...]
 
 
-def call(kernel, outs, scratch, args, micros, mib, spaces=None, far=(), near=()):
+def call(kernel, outs, scratch, args, micros, mib, spaces=None, near=(), kept=0):
     spaces = spaces or [pltpu.VMEM] * len(args)
     return pl.pallas_call(
         kernel,
         out_shape=[
-            pltpu.HBM(*entry)
-            if at in far
-            else (pltpu.VMEM if at in near else jax.ShapeDtypeStruct)(*entry)
+            (pltpu.VMEM if at in near else jax.ShapeDtypeStruct)(*entry)
             for at, entry in enumerate(outs)
         ],
         in_specs=[pl.BlockSpec(memory_space=space) for space in spaces],
         out_specs=[
-            pl.BlockSpec(memory_space=pltpu.HBM if at in far else pltpu.VMEM)
+            pl.BlockSpec(memory_space=pltpu.VMEM if at < len(outs) - kept else pl.ANY)
             for at in range(len(outs))
         ],
+        input_output_aliases={
+            len(args) - kept + k: len(outs) - kept + k for k in range(kept)
+        },
         scratch_shapes=[
             pltpu.VMEM(*entry) if isinstance(entry, tuple) else entry for entry in scratch
         ],
@@ -825,9 +812,7 @@
             ((1,) + up_weight.shape[1:], BF16),
             ((1,) + down_turned.shape[1:], BF16),
             stack_shape,
-            probs_shape,
             pltpu.SemaphoreType.DMA((9,)),
-            pltpu.SemaphoreType.DMA((wins,)),
         ],
         [
             pltpu.with_memory_space_constraint(arg, pltpu.HBM)
@@ -839,8 +824,7 @@
         8,
         16,
         [pltpu.HBM] * 9,
-        (5,),
-        (0, 3, 4, 6, 8),
+        near=(0, 3, 4, 5, 6, 8),
     )
     lon_head = lon_send(head, -1)
     diag_head = diag_send(head, -1)
@@ -851,14 +835,16 @@
         [tab_scr, rows_scr, wide_scr],
         (table, spread, hidden0),
         3,
-        10,
+        12,
         near=(1,),
     )
 
+    saved = [x0, qkv0, mixed0, probs0, resid0, active0, slope0]
     (
         dhead, dtail, n1, field1, mixed1, low1, n2, hg1, active1, g1, sums1, gains1,
+        *saved,
     ) = call(
-        functools.partial(second_kernel, lat_total),
+        functools.partial(second_kernel, lat_total, len(saved)),
         [
             ((rows - cut, width), BF16),
             ((cut, width), BF16),
@@ -872,6 +858,7 @@
             (token, BF16),
             sums_shape,
             ((2, width), F32),
+            *[(value.shape, value.dtype) for value in saved],
         ],
         [
             (token, F32),
@@ -885,10 +872,15 @@
         (
             tail, lon_head, lat_tail, diag_head, bias1, qkv_weight, proj_weight, up_weight,
             down_turned, norm_gain,
+            *[pltpu.with_memory_space_constraint(value, pltpu.VMEM) for value in saved],
         ),
         19,
         16,
-    )
+        [pltpu.VMEM] * 10 + [pl.ANY] * len(saved),
+        near=tuple(range(12, 12 + len(saved))),
+        kept=len(saved),
+    )
+    x0, qkv0, mixed0, probs0, resid0, active0, slope0 = saved
     lon_tail = lon_send(dtail, 1)
     diag_tail = diag_send(dtail, 1)
     lat_dhead = lat_swap(dhead)
@@ -908,9 +900,7 @@
     )
     pieces_a = lax.all_to_all(part_a, "lon", 0, 0)
 
-    near = 1
-    probs_far = pltpu.with_memory_space_constraint(probs0, pltpu.HBM)
-    keep_b, give_b, rg0, dmix0, gain_two, probs_near = call(
+    keep_b, give_b, rg0, dmix0, gain_two = call(
         third_kernel,
         [
             units(lon_size, units_b),
@@ -918,24 +908,14 @@
             (token, F32),
             (token, BF16),
             ((1, width), F32),
-            ((near,) + probs_shape[0][1:], F32),
-        ],
-        [
-            (token, F32),
-            (token, F32),
-            m192,
-            m768,
-            mdown,
-            flat_scr(units_b),
-            pltpu.SemaphoreType.DMA,
-        ],
+        ],
+        [(token, F32), (token, F32), m192, m768, mdown, flat_scr(units_b)],
         (
             dhead, lon_tail, lat_dhead, diag_tail, resid0, slope0, active0, mixed0, proj_weight,
-            up_weight, down_turned, norm_gain, probs_far, part_a,
+            up_weight, down_turned, norm_gain, part_a,
         ),
         3,
         14,
-        [pltpu.VMEM] * 12 + [pltpu.HBM, pltpu.VMEM],
     )
     got_b = lat_swap(give_b)
 
@@ -955,16 +935,10 @@
             token_scr,
             stack_shape,
             stack_shape,
-            ((wins - near,) + probs_shape[0][1:], F32),
-            pltpu.SemaphoreType.DMA((wins - near,)),
-        ],
-        (
-            x0, qkv0, probs_near, probs_far, dmix0, rg0, gain_two, gains1, qkv_weight,
-            norm_gain,
-        ),
-        8,
+        ],
+        (x0, qkv0, probs0, dmix0, rg0, gain_two, gains1, qkv_weight, norm_gain),
+        7,
         14,
-        [pltpu.VMEM] * 3 + [pltpu.HBM] + [pltpu.VMEM] * 6,
     )
     got_c = lat_swap(give_c)
     units_bc = units_b + units_c + extra
@@ -978,7 +952,8 @@
     )
     got_x = x_swap(give_x)
     (sum_a,) = call(sum_pieces, [units(units_a + extra)], [], (pieces_a, keep_x), 1, 10)
-    (part_z,) = call(add_pair, [units(zs, units_bc)], [], (keep_x, got_x), 1, 10)
+    moved_a = [lon_send(sum_a, 2 * k) for k in range(1, zs)]
+    (part_z,) = call(add_pair, [units(zs, units_bc)], [], (keep_x, got_x, moved_a[0]), 1, 10)
     pieces_bc = lax.all_to_all(
         part_z,
         "lon",
@@ -987,26 +962,19 @@
         axis_index_groups=[[2 * z + x for z in range(zs)] for x in range(2)],
     )
 
-    (same,) = call(
-        join_z,
-        [units(zs, units_a + extra)],
-        [],
-        [sum_a] + [lon_send(sum_a, 2 * k) for k in range(1, zs)] + [part_z],
-        1,
-        10,
-    )
+    (same,) = call(join_z, [units(zs, units_a + extra)], [], [sum_a, *moved_a, part_z], 1, 10)
+    same_x = x_swap(same)
+    cross = lat_swap(same)
+    cross_x = lat_swap(same_x)
     (sum_bc,) = call(
         sum_pieces,
         [units(lon_size, units_bc)],
         [],
-        (pieces_bc, same),
+        (pieces_bc, same_x),
         1,
         10,
     )
     whole_bc = lax.all_to_all(sum_bc, "lon", 0, 0)
-    same_x = x_swap(same)
-    cross = lat_swap(same)
-    cross_x = lat_swap(same_x)
     oth_bc = lat_swap(whole_bc)
 
     flat_rows = (2 * block_rows * 128 + norm_gain.size) // 128

time: 109 us -> 102 us (0.936)
  waiting for transfers between devices: 34.4 us -> 14.9 us
  blocking collectives: 0 us -> 19.2 us
  starting transfers between devices: 31.8 us -> 27.2 us
  Pallas kernels: 35.9 us -> 34.3 us
    all_to_all x0 -> x1, blocking collectives: none -> 19.2 us  [shards(): whole_bc = lax.all_to_all(sum_bc, 'lon', 0, 0)]
    all_to_all x1 -> x0, waiting for transfers between devices: 12.1 us -> none  [shards(): whole_bc = lax.all_to_all(sum_bc, 'lon', 0, 0)]
    ppermute x5, waiting for transfers between devices: 10.9 us -> 1.76 us  [lon_send(): lax.ppermute(value, 'lon', [(s, (s + step) % count) for s in range(count)])]
    all_to_all x1 -> x0, starting transfers between devices: 3.54 us -> none  [shards(): whole_bc = lax.all_to_all(sum_bc, 'lon', 0, 0)]
    pallas_call x14, Pallas kernels: 35.9 us -> 34.3 us  [call(): pl.pallas_call(kernel, out_shape=[(pltpu.VMEM if at in near else jax.Shap...]
    ppermute x2, waiting for transfers between devices: 6.99 us -> 8.48 us  [x_swap(): return lax.ppermute(value, 'lon', [(s, s ^ 1) for s in range(count)])]
    unnamed x34 -> x38, local copies, waits for them, and re-layouts: 5.87 us -> 5.06 us
  transfers between devices with their start and end apart: 20 -> 19, of which waited for: 9 -> 8; matrix products, arithmetic and copies ran while one was open for 0% -> 0% of each run, Pallas kernels for 14% -> 15%
where the time goes in v12:
time: 102 us
  Pallas kernels  34.3 us (34%)
  starting transfers between devices  27.2 us (27%)
  blocking collectives  19.2 us (19%)
  waiting for transfers between devices  14.9 us (15%)
  local copies, waits for them, and re-layouts  5.06 us (5%)
    pallas_call x14, Pallas kernels, call(): pl.pallas_call(kernel, out_shape=[(pltpu.VMEM if at in near else jax.Shap...  34.3 us
    all_to_all x1, blocking collectives, shards(): whole_bc = lax.all_to_all(sum_bc, 'lon', 0, 0)  19.2 us
    ppermute x2, waiting for transfers between devices, x_swap(): return lax.ppermute(value, 'lon', [(s, s ^ 1) for s in range(count)])  8.48 us
    all_to_all x1, starting transfers between devices, shards(): pieces_a = lax.all_to_all(part_a, 'lon', 0, 0)  6.08 us
    ppermute x2, starting transfers between devices, diag_send(): return lax.ppermute(value, ('lon', 'lat'), pairs)  5.64 us
    unnamed x38, local copies, waits for them, and re-layouts  5.06 us
    ppermute x5, starting transfers between devices, lon_send(): lax.ppermute(value, 'lon', [(s, (s + step) % count) for s in range(count)])  4.98 us
    all_to_all x1, starting transfers between devices, shards(): lax.all_to_all(part_z, 'lon', 0, 0, axis_index_groups=[[2 * z + x for z i...  4.81 us
  transfers between devices with their start and end apart: 19, of which 8 were waited for; matrix products, arithmetic and copies ran while one was open for 0% of the time, Pallas kernels for 15%

profile of v12, /device:TPU:0, one launch (start us, length us, event | category | flops | bytes accessed | tf_op | source)
XLA Modules:
  0.0 101.5 jit_solution(17912354213541831304)
XLA Ops:
  0.6 0.0 copy-start.6
  0.7 6.6 %shard_map.112 = (bf16[576,192]{1,0:T(8,128)(2,1)S(1)}, bf16[2,504,192]{2,1,0:T(8,128)(2,1)S(1)}, bf16[2,72,192]{2,1,0:T(8,128)(2,1)S(1)}, bf16[576,576]{1,0:T(8...) custom-call(bf16[2,12,24,192]{3,2,1,0:T(8,128)(2,1)} %tokens_in.1, ...), custom_call_target="tpu_custom_call" | custom-call | flops 8800000000 | bytes 100000 | tf_op jit(solution)/shard_map/pallas_call | solution.py:695
  7.2 0.5 collective-permute-start.1
  7.7 5.6 %collective-permute-start.2 = (bf16[2,72,192]{2,1,0:T(8,128)(2,1)S(1)}, bf16[2,72,192]{2,1,0:T(8,128)(2,1)S(1)}, u32[]{:S(2)}, u32[]{:S(2)}) collective-permute-start(bf16[2,72,192]{2,1,0:T(8,128)(2,1)S(1)} %get-tuple-element.53), channel_id=1, source_target_pairs={{0,15},{1,14},{2,1},{3,0},{4,3},{5,2},{6,5},{7,4},{8,7},{9,6},{10,... | collective-permute-start | bytes 165896 | tf_op jit(solution)/shard_map/ppermute | solution.py:739
  13.4 0.5 collective-permute-start
  13.9 0.0 copy-start.2
  13.9 0.0 copy-start.4
  14.0 2.0 %shard_map.113 = (f32[864,144]{1,0:T(8,128)S(1)}, bf16[576,768]{1,0:T(8,128)(2,1)S(1)}) custom-call(f32[2,6,1,6336]{3,2,1,0:T(1,128)S(1)} %bitcast.8, bf16[2,132,384]{2,1,0:T(8,128)(2,1)S(1)} %copy-done.6, f32[576,768]{1,0:T(8,128)S(1)} %get-tuple-element.54.hidden), custom_call_target="tpu_custom_call" | custom-call | flops 3300000000 | bytes 100000 | tf_op jit(solution)/shard_map/pallas_call | solution.py:695
  15.9 0.0 collective-permute-done.2.diag_head
  16.0 1.8 %collective-permute-done.lon_head = bf16[2,72,192]{2,1,0:T(8,128)(2,1)S(1)} collective-permute-done((bf16[2,72,192]{2,1,0:T(8,128)(2,1)S(1)}, bf16[2,72,192]{2,1,0:T(8,128)(2,1)S(1)}, u32[]{:S(2)}, u32[]{:S(2)}) %collective-permute-start) | collective-permute-done | bytes 55328 | tf_op jit(solution)/shard_map/ppermute | solution.py:725
  17.8 8.9 %shard_map.114 = (bf16[504,192]{1,0:T(8,128)(2,1)S(1)}, bf16[72,192]{1,0:T(8,128)(2,1)S(1)}, bf16[576,192]{1,0:T(8,128)(2,1)S(1)}, bf16[576,576]{1,0:T(8,128)(2,...) custom-call(bf16[2,504,192]{2,1,0:T(8,128)(2,1)S(1)} %get-tuple-elem, ...), custom_call_target="tpu_custom_call", output_to_operand_aliasing={{12}: (10, {}), {13}: (11, {}), {14}: (12, {}), {15}: (13, ... | custom-call | flops 20899999744 | bytes 100000 | tf_op jit(solution)/shard_map/pallas_call | solution.py:695
  26.7 0.7 copy-done.13
  27.4 1.6 %shard_map.115 = (bf16[8,27,8,128]{3,2,1,0:T(8,128)(2,1)S(1)}, bf16[8,27,8,128]{3,2,1,0:T(8,128)(2,1)S(1)}, bf16[8,5,8,128]{3,2,1,0:T(8,128)(2,1)S(1)}) custom-call(bf16[576,192]{1,0:T(8,128)(2,1)S(1)} %get-tuple-element.72.n1, bf16[576,576]{1,0:T(8,128)(2,1)S(1)} %get-tuple-element.73.field, bf16[576,192]{1,0:T(8,128)(2,1)S(1)} %get-tuple-element.74.mixed, ...), custom_call_target="tpu_custom_call" | custom-call | flops 3300000000 | bytes 100000 | tf_op jit(solution)/shard_map/pallas_call | solution.py:695
  29.1 0.6 copy-done.11
  29.7 0.3 copy-done.15
  30.0 0.0 copy-done.17
  30.1 0.5 collective-permute-start.4
  30.6 1.3 %collective-permute-done.6.refs_1_ = bf16[8,27,8,128]{3,2,1,0:T(8,128)(2,1)S(1)} collective-permute-done((bf16[8,27,8,128]{3,2,1,0:T(8,128)(2,1)S(1)}, bf16[8,27,8,128]{3,2,1,0:T(8,128)(2,1)S(1)}, u32[]{:S(2)}, u32[]{:S(2)}) %collective-permute-start.6) | collective-permute-done | bytes 442400 | tf_op jit(solution)/shard_map/ppermute | solution.py:720
  31.9 0.9 shard_map.116.order
  32.8 6.1 %all-to-all-start = ((bf16[8,32,8,128]{3,2,1,0:T(8,128)(2,1)}), bf16[8,32,8,128]{3,2,1,0:T(8,128)(2,1)S(1)}, u32[]{:S(2)}, u32[]{:S(2)}) async-start(bf16[8,32,8,128]{3,2,1,0:T(8,128)(2,1)} %shard_map.116.order), calls=%async_computation | async-start | bytes 1048576 | tf_op jit(solution)/shard_map/all_to_all | solution.py:901
  38.9 1.2 %copy-done.8 = bf16[576,768]{1,0:T(8,128)(2,1)S(1)} copy-done((bf16[576,768]{1,0:T(8,128)(2,1)S(1)}, bf16[576,768]{1,0:T(8,128)(2,1)}, u32[]{:S(2)}) %copy-start.8) | copy-done | bytes 884760
  40.0 1.2 %copy-done.10 = bf16[576,768]{1,0:T(8,128)(2,1)S(1)} copy-done((bf16[576,768]{1,0:T(8,128)(2,1)S(1)}, bf16[576,768]{1,0:T(8,128)(2,1)}, u32[]{:S(2)}) %copy-start.10) | copy-done | bytes 884760
  41.2 1.0 copy-done.14
  42.2 3.3 %shard_map.117 = (bf16[8,21,8,128]{3,2,1,0:T(8,128)(2,1)S(1)}, bf16[8,21,8,128]{3,2,1,0:T(8,128)(2,1)S(1)}, f32[576,192]{1,0:T(8,128)S(1)}, bf16[576,192]{1,0:T(8,128)(2,1)S(1)}, f32[1,192]{1,0:T(1,128)S(1)}) custom-call(bf16[504,192]{1,0:T(8,128)(2,1)S(1)} %get-tuple-element.66.head, bf16[72,192]{1,0:T(8,128)(2,1)S(1)} %collective-permute-done.3.lon_tail, ...), custom_call_target="tpu_custom_call" | custom-call | flops 3300000000 | bytes 100000 | tf_op jit(solution)/shard_map/pallas_call | solution.py:695
  45.5 0.1 collective-permute-start.7
  45.6 6.0 %shard_map.118 = (bf16[2,12,24,192]{3,2,1,0:T(8,128)(2,1)}, bf16[8,7,8,128]{3,2,1,0:T(8,128)(2,1)S(1)}, bf16[8,7,8,128]{3,2,1,0:T(8,128)(2,1)S(1)}, bf16[8,5,8,128]{3,2,1,0:T(8,128)(2,1)S(1)}) custom-call(bf16[576,192]{1,0:T(8,128)(2,1)S(1)} %copy-done.18, bf16[576,576]{1,0:T(8,128)(2,1)S(1)} %copy-done.16, f32[4,6,144,144]{3,2,1,0:T(8,128)S(1)} %copy-done.12, ...), custom_call_target="tpu_custom_call" | custom-call | flops 7699999744 | bytes 100000 | tf_op jit(solution)/shard_map/pallas_call | solution.py:695
  51.6 0.5 collective-permute-start.8
  52.1 1.0 collective-permute-done.8.refs_3_
  53.0 0.1 shard_map.119
  53.1 2.1 %collective-permute-start.12 = (bf16[4,33,8,128]{3,2,1,0:T(8,128)(2,1)S(1)}, bf16[4,33,8,128]{3,2,1,0:T(8,128)(2,1)S(1)}, u32[]{:S(2)}, u32[]{:S(2)}) collective-permute-start(bf16[4,33,8,128]{3,2,1,0:T(8,128)(2,1)S(1)} %get-tuple-element.95), channel_id=1, source_target_pairs={{0,2},{2,0},{4,6},{6,4},{8,10},{10,8},{12,14},{14,12},{1,3},{3,1},... | collective-permute-start | bytes 811016 | tf_op jit(solution)/shard_map/ppermute | solution.py:730
  55.2 0.1 shard_map.120.refs_0_
  55.3 1.5 %collective-permute-start.9 = (bf16[32,8,128]{2,1,0:T(8,128)(2,1)S(1)}, bf16[32,8,128]{2,1,0:T(8,128)(2,1)S(1)}, u32[]{:S(2)}, u32[]{:S(2)}) collective-permute-start(bf16[32,8,128]{2,1,0:T(8,128)(2,1)S(1)} %shard_map.120.refs_0_), channel_id=1, source_target_pairs={{0,4},{2,6},{4,8},{6,10},{8,12},{10,14},{12,0},{14,2},{1,5},{3,7},... | collective-permute-start | bytes 196616 | tf_op jit(solution)/shard_map/ppermute | solution.py:725
  56.8 2.4 %collective-permute-start.11 = (bf16[32,8,128]{2,1,0:T(8,128)(2,1)S(1)}, bf16[32,8,128]{2,1,0:T(8,128)(2,1)S(1)}, u32[]{:S(2)}, u32[]{:S(2)}) collective-permute-start(bf16[32,8,128]{2,1,0:T(8,128)(2,1)S(1)} %shard_map.120.refs_0_), channel_id=1, source_target_pairs={{0,12},{2,14},{4,0},{6,2},{8,4},{10,6},{12,8},{14,10},{1,13},{3,15... | collective-permute-start | bytes 196616 | tf_op jit(solution)/shard_map/ppermute | solution.py:725
  59.2 0.6 collective-permute-start.10
  59.8 2.5 %collective-permute-done.12.got = bf16[4,33,8,128]{3,2,1,0:T(8,128)(2,1)S(1)} collective-permute-done((bf16[4,33,8,128]{3,2,1,0:T(8,128)(2,1)S(1)}, bf16[4,33,8,128]{3,2,1,0:T(8,128)(2,1)S(1)}, u32[]{:S(2)}, u32[]{:S(2)}) %collective-permute-start.12) | collective-permute-done | bytes 270368 | tf_op jit(solution)/shard_map/ppermute | solution.py:730
  62.2 0.8 shard_map.121.refs_4_
  63.0 4.8 %all-to-all-start.1 = ((bf16[4,33,8,128]{3,2,1,0:T(8,128)(2,1)}), bf16[4,33,8,128]{3,2,1,0:T(8,128)(2,1)S(1)}, u32[]{:S(2)}, u32[]{:S(2)}) async-start(bf16[4,33,8,128]{3,2,1,0:T(8,128)(2,1)} %shard_map.121.refs_4_), calls=%async_computation.1 | async-start | bytes 540672 | tf_op jit(solution)/shard_map/all_to_all | solution.py:957
  67.8 1.0 shard_map.122.same
  68.8 1.5 %collective-permute-start.13 = (bf16[4,32,8,128]{3,2,1,0:T(8,128)(2,1)S(1)}, bf16[4,32,8,128]{3,2,1,0:T(8,128)(2,1)S(1)}, u32[]{:S(2)}, u32[]{:S(2)}) collective-permute-start(bf16[4,32,8,128]{3,2,1,0:T(8,128)(2,1)S(1)} %shard_map.122.same), channel_id=1, source_target_pairs={{0,2},{2,0},{4,6},{6,4},{8,10},{10,8},{12,14},{14,12},{1,3},{3,1},... | collective-permute-start | bytes 786440 | tf_op jit(solution)/shard_map/ppermute | solution.py:730
  70.4 6.0 %collective-permute-done.13.same_x.order = bf16[4,32,8,128]{3,2,1,0:T(8,128)(2,1)S(1)} collective-permute-done((bf16[4,32,8,128]{3,2,1,0:T(8,128)(2,1)S(1)}, bf16[4,32,8,128]{3,2,1,0:T(8,128)(2,1)S(1)}, u32[]{:S(2)}, u32[]{:S(2)}) %collective-permute-start.13) | collective-permute-done | bytes 262176 | tf_op jit(solution)/shard_map/ppermute | solution.py:730
  76.4 0.2 all-to-all-done.1.pieces
  76.6 0.1 shard_map.124
  76.6 19.2 %all_to_all.15.own_bc = bf16[8,33,8,128]{3,2,1,0:T(8,128)(2,1)S(1)} all-to-all(bf16[8,33,8,128]{3,2,1,0:T(8,128)(2,1)S(1)} %shard_map.124), channel_id=1, replica_groups=mesh['grp'=2,'lon'=8,'lat'=2] {'lon'}, dimensions={0} | all-to-all | bytes 1081344 | tf_op jit(solution)/shard_map/all_to_all | solution.py:977
  95.9 0.5 collective-permute-start.14
  96.4 1.8 %collective-permute-done.14.cross = bf16[4,32,8,128]{3,2,1,0:T(8,128)(2,1)S(1)} collective-permute-done((bf16[4,32,8,128]{3,2,1,0:T(8,128)(2,1)S(1)}, bf16[4,32,8,128]{3,2,1,0:T(8,128)(2,1)S(1)}, u32[]{:S(2)}, u32[]{:S(2)}) %collective-permute-start.14) | collective-permute-done | bytes 262176 | tf_op jit(solution)/shard_map/ppermute | solution.py:720
  98.2 0.4 collective-permute-done.15.cross_x
  98.5 0.6 shard_map.123
  99.2 2.4 %shard_map.125 = (bf16[6918,128]{1,0:T(8,128)(2,1)}, f32[2,6,1,6336]{3,2,1,0:T(1,128)}) custom-call(bf16[2,132,384]{2,1,0:T(8,128)(2,1)S(1)} %copy-done.6, f32[3456,128]{1,0:T(8,128)S(1)} %get-tuple-element.96.flat_a, f32[8,128]{1,0:T(8,128)S(1)} %get-tuple-element.97.squares, f32[6,1,6336]{2,1,0:T(1,128)S(1)} %get-tuple-element.98.bias_late, ...), custom_call_target="tpu_custom_call" | custom-call | flops 2200000000 | bytes 100000 | tf_op jit(solution)/shard_map/pallas_call | solution.py:695
  (43 shorter events, 0.1 us)
Async XLA Ops:
  0.6 13.3 %copy-start.3 = (f32[2,1,6,6336]{3,1,2,0:T(1,128)S(1)}, f32[2,1,6,6336]{3,1,2,0:T(1,128)}, u32[]{:S(2)}) copy-start(f32[2,1,6,6336]{3,1,2,0:T(1,128)} %param.16) | copy-start | bytes 912388
  0.6 13.3 %copy-start.6 = (bf16[2,132,384]{2,1,0:T(8,128)(2,1)S(1)}, bf16[2,132,384]{2,1,0:T(8,128)(2,1)}, u32[]{:S(2)}) copy-start(bf16[2,132,384]{2,1,0:T(8,128)(2,1)} %constant.2.clone.spread_in.spread) | copy-start | bytes 608260
  7.2 10.5 %collective-permute-start.1 = (bf16[2,504,192]{2,1,0:T(8,128)(2,1)S(1)}, bf16[2,504,192]{2,1,0:T(8,128)(2,1)S(1)}, u32[]{:S(2)}, u32[]{:S(2)}) collective-permute-start(bf16[2,504,192]{2,1,0:T(8,128)(2,1)S(1)} %get-tuple-element.52.tail), channel_id=1, source_target_pairs={{0,1},{1,0},{2,3},{3,2},{4,5},{5,4},{6,7},{7,6},{8,9},{9,8},{10,11... | collective-permute-start | bytes 1161224 | tf_op jit(solution)/shard_map/ppermute | solution.py:720
  7.7 8.2 %collective-permute-start.2 = (bf16[2,72,192]{2,1,0:T(8,128)(2,1)S(1)}, bf16[2,72,192]{2,1,0:T(8,128)(2,1)S(1)}, u32[]{:S(2)}, u32[]{:S(2)}) collective-permute-start(bf16[2,72,192]{2,1,0:T(8,128)(2,1)S(1)} %get-tuple-element.53), channel_id=1, source_target_pairs={{0,15},{1,14},{2,1},{3,0},{4,3},{5,2},{6,5},{7,4},{8,7},{9,6},{10,... | collective-permute-start | bytes 165896 | tf_op jit(solution)/shard_map/ppermute | solution.py:739
  13.4 4.4 %collective-permute-start = (bf16[2,72,192]{2,1,0:T(8,128)(2,1)S(1)}, bf16[2,72,192]{2,1,0:T(8,128)(2,1)S(1)}, u32[]{:S(2)}, u32[]{:S(2)}) collective-permute-start(bf16[2,72,192]{2,1,0:T(8,128)(2,1)S(1)} %get-tuple-element.53), channel_id=1, source_target_pairs={{0,14},{2,0},{4,2},{6,4},{8,6},{10,8},{12,10},{14,12},{1,15},{3,1}... | collective-permute-start | bytes 165896 | tf_op jit(solution)/shard_map/ppermute | solution.py:725
  13.9 3.8 %copy-start = (bf16[2,192,768]{2,1,0:T(8,128)(2,1)S(1)}, bf16[2,192,768]{2,1,0:T(8,128)(2,1)}, u32[]{:S(2)}) copy-start(bf16[2,192,768]{2,1,0:T(8,128)(2,1)} %up_w.3) | copy-start | bytes 1769476
  13.9 3.8 %copy-start.1 = (bf16[2,768,192]{1,2,0:T(8,128)(2,1)S(1)}, bf16[2,768,192]{1,2,0:T(8,128)(2,1)}, u32[]{:S(2)}) copy-start(bf16[2,768,192]{1,2,0:T(8,128)(2,1)} %param.14) | copy-start | bytes 1769476
  13.9 3.8 %copy-start.2 = (bf16[2,192,576]{2,1,0:T(8,128)(2,1)S(1)}, bf16[2,192,576]{2,1,0:T(8,128)(2,1)}, u32[]{:S(2)}) copy-start(bf16[2,192,576]{2,1,0:T(8,128)(2,1)} %qkv_w.3) | copy-start | bytes 1327108
  13.9 3.8 %copy-start.4 = (bf16[2,192,192]{2,1,0:T(8,128)(2,1)S(1)}, bf16[2,192,192]{2,1,0:T(8,128)(2,1)}, u32[]{:S(2)}) copy-start(bf16[2,192,192]{2,1,0:T(8,128)(2,1)} %proj_w.3) | copy-start | bytes 442372
  14.0 3.8 %copy-start.5 = (f32[2,2,192]{2,1,0:T(2,128)S(1)}, f32[2,2,192]{2,1,0:T(2,128)}, u32[]{:S(2)}) copy-start(f32[2,2,192]{2,1,0:T(2,128)} %gains.5) | copy-start | bytes 9220
  26.7 0.7 copy-start.13
  27.4 1.7 %copy-start.7 = (bf16[576,768]{1,0:T(8,128)(2,1)}, bf16[576,768]{1,0:T(8,128)(2,1)S(1)}, u32[]{:S(2)}) copy-start(bf16[576,768]{1,0:T(8,128)(2,1)S(1)} %get-tuple-element.70.active) | copy-start | bytes 2654212
  27.4 1.7 %copy-start.9 = (bf16[576,768]{1,0:T(8,128)(2,1)}, bf16[576,768]{1,0:T(8,128)(2,1)S(1)}, u32[]{:S(2)}) copy-start(bf16[576,768]{1,0:T(8,128)(2,1)S(1)} %get-tuple-element.69.slope) | copy-start | bytes 2654212
  27.4 2.3 %copy-start.11 = (f32[4,6,144,144]{3,2,1,0:T(8,128)}, f32[4,6,144,144]{3,2,1,0:T(8,128)S(1)}, u32[]{:S(2)}) copy-start(f32[4,6,144,144]{3,2,1,0:T(8,128)S(1)} %get-tuple-element.65.probs) | copy-start | bytes 5971972
  27.4 2.6 %copy-start.15 = (bf16[576,576]{1,0:T(8,128)(2,1)}, bf16[576,576]{1,0:T(8,128)(2,1)S(1)}, u32[]{:S(2)}) copy-start(bf16[576,576]{1,0:T(8,128)(2,1)S(1)} %get-tuple-element.64.qkv) | copy-start | bytes 1990660
  27.4 2.7 %copy-start.17 = (bf16[576,192]{1,0:T(8,128)(2,1)}, bf16[576,192]{1,0:T(8,128)(2,1)S(1)}, u32[]{:S(2)}) copy-start(bf16[576,192]{1,0:T(8,128)(2,1)S(1)} %get-tuple-element.63.x_in) | copy-start | bytes 663556
  30.1 1.8 %collective-permute-start.6 = (bf16[8,27,8,128]{3,2,1,0:T(8,128)(2,1)S(1)}, bf16[8,27,8,128]{3,2,1,0:T(8,128)(2,1)S(1)}, u32[]{:S(2)}, u32[]{:S(2)}) collective-permute-start(bf16[8,27,8,128]{3,2,1,0:T(8,128)(2,1)S(1)} %get-tuple-element.82), channel_id=1, source_target_pairs={{0,1},{1,0},{2,3},{3,2},{4,5},{5,4},{6,7},{7,6},{8,9},{9,8},{10,11... | collective-permute-start | bytes 1327112 | tf_op jit(solution)/shard_map/ppermute | solution.py:720
  30.1 8.8 %collective-permute-start.4 = (bf16[504,192]{1,0:T(8,128)(2,1)S(1)}, bf16[504,192]{1,0:T(8,128)(2,1)S(1)}, u32[]{:S(2)}, u32[]{:S(2)}) collective-permute-start(bf16[504,192]{1,0:T(8,128)(2,1)S(1)} %get-tuple-element.66.head), channel_id=1, source_target_pairs={{0,1},{1,0},{2,3},{3,2},{4,5},{5,4},{6,7},{7,6},{8,9},{9,8},{10,11... | collective-permute-start | bytes 580616 | tf_op jit(solution)/shard_map/ppermute | solution.py:720
  30.6 8.3 %collective-permute-start.5 = (bf16[72,192]{1,0:T(8,128)(2,1)S(1)}, bf16[72,192]{1,0:T(8,128)(2,1)S(1)}, u32[]{:S(2)}, u32[]{:S(2)}) collective-permute-start(bf16[72,192]{1,0:T(8,128)(2,1)S(1)} %get-tuple-element.67), channel_id=1, source_target_pairs={{0,3},{1,2},{2,5},{3,4},{4,7},{5,6},{6,9},{7,8},{8,11},{9,10},{10,... | collective-permute-start | bytes 82952 | tf_op jit(solution)/shard_map/ppermute | solution.py:739
  30.6 8.3 %collective-permute-start.3 = (bf16[72,192]{1,0:T(8,128)(2,1)S(1)}, bf16[72,192]{1,0:T(8,128)(2,1)S(1)}, u32[]{:S(2)}, u32[]{:S(2)}) collective-permute-start(bf16[72,192]{1,0:T(8,128)(2,1)S(1)} %get-tuple-element.67), channel_id=1, source_target_pairs={{0,2},{2,4},{4,6},{6,8},{8,10},{10,12},{12,14},{14,0},{1,3},{3,5},... | collective-permute-start | bytes 82952 | tf_op jit(solution)/shard_map/ppermute | solution.py:725
  32.8 22.5 %all-to-all-start = ((bf16[8,32,8,128]{3,2,1,0:T(8,128)(2,1)}), bf16[8,32,8,128]{3,2,1,0:T(8,128)(2,1)S(1)}, u32[]{:S(2)}, u32[]{:S(2)}) async-start(bf16[8,32,8,128]{3,2,1,0:T(8,128)(2,1)} %shard_map.116.order), calls=%async_computation | async-start | bytes 1048576 | tf_op jit(solution)/shard_map/all_to_all | solution.py:901
  38.9 1.2 %copy-start.8 = (bf16[576,768]{1,0:T(8,128)(2,1)S(1)}, bf16[576,768]{1,0:T(8,128)(2,1)}, u32[]{:S(2)}) copy-start(bf16[576,768]{1,0:T(8,128)(2,1)} %copy-done.7) | copy-start | bytes 2654212
  40.0 1.2 %copy-start.10 = (bf16[576,768]{1,0:T(8,128)(2,1)S(1)}, bf16[576,768]{1,0:T(8,128)(2,1)}, u32[]{:S(2)}) copy-start(bf16[576,768]{1,0:T(8,128)(2,1)} %copy-done.9) | copy-start | bytes 2654212
  41.2 1.0 copy-start.14
  42.2 3.4 %copy-start.12 = (f32[4,6,144,144]{3,2,1,0:T(8,128)S(1)}, f32[4,6,144,144]{3,2,1,0:T(8,128)}, u32[]{:S(2)}) copy-start(f32[4,6,144,144]{3,2,1,0:T(8,128)} %copy-done.11) | copy-start | bytes 5971972
  42.2 3.4 %copy-start.16 = (bf16[576,576]{1,0:T(8,128)(2,1)S(1)}, bf16[576,576]{1,0:T(8,128)(2,1)}, u32[]{:S(2)}) copy-start(bf16[576,576]{1,0:T(8,128)(2,1)} %copy-done.15) | copy-start | bytes 1990660
  42.2 3.4 %copy-start.18 = (bf16[576,192]{1,0:T(8,128)(2,1)S(1)}, bf16[576,192]{1,0:T(8,128)(2,1)}, u32[]{:S(2)}) copy-start(bf16[576,192]{1,0:T(8,128)(2,1)} %copy-done.17) | copy-start | bytes 663556
  45.5 7.5 %collective-permute-start.7 = (bf16[8,21,8,128]{3,2,1,0:T(8,128)(2,1)S(1)}, bf16[8,21,8,128]{3,2,1,0:T(8,128)(2,1)S(1)}, u32[]{:S(2)}, u32[]{:S(2)}) collective-permute-start(bf16[8,21,8,128]{3,2,1,0:T(8,128)(2,1)S(1)} %get-tuple-element.90), channel_id=1, source_target_pairs={{0,1},{1,0},{2,3},{3,2},{4,5},{5,4},{6,7},{7,6},{8,9},{9,8},{10,11... | collective-permute-start | bytes 1032200 | tf_op jit(solution)/shard_map/ppermute | solution.py:720
  51.6 1.4 %collective-permute-start.8 = (bf16[8,7,8,128]{3,2,1,0:T(8,128)(2,1)S(1)}, bf16[8,7,8,128]{3,2,1,0:T(8,128)(2,1)S(1)}, u32[]{:S(2)}, u32[]{:S(2)}) collective-permute-start(bf16[8,7,8,128]{3,2,1,0:T(8,128)(2,1)S(1)} %get-tuple-element.92), channel_id=1, source_target_pairs={{0,1},{1,0},{2,3},{3,2},{4,5},{5,4},{6,7},{7,6},{8,9},{9,8},{10,11... | collective-permute-start | bytes 344072 | tf_op jit(solution)/shard_map/ppermute | solution.py:720
  53.1 9.1 %collective-permute-start.12 = (bf16[4,33,8,128]{3,2,1,0:T(8,128)(2,1)S(1)}, bf16[4,33,8,128]{3,2,1,0:T(8,128)(2,1)S(1)}, u32[]{:S(2)}, u32[]{:S(2)}) collective-permute-start(bf16[4,33,8,128]{3,2,1,0:T(8,128)(2,1)S(1)} %get-tuple-element.95), channel_id=1, source_target_pairs={{0,2},{2,0},{4,6},{6,4},{8,10},{10,8},{12,14},{14,12},{1,3},{3,1},... | collective-permute-start | bytes 811016 | tf_op jit(solution)/shard_map/ppermute | solution.py:730
  55.3 6.9 %collective-permute-start.9 = (bf16[32,8,128]{2,1,0:T(8,128)(2,1)S(1)}, bf16[32,8,128]{2,1,0:T(8,128)(2,1)S(1)}, u32[]{:S(2)}, u32[]{:S(2)}) collective-permute-start(bf16[32,8,128]{2,1,0:T(8,128)(2,1)S(1)} %shard_map.120.refs_0_), channel_id=1, source_target_pairs={{0,4},{2,6},{4,8},{6,10},{8,12},{10,14},{12,0},{14,2},{1,5},{3,7},... | collective-permute-start | bytes 196616 | tf_op jit(solution)/shard_map/ppermute | solution.py:725
  56.8 11.0 %collective-permute-start.11 = (bf16[32,8,128]{2,1,0:T(8,128)(2,1)S(1)}, bf16[32,8,128]{2,1,0:T(8,128)(2,1)S(1)}, u32[]{:S(2)}, u32[]{:S(2)}) collective-permute-start(bf16[32,8,128]{2,1,0:T(8,128)(2,1)S(1)} %shard_map.120.refs_0_), channel_id=1, source_target_pairs={{0,12},{2,14},{4,0},{6,2},{8,4},{10,6},{12,8},{14,10},{1,13},{3,15... | collective-permute-start | bytes 196616 | tf_op jit(solution)/shard_map/ppermute | solution.py:725
  59.2 8.6 %collective-permute-start.10 = (bf16[32,8,128]{2,1,0:T(8,128)(2,1)S(1)}, bf16[32,8,128]{2,1,0:T(8,128)(2,1)S(1)}, u32[]{:S(2)}, u32[]{:S(2)}) collective-permute-start(bf16[32,8,128]{2,1,0:T(8,128)(2,1)S(1)} %shard_map.120.refs_0_), channel_id=1, source_target_pairs={{0,8},{2,10},{4,12},{6,14},{8,0},{10,2},{12,4},{14,6},{1,9},{3,11}... | collective-permute-start | bytes 196616 | tf_op jit(solution)/shard_map/ppermute | solution.py:725
  63.0 13.6 %all-to-all-start.1 = ((bf16[4,33,8,128]{3,2,1,0:T(8,128)(2,1)}), bf16[4,33,8,128]{3,2,1,0:T(8,128)(2,1)S(1)}, u32[]{:S(2)}, u32[]{:S(2)}) async-start(bf16[4,33,8,128]{3,2,1,0:T(8,128)(2,1)} %shard_map.121.refs_4_), calls=%async_computation.1 | async-start | bytes 540672 | tf_op jit(solution)/shard_map/all_to_all | solution.py:957
  68.8 7.5 %collective-permute-start.13 = (bf16[4,32,8,128]{3,2,1,0:T(8,128)(2,1)S(1)}, bf16[4,32,8,128]{3,2,1,0:T(8,128)(2,1)S(1)}, u32[]{:S(2)}, u32[]{:S(2)}) collective-permute-start(bf16[4,32,8,128]{3,2,1,0:T(8,128)(2,1)S(1)} %shard_map.122.same), channel_id=1, source_target_pairs={{0,2},{2,0},{4,6},{6,4},{8,10},{10,8},{12,14},{14,12},{1,3},{3,1},... | collective-permute-start | bytes 786440 | tf_op jit(solution)/shard_map/ppermute | solution.py:730
  95.9 3.3 %collective-permute-start.16 = (bf16[8,33,8,128]{3,2,1,0:T(8,128)(2,1)S(1)}, bf16[8,33,8,128]{3,2,1,0:T(8,128)(2,1)S(1)}, u32[]{:S(2)}, u32[]{:S(2)}) collective-permute-start(bf16[8,33,8,128]{3,2,1,0:T(8,128)(2,1)S(1)} %all_to_all.15.own_bc), channel_id=1, source_target_pairs={{0,1},{1,0},{2,3},{3,2},{4,5},{5,4},{6,7},{7,6},{8,9},{9,8},{10,11... | collective-permute-start | bytes 1622024 | tf_op jit(solution)/shard_map/ppermute | solution.py:720
  95.9 2.3 %collective-permute-start.14 = (bf16[4,32,8,128]{3,2,1,0:T(8,128)(2,1)S(1)}, bf16[4,32,8,128]{3,2,1,0:T(8,128)(2,1)S(1)}, u32[]{:S(2)}, u32[]{:S(2)}) collective-permute-start(bf16[4,32,8,128]{3,2,1,0:T(8,128)(2,1)S(1)} %shard_map.122.same), channel_id=1, source_target_pairs={{0,1},{1,0},{2,3},{3,2},{4,5},{5,4},{6,7},{7,6},{8,9},{9,8},{10,11... | collective-permute-start | bytes 786440 | tf_op jit(solution)/shard_map/ppermute | solution.py:720
  96.4 2.2 %collective-permute-start.15 = (bf16[4,32,8,128]{3,2,1,0:T(8,128)(2,1)S(1)}, bf16[4,32,8,128]{3,2,1,0:T(8,128)(2,1)S(1)}, u32[]{:S(2)}, u32[]{:S(2)}) collective-permute-start(bf16[4,32,8,128]{3,2,1,0:T(8,128)(2,1)S(1)} %collective-permute-done.13.same_x.order), channel_id=1, source_target_pairs={{0,1},{1,0},{2,3},{3,2},{4,5},{5,4},{6,7},{7,6},{8,9},{9,8},{10,11... | collective-permute-start | bytes 786440 | tf_op jit(solution)/shard_map/ppermute | solution.py:720

commit v13 on v12

--- a/solution.py
+++ b/solution.py
@@ -482,17 +482,6 @@
     bias_units(sums, bias_out)
 
 
-def lat_sums(*refs):
-    out = refs[-1]
-    at = 0
-    for k in range(0, len(refs) - 2, 2):
-        keep, got = refs[k], refs[k + 1]
-        count = keep.shape[1]
-        out[:, at : at + count] = (keep[...].astype(F32) + got[...].astype(F32)).astype(BF16)
-        at += count
-    out[:, at:] = refs[-2][...]
-
-
 def lat_sums_split(*refs):
     keep_out, give_out = refs[-2:]
     x = lax.rem(lax.axis_index("lon"), 2)
@@ -507,6 +496,21 @@
                 out[z, at : at + count] = total.astype(BF16)
                 at += count
             out[z, at:] = refs[-3][j]
+
+
+def split_z(keep, got, order, own_out, *give_outs):
+    count = keep.shape[0]
+    z = lax.div(lax.axis_index("lon"), 2)
+    for k, out in enumerate((own_out,) + give_outs):
+        at = lax.rem(z + k, count)
+        out[...] = (keep[at].astype(F32) + got[at].astype(F32)).astype(BF16)
+
+
+def sum_refs(*refs):
+    total = refs[0][...].astype(F32)
+    for ref in refs[1:-2]:
+        total = total + ref[...].astype(F32)
+    refs[-1][...] = total.astype(BF16)
 
 
 def add_pair(keep, got, order, out):
@@ -895,10 +899,11 @@
     )
     got_a = lat_swap(give_a)
 
-    (part_a,) = call(
-        lat_sums, [units(lon_size, units_a + extra)], [], (keep_a, got_a, bias_a), 1, 10
-    )
-    pieces_a = lax.all_to_all(part_a, "lon", 0, 0)
+    units_xa = units_a + extra
+    keep_xa, give_xa = call(
+        lat_sums_split, [units(zs, units_xa)] * 2, [], (keep_a, got_a, bias_a), 1, 10
+    )
+    got_xa = x_swap(give_xa)
 
     keep_b, give_b, rg0, dmix0, gain_two = call(
         third_kernel,
@@ -912,7 +917,7 @@
         [(token, F32), (token, F32), m192, m768, mdown, flat_scr(units_b)],
         (
             dhead, lon_tail, lat_dhead, diag_tail, resid0, slope0, active0, mixed0, proj_weight,
-            up_weight, down_turned, norm_gain, part_a,
+            up_weight, down_turned, norm_gain, keep_xa,
         ),
         3,
         14,
@@ -951,9 +956,11 @@
         10,
     )
     got_x = x_swap(give_x)
-    (sum_a,) = call(sum_pieces, [units(units_a + extra)], [], (pieces_a, keep_x), 1, 10)
-    moved_a = [lon_send(sum_a, 2 * k) for k in range(1, zs)]
-    (part_z,) = call(add_pair, [units(zs, units_bc)], [], (keep_x, got_x, moved_a[0]), 1, 10)
+    own_a, *gives_a = call(
+        split_z, [units(units_xa)] * zs, [], (keep_xa, got_xa, keep_x), 1, 10
+    )
+    gots_a = [lon_send(give, 2 * (k + 1)) for k, give in enumerate(gives_a)]
+    (part_z,) = call(add_pair, [units(zs, units_bc)], [], (keep_x, got_x, gots_a[0]), 1, 10)
     pieces_bc = lax.all_to_all(
         part_z,
         "lon",
@@ -961,18 +968,14 @@
         0,
         axis_index_groups=[[2 * z + x for z in range(zs)] for x in range(2)],
     )
-
-    (same,) = call(join_z, [units(zs, units_a + extra)], [], [sum_a, *moved_a, part_z], 1, 10)
+    (sum_a,) = call(sum_refs, [units(units_xa)], [], (own_a, *gots_a, part_z), 1, 10)
+    moved_a = [lon_send(sum_a, 2 * k) for k in range(1, zs)]
+    (same,) = call(join_z, [units(zs, units_xa)], [], [sum_a, *moved_a, part_z], 1, 10)
     same_x = x_swap(same)
     cross = lat_swap(same)
     cross_x = lat_swap(same_x)
     (sum_bc,) = call(
-        sum_pieces,
-        [units(lon_size, units_bc)],
-        [],
-        (pieces_bc, same_x),
-        1,
-        10,
+        sum_pieces, [units(lon_size, units_bc)], [], (pieces_bc, same), 1, 10
     )
     whole_bc = lax.all_to_all(sum_bc, "lon", 0, 0)
     oth_bc = lat_swap(whole_bc)

time: 102 us -> 110 us (1.078)
  waiting for transfers between devices: 14.9 us -> 49.3 us
  blocking collectives: 19.2 us -> 0 us
  local copies, waits for them, and re-layouts: 5.06 us -> 0.04 us
  starting transfers between devices: 27.2 us -> 25.6 us
    ppermute x5 -> x8, waiting for transfers between devices: 1.76 us -> 21.3 us  [lon_send(): lax.ppermute(value, 'lon', [(s, (s + step) % count) for s in range(count)])]
    all_to_all x1 -> x0, blocking collectives: 19.2 us -> none  [shards(): whole_bc = lax.all_to_all(sum_bc, 'lon', 0, 0)]
    all_to_all x1, waiting for transfers between devices: 0.01 us -> 11.8 us  [shards(): whole_bc = lax.all_to_all(sum_bc, 'lon', 0, 0)]
    unnamed x38 -> x14, local copies, waits for them, and re-layouts: 5.06 us -> 0.04 us
    ppermute x2, waiting for transfers between devices: 0.03 us -> 4.81 us  [diag_send(): return lax.ppermute(value, ('lon', 'lat'), pairs)]
    ppermute x5 -> x8, starting transfers between devices: 4.98 us -> 7.8 us  [lon_send(): lax.ppermute(value, 'lon', [(s, (s + step) % count) for s in range(count)])]
    all_to_all x1, starting transfers between devices: 6.08 us -> 3.54 us  [shards(): whole_bc = lax.all_to_all(sum_bc, 'lon', 0, 0)]
    ppermute x2 -> x3, waiting for transfers between devices: 8.48 us -> 6.95 us  [x_swap(): return lax.ppermute(value, 'lon', [(s, s ^ 1) for s in range(count)])]
  transfers between devices with their start and end apart: 19 -> 23, of which waited for: 8 -> 14; matrix products, arithmetic and copies ran while one was open for 0% -> 0% of each run, Pallas kernels for 15% -> 10%
where the time goes in v13:
time: 110 us
  waiting for transfers between devices  49.3 us (45%)
  Pallas kernels  33.9 us (31%)
  starting transfers between devices  25.6 us (23%)
    pallas_call x15, Pallas kernels, call(): pl.pallas_call(kernel, out_shape=[(pltpu.VMEM if at in near else jax.Shap...  33.9 us
    ppermute x8, waiting for transfers between devices, lon_send(): lax.ppermute(value, 'lon', [(s, (s + step) % count) for s in range(count)])  21.3 us
    all_to_all x1, waiting for transfers between devices, shards(): whole_bc = lax.all_to_all(sum_bc, 'lon', 0, 0)  11.8 us
    ppermute x8, starting transfers between devices, lon_send(): lax.ppermute(value, 'lon', [(s, (s + step) % count) for s in range(count)])  7.8 us
    ppermute x3, waiting for transfers between devices, x_swap(): return lax.ppermute(value, 'lon', [(s, s ^ 1) for s in range(count)])  6.95 us
    ppermute x2, starting transfers between devices, diag_send(): return lax.ppermute(value, ('lon', 'lat'), pairs)  5.64 us
    ppermute x2, waiting for transfers between devices, diag_send(): return lax.ppermute(value, ('lon', 'lat'), pairs)  4.81 us
    ppermute x8, waiting for transfers between devices, lat_swap(): return lax.ppermute(value, 'lat', [(0, 1), (1, 0)])  4.41 us
  transfers between devices with their start and end apart: 23, of which 14 were waited for; matrix products, arithmetic and copies ran while one was open for 0% of the time, Pallas kernels for 10%

profile of v13, /device:TPU:0, one launch (start us, length us, event | category | flops | bytes accessed | tf_op | source)
XLA Modules:
  0.0 109.7 jit_solution(4880424328144806212)
XLA Ops:
  0.7 6.6 %shard_map.112 = (bf16[576,192]{1,0:T(8,128)(2,1)S(1)}, bf16[2,504,192]{2,1,0:T(8,128)(2,1)S(1)}, bf16[2,72,192]{2,1,0:T(8,128)(2,1)S(1)}, bf16[576,576]{1,0:T(8...) custom-call(bf16[2,12,24,192]{3,2,1,0:T(8,128)(2,1)} %tokens_in.1, ...), custom_call_target="tpu_custom_call" | custom-call | flops 8800000000 | bytes 100000 | tf_op jit(solution)/shard_map/pallas_call | solution.py:699
  7.2 0.5 collective-permute-start.1
  7.7 5.6 %collective-permute-start.2 = (bf16[2,72,192]{2,1,0:T(8,128)(2,1)S(1)}, bf16[2,72,192]{2,1,0:T(8,128)(2,1)S(1)}, u32[]{:S(2)}, u32[]{:S(2)}) collective-permute-start(bf16[2,72,192]{2,1,0:T(8,128)(2,1)S(1)} %get-tuple-element.59), channel_id=1, source_target_pairs={{0,15},{1,14},{2,1},{3,0},{4,3},{5,2},{6,5},{7,4},{8,7},{9,6},{10,... | collective-permute-start | bytes 165896 | tf_op jit(solution)/shard_map/ppermute | solution.py:743
  13.4 0.5 collective-permute-start
  14.0 2.0 %shard_map.113 = (f32[864,144]{1,0:T(8,128)S(1)}, bf16[576,768]{1,0:T(8,128)(2,1)S(1)}) custom-call(f32[2,6,1,6336]{3,2,1,0:T(1,128)S(1)} %bitcast.8, bf16[2,132,384]{2,1,0:T(8,128)(2,1)S(1)} %copy-done.6, f32[576,768]{1,0:T(8,128)S(1)} %get-tuple-element.60.hidden), custom_call_target="tpu_custom_call" | custom-call | flops 3300000000 | bytes 100000 | tf_op jit(solution)/shard_map/pallas_call | solution.py:699
  15.9 0.0 collective-permute-done.2.diag_head
  16.0 1.8 %collective-permute-done.lon_head = bf16[2,72,192]{2,1,0:T(8,128)(2,1)S(1)} collective-permute-done((bf16[2,72,192]{2,1,0:T(8,128)(2,1)S(1)}, bf16[2,72,192]{2,1,0:T(8,128)(2,1)S(1)}, u32[]{:S(2)}, u32[]{:S(2)}) %collective-permute-start) | collective-permute-done | bytes 55328 | tf_op jit(solution)/shard_map/ppermute | solution.py:729
  17.8 8.9 %shard_map.114 = (bf16[504,192]{1,0:T(8,128)(2,1)S(1)}, bf16[72,192]{1,0:T(8,128)(2,1)S(1)}, bf16[576,192]{1,0:T(8,128)(2,1)S(1)}, bf16[576,576]{1,0:T(8,128)(2,...) custom-call(bf16[2,504,192]{2,1,0:T(8,128)(2,1)S(1)} %get-tuple-elem, ...), custom_call_target="tpu_custom_call", output_to_operand_aliasing={{12}: (10, {}), {13}: (11, {}), {14}: (12, {}), {15}: (13, ... | custom-call | flops 20899999744 | bytes 100000 | tf_op jit(solution)/shard_map/pallas_call | solution.py:699
  26.7 1.6 %shard_map.115 = (bf16[8,27,8,128]{3,2,1,0:T(8,128)(2,1)S(1)}, bf16[8,27,8,128]{3,2,1,0:T(8,128)(2,1)S(1)}, bf16[8,5,8,128]{3,2,1,0:T(8,128)(2,1)S(1)}) custom-call(bf16[576,192]{1,0:T(8,128)(2,1)S(1)} %get-tuple-element.78.n1, bf16[576,576]{1,0:T(8,128)(2,1)S(1)} %get-tuple-element.79.field, bf16[576,192]{1,0:T(8,128)(2,1)S(1)} %get-tuple-element.80.mixed, ...), custom_call_target="tpu_custom_call" | custom-call | flops 3300000000 | bytes 100000 | tf_op jit(solution)/shard_map/pallas_call | solution.py:699
  28.3 0.1 collective-permute-start.6
  28.4 0.5 collective-permute-start.4
  28.9 1.3 %collective-permute-done.6.refs_1_ = bf16[8,27,8,128]{3,2,1,0:T(8,128)(2,1)S(1)} collective-permute-done((bf16[8,27,8,128]{3,2,1,0:T(8,128)(2,1)S(1)}, bf16[8,27,8,128]{3,2,1,0:T(8,128)(2,1)S(1)}, u32[]{:S(2)}, u32[]{:S(2)}) %collective-permute-start.6) | collective-permute-done | bytes 442400 | tf_op jit(solution)/shard_map/ppermute | solution.py:724
  30.2 0.1 shard_map.116
  30.3 4.8 %collective-permute-done.5.diag_tail = bf16[72,192]{1,0:T(8,128)(2,1)S(1)} collective-permute-done((bf16[72,192]{1,0:T(8,128)(2,1)S(1)}, bf16[72,192]{1,0:T(8,128)(2,1)S(1)}, u32[]{:S(2)}, u32[]{:S(2)}) %collective-permute-start.5) | collective-permute-done | bytes 27680 | tf_op jit(solution)/shard_map/ppermute | solution.py:743
  35.1 1.1 collective-permute-done.3.lon_tail
  36.2 2.2 %shard_map.117 = (bf16[8,21,8,128]{3,2,1,0:T(8,128)(2,1)S(1)}, bf16[8,21,8,128]{3,2,1,0:T(8,128)(2,1)S(1)}, f32[576,192]{1,0:T(8,128)S(1)}, bf16[576,192]{1,0:T(8,128)(2,1)S(1)}, f32[1,192]{1,0:T(1,128)S(1)}) custom-call(bf16[504,192]{1,0:T(8,128)(2,1)S(1)} %get-tuple-element.72.head, bf16[72,192]{1,0:T(8,128)(2,1)S(1)} %collective-permute-done.3.lon_tail, ...), custom_call_target="tpu_custom_call" | custom-call | flops 3300000000 | bytes 100000 | tf_op jit(solution)/shard_map/pallas_call | solution.py:699
  38.4 0.1 collective-permute-start.8
  38.4 5.7 %shard_map.118 = (bf16[2,12,24,192]{3,2,1,0:T(8,128)(2,1)}, bf16[8,7,8,128]{3,2,1,0:T(8,128)(2,1)S(1)}, bf16[8,7,8,128]{3,2,1,0:T(8,128)(2,1)S(1)}, bf16[8,5,8,128]{3,2,1,0:T(8,128)(2,1)S(1)}) custom-call(bf16[576,192]{1,0:T(8,128)(2,1)S(1)} %get-tuple-element.69.x_in, bf16[576,576]{1,0:T(8,128)(2,1)S(1)} %get-tuple-element.70.qkv, ...), custom_call_target="tpu_custom_call" | custom-call | flops 7699999744 | bytes 100000 | tf_op jit(solution)/shard_map/pallas_call | solution.py:699
  44.2 0.5 collective-permute-start.9
  44.7 1.0 collective-permute-done.9.refs_3_
  45.6 0.1 shard_map.119
  45.8 1.1 %collective-permute-start.13 = (bf16[4,33,8,128]{3,2,1,0:T(8,128)(2,1)S(1)}, bf16[4,33,8,128]{3,2,1,0:T(8,128)(2,1)S(1)}, u32[]{:S(2)}, u32[]{:S(2)}) collective-permute-start(bf16[4,33,8,128]{3,2,1,0:T(8,128)(2,1)S(1)} %get-tuple-element.107), channel_id=1, source_target_pairs={{0,2},{2,0},{4,6},{6,4},{8,10},{10,8},{12,14},{14,12},{1,3},{3,1},... | collective-permute-start | bytes 811016 | tf_op jit(solution)/shard_map/ppermute | solution.py:734
  46.9 6.9 %collective-permute-done.7.got = bf16[4,32,8,128]{3,2,1,0:T(8,128)(2,1)S(1)} collective-permute-done((bf16[4,32,8,128]{3,2,1,0:T(8,128)(2,1)S(1)}, bf16[4,32,8,128]{3,2,1,0:T(8,128)(2,1)S(1)}, u32[]{:S(2)}, u32[]{:S(2)}) %collective-permute-start.7) | collective-permute-done | bytes 262176 | tf_op jit(solution)/shard_map/ppermute | solution.py:734
  53.8 0.1 shard_map.120
  53.9 0.1 collective-permute-start.10
  54.0 6.0 %collective-permute-done.10.order.refs_1_ = bf16[32,8,128]{2,1,0:T(8,128)(2,1)S(1)} collective-permute-done((bf16[32,8,128]{2,1,0:T(8,128)(2,1)S(1)}, bf16[32,8,128]{2,1,0:T(8,128)(2,1)S(1)}, u32[]{:S(2)}, u32[]{:S(2)}) %collective-permute-start.10) | collective-permute-done | bytes 65568 | tf_op jit(solution)/shard_map/ppermute | solution.py:729
  60.0 0.8 shard_map.121.refs_4_
  60.8 3.4 %all-to-all-start = ((bf16[4,33,8,128]{3,2,1,0:T(8,128)(2,1)}), bf16[4,33,8,128]{3,2,1,0:T(8,128)(2,1)S(1)}, u32[]{:S(2)}, u32[]{:S(2)}) async-start(bf16[4,33,8,128]{3,2,1,0:T(8,128)(2,1)} %shard_map.121.refs_4_), calls=%async_computation | async-start | bytes 540672 | tf_op jit(solution)/shard_map/all_to_all | solution.py:964
  64.3 2.9 %collective-permute-start.11 = (bf16[32,8,128]{2,1,0:T(8,128)(2,1)S(1)}, bf16[32,8,128]{2,1,0:T(8,128)(2,1)S(1)}, u32[]{:S(2)}, u32[]{:S(2)}) collective-permute-start(bf16[32,8,128]{2,1,0:T(8,128)(2,1)S(1)} %get-tuple-element.105), channel_id=1, source_target_pairs={{0,8},{2,10},{4,12},{6,14},{8,0},{10,2},{12,4},{14,6},{1,9},{3,11}... | collective-permute-start | bytes 196616 | tf_op jit(solution)/shard_map/ppermute | solution.py:729
  67.1 1.5 %collective-permute-start.12 = (bf16[32,8,128]{2,1,0:T(8,128)(2,1)S(1)}, bf16[32,8,128]{2,1,0:T(8,128)(2,1)S(1)}, u32[]{:S(2)}, u32[]{:S(2)}) collective-permute-start(bf16[32,8,128]{2,1,0:T(8,128)(2,1)S(1)} %get-tuple-element.106), channel_id=1, source_target_pairs={{0,12},{2,14},{4,0},{6,2},{8,4},{10,6},{12,8},{14,10},{1,13},{3,15... | collective-permute-start | bytes 196616 | tf_op jit(solution)/shard_map/ppermute | solution.py:729
  68.6 6.5 %collective-permute-done.11.refs_2_ = bf16[32,8,128]{2,1,0:T(8,128)(2,1)S(1)} collective-permute-done((bf16[32,8,128]{2,1,0:T(8,128)(2,1)S(1)}, bf16[32,8,128]{2,1,0:T(8,128)(2,1)S(1)}, u32[]{:S(2)}, u32[]{:S(2)}) %collective-permute-start.11) | collective-permute-done | bytes 65568 | tf_op jit(solution)/shard_map/ppermute | solution.py:729
  75.1 1.0 shard_map.122.refs_0_
  76.1 2.2 %collective-permute-start.16 = (bf16[32,8,128]{2,1,0:T(8,128)(2,1)S(1)}, bf16[32,8,128]{2,1,0:T(8,128)(2,1)S(1)}, u32[]{:S(2)}, u32[]{:S(2)}) collective-permute-start(bf16[32,8,128]{2,1,0:T(8,128)(2,1)S(1)} %shard_map.122.refs_0_), channel_id=1, source_target_pairs={{0,12},{2,14},{4,0},{6,2},{8,4},{10,6},{12,8},{14,10},{1,13},{3,15... | collective-permute-start | bytes 196616 | tf_op jit(solution)/shard_map/ppermute | solution.py:729
  78.3 0.6 collective-permute-start.15
  78.8 0.1 collective-permute-start.14
  78.9 1.5 %collective-permute-done.16.refs_3_ = bf16[32,8,128]{2,1,0:T(8,128)(2,1)S(1)} collective-permute-done((bf16[32,8,128]{2,1,0:T(8,128)(2,1)S(1)}, bf16[32,8,128]{2,1,0:T(8,128)(2,1)S(1)}, u32[]{:S(2)}, u32[]{:S(2)}) %collective-permute-start.16) | collective-permute-done | bytes 65568 | tf_op jit(solution)/shard_map/ppermute | solution.py:729
  80.4 3.5 %collective-permute-done.15.refs_2_ = bf16[32,8,128]{2,1,0:T(8,128)(2,1)S(1)} collective-permute-done((bf16[32,8,128]{2,1,0:T(8,128)(2,1)S(1)}, bf16[32,8,128]{2,1,0:T(8,128)(2,1)S(1)}, u32[]{:S(2)}, u32[]{:S(2)}) %collective-permute-start.15) | collective-permute-done | bytes 65568 | tf_op jit(solution)/shard_map/ppermute | solution.py:729
  83.9 1.0 collective-permute-done.14.refs_1_
  84.9 1.0 shard_map.123.same.order
  85.9 0.9 shard_map.125
  86.8 3.5 %all-to-all-start.1 = ((bf16[8,33,8,128]{3,2,1,0:T(8,128)(2,1)}), bf16[8,33,8,128]{3,2,1,0:T(8,128)(2,1)S(1)}, u32[]{:S(2)}, u32[]{:S(2)}) async-start(bf16[8,33,8,128]{3,2,1,0:T(8,128)(2,1)} %shard_map.125), calls=%async_computation.1 | async-start | bytes 1081344 | tf_op jit(solution)/shard_map/all_to_all | solution.py:980
  90.3 1.9 %collective-permute-start.17 = (bf16[4,32,8,128]{3,2,1,0:T(8,128)(2,1)S(1)}, bf16[4,32,8,128]{3,2,1,0:T(8,128)(2,1)S(1)}, u32[]{:S(2)}, u32[]{:S(2)}) collective-permute-start(bf16[4,32,8,128]{3,2,1,0:T(8,128)(2,1)S(1)} %shard_map.123.same.order), channel_id=1, source_target_pairs={{0,2},{2,0},{4,6},{6,4},{8,10},{10,8},{12,14},{14,12},{1,3},{3,1},... | collective-permute-start | bytes 786440 | tf_op jit(solution)/shard_map/ppermute | solution.py:734
  92.2 11.8 %all-to-all-done.1.own_bc = bf16[8,33,8,128]{3,2,1,0:T(8,128)(2,1)S(1)} async-done(((bf16[8,33,8,128]{3,2,1,0:T(8,128)(2,1)}), bf16[8,33,8,128]{3,2,1,0:T(8,128)(2,1)S(1)}, u32[]{:S(2)}, u32[]{:S(2)}) %all-to-all-start.1) | async-done | bytes 540704 | tf_op jit(solution)/shard_map/all_to_all | solution.py:980
  104.0 0.5 collective-permute-start.18
  104.5 1.8 %collective-permute-done.18.cross = bf16[4,32,8,128]{3,2,1,0:T(8,128)(2,1)S(1)} collective-permute-done((bf16[4,32,8,128]{3,2,1,0:T(8,128)(2,1)S(1)}, bf16[4,32,8,128]{3,2,1,0:T(8,128)(2,1)S(1)}, u32[]{:S(2)}, u32[]{:S(2)}) %collective-permute-start.18) | collective-permute-done | bytes 262176 | tf_op jit(solution)/shard_map/ppermute | solution.py:724
  106.3 0.4 collective-permute-done.19.cross_x
  106.7 0.6 shard_map.124
  107.3 2.4 %shard_map.126 = (bf16[6918,128]{1,0:T(8,128)(2,1)}, f32[2,6,1,6336]{3,2,1,0:T(1,128)}) custom-call(bf16[2,132,384]{2,1,0:T(8,128)(2,1)S(1)} %copy-done.6, f32[3456,128]{1,0:T(8,128)S(1)} %get-tuple-element.108.flat_a, f32[8,128]{1,0:T(8,128)S(1)} %get-tuple-element.109.squares, f32[6,1,6336]{2,1,0:T(1,128)S(1)} %get-tuple-element.110.bias_late, ...), custom_call_target="tpu_custom_call" | custom-call | flops 2200000000 | bytes 100000 | tf_op jit(solution)/shard_map/pallas_call | solution.py:699
  (27 shorter events, 0.1 us)
Async XLA Ops:
  0.6 13.3 %copy-start.3 = (f32[2,1,6,6336]{3,1,2,0:T(1,128)S(1)}, f32[2,1,6,6336]{3,1,2,0:T(1,128)}, u32[]{:S(2)}) copy-start(f32[2,1,6,6336]{3,1,2,0:T(1,128)} %param.16) | copy-start | bytes 912388
  0.6 13.3 %copy-start.6 = (bf16[2,132,384]{2,1,0:T(8,128)(2,1)S(1)}, bf16[2,132,384]{2,1,0:T(8,128)(2,1)}, u32[]{:S(2)}) copy-start(bf16[2,132,384]{2,1,0:T(8,128)(2,1)} %constant.2.clone.spread_in.spread) | copy-start | bytes 608260
  7.2 10.5 %collective-permute-start.1 = (bf16[2,504,192]{2,1,0:T(8,128)(2,1)S(1)}, bf16[2,504,192]{2,1,0:T(8,128)(2,1)S(1)}, u32[]{:S(2)}, u32[]{:S(2)}) collective-permute-start(bf16[2,504,192]{2,1,0:T(8,128)(2,1)S(1)} %get-tuple-element.58.tail), channel_id=1, source_target_pairs={{0,1},{1,0},{2,3},{3,2},{4,5},{5,4},{6,7},{7,6},{8,9},{9,8},{10,11... | collective-permute-start | bytes 1161224 | tf_op jit(solution)/shard_map/ppermute | solution.py:724
  7.7 8.2 %collective-permute-start.2 = (bf16[2,72,192]{2,1,0:T(8,128)(2,1)S(1)}, bf16[2,72,192]{2,1,0:T(8,128)(2,1)S(1)}, u32[]{:S(2)}, u32[]{:S(2)}) collective-permute-start(bf16[2,72,192]{2,1,0:T(8,128)(2,1)S(1)} %get-tuple-element.59), channel_id=1, source_target_pairs={{0,15},{1,14},{2,1},{3,0},{4,3},{5,2},{6,5},{7,4},{8,7},{9,6},{10,... | collective-permute-start | bytes 165896 | tf_op jit(solution)/shard_map/ppermute | solution.py:743
  13.4 4.4 %collective-permute-start = (bf16[2,72,192]{2,1,0:T(8,128)(2,1)S(1)}, bf16[2,72,192]{2,1,0:T(8,128)(2,1)S(1)}, u32[]{:S(2)}, u32[]{:S(2)}) collective-permute-start(bf16[2,72,192]{2,1,0:T(8,128)(2,1)S(1)} %get-tuple-element.59), channel_id=1, source_target_pairs={{0,14},{2,0},{4,2},{6,4},{8,6},{10,8},{12,10},{14,12},{1,15},{3,1}... | collective-permute-start | bytes 165896 | tf_op jit(solution)/shard_map/ppermute | solution.py:729
  13.9 3.8 %copy-start = (bf16[2,192,768]{2,1,0:T(8,128)(2,1)S(1)}, bf16[2,192,768]{2,1,0:T(8,128)(2,1)}, u32[]{:S(2)}) copy-start(bf16[2,192,768]{2,1,0:T(8,128)(2,1)} %up_w.3) | copy-start | bytes 1769476
  13.9 3.8 %copy-start.1 = (bf16[2,768,192]{1,2,0:T(8,128)(2,1)S(1)}, bf16[2,768,192]{1,2,0:T(8,128)(2,1)}, u32[]{:S(2)}) copy-start(bf16[2,768,192]{1,2,0:T(8,128)(2,1)} %param.14) | copy-start | bytes 1769476
  13.9 3.8 %copy-start.2 = (bf16[2,192,576]{2,1,0:T(8,128)(2,1)S(1)}, bf16[2,192,576]{2,1,0:T(8,128)(2,1)}, u32[]{:S(2)}) copy-start(bf16[2,192,576]{2,1,0:T(8,128)(2,1)} %qkv_w.3) | copy-start | bytes 1327108
  13.9 3.8 %copy-start.4 = (bf16[2,192,192]{2,1,0:T(8,128)(2,1)S(1)}, bf16[2,192,192]{2,1,0:T(8,128)(2,1)}, u32[]{:S(2)}) copy-start(bf16[2,192,192]{2,1,0:T(8,128)(2,1)} %proj_w.3) | copy-start | bytes 442372
  14.0 3.8 %copy-start.5 = (f32[2,2,192]{2,1,0:T(2,128)S(1)}, f32[2,2,192]{2,1,0:T(2,128)}, u32[]{:S(2)}) copy-start(f32[2,2,192]{2,1,0:T(2,128)} %gains.5) | copy-start | bytes 9220
  28.3 1.8 %collective-permute-start.6 = (bf16[8,27,8,128]{3,2,1,0:T(8,128)(2,1)S(1)}, bf16[8,27,8,128]{3,2,1,0:T(8,128)(2,1)S(1)}, u32[]{:S(2)}, u32[]{:S(2)}) collective-permute-start(bf16[8,27,8,128]{3,2,1,0:T(8,128)(2,1)S(1)} %get-tuple-element.88), channel_id=1, source_target_pairs={{0,1},{1,0},{2,3},{3,2},{4,5},{5,4},{6,7},{7,6},{8,9},{9,8},{10,11... | collective-permute-start | bytes 1327112 | tf_op jit(solution)/shard_map/ppermute | solution.py:724
  28.4 7.8 %collective-permute-start.4 = (bf16[504,192]{1,0:T(8,128)(2,1)S(1)}, bf16[504,192]{1,0:T(8,128)(2,1)S(1)}, u32[]{:S(2)}, u32[]{:S(2)}) collective-permute-start(bf16[504,192]{1,0:T(8,128)(2,1)S(1)} %get-tuple-element.72.head), channel_id=1, source_target_pairs={{0,1},{1,0},{2,3},{3,2},{4,5},{5,4},{6,7},{7,6},{8,9},{9,8},{10,11... | collective-permute-start | bytes 580616 | tf_op jit(solution)/shard_map/ppermute | solution.py:724
  28.9 6.2 %collective-permute-start.5 = (bf16[72,192]{1,0:T(8,128)(2,1)S(1)}, bf16[72,192]{1,0:T(8,128)(2,1)S(1)}, u32[]{:S(2)}, u32[]{:S(2)}) collective-permute-start(bf16[72,192]{1,0:T(8,128)(2,1)S(1)} %get-tuple-element.73), channel_id=1, source_target_pairs={{0,3},{1,2},{2,5},{3,4},{4,7},{5,6},{6,9},{7,8},{8,11},{9,10},{10,... | collective-permute-start | bytes 82952 | tf_op jit(solution)/shard_map/ppermute | solution.py:743
  28.9 7.3 %collective-permute-start.3 = (bf16[72,192]{1,0:T(8,128)(2,1)S(1)}, bf16[72,192]{1,0:T(8,128)(2,1)S(1)}, u32[]{:S(2)}, u32[]{:S(2)}) collective-permute-start(bf16[72,192]{1,0:T(8,128)(2,1)S(1)} %get-tuple-element.73), channel_id=1, source_target_pairs={{0,2},{2,4},{4,6},{6,8},{8,10},{10,12},{12,14},{14,0},{1,3},{3,5},... | collective-permute-start | bytes 82952 | tf_op jit(solution)/shard_map/ppermute | solution.py:729
  38.4 7.3 %collective-permute-start.8 = (bf16[8,21,8,128]{3,2,1,0:T(8,128)(2,1)S(1)}, bf16[8,21,8,128]{3,2,1,0:T(8,128)(2,1)S(1)}, u32[]{:S(2)}, u32[]{:S(2)}) collective-permute-start(bf16[8,21,8,128]{3,2,1,0:T(8,128)(2,1)S(1)} %get-tuple-element.98), channel_id=1, source_target_pairs={{0,1},{1,0},{2,3},{3,2},{4,5},{5,4},{6,7},{7,6},{8,9},{9,8},{10,11... | collective-permute-start | bytes 1032200 | tf_op jit(solution)/shard_map/ppermute | solution.py:724
  44.2 1.5 %collective-permute-start.9 = (bf16[8,7,8,128]{3,2,1,0:T(8,128)(2,1)S(1)}, bf16[8,7,8,128]{3,2,1,0:T(8,128)(2,1)S(1)}, u32[]{:S(2)}, u32[]{:S(2)}) collective-permute-start(bf16[8,7,8,128]{3,2,1,0:T(8,128)(2,1)S(1)} %get-tuple-element.100), channel_id=1, source_target_pairs={{0,1},{1,0},{2,3},{3,2},{4,5},{5,4},{6,7},{7,6},{8,9},{9,8},{10,11... | collective-permute-start | bytes 344072 | tf_op jit(solution)/shard_map/ppermute | solution.py:724
  44.7 9.2 %collective-permute-start.7 = (bf16[4,32,8,128]{3,2,1,0:T(8,128)(2,1)S(1)}, bf16[4,32,8,128]{3,2,1,0:T(8,128)(2,1)S(1)}, u32[]{:S(2)}, u32[]{:S(2)}) collective-permute-start(bf16[4,32,8,128]{3,2,1,0:T(8,128)(2,1)S(1)} %get-tuple-element.96), channel_id=1, source_target_pairs={{0,2},{2,0},{4,6},{6,4},{8,10},{10,8},{12,14},{14,12},{1,3},{3,1},... | collective-permute-start | bytes 786440 | tf_op jit(solution)/shard_map/ppermute | solution.py:734
  45.8 14.3 %collective-permute-start.13 = (bf16[4,33,8,128]{3,2,1,0:T(8,128)(2,1)S(1)}, bf16[4,33,8,128]{3,2,1,0:T(8,128)(2,1)S(1)}, u32[]{:S(2)}, u32[]{:S(2)}) collective-permute-start(bf16[4,33,8,128]{3,2,1,0:T(8,128)(2,1)S(1)} %get-tuple-element.107), channel_id=1, source_target_pairs={{0,2},{2,0},{4,6},{6,4},{8,10},{10,8},{12,14},{14,12},{1,3},{3,1},... | collective-permute-start | bytes 811016 | tf_op jit(solution)/shard_map/ppermute | solution.py:734
  53.9 6.1 %collective-permute-start.10 = (bf16[32,8,128]{2,1,0:T(8,128)(2,1)S(1)}, bf16[32,8,128]{2,1,0:T(8,128)(2,1)S(1)}, u32[]{:S(2)}, u32[]{:S(2)}) collective-permute-start(bf16[32,8,128]{2,1,0:T(8,128)(2,1)S(1)} %get-tuple-element.104), channel_id=1, source_target_pairs={{0,4},{2,6},{4,8},{6,10},{8,12},{10,14},{12,0},{14,2},{1,5},{3,7},... | collective-permute-start | bytes 196616 | tf_op jit(solution)/shard_map/ppermute | solution.py:729
  60.8 25.1 %all-to-all-start = ((bf16[4,33,8,128]{3,2,1,0:T(8,128)(2,1)}), bf16[4,33,8,128]{3,2,1,0:T(8,128)(2,1)S(1)}, u32[]{:S(2)}, u32[]{:S(2)}) async-start(bf16[4,33,8,128]{3,2,1,0:T(8,128)(2,1)} %shard_map.121.refs_4_), calls=%async_computation | async-start | bytes 540672 | tf_op jit(solution)/shard_map/all_to_all | solution.py:964
  64.3 10.8 %collective-permute-start.11 = (bf16[32,8,128]{2,1,0:T(8,128)(2,1)S(1)}, bf16[32,8,128]{2,1,0:T(8,128)(2,1)S(1)}, u32[]{:S(2)}, u32[]{:S(2)}) collective-permute-start(bf16[32,8,128]{2,1,0:T(8,128)(2,1)S(1)} %get-tuple-element.105), channel_id=1, source_target_pairs={{0,8},{2,10},{4,12},{6,14},{8,0},{10,2},{12,4},{14,6},{1,9},{3,11}... | collective-permute-start | bytes 196616 | tf_op jit(solution)/shard_map/ppermute | solution.py:729
  67.1 7.9 %collective-permute-start.12 = (bf16[32,8,128]{2,1,0:T(8,128)(2,1)S(1)}, bf16[32,8,128]{2,1,0:T(8,128)(2,1)S(1)}, u32[]{:S(2)}, u32[]{:S(2)}) collective-permute-start(bf16[32,8,128]{2,1,0:T(8,128)(2,1)S(1)} %get-tuple-element.106), channel_id=1, source_target_pairs={{0,12},{2,14},{4,0},{6,2},{8,4},{10,6},{12,8},{14,10},{1,13},{3,15... | collective-permute-start | bytes 196616 | tf_op jit(solution)/shard_map/ppermute | solution.py:729
  76.1 4.3 %collective-permute-start.16 = (bf16[32,8,128]{2,1,0:T(8,128)(2,1)S(1)}, bf16[32,8,128]{2,1,0:T(8,128)(2,1)S(1)}, u32[]{:S(2)}, u32[]{:S(2)}) collective-permute-start(bf16[32,8,128]{2,1,0:T(8,128)(2,1)S(1)} %shard_map.122.refs_0_), channel_id=1, source_target_pairs={{0,12},{2,14},{4,0},{6,2},{8,4},{10,6},{12,8},{14,10},{1,13},{3,15... | collective-permute-start | bytes 196616 | tf_op jit(solution)/shard_map/ppermute | solution.py:729
  78.3 5.6 %collective-permute-start.15 = (bf16[32,8,128]{2,1,0:T(8,128)(2,1)S(1)}, bf16[32,8,128]{2,1,0:T(8,128)(2,1)S(1)}, u32[]{:S(2)}, u32[]{:S(2)}) collective-permute-start(bf16[32,8,128]{2,1,0:T(8,128)(2,1)S(1)} %shard_map.122.refs_0_), channel_id=1, source_target_pairs={{0,8},{2,10},{4,12},{6,14},{8,0},{10,2},{12,4},{14,6},{1,9},{3,11}... | collective-permute-start | bytes 196616 | tf_op jit(solution)/shard_map/ppermute | solution.py:729
  78.8 6.1 %collective-permute-start.14 = (bf16[32,8,128]{2,1,0:T(8,128)(2,1)S(1)}, bf16[32,8,128]{2,1,0:T(8,128)(2,1)S(1)}, u32[]{:S(2)}, u32[]{:S(2)}) collective-permute-start(bf16[32,8,128]{2,1,0:T(8,128)(2,1)S(1)} %shard_map.122.refs_0_), channel_id=1, source_target_pairs={{0,4},{2,6},{4,8},{6,10},{8,12},{10,14},{12,0},{14,2},{1,5},{3,7},... | collective-permute-start | bytes 196616 | tf_op jit(solution)/shard_map/ppermute | solution.py:729
  86.8 17.2 %all-to-all-start.1 = ((bf16[8,33,8,128]{3,2,1,0:T(8,128)(2,1)}), bf16[8,33,8,128]{3,2,1,0:T(8,128)(2,1)S(1)}, u32[]{:S(2)}, u32[]{:S(2)}) async-start(bf16[8,33,8,128]{3,2,1,0:T(8,128)(2,1)} %shard_map.125), calls=%async_computation.1 | async-start | bytes 1081344 | tf_op jit(solution)/shard_map/all_to_all | solution.py:980
  90.3 14.2 %collective-permute-start.17 = (bf16[4,32,8,128]{3,2,1,0:T(8,128)(2,1)S(1)}, bf16[4,32,8,128]{3,2,1,0:T(8,128)(2,1)S(1)}, u32[]{:S(2)}, u32[]{:S(2)}) collective-permute-start(bf16[4,32,8,128]{3,2,1,0:T(8,128)(2,1)S(1)} %shard_map.123.same.order), channel_id=1, source_target_pairs={{0,2},{2,0},{4,6},{6,4},{8,10},{10,8},{12,14},{14,12},{1,3},{3,1},... | collective-permute-start | bytes 786440 | tf_op jit(solution)/shard_map/ppermute | solution.py:734
  104.0 3.3 %collective-permute-start.20 = (bf16[8,33,8,128]{3,2,1,0:T(8,128)(2,1)S(1)}, bf16[8,33,8,128]{3,2,1,0:T(8,128)(2,1)S(1)}, u32[]{:S(2)}, u32[]{:S(2)}) collective-permute-start(bf16[8,33,8,128]{3,2,1,0:T(8,128)(2,1)S(1)} %all-to-all-done.1.own_bc), channel_id=1, source_target_pairs={{0,1},{1,0},{2,3},{3,2},{4,5},{5,4},{6,7},{7,6},{8,9},{9,8},{10,11... | collective-permute-start | bytes 1622024 | tf_op jit(solution)/shard_map/ppermute | solution.py:724
  104.0 2.3 %collective-permute-start.18 = (bf16[4,32,8,128]{3,2,1,0:T(8,128)(2,1)S(1)}, bf16[4,32,8,128]{3,2,1,0:T(8,128)(2,1)S(1)}, u32[]{:S(2)}, u32[]{:S(2)}) collective-permute-start(bf16[4,32,8,128]{3,2,1,0:T(8,128)(2,1)S(1)} %shard_map.123.same.order), channel_id=1, source_target_pairs={{0,1},{1,0},{2,3},{3,2},{4,5},{5,4},{6,7},{7,6},{8,9},{9,8},{10,11... | collective-permute-start | bytes 786440 | tf_op jit(solution)/shard_map/ppermute | solution.py:724
  104.5 2.2 %collective-permute-start.19 = (bf16[4,32,8,128]{3,2,1,0:T(8,128)(2,1)S(1)}, bf16[4,32,8,128]{3,2,1,0:T(8,128)(2,1)S(1)}, u32[]{:S(2)}, u32[]{:S(2)}) collective-permute-start(bf16[4,32,8,128]{3,2,1,0:T(8,128)(2,1)S(1)} %collective-permute-done.17.same_x), channel_id=1, source_target_pairs={{0,1},{1,0},{2,3},{3,2},{4,5},{5,4},{6,7},{7,6},{8,9},{9,8},{10,11... | collective-permute-start | bytes 786440 | tf_op jit(solution)/shard_map/ppermute | solution.py:724

commit v14 on v13

--- a/solution.py
+++ b/solution.py
@@ -489,16 +489,16 @@
         for z in range(out.shape[0]):
             j = 2 * z + side
             at = 0
-            for k in range(0, len(refs) - 3, 2):
+            for k in range(0, len(refs) - 4, 2):
                 keep, got = refs[k], refs[k + 1]
                 count = keep.shape[1]
                 total = keep[j].astype(F32) + got[j].astype(F32)
                 out[z, at : at + count] = total.astype(BF16)
                 at += count
-            out[z, at:] = refs[-3][j]
-
-
-def split_z(keep, got, order, own_out, *give_outs):
+            out[z, at:] = refs[-4][j]
+
+
+def split_z(keep, got, own_out, *give_outs):
     count = keep.shape[0]
     z = lax.div(lax.axis_index("lon"), 2)
     for k, out in enumerate((own_out,) + give_outs):
@@ -901,7 +901,7 @@
 
     units_xa = units_a + extra
     keep_xa, give_xa = call(
-        lat_sums_split, [units(zs, units_xa)] * 2, [], (keep_a, got_a, bias_a), 1, 10
+        lat_sums_split, [units(zs, units_xa)] * 2, [], (keep_a, got_a, bias_a, keep_a), 1, 10
     )
     got_xa = x_swap(give_xa)
 
@@ -946,21 +946,22 @@
         14,
     )
     got_c = lat_swap(give_c)
+    own_a, *gives_a = call(
+        split_z, [units(units_xa)] * zs, [], (keep_xa, got_xa), 1, 10
+    )
+    gots_a = [lon_send(give, 2 * (k + 1)) for k, give in enumerate(gives_a)]
     units_bc = units_b + units_c + extra
     keep_x, give_x = call(
         lat_sums_split,
         [units(zs, units_bc)] * 2,
         [],
-        (keep_b, got_b, keep_c, got_c, bias_c),
+        (keep_b, got_b, keep_c, got_c, bias_c, own_a),
         1,
         10,
     )
     got_x = x_swap(give_x)
-    own_a, *gives_a = call(
-        split_z, [units(units_xa)] * zs, [], (keep_xa, got_xa, keep_x), 1, 10
-    )
-    gots_a = [lon_send(give, 2 * (k + 1)) for k, give in enumerate(gives_a)]
-    (part_z,) = call(add_pair, [units(zs, units_bc)], [], (keep_x, got_x, gots_a[0]), 1, 10)
+    (sum_a,) = call(sum_refs, [units(units_xa)], [], (own_a, *gots_a, keep_x), 1, 10)
+    (part_z,) = call(add_pair, [units(zs, units_bc)], [], (keep_x, got_x, sum_a), 1, 10)
     pieces_bc = lax.all_to_all(
         part_z,
         "lon",
@@ -968,7 +969,6 @@
         0,
         axis_index_groups=[[2 * z + x for z in range(zs)] for x in range(2)],
     )
-    (sum_a,) = call(sum_refs, [units(units_xa)], [], (own_a, *gots_a, part_z), 1, 10)
     moved_a = [lon_send(sum_a, 2 * k) for k in range(1, zs)]
     (same,) = call(join_z, [units(zs, units_xa)], [], [sum_a, *moved_a, part_z], 1, 10)
     same_x = x_swap(same)

time: 110 us -> 99.6 us (0.905)
  waiting for transfers between devices: 49.3 us -> 37.6 us
  starting transfers between devices: 25.6 us -> 27.9 us
    ppermute x3, waiting for transfers between devices: 6.95 us -> 0.01 us  [x_swap(): return lax.ppermute(value, 'lon', [(s, s ^ 1) for s in range(count)])]
    ppermute x8, waiting for transfers between devices: 21.3 us -> 17.3 us  [lon_send(): lax.ppermute(value, 'lon', [(s, (s + step) % count) for s in range(count)])]
    ppermute x8, starting transfers between devices: 7.8 us -> 9.38 us  [lon_send(): lax.ppermute(value, 'lon', [(s, (s + step) % count) for s in range(count)])]
  transfers between devices with their start and end apart: 23 -> 23, of which waited for: 14 -> 12; matrix products, arithmetic and copies ran while one was open for 0% -> 0% of each run, Pallas kernels for 10% -> 12%
where the time goes in v14:
time: 99.6 us; the launch traced here: 99.3 us
  waiting for transfers between devices  37.6 us (38%)
  Pallas kernels  32.9 us (33%)
  starting transfers between devices  27.9 us (28%)
    pallas_call x15, Pallas kernels, call(): pl.pallas_call(kernel, out_shape=[(pltpu.VMEM if at in near else jax.Shap...  32.9 us
    ppermute x8, waiting for transfers between devices, lon_send(): lax.ppermute(value, 'lon', [(s, (s + step) % count) for s in range(count)])  17.3 us
    all_to_all x1, waiting for transfers between devices, shards(): whole_bc = lax.all_to_all(sum_bc, 'lon', 0, 0)  12.1 us
    ppermute x8, starting transfers between devices, lon_send(): lax.ppermute(value, 'lon', [(s, (s + step) % count) for s in range(count)])  9.38 us
    ppermute x2, starting transfers between devices, diag_send(): return lax.ppermute(value, ('lon', 'lat'), pairs)  5.64 us
    ppermute x8, waiting for transfers between devices, lat_swap(): return lax.ppermute(value, 'lat', [(0, 1), (1, 0)])  4.35 us
    all_to_all x1, starting transfers between devices, shards(): lax.all_to_all(part_z, 'lon', 0, 0, axis_index_groups=[[2 * z + x for z i...  4.1 us
    ppermute x2, waiting for transfers between devices, diag_send(): return lax.ppermute(value, ('lon', 'lat'), pairs)  3.79 us
  transfers between devices with their start and end apart: 23, of which 12 were waited for; matrix products, arithmetic and copies ran while one was open for 0% of the time, Pallas kernels for 12%

profile of v14, /device:TPU:0, one launch (start us, length us, event | category | flops | bytes accessed | tf_op | source)
XLA Modules:
  0.0 99.3 jit_solution(10159955633497870053)
XLA Ops:
  0.6 0.0 copy-start.6
  0.7 6.6 %shard_map.112 = (bf16[576,192]{1,0:T(8,128)(2,1)S(1)}, bf16[2,504,192]{2,1,0:T(8,128)(2,1)S(1)}, bf16[2,72,192]{2,1,0:T(8,128)(2,1)S(1)}, bf16[576,576]{1,0:T(8...) custom-call(bf16[2,12,24,192]{3,2,1,0:T(8,128)(2,1)} %tokens_in.1, ...), custom_call_target="tpu_custom_call" | custom-call | flops 8800000000 | bytes 100000 | tf_op jit(solution)/shard_map/pallas_call | solution.py:699
  7.2 0.5 collective-permute-start.1
  7.7 5.6 %collective-permute-start.2 = (bf16[2,72,192]{2,1,0:T(8,128)(2,1)S(1)}, bf16[2,72,192]{2,1,0:T(8,128)(2,1)S(1)}, u32[]{:S(2)}, u32[]{:S(2)}) collective-permute-start(bf16[2,72,192]{2,1,0:T(8,128)(2,1)S(1)} %get-tuple-element.59), channel_id=1, source_target_pairs={{0,15},{1,14},{2,1},{3,0},{4,3},{5,2},{6,5},{7,4},{8,7},{9,6},{10,... | collective-permute-start | bytes 165896 | tf_op jit(solution)/shard_map/ppermute | solution.py:743
  13.4 0.5 collective-permute-start
  13.9 0.0 copy-start.2
  14.0 2.0 %shard_map.113 = (f32[864,144]{1,0:T(8,128)S(1)}, bf16[576,768]{1,0:T(8,128)(2,1)S(1)}) custom-call(f32[2,6,1,6336]{3,2,1,0:T(1,128)S(1)} %bitcast.8, bf16[2,132,384]{2,1,0:T(8,128)(2,1)S(1)} %copy-done.6, f32[576,768]{1,0:T(8,128)S(1)} %get-tuple-element.60.hidden), custom_call_target="tpu_custom_call" | custom-call | flops 3300000000 | bytes 100000 | tf_op jit(solution)/shard_map/pallas_call | solution.py:699
  15.9 0.0 collective-permute-done.2.diag_head
  16.0 1.8 %collective-permute-done.lon_head = bf16[2,72,192]{2,1,0:T(8,128)(2,1)S(1)} collective-permute-done((bf16[2,72,192]{2,1,0:T(8,128)(2,1)S(1)}, bf16[2,72,192]{2,1,0:T(8,128)(2,1)S(1)}, u32[]{:S(2)}, u32[]{:S(2)}) %collective-permute-start) | collective-permute-done | bytes 55328 | tf_op jit(solution)/shard_map/ppermute | solution.py:729
  17.8 8.9 %shard_map.114 = (bf16[504,192]{1,0:T(8,128)(2,1)S(1)}, bf16[72,192]{1,0:T(8,128)(2,1)S(1)}, bf16[576,192]{1,0:T(8,128)(2,1)S(1)}, bf16[576,576]{1,0:T(8,128)(2,...) custom-call(bf16[2,504,192]{2,1,0:T(8,128)(2,1)S(1)} %get-tuple-elem, ...), custom_call_target="tpu_custom_call", output_to_operand_aliasing={{12}: (10, {}), {13}: (11, {}), {14}: (12, {}), {15}: (13, ... | custom-call | flops 20899999744 | bytes 100000 | tf_op jit(solution)/shard_map/pallas_call | solution.py:699
  26.7 1.6 %shard_map.115 = (bf16[8,27,8,128]{3,2,1,0:T(8,128)(2,1)S(1)}, bf16[8,27,8,128]{3,2,1,0:T(8,128)(2,1)S(1)}, bf16[8,5,8,128]{3,2,1,0:T(8,128)(2,1)S(1)}) custom-call(bf16[576,192]{1,0:T(8,128)(2,1)S(1)} %get-tuple-element.78.n1, bf16[576,576]{1,0:T(8,128)(2,1)S(1)} %get-tuple-element.79.field, bf16[576,192]{1,0:T(8,128)(2,1)S(1)} %get-tuple-element.80.mixed, ...), custom_call_target="tpu_custom_call" | custom-call | flops 3300000000 | bytes 100000 | tf_op jit(solution)/shard_map/pallas_call | solution.py:699
  28.3 0.1 collective-permute-start.6
  28.4 0.5 collective-permute-start.4
  28.9 1.3 %collective-permute-done.6.refs_1_ = bf16[8,27,8,128]{3,2,1,0:T(8,128)(2,1)S(1)} collective-permute-done((bf16[8,27,8,128]{3,2,1,0:T(8,128)(2,1)S(1)}, bf16[8,27,8,128]{3,2,1,0:T(8,128)(2,1)S(1)}, u32[]{:S(2)}, u32[]{:S(2)}) %collective-permute-start.6) | collective-permute-done | bytes 442400 | tf_op jit(solution)/shard_map/ppermute | solution.py:724
  30.2 0.1 shard_map.116
  30.3 1.1 %collective-permute-start.7 = (bf16[4,32,8,128]{3,2,1,0:T(8,128)(2,1)S(1)}, bf16[4,32,8,128]{3,2,1,0:T(8,128)(2,1)S(1)}, u32[]{:S(2)}, u32[]{:S(2)}) collective-permute-start(bf16[4,32,8,128]{3,2,1,0:T(8,128)(2,1)S(1)} %get-tuple-element.96), channel_id=1, source_target_pairs={{0,2},{2,0},{4,6},{6,4},{8,10},{10,8},{12,14},{14,12},{1,3},{3,1},... | collective-permute-start | bytes 786440 | tf_op jit(solution)/shard_map/ppermute | solution.py:734
  31.4 3.8 %collective-permute-done.5.diag_tail = bf16[72,192]{1,0:T(8,128)(2,1)S(1)} collective-permute-done((bf16[72,192]{1,0:T(8,128)(2,1)S(1)}, bf16[72,192]{1,0:T(8,128)(2,1)S(1)}, u32[]{:S(2)}, u32[]{:S(2)}) %collective-permute-start.5) | collective-permute-done | bytes 27680 | tf_op jit(solution)/shard_map/ppermute | solution.py:743
  35.2 1.1 %collective-permute-done.3.lon_tail = bf16[72,192]{1,0:T(8,128)(2,1)S(1)} collective-permute-done((bf16[72,192]{1,0:T(8,128)(2,1)S(1)}, bf16[72,192]{1,0:T(8,128)(2,1)S(1)}, u32[]{:S(2)}, u32[]{:S(2)}) %collective-permute-start.3) | collective-permute-done | bytes 27680 | tf_op jit(solution)/shard_map/ppermute | solution.py:729
  36.3 2.2 %shard_map.117 = (bf16[8,21,8,128]{3,2,1,0:T(8,128)(2,1)S(1)}, bf16[8,21,8,128]{3,2,1,0:T(8,128)(2,1)S(1)}, f32[576,192]{1,0:T(8,128)S(1)}, bf16[576,192]{1,0:T(8,128)(2,1)S(1)}, f32[1,192]{1,0:T(1,128)S(1)}) custom-call(bf16[504,192]{1,0:T(8,128)(2,1)S(1)} %get-tuple-element.72.head, bf16[72,192]{1,0:T(8,128)(2,1)S(1)} %collective-permute-done.3.lon_tail, ...), custom_call_target="tpu_custom_call" | custom-call | flops 3300000000 | bytes 100000 | tf_op jit(solution)/shard_map/pallas_call | solution.py:699
  38.5 0.1 collective-permute-start.11
  38.5 5.7 %shard_map.118 = (bf16[2,12,24,192]{3,2,1,0:T(8,128)(2,1)}, bf16[8,7,8,128]{3,2,1,0:T(8,128)(2,1)S(1)}, bf16[8,7,8,128]{3,2,1,0:T(8,128)(2,1)S(1)}, bf16[8,5,8,128]{3,2,1,0:T(8,128)(2,1)S(1)}) custom-call(bf16[576,192]{1,0:T(8,128)(2,1)S(1)} %get-tuple-element.69.x_in, bf16[576,576]{1,0:T(8,128)(2,1)S(1)} %get-tuple-element.70.qkv, ...), custom_call_target="tpu_custom_call" | custom-call | flops 7699999744 | bytes 100000 | tf_op jit(solution)/shard_map/pallas_call | solution.py:699
  44.3 0.5 collective-permute-start.12
  44.8 0.1 shard_map.119
  44.8 0.9 collective-permute-done.12.refs_3_
  45.7 0.1 shard_map.120
  45.9 0.1 collective-permute-start.16
  45.9 0.1 collective-permute-start.8
  46.0 3.0 %collective-permute-start.9 = (bf16[32,8,128]{2,1,0:T(8,128)(2,1)S(1)}, bf16[32,8,128]{2,1,0:T(8,128)(2,1)S(1)}, u32[]{:S(2)}, u32[]{:S(2)}) collective-permute-start(bf16[32,8,128]{2,1,0:T(8,128)(2,1)S(1)} %get-tuple-element.99), channel_id=1, source_target_pairs={{0,8},{2,10},{4,12},{6,14},{8,0},{10,2},{12,4},{14,6},{1,9},{3,11}... | collective-permute-start | bytes 196616 | tf_op jit(solution)/shard_map/ppermute | solution.py:729
  49.0 0.9 collective-permute-start.10
  49.8 3.0 %collective-permute-done.8.refs_1_ = bf16[32,8,128]{2,1,0:T(8,128)(2,1)S(1)} collective-permute-done((bf16[32,8,128]{2,1,0:T(8,128)(2,1)S(1)}, bf16[32,8,128]{2,1,0:T(8,128)(2,1)S(1)}, u32[]{:S(2)}, u32[]{:S(2)}) %collective-permute-start.8) | collective-permute-done | bytes 65568 | tf_op jit(solution)/shard_map/ppermute | solution.py:729
  52.8 1.8 %collective-permute-done.9.refs_2_ = bf16[32,8,128]{2,1,0:T(8,128)(2,1)S(1)} collective-permute-done((bf16[32,8,128]{2,1,0:T(8,128)(2,1)S(1)}, bf16[32,8,128]{2,1,0:T(8,128)(2,1)S(1)}, u32[]{:S(2)}, u32[]{:S(2)}) %collective-permute-start.9) | collective-permute-done | bytes 65568 | tf_op jit(solution)/shard_map/ppermute | solution.py:729
  54.7 0.0 collective-permute-done.16.got
  54.7 0.8 shard_map.122.refs_4_
  55.4 4.1 %all-to-all-start = ((bf16[4,33,8,128]{3,2,1,0:T(8,128)(2,1)}), bf16[4,33,8,128]{3,2,1,0:T(8,128)(2,1)S(1)}, u32[]{:S(2)}, u32[]{:S(2)}) async-start(bf16[4,33,8,128]{3,2,1,0:T(8,128)(2,1)} %shard_map.122.refs_4_), calls=%async_computation | async-start | bytes 540672 | tf_op jit(solution)/shard_map/all_to_all | solution.py:965
  59.6 3.8 %collective-permute-start.15 = (bf16[32,8,128]{2,1,0:T(8,128)(2,1)S(1)}, bf16[32,8,128]{2,1,0:T(8,128)(2,1)S(1)}, u32[]{:S(2)}, u32[]{:S(2)}) collective-permute-start(bf16[32,8,128]{2,1,0:T(8,128)(2,1)S(1)} %shard_map.121.order.refs_0_), channel_id=1, source_target_pairs={{0,12},{2,14},{4,0},{6,2},{8,4},{10,6},{12,8},{14,10},{1,13},{3,15... | collective-permute-start | bytes 196616 | tf_op jit(solution)/shard_map/ppermute | solution.py:729
  63.4 1.1 %collective-permute-start.13 = (bf16[32,8,128]{2,1,0:T(8,128)(2,1)S(1)}, bf16[32,8,128]{2,1,0:T(8,128)(2,1)S(1)}, u32[]{:S(2)}, u32[]{:S(2)}) collective-permute-start(bf16[32,8,128]{2,1,0:T(8,128)(2,1)S(1)} %shard_map.121.order.refs_0_), channel_id=1, source_target_pairs={{0,4},{2,6},{4,8},{6,10},{8,12},{10,14},{12,0},{14,2},{1,5},{3,7},... | collective-permute-start | bytes 196616 | tf_op jit(solution)/shard_map/ppermute | solution.py:729
  64.5 2.4 %collective-permute-done.15.refs_3_ = bf16[32,8,128]{2,1,0:T(8,128)(2,1)S(1)} collective-permute-done((bf16[32,8,128]{2,1,0:T(8,128)(2,1)S(1)}, bf16[32,8,128]{2,1,0:T(8,128)(2,1)S(1)}, u32[]{:S(2)}, u32[]{:S(2)}) %collective-permute-start.15) | collective-permute-done | bytes 65568 | tf_op jit(solution)/shard_map/ppermute | solution.py:729
  66.9 7.3 %collective-permute-done.14.refs_2_ = bf16[32,8,128]{2,1,0:T(8,128)(2,1)S(1)} collective-permute-done((bf16[32,8,128]{2,1,0:T(8,128)(2,1)S(1)}, bf16[32,8,128]{2,1,0:T(8,128)(2,1)S(1)}, u32[]{:S(2)}, u32[]{:S(2)}) %collective-permute-start.14) | collective-permute-done | bytes 65568 | tf_op jit(solution)/shard_map/ppermute | solution.py:729
  74.2 1.0 shard_map.123.same.order
  75.2 0.9 shard_map.125
  76.1 3.5 %all-to-all-start.1 = ((bf16[8,33,8,128]{3,2,1,0:T(8,128)(2,1)}), bf16[8,33,8,128]{3,2,1,0:T(8,128)(2,1)S(1)}, u32[]{:S(2)}, u32[]{:S(2)}) async-start(bf16[8,33,8,128]{3,2,1,0:T(8,128)(2,1)} %shard_map.125), calls=%async_computation.1 | async-start | bytes 1081344 | tf_op jit(solution)/shard_map/all_to_all | solution.py:980
  79.6 1.9 %collective-permute-start.17 = (bf16[4,32,8,128]{3,2,1,0:T(8,128)(2,1)S(1)}, bf16[4,32,8,128]{3,2,1,0:T(8,128)(2,1)S(1)}, u32[]{:S(2)}, u32[]{:S(2)}) collective-permute-start(bf16[4,32,8,128]{3,2,1,0:T(8,128)(2,1)S(1)} %shard_map.123.same.order), channel_id=1, source_target_pairs={{0,2},{2,0},{4,6},{6,4},{8,10},{10,8},{12,14},{14,12},{1,3},{3,1},... | collective-permute-start | bytes 786440 | tf_op jit(solution)/shard_map/ppermute | solution.py:734
  81.5 12.1 %all-to-all-done.1.own_bc = bf16[8,33,8,128]{3,2,1,0:T(8,128)(2,1)S(1)} async-done(((bf16[8,33,8,128]{3,2,1,0:T(8,128)(2,1)}), bf16[8,33,8,128]{3,2,1,0:T(8,128)(2,1)S(1)}, u32[]{:S(2)}, u32[]{:S(2)}) %all-to-all-start.1) | async-done | bytes 540704 | tf_op jit(solution)/shard_map/all_to_all | solution.py:980
  93.6 0.5 collective-permute-start.18
  94.1 1.8 %collective-permute-done.18.cross = bf16[4,32,8,128]{3,2,1,0:T(8,128)(2,1)S(1)} collective-permute-done((bf16[4,32,8,128]{3,2,1,0:T(8,128)(2,1)S(1)}, bf16[4,32,8,128]{3,2,1,0:T(8,128)(2,1)S(1)}, u32[]{:S(2)}, u32[]{:S(2)}) %collective-permute-start.18) | collective-permute-done | bytes 262176 | tf_op jit(solution)/shard_map/ppermute | solution.py:724
  95.9 0.4 collective-permute-done.19.cross_x
  96.3 0.6 shard_map.124
  96.9 2.4 %shard_map.126 = (bf16[6918,128]{1,0:T(8,128)(2,1)}, f32[2,6,1,6336]{3,2,1,0:T(1,128)}) custom-call(bf16[2,132,384]{2,1,0:T(8,128)(2,1)S(1)} %copy-done.6, f32[3456,128]{1,0:T(8,128)S(1)} %get-tuple-element.108.flat_a, f32[8,128]{1,0:T(8,128)S(1)} %get-tuple-element.109.squares, f32[6,1,6336]{2,1,0:T(1,128)S(1)} %get-tuple-element.110.bias_late, ...), custom_call_target="tpu_custom_call" | custom-call | flops 2200000000 | bytes 100000 | tf_op jit(solution)/shard_map/pallas_call | solution.py:699
  (27 shorter events, 0.1 us)
Async XLA Ops:
  0.6 13.3 %copy-start.3 = (f32[2,1,6,6336]{3,1,2,0:T(1,128)S(1)}, f32[2,1,6,6336]{3,1,2,0:T(1,128)}, u32[]{:S(2)}) copy-start(f32[2,1,6,6336]{3,1,2,0:T(1,128)} %param.16) | copy-start | bytes 912388
  0.6 13.3 %copy-start.6 = (bf16[2,132,384]{2,1,0:T(8,128)(2,1)S(1)}, bf16[2,132,384]{2,1,0:T(8,128)(2,1)}, u32[]{:S(2)}) copy-start(bf16[2,132,384]{2,1,0:T(8,128)(2,1)} %constant.2.clone.spread_in.spread) | copy-start | bytes 608260
  7.2 10.5 %collective-permute-start.1 = (bf16[2,504,192]{2,1,0:T(8,128)(2,1)S(1)}, bf16[2,504,192]{2,1,0:T(8,128)(2,1)S(1)}, u32[]{:S(2)}, u32[]{:S(2)}) collective-permute-start(bf16[2,504,192]{2,1,0:T(8,128)(2,1)S(1)} %get-tuple-element.58.tail), channel_id=1, source_target_pairs={{0,1},{1,0},{2,3},{3,2},{4,5},{5,4},{6,7},{7,6},{8,9},{9,8},{10,11... | collective-permute-start | bytes 1161224 | tf_op jit(solution)/shard_map/ppermute | solution.py:724
  7.7 8.2 %collective-permute-start.2 = (bf16[2,72,192]{2,1,0:T(8,128)(2,1)S(1)}, bf16[2,72,192]{2,1,0:T(8,128)(2,1)S(1)}, u32[]{:S(2)}, u32[]{:S(2)}) collective-permute-start(bf16[2,72,192]{2,1,0:T(8,128)(2,1)S(1)} %get-tuple-element.59), channel_id=1, source_target_pairs={{0,15},{1,14},{2,1},{3,0},{4,3},{5,2},{6,5},{7,4},{8,7},{9,6},{10,... | collective-permute-start | bytes 165896 | tf_op jit(solution)/shard_map/ppermute | solution.py:743
  13.4 4.4 %collective-permute-start = (bf16[2,72,192]{2,1,0:T(8,128)(2,1)S(1)}, bf16[2,72,192]{2,1,0:T(8,128)(2,1)S(1)}, u32[]{:S(2)}, u32[]{:S(2)}) collective-permute-start(bf16[2,72,192]{2,1,0:T(8,128)(2,1)S(1)} %get-tuple-element.59), channel_id=1, source_target_pairs={{0,14},{2,0},{4,2},{6,4},{8,6},{10,8},{12,10},{14,12},{1,15},{3,1}... | collective-permute-start | bytes 165896 | tf_op jit(solution)/shard_map/ppermute | solution.py:729
  13.9 3.8 %copy-start = (bf16[2,192,768]{2,1,0:T(8,128)(2,1)S(1)}, bf16[2,192,768]{2,1,0:T(8,128)(2,1)}, u32[]{:S(2)}) copy-start(bf16[2,192,768]{2,1,0:T(8,128)(2,1)} %up_w.3) | copy-start | bytes 1769476
  13.9 3.8 %copy-start.1 = (bf16[2,768,192]{1,2,0:T(8,128)(2,1)S(1)}, bf16[2,768,192]{1,2,0:T(8,128)(2,1)}, u32[]{:S(2)}) copy-start(bf16[2,768,192]{1,2,0:T(8,128)(2,1)} %param.14) | copy-start | bytes 1769476
  13.9 3.8 %copy-start.2 = (bf16[2,192,576]{2,1,0:T(8,128)(2,1)S(1)}, bf16[2,192,576]{2,1,0:T(8,128)(2,1)}, u32[]{:S(2)}) copy-start(bf16[2,192,576]{2,1,0:T(8,128)(2,1)} %qkv_w.3) | copy-start | bytes 1327108
  13.9 3.8 %copy-start.4 = (bf16[2,192,192]{2,1,0:T(8,128)(2,1)S(1)}, bf16[2,192,192]{2,1,0:T(8,128)(2,1)}, u32[]{:S(2)}) copy-start(bf16[2,192,192]{2,1,0:T(8,128)(2,1)} %proj_w.3) | copy-start | bytes 442372
  13.9 3.8 %copy-start.5 = (f32[2,2,192]{2,1,0:T(2,128)S(1)}, f32[2,2,192]{2,1,0:T(2,128)}, u32[]{:S(2)}) copy-start(f32[2,2,192]{2,1,0:T(2,128)} %gains.5) | copy-start | bytes 9220
  28.3 1.8 %collective-permute-start.6 = (bf16[8,27,8,128]{3,2,1,0:T(8,128)(2,1)S(1)}, bf16[8,27,8,128]{3,2,1,0:T(8,128)(2,1)S(1)}, u32[]{:S(2)}, u32[]{:S(2)}) collective-permute-start(bf16[8,27,8,128]{3,2,1,0:T(8,128)(2,1)S(1)} %get-tuple-element.88), channel_id=1, source_target_pairs={{0,1},{1,0},{2,3},{3,2},{4,5},{5,4},{6,7},{7,6},{8,9},{9,8},{10,11... | collective-permute-start | bytes 1327112 | tf_op jit(solution)/shard_map/ppermute | solution.py:724
  28.4 7.9 %collective-permute-start.4 = (bf16[504,192]{1,0:T(8,128)(2,1)S(1)}, bf16[504,192]{1,0:T(8,128)(2,1)S(1)}, u32[]{:S(2)}, u32[]{:S(2)}) collective-permute-start(bf16[504,192]{1,0:T(8,128)(2,1)S(1)} %get-tuple-element.72.head), channel_id=1, source_target_pairs={{0,1},{1,0},{2,3},{3,2},{4,5},{5,4},{6,7},{7,6},{8,9},{9,8},{10,11... | collective-permute-start | bytes 580616 | tf_op jit(solution)/shard_map/ppermute | solution.py:724
  28.9 6.3 %collective-permute-start.5 = (bf16[72,192]{1,0:T(8,128)(2,1)S(1)}, bf16[72,192]{1,0:T(8,128)(2,1)S(1)}, u32[]{:S(2)}, u32[]{:S(2)}) collective-permute-start(bf16[72,192]{1,0:T(8,128)(2,1)S(1)} %get-tuple-element.73), channel_id=1, source_target_pairs={{0,3},{1,2},{2,5},{3,4},{4,7},{5,6},{6,9},{7,8},{8,11},{9,10},{10,... | collective-permute-start | bytes 82952 | tf_op jit(solution)/shard_map/ppermute | solution.py:743
  28.9 7.4 %collective-permute-start.3 = (bf16[72,192]{1,0:T(8,128)(2,1)S(1)}, bf16[72,192]{1,0:T(8,128)(2,1)S(1)}, u32[]{:S(2)}, u32[]{:S(2)}) collective-permute-start(bf16[72,192]{1,0:T(8,128)(2,1)S(1)} %get-tuple-element.73), channel_id=1, source_target_pairs={{0,2},{2,4},{4,6},{6,8},{8,10},{10,12},{12,14},{14,0},{1,3},{3,5},... | collective-permute-start | bytes 82952 | tf_op jit(solution)/shard_map/ppermute | solution.py:729
  30.3 14.5 %collective-permute-start.7 = (bf16[4,32,8,128]{3,2,1,0:T(8,128)(2,1)S(1)}, bf16[4,32,8,128]{3,2,1,0:T(8,128)(2,1)S(1)}, u32[]{:S(2)}, u32[]{:S(2)}) collective-permute-start(bf16[4,32,8,128]{3,2,1,0:T(8,128)(2,1)S(1)} %get-tuple-element.96), channel_id=1, source_target_pairs={{0,2},{2,0},{4,6},{6,4},{8,10},{10,8},{12,14},{14,12},{1,3},{3,1},... | collective-permute-start | bytes 786440 | tf_op jit(solution)/shard_map/ppermute | solution.py:734
  38.5 7.3 %collective-permute-start.11 = (bf16[8,21,8,128]{3,2,1,0:T(8,128)(2,1)S(1)}, bf16[8,21,8,128]{3,2,1,0:T(8,128)(2,1)S(1)}, u32[]{:S(2)}, u32[]{:S(2)}) collective-permute-start(bf16[8,21,8,128]{3,2,1,0:T(8,128)(2,1)S(1)} %get-tuple-element.102), channel_id=1, source_target_pairs={{0,1},{1,0},{2,3},{3,2},{4,5},{5,4},{6,7},{7,6},{8,9},{9,8},{10,11... | collective-permute-start | bytes 1032200 | tf_op jit(solution)/shard_map/ppermute | solution.py:724
  44.3 1.5 %collective-permute-start.12 = (bf16[8,7,8,128]{3,2,1,0:T(8,128)(2,1)S(1)}, bf16[8,7,8,128]{3,2,1,0:T(8,128)(2,1)S(1)}, u32[]{:S(2)}, u32[]{:S(2)}) collective-permute-start(bf16[8,7,8,128]{3,2,1,0:T(8,128)(2,1)S(1)} %get-tuple-element.104), channel_id=1, source_target_pairs={{0,1},{1,0},{2,3},{3,2},{4,5},{5,4},{6,7},{7,6},{8,9},{9,8},{10,11... | collective-permute-start | bytes 344072 | tf_op jit(solution)/shard_map/ppermute | solution.py:724
  45.9 8.8 %collective-permute-start.16 = (bf16[4,33,8,128]{3,2,1,0:T(8,128)(2,1)S(1)}, bf16[4,33,8,128]{3,2,1,0:T(8,128)(2,1)S(1)}, u32[]{:S(2)}, u32[]{:S(2)}) collective-permute-start(bf16[4,33,8,128]{3,2,1,0:T(8,128)(2,1)S(1)} %get-tuple-element.107), channel_id=1, source_target_pairs={{0,2},{2,0},{4,6},{6,4},{8,10},{10,8},{12,14},{14,12},{1,3},{3,1},... | collective-permute-start | bytes 811016 | tf_op jit(solution)/shard_map/ppermute | solution.py:734
  45.9 6.9 %collective-permute-start.8 = (bf16[32,8,128]{2,1,0:T(8,128)(2,1)S(1)}, bf16[32,8,128]{2,1,0:T(8,128)(2,1)S(1)}, u32[]{:S(2)}, u32[]{:S(2)}) collective-permute-start(bf16[32,8,128]{2,1,0:T(8,128)(2,1)S(1)} %get-tuple-element.98), channel_id=1, source_target_pairs={{0,4},{2,6},{4,8},{6,10},{8,12},{10,14},{12,0},{14,2},{1,5},{3,7},... | collective-permute-start | bytes 196616 | tf_op jit(solution)/shard_map/ppermute | solution.py:729
  46.0 8.6 %collective-permute-start.9 = (bf16[32,8,128]{2,1,0:T(8,128)(2,1)S(1)}, bf16[32,8,128]{2,1,0:T(8,128)(2,1)S(1)}, u32[]{:S(2)}, u32[]{:S(2)}) collective-permute-start(bf16[32,8,128]{2,1,0:T(8,128)(2,1)S(1)} %get-tuple-element.99), channel_id=1, source_target_pairs={{0,8},{2,10},{4,12},{6,14},{8,0},{10,2},{12,4},{14,6},{1,9},{3,11}... | collective-permute-start | bytes 196616 | tf_op jit(solution)/shard_map/ppermute | solution.py:729
  49.0 5.7 %collective-permute-start.10 = (bf16[32,8,128]{2,1,0:T(8,128)(2,1)S(1)}, bf16[32,8,128]{2,1,0:T(8,128)(2,1)S(1)}, u32[]{:S(2)}, u32[]{:S(2)}) collective-permute-start(bf16[32,8,128]{2,1,0:T(8,128)(2,1)S(1)} %get-tuple-element.100), channel_id=1, source_target_pairs={{0,12},{2,14},{4,0},{6,2},{8,4},{10,6},{12,8},{14,10},{1,13},{3,15... | collective-permute-start | bytes 196616 | tf_op jit(solution)/shard_map/ppermute | solution.py:729
  55.4 19.8 %all-to-all-start = ((bf16[4,33,8,128]{3,2,1,0:T(8,128)(2,1)}), bf16[4,33,8,128]{3,2,1,0:T(8,128)(2,1)S(1)}, u32[]{:S(2)}, u32[]{:S(2)}) async-start(bf16[4,33,8,128]{3,2,1,0:T(8,128)(2,1)} %shard_map.122.refs_4_), calls=%async_computation | async-start | bytes 540672 | tf_op jit(solution)/shard_map/all_to_all | solution.py:965
  59.6 7.4 %collective-permute-start.15 = (bf16[32,8,128]{2,1,0:T(8,128)(2,1)S(1)}, bf16[32,8,128]{2,1,0:T(8,128)(2,1)S(1)}, u32[]{:S(2)}, u32[]{:S(2)}) collective-permute-start(bf16[32,8,128]{2,1,0:T(8,128)(2,1)S(1)} %shard_map.121.order.refs_0_), channel_id=1, source_target_pairs={{0,12},{2,14},{4,0},{6,2},{8,4},{10,6},{12,8},{14,10},{1,13},{3,15... | collective-permute-start | bytes 196616 | tf_op jit(solution)/shard_map/ppermute | solution.py:729
  63.4 10.8 %collective-permute-start.14 = (bf16[32,8,128]{2,1,0:T(8,128)(2,1)S(1)}, bf16[32,8,128]{2,1,0:T(8,128)(2,1)S(1)}, u32[]{:S(2)}, u32[]{:S(2)}) collective-permute-start(bf16[32,8,128]{2,1,0:T(8,128)(2,1)S(1)} %shard_map.121.order.refs_0_), channel_id=1, source_target_pairs={{0,8},{2,10},{4,12},{6,14},{8,0},{10,2},{12,4},{14,6},{1,9},{3,11}... | collective-permute-start | bytes 196616 | tf_op jit(solution)/shard_map/ppermute | solution.py:729
  63.4 10.8 %collective-permute-start.13 = (bf16[32,8,128]{2,1,0:T(8,128)(2,1)S(1)}, bf16[32,8,128]{2,1,0:T(8,128)(2,1)S(1)}, u32[]{:S(2)}, u32[]{:S(2)}) collective-permute-start(bf16[32,8,128]{2,1,0:T(8,128)(2,1)S(1)} %shard_map.121.order.refs_0_), channel_id=1, source_target_pairs={{0,4},{2,6},{4,8},{6,10},{8,12},{10,14},{12,0},{14,2},{1,5},{3,7},... | collective-permute-start | bytes 196616 | tf_op jit(solution)/shard_map/ppermute | solution.py:729
  76.1 17.5 %all-to-all-start.1 = ((bf16[8,33,8,128]{3,2,1,0:T(8,128)(2,1)}), bf16[8,33,8,128]{3,2,1,0:T(8,128)(2,1)S(1)}, u32[]{:S(2)}, u32[]{:S(2)}) async-start(bf16[8,33,8,128]{3,2,1,0:T(8,128)(2,1)} %shard_map.125), calls=%async_computation.1 | async-start | bytes 1081344 | tf_op jit(solution)/shard_map/all_to_all | solution.py:980
  79.6 14.5 %collective-permute-start.17 = (bf16[4,32,8,128]{3,2,1,0:T(8,128)(2,1)S(1)}, bf16[4,32,8,128]{3,2,1,0:T(8,128)(2,1)S(1)}, u32[]{:S(2)}, u32[]{:S(2)}) collective-permute-start(bf16[4,32,8,128]{3,2,1,0:T(8,128)(2,1)S(1)} %shard_map.123.same.order), channel_id=1, source_target_pairs={{0,2},{2,0},{4,6},{6,4},{8,10},{10,8},{12,14},{14,12},{1,3},{3,1},... | collective-permute-start | bytes 786440 | tf_op jit(solution)/shard_map/ppermute | solution.py:734
  93.6 3.3 %collective-permute-start.20 = (bf16[8,33,8,128]{3,2,1,0:T(8,128)(2,1)S(1)}, bf16[8,33,8,128]{3,2,1,0:T(8,128)(2,1)S(1)}, u32[]{:S(2)}, u32[]{:S(2)}) collective-permute-start(bf16[8,33,8,128]{3,2,1,0:T(8,128)(2,1)S(1)} %all-to-all-done.1.own_bc), channel_id=1, source_target_pairs={{0,1},{1,0},{2,3},{3,2},{4,5},{5,4},{6,7},{7,6},{8,9},{9,8},{10,11... | collective-permute-start | bytes 1622024 | tf_op jit(solution)/shard_map/ppermute | solution.py:724
  93.6 2.3 %collective-permute-start.18 = (bf16[4,32,8,128]{3,2,1,0:T(8,128)(2,1)S(1)}, bf16[4,32,8,128]{3,2,1,0:T(8,128)(2,1)S(1)}, u32[]{:S(2)}, u32[]{:S(2)}) collective-permute-start(bf16[4,32,8,128]{3,2,1,0:T(8,128)(2,1)S(1)} %shard_map.123.same.order), channel_id=1, source_target_pairs={{0,1},{1,0},{2,3},{3,2},{4,5},{5,4},{6,7},{7,6},{8,9},{9,8},{10,11... | collective-permute-start | bytes 786440 | tf_op jit(solution)/shard_map/ppermute | solution.py:724
  94.1 2.2 %collective-permute-start.19 = (bf16[4,32,8,128]{3,2,1,0:T(8,128)(2,1)S(1)}, bf16[4,32,8,128]{3,2,1,0:T(8,128)(2,1)S(1)}, u32[]{:S(2)}, u32[]{:S(2)}) collective-permute-start(bf16[4,32,8,128]{3,2,1,0:T(8,128)(2,1)S(1)} %collective-permute-done.17.same_x), channel_id=1, source_target_pairs={{0,1},{1,0},{2,3},{3,2},{4,5},{5,4},{6,7},{7,6},{8,9},{9,8},{10,11... | collective-permute-start | bytes 786440 | tf_op jit(solution)/shard_map/ppermute | solution.py:724

commit v15 on v14

--- a/solution.py
+++ b/solution.py
@@ -482,28 +482,25 @@
     bias_units(sums, bias_out)
 
 
-def lat_sums_split(*refs):
+def lat_split(keep, got, *refs):
     keep_out, give_out = refs[-2:]
+    units = keep.shape[1]
     x = lax.rem(lax.axis_index("lon"), 2)
     for out, side in ((keep_out, x), (give_out, 1 - x)):
         for z in range(out.shape[0]):
             j = 2 * z + side
-            at = 0
-            for k in range(0, len(refs) - 4, 2):
-                keep, got = refs[k], refs[k + 1]
-                count = keep.shape[1]
-                total = keep[j].astype(F32) + got[j].astype(F32)
-                out[z, at : at + count] = total.astype(BF16)
-                at += count
-            out[z, at:] = refs[-4][j]
-
-
-def split_z(keep, got, own_out, *give_outs):
-    count = keep.shape[0]
+            out[z, 0:units] = (keep[j].astype(F32) + got[j].astype(F32)).astype(BF16)
+            if out.shape[1] > units:
+                out[z, units:] = refs[0][j]
+
+
+def split_z(first, second, got_first, got_second, *outs):
+    count, cut = first.shape[:2]
     z = lax.div(lax.axis_index("lon"), 2)
-    for k, out in enumerate((own_out,) + give_outs):
+    for k, out in enumerate(outs):
         at = lax.rem(z + k, count)
-        out[...] = (keep[at].astype(F32) + got[at].astype(F32)).astype(BF16)
+        out[0:cut] = (first[at].astype(F32) + got_first[at].astype(F32)).astype(BF16)
+        out[cut:] = (second[at].astype(F32) + got_second[at].astype(F32)).astype(BF16)
 
 
 def sum_refs(*refs):
@@ -583,7 +580,7 @@
 
 
 def fourth_kernel(
-    x_in, qkv, probs, dmix, rg, gain_two, gains_late, qkv_w, gains,
+    x_in, qkv, probs, dmix, rg, gain_two, gains_late, order, qkv_w, gains,
     tokens_out, keep, give, bias_out,
     field, sums, m576, flat_scr, dx_scr, low_scr, prob_scr,
 ):
@@ -655,7 +652,7 @@
 
 
 def late_kernel(
-    units_a, spread, same, same_x, cross, cross_x, flat_out, squares_out, bias_out,
+    units_a, extra, spread, same, same_x, cross, cross_x, flat_out, squares_out, bias_out,
     rows_scr, wide_scr, tab_scr, a,
 ):
     lat = lax.axis_index("lat")
@@ -665,32 +662,34 @@
         a[lat, 2 * z + 1 - x] = same_x[z]
         a[1 - lat, 2 * z + x] = cross[z]
         a[1 - lat, 2 * z + 1 - x] = cross_x[z]
-    squares_out[...] = place(a, 0, units_a, [(0, flat_out.shape[0])], flat_out)
+    total = place(a, 0, units_a, [(0, 3456)], flat_out)
+    squares_out[...] = total + place(
+        a, units_a + extra, a.shape[2], [(3456, flat_out.shape[0] - 3456)], flat_out
+    )
     bias_rows(a, units_a, spread, bias_out, rows_scr, wide_scr, tab_scr)
 
 
 def last_kernel(
-    units_b, units_c, spread, flat_a, squares, bias_late, own_bc, oth_bc, update_out, bias_out,
-    scr, rows_scr, wide_scr, tab_scr, bc,
+    units_c, spread, flat_ab, squares, bias_late, own_c, oth_c, update_out, bias_out,
+    scr, rows_scr, wide_scr, tab_scr, c,
 ):
     lat = lax.axis_index("lat")
-    for j in range(own_bc.shape[0]):
-        bc[lat, j] = own_bc[j]
-        bc[1 - lat, j] = oth_bc[j]
-    total = squares[...]
-    total = total + place(bc, 0, units_b, [(864, 288), (1152, 1152), (2304, 1152)], scr)
-    total = total + place(bc, units_b, units_b + units_c, [(0, 864), (3456, 8)], scr)
+    for j in range(own_c.shape[0]):
+        c[lat, j] = own_c[j]
+        c[1 - lat, j] = oth_c[j]
+    total = squares[...] + place(c, 0, units_c, [(0, 872)], scr)
     count = update_out.shape[0]
     mean = jnp.sum(total) * (1.0 / (count * 128))
     scale = lax.rsqrt(mean + 1e-06)
-    early, late = (0, 1728, 2304, 4608), (864, 2016, 3456, 5760)
+    update_out[0:864, :] = (scr[0:864, :] * scale).astype(BF16)
     at = 0
-    for first, second, rows in zip(early, late, (864, 288, 1152, 1152)):
-        update_out[first : first + rows, :] = (scr[at : at + rows, :] * scale).astype(BF16)
-        update_out[second : second + rows, :] = (flat_a[at : at + rows, :] * scale).astype(BF16)
+    for where, rows in (
+        (864, 864), (2016, 288), (3456, 1152), (5760, 1152), (1728, 288), (2304, 1152), (4608, 1152)
+    ):
+        update_out[where : where + rows, :] = (flat_ab[at : at + rows, :] * scale).astype(BF16)
         at += rows
-    update_out[6912:count, :] = (scr[at : at + count - 6912, :] * scale).astype(BF16)
-    bias_rows(bc, units_b + units_c, spread, bias_out.at[0], rows_scr, wide_scr, tab_scr)
+    update_out[6912:count, :] = (scr[864 : 864 + count - 6912, :] * scale).astype(BF16)
+    bias_rows(c, units_c, spread, bias_out.at[0], rows_scr, wide_scr, tab_scr)
     bias_out[1] = bias_late[...]
 
 
@@ -901,7 +900,7 @@
 
     units_xa = units_a + extra
     keep_xa, give_xa = call(
-        lat_sums_split, [units(zs, units_xa)] * 2, [], (keep_a, got_a, bias_a, keep_a), 1, 10
+        lat_split, [units(zs, units_xa)] * 2, [], (keep_a, got_a, bias_a), 1, 10
     )
     got_xa = x_swap(give_xa)
 
@@ -923,6 +922,10 @@
         14,
     )
     got_b = lat_swap(give_b)
+    keep_xb, give_xb = call(
+        lat_split, [units(zs, units_b)] * 2, [], (keep_b, got_b), 1, 10
+    )
+    got_xb = x_swap(give_xb)
 
     tokens_grad, keep_c, give_c, bias_c = call(
         fourth_kernel,
@@ -941,64 +944,57 @@
             stack_shape,
             stack_shape,
         ],
-        (x0, qkv0, probs0, dmix0, rg0, gain_two, gains1, qkv_weight, norm_gain),
+        (x0, qkv0, probs0, dmix0, rg0, gain_two, gains1, keep_xb, qkv_weight, norm_gain),
         7,
         14,
     )
     got_c = lat_swap(give_c)
-    own_a, *gives_a = call(
-        split_z, [units(units_xa)] * zs, [], (keep_xa, got_xa), 1, 10
-    )
-    gots_a = [lon_send(give, 2 * (k + 1)) for k, give in enumerate(gives_a)]
-    units_bc = units_b + units_c + extra
+    units_ab = units_xa + units_b
+    own_ab, *gives_ab = call(
+        split_z, [units(units_ab)] * zs, [], (keep_xa, keep_xb, got_xa, got_xb), 1, 10
+    )
+    gots_ab = [lon_send(give, 2 * (k + 1)) for k, give in enumerate(gives_ab)]
+    units_xc = units_c + extra
     keep_x, give_x = call(
-        lat_sums_split,
-        [units(zs, units_bc)] * 2,
-        [],
-        (keep_b, got_b, keep_c, got_c, bias_c, own_a),
-        1,
-        10,
+        lat_split, [units(zs, units_xc)] * 2, [], (keep_c, got_c, bias_c, own_ab), 1, 10
     )
     got_x = x_swap(give_x)
-    (sum_a,) = call(sum_refs, [units(units_xa)], [], (own_a, *gots_a, keep_x), 1, 10)
-    (part_z,) = call(add_pair, [units(zs, units_bc)], [], (keep_x, got_x, sum_a), 1, 10)
-    pieces_bc = lax.all_to_all(
+    (sum_ab,) = call(sum_refs, [units(units_ab)], [], (own_ab, *gots_ab, keep_x), 1, 10)
+    (part_z,) = call(add_pair, [units(zs, units_xc)], [], (keep_x, got_x, sum_ab), 1, 10)
+    pieces_c = lax.all_to_all(
         part_z,
         "lon",
         0,
         0,
         axis_index_groups=[[2 * z + x for z in range(zs)] for x in range(2)],
     )
-    moved_a = [lon_send(sum_a, 2 * k) for k in range(1, zs)]
-    (same,) = call(join_z, [units(zs, units_xa)], [], [sum_a, *moved_a, part_z], 1, 10)
+    moved_ab = [lon_send(sum_ab, 2 * k) for k in range(1, zs)]
+    (sum_c,) = call(
+        sum_pieces, [units(lon_size, units_xc)], [], (pieces_c, moved_ab[0]), 1, 10
+    )
+    whole_c = lax.all_to_all(sum_c, "lon", 0, 0)
+    (same,) = call(join_z, [units(zs, units_ab)], [], [sum_ab, *moved_ab, sum_c], 1, 10)
     same_x = x_swap(same)
     cross = lat_swap(same)
     cross_x = lat_swap(same_x)
-    (sum_bc,) = call(
-        sum_pieces, [units(lon_size, units_bc)], [], (pieces_bc, same), 1, 10
-    )
-    whole_bc = lax.all_to_all(sum_bc, "lon", 0, 0)
-    oth_bc = lat_swap(whole_bc)
+    oth_c = lat_swap(whole_c)
 
     flat_rows = (2 * block_rows * 128 + norm_gain.size) // 128
     fold_scr = [((CHUNK * 8, PAIR), F32), wide_scr, tab_scr]
-    flat_a, squares, bias_late = call(
-        functools.partial(late_kernel, units_a),
-        [((block_rows, 128), F32), ((UNIT, 128), F32), (table.shape[1:], F32)],
-        [*fold_scr, units(2, lon_size, units_a + extra)],
+    ab_rows = 2 * block_rows - qkv_rows
+    flat_ab, squares, bias_late = call(
+        functools.partial(late_kernel, units_a, extra),
+        [((ab_rows, 128), F32), ((UNIT, 128), F32), (table.shape[1:], F32)],
+        [*fold_scr, units(2, lon_size, units_ab)],
         (spread, same, same_x, cross, cross_x),
         2,
         14,
     )
     update, bias_grad = call(
-        functools.partial(last_kernel, units_b, units_c),
+        functools.partial(last_kernel, units_c),
         [((flat_rows, 128), BF16), (table.shape, F32)],
-        [
-            ((block_rows + 8, 128), F32),
-            *fold_scr,
-            units(2, lon_size, units_b + units_c + extra),
-        ],
-        (spread, flat_a, squares, bias_late, whole_bc, oth_bc),
+        [((872, 128), F32), *fold_scr, units(2, lon_size, units_xc)],
+        (spread, flat_ab, squares, bias_late, whole_c, oth_c),
         2,
         14,
     )

time: 99.6 us -> 109 us (1.094)
  blocking collectives: 0 us -> 11.3 us
  starting transfers between devices: 27.9 us -> 21.3 us
  waiting for transfers between devices: 37.6 us -> 44 us
  Pallas kernels: 32.9 us -> 30.8 us
    ppermute x3 -> x4, waiting for transfers between devices: 0.01 us -> 15.5 us  [x_swap(): return lax.ppermute(value, 'lon', [(s, s ^ 1) for s in range(count)])]
    all_to_all x1 -> x0, waiting for transfers between devices: 12.1 us -> none  [shards(): whole_bc = lax.all_to_all(sum_bc, 'lon', 0, 0)]
    all_to_all x0 -> x1, blocking collectives: none -> 11.3 us  [shards(): whole_c = lax.all_to_all(sum_c, 'lon', 0, 0)]
    all_to_all x1 -> x0, starting transfers between devices: 3.54 us -> none  [shards(): whole_bc = lax.all_to_all(sum_bc, 'lon', 0, 0)]
    ppermute x8, waiting for transfers between devices: 17.3 us -> 20.1 us  [lon_send(): lax.ppermute(value, 'lon', [(s, (s + step) % count) for s in range(count)])]
    pallas_call x15 -> x16, Pallas kernels: 32.9 us -> 30.8 us  [call(): pl.pallas_call(kernel, out_shape=[(pltpu.VMEM if at in near else jax.Shap...]
    ppermute x3 -> x4, starting transfers between devices: 3.11 us -> 1.45 us  [x_swap(): return lax.ppermute(value, 'lon', [(s, s ^ 1) for s in range(count)])]
  transfers between devices with their start and end apart: 23 -> 23, of which waited for: 12 -> 14; matrix products, arithmetic and copies ran while one was open for 0% -> 0% of each run, Pallas kernels for 12% -> 8%
where the time goes in v15:
time: 109 us; the launch traced here: 108 us
  waiting for transfers between devices  44 us (40%)
  Pallas kernels  30.8 us (28%)
  starting transfers between devices  21.3 us (20%)
  blocking collectives  11.3 us (10%)
    pallas_call x16, Pallas kernels, call(): pl.pallas_call(kernel, out_shape=[(pltpu.VMEM if at in near else jax.Shap...  30.8 us
    ppermute x8, waiting for transfers between devices, lon_send(): lax.ppermute(value, 'lon', [(s, (s + step) % count) for s in range(count)])  20.1 us
    ppermute x4, waiting for transfers between devices, x_swap(): return lax.ppermute(value, 'lon', [(s, s ^ 1) for s in range(count)])  15.5 us
    all_to_all x1, blocking collectives, shards(): whole_c = lax.all_to_all(sum_c, 'lon', 0, 0)  11.3 us
    ppermute x8, starting transfers between devices, lon_send(): lax.ppermute(value, 'lon', [(s, (s + step) % count) for s in range(count)])  9.36 us
    ppermute x2, starting transfers between devices, diag_send(): return lax.ppermute(value, ('lon', 'lat'), pairs)  5.64 us
    ppermute x2, waiting for transfers between devices, diag_send(): return lax.ppermute(value, ('lon', 'lat'), pairs)  4.81 us
    all_to_all x1, starting transfers between devices, shards(): lax.all_to_all(part_z, 'lon', 0, 0, axis_index_groups=[[2 * z + x for z i...  3.75 us
  transfers between devices with their start and end apart: 23, of which 14 were waited for; matrix products, arithmetic and copies ran while one was open for 0% of the time, Pallas kernels for 8%

profile of v15, /device:TPU:0, one launch (start us, length us, event | category | flops | bytes accessed | tf_op | source)
XLA Modules:
  0.0 108.3 jit_solution(17808317167376590696)
XLA Ops:
  0.6 0.0 copy-start.6
  0.7 6.6 %shard_map.112 = (bf16[576,192]{1,0:T(8,128)(2,1)S(1)}, bf16[2,504,192]{2,1,0:T(8,128)(2,1)S(1)}, bf16[2,72,192]{2,1,0:T(8,128)(2,1)S(1)}, bf16[576,576]{1,0:T(8...) custom-call(bf16[2,12,24,192]{3,2,1,0:T(8,128)(2,1)} %tokens_in.1, ...), custom_call_target="tpu_custom_call" | custom-call | flops 8800000000 | bytes 100000 | tf_op jit(solution)/shard_map/pallas_call | solution.py:698
  7.2 0.5 collective-permute-start.1
  7.7 5.6 %collective-permute-start.2 = (bf16[2,72,192]{2,1,0:T(8,128)(2,1)S(1)}, bf16[2,72,192]{2,1,0:T(8,128)(2,1)S(1)}, u32[]{:S(2)}, u32[]{:S(2)}) collective-permute-start(bf16[2,72,192]{2,1,0:T(8,128)(2,1)S(1)} %get-tuple-element.61), channel_id=1, source_target_pairs={{0,15},{1,14},{2,1},{3,0},{4,3},{5,2},{6,5},{7,4},{8,7},{9,6},{10,... | collective-permute-start | bytes 165896 | tf_op jit(solution)/shard_map/ppermute | solution.py:742
  13.4 0.5 collective-permute-start
  13.9 0.0 copy-start.5
  14.0 2.0 %shard_map.113 = (f32[864,144]{1,0:T(8,128)S(1)}, bf16[576,768]{1,0:T(8,128)(2,1)S(1)}) custom-call(f32[2,6,1,6336]{3,2,1,0:T(1,128)S(1)} %bitcast.8, bf16[2,132,384]{2,1,0:T(8,128)(2,1)S(1)} %copy-done.6, f32[576,768]{1,0:T(8,128)S(1)} %get-tuple-element.62.hidden), custom_call_target="tpu_custom_call" | custom-call | flops 3300000000 | bytes 100000 | tf_op jit(solution)/shard_map/pallas_call | solution.py:698
  15.9 0.0 collective-permute-done.2.diag_head
  16.0 1.8 %collective-permute-done.lon_head = bf16[2,72,192]{2,1,0:T(8,128)(2,1)S(1)} collective-permute-done((bf16[2,72,192]{2,1,0:T(8,128)(2,1)S(1)}, bf16[2,72,192]{2,1,0:T(8,128)(2,1)S(1)}, u32[]{:S(2)}, u32[]{:S(2)}) %collective-permute-start) | collective-permute-done | bytes 55328 | tf_op jit(solution)/shard_map/ppermute | solution.py:728
  17.8 8.9 %shard_map.114 = (bf16[504,192]{1,0:T(8,128)(2,1)S(1)}, bf16[72,192]{1,0:T(8,128)(2,1)S(1)}, bf16[576,192]{1,0:T(8,128)(2,1)S(1)}, bf16[576,576]{1,0:T(8,128)(2,...) custom-call(bf16[2,504,192]{2,1,0:T(8,128)(2,1)S(1)} %get-tuple-elem, ...), custom_call_target="tpu_custom_call", output_to_operand_aliasing={{12}: (10, {}), {13}: (11, {}), {14}: (12, {}), {15}: (13, ... | custom-call | flops 20899999744 | bytes 100000 | tf_op jit(solution)/shard_map/pallas_call | solution.py:698
  26.7 1.6 %shard_map.115 = (bf16[8,27,8,128]{3,2,1,0:T(8,128)(2,1)S(1)}, bf16[8,27,8,128]{3,2,1,0:T(8,128)(2,1)S(1)}, bf16[8,5,8,128]{3,2,1,0:T(8,128)(2,1)S(1)}) custom-call(bf16[576,192]{1,0:T(8,128)(2,1)S(1)} %get-tuple-element.80.n1, bf16[576,576]{1,0:T(8,128)(2,1)S(1)} %get-tuple-element.81.field, bf16[576,192]{1,0:T(8,128)(2,1)S(1)} %get-tuple-element.82.mixed, ...), custom_call_target="tpu_custom_call" | custom-call | flops 3300000000 | bytes 100000 | tf_op jit(solution)/shard_map/pallas_call | solution.py:698
  28.3 0.1 collective-permute-start.6
  28.4 0.5 collective-permute-start.4
  28.9 1.3 %collective-permute-done.6.got = bf16[8,27,8,128]{3,2,1,0:T(8,128)(2,1)S(1)} collective-permute-done((bf16[8,27,8,128]{3,2,1,0:T(8,128)(2,1)S(1)}, bf16[8,27,8,128]{3,2,1,0:T(8,128)(2,1)S(1)}, u32[]{:S(2)}, u32[]{:S(2)}) %collective-permute-start.6) | collective-permute-done | bytes 442400 | tf_op jit(solution)/shard_map/ppermute | solution.py:723
  30.2 0.1 shard_map.116
  30.3 4.8 %collective-permute-done.5.diag_tail = bf16[72,192]{1,0:T(8,128)(2,1)S(1)} collective-permute-done((bf16[72,192]{1,0:T(8,128)(2,1)S(1)}, bf16[72,192]{1,0:T(8,128)(2,1)S(1)}, u32[]{:S(2)}, u32[]{:S(2)}) %collective-permute-start.5) | collective-permute-done | bytes 27680 | tf_op jit(solution)/shard_map/ppermute | solution.py:742
  35.1 1.1 %collective-permute-done.3.lon_tail = bf16[72,192]{1,0:T(8,128)(2,1)S(1)} collective-permute-done((bf16[72,192]{1,0:T(8,128)(2,1)S(1)}, bf16[72,192]{1,0:T(8,128)(2,1)S(1)}, u32[]{:S(2)}, u32[]{:S(2)}) %collective-permute-start.3) | collective-permute-done | bytes 27680 | tf_op jit(solution)/shard_map/ppermute | solution.py:728
  36.2 2.2 %shard_map.117 = (bf16[8,21,8,128]{3,2,1,0:T(8,128)(2,1)S(1)}, bf16[8,21,8,128]{3,2,1,0:T(8,128)(2,1)S(1)}, f32[576,192]{1,0:T(8,128)S(1)}, bf16[576,192]{1,0:T(8,128)(2,1)S(1)}, f32[1,192]{1,0:T(1,128)S(1)}) custom-call(bf16[504,192]{1,0:T(8,128)(2,1)S(1)} %get-tuple-element.74.head, bf16[72,192]{1,0:T(8,128)(2,1)S(1)} %collective-permute-done.3.lon_tail, ...), custom_call_target="tpu_custom_call" | custom-call | flops 3300000000 | bytes 100000 | tf_op jit(solution)/shard_map/pallas_call | solution.py:698
  38.3 0.1 collective-permute-start.7
  38.4 0.1 collective-permute-start.8
  38.5 1.6 %collective-permute-done.7.got = bf16[8,21,8,128]{3,2,1,0:T(8,128)(2,1)S(1)} collective-permute-done((bf16[8,21,8,128]{3,2,1,0:T(8,128)(2,1)S(1)}, bf16[8,21,8,128]{3,2,1,0:T(8,128)(2,1)S(1)}, u32[]{:S(2)}, u32[]{:S(2)}) %collective-permute-start.7) | collective-permute-done | bytes 344096 | tf_op jit(solution)/shard_map/ppermute | solution.py:723
  40.0 0.1 shard_map.118
  40.1 0.5 collective-permute-start.9
  40.7 5.7 %shard_map.119 = (bf16[2,12,24,192]{3,2,1,0:T(8,128)(2,1)}, bf16[8,7,8,128]{3,2,1,0:T(8,128)(2,1)S(1)}, bf16[8,7,8,128]{3,2,1,0:T(8,128)(2,1)S(1)}, bf16[8,5,8,128]{3,2,1,0:T(8,128)(2,1)S(1)}) custom-call(bf16[576,192]{1,0:T(8,128)(2,1)S(1)} %get-tuple-element.71.x_in, bf16[576,576]{1,0:T(8,128)(2,1)S(1)} %get-tuple-element.72.qkv, ...), custom_call_target="tpu_custom_call" | custom-call | flops 7699999744 | bytes 100000 | tf_op jit(solution)/shard_map/pallas_call | solution.py:698
  46.4 1.2 %collective-permute-done.8.got_first = bf16[4,32,8,128]{3,2,1,0:T(8,128)(2,1)S(1)} collective-permute-done((bf16[4,32,8,128]{3,2,1,0:T(8,128)(2,1)S(1)}, bf16[4,32,8,128]{3,2,1,0:T(8,128)(2,1)S(1)}, u32[]{:S(2)}, u32[]{:S(2)}) %collective-permute-start.8) | collective-permute-done | bytes 262176 | tf_op jit(solution)/shard_map/ppermute | solution.py:733
  47.6 3.2 %collective-permute-done.9.got_second = bf16[4,21,8,128]{3,2,1,0:T(8,128)(2,1)S(1)} collective-permute-done((bf16[4,21,8,128]{3,2,1,0:T(8,128)(2,1)S(1)}, bf16[4,21,8,128]{3,2,1,0:T(8,128)(2,1)S(1)}, u32[]{:S(2)}, u32[]{:S(2)}) %collective-permute-start.9) | collective-permute-done | bytes 172064 | tf_op jit(solution)/shard_map/ppermute | solution.py:733
  50.8 0.1 shard_map.120
  50.9 0.1 collective-permute-start.10
  51.0 2.8 %collective-permute-start.11 = (bf16[53,8,128]{2,1,0:T(8,128)(2,1)S(1)}, bf16[53,8,128]{2,1,0:T(8,128)(2,1)S(1)}, u32[]{:S(2)}, u32[]{:S(2)}) collective-permute-start(bf16[53,8,128]{2,1,0:T(8,128)(2,1)S(1)} %get-tuple-element.105), channel_id=1, source_target_pairs={{0,8},{2,10},{4,12},{6,14},{8,0},{10,2},{12,4},{14,6},{1,9},{3,11}... | collective-permute-start | bytes 325640 | tf_op jit(solution)/shard_map/ppermute | solution.py:728
  53.8 1.0 collective-permute-start.12
  54.9 0.3 collective-permute-start.17
  55.2 3.5 %collective-permute-done.10.refs_1_ = bf16[53,8,128]{2,1,0:T(8,128)(2,1)S(1)} collective-permute-done((bf16[53,8,128]{2,1,0:T(8,128)(2,1)S(1)}, bf16[53,8,128]{2,1,0:T(8,128)(2,1)S(1)}, u32[]{:S(2)}, u32[]{:S(2)}) %collective-permute-start.10) | collective-permute-done | bytes 108576 | tf_op jit(solution)/shard_map/ppermute | solution.py:728
  58.7 3.4 %collective-permute-done.11.refs_2_ = bf16[53,8,128]{2,1,0:T(8,128)(2,1)S(1)} collective-permute-done((bf16[53,8,128]{2,1,0:T(8,128)(2,1)S(1)}, bf16[53,8,128]{2,1,0:T(8,128)(2,1)S(1)}, u32[]{:S(2)}, u32[]{:S(2)}) %collective-permute-start.11) | collective-permute-done | bytes 108576 | tf_op jit(solution)/shard_map/ppermute | solution.py:728
  62.1 0.1 shard_map.122.order.refs_0_
  62.2 0.7 shard_map.123
  62.9 3.7 %all-to-all-start = ((bf16[4,12,8,128]{3,2,1,0:T(8,128)(2,1)}), bf16[4,12,8,128]{3,2,1,0:T(8,128)(2,1)S(1)}, u32[]{:S(2)}, u32[]{:S(2)}) async-start(bf16[4,12,8,128]{3,2,1,0:T(8,128)(2,1)} %shard_map.123), calls=%async_computation | async-start | bytes 196608 | tf_op jit(solution)/shard_map/all_to_all | solution.py:964
  66.6 2.0 %collective-permute-start.14 = (bf16[53,8,128]{2,1,0:T(8,128)(2,1)S(1)}, bf16[53,8,128]{2,1,0:T(8,128)(2,1)S(1)}, u32[]{:S(2)}, u32[]{:S(2)}) collective-permute-start(bf16[53,8,128]{2,1,0:T(8,128)(2,1)S(1)} %shard_map.122.order.refs_0_), channel_id=1, source_target_pairs={{0,4},{2,6},{4,8},{6,10},{8,12},{10,14},{12,0},{14,2},{1,5},{3,7},... | collective-permute-start | bytes 325640 | tf_op jit(solution)/shard_map/ppermute | solution.py:728
  68.7 1.8 %collective-permute-start.16 = (bf16[53,8,128]{2,1,0:T(8,128)(2,1)S(1)}, bf16[53,8,128]{2,1,0:T(8,128)(2,1)S(1)}, u32[]{:S(2)}, u32[]{:S(2)}) collective-permute-start(bf16[53,8,128]{2,1,0:T(8,128)(2,1)S(1)} %shard_map.122.order.refs_0_), channel_id=1, source_target_pairs={{0,12},{2,14},{4,0},{6,2},{8,4},{10,6},{12,8},{14,10},{1,13},{3,15... | collective-permute-start | bytes 325640 | tf_op jit(solution)/shard_map/ppermute | solution.py:728
  70.5 1.1 %collective-permute-start.15 = (bf16[53,8,128]{2,1,0:T(8,128)(2,1)S(1)}, bf16[53,8,128]{2,1,0:T(8,128)(2,1)S(1)}, u32[]{:S(2)}, u32[]{:S(2)}) collective-permute-start(bf16[53,8,128]{2,1,0:T(8,128)(2,1)S(1)} %shard_map.122.order.refs_0_), channel_id=1, source_target_pairs={{0,8},{2,10},{4,12},{6,14},{8,0},{10,2},{12,4},{14,6},{1,9},{3,11}... | collective-permute-start | bytes 325640 | tf_op jit(solution)/shard_map/ppermute | solution.py:728
  71.6 4.6 %collective-permute-done.14.order.refs_1_ = bf16[53,8,128]{2,1,0:T(8,128)(2,1)S(1)} collective-permute-done((bf16[53,8,128]{2,1,0:T(8,128)(2,1)S(1)}, bf16[53,8,128]{2,1,0:T(8,128)(2,1)S(1)}, u32[]{:S(2)}, u32[]{:S(2)}) %collective-permute-start.14) | collective-permute-done | bytes 108576 | tf_op jit(solution)/shard_map/ppermute | solution.py:728
  76.2 0.1 collective-permute-done.16.refs_3_
  76.3 5.6 %collective-permute-done.15.refs_2_ = bf16[53,8,128]{2,1,0:T(8,128)(2,1)S(1)} collective-permute-done((bf16[53,8,128]{2,1,0:T(8,128)(2,1)S(1)}, bf16[53,8,128]{2,1,0:T(8,128)(2,1)S(1)}, u32[]{:S(2)}, u32[]{:S(2)}) %collective-permute-start.15) | collective-permute-done | bytes 108576 | tf_op jit(solution)/shard_map/ppermute | solution.py:728
  82.0 0.5 collective-permute-start.18
  82.5 11.0 %collective-permute-done.18.same_x = bf16[4,53,8,128]{3,2,1,0:T(8,128)(2,1)S(1)} collective-permute-done((bf16[4,53,8,128]{3,2,1,0:T(8,128)(2,1)S(1)}, bf16[4,53,8,128]{3,2,1,0:T(8,128)(2,1)S(1)}, u32[]{:S(2)}, u32[]{:S(2)}) %collective-permute-start.18) | collective-permute-done | bytes 434208 | tf_op jit(solution)/shard_map/ppermute | solution.py:733
  93.6 11.3 %all_to_all.10.own_c = bf16[8,12,8,128]{3,2,1,0:T(8,128)(2,1)S(1)} all-to-all(bf16[8,12,8,128]{3,2,1,0:T(8,128)(2,1)S(1)} %shard_map.124.refs_4_), channel_id=1, replica_groups=mesh['grp'=2,'lon'=8,'lat'=2] {'lon'}, dimensions={0} | all-to-all | bytes 393216 | tf_op jit(solution)/shard_map/all_to_all | solution.py:975
  104.9 0.7 shard_map.126
  105.5 0.8 collective-permute-done.21.oth_c
  106.3 2.0 %shard_map.127 = (bf16[6918,128]{1,0:T(8,128)(2,1)}, f32[2,6,1,6336]{3,2,1,0:T(1,128)}) custom-call(bf16[2,132,384]{2,1,0:T(8,128)(2,1)S(1)} %copy-done.6, f32[6048,128]{1,0:T(8,128)S(1)} %get-tuple-element.112.flat_ab, f32[8,128]{1,0:T(8,128)S(1)} %get-tuple-element.113.squares, f32[6,1,6336]{2,1,0:T(1,128)S(1)} %get-tuple-element.114.bias_late, ...), custom_call_target="tpu_custom_call" | custom-call | flops 2200000000 | bytes 100000 | tf_op jit(solution)/shard_map/pallas_call | solution.py:698
  (29 shorter events, 0.2 us)
Async XLA Ops:
  0.6 13.3 %copy-start.3 = (f32[2,1,6,6336]{3,1,2,0:T(1,128)S(1)}, f32[2,1,6,6336]{3,1,2,0:T(1,128)}, u32[]{:S(2)}) copy-start(f32[2,1,6,6336]{3,1,2,0:T(1,128)} %param.16) | copy-start | bytes 912388
  0.6 13.3 %copy-start.6 = (bf16[2,132,384]{2,1,0:T(8,128)(2,1)S(1)}, bf16[2,132,384]{2,1,0:T(8,128)(2,1)}, u32[]{:S(2)}) copy-start(bf16[2,132,384]{2,1,0:T(8,128)(2,1)} %constant.2.clone.spread_in.spread) | copy-start | bytes 608260
  7.2 10.5 %collective-permute-start.1 = (bf16[2,504,192]{2,1,0:T(8,128)(2,1)S(1)}, bf16[2,504,192]{2,1,0:T(8,128)(2,1)S(1)}, u32[]{:S(2)}, u32[]{:S(2)}) collective-permute-start(bf16[2,504,192]{2,1,0:T(8,128)(2,1)S(1)} %get-tuple-element.60.tail), channel_id=1, source_target_pairs={{0,1},{1,0},{2,3},{3,2},{4,5},{5,4},{6,7},{7,6},{8,9},{9,8},{10,11... | collective-permute-start | bytes 1161224 | tf_op jit(solution)/shard_map/ppermute | solution.py:723
  7.7 8.2 %collective-permute-start.2 = (bf16[2,72,192]{2,1,0:T(8,128)(2,1)S(1)}, bf16[2,72,192]{2,1,0:T(8,128)(2,1)S(1)}, u32[]{:S(2)}, u32[]{:S(2)}) collective-permute-start(bf16[2,72,192]{2,1,0:T(8,128)(2,1)S(1)} %get-tuple-element.61), channel_id=1, source_target_pairs={{0,15},{1,14},{2,1},{3,0},{4,3},{5,2},{6,5},{7,4},{8,7},{9,6},{10,... | collective-permute-start | bytes 165896 | tf_op jit(solution)/shard_map/ppermute | solution.py:742
  13.4 4.4 %collective-permute-start = (bf16[2,72,192]{2,1,0:T(8,128)(2,1)S(1)}, bf16[2,72,192]{2,1,0:T(8,128)(2,1)S(1)}, u32[]{:S(2)}, u32[]{:S(2)}) collective-permute-start(bf16[2,72,192]{2,1,0:T(8,128)(2,1)S(1)} %get-tuple-element.61), channel_id=1, source_target_pairs={{0,14},{2,0},{4,2},{6,4},{8,6},{10,8},{12,10},{14,12},{1,15},{3,1}... | collective-permute-start | bytes 165896 | tf_op jit(solution)/shard_map/ppermute | solution.py:728
  13.9 3.8 %copy-start = (bf16[2,192,768]{2,1,0:T(8,128)(2,1)S(1)}, bf16[2,192,768]{2,1,0:T(8,128)(2,1)}, u32[]{:S(2)}) copy-start(bf16[2,192,768]{2,1,0:T(8,128)(2,1)} %up_w.3) | copy-start | bytes 1769476
  13.9 3.8 %copy-start.1 = (bf16[2,768,192]{1,2,0:T(8,128)(2,1)S(1)}, bf16[2,768,192]{1,2,0:T(8,128)(2,1)}, u32[]{:S(2)}) copy-start(bf16[2,768,192]{1,2,0:T(8,128)(2,1)} %param.14) | copy-start | bytes 1769476
  13.9 3.8 %copy-start.2 = (bf16[2,192,576]{2,1,0:T(8,128)(2,1)S(1)}, bf16[2,192,576]{2,1,0:T(8,128)(2,1)}, u32[]{:S(2)}) copy-start(bf16[2,192,576]{2,1,0:T(8,128)(2,1)} %qkv_w.3) | copy-start | bytes 1327108
  13.9 3.8 %copy-start.4 = (bf16[2,192,192]{2,1,0:T(8,128)(2,1)S(1)}, bf16[2,192,192]{2,1,0:T(8,128)(2,1)}, u32[]{:S(2)}) copy-start(bf16[2,192,192]{2,1,0:T(8,128)(2,1)} %proj_w.3) | copy-start | bytes 442372
  13.9 3.8 %copy-start.5 = (f32[2,2,192]{2,1,0:T(2,128)S(1)}, f32[2,2,192]{2,1,0:T(2,128)}, u32[]{:S(2)}) copy-start(f32[2,2,192]{2,1,0:T(2,128)} %gains.5) | copy-start | bytes 9220
  28.3 1.8 %collective-permute-start.6 = (bf16[8,27,8,128]{3,2,1,0:T(8,128)(2,1)S(1)}, bf16[8,27,8,128]{3,2,1,0:T(8,128)(2,1)S(1)}, u32[]{:S(2)}, u32[]{:S(2)}) collective-permute-start(bf16[8,27,8,128]{3,2,1,0:T(8,128)(2,1)S(1)} %get-tuple-element.90), channel_id=1, source_target_pairs={{0,1},{1,0},{2,3},{3,2},{4,5},{5,4},{6,7},{7,6},{8,9},{9,8},{10,11... | collective-permute-start | bytes 1327112 | tf_op jit(solution)/shard_map/ppermute | solution.py:723
  28.4 7.8 %collective-permute-start.4 = (bf16[504,192]{1,0:T(8,128)(2,1)S(1)}, bf16[504,192]{1,0:T(8,128)(2,1)S(1)}, u32[]{:S(2)}, u32[]{:S(2)}) collective-permute-start(bf16[504,192]{1,0:T(8,128)(2,1)S(1)} %get-tuple-element.74.head), channel_id=1, source_target_pairs={{0,1},{1,0},{2,3},{3,2},{4,5},{5,4},{6,7},{7,6},{8,9},{9,8},{10,11... | collective-permute-start | bytes 580616 | tf_op jit(solution)/shard_map/ppermute | solution.py:723
  28.9 6.2 %collective-permute-start.5 = (bf16[72,192]{1,0:T(8,128)(2,1)S(1)}, bf16[72,192]{1,0:T(8,128)(2,1)S(1)}, u32[]{:S(2)}, u32[]{:S(2)}) collective-permute-start(bf16[72,192]{1,0:T(8,128)(2,1)S(1)} %get-tuple-element.75), channel_id=1, source_target_pairs={{0,3},{1,2},{2,5},{3,4},{4,7},{5,6},{6,9},{7,8},{8,11},{9,10},{10,... | collective-permute-start | bytes 82952 | tf_op jit(solution)/shard_map/ppermute | solution.py:742
  28.9 7.3 %collective-permute-start.3 = (bf16[72,192]{1,0:T(8,128)(2,1)S(1)}, bf16[72,192]{1,0:T(8,128)(2,1)S(1)}, u32[]{:S(2)}, u32[]{:S(2)}) collective-permute-start(bf16[72,192]{1,0:T(8,128)(2,1)S(1)} %get-tuple-element.75), channel_id=1, source_target_pairs={{0,2},{2,4},{4,6},{6,8},{8,10},{10,12},{12,14},{14,0},{1,3},{3,5},... | collective-permute-start | bytes 82952 | tf_op jit(solution)/shard_map/ppermute | solution.py:728
  38.3 1.7 %collective-permute-start.7 = (bf16[8,21,8,128]{3,2,1,0:T(8,128)(2,1)S(1)}, bf16[8,21,8,128]{3,2,1,0:T(8,128)(2,1)S(1)}, u32[]{:S(2)}, u32[]{:S(2)}) collective-permute-start(bf16[8,21,8,128]{3,2,1,0:T(8,128)(2,1)S(1)} %get-tuple-element.98), channel_id=1, source_target_pairs={{0,1},{1,0},{2,3},{3,2},{4,5},{5,4},{6,7},{7,6},{8,9},{9,8},{10,11... | collective-permute-start | bytes 1032200 | tf_op jit(solution)/shard_map/ppermute | solution.py:723
  38.4 9.2 %collective-permute-start.8 = (bf16[4,32,8,128]{3,2,1,0:T(8,128)(2,1)S(1)}, bf16[4,32,8,128]{3,2,1,0:T(8,128)(2,1)S(1)}, u32[]{:S(2)}, u32[]{:S(2)}) collective-permute-start(bf16[4,32,8,128]{3,2,1,0:T(8,128)(2,1)S(1)} %get-tuple-element.101), channel_id=1, source_target_pairs={{0,2},{2,0},{4,6},{6,4},{8,10},{10,8},{12,14},{14,12},{1,3},{3,1},... | collective-permute-start | bytes 786440 | tf_op jit(solution)/shard_map/ppermute | solution.py:733
  40.1 10.7 %collective-permute-start.9 = (bf16[4,21,8,128]{3,2,1,0:T(8,128)(2,1)S(1)}, bf16[4,21,8,128]{3,2,1,0:T(8,128)(2,1)S(1)}, u32[]{:S(2)}, u32[]{:S(2)}) collective-permute-start(bf16[4,21,8,128]{3,2,1,0:T(8,128)(2,1)S(1)} %get-tuple-element.102), channel_id=1, source_target_pairs={{0,2},{2,0},{4,6},{6,4},{8,10},{10,8},{12,14},{14,12},{1,3},{3,1},... | collective-permute-start | bytes 516104 | tf_op jit(solution)/shard_map/ppermute | solution.py:733
  46.4 8.4 %collective-permute-start.13 = (bf16[8,7,8,128]{3,2,1,0:T(8,128)(2,1)S(1)}, bf16[8,7,8,128]{3,2,1,0:T(8,128)(2,1)S(1)}, u32[]{:S(2)}, u32[]{:S(2)}) collective-permute-start(bf16[8,7,8,128]{3,2,1,0:T(8,128)(2,1)S(1)} %get-tuple-element.108), channel_id=1, source_target_pairs={{0,1},{1,0},{2,3},{3,2},{4,5},{5,4},{6,7},{7,6},{8,9},{9,8},{10,11... | collective-permute-start | bytes 344072 | tf_op jit(solution)/shard_map/ppermute | solution.py:723
  50.9 7.8 %collective-permute-start.10 = (bf16[53,8,128]{2,1,0:T(8,128)(2,1)S(1)}, bf16[53,8,128]{2,1,0:T(8,128)(2,1)S(1)}, u32[]{:S(2)}, u32[]{:S(2)}) collective-permute-start(bf16[53,8,128]{2,1,0:T(8,128)(2,1)S(1)} %get-tuple-element.104), channel_id=1, source_target_pairs={{0,4},{2,6},{4,8},{6,10},{8,12},{10,14},{12,0},{14,2},{1,5},{3,7},... | collective-permute-start | bytes 325640 | tf_op jit(solution)/shard_map/ppermute | solution.py:728
  51.0 11.2 %collective-permute-start.11 = (bf16[53,8,128]{2,1,0:T(8,128)(2,1)S(1)}, bf16[53,8,128]{2,1,0:T(8,128)(2,1)S(1)}, u32[]{:S(2)}, u32[]{:S(2)}) collective-permute-start(bf16[53,8,128]{2,1,0:T(8,128)(2,1)S(1)} %get-tuple-element.105), channel_id=1, source_target_pairs={{0,8},{2,10},{4,12},{6,14},{8,0},{10,2},{12,4},{14,6},{1,9},{3,11}... | collective-permute-start | bytes 325640 | tf_op jit(solution)/shard_map/ppermute | solution.py:728
  53.8 8.3 %collective-permute-start.12 = (bf16[53,8,128]{2,1,0:T(8,128)(2,1)S(1)}, bf16[53,8,128]{2,1,0:T(8,128)(2,1)S(1)}, u32[]{:S(2)}, u32[]{:S(2)}) collective-permute-start(bf16[53,8,128]{2,1,0:T(8,128)(2,1)S(1)} %get-tuple-element.106), channel_id=1, source_target_pairs={{0,12},{2,14},{4,0},{6,2},{8,4},{10,6},{12,8},{14,10},{1,13},{3,15... | collective-permute-start | bytes 325640 | tf_op jit(solution)/shard_map/ppermute | solution.py:728
  54.9 7.4 %collective-permute-start.17 = (bf16[4,12,8,128]{3,2,1,0:T(8,128)(2,1)S(1)}, bf16[4,12,8,128]{3,2,1,0:T(8,128)(2,1)S(1)}, u32[]{:S(2)}, u32[]{:S(2)}) collective-permute-start(bf16[4,12,8,128]{3,2,1,0:T(8,128)(2,1)S(1)} %get-tuple-element.111), channel_id=1, source_target_pairs={{0,2},{2,0},{4,6},{6,4},{8,10},{10,8},{12,14},{14,12},{1,3},{3,1},... | collective-permute-start | bytes 294920 | tf_op jit(solution)/shard_map/ppermute | solution.py:733
  62.9 13.3 %all-to-all-start = ((bf16[4,12,8,128]{3,2,1,0:T(8,128)(2,1)}), bf16[4,12,8,128]{3,2,1,0:T(8,128)(2,1)S(1)}, u32[]{:S(2)}, u32[]{:S(2)}) async-start(bf16[4,12,8,128]{3,2,1,0:T(8,128)(2,1)} %shard_map.123), calls=%async_computation | async-start | bytes 196608 | tf_op jit(solution)/shard_map/all_to_all | solution.py:964
  66.6 9.6 %collective-permute-start.14 = (bf16[53,8,128]{2,1,0:T(8,128)(2,1)S(1)}, bf16[53,8,128]{2,1,0:T(8,128)(2,1)S(1)}, u32[]{:S(2)}, u32[]{:S(2)}) collective-permute-start(bf16[53,8,128]{2,1,0:T(8,128)(2,1)S(1)} %shard_map.122.order.refs_0_), channel_id=1, source_target_pairs={{0,4},{2,6},{4,8},{6,10},{8,12},{10,14},{12,0},{14,2},{1,5},{3,7},... | collective-permute-start | bytes 325640 | tf_op jit(solution)/shard_map/ppermute | solution.py:728
  68.7 7.6 %collective-permute-start.16 = (bf16[53,8,128]{2,1,0:T(8,128)(2,1)S(1)}, bf16[53,8,128]{2,1,0:T(8,128)(2,1)S(1)}, u32[]{:S(2)}, u32[]{:S(2)}) collective-permute-start(bf16[53,8,128]{2,1,0:T(8,128)(2,1)S(1)} %shard_map.122.order.refs_0_), channel_id=1, source_target_pairs={{0,12},{2,14},{4,0},{6,2},{8,4},{10,6},{12,8},{14,10},{1,13},{3,15... | collective-permute-start | bytes 325640 | tf_op jit(solution)/shard_map/ppermute | solution.py:728
  70.5 11.4 %collective-permute-start.15 = (bf16[53,8,128]{2,1,0:T(8,128)(2,1)S(1)}, bf16[53,8,128]{2,1,0:T(8,128)(2,1)S(1)}, u32[]{:S(2)}, u32[]{:S(2)}) collective-permute-start(bf16[53,8,128]{2,1,0:T(8,128)(2,1)S(1)} %shard_map.122.order.refs_0_), channel_id=1, source_target_pairs={{0,8},{2,10},{4,12},{6,14},{8,0},{10,2},{12,4},{14,6},{1,9},{3,11}... | collective-permute-start | bytes 325640 | tf_op jit(solution)/shard_map/ppermute | solution.py:728
  82.0 11.6 %collective-permute-start.18 = (bf16[4,53,8,128]{3,2,1,0:T(8,128)(2,1)S(1)}, bf16[4,53,8,128]{3,2,1,0:T(8,128)(2,1)S(1)}, u32[]{:S(2)}, u32[]{:S(2)}) collective-permute-start(bf16[4,53,8,128]{3,2,1,0:T(8,128)(2,1)S(1)} %shard_map.125.same), channel_id=1, source_target_pairs={{0,2},{2,0},{4,6},{6,4},{8,10},{10,8},{12,14},{14,12},{1,3},{3,1},... | collective-permute-start | bytes 1302536 | tf_op jit(solution)/shard_map/ppermute | solution.py:733
  82.5 22.4 %collective-permute-start.19 = (bf16[4,53,8,128]{3,2,1,0:T(8,128)(2,1)S(1)}, bf16[4,53,8,128]{3,2,1,0:T(8,128)(2,1)S(1)}, u32[]{:S(2)}, u32[]{:S(2)}) collective-permute-start(bf16[4,53,8,128]{3,2,1,0:T(8,128)(2,1)S(1)} %shard_map.125.same), channel_id=1, source_target_pairs={{0,1},{1,0},{2,3},{3,2},{4,5},{5,4},{6,7},{7,6},{8,9},{9,8},{10,11... | collective-permute-start | bytes 1302536 | tf_op jit(solution)/shard_map/ppermute | solution.py:723
  93.6 11.3 %collective-permute-start.20 = (bf16[4,53,8,128]{3,2,1,0:T(8,128)(2,1)S(1)}, bf16[4,53,8,128]{3,2,1,0:T(8,128)(2,1)S(1)}, u32[]{:S(2)}, u32[]{:S(2)}) collective-permute-start(bf16[4,53,8,128]{3,2,1,0:T(8,128)(2,1)S(1)} %collective-permute-done.18.same_x), channel_id=1, source_target_pairs={{0,1},{1,0},{2,3},{3,2},{4,5},{5,4},{6,7},{7,6},{8,9},{9,8},{10,11... | collective-permute-start | bytes 1302536 | tf_op jit(solution)/shard_map/ppermute | solution.py:723
  104.9 1.4 %collective-permute-start.21 = (bf16[8,12,8,128]{3,2,1,0:T(8,128)(2,1)S(1)}, bf16[8,12,8,128]{3,2,1,0:T(8,128)(2,1)S(1)}, u32[]{:S(2)}, u32[]{:S(2)}) collective-permute-start(bf16[8,12,8,128]{3,2,1,0:T(8,128)(2,1)S(1)} %all_to_all.10.own_c), channel_id=1, source_target_pairs={{0,1},{1,0},{2,3},{3,2},{4,5},{5,4},{6,7},{7,6},{8,9},{9,8},{10,11... | collective-permute-start | bytes 589832 | tf_op jit(solution)/shard_map/ppermute | solution.py:723

commit v16 on v15

--- a/solution.py
+++ b/solution.py
@@ -518,12 +518,8 @@
     total = pieces[0].astype(F32)
     for k in range(1, pieces.shape[0]):
         total = total + pieces[k].astype(F32)
-    total = total.astype(BF16)
-    if len(out.shape) == len(pieces.shape):
-        for k in range(out.shape[0]):
-            out[k] = total
-    else:
-        out[...] = total
+    for k in range(out.shape[0]):
+        out[k] = total.astype(BF16)
 
 
 def join_z(*refs):
@@ -669,27 +665,33 @@
     bias_rows(a, units_a, spread, bias_out, rows_scr, wide_scr, tab_scr)
 
 
-def last_kernel(
-    units_c, spread, flat_ab, squares, bias_late, own_c, oth_c, update_out, bias_out,
-    scr, rows_scr, wide_scr, tab_scr, c,
+def near_kernel(
+    units_c, spread, own_c, oth_c, flat_out, squares_out, bias_out,
+    rows_scr, wide_scr, tab_scr, c,
 ):
     lat = lax.axis_index("lat")
     for j in range(own_c.shape[0]):
         c[lat, j] = own_c[j]
         c[1 - lat, j] = oth_c[j]
-    total = squares[...] + place(c, 0, units_c, [(0, 872)], scr)
+    squares_out[...] = place(c, 0, units_c, [(0, flat_out.shape[0])], flat_out)
+    bias_rows(c, units_c, spread, bias_out, rows_scr, wide_scr, tab_scr)
+
+
+def last_kernel(
+    flat_ab, squares_ab, bias_late, flat_c, squares_c, bias_near, update_out, bias_out
+):
     count = update_out.shape[0]
-    mean = jnp.sum(total) * (1.0 / (count * 128))
+    mean = jnp.sum(squares_ab[...] + squares_c[...]) * (1.0 / (count * 128))
     scale = lax.rsqrt(mean + 1e-06)
-    update_out[0:864, :] = (scr[0:864, :] * scale).astype(BF16)
+    update_out[0:864, :] = (flat_c[0:864, :] * scale).astype(BF16)
     at = 0
     for where, rows in (
         (864, 864), (2016, 288), (3456, 1152), (5760, 1152), (1728, 288), (2304, 1152), (4608, 1152)
     ):
         update_out[where : where + rows, :] = (flat_ab[at : at + rows, :] * scale).astype(BF16)
         at += rows
-    update_out[6912:count, :] = (scr[864 : 864 + count - 6912, :] * scale).astype(BF16)
-    bias_rows(c, units_c, spread, bias_out.at[0], rows_scr, wide_scr, tab_scr)
+    update_out[6912:count, :] = (flat_c[864 : 864 + count - 6912, :] * scale).astype(BF16)
+    bias_out[0] = bias_near[...]
     bias_out[1] = bias_late[...]
 
 
@@ -916,9 +918,9 @@
         [(token, F32), (token, F32), m192, m768, mdown, flat_scr(units_b)],
         (
             dhead, lon_tail, lat_dhead, diag_tail, resid0, slope0, active0, mixed0, proj_weight,
-            up_weight, down_turned, norm_gain, keep_xa,
+            up_weight, down_turned, norm_gain, got_xa,
         ),
-        3,
+        0.1,
         14,
     )
     got_b = lat_swap(give_b)
@@ -945,7 +947,7 @@
             stack_shape,
         ],
         (x0, qkv0, probs0, dmix0, rg0, gain_two, gains1, keep_xb, qkv_weight, norm_gain),
-        7,
+        2,
         14,
     )
     got_c = lat_swap(give_c)
@@ -970,19 +972,19 @@
     )
     moved_ab = [lon_send(sum_ab, 2 * k) for k in range(1, zs)]
     (sum_c,) = call(
-        sum_pieces, [units(lon_size, units_xc)], [], (pieces_c, moved_ab[0]), 1, 10
-    )
-    whole_c = lax.all_to_all(sum_c, "lon", 0, 0)
+        sum_pieces, [units(lon_size, units_xc)], [], (pieces_c, sum_ab), 1, 10
+    )
     (same,) = call(join_z, [units(zs, units_ab)], [], [sum_ab, *moved_ab, sum_c], 1, 10)
     same_x = x_swap(same)
     cross = lat_swap(same)
     cross_x = lat_swap(same_x)
+    whole_c = lax.all_to_all(sum_c, "lon", 0, 0)
     oth_c = lat_swap(whole_c)
 
     flat_rows = (2 * block_rows * 128 + norm_gain.size) // 128
     fold_scr = [((CHUNK * 8, PAIR), F32), wide_scr, tab_scr]
     ab_rows = 2 * block_rows - qkv_rows
-    flat_ab, squares, bias_late = call(
+    flat_ab, squares_ab, bias_late = call(
         functools.partial(late_kernel, units_a, extra),
         [((ab_rows, 128), F32), ((UNIT, 128), F32), (table.shape[1:], F32)],
         [*fold_scr, units(2, lon_size, units_ab)],
@@ -990,11 +992,19 @@
         2,
         14,
     )
+    flat_c, squares_c, bias_near = call(
+        functools.partial(near_kernel, units_c),
+        [((872, 128), F32), ((UNIT, 128), F32), (table.shape[1:], F32)],
+        [*fold_scr, units(2, lon_size, units_xc)],
+        (spread, whole_c, oth_c),
+        20,
+        14,
+    )
     update, bias_grad = call(
-        functools.partial(last_kernel, units_c),
+        last_kernel,
         [((flat_rows, 128), BF16), (table.shape, F32)],
-        [((872, 128), F32), *fold_scr, units(2, lon_size, units_xc)],
-        (spread, flat_ab, squares, bias_late, whole_c, oth_c),
+        [],
+        (flat_ab, squares_ab, bias_late, flat_c, squares_c, bias_near),
         2,
         14,
     )

time: 109 us -> 102 us (0.936)
  blocking collectives: 11.3 us -> 0 us
  starting transfers between devices: 21.3 us -> 28.8 us
  waiting for transfers between devices: 44 us -> 38.7 us
  Pallas kernels: 30.8 us -> 32.8 us
    all_to_all x1 -> x0, blocking collectives: 11.3 us -> none  [shards(): whole_c = lax.all_to_all(sum_c, 'lon', 0, 0)]
    ppermute x4, waiting for transfers between devices: 15.5 us -> 9.96 us  [x_swap(): return lax.ppermute(value, 'lon', [(s, s ^ 1) for s in range(count)])]
    all_to_all x0 -> x1, starting transfers between devices: none -> 3.39 us  [shards(): whole_c = lax.all_to_all(sum_c, 'lon', 0, 0)]
    ppermute x8, waiting for transfers between devices: 20.1 us -> 17.9 us  [lon_send(): lax.ppermute(value, 'lon', [(s, (s + step) % count) for s in range(count)])]
    pallas_call x16 -> x17, Pallas kernels: 30.8 us -> 32.8 us  [call(): pl.pallas_call(kernel, out_shape=[(pltpu.VMEM if at in near else jax.Shap...]
    ppermute x2, starting transfers between devices: 5.64 us -> 7.56 us  [diag_send(): return lax.ppermute(value, ('lon', 'lat'), pairs)]
    ppermute x8, starting transfers between devices: 9.36 us -> 11.1 us  [lon_send(): lax.ppermute(value, 'lon', [(s, (s + step) % count) for s in range(count)])]
    all_to_all x1, waiting for transfers between devices: 0.01 us -> 1.38 us  [shards(): lax.all_to_all(part_z, 'lon', 0, 0, axis_index_groups=[[2 * z + x for z i...]
  transfers between devices with their start and end apart: 23 -> 24, of which waited for: 14 -> 14; matrix products, arithmetic and copies ran while one was open for 0% -> 0% of each run, Pallas kernels for 8% -> 10%
where the time goes in v16:
time: 102 us; the launch traced here: 101 us
  waiting for transfers between devices  38.7 us (38%)
  Pallas kernels  32.8 us (32%)
  starting transfers between devices  28.8 us (28%)
    pallas_call x17, Pallas kernels, call(): pl.pallas_call(kernel, out_shape=[(pltpu.VMEM if at in near else jax.Shap...  32.8 us
    ppermute x8, waiting for transfers between devices, lon_send(): lax.ppermute(value, 'lon', [(s, (s + step) % count) for s in range(count)])  17.9 us
    ppermute x8, starting transfers between devices, lon_send(): lax.ppermute(value, 'lon', [(s, (s + step) % count) for s in range(count)])  11.1 us
    ppermute x4, waiting for transfers between devices, x_swap(): return lax.ppermute(value, 'lon', [(s, s ^ 1) for s in range(count)])  9.96 us
    ppermute x2, starting transfers between devices, diag_send(): return lax.ppermute(value, ('lon', 'lat'), pairs)  7.56 us
    ppermute x8, waiting for transfers between devices, lat_swap(): return lax.ppermute(value, 'lat', [(0, 1), (1, 0)])  4.64 us
    ppermute x2, waiting for transfers between devices, diag_send(): return lax.ppermute(value, ('lon', 'lat'), pairs)  4.57 us
    all_to_all x1, starting transfers between devices, shards(): lax.all_to_all(part_z, 'lon', 0, 0, axis_index_groups=[[2 * z + x for z i...  4.12 us
  transfers between devices with their start and end apart: 24, of which 14 were waited for; matrix products, arithmetic and copies ran while one was open for 0% of the time, Pallas kernels for 10%

profile of v16, /device:TPU:0, one launch (start us, length us, event | category | flops | bytes accessed | tf_op | source)
XLA Modules:
  0.0 101.2 jit_solution(12104647052099260759)
XLA Ops:
  0.7 6.6 %shard_map.112 = (bf16[576,192]{1,0:T(8,128)(2,1)S(1)}, bf16[2,504,192]{2,1,0:T(8,128)(2,1)S(1)}, bf16[2,72,192]{2,1,0:T(8,128)(2,1)S(1)}, bf16[576,576]{1,0:T(8...) custom-call(bf16[2,12,24,192]{3,2,1,0:T(8,128)(2,1)} %tokens_in.1, ...), custom_call_target="tpu_custom_call" | custom-call | flops 8800000000 | bytes 100000 | tf_op jit(solution)/shard_map/pallas_call | solution.py:700
  7.2 0.5 collective-permute-start.1
  7.7 5.6 %collective-permute-start.2 = (bf16[2,72,192]{2,1,0:T(8,128)(2,1)S(1)}, bf16[2,72,192]{2,1,0:T(8,128)(2,1)S(1)}, u32[]{:S(2)}, u32[]{:S(2)}) collective-permute-start(bf16[2,72,192]{2,1,0:T(8,128)(2,1)S(1)} %get-tuple-element.64), channel_id=1, source_target_pairs={{0,15},{1,14},{2,1},{3,0},{4,3},{5,2},{6,5},{7,4},{8,7},{9,6},{10,... | collective-permute-start | bytes 165896 | tf_op jit(solution)/shard_map/ppermute | solution.py:744
  13.4 0.5 collective-permute-start
  14.0 2.1 %shard_map.113 = (f32[864,144]{1,0:T(8,128)S(1)}, bf16[576,768]{1,0:T(8,128)(2,1)S(1)}) custom-call(f32[2,6,1,6336]{3,2,1,0:T(1,128)S(1)} %bitcast.8, bf16[2,132,384]{2,1,0:T(8,128)(2,1)S(1)} %copy-done.6, f32[576,768]{1,0:T(8,128)S(1)} %get-tuple-element.65.hidden), custom_call_target="tpu_custom_call" | custom-call | flops 3300000000 | bytes 100000 | tf_op jit(solution)/shard_map/pallas_call | solution.py:700
  16.0 1.7 %collective-permute-done.lon_head = bf16[2,72,192]{2,1,0:T(8,128)(2,1)S(1)} collective-permute-done((bf16[2,72,192]{2,1,0:T(8,128)(2,1)S(1)}, bf16[2,72,192]{2,1,0:T(8,128)(2,1)S(1)}, u32[]{:S(2)}, u32[]{:S(2)}) %collective-permute-start) | collective-permute-done | bytes 55328 | tf_op jit(solution)/shard_map/ppermute | solution.py:730
  17.8 8.9 %shard_map.114 = (bf16[504,192]{1,0:T(8,128)(2,1)S(1)}, bf16[72,192]{1,0:T(8,128)(2,1)S(1)}, bf16[576,192]{1,0:T(8,128)(2,1)S(1)}, bf16[576,576]{1,0:T(8,128)(2,...) custom-call(bf16[2,504,192]{2,1,0:T(8,128)(2,1)S(1)} %get-tuple-elem, ...), custom_call_target="tpu_custom_call", output_to_operand_aliasing={{12}: (10, {}), {13}: (11, {}), {14}: (12, {}), {15}: (13, ... | custom-call | flops 20899999744 | bytes 100000 | tf_op jit(solution)/shard_map/pallas_call | solution.py:700
  26.7 1.6 %shard_map.115 = (bf16[8,27,8,128]{3,2,1,0:T(8,128)(2,1)S(1)}, bf16[8,27,8,128]{3,2,1,0:T(8,128)(2,1)S(1)}, bf16[8,5,8,128]{3,2,1,0:T(8,128)(2,1)S(1)}) custom-call(bf16[576,192]{1,0:T(8,128)(2,1)S(1)} %get-tuple-element.83.n1, bf16[576,576]{1,0:T(8,128)(2,1)S(1)} %get-tuple-element.84.field, bf16[576,192]{1,0:T(8,128)(2,1)S(1)} %get-tuple-element.85.mixed, ...), custom_call_target="tpu_custom_call" | custom-call | flops 3300000000 | bytes 100000 | tf_op jit(solution)/shard_map/pallas_call | solution.py:700
  28.4 1.8 %collective-permute-done.6.got = bf16[8,27,8,128]{3,2,1,0:T(8,128)(2,1)S(1)} collective-permute-done((bf16[8,27,8,128]{3,2,1,0:T(8,128)(2,1)S(1)}, bf16[8,27,8,128]{3,2,1,0:T(8,128)(2,1)S(1)}, u32[]{:S(2)}, u32[]{:S(2)}) %collective-permute-start.6) | collective-permute-done | bytes 442400 | tf_op jit(solution)/shard_map/ppermute | solution.py:725
  30.2 0.1 shard_map.116
  30.3 0.1 collective-permute-start.7
  30.4 0.2 collective-permute-start.4
  30.6 1.9 %collective-permute-start.5 = (bf16[72,192]{1,0:T(8,128)(2,1)S(1)}, bf16[72,192]{1,0:T(8,128)(2,1)S(1)}, u32[]{:S(2)}, u32[]{:S(2)}) collective-permute-start(bf16[72,192]{1,0:T(8,128)(2,1)S(1)} %get-tuple-element.78), channel_id=1, source_target_pairs={{0,3},{1,2},{2,5},{3,4},{4,7},{5,6},{6,9},{7,8},{8,11},{9,10},{10,... | collective-permute-start | bytes 82952 | tf_op jit(solution)/shard_map/ppermute | solution.py:744
  32.5 0.6 collective-permute-start.3
  33.1 4.6 %collective-permute-done.5.diag_tail = bf16[72,192]{1,0:T(8,128)(2,1)S(1)} collective-permute-done((bf16[72,192]{1,0:T(8,128)(2,1)S(1)}, bf16[72,192]{1,0:T(8,128)(2,1)S(1)}, u32[]{:S(2)}, u32[]{:S(2)}) %collective-permute-start.5) | collective-permute-done | bytes 27680 | tf_op jit(solution)/shard_map/ppermute | solution.py:744
  37.7 1.6 %collective-permute-done.3.lon_tail = bf16[72,192]{1,0:T(8,128)(2,1)S(1)} collective-permute-done((bf16[72,192]{1,0:T(8,128)(2,1)S(1)}, bf16[72,192]{1,0:T(8,128)(2,1)S(1)}, u32[]{:S(2)}, u32[]{:S(2)}) %collective-permute-start.3) | collective-permute-done | bytes 27680 | tf_op jit(solution)/shard_map/ppermute | solution.py:730
  39.3 1.0 %collective-permute-done.7.order.got_first = bf16[4,32,8,128]{3,2,1,0:T(8,128)(2,1)S(1)} collective-permute-done((bf16[4,32,8,128]{3,2,1,0:T(8,128)(2,1)S(1)}, bf16[4,32,8,128]{3,2,1,0:T(8,128)(2,1)S(1)}, u32[]{:S(2)}, u32[]{:S(2)}) %collective-permute-start.7) | collective-permute-done | bytes 262176 | tf_op jit(solution)/shard_map/ppermute | solution.py:735
  40.3 2.2 %shard_map.117 = (bf16[8,21,8,128]{3,2,1,0:T(8,128)(2,1)S(1)}, bf16[8,21,8,128]{3,2,1,0:T(8,128)(2,1)S(1)}, f32[576,192]{1,0:T(8,128)S(1)}, bf16[576,192]{1,0:T(8,128)(2,1)S(1)}, f32[1,192]{1,0:T(1,128)S(1)}) custom-call(bf16[504,192]{1,0:T(8,128)(2,1)S(1)} %get-tuple-element.77.head, bf16[72,192]{1,0:T(8,128)(2,1)S(1)} %collective-permute-done.3.lon_tail, ...), custom_call_target="tpu_custom_call" | custom-call | flops 110000000 | bytes 100000 | tf_op jit(solution)/shard_map/pallas_call | solution.py:700
  42.5 0.1 collective-permute-start.8
  42.6 1.6 %collective-permute-done.8.got = bf16[8,21,8,128]{3,2,1,0:T(8,128)(2,1)S(1)} collective-permute-done((bf16[8,21,8,128]{3,2,1,0:T(8,128)(2,1)S(1)}, bf16[8,21,8,128]{3,2,1,0:T(8,128)(2,1)S(1)}, u32[]{:S(2)}, u32[]{:S(2)}) %collective-permute-start.8) | collective-permute-done | bytes 344096 | tf_op jit(solution)/shard_map/ppermute | solution.py:725
  44.2 0.1 shard_map.118
  44.3 0.4 collective-permute-start.9
  44.6 5.7 %shard_map.119 = (bf16[2,12,24,192]{3,2,1,0:T(8,128)(2,1)}, bf16[8,7,8,128]{3,2,1,0:T(8,128)(2,1)S(1)}, bf16[8,7,8,128]{3,2,1,0:T(8,128)(2,1)S(1)}, bf16[8,5,8,128]{3,2,1,0:T(8,128)(2,1)S(1)}) custom-call(bf16[576,192]{1,0:T(8,128)(2,1)S(1)} %get-tuple-element.74.x_in, bf16[576,576]{1,0:T(8,128)(2,1)S(1)} %get-tuple-element.75.qkv, ...), custom_call_target="tpu_custom_call" | custom-call | flops 2200000000 | bytes 100000 | tf_op jit(solution)/shard_map/pallas_call | solution.py:700
  50.4 0.4 collective-permute-done.9.got_second
  50.8 0.1 shard_map.120
  50.9 0.6 collective-permute-start.10
  51.4 4.4 %collective-permute-start.11 = (bf16[53,8,128]{2,1,0:T(8,128)(2,1)S(1)}, bf16[53,8,128]{2,1,0:T(8,128)(2,1)S(1)}, u32[]{:S(2)}, u32[]{:S(2)}) collective-permute-start(bf16[53,8,128]{2,1,0:T(8,128)(2,1)S(1)} %get-tuple-element.108), channel_id=1, source_target_pairs={{0,8},{2,10},{4,12},{6,14},{8,0},{10,2},{12,4},{14,6},{1,9},{3,11}... | collective-permute-start | bytes 325640 | tf_op jit(solution)/shard_map/ppermute | solution.py:730
  55.9 0.7 collective-permute-start.17
  56.6 2.6 %collective-permute-done.10.refs_1_ = bf16[53,8,128]{2,1,0:T(8,128)(2,1)S(1)} collective-permute-done((bf16[53,8,128]{2,1,0:T(8,128)(2,1)S(1)}, bf16[53,8,128]{2,1,0:T(8,128)(2,1)S(1)}, u32[]{:S(2)}, u32[]{:S(2)}) %collective-permute-start.10) | collective-permute-done | bytes 108576 | tf_op jit(solution)/shard_map/ppermute | solution.py:730
  59.2 4.4 %collective-permute-done.11.refs_2_ = bf16[53,8,128]{2,1,0:T(8,128)(2,1)S(1)} collective-permute-done((bf16[53,8,128]{2,1,0:T(8,128)(2,1)S(1)}, bf16[53,8,128]{2,1,0:T(8,128)(2,1)S(1)}, u32[]{:S(2)}, u32[]{:S(2)}) %collective-permute-start.11) | collective-permute-done | bytes 108576 | tf_op jit(solution)/shard_map/ppermute | solution.py:730
  63.7 0.1 shard_map.122.order.refs_0_
  63.7 0.7 shard_map.123
  64.4 4.1 %all-to-all-start = ((bf16[4,12,8,128]{3,2,1,0:T(8,128)(2,1)}), bf16[4,12,8,128]{3,2,1,0:T(8,128)(2,1)S(1)}, u32[]{:S(2)}, u32[]{:S(2)}) async-start(bf16[4,12,8,128]{3,2,1,0:T(8,128)(2,1)} %shard_map.123), calls=%async_computation | async-start | bytes 196608 | tf_op jit(solution)/shard_map/all_to_all | solution.py:966
  68.5 3.8 %collective-permute-start.16 = (bf16[53,8,128]{2,1,0:T(8,128)(2,1)S(1)}, bf16[53,8,128]{2,1,0:T(8,128)(2,1)S(1)}, u32[]{:S(2)}, u32[]{:S(2)}) collective-permute-start(bf16[53,8,128]{2,1,0:T(8,128)(2,1)S(1)} %shard_map.122.order.refs_0_), channel_id=1, source_target_pairs={{0,12},{2,14},{4,0},{6,2},{8,4},{10,6},{12,8},{14,10},{1,13},{3,15... | collective-permute-start | bytes 325640 | tf_op jit(solution)/shard_map/ppermute | solution.py:730
  72.3 1.1 %collective-permute-start.14 = (bf16[53,8,128]{2,1,0:T(8,128)(2,1)S(1)}, bf16[53,8,128]{2,1,0:T(8,128)(2,1)S(1)}, u32[]{:S(2)}, u32[]{:S(2)}) collective-permute-start(bf16[53,8,128]{2,1,0:T(8,128)(2,1)S(1)} %shard_map.122.order.refs_0_), channel_id=1, source_target_pairs={{0,4},{2,6},{4,8},{6,10},{8,12},{10,14},{12,0},{14,2},{1,5},{3,7},... | collective-permute-start | bytes 325640 | tf_op jit(solution)/shard_map/ppermute | solution.py:730
  73.5 1.4 %all-to-all-done.pieces = bf16[4,12,8,128]{3,2,1,0:T(8,128)(2,1)S(1)} async-done(((bf16[4,12,8,128]{3,2,1,0:T(8,128)(2,1)}), bf16[4,12,8,128]{3,2,1,0:T(8,128)(2,1)S(1)}, u32[]{:S(2)}, u32[]{:S(2)}) %all-to-all-start) | async-done | bytes 98336 | tf_op jit(solution)/shard_map/all_to_all | solution.py:966
  74.9 0.7 shard_map.124.refs_4_
  75.5 3.4 %all-to-all-start.1 = ((bf16[8,12,8,128]{3,2,1,0:T(8,128)(2,1)}), bf16[8,12,8,128]{3,2,1,0:T(8,128)(2,1)S(1)}, u32[]{:S(2)}, u32[]{:S(2)}) async-start(bf16[8,12,8,128]{3,2,1,0:T(8,128)(2,1)} %shard_map.124.refs_4_), calls=%async_computation.1 | async-start | bytes 393216 | tf_op jit(solution)/shard_map/all_to_all | solution.py:981
  79.0 7.6 %collective-permute-done.15.refs_2_ = bf16[53,8,128]{2,1,0:T(8,128)(2,1)S(1)} collective-permute-done((bf16[53,8,128]{2,1,0:T(8,128)(2,1)S(1)}, bf16[53,8,128]{2,1,0:T(8,128)(2,1)S(1)}, u32[]{:S(2)}, u32[]{:S(2)}) %collective-permute-start.15) | collective-permute-done | bytes 108576 | tf_op jit(solution)/shard_map/ppermute | solution.py:730
  86.6 1.0 shard_map.125.same
  87.5 0.1 collective-permute-start.18
  87.6 0.2 all-to-all-done.1.own_c
  87.8 0.5 collective-permute-start.19
  88.4 8.6 %collective-permute-done.18.same_x = bf16[4,53,8,128]{3,2,1,0:T(8,128)(2,1)S(1)} collective-permute-done((bf16[4,53,8,128]{3,2,1,0:T(8,128)(2,1)S(1)}, bf16[4,53,8,128]{3,2,1,0:T(8,128)(2,1)S(1)}, u32[]{:S(2)}, u32[]{:S(2)}) %collective-permute-start.18) | collective-permute-done | bytes 434208 | tf_op jit(solution)/shard_map/ppermute | solution.py:735
  96.9 0.5 shard_map.127
  97.5 1.2 %collective-permute-done.20.cross_x = bf16[4,53,8,128]{3,2,1,0:T(8,128)(2,1)S(1)} collective-permute-done((bf16[4,53,8,128]{3,2,1,0:T(8,128)(2,1)S(1)}, bf16[4,53,8,128]{3,2,1,0:T(8,128)(2,1)S(1)}, u32[]{:S(2)}, u32[]{:S(2)}) %collective-permute-start.20) | collective-permute-done | bytes 434208 | tf_op jit(solution)/shard_map/ppermute | solution.py:725
  98.7 0.7 shard_map.126
  99.4 1.8 %shard_map.128 = (bf16[6918,128]{1,0:T(8,128)(2,1)}, f32[2,6,1,6336]{3,2,1,0:T(1,128)}) custom-call(f32[6048,128]{1,0:T(8,128)S(1)} %get-tuple-element.115.flat_ab, f32[8,128]{1,0:T(8,128)S(1)} %get-tuple-element.116.squares_ab, f32[6,1,6336]{2,1,0:T(1,128)S(1)} %get-tuple-element.117.bias_late, f32[872,128]{1,0:T(8,128)S(1)} %get-tuple-element.118.flat_c, ...), custom_call_target="tpu_custom_call" | custom-call | flops 2200000000 | bytes 100000 | tf_op jit(solution)/shard_map/pallas_call | solution.py:700
  (31 shorter events, 0.2 us)
Async XLA Ops:
  0.6 13.3 %copy-start.5 = (f32[2,1,6,6336]{3,1,2,0:T(1,128)S(1)}, f32[2,1,6,6336]{3,1,2,0:T(1,128)}, u32[]{:S(2)}) copy-start(f32[2,1,6,6336]{3,1,2,0:T(1,128)} %param.16) | copy-start | bytes 912388
  0.6 13.3 %copy-start.6 = (bf16[2,132,384]{2,1,0:T(8,128)(2,1)S(1)}, bf16[2,132,384]{2,1,0:T(8,128)(2,1)}, u32[]{:S(2)}) copy-start(bf16[2,132,384]{2,1,0:T(8,128)(2,1)} %constant.2.clone.spread_in.spread) | copy-start | bytes 608260
  7.2 10.5 %collective-permute-start.1 = (bf16[2,504,192]{2,1,0:T(8,128)(2,1)S(1)}, bf16[2,504,192]{2,1,0:T(8,128)(2,1)S(1)}, u32[]{:S(2)}, u32[]{:S(2)}) collective-permute-start(bf16[2,504,192]{2,1,0:T(8,128)(2,1)S(1)} %get-tuple-element.63.tail), channel_id=1, source_target_pairs={{0,1},{1,0},{2,3},{3,2},{4,5},{5,4},{6,7},{7,6},{8,9},{9,8},{10,11... | collective-permute-start | bytes 1161224 | tf_op jit(solution)/shard_map/ppermute | solution.py:725
  7.7 8.3 %collective-permute-start.2 = (bf16[2,72,192]{2,1,0:T(8,128)(2,1)S(1)}, bf16[2,72,192]{2,1,0:T(8,128)(2,1)S(1)}, u32[]{:S(2)}, u32[]{:S(2)}) collective-permute-start(bf16[2,72,192]{2,1,0:T(8,128)(2,1)S(1)} %get-tuple-element.64), channel_id=1, source_target_pairs={{0,15},{1,14},{2,1},{3,0},{4,3},{5,2},{6,5},{7,4},{8,7},{9,6},{10,... | collective-permute-start | bytes 165896 | tf_op jit(solution)/shard_map/ppermute | solution.py:744
  13.4 4.4 %collective-permute-start = (bf16[2,72,192]{2,1,0:T(8,128)(2,1)S(1)}, bf16[2,72,192]{2,1,0:T(8,128)(2,1)S(1)}, u32[]{:S(2)}, u32[]{:S(2)}) collective-permute-start(bf16[2,72,192]{2,1,0:T(8,128)(2,1)S(1)} %get-tuple-element.64), channel_id=1, source_target_pairs={{0,14},{2,0},{4,2},{6,4},{8,6},{10,8},{12,10},{14,12},{1,15},{3,1}... | collective-permute-start | bytes 165896 | tf_op jit(solution)/shard_map/ppermute | solution.py:730
  13.9 3.8 %copy-start = (bf16[2,192,768]{2,1,0:T(8,128)(2,1)S(1)}, bf16[2,192,768]{2,1,0:T(8,128)(2,1)}, u32[]{:S(2)}) copy-start(bf16[2,192,768]{2,1,0:T(8,128)(2,1)} %up_w.3) | copy-start | bytes 1769476
  13.9 3.8 %copy-start.1 = (bf16[2,768,192]{1,2,0:T(8,128)(2,1)S(1)}, bf16[2,768,192]{1,2,0:T(8,128)(2,1)}, u32[]{:S(2)}) copy-start(bf16[2,768,192]{1,2,0:T(8,128)(2,1)} %param.14) | copy-start | bytes 1769476
  13.9 3.8 %copy-start.2 = (bf16[2,192,192]{2,1,0:T(8,128)(2,1)S(1)}, bf16[2,192,192]{2,1,0:T(8,128)(2,1)}, u32[]{:S(2)}) copy-start(bf16[2,192,192]{2,1,0:T(8,128)(2,1)} %proj_w.3) | copy-start | bytes 442372
  13.9 3.8 %copy-start.3 = (f32[2,2,192]{2,1,0:T(2,128)S(1)}, f32[2,2,192]{2,1,0:T(2,128)}, u32[]{:S(2)}) copy-start(f32[2,2,192]{2,1,0:T(2,128)} %gains.5) | copy-start | bytes 9220
  14.0 3.8 %copy-start.4 = (bf16[2,192,576]{2,1,0:T(8,128)(2,1)S(1)}, bf16[2,192,576]{2,1,0:T(8,128)(2,1)}, u32[]{:S(2)}) copy-start(bf16[2,192,576]{2,1,0:T(8,128)(2,1)} %qkv_w.3) | copy-start | bytes 1327108
  28.3 1.8 %collective-permute-start.6 = (bf16[8,27,8,128]{3,2,1,0:T(8,128)(2,1)S(1)}, bf16[8,27,8,128]{3,2,1,0:T(8,128)(2,1)S(1)}, u32[]{:S(2)}, u32[]{:S(2)}) collective-permute-start(bf16[8,27,8,128]{3,2,1,0:T(8,128)(2,1)S(1)} %get-tuple-element.93), channel_id=1, source_target_pairs={{0,1},{1,0},{2,3},{3,2},{4,5},{5,4},{6,7},{7,6},{8,9},{9,8},{10,11... | collective-permute-start | bytes 1327112 | tf_op jit(solution)/shard_map/ppermute | solution.py:725
  30.3 10.0 %collective-permute-start.7 = (bf16[4,32,8,128]{3,2,1,0:T(8,128)(2,1)S(1)}, bf16[4,32,8,128]{3,2,1,0:T(8,128)(2,1)S(1)}, u32[]{:S(2)}, u32[]{:S(2)}) collective-permute-start(bf16[4,32,8,128]{3,2,1,0:T(8,128)(2,1)S(1)} %get-tuple-element.95), channel_id=1, source_target_pairs={{0,2},{2,0},{4,6},{6,4},{8,10},{10,8},{12,14},{14,12},{1,3},{3,1},... | collective-permute-start | bytes 786440 | tf_op jit(solution)/shard_map/ppermute | solution.py:735
  30.4 8.9 %collective-permute-start.4 = (bf16[504,192]{1,0:T(8,128)(2,1)S(1)}, bf16[504,192]{1,0:T(8,128)(2,1)S(1)}, u32[]{:S(2)}, u32[]{:S(2)}) collective-permute-start(bf16[504,192]{1,0:T(8,128)(2,1)S(1)} %get-tuple-element.77.head), channel_id=1, source_target_pairs={{0,1},{1,0},{2,3},{3,2},{4,5},{5,4},{6,7},{7,6},{8,9},{9,8},{10,11... | collective-permute-start | bytes 580616 | tf_op jit(solution)/shard_map/ppermute | solution.py:725
  30.6 7.1 %collective-permute-start.5 = (bf16[72,192]{1,0:T(8,128)(2,1)S(1)}, bf16[72,192]{1,0:T(8,128)(2,1)S(1)}, u32[]{:S(2)}, u32[]{:S(2)}) collective-permute-start(bf16[72,192]{1,0:T(8,128)(2,1)S(1)} %get-tuple-element.78), channel_id=1, source_target_pairs={{0,3},{1,2},{2,5},{3,4},{4,7},{5,6},{6,9},{7,8},{8,11},{9,10},{10,... | collective-permute-start | bytes 82952 | tf_op jit(solution)/shard_map/ppermute | solution.py:744
  32.5 6.8 %collective-permute-start.3 = (bf16[72,192]{1,0:T(8,128)(2,1)S(1)}, bf16[72,192]{1,0:T(8,128)(2,1)S(1)}, u32[]{:S(2)}, u32[]{:S(2)}) collective-permute-start(bf16[72,192]{1,0:T(8,128)(2,1)S(1)} %get-tuple-element.78), channel_id=1, source_target_pairs={{0,2},{2,4},{4,6},{6,8},{8,10},{10,12},{12,14},{14,0},{1,3},{3,5},... | collective-permute-start | bytes 82952 | tf_op jit(solution)/shard_map/ppermute | solution.py:730
  42.5 1.7 %collective-permute-start.8 = (bf16[8,21,8,128]{3,2,1,0:T(8,128)(2,1)S(1)}, bf16[8,21,8,128]{3,2,1,0:T(8,128)(2,1)S(1)}, u32[]{:S(2)}, u32[]{:S(2)}) collective-permute-start(bf16[8,21,8,128]{3,2,1,0:T(8,128)(2,1)S(1)} %get-tuple-element.101), channel_id=1, source_target_pairs={{0,1},{1,0},{2,3},{3,2},{4,5},{5,4},{6,7},{7,6},{8,9},{9,8},{10,11... | collective-permute-start | bytes 1032200 | tf_op jit(solution)/shard_map/ppermute | solution.py:725
  44.3 6.5 %collective-permute-start.9 = (bf16[4,21,8,128]{3,2,1,0:T(8,128)(2,1)S(1)}, bf16[4,21,8,128]{3,2,1,0:T(8,128)(2,1)S(1)}, u32[]{:S(2)}, u32[]{:S(2)}) collective-permute-start(bf16[4,21,8,128]{3,2,1,0:T(8,128)(2,1)S(1)} %get-tuple-element.105), channel_id=1, source_target_pairs={{0,2},{2,0},{4,6},{6,4},{8,10},{10,8},{12,14},{14,12},{1,3},{3,1},... | collective-permute-start | bytes 516104 | tf_op jit(solution)/shard_map/ppermute | solution.py:735
  50.4 5.5 %collective-permute-start.13 = (bf16[8,7,8,128]{3,2,1,0:T(8,128)(2,1)S(1)}, bf16[8,7,8,128]{3,2,1,0:T(8,128)(2,1)S(1)}, u32[]{:S(2)}, u32[]{:S(2)}) collective-permute-start(bf16[8,7,8,128]{3,2,1,0:T(8,128)(2,1)S(1)} %get-tuple-element.111), channel_id=1, source_target_pairs={{0,1},{1,0},{2,3},{3,2},{4,5},{5,4},{6,7},{7,6},{8,9},{9,8},{10,11... | collective-permute-start | bytes 344072 | tf_op jit(solution)/shard_map/ppermute | solution.py:725
  50.9 8.4 %collective-permute-start.10 = (bf16[53,8,128]{2,1,0:T(8,128)(2,1)S(1)}, bf16[53,8,128]{2,1,0:T(8,128)(2,1)S(1)}, u32[]{:S(2)}, u32[]{:S(2)}) collective-permute-start(bf16[53,8,128]{2,1,0:T(8,128)(2,1)S(1)} %get-tuple-element.107), channel_id=1, source_target_pairs={{0,4},{2,6},{4,8},{6,10},{8,12},{10,14},{12,0},{14,2},{1,5},{3,7},... | collective-permute-start | bytes 325640 | tf_op jit(solution)/shard_map/ppermute | solution.py:730
  51.4 12.2 %collective-permute-start.11 = (bf16[53,8,128]{2,1,0:T(8,128)(2,1)S(1)}, bf16[53,8,128]{2,1,0:T(8,128)(2,1)S(1)}, u32[]{:S(2)}, u32[]{:S(2)}) collective-permute-start(bf16[53,8,128]{2,1,0:T(8,128)(2,1)S(1)} %get-tuple-element.108), channel_id=1, source_target_pairs={{0,8},{2,10},{4,12},{6,14},{8,0},{10,2},{12,4},{14,6},{1,9},{3,11}... | collective-permute-start | bytes 325640 | tf_op jit(solution)/shard_map/ppermute | solution.py:730
  55.8 7.8 %collective-permute-start.12 = (bf16[53,8,128]{2,1,0:T(8,128)(2,1)S(1)}, bf16[53,8,128]{2,1,0:T(8,128)(2,1)S(1)}, u32[]{:S(2)}, u32[]{:S(2)}) collective-permute-start(bf16[53,8,128]{2,1,0:T(8,128)(2,1)S(1)} %get-tuple-element.109), channel_id=1, source_target_pairs={{0,12},{2,14},{4,0},{6,2},{8,4},{10,6},{12,8},{14,10},{1,13},{3,15... | collective-permute-start | bytes 325640 | tf_op jit(solution)/shard_map/ppermute | solution.py:730
  55.9 7.8 %collective-permute-start.17 = (bf16[4,12,8,128]{3,2,1,0:T(8,128)(2,1)S(1)}, bf16[4,12,8,128]{3,2,1,0:T(8,128)(2,1)S(1)}, u32[]{:S(2)}, u32[]{:S(2)}) collective-permute-start(bf16[4,12,8,128]{3,2,1,0:T(8,128)(2,1)S(1)} %get-tuple-element.114), channel_id=1, source_target_pairs={{0,2},{2,0},{4,6},{6,4},{8,10},{10,8},{12,14},{14,12},{1,3},{3,1},... | collective-permute-start | bytes 294920 | tf_op jit(solution)/shard_map/ppermute | solution.py:735
  64.4 10.5 %all-to-all-start = ((bf16[4,12,8,128]{3,2,1,0:T(8,128)(2,1)}), bf16[4,12,8,128]{3,2,1,0:T(8,128)(2,1)S(1)}, u32[]{:S(2)}, u32[]{:S(2)}) async-start(bf16[4,12,8,128]{3,2,1,0:T(8,128)(2,1)} %shard_map.123), calls=%async_computation | async-start | bytes 196608 | tf_op jit(solution)/shard_map/all_to_all | solution.py:966
  68.5 10.4 %collective-permute-start.16 = (bf16[53,8,128]{2,1,0:T(8,128)(2,1)S(1)}, bf16[53,8,128]{2,1,0:T(8,128)(2,1)S(1)}, u32[]{:S(2)}, u32[]{:S(2)}) collective-permute-start(bf16[53,8,128]{2,1,0:T(8,128)(2,1)S(1)} %shard_map.122.order.refs_0_), channel_id=1, source_target_pairs={{0,12},{2,14},{4,0},{6,2},{8,4},{10,6},{12,8},{14,10},{1,13},{3,15... | collective-permute-start | bytes 325640 | tf_op jit(solution)/shard_map/ppermute | solution.py:730
  72.3 14.2 %collective-permute-start.15 = (bf16[53,8,128]{2,1,0:T(8,128)(2,1)S(1)}, bf16[53,8,128]{2,1,0:T(8,128)(2,1)S(1)}, u32[]{:S(2)}, u32[]{:S(2)}) collective-permute-start(bf16[53,8,128]{2,1,0:T(8,128)(2,1)S(1)} %shard_map.122.order.refs_0_), channel_id=1, source_target_pairs={{0,8},{2,10},{4,12},{6,14},{8,0},{10,2},{12,4},{14,6},{1,9},{3,11}... | collective-permute-start | bytes 325640 | tf_op jit(solution)/shard_map/ppermute | solution.py:730
  72.3 14.2 %collective-permute-start.14 = (bf16[53,8,128]{2,1,0:T(8,128)(2,1)S(1)}, bf16[53,8,128]{2,1,0:T(8,128)(2,1)S(1)}, u32[]{:S(2)}, u32[]{:S(2)}) collective-permute-start(bf16[53,8,128]{2,1,0:T(8,128)(2,1)S(1)} %shard_map.122.order.refs_0_), channel_id=1, source_target_pairs={{0,4},{2,6},{4,8},{6,10},{8,12},{10,14},{12,0},{14,2},{1,5},{3,7},... | collective-permute-start | bytes 325640 | tf_op jit(solution)/shard_map/ppermute | solution.py:730
  75.5 12.3 %all-to-all-start.1 = ((bf16[8,12,8,128]{3,2,1,0:T(8,128)(2,1)}), bf16[8,12,8,128]{3,2,1,0:T(8,128)(2,1)S(1)}, u32[]{:S(2)}, u32[]{:S(2)}) async-start(bf16[8,12,8,128]{3,2,1,0:T(8,128)(2,1)} %shard_map.124.refs_4_), calls=%async_computation.1 | async-start | bytes 393216 | tf_op jit(solution)/shard_map/all_to_all | solution.py:981
  87.5 9.4 %collective-permute-start.18 = (bf16[4,53,8,128]{3,2,1,0:T(8,128)(2,1)S(1)}, bf16[4,53,8,128]{3,2,1,0:T(8,128)(2,1)S(1)}, u32[]{:S(2)}, u32[]{:S(2)}) collective-permute-start(bf16[4,53,8,128]{3,2,1,0:T(8,128)(2,1)S(1)} %shard_map.125.same), channel_id=1, source_target_pairs={{0,2},{2,0},{4,6},{6,4},{8,10},{10,8},{12,14},{14,12},{1,3},{3,1},... | collective-permute-start | bytes 1302536 | tf_op jit(solution)/shard_map/ppermute | solution.py:735
  87.8 9.1 %collective-permute-start.21 = (bf16[8,12,8,128]{3,2,1,0:T(8,128)(2,1)S(1)}, bf16[8,12,8,128]{3,2,1,0:T(8,128)(2,1)S(1)}, u32[]{:S(2)}, u32[]{:S(2)}) collective-permute-start(bf16[8,12,8,128]{3,2,1,0:T(8,128)(2,1)S(1)} %all-to-all-done.1.own_c), channel_id=1, source_target_pairs={{0,1},{1,0},{2,3},{3,2},{4,5},{5,4},{6,7},{7,6},{8,9},{9,8},{10,11... | collective-permute-start | bytes 589832 | tf_op jit(solution)/shard_map/ppermute | solution.py:725
  87.8 9.6 %collective-permute-start.19 = (bf16[4,53,8,128]{3,2,1,0:T(8,128)(2,1)S(1)}, bf16[4,53,8,128]{3,2,1,0:T(8,128)(2,1)S(1)}, u32[]{:S(2)}, u32[]{:S(2)}) collective-permute-start(bf16[4,53,8,128]{3,2,1,0:T(8,128)(2,1)S(1)} %shard_map.125.same), channel_id=1, source_target_pairs={{0,1},{1,0},{2,3},{3,2},{4,5},{5,4},{6,7},{7,6},{8,9},{9,8},{10,11... | collective-permute-start | bytes 1302536 | tf_op jit(solution)/shard_map/ppermute | solution.py:725
  96.9 1.8 %collective-permute-start.20 = (bf16[4,53,8,128]{3,2,1,0:T(8,128)(2,1)S(1)}, bf16[4,53,8,128]{3,2,1,0:T(8,128)(2,1)S(1)}, u32[]{:S(2)}, u32[]{:S(2)}) collective-permute-start(bf16[4,53,8,128]{3,2,1,0:T(8,128)(2,1)S(1)} %collective-permute-done.18.same_x), channel_id=1, source_target_pairs={{0,1},{1,0},{2,3},{3,2},{4,5},{5,4},{6,7},{7,6},{8,9},{9,8},{10,11... | collective-permute-start | bytes 1302536 | tf_op jit(solution)/shard_map/ppermute | solution.py:725

commit v17 on v14

--- a/solution.py
+++ b/solution.py
@@ -175,16 +175,17 @@
     return jnp.concatenate([v * mask for mask in masks], axis=0)
 
 
-def pick_heads(v, masks):
-    total = v[0:WIN] * masks[0]
-    for h in range(1, HEADS):
-        total = total + v[h * WIN : (h + 1) * WIN] * masks[h]
+def pick_heads(v, width):
+    lane = lax.broadcasted_iota(jnp.int32, (1, width), 1)
+    size = width // HEADS
+    total = v[(HEADS - 1) * WIN :]
+    for h in range(HEADS - 1, 0, -1):
+        total = jnp.where(lane < h * size, v[(h - 1) * WIN : h * WIN], total)
     return total
 
 
 def attend(qkv, bias, mixed, probs, stack_scr, width):
     masks = head_masks(width, BF16)
-    masks32 = head_masks(width, F32)
     scale = (width // HEADS) ** -0.5
 
     def window(w, carry):
@@ -200,7 +201,7 @@
             p = weights * (1.0 / jnp.sum(weights, axis=-1, keepdims=True))
             probs[w, h] = p
             stack_scr[part, :] = p.astype(BF16)
-        mixed[rows, :] = pick_heads(dot(stack_scr[...], v), masks32).astype(BF16)
+        mixed[rows, :] = pick_heads(dot(stack_scr[...], v), width).astype(BF16)
         return carry
 
     lax.fori_loop(0, probs.shape[0], window, 0, unroll=True)
@@ -208,7 +209,6 @@
 
 def attend_back(qkv, probs, dmix, field, sums, low_scr, prob_scr, width):
     masks = head_masks(width, BF16)
-    masks32 = head_masks(width, F32)
     scale = (width // HEADS) ** -0.5
 
     def window(w, carry):
@@ -227,7 +227,7 @@
             low_scr[part, :] = ds.astype(BF16)
             prob_scr[part, :] = p.astype(BF16)
         low = low_scr[...]
-        dq = pick_heads(dot(low, k), masks32)
+        dq = pick_heads(dot(low, k), width)
         dk = dot_tn(low, stack_heads(q, masks))
         dv = dot_tn(prob_scr[...], up)
         field[rows, 0:width] = (dq * scale).astype(BF16)
@@ -894,14 +894,14 @@
         [units(lon_size, units_a), units(lon_size, units_a), units(lon_size, extra)],
         [m576, m192, m768, mdown, flat_scr(units_a)],
         (n1, field1, mixed1, low1, n2, hg1, active1, g1, sums1),
-        3,
+        0.01,
         14,
     )
     got_a = lat_swap(give_a)
 
     units_xa = units_a + extra
     keep_xa, give_xa = call(
-        lat_sums_split, [units(zs, units_xa)] * 2, [], (keep_a, got_a, bias_a, keep_a), 1, 10
+        lat_sums_split, [units(zs, units_xa)] * 2, [], (keep_a, got_a, bias_a, keep_a), 0.01, 10
     )
     got_xa = x_swap(give_xa)
 

time: 99.6 us -> 99.3 us (level)
  no operation moved by 1% of the time
where the time goes in v17:
time: 99.3 us; the launch traced here: 99 us
  waiting for transfers between devices  37.6 us (38%)
  Pallas kernels  32.6 us (33%)
  starting transfers between devices  27.9 us (28%)
    pallas_call x15, Pallas kernels, call(): pl.pallas_call(kernel, out_shape=[(pltpu.VMEM if at in near else jax.Shap...  32.6 us
    ppermute x8, waiting for transfers between devices, lon_send(): lax.ppermute(value, 'lon', [(s, (s + step) % count) for s in range(count)])  17.3 us
    all_to_all x1, waiting for transfers between devices, shards(): whole_bc = lax.all_to_all(sum_bc, 'lon', 0, 0)  12.1 us
    ppermute x8, starting transfers between devices, lon_send(): lax.ppermute(value, 'lon', [(s, (s + step) % count) for s in range(count)])  9.39 us
    ppermute x2, starting transfers between devices, diag_send(): return lax.ppermute(value, ('lon', 'lat'), pairs)  5.64 us
    ppermute x8, waiting for transfers between devices, lat_swap(): return lax.ppermute(value, 'lat', [(0, 1), (1, 0)])  4.35 us
    all_to_all x1, starting transfers between devices, shards(): lax.all_to_all(part_z, 'lon', 0, 0, axis_index_groups=[[2 * z + x for z i...  4.11 us
    ppermute x2, waiting for transfers between devices, diag_send(): return lax.ppermute(value, ('lon', 'lat'), pairs)  3.8 us
  transfers between devices with their start and end apart: 23, of which 12 were waited for; matrix products, arithmetic and copies ran while one was open for 0% of the time, Pallas kernels for 12%

profile of v17, /device:TPU:0, one launch (start us, length us, event | category | flops | bytes accessed | tf_op | source)
XLA Modules:
  0.0 99.0 jit_solution(6403973946806600166)
XLA Ops:
  0.6 0.0 copy-start.6
  0.7 6.4 %shard_map.112 = (bf16[576,192]{1,0:T(8,128)(2,1)S(1)}, bf16[2,504,192]{2,1,0:T(8,128)(2,1)S(1)}, bf16[2,72,192]{2,1,0:T(8,128)(2,1)S(1)}, bf16[576,576]{1,0:T(8...) custom-call(bf16[2,12,24,192]{3,2,1,0:T(8,128)(2,1)} %tokens_in.1, ...), custom_call_target="tpu_custom_call" | custom-call | flops 8800000000 | bytes 100000 | tf_op jit(solution)/shard_map/pallas_call | solution.py:699
  7.1 0.5 collective-permute-start.1
  7.6 5.6 %collective-permute-start.2 = (bf16[2,72,192]{2,1,0:T(8,128)(2,1)S(1)}, bf16[2,72,192]{2,1,0:T(8,128)(2,1)S(1)}, u32[]{:S(2)}, u32[]{:S(2)}) collective-permute-start(bf16[2,72,192]{2,1,0:T(8,128)(2,1)S(1)} %get-tuple-element.59), channel_id=1, source_target_pairs={{0,15},{1,14},{2,1},{3,0},{4,3},{5,2},{6,5},{7,4},{8,7},{9,6},{10,... | collective-permute-start | bytes 165896 | tf_op jit(solution)/shard_map/ppermute | solution.py:743
  13.2 0.5 collective-permute-start
  13.8 0.0 copy-start.4
  13.8 2.0 %shard_map.113 = (f32[864,144]{1,0:T(8,128)S(1)}, bf16[576,768]{1,0:T(8,128)(2,1)S(1)}) custom-call(f32[2,6,1,6336]{3,2,1,0:T(1,128)S(1)} %bitcast.8, bf16[2,132,384]{2,1,0:T(8,128)(2,1)S(1)} %copy-done.6, f32[576,768]{1,0:T(8,128)S(1)} %get-tuple-element.60.hidden), custom_call_target="tpu_custom_call" | custom-call | flops 3300000000 | bytes 100000 | tf_op jit(solution)/shard_map/pallas_call | solution.py:699
  15.8 0.0 collective-permute-done.2.diag_head
  15.8 1.8 %collective-permute-done.lon_head = bf16[2,72,192]{2,1,0:T(8,128)(2,1)S(1)} collective-permute-done((bf16[2,72,192]{2,1,0:T(8,128)(2,1)S(1)}, bf16[2,72,192]{2,1,0:T(8,128)(2,1)S(1)}, u32[]{:S(2)}, u32[]{:S(2)}) %collective-permute-start) | collective-permute-done | bytes 55328 | tf_op jit(solution)/shard_map/ppermute | solution.py:729
  17.6 8.8 %shard_map.114 = (bf16[504,192]{1,0:T(8,128)(2,1)S(1)}, bf16[72,192]{1,0:T(8,128)(2,1)S(1)}, bf16[576,192]{1,0:T(8,128)(2,1)S(1)}, bf16[576,576]{1,0:T(8,128)(2,...) custom-call(bf16[2,504,192]{2,1,0:T(8,128)(2,1)S(1)} %get-tuple-elem, ...), custom_call_target="tpu_custom_call", output_to_operand_aliasing={{12}: (10, {}), {13}: (11, {}), {14}: (12, {}), {15}: (13, ... | custom-call | flops 20899999744 | bytes 100000 | tf_op jit(solution)/shard_map/pallas_call | solution.py:699
  26.4 1.6 %shard_map.115 = (bf16[8,27,8,128]{3,2,1,0:T(8,128)(2,1)S(1)}, bf16[8,27,8,128]{3,2,1,0:T(8,128)(2,1)S(1)}, bf16[8,5,8,128]{3,2,1,0:T(8,128)(2,1)S(1)}) custom-call(bf16[576,192]{1,0:T(8,128)(2,1)S(1)} %get-tuple-element.78.n1, bf16[576,576]{1,0:T(8,128)(2,1)S(1)} %get-tuple-element.79.field, bf16[576,192]{1,0:T(8,128)(2,1)S(1)} %get-tuple-element.80.mixed, ...), custom_call_target="tpu_custom_call" | custom-call | flops 11000000 | bytes 100000 | tf_op jit(solution)/shard_map/pallas_call | solution.py:699
  28.1 0.1 collective-permute-start.6
  28.1 0.5 collective-permute-start.4
  28.6 1.3 %collective-permute-done.6.refs_1_ = bf16[8,27,8,128]{3,2,1,0:T(8,128)(2,1)S(1)} collective-permute-done((bf16[8,27,8,128]{3,2,1,0:T(8,128)(2,1)S(1)}, bf16[8,27,8,128]{3,2,1,0:T(8,128)(2,1)S(1)}, u32[]{:S(2)}, u32[]{:S(2)}) %collective-permute-start.6) | collective-permute-done | bytes 442400 | tf_op jit(solution)/shard_map/ppermute | solution.py:724
  29.9 0.1 shard_map.116
  30.0 1.1 %collective-permute-start.7 = (bf16[4,32,8,128]{3,2,1,0:T(8,128)(2,1)S(1)}, bf16[4,32,8,128]{3,2,1,0:T(8,128)(2,1)S(1)}, u32[]{:S(2)}, u32[]{:S(2)}) collective-permute-start(bf16[4,32,8,128]{3,2,1,0:T(8,128)(2,1)S(1)} %get-tuple-element.96), channel_id=1, source_target_pairs={{0,2},{2,0},{4,6},{6,4},{8,10},{10,8},{12,14},{14,12},{1,3},{3,1},... | collective-permute-start | bytes 786440 | tf_op jit(solution)/shard_map/ppermute | solution.py:734
  31.1 3.8 %collective-permute-done.5.diag_tail = bf16[72,192]{1,0:T(8,128)(2,1)S(1)} collective-permute-done((bf16[72,192]{1,0:T(8,128)(2,1)S(1)}, bf16[72,192]{1,0:T(8,128)(2,1)S(1)}, u32[]{:S(2)}, u32[]{:S(2)}) %collective-permute-start.5) | collective-permute-done | bytes 27680 | tf_op jit(solution)/shard_map/ppermute | solution.py:743
  34.9 1.1 %collective-permute-done.3.lon_tail = bf16[72,192]{1,0:T(8,128)(2,1)S(1)} collective-permute-done((bf16[72,192]{1,0:T(8,128)(2,1)S(1)}, bf16[72,192]{1,0:T(8,128)(2,1)S(1)}, u32[]{:S(2)}, u32[]{:S(2)}) %collective-permute-start.3) | collective-permute-done | bytes 27680 | tf_op jit(solution)/shard_map/ppermute | solution.py:729
  36.0 2.2 %shard_map.117 = (bf16[8,21,8,128]{3,2,1,0:T(8,128)(2,1)S(1)}, bf16[8,21,8,128]{3,2,1,0:T(8,128)(2,1)S(1)}, f32[576,192]{1,0:T(8,128)S(1)}, bf16[576,192]{1,0:T(8,128)(2,1)S(1)}, f32[1,192]{1,0:T(1,128)S(1)}) custom-call(bf16[504,192]{1,0:T(8,128)(2,1)S(1)} %get-tuple-element.72.head, bf16[72,192]{1,0:T(8,128)(2,1)S(1)} %collective-permute-done.3.lon_tail, ...), custom_call_target="tpu_custom_call" | custom-call | flops 3300000000 | bytes 100000 | tf_op jit(solution)/shard_map/pallas_call | solution.py:699
  38.2 0.1 collective-permute-start.11
  38.3 5.7 %shard_map.118 = (bf16[2,12,24,192]{3,2,1,0:T(8,128)(2,1)}, bf16[8,7,8,128]{3,2,1,0:T(8,128)(2,1)S(1)}, bf16[8,7,8,128]{3,2,1,0:T(8,128)(2,1)S(1)}, bf16[8,5,8,128]{3,2,1,0:T(8,128)(2,1)S(1)}) custom-call(bf16[576,192]{1,0:T(8,128)(2,1)S(1)} %get-tuple-element.69.x_in, bf16[576,576]{1,0:T(8,128)(2,1)S(1)} %get-tuple-element.70.qkv, ...), custom_call_target="tpu_custom_call" | custom-call | flops 7699999744 | bytes 100000 | tf_op jit(solution)/shard_map/pallas_call | solution.py:699
  44.0 0.5 collective-permute-start.12
  44.5 0.1 shard_map.119
  44.6 0.9 collective-permute-done.12.refs_3_
  45.5 0.1 shard_map.120
  45.6 0.1 collective-permute-start.16
  45.7 0.1 collective-permute-start.8
  45.7 3.0 %collective-permute-start.9 = (bf16[32,8,128]{2,1,0:T(8,128)(2,1)S(1)}, bf16[32,8,128]{2,1,0:T(8,128)(2,1)S(1)}, u32[]{:S(2)}, u32[]{:S(2)}) collective-permute-start(bf16[32,8,128]{2,1,0:T(8,128)(2,1)S(1)} %get-tuple-element.99), channel_id=1, source_target_pairs={{0,8},{2,10},{4,12},{6,14},{8,0},{10,2},{12,4},{14,6},{1,9},{3,11}... | collective-permute-start | bytes 196616 | tf_op jit(solution)/shard_map/ppermute | solution.py:729
  48.7 0.9 collective-permute-start.10
  49.6 3.0 %collective-permute-done.8.refs_1_ = bf16[32,8,128]{2,1,0:T(8,128)(2,1)S(1)} collective-permute-done((bf16[32,8,128]{2,1,0:T(8,128)(2,1)S(1)}, bf16[32,8,128]{2,1,0:T(8,128)(2,1)S(1)}, u32[]{:S(2)}, u32[]{:S(2)}) %collective-permute-start.8) | collective-permute-done | bytes 65568 | tf_op jit(solution)/shard_map/ppermute | solution.py:729
  52.5 1.8 %collective-permute-done.9.refs_2_ = bf16[32,8,128]{2,1,0:T(8,128)(2,1)S(1)} collective-permute-done((bf16[32,8,128]{2,1,0:T(8,128)(2,1)S(1)}, bf16[32,8,128]{2,1,0:T(8,128)(2,1)S(1)}, u32[]{:S(2)}, u32[]{:S(2)}) %collective-permute-start.9) | collective-permute-done | bytes 65568 | tf_op jit(solution)/shard_map/ppermute | solution.py:729
  54.4 0.0 collective-permute-done.16.got
  54.4 0.8 shard_map.122.refs_4_
  55.2 4.1 %all-to-all-start = ((bf16[4,33,8,128]{3,2,1,0:T(8,128)(2,1)}), bf16[4,33,8,128]{3,2,1,0:T(8,128)(2,1)S(1)}, u32[]{:S(2)}, u32[]{:S(2)}) async-start(bf16[4,33,8,128]{3,2,1,0:T(8,128)(2,1)} %shard_map.122.refs_4_), calls=%async_computation | async-start | bytes 540672 | tf_op jit(solution)/shard_map/all_to_all | solution.py:965
  59.3 3.8 %collective-permute-start.15 = (bf16[32,8,128]{2,1,0:T(8,128)(2,1)S(1)}, bf16[32,8,128]{2,1,0:T(8,128)(2,1)S(1)}, u32[]{:S(2)}, u32[]{:S(2)}) collective-permute-start(bf16[32,8,128]{2,1,0:T(8,128)(2,1)S(1)} %shard_map.121.order.refs_0_), channel_id=1, source_target_pairs={{0,12},{2,14},{4,0},{6,2},{8,4},{10,6},{12,8},{14,10},{1,13},{3,15... | collective-permute-start | bytes 196616 | tf_op jit(solution)/shard_map/ppermute | solution.py:729
  63.1 1.1 %collective-permute-start.13 = (bf16[32,8,128]{2,1,0:T(8,128)(2,1)S(1)}, bf16[32,8,128]{2,1,0:T(8,128)(2,1)S(1)}, u32[]{:S(2)}, u32[]{:S(2)}) collective-permute-start(bf16[32,8,128]{2,1,0:T(8,128)(2,1)S(1)} %shard_map.121.order.refs_0_), channel_id=1, source_target_pairs={{0,4},{2,6},{4,8},{6,10},{8,12},{10,14},{12,0},{14,2},{1,5},{3,7},... | collective-permute-start | bytes 196616 | tf_op jit(solution)/shard_map/ppermute | solution.py:729
  64.2 2.4 %collective-permute-done.15.refs_3_ = bf16[32,8,128]{2,1,0:T(8,128)(2,1)S(1)} collective-permute-done((bf16[32,8,128]{2,1,0:T(8,128)(2,1)S(1)}, bf16[32,8,128]{2,1,0:T(8,128)(2,1)S(1)}, u32[]{:S(2)}, u32[]{:S(2)}) %collective-permute-start.15) | collective-permute-done | bytes 65568 | tf_op jit(solution)/shard_map/ppermute | solution.py:729
  66.6 7.3 %collective-permute-done.14.refs_2_ = bf16[32,8,128]{2,1,0:T(8,128)(2,1)S(1)} collective-permute-done((bf16[32,8,128]{2,1,0:T(8,128)(2,1)S(1)}, bf16[32,8,128]{2,1,0:T(8,128)(2,1)S(1)}, u32[]{:S(2)}, u32[]{:S(2)}) %collective-permute-start.14) | collective-permute-done | bytes 65568 | tf_op jit(solution)/shard_map/ppermute | solution.py:729
  73.9 1.0 shard_map.123.same.order
  74.9 0.9 shard_map.125
  75.8 3.5 %all-to-all-start.1 = ((bf16[8,33,8,128]{3,2,1,0:T(8,128)(2,1)}), bf16[8,33,8,128]{3,2,1,0:T(8,128)(2,1)S(1)}, u32[]{:S(2)}, u32[]{:S(2)}) async-start(bf16[8,33,8,128]{3,2,1,0:T(8,128)(2,1)} %shard_map.125), calls=%async_computation.1 | async-start | bytes 1081344 | tf_op jit(solution)/shard_map/all_to_all | solution.py:980
  79.3 1.9 %collective-permute-start.17 = (bf16[4,32,8,128]{3,2,1,0:T(8,128)(2,1)S(1)}, bf16[4,32,8,128]{3,2,1,0:T(8,128)(2,1)S(1)}, u32[]{:S(2)}, u32[]{:S(2)}) collective-permute-start(bf16[4,32,8,128]{3,2,1,0:T(8,128)(2,1)S(1)} %shard_map.123.same.order), channel_id=1, source_target_pairs={{0,2},{2,0},{4,6},{6,4},{8,10},{10,8},{12,14},{14,12},{1,3},{3,1},... | collective-permute-start | bytes 786440 | tf_op jit(solution)/shard_map/ppermute | solution.py:734
  81.2 12.1 %all-to-all-done.1.own_bc = bf16[8,33,8,128]{3,2,1,0:T(8,128)(2,1)S(1)} async-done(((bf16[8,33,8,128]{3,2,1,0:T(8,128)(2,1)}), bf16[8,33,8,128]{3,2,1,0:T(8,128)(2,1)S(1)}, u32[]{:S(2)}, u32[]{:S(2)}) %all-to-all-start.1) | async-done | bytes 540704 | tf_op jit(solution)/shard_map/all_to_all | solution.py:980
  93.3 0.5 collective-permute-start.18
  93.8 1.8 %collective-permute-done.18.cross = bf16[4,32,8,128]{3,2,1,0:T(8,128)(2,1)S(1)} collective-permute-done((bf16[4,32,8,128]{3,2,1,0:T(8,128)(2,1)S(1)}, bf16[4,32,8,128]{3,2,1,0:T(8,128)(2,1)S(1)}, u32[]{:S(2)}, u32[]{:S(2)}) %collective-permute-start.18) | collective-permute-done | bytes 262176 | tf_op jit(solution)/shard_map/ppermute | solution.py:724
  95.6 0.4 collective-permute-done.19.cross_x
  96.0 0.6 shard_map.124
  96.6 2.4 %shard_map.126 = (bf16[6918,128]{1,0:T(8,128)(2,1)}, f32[2,6,1,6336]{3,2,1,0:T(1,128)}) custom-call(bf16[2,132,384]{2,1,0:T(8,128)(2,1)S(1)} %copy-done.6, f32[3456,128]{1,0:T(8,128)S(1)} %get-tuple-element.108.flat_a, f32[8,128]{1,0:T(8,128)S(1)} %get-tuple-element.109.squares, f32[6,1,6336]{2,1,0:T(1,128)S(1)} %get-tuple-element.110.bias_late, ...), custom_call_target="tpu_custom_call" | custom-call | flops 2200000000 | bytes 100000 | tf_op jit(solution)/shard_map/pallas_call | solution.py:699
  (27 shorter events, 0.1 us)
Async XLA Ops:
  0.6 13.1 %copy-start.3 = (f32[2,1,6,6336]{3,1,2,0:T(1,128)S(1)}, f32[2,1,6,6336]{3,1,2,0:T(1,128)}, u32[]{:S(2)}) copy-start(f32[2,1,6,6336]{3,1,2,0:T(1,128)} %param.16) | copy-start | bytes 912388
  0.6 13.1 %copy-start.6 = (bf16[2,132,384]{2,1,0:T(8,128)(2,1)S(1)}, bf16[2,132,384]{2,1,0:T(8,128)(2,1)}, u32[]{:S(2)}) copy-start(bf16[2,132,384]{2,1,0:T(8,128)(2,1)} %constant.2.clone.spread_in.spread) | copy-start | bytes 608260
  7.1 10.5 %collective-permute-start.1 = (bf16[2,504,192]{2,1,0:T(8,128)(2,1)S(1)}, bf16[2,504,192]{2,1,0:T(8,128)(2,1)S(1)}, u32[]{:S(2)}, u32[]{:S(2)}) collective-permute-start(bf16[2,504,192]{2,1,0:T(8,128)(2,1)S(1)} %get-tuple-element.58.tail), channel_id=1, source_target_pairs={{0,1},{1,0},{2,3},{3,2},{4,5},{5,4},{6,7},{7,6},{8,9},{9,8},{10,11... | collective-permute-start | bytes 1161224 | tf_op jit(solution)/shard_map/ppermute | solution.py:724
  7.6 8.2 %collective-permute-start.2 = (bf16[2,72,192]{2,1,0:T(8,128)(2,1)S(1)}, bf16[2,72,192]{2,1,0:T(8,128)(2,1)S(1)}, u32[]{:S(2)}, u32[]{:S(2)}) collective-permute-start(bf16[2,72,192]{2,1,0:T(8,128)(2,1)S(1)} %get-tuple-element.59), channel_id=1, source_target_pairs={{0,15},{1,14},{2,1},{3,0},{4,3},{5,2},{6,5},{7,4},{8,7},{9,6},{10,... | collective-permute-start | bytes 165896 | tf_op jit(solution)/shard_map/ppermute | solution.py:743
  13.2 4.4 %collective-permute-start = (bf16[2,72,192]{2,1,0:T(8,128)(2,1)S(1)}, bf16[2,72,192]{2,1,0:T(8,128)(2,1)S(1)}, u32[]{:S(2)}, u32[]{:S(2)}) collective-permute-start(bf16[2,72,192]{2,1,0:T(8,128)(2,1)S(1)} %get-tuple-element.59), channel_id=1, source_target_pairs={{0,14},{2,0},{4,2},{6,4},{8,6},{10,8},{12,10},{14,12},{1,15},{3,1}... | collective-permute-start | bytes 165896 | tf_op jit(solution)/shard_map/ppermute | solution.py:729
  13.8 3.8 %copy-start = (bf16[2,192,768]{2,1,0:T(8,128)(2,1)S(1)}, bf16[2,192,768]{2,1,0:T(8,128)(2,1)}, u32[]{:S(2)}) copy-start(bf16[2,192,768]{2,1,0:T(8,128)(2,1)} %up_w.3) | copy-start | bytes 1769476
  13.8 3.8 %copy-start.1 = (bf16[2,768,192]{1,2,0:T(8,128)(2,1)S(1)}, bf16[2,768,192]{1,2,0:T(8,128)(2,1)}, u32[]{:S(2)}) copy-start(bf16[2,768,192]{1,2,0:T(8,128)(2,1)} %param.14) | copy-start | bytes 1769476
  13.8 3.8 %copy-start.2 = (bf16[2,192,576]{2,1,0:T(8,128)(2,1)S(1)}, bf16[2,192,576]{2,1,0:T(8,128)(2,1)}, u32[]{:S(2)}) copy-start(bf16[2,192,576]{2,1,0:T(8,128)(2,1)} %qkv_w.3) | copy-start | bytes 1327108
  13.8 3.8 %copy-start.4 = (bf16[2,192,192]{2,1,0:T(8,128)(2,1)S(1)}, bf16[2,192,192]{2,1,0:T(8,128)(2,1)}, u32[]{:S(2)}) copy-start(bf16[2,192,192]{2,1,0:T(8,128)(2,1)} %proj_w.3) | copy-start | bytes 442372
  13.8 3.8 %copy-start.5 = (f32[2,2,192]{2,1,0:T(2,128)S(1)}, f32[2,2,192]{2,1,0:T(2,128)}, u32[]{:S(2)}) copy-start(f32[2,2,192]{2,1,0:T(2,128)} %gains.5) | copy-start | bytes 9220
  28.1 1.8 %collective-permute-start.6 = (bf16[8,27,8,128]{3,2,1,0:T(8,128)(2,1)S(1)}, bf16[8,27,8,128]{3,2,1,0:T(8,128)(2,1)S(1)}, u32[]{:S(2)}, u32[]{:S(2)}) collective-permute-start(bf16[8,27,8,128]{3,2,1,0:T(8,128)(2,1)S(1)} %get-tuple-element.88), channel_id=1, source_target_pairs={{0,1},{1,0},{2,3},{3,2},{4,5},{5,4},{6,7},{7,6},{8,9},{9,8},{10,11... | collective-permute-start | bytes 1327112 | tf_op jit(solution)/shard_map/ppermute | solution.py:724
  28.1 7.9 %collective-permute-start.4 = (bf16[504,192]{1,0:T(8,128)(2,1)S(1)}, bf16[504,192]{1,0:T(8,128)(2,1)S(1)}, u32[]{:S(2)}, u32[]{:S(2)}) collective-permute-start(bf16[504,192]{1,0:T(8,128)(2,1)S(1)} %get-tuple-element.72.head), channel_id=1, source_target_pairs={{0,1},{1,0},{2,3},{3,2},{4,5},{5,4},{6,7},{7,6},{8,9},{9,8},{10,11... | collective-permute-start | bytes 580616 | tf_op jit(solution)/shard_map/ppermute | solution.py:724
  28.6 6.3 %collective-permute-start.5 = (bf16[72,192]{1,0:T(8,128)(2,1)S(1)}, bf16[72,192]{1,0:T(8,128)(2,1)S(1)}, u32[]{:S(2)}, u32[]{:S(2)}) collective-permute-start(bf16[72,192]{1,0:T(8,128)(2,1)S(1)} %get-tuple-element.73), channel_id=1, source_target_pairs={{0,3},{1,2},{2,5},{3,4},{4,7},{5,6},{6,9},{7,8},{8,11},{9,10},{10,... | collective-permute-start | bytes 82952 | tf_op jit(solution)/shard_map/ppermute | solution.py:743
  28.6 7.4 %collective-permute-start.3 = (bf16[72,192]{1,0:T(8,128)(2,1)S(1)}, bf16[72,192]{1,0:T(8,128)(2,1)S(1)}, u32[]{:S(2)}, u32[]{:S(2)}) collective-permute-start(bf16[72,192]{1,0:T(8,128)(2,1)S(1)} %get-tuple-element.73), channel_id=1, source_target_pairs={{0,2},{2,4},{4,6},{6,8},{8,10},{10,12},{12,14},{14,0},{1,3},{3,5},... | collective-permute-start | bytes 82952 | tf_op jit(solution)/shard_map/ppermute | solution.py:729
  30.0 14.5 %collective-permute-start.7 = (bf16[4,32,8,128]{3,2,1,0:T(8,128)(2,1)S(1)}, bf16[4,32,8,128]{3,2,1,0:T(8,128)(2,1)S(1)}, u32[]{:S(2)}, u32[]{:S(2)}) collective-permute-start(bf16[4,32,8,128]{3,2,1,0:T(8,128)(2,1)S(1)} %get-tuple-element.96), channel_id=1, source_target_pairs={{0,2},{2,0},{4,6},{6,4},{8,10},{10,8},{12,14},{14,12},{1,3},{3,1},... | collective-permute-start | bytes 786440 | tf_op jit(solution)/shard_map/ppermute | solution.py:734
  38.2 7.3 %collective-permute-start.11 = (bf16[8,21,8,128]{3,2,1,0:T(8,128)(2,1)S(1)}, bf16[8,21,8,128]{3,2,1,0:T(8,128)(2,1)S(1)}, u32[]{:S(2)}, u32[]{:S(2)}) collective-permute-start(bf16[8,21,8,128]{3,2,1,0:T(8,128)(2,1)S(1)} %get-tuple-element.102), channel_id=1, source_target_pairs={{0,1},{1,0},{2,3},{3,2},{4,5},{5,4},{6,7},{7,6},{8,9},{9,8},{10,11... | collective-permute-start | bytes 1032200 | tf_op jit(solution)/shard_map/ppermute | solution.py:724
  44.0 1.5 %collective-permute-start.12 = (bf16[8,7,8,128]{3,2,1,0:T(8,128)(2,1)S(1)}, bf16[8,7,8,128]{3,2,1,0:T(8,128)(2,1)S(1)}, u32[]{:S(2)}, u32[]{:S(2)}) collective-permute-start(bf16[8,7,8,128]{3,2,1,0:T(8,128)(2,1)S(1)} %get-tuple-element.104), channel_id=1, source_target_pairs={{0,1},{1,0},{2,3},{3,2},{4,5},{5,4},{6,7},{7,6},{8,9},{9,8},{10,11... | collective-permute-start | bytes 344072 | tf_op jit(solution)/shard_map/ppermute | solution.py:724
  45.6 8.8 %collective-permute-start.16 = (bf16[4,33,8,128]{3,2,1,0:T(8,128)(2,1)S(1)}, bf16[4,33,8,128]{3,2,1,0:T(8,128)(2,1)S(1)}, u32[]{:S(2)}, u32[]{:S(2)}) collective-permute-start(bf16[4,33,8,128]{3,2,1,0:T(8,128)(2,1)S(1)} %get-tuple-element.107), channel_id=1, source_target_pairs={{0,2},{2,0},{4,6},{6,4},{8,10},{10,8},{12,14},{14,12},{1,3},{3,1},... | collective-permute-start | bytes 811016 | tf_op jit(solution)/shard_map/ppermute | solution.py:734
  45.7 6.9 %collective-permute-start.8 = (bf16[32,8,128]{2,1,0:T(8,128)(2,1)S(1)}, bf16[32,8,128]{2,1,0:T(8,128)(2,1)S(1)}, u32[]{:S(2)}, u32[]{:S(2)}) collective-permute-start(bf16[32,8,128]{2,1,0:T(8,128)(2,1)S(1)} %get-tuple-element.98), channel_id=1, source_target_pairs={{0,4},{2,6},{4,8},{6,10},{8,12},{10,14},{12,0},{14,2},{1,5},{3,7},... | collective-permute-start | bytes 196616 | tf_op jit(solution)/shard_map/ppermute | solution.py:729
  45.7 8.6 %collective-permute-start.9 = (bf16[32,8,128]{2,1,0:T(8,128)(2,1)S(1)}, bf16[32,8,128]{2,1,0:T(8,128)(2,1)S(1)}, u32[]{:S(2)}, u32[]{:S(2)}) collective-permute-start(bf16[32,8,128]{2,1,0:T(8,128)(2,1)S(1)} %get-tuple-element.99), channel_id=1, source_target_pairs={{0,8},{2,10},{4,12},{6,14},{8,0},{10,2},{12,4},{14,6},{1,9},{3,11}... | collective-permute-start | bytes 196616 | tf_op jit(solution)/shard_map/ppermute | solution.py:729
  48.7 5.7 %collective-permute-start.10 = (bf16[32,8,128]{2,1,0:T(8,128)(2,1)S(1)}, bf16[32,8,128]{2,1,0:T(8,128)(2,1)S(1)}, u32[]{:S(2)}, u32[]{:S(2)}) collective-permute-start(bf16[32,8,128]{2,1,0:T(8,128)(2,1)S(1)} %get-tuple-element.100), channel_id=1, source_target_pairs={{0,12},{2,14},{4,0},{6,2},{8,4},{10,6},{12,8},{14,10},{1,13},{3,15... | collective-permute-start | bytes 196616 | tf_op jit(solution)/shard_map/ppermute | solution.py:729
  55.2 19.8 %all-to-all-start = ((bf16[4,33,8,128]{3,2,1,0:T(8,128)(2,1)}), bf16[4,33,8,128]{3,2,1,0:T(8,128)(2,1)S(1)}, u32[]{:S(2)}, u32[]{:S(2)}) async-start(bf16[4,33,8,128]{3,2,1,0:T(8,128)(2,1)} %shard_map.122.refs_4_), calls=%async_computation | async-start | bytes 540672 | tf_op jit(solution)/shard_map/all_to_all | solution.py:965
  59.3 7.4 %collective-permute-start.15 = (bf16[32,8,128]{2,1,0:T(8,128)(2,1)S(1)}, bf16[32,8,128]{2,1,0:T(8,128)(2,1)S(1)}, u32[]{:S(2)}, u32[]{:S(2)}) collective-permute-start(bf16[32,8,128]{2,1,0:T(8,128)(2,1)S(1)} %shard_map.121.order.refs_0_), channel_id=1, source_target_pairs={{0,12},{2,14},{4,0},{6,2},{8,4},{10,6},{12,8},{14,10},{1,13},{3,15... | collective-permute-start | bytes 196616 | tf_op jit(solution)/shard_map/ppermute | solution.py:729
  63.1 10.8 %collective-permute-start.14 = (bf16[32,8,128]{2,1,0:T(8,128)(2,1)S(1)}, bf16[32,8,128]{2,1,0:T(8,128)(2,1)S(1)}, u32[]{:S(2)}, u32[]{:S(2)}) collective-permute-start(bf16[32,8,128]{2,1,0:T(8,128)(2,1)S(1)} %shard_map.121.order.refs_0_), channel_id=1, source_target_pairs={{0,8},{2,10},{4,12},{6,14},{8,0},{10,2},{12,4},{14,6},{1,9},{3,11}... | collective-permute-start | bytes 196616 | tf_op jit(solution)/shard_map/ppermute | solution.py:729
  63.1 10.8 %collective-permute-start.13 = (bf16[32,8,128]{2,1,0:T(8,128)(2,1)S(1)}, bf16[32,8,128]{2,1,0:T(8,128)(2,1)S(1)}, u32[]{:S(2)}, u32[]{:S(2)}) collective-permute-start(bf16[32,8,128]{2,1,0:T(8,128)(2,1)S(1)} %shard_map.121.order.refs_0_), channel_id=1, source_target_pairs={{0,4},{2,6},{4,8},{6,10},{8,12},{10,14},{12,0},{14,2},{1,5},{3,7},... | collective-permute-start | bytes 196616 | tf_op jit(solution)/shard_map/ppermute | solution.py:729
  75.8 17.5 %all-to-all-start.1 = ((bf16[8,33,8,128]{3,2,1,0:T(8,128)(2,1)}), bf16[8,33,8,128]{3,2,1,0:T(8,128)(2,1)S(1)}, u32[]{:S(2)}, u32[]{:S(2)}) async-start(bf16[8,33,8,128]{3,2,1,0:T(8,128)(2,1)} %shard_map.125), calls=%async_computation.1 | async-start | bytes 1081344 | tf_op jit(solution)/shard_map/all_to_all | solution.py:980
  79.3 14.5 %collective-permute-start.17 = (bf16[4,32,8,128]{3,2,1,0:T(8,128)(2,1)S(1)}, bf16[4,32,8,128]{3,2,1,0:T(8,128)(2,1)S(1)}, u32[]{:S(2)}, u32[]{:S(2)}) collective-permute-start(bf16[4,32,8,128]{3,2,1,0:T(8,128)(2,1)S(1)} %shard_map.123.same.order), channel_id=1, source_target_pairs={{0,2},{2,0},{4,6},{6,4},{8,10},{10,8},{12,14},{14,12},{1,3},{3,1},... | collective-permute-start | bytes 786440 | tf_op jit(solution)/shard_map/ppermute | solution.py:734
  93.3 3.3 %collective-permute-start.20 = (bf16[8,33,8,128]{3,2,1,0:T(8,128)(2,1)S(1)}, bf16[8,33,8,128]{3,2,1,0:T(8,128)(2,1)S(1)}, u32[]{:S(2)}, u32[]{:S(2)}) collective-permute-start(bf16[8,33,8,128]{3,2,1,0:T(8,128)(2,1)S(1)} %all-to-all-done.1.own_bc), channel_id=1, source_target_pairs={{0,1},{1,0},{2,3},{3,2},{4,5},{5,4},{6,7},{7,6},{8,9},{9,8},{10,11... | collective-permute-start | bytes 1622024 | tf_op jit(solution)/shard_map/ppermute | solution.py:724
  93.3 2.3 %collective-permute-start.18 = (bf16[4,32,8,128]{3,2,1,0:T(8,128)(2,1)S(1)}, bf16[4,32,8,128]{3,2,1,0:T(8,128)(2,1)S(1)}, u32[]{:S(2)}, u32[]{:S(2)}) collective-permute-start(bf16[4,32,8,128]{3,2,1,0:T(8,128)(2,1)S(1)} %shard_map.123.same.order), channel_id=1, source_target_pairs={{0,1},{1,0},{2,3},{3,2},{4,5},{5,4},{6,7},{7,6},{8,9},{9,8},{10,11... | collective-permute-start | bytes 786440 | tf_op jit(solution)/shard_map/ppermute | solution.py:724
  93.8 2.2 %collective-permute-start.19 = (bf16[4,32,8,128]{3,2,1,0:T(8,128)(2,1)S(1)}, bf16[4,32,8,128]{3,2,1,0:T(8,128)(2,1)S(1)}, u32[]{:S(2)}, u32[]{:S(2)}) collective-permute-start(bf16[4,32,8,128]{3,2,1,0:T(8,128)(2,1)S(1)} %collective-permute-done.17.same_x), channel_id=1, source_target_pairs={{0,1},{1,0},{2,3},{3,2},{4,5},{5,4},{6,7},{7,6},{8,9},{9,8},{10,11... | collective-permute-start | bytes 786440 | tf_op jit(solution)/shard_map/ppermute | solution.py:724

commit v18 on v17

--- a/solution.py
+++ b/solution.py
@@ -669,28 +669,35 @@
     bias_rows(a, units_a, spread, bias_out, rows_scr, wide_scr, tab_scr)
 
 
-def last_kernel(
-    units_b, units_c, spread, flat_a, squares, bias_late, own_bc, oth_bc, update_out, bias_out,
-    scr, rows_scr, wide_scr, tab_scr, bc,
+def near_kernel(
+    units_b, units_c, spread, own_bc, oth_bc, flat_out, squares_out, bias_out,
+    rows_scr, wide_scr, tab_scr, bc,
 ):
     lat = lax.axis_index("lat")
     for j in range(own_bc.shape[0]):
         bc[lat, j] = own_bc[j]
         bc[1 - lat, j] = oth_bc[j]
-    total = squares[...]
-    total = total + place(bc, 0, units_b, [(864, 288), (1152, 1152), (2304, 1152)], scr)
-    total = total + place(bc, units_b, units_b + units_c, [(0, 864), (3456, 8)], scr)
+    total = place(bc, 0, units_b, [(864, 288), (1152, 1152), (2304, 1152)], flat_out)
+    squares_out[...] = total + place(
+        bc, units_b, units_b + units_c, [(0, 864), (3456, 8)], flat_out
+    )
+    bias_rows(bc, units_b + units_c, spread, bias_out, rows_scr, wide_scr, tab_scr)
+
+
+def last_kernel(
+    flat_a, squares_a, bias_late, flat_bc, squares_bc, bias_near, update_out, bias_out
+):
     count = update_out.shape[0]
-    mean = jnp.sum(total) * (1.0 / (count * 128))
+    mean = jnp.sum(squares_a[...] + squares_bc[...]) * (1.0 / (count * 128))
     scale = lax.rsqrt(mean + 1e-06)
     early, late = (0, 1728, 2304, 4608), (864, 2016, 3456, 5760)
     at = 0
     for first, second, rows in zip(early, late, (864, 288, 1152, 1152)):
-        update_out[first : first + rows, :] = (scr[at : at + rows, :] * scale).astype(BF16)
+        update_out[first : first + rows, :] = (flat_bc[at : at + rows, :] * scale).astype(BF16)
         update_out[second : second + rows, :] = (flat_a[at : at + rows, :] * scale).astype(BF16)
         at += rows
-    update_out[6912:count, :] = (scr[at : at + count - 6912, :] * scale).astype(BF16)
-    bias_rows(bc, units_b + units_c, spread, bias_out.at[0], rows_scr, wide_scr, tab_scr)
+    update_out[6912:count, :] = (flat_bc[at : at + count - 6912, :] * scale).astype(BF16)
+    bias_out[0] = bias_near[...]
     bias_out[1] = bias_late[...]
 
 
@@ -975,7 +982,7 @@
     cross = lat_swap(same)
     cross_x = lat_swap(same_x)
     (sum_bc,) = call(
-        sum_pieces, [units(lon_size, units_bc)], [], (pieces_bc, same), 1, 10
+        sum_pieces, [units(lon_size, units_bc)], [], (pieces_bc, moved_a[0]), 1, 10
     )
     whole_bc = lax.all_to_all(sum_bc, "lon", 0, 0)
     oth_bc = lat_swap(whole_bc)
@@ -990,15 +997,19 @@
         2,
         14,
     )
+    flat_bc, squares_bc, bias_near = call(
+        functools.partial(near_kernel, units_b, units_c),
+        [((block_rows + 8, 128), F32), ((UNIT, 128), F32), (table.shape[1:], F32)],
+        [*fold_scr, units(2, lon_size, units_bc)],
+        (spread, whole_bc, oth_bc),
+        20,
+        14,
+    )
     update, bias_grad = call(
-        functools.partial(last_kernel, units_b, units_c),
+        last_kernel,
         [((flat_rows, 128), BF16), (table.shape, F32)],
-        [
-            ((block_rows + 8, 128), F32),
-            *fold_scr,
-            units(2, lon_size, units_b + units_c + extra),
-        ],
-        (spread, flat_a, squares, bias_late, whole_bc, oth_bc),
+        [],
+        (flat_a, squares, bias_late, flat_bc, squares_bc, bias_near),
         2,
         14,
     )

time: 99.3 us -> 104 us (1.047)
  waiting for transfers between devices: 37.6 us -> 41.8 us
    all_to_all x1, waiting for transfers between devices: 12.1 us -> 0.01 us  [shards(): whole_bc = lax.all_to_all(sum_bc, 'lon', 0, 0)]
    ppermute x8, waiting for transfers between devices: 17.3 us -> 29.3 us  [lon_send(): lax.ppermute(value, 'lon', [(s, (s + step) % count) for s in range(count)])]
    ppermute x3, waiting for transfers between devices: 0.01 us -> 4.41 us  [x_swap(): return lax.ppermute(value, 'lon', [(s, s ^ 1) for s in range(count)])]
    pallas_call x15 -> x16, Pallas kernels: 32.6 us -> 32.7 us  [call(): pl.pallas_call(kernel, out_shape=[(pltpu.VMEM if at in near else jax.Shap...]
  transfers between devices with their start and end apart: 23 -> 23, of which waited for: 12 -> 13; matrix products, arithmetic and copies ran while one was open for 0% -> 0% of each run, Pallas kernels for 12% -> 11%
where the time goes in v18:
time: 104 us
  waiting for transfers between devices  41.8 us (40%)
  Pallas kernels  32.7 us (31%)
  starting transfers between devices  28.4 us (27%)
    pallas_call x16, Pallas kernels, call(): pl.pallas_call(kernel, out_shape=[(pltpu.VMEM if at in near else jax.Shap...  32.7 us
    ppermute x8, waiting for transfers between devices, lon_send(): lax.ppermute(value, 'lon', [(s, (s + step) % count) for s in range(count)])  29.3 us
    ppermute x8, starting transfers between devices, lon_send(): lax.ppermute(value, 'lon', [(s, (s + step) % count) for s in range(count)])  10.2 us
    ppermute x2, starting transfers between devices, diag_send(): return lax.ppermute(value, ('lon', 'lat'), pairs)  5.64 us
    ppermute x3, waiting for transfers between devices, x_swap(): return lax.ppermute(value, 'lon', [(s, s ^ 1) for s in range(count)])  4.41 us
    all_to_all x1, starting transfers between devices, shards(): lax.all_to_all(part_z, 'lon', 0, 0, axis_index_groups=[[2 * z + x for z i...  4.11 us
    ppermute x2, waiting for transfers between devices, diag_send(): return lax.ppermute(value, ('lon', 'lat'), pairs)  3.8 us
    ppermute x8, waiting for transfers between devices, lat_swap(): return lax.ppermute(value, 'lat', [(0, 1), (1, 0)])  3.71 us
  transfers between devices with their start and end apart: 23, of which 13 were waited for; matrix products, arithmetic and copies ran while one was open for 0% of the time, Pallas kernels for 11%

profile of v18, /device:TPU:0, one launch (start us, length us, event | category | flops | bytes accessed | tf_op | source)
XLA Modules:
  0.0 103.7 jit_solution(8863886402205139419)
XLA Ops:
  0.7 6.4 %shard_map.112 = (bf16[576,192]{1,0:T(8,128)(2,1)S(1)}, bf16[2,504,192]{2,1,0:T(8,128)(2,1)S(1)}, bf16[2,72,192]{2,1,0:T(8,128)(2,1)S(1)}, bf16[576,576]{1,0:T(8...) custom-call(bf16[2,12,24,192]{3,2,1,0:T(8,128)(2,1)} %tokens_in.1, ...), custom_call_target="tpu_custom_call" | custom-call | flops 8800000000 | bytes 100000 | tf_op jit(solution)/shard_map/pallas_call | solution.py:706
  7.1 0.5 collective-permute-start.1
  7.6 5.6 %collective-permute-start.2 = (bf16[2,72,192]{2,1,0:T(8,128)(2,1)S(1)}, bf16[2,72,192]{2,1,0:T(8,128)(2,1)S(1)}, u32[]{:S(2)}, u32[]{:S(2)}) collective-permute-start(bf16[2,72,192]{2,1,0:T(8,128)(2,1)S(1)} %get-tuple-element.62), channel_id=1, source_target_pairs={{0,15},{1,14},{2,1},{3,0},{4,3},{5,2},{6,5},{7,4},{8,7},{9,6},{10,... | collective-permute-start | bytes 165896 | tf_op jit(solution)/shard_map/ppermute | solution.py:750
  13.2 0.5 collective-permute-start
  13.8 2.0 %shard_map.113 = (f32[864,144]{1,0:T(8,128)S(1)}, bf16[576,768]{1,0:T(8,128)(2,1)S(1)}) custom-call(f32[2,6,1,6336]{3,2,1,0:T(1,128)S(1)} %bitcast.8, bf16[2,132,384]{2,1,0:T(8,128)(2,1)S(1)} %copy-done.6, f32[576,768]{1,0:T(8,128)S(1)} %get-tuple-element.63.hidden), custom_call_target="tpu_custom_call" | custom-call | flops 3300000000 | bytes 100000 | tf_op jit(solution)/shard_map/pallas_call | solution.py:706
  15.8 0.0 collective-permute-done.2.diag_head
  15.8 1.8 %collective-permute-done.lon_head = bf16[2,72,192]{2,1,0:T(8,128)(2,1)S(1)} collective-permute-done((bf16[2,72,192]{2,1,0:T(8,128)(2,1)S(1)}, bf16[2,72,192]{2,1,0:T(8,128)(2,1)S(1)}, u32[]{:S(2)}, u32[]{:S(2)}) %collective-permute-start) | collective-permute-done | bytes 55328 | tf_op jit(solution)/shard_map/ppermute | solution.py:736
  17.6 8.8 %shard_map.114 = (bf16[504,192]{1,0:T(8,128)(2,1)S(1)}, bf16[72,192]{1,0:T(8,128)(2,1)S(1)}, bf16[576,192]{1,0:T(8,128)(2,1)S(1)}, bf16[576,576]{1,0:T(8,128)(2,...) custom-call(bf16[2,504,192]{2,1,0:T(8,128)(2,1)S(1)} %get-tuple-elem, ...), custom_call_target="tpu_custom_call", output_to_operand_aliasing={{12}: (10, {}), {13}: (11, {}), {14}: (12, {}), {15}: (13, ... | custom-call | flops 20899999744 | bytes 100000 | tf_op jit(solution)/shard_map/pallas_call | solution.py:706
  26.4 1.6 %shard_map.115 = (bf16[8,27,8,128]{3,2,1,0:T(8,128)(2,1)S(1)}, bf16[8,27,8,128]{3,2,1,0:T(8,128)(2,1)S(1)}, bf16[8,5,8,128]{3,2,1,0:T(8,128)(2,1)S(1)}) custom-call(bf16[576,192]{1,0:T(8,128)(2,1)S(1)} %get-tuple-element.81.n1, bf16[576,576]{1,0:T(8,128)(2,1)S(1)} %get-tuple-element.82.field, bf16[576,192]{1,0:T(8,128)(2,1)S(1)} %get-tuple-element.83.mixed, ...), custom_call_target="tpu_custom_call" | custom-call | flops 11000000 | bytes 100000 | tf_op jit(solution)/shard_map/pallas_call | solution.py:706
  28.1 0.1 collective-permute-start.6
  28.1 0.5 collective-permute-start.4
  28.6 1.3 %collective-permute-done.6.refs_1_ = bf16[8,27,8,128]{3,2,1,0:T(8,128)(2,1)S(1)} collective-permute-done((bf16[8,27,8,128]{3,2,1,0:T(8,128)(2,1)S(1)}, bf16[8,27,8,128]{3,2,1,0:T(8,128)(2,1)S(1)}, u32[]{:S(2)}, u32[]{:S(2)}) %collective-permute-start.6) | collective-permute-done | bytes 442400 | tf_op jit(solution)/shard_map/ppermute | solution.py:731
  29.9 0.1 shard_map.116
  30.0 1.1 %collective-permute-start.7 = (bf16[4,32,8,128]{3,2,1,0:T(8,128)(2,1)S(1)}, bf16[4,32,8,128]{3,2,1,0:T(8,128)(2,1)S(1)}, u32[]{:S(2)}, u32[]{:S(2)}) collective-permute-start(bf16[4,32,8,128]{3,2,1,0:T(8,128)(2,1)S(1)} %get-tuple-element.99), channel_id=1, source_target_pairs={{0,2},{2,0},{4,6},{6,4},{8,10},{10,8},{12,14},{14,12},{1,3},{3,1},... | collective-permute-start | bytes 786440 | tf_op jit(solution)/shard_map/ppermute | solution.py:741
  31.1 3.8 %collective-permute-done.5.diag_tail = bf16[72,192]{1,0:T(8,128)(2,1)S(1)} collective-permute-done((bf16[72,192]{1,0:T(8,128)(2,1)S(1)}, bf16[72,192]{1,0:T(8,128)(2,1)S(1)}, u32[]{:S(2)}, u32[]{:S(2)}) %collective-permute-start.5) | collective-permute-done | bytes 27680 | tf_op jit(solution)/shard_map/ppermute | solution.py:750
  34.9 1.1 %collective-permute-done.3.lon_tail = bf16[72,192]{1,0:T(8,128)(2,1)S(1)} collective-permute-done((bf16[72,192]{1,0:T(8,128)(2,1)S(1)}, bf16[72,192]{1,0:T(8,128)(2,1)S(1)}, u32[]{:S(2)}, u32[]{:S(2)}) %collective-permute-start.3) | collective-permute-done | bytes 27680 | tf_op jit(solution)/shard_map/ppermute | solution.py:736
  36.0 2.2 %shard_map.117 = (bf16[8,21,8,128]{3,2,1,0:T(8,128)(2,1)S(1)}, bf16[8,21,8,128]{3,2,1,0:T(8,128)(2,1)S(1)}, f32[576,192]{1,0:T(8,128)S(1)}, bf16[576,192]{1,0:T(8,128)(2,1)S(1)}, f32[1,192]{1,0:T(1,128)S(1)}) custom-call(bf16[504,192]{1,0:T(8,128)(2,1)S(1)} %get-tuple-element.75.head, bf16[72,192]{1,0:T(8,128)(2,1)S(1)} %collective-permute-done.3.lon_tail, ...), custom_call_target="tpu_custom_call" | custom-call | flops 3300000000 | bytes 100000 | tf_op jit(solution)/shard_map/pallas_call | solution.py:706
  38.2 0.1 collective-permute-start.11
  38.3 5.7 %shard_map.118 = (bf16[2,12,24,192]{3,2,1,0:T(8,128)(2,1)}, bf16[8,7,8,128]{3,2,1,0:T(8,128)(2,1)S(1)}, bf16[8,7,8,128]{3,2,1,0:T(8,128)(2,1)S(1)}, bf16[8,5,8,128]{3,2,1,0:T(8,128)(2,1)S(1)}) custom-call(bf16[576,192]{1,0:T(8,128)(2,1)S(1)} %get-tuple-element.72.x_in, bf16[576,576]{1,0:T(8,128)(2,1)S(1)} %get-tuple-element.73.qkv, ...), custom_call_target="tpu_custom_call" | custom-call | flops 7699999744 | bytes 100000 | tf_op jit(solution)/shard_map/pallas_call | solution.py:706
  44.0 0.5 collective-permute-start.12
  44.5 0.1 shard_map.119
  44.6 0.9 collective-permute-done.12.refs_3_
  45.5 0.1 shard_map.120
  45.6 0.1 collective-permute-start.16
  45.7 0.1 collective-permute-start.8
  45.7 3.0 %collective-permute-start.9 = (bf16[32,8,128]{2,1,0:T(8,128)(2,1)S(1)}, bf16[32,8,128]{2,1,0:T(8,128)(2,1)S(1)}, u32[]{:S(2)}, u32[]{:S(2)}) collective-permute-start(bf16[32,8,128]{2,1,0:T(8,128)(2,1)S(1)} %get-tuple-element.102), channel_id=1, source_target_pairs={{0,8},{2,10},{4,12},{6,14},{8,0},{10,2},{12,4},{14,6},{1,9},{3,11}... | collective-permute-start | bytes 196616 | tf_op jit(solution)/shard_map/ppermute | solution.py:736
  48.7 0.9 collective-permute-start.10
  49.6 3.0 %collective-permute-done.8.refs_1_ = bf16[32,8,128]{2,1,0:T(8,128)(2,1)S(1)} collective-permute-done((bf16[32,8,128]{2,1,0:T(8,128)(2,1)S(1)}, bf16[32,8,128]{2,1,0:T(8,128)(2,1)S(1)}, u32[]{:S(2)}, u32[]{:S(2)}) %collective-permute-start.8) | collective-permute-done | bytes 65568 | tf_op jit(solution)/shard_map/ppermute | solution.py:736
  52.5 1.8 %collective-permute-done.9.refs_2_ = bf16[32,8,128]{2,1,0:T(8,128)(2,1)S(1)} collective-permute-done((bf16[32,8,128]{2,1,0:T(8,128)(2,1)S(1)}, bf16[32,8,128]{2,1,0:T(8,128)(2,1)S(1)}, u32[]{:S(2)}, u32[]{:S(2)}) %collective-permute-start.9) | collective-permute-done | bytes 65568 | tf_op jit(solution)/shard_map/ppermute | solution.py:736
  54.4 0.0 collective-permute-done.16.got
  54.4 0.8 shard_map.122.refs_4_
  55.2 4.1 %all-to-all-start = ((bf16[4,33,8,128]{3,2,1,0:T(8,128)(2,1)}), bf16[4,33,8,128]{3,2,1,0:T(8,128)(2,1)S(1)}, u32[]{:S(2)}, u32[]{:S(2)}) async-start(bf16[4,33,8,128]{3,2,1,0:T(8,128)(2,1)} %shard_map.122.refs_4_), calls=%async_computation | async-start | bytes 540672 | tf_op jit(solution)/shard_map/all_to_all | solution.py:972
  59.3 2.0 %collective-permute-start.13 = (bf16[32,8,128]{2,1,0:T(8,128)(2,1)S(1)}, bf16[32,8,128]{2,1,0:T(8,128)(2,1)S(1)}, u32[]{:S(2)}, u32[]{:S(2)}) collective-permute-start(bf16[32,8,128]{2,1,0:T(8,128)(2,1)S(1)} %shard_map.121.order.refs_0_), channel_id=1, source_target_pairs={{0,4},{2,6},{4,8},{6,10},{8,12},{10,14},{12,0},{14,2},{1,5},{3,7},... | collective-permute-start | bytes 196616 | tf_op jit(solution)/shard_map/ppermute | solution.py:736
  61.3 7.9 %collective-permute-done.13.refs_1_.order = bf16[32,8,128]{2,1,0:T(8,128)(2,1)S(1)} collective-permute-done((bf16[32,8,128]{2,1,0:T(8,128)(2,1)S(1)}, bf16[32,8,128]{2,1,0:T(8,128)(2,1)S(1)}, u32[]{:S(2)}, u32[]{:S(2)}) %collective-permute-start.13) | collective-permute-done | bytes 65568 | tf_op jit(solution)/shard_map/ppermute | solution.py:736
  69.2 0.5 all-to-all-done.pieces
  69.7 0.9 shard_map.125
  70.6 3.5 %all-to-all-start.1 = ((bf16[8,33,8,128]{3,2,1,0:T(8,128)(2,1)}), bf16[8,33,8,128]{3,2,1,0:T(8,128)(2,1)S(1)}, u32[]{:S(2)}, u32[]{:S(2)}) async-start(bf16[8,33,8,128]{3,2,1,0:T(8,128)(2,1)} %shard_map.125), calls=%async_computation.1 | async-start | bytes 1081344 | tf_op jit(solution)/shard_map/all_to_all | solution.py:987
  74.1 3.8 %collective-permute-start.15 = (bf16[32,8,128]{2,1,0:T(8,128)(2,1)S(1)}, bf16[32,8,128]{2,1,0:T(8,128)(2,1)S(1)}, u32[]{:S(2)}, u32[]{:S(2)}) collective-permute-start(bf16[32,8,128]{2,1,0:T(8,128)(2,1)S(1)} %shard_map.121.order.refs_0_), channel_id=1, source_target_pairs={{0,12},{2,14},{4,0},{6,2},{8,4},{10,6},{12,8},{14,10},{1,13},{3,15... | collective-permute-start | bytes 196616 | tf_op jit(solution)/shard_map/ppermute | solution.py:736
  77.9 5.8 %collective-permute-done.15.refs_3_ = bf16[32,8,128]{2,1,0:T(8,128)(2,1)S(1)} collective-permute-done((bf16[32,8,128]{2,1,0:T(8,128)(2,1)S(1)}, bf16[32,8,128]{2,1,0:T(8,128)(2,1)S(1)}, u32[]{:S(2)}, u32[]{:S(2)}) %collective-permute-start.15) | collective-permute-done | bytes 65568 | tf_op jit(solution)/shard_map/ppermute | solution.py:736
  83.6 8.1 %collective-permute-done.14.refs_2_ = bf16[32,8,128]{2,1,0:T(8,128)(2,1)S(1)} collective-permute-done((bf16[32,8,128]{2,1,0:T(8,128)(2,1)S(1)}, bf16[32,8,128]{2,1,0:T(8,128)(2,1)S(1)}, u32[]{:S(2)}, u32[]{:S(2)}) %collective-permute-start.14) | collective-permute-done | bytes 65568 | tf_op jit(solution)/shard_map/ppermute | solution.py:736
  91.7 1.0 shard_map.123.same
  92.7 1.5 %collective-permute-start.17 = (bf16[4,32,8,128]{3,2,1,0:T(8,128)(2,1)S(1)}, bf16[4,32,8,128]{3,2,1,0:T(8,128)(2,1)S(1)}, u32[]{:S(2)}, u32[]{:S(2)}) collective-permute-start(bf16[4,32,8,128]{3,2,1,0:T(8,128)(2,1)S(1)} %shard_map.123.same), channel_id=1, source_target_pairs={{0,2},{2,0},{4,6},{6,4},{8,10},{10,8},{12,14},{14,12},{1,3},{3,1},... | collective-permute-start | bytes 786440 | tf_op jit(solution)/shard_map/ppermute | solution.py:741
  94.2 0.5 collective-permute-start.18
  94.8 4.4 %collective-permute-done.17.same_x = bf16[4,32,8,128]{3,2,1,0:T(8,128)(2,1)S(1)} collective-permute-done((bf16[4,32,8,128]{3,2,1,0:T(8,128)(2,1)S(1)}, bf16[4,32,8,128]{3,2,1,0:T(8,128)(2,1)S(1)}, u32[]{:S(2)}, u32[]{:S(2)}) %collective-permute-start.17) | collective-permute-done | bytes 262176 | tf_op jit(solution)/shard_map/ppermute | solution.py:741
  99.2 1.5 %collective-permute-done.19.cross_x = bf16[4,32,8,128]{3,2,1,0:T(8,128)(2,1)S(1)} collective-permute-done((bf16[4,32,8,128]{3,2,1,0:T(8,128)(2,1)S(1)}, bf16[4,32,8,128]{3,2,1,0:T(8,128)(2,1)S(1)}, u32[]{:S(2)}, u32[]{:S(2)}) %collective-permute-start.19) | collective-permute-done | bytes 262176 | tf_op jit(solution)/shard_map/ppermute | solution.py:731
  100.7 0.6 shard_map.124
  101.3 0.6 shard_map.126
  101.9 1.8 %shard_map.127 = (bf16[6918,128]{1,0:T(8,128)(2,1)}, f32[2,6,1,6336]{3,2,1,0:T(1,128)}) custom-call(f32[3456,128]{1,0:T(8,128)S(1)} %get-tuple-element.111.flat_a, f32[8,128]{1,0:T(8,128)S(1)} %get-tuple-element.112.squares_a, f32[6,1,6336]{2,1,0:T(1,128)S(1)} %get-tuple-element.113.bias_late, f32[3464,128]{1,0:T(8,128)S(1)} %get-tuple-element.114.flat_bc, ...), custom_call_target="tpu_custom_call" | custom-call | flops 2200000000 | bytes 100000 | tf_op jit(solution)/shard_map/pallas_call | solution.py:706
  (28 shorter events, 0.1 us)
Async XLA Ops:
  0.6 13.1 %copy-start.3 = (f32[2,1,6,6336]{3,1,2,0:T(1,128)S(1)}, f32[2,1,6,6336]{3,1,2,0:T(1,128)}, u32[]{:S(2)}) copy-start(f32[2,1,6,6336]{3,1,2,0:T(1,128)} %param.16) | copy-start | bytes 912388
  0.6 13.1 %copy-start.6 = (bf16[2,132,384]{2,1,0:T(8,128)(2,1)S(1)}, bf16[2,132,384]{2,1,0:T(8,128)(2,1)}, u32[]{:S(2)}) copy-start(bf16[2,132,384]{2,1,0:T(8,128)(2,1)} %constant.2.clone.spread_in.spread) | copy-start | bytes 608260
  7.1 10.5 %collective-permute-start.1 = (bf16[2,504,192]{2,1,0:T(8,128)(2,1)S(1)}, bf16[2,504,192]{2,1,0:T(8,128)(2,1)S(1)}, u32[]{:S(2)}, u32[]{:S(2)}) collective-permute-start(bf16[2,504,192]{2,1,0:T(8,128)(2,1)S(1)} %get-tuple-element.61.tail), channel_id=1, source_target_pairs={{0,1},{1,0},{2,3},{3,2},{4,5},{5,4},{6,7},{7,6},{8,9},{9,8},{10,11... | collective-permute-start | bytes 1161224 | tf_op jit(solution)/shard_map/ppermute | solution.py:731
  7.6 8.2 %collective-permute-start.2 = (bf16[2,72,192]{2,1,0:T(8,128)(2,1)S(1)}, bf16[2,72,192]{2,1,0:T(8,128)(2,1)S(1)}, u32[]{:S(2)}, u32[]{:S(2)}) collective-permute-start(bf16[2,72,192]{2,1,0:T(8,128)(2,1)S(1)} %get-tuple-element.62), channel_id=1, source_target_pairs={{0,15},{1,14},{2,1},{3,0},{4,3},{5,2},{6,5},{7,4},{8,7},{9,6},{10,... | collective-permute-start | bytes 165896 | tf_op jit(solution)/shard_map/ppermute | solution.py:750
  13.2 4.4 %collective-permute-start = (bf16[2,72,192]{2,1,0:T(8,128)(2,1)S(1)}, bf16[2,72,192]{2,1,0:T(8,128)(2,1)S(1)}, u32[]{:S(2)}, u32[]{:S(2)}) collective-permute-start(bf16[2,72,192]{2,1,0:T(8,128)(2,1)S(1)} %get-tuple-element.62), channel_id=1, source_target_pairs={{0,14},{2,0},{4,2},{6,4},{8,6},{10,8},{12,10},{14,12},{1,15},{3,1}... | collective-permute-start | bytes 165896 | tf_op jit(solution)/shard_map/ppermute | solution.py:736
  13.8 3.8 %copy-start = (bf16[2,192,768]{2,1,0:T(8,128)(2,1)S(1)}, bf16[2,192,768]{2,1,0:T(8,128)(2,1)}, u32[]{:S(2)}) copy-start(bf16[2,192,768]{2,1,0:T(8,128)(2,1)} %up_w.3) | copy-start | bytes 1769476
  13.8 3.8 %copy-start.1 = (bf16[2,768,192]{1,2,0:T(8,128)(2,1)S(1)}, bf16[2,768,192]{1,2,0:T(8,128)(2,1)}, u32[]{:S(2)}) copy-start(bf16[2,768,192]{1,2,0:T(8,128)(2,1)} %param.14) | copy-start | bytes 1769476
  13.8 3.8 %copy-start.2 = (bf16[2,192,576]{2,1,0:T(8,128)(2,1)S(1)}, bf16[2,192,576]{2,1,0:T(8,128)(2,1)}, u32[]{:S(2)}) copy-start(bf16[2,192,576]{2,1,0:T(8,128)(2,1)} %qkv_w.3) | copy-start | bytes 1327108
  13.8 3.8 %copy-start.4 = (bf16[2,192,192]{2,1,0:T(8,128)(2,1)S(1)}, bf16[2,192,192]{2,1,0:T(8,128)(2,1)}, u32[]{:S(2)}) copy-start(bf16[2,192,192]{2,1,0:T(8,128)(2,1)} %proj_w.3) | copy-start | bytes 442372
  13.8 3.8 %copy-start.5 = (f32[2,2,192]{2,1,0:T(2,128)S(1)}, f32[2,2,192]{2,1,0:T(2,128)}, u32[]{:S(2)}) copy-start(f32[2,2,192]{2,1,0:T(2,128)} %gains.5) | copy-start | bytes 9220
  28.1 1.8 %collective-permute-start.6 = (bf16[8,27,8,128]{3,2,1,0:T(8,128)(2,1)S(1)}, bf16[8,27,8,128]{3,2,1,0:T(8,128)(2,1)S(1)}, u32[]{:S(2)}, u32[]{:S(2)}) collective-permute-start(bf16[8,27,8,128]{3,2,1,0:T(8,128)(2,1)S(1)} %get-tuple-element.91), channel_id=1, source_target_pairs={{0,1},{1,0},{2,3},{3,2},{4,5},{5,4},{6,7},{7,6},{8,9},{9,8},{10,11... | collective-permute-start | bytes 1327112 | tf_op jit(solution)/shard_map/ppermute | solution.py:731
  28.1 7.9 %collective-permute-start.4 = (bf16[504,192]{1,0:T(8,128)(2,1)S(1)}, bf16[504,192]{1,0:T(8,128)(2,1)S(1)}, u32[]{:S(2)}, u32[]{:S(2)}) collective-permute-start(bf16[504,192]{1,0:T(8,128)(2,1)S(1)} %get-tuple-element.75.head), channel_id=1, source_target_pairs={{0,1},{1,0},{2,3},{3,2},{4,5},{5,4},{6,7},{7,6},{8,9},{9,8},{10,11... | collective-permute-start | bytes 580616 | tf_op jit(solution)/shard_map/ppermute | solution.py:731
  28.6 6.3 %collective-permute-start.5 = (bf16[72,192]{1,0:T(8,128)(2,1)S(1)}, bf16[72,192]{1,0:T(8,128)(2,1)S(1)}, u32[]{:S(2)}, u32[]{:S(2)}) collective-permute-start(bf16[72,192]{1,0:T(8,128)(2,1)S(1)} %get-tuple-element.76), channel_id=1, source_target_pairs={{0,3},{1,2},{2,5},{3,4},{4,7},{5,6},{6,9},{7,8},{8,11},{9,10},{10,... | collective-permute-start | bytes 82952 | tf_op jit(solution)/shard_map/ppermute | solution.py:750
  28.6 7.4 %collective-permute-start.3 = (bf16[72,192]{1,0:T(8,128)(2,1)S(1)}, bf16[72,192]{1,0:T(8,128)(2,1)S(1)}, u32[]{:S(2)}, u32[]{:S(2)}) collective-permute-start(bf16[72,192]{1,0:T(8,128)(2,1)S(1)} %get-tuple-element.76), channel_id=1, source_target_pairs={{0,2},{2,4},{4,6},{6,8},{8,10},{10,12},{12,14},{14,0},{1,3},{3,5},... | collective-permute-start | bytes 82952 | tf_op jit(solution)/shard_map/ppermute | solution.py:736
  30.0 14.5 %collective-permute-start.7 = (bf16[4,32,8,128]{3,2,1,0:T(8,128)(2,1)S(1)}, bf16[4,32,8,128]{3,2,1,0:T(8,128)(2,1)S(1)}, u32[]{:S(2)}, u32[]{:S(2)}) collective-permute-start(bf16[4,32,8,128]{3,2,1,0:T(8,128)(2,1)S(1)} %get-tuple-element.99), channel_id=1, source_target_pairs={{0,2},{2,0},{4,6},{6,4},{8,10},{10,8},{12,14},{14,12},{1,3},{3,1},... | collective-permute-start | bytes 786440 | tf_op jit(solution)/shard_map/ppermute | solution.py:741
  38.2 7.3 %collective-permute-start.11 = (bf16[8,21,8,128]{3,2,1,0:T(8,128)(2,1)S(1)}, bf16[8,21,8,128]{3,2,1,0:T(8,128)(2,1)S(1)}, u32[]{:S(2)}, u32[]{:S(2)}) collective-permute-start(bf16[8,21,8,128]{3,2,1,0:T(8,128)(2,1)S(1)} %get-tuple-element.105), channel_id=1, source_target_pairs={{0,1},{1,0},{2,3},{3,2},{4,5},{5,4},{6,7},{7,6},{8,9},{9,8},{10,11... | collective-permute-start | bytes 1032200 | tf_op jit(solution)/shard_map/ppermute | solution.py:731
  44.0 1.5 %collective-permute-start.12 = (bf16[8,7,8,128]{3,2,1,0:T(8,128)(2,1)S(1)}, bf16[8,7,8,128]{3,2,1,0:T(8,128)(2,1)S(1)}, u32[]{:S(2)}, u32[]{:S(2)}) collective-permute-start(bf16[8,7,8,128]{3,2,1,0:T(8,128)(2,1)S(1)} %get-tuple-element.107), channel_id=1, source_target_pairs={{0,1},{1,0},{2,3},{3,2},{4,5},{5,4},{6,7},{7,6},{8,9},{9,8},{10,11... | collective-permute-start | bytes 344072 | tf_op jit(solution)/shard_map/ppermute | solution.py:731
  45.6 8.8 %collective-permute-start.16 = (bf16[4,33,8,128]{3,2,1,0:T(8,128)(2,1)S(1)}, bf16[4,33,8,128]{3,2,1,0:T(8,128)(2,1)S(1)}, u32[]{:S(2)}, u32[]{:S(2)}) collective-permute-start(bf16[4,33,8,128]{3,2,1,0:T(8,128)(2,1)S(1)} %get-tuple-element.110), channel_id=1, source_target_pairs={{0,2},{2,0},{4,6},{6,4},{8,10},{10,8},{12,14},{14,12},{1,3},{3,1},... | collective-permute-start | bytes 811016 | tf_op jit(solution)/shard_map/ppermute | solution.py:741
  45.7 6.9 %collective-permute-start.8 = (bf16[32,8,128]{2,1,0:T(8,128)(2,1)S(1)}, bf16[32,8,128]{2,1,0:T(8,128)(2,1)S(1)}, u32[]{:S(2)}, u32[]{:S(2)}) collective-permute-start(bf16[32,8,128]{2,1,0:T(8,128)(2,1)S(1)} %get-tuple-element.101), channel_id=1, source_target_pairs={{0,4},{2,6},{4,8},{6,10},{8,12},{10,14},{12,0},{14,2},{1,5},{3,7},... | collective-permute-start | bytes 196616 | tf_op jit(solution)/shard_map/ppermute | solution.py:736
  45.7 8.6 %collective-permute-start.9 = (bf16[32,8,128]{2,1,0:T(8,128)(2,1)S(1)}, bf16[32,8,128]{2,1,0:T(8,128)(2,1)S(1)}, u32[]{:S(2)}, u32[]{:S(2)}) collective-permute-start(bf16[32,8,128]{2,1,0:T(8,128)(2,1)S(1)} %get-tuple-element.102), channel_id=1, source_target_pairs={{0,8},{2,10},{4,12},{6,14},{8,0},{10,2},{12,4},{14,6},{1,9},{3,11}... | collective-permute-start | bytes 196616 | tf_op jit(solution)/shard_map/ppermute | solution.py:736
  48.7 5.7 %collective-permute-start.10 = (bf16[32,8,128]{2,1,0:T(8,128)(2,1)S(1)}, bf16[32,8,128]{2,1,0:T(8,128)(2,1)S(1)}, u32[]{:S(2)}, u32[]{:S(2)}) collective-permute-start(bf16[32,8,128]{2,1,0:T(8,128)(2,1)S(1)} %get-tuple-element.103), channel_id=1, source_target_pairs={{0,12},{2,14},{4,0},{6,2},{8,4},{10,6},{12,8},{14,10},{1,13},{3,15... | collective-permute-start | bytes 196616 | tf_op jit(solution)/shard_map/ppermute | solution.py:736
  55.2 14.5 %all-to-all-start = ((bf16[4,33,8,128]{3,2,1,0:T(8,128)(2,1)}), bf16[4,33,8,128]{3,2,1,0:T(8,128)(2,1)S(1)}, u32[]{:S(2)}, u32[]{:S(2)}) async-start(bf16[4,33,8,128]{3,2,1,0:T(8,128)(2,1)} %shard_map.122.refs_4_), calls=%async_computation | async-start | bytes 540672 | tf_op jit(solution)/shard_map/all_to_all | solution.py:972
  59.3 9.9 %collective-permute-start.13 = (bf16[32,8,128]{2,1,0:T(8,128)(2,1)S(1)}, bf16[32,8,128]{2,1,0:T(8,128)(2,1)S(1)}, u32[]{:S(2)}, u32[]{:S(2)}) collective-permute-start(bf16[32,8,128]{2,1,0:T(8,128)(2,1)S(1)} %shard_map.121.order.refs_0_), channel_id=1, source_target_pairs={{0,4},{2,6},{4,8},{6,10},{8,12},{10,14},{12,0},{14,2},{1,5},{3,7},... | collective-permute-start | bytes 196616 | tf_op jit(solution)/shard_map/ppermute | solution.py:736
  70.6 23.7 %all-to-all-start.1 = ((bf16[8,33,8,128]{3,2,1,0:T(8,128)(2,1)}), bf16[8,33,8,128]{3,2,1,0:T(8,128)(2,1)S(1)}, u32[]{:S(2)}, u32[]{:S(2)}) async-start(bf16[8,33,8,128]{3,2,1,0:T(8,128)(2,1)} %shard_map.125), calls=%async_computation.1 | async-start | bytes 1081344 | tf_op jit(solution)/shard_map/all_to_all | solution.py:987
  74.1 9.5 %collective-permute-start.15 = (bf16[32,8,128]{2,1,0:T(8,128)(2,1)S(1)}, bf16[32,8,128]{2,1,0:T(8,128)(2,1)S(1)}, u32[]{:S(2)}, u32[]{:S(2)}) collective-permute-start(bf16[32,8,128]{2,1,0:T(8,128)(2,1)S(1)} %shard_map.121.order.refs_0_), channel_id=1, source_target_pairs={{0,12},{2,14},{4,0},{6,2},{8,4},{10,6},{12,8},{14,10},{1,13},{3,15... | collective-permute-start | bytes 196616 | tf_op jit(solution)/shard_map/ppermute | solution.py:736
  77.9 13.9 %collective-permute-start.14 = (bf16[32,8,128]{2,1,0:T(8,128)(2,1)S(1)}, bf16[32,8,128]{2,1,0:T(8,128)(2,1)S(1)}, u32[]{:S(2)}, u32[]{:S(2)}) collective-permute-start(bf16[32,8,128]{2,1,0:T(8,128)(2,1)S(1)} %shard_map.121.order.refs_0_), channel_id=1, source_target_pairs={{0,8},{2,10},{4,12},{6,14},{8,0},{10,2},{12,4},{14,6},{1,9},{3,11}... | collective-permute-start | bytes 196616 | tf_op jit(solution)/shard_map/ppermute | solution.py:736
  92.7 6.4 %collective-permute-start.17 = (bf16[4,32,8,128]{3,2,1,0:T(8,128)(2,1)S(1)}, bf16[4,32,8,128]{3,2,1,0:T(8,128)(2,1)S(1)}, u32[]{:S(2)}, u32[]{:S(2)}) collective-permute-start(bf16[4,32,8,128]{3,2,1,0:T(8,128)(2,1)S(1)} %shard_map.123.same), channel_id=1, source_target_pairs={{0,2},{2,0},{4,6},{6,4},{8,10},{10,8},{12,14},{14,12},{1,3},{3,1},... | collective-permute-start | bytes 786440 | tf_op jit(solution)/shard_map/ppermute | solution.py:741
  94.2 7.1 %collective-permute-start.20 = (bf16[8,33,8,128]{3,2,1,0:T(8,128)(2,1)S(1)}, bf16[8,33,8,128]{3,2,1,0:T(8,128)(2,1)S(1)}, u32[]{:S(2)}, u32[]{:S(2)}) collective-permute-start(bf16[8,33,8,128]{3,2,1,0:T(8,128)(2,1)S(1)} %all-to-all-done.1.own_bc), channel_id=1, source_target_pairs={{0,1},{1,0},{2,3},{3,2},{4,5},{5,4},{6,7},{7,6},{8,9},{9,8},{10,11... | collective-permute-start | bytes 1622024 | tf_op jit(solution)/shard_map/ppermute | solution.py:731
  94.2 4.9 %collective-permute-start.18 = (bf16[4,32,8,128]{3,2,1,0:T(8,128)(2,1)S(1)}, bf16[4,32,8,128]{3,2,1,0:T(8,128)(2,1)S(1)}, u32[]{:S(2)}, u32[]{:S(2)}) collective-permute-start(bf16[4,32,8,128]{3,2,1,0:T(8,128)(2,1)S(1)} %shard_map.123.same), channel_id=1, source_target_pairs={{0,1},{1,0},{2,3},{3,2},{4,5},{5,4},{6,7},{7,6},{8,9},{9,8},{10,11... | collective-permute-start | bytes 786440 | tf_op jit(solution)/shard_map/ppermute | solution.py:731
  99.2 1.5 %collective-permute-start.19 = (bf16[4,32,8,128]{3,2,1,0:T(8,128)(2,1)S(1)}, bf16[4,32,8,128]{3,2,1,0:T(8,128)(2,1)S(1)}, u32[]{:S(2)}, u32[]{:S(2)}) collective-permute-start(bf16[4,32,8,128]{3,2,1,0:T(8,128)(2,1)S(1)} %collective-permute-done.17.same_x), channel_id=1, source_target_pairs={{0,1},{1,0},{2,3},{3,2},{4,5},{5,4},{6,7},{7,6},{8,9},{9,8},{10,11... | collective-permute-start | bytes 786440 | tf_op jit(solution)/shard_map/ppermute | solution.py:731
